TPU v7x, 32 devices: a whole 2x2x4 slice. The times are simulated.
32 devices in a mesh: rhs: 2 (over x), row: 8 (over z, y), col: 2 (over core).
Axes of the slice: x: 2, y: 2, z: 4, core: 2. Of those that a mesh axis runs over, the one named last changes fastest.
Arguments:
- tiles: bfloat16 [2080, 128, 128], P(('row', 'col')), as said below
- tile_rows: int32 [2080], P(('row', 'col')), may hold values from 0 to 3, as said below
- tile_cols: int32 [2080], P(('row', 'col')), may hold values from 0 to 31
- tile_count: int32 [16], P(('row', 'col')), may hold values from 2 to 130, as said below
- signs: int32 [64, 4096], P('rhs', ('row', 'col')), parts along dimension 0, may hold values from -1 to 1, as said below
- vertex_weight: float32 [4096], P(('row', 'col')), as said below
- column_scale: float32 [64], P('rhs'), parts along dimension 0, may hold values from 0.3 to 3
Outputs:
- solution: float32 [64, 4096], P('rhs', ('row', 'col')), parts along dimension 0
- residual: float32 [64, 4096], P('rhs', ('row', 'col')), parts along dimension 0
There are 2 independent parts, one for each index of `rhs`. A program takes and returns all parts, laid end to end along the dimension named above; an argument that names none is the same for every part. Nothing has to cross between parts.
Inputs may be any that keep to these rules, and one draw needn't show every extreme that they name: Live tiles pair up: a live slot holding block (i, j) has a live partner slot holding block (j, i) whose tile is its transpose, and a tile of a block (i, i) is symmetric. Every diagonal entry of A exceeds the sum of the magnitudes of the other entries of its row; off-diagonal entries are at most 0. Padded slots hold arbitrary finite values. A live slot of a device in row group r, col index c lies in block row r * 4 + tile_rows and in a block column b with (b // 2) % 2 == c. `tile_count`: live slots come first on each device; every device holds the diagonal tile of each block b of its row group with (b // 2) % 2 equal to its col index. `signs`: every entry is -1 or 1. `vertex_weight`: every weight lies between 0.2 and 3.
All inputs are finite; a program needn't handle non-finite values.
Results may differ from a plain program's by a relative error of at most 0.01.
The roundings to bfloat16 on the way count: a program that leaves them out, or rounds other values in their place, can miss the bound.
Values may be sent and summed in bfloat16 or wider, within the bound.
No kernel may reach another device: no remote copies, remote signals or barrier semaphores. Data moves between devices by JAX's collectives and lax.ppermute only.
A program may use at most 64 MiB of HBM per device.

v0:
```python
import jax
import jax.numpy as jnp
from jax import lax
from jax.sharding import PartitionSpec as P

ITERS = 3


def gram_of(left, right):
    return jnp.dot(
        left, right.T, precision=lax.Precision.HIGHEST, preferred_element_type=jnp.float32
    )


def full_dot(left, right):
    return jnp.dot(left, right, precision=lax.Precision.HIGHEST, preferred_element_type=jnp.float32)


def solve_spd(matrix, target):
    symmetric = 0.5 * (matrix + matrix.T)
    factor = jnp.linalg.cholesky(symmetric)
    return jax.scipy.linalg.cho_solve((factor, True), target)


def per_device(tiles, tile_rows, tile_cols, tile_count, signs, vertex_weight, column_scale):
    sketch = signs.shape[0]
    rows_dev = signs.shape[1]
    tile_size = tiles.shape[1]
    slot_count = tiles.shape[0]
    blocks = rows_dev // tile_size
    col_devices = lax.axis_size("col")
    right_side = signs.astype(jnp.float32) * vertex_weight[None, :] * column_scale[:, None]
    piece_index = tile_cols // blocks
    within = tile_cols % blocks
    gather_offset = piece_index // col_devices * rows_dev + within * tile_size
    live_count = tile_count[0]
    group_size = min(32, slot_count)
    turn_count = (live_count + group_size - 1) // group_size

    def slice_columns(source, offsets):
        return jax.vmap(
            lambda offset: lax.dynamic_slice_in_dim(source, offset, tile_size, 1), out_axes=1
        )(offsets)

    solution = jnp.zeros_like(right_side)
    residual = right_side
    direction = right_side
    norm_now = lax.psum(gram_of(residual, residual), ("row", "col"))
    for iteration in range(ITERS):
        outgoing = direction.astype(jnp.bfloat16)
        gathered = lax.all_gather(outgoing, "row", axis=1, tiled=True)

        def add_rows(running, tile_group, slot_index, keep_mask):
            picked = slice_columns(gathered, gather_offset[slot_index])
            product = jnp.einsum(
                "gab,sgb->sga", tile_group, picked, preferred_element_type=jnp.float32
            )
            product = product * keep_mask[None, :, None]
            return running.at[:, tile_rows[slot_index], :].add(product)

        contribute = add_rows

        def one_turn(turn_index, running):
            first = jnp.minimum(turn_index * group_size, slot_count - group_size)
            slot_index = first + jnp.arange(group_size, dtype=jnp.int32)
            keep_mask = (
                (slot_index >= turn_index * group_size) & (slot_index < live_count)
            ).astype(jnp.float32)
            tile_group = lax.dynamic_slice_in_dim(tiles, first, group_size, 0)
            return contribute(running, tile_group, slot_index, keep_mask)

        partial_sum = lax.fori_loop(
            0,
            turn_count,
            one_turn,
            jnp.zeros((sketch, col_devices * blocks, tile_size), jnp.float32),
        )
        image = lax.psum_scatter(
            partial_sum.reshape(sketch, col_devices * rows_dev),
            "col",
            scatter_dimension=1,
            tiled=True,
        )
        curvature = lax.psum(gram_of(direction, image), ("row", "col"))
        alpha = solve_spd(curvature, norm_now)
        solution = solution + full_dot(alpha.T, direction)
        residual = residual - full_dot(alpha.T, image)
        if iteration + 1 < ITERS:
            norm_next = lax.psum(gram_of(residual, residual), ("row", "col"))
            beta = solve_spd(norm_now, norm_next)
            direction = residual + full_dot(beta.T, direction)
            norm_now = norm_next
    return (solution, residual)


def solution(mesh):
    return jax.shard_map(
        per_device,
        mesh=mesh,
        in_specs=(
            P(("row", "col"), None, None),
            P(("row", "col")),
            P(("row", "col")),
            P(("row", "col")),
            P("rhs", ("row", "col")),
            P(("row", "col")),
            P("rhs"),
        ),
        out_specs=(P("rhs", ("row", "col")), P("rhs", ("row", "col"))),
        check_vma=False,
    )
```

profile of v0, /device:TPU:0, one launch (start us, length us, event | category | flops | bytes accessed | tf_op | source)
XLA Modules:
  0.0 1252.2 jit_solution(16027760737959070072)
XLA Ops:
  9.4 32.3 %all_gather.9 = bf16[32,2048]{1,0:T(8,128)(2,1)S(1)} all-gather(bf16[32,256]{1,0:T(8,128)(2,1)S(1)} %fusion.55), channel_id=1, replica_groups=mesh['rhs'=2,'row'=8,'col'=2] {'row'}, dimensions={1}, use_global_device_ids=true | all-gather | bytes 147456 | tf_op jit(solution)/shard_map/all_gather | solution.py:51
  41.8 159.2 %while.37 = (s32[]{:T(128)}, f32[32,4,128]{2,0,1:T(8,128)S(1)}, s32[]{:T(128)}, s32[130]{0:T(256)}, s32[130]{0:T(256)S(1)}, /*index=5*/bf16[32,2048]{1,0:T(8,128...) while((s32[]{:T(128)}, f32[32,4,128]{2,0,1:T(8,128)S(1)}, ...), condition=%wide.region_2.3_spmd, body=%wide.region_0.2_spmd.sunk | while | flops 33818088 | bytes 3431032 | solution.py:72
  41.8 1.4 gather_fusion.4
  44.0 46.4 %while.42 = (s32[]{:T(128)}, bf16[32,2048]{1,0:T(8,128)(2,1)S(1)}, s32[32,2]{0,1:T(2,128)S(1)}, bf16[32,32,128]{2,1,0:T(8,128)(2,1)S(1)}, s32[]{:T(128)}) while((s32[]{:T(128)}, bf16[32,2048]{1,0:T(8,128)(2,1)S(1)}, s32[32,2]{0,1:T(2,128)S(1)}, bf16[32,32,128]{2,1,0:T(8,128)(2,1)S(1)}, s32[]{:T(128)}) %tuple.104), condition=%wide.while_cond, body=%wide.while_body.sunk | while | flops 2 | bytes 16489 | solution.py:42
  91.0 1.9 convolution_multiply_fusion.6
  92.9 1.9 scatter_fusion.2
  94.9 1.4 gather_fusion.4
  97.0 46.4 %while.42 = (s32[]{:T(128)}, bf16[32,2048]{1,0:T(8,128)(2,1)S(1)}, s32[32,2]{0,1:T(2,128)S(1)}, bf16[32,32,128]{2,1,0:T(8,128)(2,1)S(1)}, s32[]{:T(128)}) while((s32[]{:T(128)}, bf16[32,2048]{1,0:T(8,128)(2,1)S(1)}, s32[32,2]{0,1:T(2,128)S(1)}, bf16[32,32,128]{2,1,0:T(8,128)(2,1)S(1)}, s32[]{:T(128)}) %tuple.104), condition=%wide.while_cond, body=%wide.while_body.sunk | while | flops 2 | bytes 16489 | solution.py:42
  144.1 1.9 convolution_multiply_fusion.6
  146.0 1.9 scatter_fusion.2
  147.9 1.4 gather_fusion.4
  150.1 46.4 %while.42 = (s32[]{:T(128)}, bf16[32,2048]{1,0:T(8,128)(2,1)S(1)}, s32[32,2]{0,1:T(2,128)S(1)}, bf16[32,32,128]{2,1,0:T(8,128)(2,1)S(1)}, s32[]{:T(128)}) while((s32[]{:T(128)}, bf16[32,2048]{1,0:T(8,128)(2,1)S(1)}, s32[32,2]{0,1:T(2,128)S(1)}, bf16[32,32,128]{2,1,0:T(8,128)(2,1)S(1)}, s32[]{:T(128)}) %tuple.104), condition=%wide.while_cond, body=%wide.while_body.sunk | while | flops 2 | bytes 16489 | solution.py:42
  197.2 1.9 convolution_multiply_fusion.6
  199.1 1.9 scatter_fusion.2
  201.9 108.0 %reduce-scatter.4.cloned.1.call-done = f32[32,256]{1,0:T(8,128)} async-done(((f32[32,512]{1,0:T(8,128)}), f32[32,256]{1,0:T(8,128)}) %reduce-scatter.4.cloned.1.call-update) | async-done | bytes 32784 | tf_op jit(solution)/shard_map/reduce_scatter | solution.py:78
  309.9 1.0 fusion.54
  310.9 61.9 %all-reduce.3 = (f32[32,32]{1,0:T(8,128)S(1)}, f32[32,32]{1,0:T(8,128)S(1)}) all-reduce(f32[32,32]{1,0:T(8,128)S(1)} %fusion.53, f32[32,32]{1,0:T(8,128)S(1)} %fusion.54), channel_id=1, replica_groups=mesh['rhs'=2,'row'=8,'col'=2] {'row','col'}, use_global_device_ids=true, to_apply=%region_7.9 | all-reduce | flops 2048 | bytes 16384 | tf_op jit(solution)/shard_map/psum | solution.py:48
  373.1 2.9 cholesky.89
  377.3 2.4 custom-call.11
  380.1 1.0 convolution_subtract_fusion.2
  381.3 57.6 %psum.44 = f32[32,32]{1,0:T(8,128)S(1)} all-reduce(f32[32,32]{1,0:T(8,128)S(1)} %fusion.58), channel_id=1, replica_groups=mesh['rhs'=2,'row'=8,'col'=2] {'row','col'}, use_global_device_ids=true, to_apply=%region_8.11 | all-reduce | flops 1024 | bytes 8192 | tf_op jit(solution)/shard_map/psum | solution.py:89
  439.0 2.9 cholesky.100
  443.2 2.4 custom-call.12
  446.4 30.5 %all_gather.10 = bf16[32,2048]{1,0:T(8,128)(2,1)S(1)} all-gather(bf16[32,256]{1,0:T(8,128)(2,1)S(1)} %get-tuple-element.234), channel_id=1, replica_groups=mesh['rhs'=2,'row'=8,'col'=2] {'row'}, dimensions={1}, use_global_device_ids=true | all-gather | bytes 147456 | tf_op jit(solution)/shard_map/all_gather | solution.py:51
  476.9 159.2 %while.39 = (s32[]{:T(128)}, f32[32,4,128]{2,0,1:T(8,128)S(1)}, s32[]{:T(128)}, s32[130]{0:T(256)}, s32[130]{0:T(256)S(1)}, /*index=5*/bf16[32,2048]{1,0:T(8,128...) while((s32[]{:T(128)}, f32[32,4,128]{2,0,1:T(8,128)S(1)}, ...), condition=%wide.region_11.14_spmd, body=%wide.region_9.13_spmd.sunk | while | flops 33818088 | bytes 3431032 | solution.py:72
  477.0 1.4 gather_fusion.2
  479.1 46.4 %while.43 = (s32[]{:T(128)}, bf16[32,2048]{1,0:T(8,128)(2,1)S(1)}, s32[32,2]{0,1:T(2,128)S(1)}, bf16[32,32,128]{2,1,0:T(8,128)(2,1)S(1)}, s32[]{:T(128)}) while((s32[]{:T(128)}, bf16[32,2048]{1,0:T(8,128)(2,1)S(1)}, s32[32,2]{0,1:T(2,128)S(1)}, bf16[32,32,128]{2,1,0:T(8,128)(2,1)S(1)}, s32[]{:T(128)}) %tuple.101), condition=%wide.while_cond.1, body=%wide.while_body.1.sunk | while | flops 2 | bytes 16489 | solution.py:42
  526.2 1.9 convolution_multiply_fusion.7
  528.1 1.9 scatter_fusion.1
  530.0 1.4 gather_fusion.2
  532.2 46.4 %while.43 = (s32[]{:T(128)}, bf16[32,2048]{1,0:T(8,128)(2,1)S(1)}, s32[32,2]{0,1:T(2,128)S(1)}, bf16[32,32,128]{2,1,0:T(8,128)(2,1)S(1)}, s32[]{:T(128)}) while((s32[]{:T(128)}, bf16[32,2048]{1,0:T(8,128)(2,1)S(1)}, s32[32,2]{0,1:T(2,128)S(1)}, bf16[32,32,128]{2,1,0:T(8,128)(2,1)S(1)}, s32[]{:T(128)}) %tuple.101), condition=%wide.while_cond.1, body=%wide.while_body.1.sunk | while | flops 2 | bytes 16489 | solution.py:42
  579.3 1.9 convolution_multiply_fusion.7
  581.2 1.9 scatter_fusion.1
  583.1 1.4 gather_fusion.2
  585.2 46.4 %while.43 = (s32[]{:T(128)}, bf16[32,2048]{1,0:T(8,128)(2,1)S(1)}, s32[32,2]{0,1:T(2,128)S(1)}, bf16[32,32,128]{2,1,0:T(8,128)(2,1)S(1)}, s32[]{:T(128)}) while((s32[]{:T(128)}, bf16[32,2048]{1,0:T(8,128)(2,1)S(1)}, s32[32,2]{0,1:T(2,128)S(1)}, bf16[32,32,128]{2,1,0:T(8,128)(2,1)S(1)}, s32[]{:T(128)}) %tuple.101), condition=%wide.while_cond.1, body=%wide.while_body.1.sunk | while | flops 2 | bytes 16489 | solution.py:42
  632.3 1.9 convolution_multiply_fusion.7
  634.2 1.9 scatter_fusion.1
  636.9 2.9 cholesky.122
  641.2 2.4 custom-call.14
  643.9 101.2 %reduce-scatter.6.cloned.1.call-done = f32[32,256]{1,0:T(8,128)} async-done(((f32[32,512]{1,0:T(8,128)}), f32[32,256]{1,0:T(8,128)}) %reduce-scatter.6.cloned.1.call-update) | async-done | bytes 32784 | tf_op jit(solution)/shard_map/reduce_scatter | solution.py:78
  746.0 61.9 %psum.45 = f32[32,32]{1,0:T(8,128)S(1)} all-reduce(f32[32,32]{1,0:T(8,128)S(1)} %fusion.59), channel_id=1, replica_groups=mesh['rhs'=2,'row'=8,'col'=2] {'row','col'}, use_global_device_ids=true, to_apply=%region_13.16 | all-reduce | flops 1024 | bytes 8192 | tf_op jit(solution)/shard_map/psum | solution.py:84
  808.1 2.9 cholesky.111
  812.4 2.4 custom-call.13
  815.2 1.0 convolution_subtract_fusion.1
  816.3 57.6 %psum.46 = f32[32,32]{1,0:T(8,128)S(1)} all-reduce(f32[32,32]{1,0:T(8,128)S(1)} %fusion.60), channel_id=1, replica_groups=mesh['rhs'=2,'row'=8,'col'=2] {'row','col'}, use_global_device_ids=true, to_apply=%region_14.17 | all-reduce | flops 1024 | bytes 8192 | tf_op jit(solution)/shard_map/psum | solution.py:89
  874.6 30.5 %all_gather.11 = bf16[32,2048]{1,0:T(8,128)(2,1)S(1)} all-gather(bf16[32,256]{1,0:T(8,128)(2,1)S(1)} %get-tuple-element.236), channel_id=1, replica_groups=mesh['rhs'=2,'row'=8,'col'=2] {'row'}, dimensions={1}, use_global_device_ids=true | all-gather | bytes 147456 | tf_op jit(solution)/shard_map/all_gather | solution.py:51
  905.1 159.2 %while.41 = (s32[]{:T(128)}, f32[32,4,128]{2,0,1:T(8,128)S(1)}, s32[]{:T(128)}, s32[130]{0:T(256)}, s32[130]{0:T(256)S(1)}, /*index=5*/bf16[32,2048]{1,0:T(8,128...) while((s32[]{:T(128)}, f32[32,4,128]{2,0,1:T(8,128)S(1)}, ...), condition=%wide.region_17.20_spmd, body=%wide.region_15.19_spmd.sunk | while | flops 33818088 | bytes 3431032 | solution.py:72
  905.1 1.4 gather_fusion
  907.3 46.4 %while.44 = (s32[]{:T(128)}, bf16[32,2048]{1,0:T(8,128)(2,1)S(1)}, s32[32,2]{0,1:T(2,128)S(1)}, bf16[32,32,128]{2,1,0:T(8,128)(2,1)S(1)}, s32[]{:T(128)}) while((s32[]{:T(128)}, bf16[32,2048]{1,0:T(8,128)(2,1)S(1)}, s32[32,2]{0,1:T(2,128)S(1)}, bf16[32,32,128]{2,1,0:T(8,128)(2,1)S(1)}, s32[]{:T(128)}) %tuple.98), condition=%wide.while_cond.2, body=%wide.while_body.2.sunk | while | flops 2 | bytes 16489 | solution.py:42
  954.3 1.9 convolution_multiply_fusion.8
  956.2 1.9 scatter_fusion
  958.2 1.4 gather_fusion
  960.3 46.4 %while.44 = (s32[]{:T(128)}, bf16[32,2048]{1,0:T(8,128)(2,1)S(1)}, s32[32,2]{0,1:T(2,128)S(1)}, bf16[32,32,128]{2,1,0:T(8,128)(2,1)S(1)}, s32[]{:T(128)}) while((s32[]{:T(128)}, bf16[32,2048]{1,0:T(8,128)(2,1)S(1)}, s32[32,2]{0,1:T(2,128)S(1)}, bf16[32,32,128]{2,1,0:T(8,128)(2,1)S(1)}, s32[]{:T(128)}) %tuple.98), condition=%wide.while_cond.2, body=%wide.while_body.2.sunk | while | flops 2 | bytes 16489 | solution.py:42
  1007.4 1.9 convolution_multiply_fusion.8
  1009.3 1.9 scatter_fusion
  1011.3 1.4 gather_fusion
  1013.4 46.4 %while.44 = (s32[]{:T(128)}, bf16[32,2048]{1,0:T(8,128)(2,1)S(1)}, s32[32,2]{0,1:T(2,128)S(1)}, bf16[32,32,128]{2,1,0:T(8,128)(2,1)S(1)}, s32[]{:T(128)}) while((s32[]{:T(128)}, bf16[32,2048]{1,0:T(8,128)(2,1)S(1)}, s32[32,2]{0,1:T(2,128)S(1)}, bf16[32,32,128]{2,1,0:T(8,128)(2,1)S(1)}, s32[]{:T(128)}) %tuple.98), condition=%wide.while_cond.2, body=%wide.while_body.2.sunk | while | flops 2 | bytes 16489 | solution.py:42
  1060.5 1.9 convolution_multiply_fusion.8
  1062.4 1.9 scatter_fusion
  1065.1 108.0 %reduce-scatter.8.cloned.1.call-done = f32[32,256]{1,0:T(8,128)} async-done(((f32[32,512]{1,0:T(8,128)}), f32[32,256]{1,0:T(8,128)}) %reduce-scatter.8.cloned.1.call-update) | async-done | bytes 32784 | tf_op jit(solution)/shard_map/reduce_scatter | solution.py:78
  1174.1 61.9 %psum.47 = f32[32,32]{1,0:T(8,128)S(1)} all-reduce(f32[32,32]{1,0:T(8,128)S(1)} %fusion.61), channel_id=1, replica_groups=mesh['rhs'=2,'row'=8,'col'=2] {'row','col'}, use_global_device_ids=true, to_apply=%region_19.22 | all-reduce | flops 1024 | bytes 8192 | tf_op jit(solution)/shard_map/psum | solution.py:84
  1236.2 2.9 cholesky.133
  1240.4 2.4 custom-call.15
  1244.1 1.6 convolution_subtract_fusion
  (1010 shorter events, 447.0 us)
Async XLA Ops:
  7.2 302.8 %reduce-scatter.4.cloned.1.call-start = ((), (), s32[]{:S(2)}) async-start(), calls=%async_computation.3 | async-start | bytes 98304 | tf_op jit(solution)/shard_map/reduce_scatter | solution.py:78
  41.7 159.9 %copy-start = (s32[32,256]{1,0:T(8,128)S(1)}, s32[32,256]{1,0:T(8,128)}, u32[]{:S(2)}) copy-start(s32[32,256]{1,0:T(8,128)} %param.20) | copy-start | bytes 98308
  41.7 159.9 %copy-start.1 = (f32[256]{0:T(256)S(1)}, f32[256]{0:T(256)}, u32[]{:S(2)}) copy-start(f32[256]{0:T(256)} %param.21) | copy-start | bytes 3076
  41.8 159.9 %copy-start.2 = (f32[32]{0:T(128)S(1)}, f32[32]{0:T(128)}, u32[]{:S(2)}) copy-start(f32[32]{0:T(128)} %param.22) | copy-start | bytes 388
  201.6 543.5 %reduce-scatter.6.cloned.1.call-start = ((), (), s32[]{:S(2)}) async-start(), calls=%async_computation.4 | async-start | bytes 98304 | tf_op jit(solution)/shard_map/reduce_scatter | solution.py:78
  636.8 536.4 %reduce-scatter.8.cloned.1.call-start = ((), (), s32[]{:S(2)}) async-start(), calls=%async_computation.5 | async-start | bytes 98304 | tf_op jit(solution)/shard_map/reduce_scatter | solution.py:78
Sparse Core Ops, SparseCore 0:
  201.7 108.1 reduce-scatter.3
  636.9 108.1 reduce-scatter.5
  1065.0 108.0 reduce-scatter.7
where the time goes:
time: 1260 us; the launch traced here: 1250 us
  local copies, waits for them, and re-layouts  439 us (35%)
  blocking collectives  394 us (31%)
  waiting for transfers between devices  317 us (25%)
  other arithmetic  58.2 us (5%)
  matrix products  27.6 us (2%)
  between operations  14.7 us (1%)
    gather x864, local copies, waits for them, and re-layouts  417 us
    reduce_scatter x3, waiting for transfers between devices, per_device(): lax.psum_scatter(partial_sum.reshape(sketch, col_devices * rows_dev), 'co...  317 us
    psum x2, blocking collectives, per_device(): curvature = lax.psum(gram_of(direction, image), ('row', 'col'))  124 us
    psum x2, blocking collectives, per_device(): norm_next = lax.psum(gram_of(residual, residual), ('row', 'col'))  115 us
    all_gather x3, blocking collectives, per_device(): gathered = lax.all_gather(outgoing, 'row', axis=1, tiled=True)  93.3 us
    psum x1, blocking collectives, per_device(): norm_now = lax.psum(gram_of(residual, residual), ('row', 'col'))  61.9 us
  transfers between devices with their start and end apart: 3, of which 3 were waited for; matrix products, arithmetic and copies ran while one was open for 1% of the time, Pallas kernels for 0%

commit v1 on v0

v1 whole, which is shorter than its diff:
```python
import functools

import jax
import jax.numpy as jnp
from jax import lax
from jax.experimental import pallas as pl
from jax.experimental.pallas import tpu as pltpu
from jax.sharding import PartitionSpec as P

ITERS = 3
LANES = 128
PIVOTS = 8
F32 = jnp.float32
BF16 = jnp.bfloat16
VMEM_BYTES = 60 * 1024 * 1024

VMEM = pl.BlockSpec(memory_space=pltpu.VMEM)
SMEM = pl.BlockSpec(memory_space=pltpu.SMEM)
ANY = pl.BlockSpec(memory_space=pl.ANY)
PARAMS = pltpu.CompilerParams(vmem_limit_bytes=VMEM_BYTES)


def mul(left, right):
    return jnp.dot(left, right, precision=lax.Precision.HIGHEST, preferred_element_type=F32)


def mul_t(left, right):
    return lax.dot_general(
        left,
        right,
        (((1,), (1,)), ((), ())),
        precision=lax.Precision.HIGHEST,
        preferred_element_type=F32,
    )


def widen(matrix):
    rows, columns = matrix.shape
    return jnp.concatenate([matrix, jnp.zeros((rows, LANES - columns), F32)], axis=1)


def solve_wide(matrix, target):
    size = matrix.shape[0]
    row_ids = lax.broadcasted_iota(jnp.int32, (size, LANES), 0)
    lane_ids = lax.broadcasted_iota(jnp.int32, (size, LANES), 1)
    work = jnp.where(lane_ids < size, matrix, pltpu.roll(target, size, 1))
    for base in range(0, size, PIVOTS):
        columns = [
            jnp.broadcast_to(work[:, base + i : base + i + 1], (size, LANES))
            for i in range(PIVOTS)
        ]
        for i in range(PIVOTS):
            pivot = base + i
            here = row_ids == pivot
            inverse = 1.0 / columns[i][pivot : pivot + 1, :]
            row = work[pivot : pivot + 1, :] * inverse
            work = jnp.where(here, row, work - columns[i] * row)
            for later in range(i + 1, PIVOTS):
                entry = columns[later][pivot : pivot + 1, :] * inverse
                columns[later] = jnp.where(here, entry, columns[later] - columns[i] * entry)
    return pltpu.roll(work, LANES - size, 1)


def dense_kernel(
    rows_dev, col_devices, row_devices,
    place_ref, count_ref, rows_ref, cols_ref, tiles_ref, out_ref, total,
):
    tile = tiles_ref.shape[1]
    blocks = rows_dev // tile
    row_place = place_ref[0]
    col_place = place_ref[1]
    col_blocks, row_blocks = total.shape[:2]

    def clear(index, carry):
        for b in range(row_blocks):
            total[index, b] = jnp.zeros((tile, tile), F32)
        return carry

    lax.fori_loop(0, col_blocks, clear, 0)

    def add(slot, carry):
        row = rows_ref[slot]
        column = cols_ref[slot]
        side = lax.rem(row // blocks + col_devices - col_place, col_devices)
        row_at = side * blocks + lax.rem(row, blocks)
        owner = column // (blocks * col_devices)
        step = lax.rem(row_place + row_devices - owner, row_devices)
        column_at = step * blocks + lax.rem(column, blocks)
        total[column_at, row_at] = total[column_at, row_at] + tiles_ref[slot].astype(F32)
        return carry

    lax.fori_loop(0, count_ref[0], add, 0)

    def split(index, carry):
        start = pl.multiple_of(index * tile, tile)
        for b in range(row_blocks):
            value = total[index, b].T
            high = value.astype(BF16)
            low = (value - high.astype(F32)).astype(BF16)
            out_ref[0, pl.ds(start, tile), pl.ds(b * tile, tile)] = high
            out_ref[1, pl.ds(start, tile), pl.ds(b * tile, tile)] = low
        return carry

    lax.fori_loop(0, col_blocks, split, 0)


def apply_dense(directions, matrix):
    width = directions[0].shape[1]
    total = None
    for k, direction in enumerate(directions):
        rounded = direction.astype(BF16)
        for part in range(2):
            term = jnp.dot(
                rounded,
                matrix[part, k * width : (k + 1) * width, :],
                preferred_element_type=F32,
            )
            total = term if total is None else total + term
    return total


def first_kernel(pieces, *refs):
    blocks = refs[: pieces + 1]
    dense_ref, out_ref, state_ref, matrix, sem = refs[pieces + 1 :]
    copy = pltpu.make_async_copy(dense_ref, matrix, sem)
    copy.start()
    values = [ref[...] for ref in blocks]
    for k, value in enumerate(values):
        state_ref[k] = value
    half = mul_t(values[0], values[0])
    for value in values[1:pieces]:
        half = half + mul_t(value, value)
    rows = 2 * values[0].shape[1]
    out_ref[:, rows:] = widen(half)
    copy.wait()
    out_ref[:, :rows] = apply_dense(values[:pieces], matrix)


def image_kernel(first, mine_ref, other_ref, direction_ref, residual_ref, *outs):
    out_ref, far_ref = outs[:2]
    last = direction_ref.shape[0] - 1
    width = direction_ref.shape[2]
    near = mine_ref[:, :width] + other_ref[:, width : 2 * width]
    far = mine_ref[:, width : 2 * width] + other_ref[:, :width]
    far_ref[...] = far
    out_ref[:, :width] = near
    if first:
        outs[2][...] = mine_ref[:, 2 * width :] + other_ref[:, 2 * width :]
    image = jnp.concatenate([near, far], axis=1)
    direction = jnp.concatenate([direction_ref[0], direction_ref[last]], axis=1)
    curvature = 0.5 * (mul_t(image, direction) + mul_t(direction, image))
    residual = jnp.concatenate([residual_ref[0], residual_ref[last]], axis=1)
    size = curvature.shape[0]
    grams = [
        curvature,
        mul_t(image, residual),
        mul_t(image, image),
        jnp.zeros((size, LANES - 3 * size), F32),
    ]
    out_ref[:, width:] = jnp.concatenate(grams, axis=1)


def inverse_kernel(norm_ref, out_ref):
    size = norm_ref.shape[0]
    norm = norm_ref[...]
    small = norm[:, :size]
    norm = widen(0.5 * (small + small.T))
    unit = lax.broadcasted_iota(jnp.int32, norm.shape, 0) == lax.broadcasted_iota(
        jnp.int32, norm.shape, 1
    )
    out_ref[...] = solve_wide(norm, jnp.where(unit, 1.0, 0.0))


def in_order(place_ref, parts, held):
    pieces = len(parts)
    for k, part in enumerate(parts):
        held[k] = part
    total = None
    for device in range(pieces):
        value = held[lax.rem(place_ref[0] + (pieces - device), pieces)]
        total = value if total is None else total + value
    return total


def step_kernel(pieces, with_solution, place_ref, *refs):
    images = refs[:pieces]
    refs = refs[pieces:]
    far_ref, direction_ref, residual_ref, norm_ref, inverse_ref, dense_ref = refs[:6]
    refs = refs[6:]
    if with_solution:
        solution_ref, refs = refs[0], refs[1:]
    out_ref, new_direction, new_residual, new_norm, new_solution, matrix, held, sem = refs
    copy = pltpu.make_async_copy(dense_ref, matrix, sem)
    copy.start()
    size, width = far_ref.shape
    grams = in_order(place_ref, [ref[:, width:] for ref in images], held)
    norm = norm_ref[...]
    alpha = solve_wide(grams, norm)[:, :size]
    alpha_t = alpha.T
    image_residual = pltpu.roll(grams, LANES - size, 1)[:, :size]
    image_image = pltpu.roll(grams, LANES - 2 * size, 1)[:, :size]
    cross = mul(alpha_t, image_residual)
    next_norm = norm[:, :size] - (cross + cross.T) + mul(alpha_t, mul(image_image, alpha))
    new_norm[...] = widen(next_norm)
    beta_t = mul(next_norm, inverse_ref[:, :size])
    step = mul(alpha_t, direction_ref[0])
    new_solution[...] = solution_ref[...] + step if with_solution else step
    directions = []
    for k in range(pieces + 1):
        image = images[k][:, :width] if k < pieces else far_ref[...]
        residual = residual_ref[k] - mul(alpha_t, image)
        direction = residual + mul(beta_t, direction_ref[k])
        new_residual[k] = residual
        new_direction[k] = direction
        directions.append(direction)
    copy.wait()
    out_ref[...] = apply_dense(directions[:pieces], matrix)


def last_image_kernel(mine_ref, other_ref, direction_ref, near_ref, gram_ref):
    last = direction_ref.shape[0] - 1
    width = direction_ref.shape[2]
    near = mine_ref[:, :width] + other_ref[:, width : 2 * width]
    far = mine_ref[:, width : 2 * width] + other_ref[:, :width]
    near_ref[...] = near
    image = jnp.concatenate([near, far], axis=1)
    direction = jnp.concatenate([direction_ref[0], direction_ref[last]], axis=1)
    gram_ref[...] = widen(0.5 * (mul_t(image, direction) + mul_t(direction, image)))


def last_kernel(pieces, place_ref, *refs):
    parts = refs[:pieces]
    image_ref, direction_ref, residual_ref, norm_ref, solution_ref = refs[pieces : pieces + 5]
    new_solution, new_residual, held = refs[pieces + 5 :]
    size = image_ref.shape[0]
    curvature = in_order(place_ref, [ref[...] for ref in parts], held)
    alpha_t = solve_wide(curvature, norm_ref[...])[:, :size].T
    new_solution[...] = solution_ref[...] + mul(alpha_t, direction_ref[0])
    new_residual[...] = residual_ref[0] - mul(alpha_t, image_ref[...])


def shape(*dims, dtype=F32):
    return jax.ShapeDtypeStruct(dims, dtype)


def per_device(tiles, tile_rows, tile_cols, tile_count, signs, vertex_weight, column_scale):
    sketch, rows_dev = signs.shape
    tile = tiles.shape[1]
    pieces = lax.axis_size("row")
    col_devices = lax.axis_size("col")
    group = col_devices * rows_dev
    depth = pieces * rows_dev
    place = jnp.stack([lax.axis_index("row"), lax.axis_index("col")]).astype(jnp.int32)

    def around(value):
        received = [
            lax.ppermute(value, "row", [(i, (i + k) % pieces) for i in range(pieces)])
            for k in range(1, pieces)
        ]
        return [value] + received

    def across(value):
        return lax.ppermute(
            value, "col", [(i, (i + 1) % col_devices) for i in range(col_devices)]
        )

    right_side = signs.astype(F32) * vertex_weight[None, :] * column_scale[:, None]
    blocks = around(right_side) + [across(right_side)]

    dense = pl.pallas_call(
        functools.partial(dense_kernel, rows_dev, col_devices, pieces),
        out_shape=shape(2, depth, group, dtype=BF16),
        in_specs=[SMEM, SMEM, SMEM, SMEM, VMEM],
        out_specs=VMEM,
        scratch_shapes=[pltpu.VMEM((depth // tile, group // tile, tile, tile), F32)],
        compiler_params=PARAMS,
        cost_estimate=pl.CostEstimate(
            flops=4 * tiles.size, bytes_accessed=4 * tiles.size, transcendentals=0
        ),
        name="dense",
    )(place, tile_count, tile_rows, tile_cols, tiles)

    matrix_scratch = [pltpu.VMEM((2, depth, group), BF16)]
    state = shape(pieces + 1, sketch, rows_dev)
    small = shape(sketch, LANES)
    piece = shape(sketch, rows_dev)

    partial_sum, direction = pl.pallas_call(
        functools.partial(first_kernel, pieces),
        out_shape=(shape(sketch, group + LANES), state),
        in_specs=[VMEM] * (pieces + 1) + [ANY],
        out_specs=(VMEM, VMEM),
        scratch_shapes=matrix_scratch + [pltpu.SemaphoreType.DMA],
        compiler_params=PARAMS,
        name="first",
    )(*blocks, dense)
    residual = direction
    norm = None
    solution = None
    for iteration in range(ITERS):
        other = across(partial_sum)
        if iteration == ITERS - 1:
            break
        outs = pl.pallas_call(
            functools.partial(image_kernel, iteration == 0),
            out_shape=(shape(sketch, rows_dev + LANES), piece) + ((small,) if iteration == 0 else ()),
            in_specs=[VMEM] * 4,
            out_specs=(VMEM,) * (3 if iteration == 0 else 2),
            compiler_params=PARAMS,
            name="image",
        )(partial_sum, other, direction, residual)
        image, far = outs[:2]
        if iteration == 0:
            norm = outs[2]
        images = around(image)
        inverse = pl.pallas_call(
            inverse_kernel,
            out_shape=small,
            in_specs=[VMEM],
            out_specs=VMEM,
            compiler_params=PARAMS,
            name="inverse",
        )(norm)
        given = (solution,) if iteration else ()
        partial_sum, direction, residual, norm, solution = pl.pallas_call(
            functools.partial(step_kernel, pieces, iteration > 0),
            out_shape=(shape(sketch, group), state, state, small, piece),
            in_specs=[SMEM] + [VMEM] * (pieces + 5) + [ANY] + [VMEM] * len(given),
            out_specs=(VMEM,) * 5,
            scratch_shapes=matrix_scratch
            + [pltpu.VMEM((pieces, sketch, LANES), F32), pltpu.SemaphoreType.DMA],
            compiler_params=PARAMS,
            name="step",
        )(place, *images, far, direction, residual, norm, inverse, dense, *given)
    image, gram = pl.pallas_call(
        last_image_kernel,
        out_shape=(piece, small),
        in_specs=[VMEM] * 3,
        out_specs=(VMEM, VMEM),
        compiler_params=PARAMS,
        name="last_image",
    )(partial_sum, other, direction)
    return pl.pallas_call(
        functools.partial(last_kernel, pieces),
        out_shape=(piece, piece),
        in_specs=[SMEM] + [VMEM] * (pieces + 5),
        out_specs=(VMEM, VMEM),
        scratch_shapes=[pltpu.VMEM((pieces, sketch, LANES), F32)],
        compiler_params=PARAMS,
        name="last",
    )(place, *around(gram), image, direction, residual, norm, solution)


def solution(mesh):
    return jax.shard_map(
        per_device,
        mesh=mesh,
        in_specs=(
            P(("row", "col"), None, None),
            P(("row", "col")),
            P(("row", "col")),
            P(("row", "col")),
            P("rhs", ("row", "col")),
            P(("row", "col")),
            P("rhs"),
        ),
        out_specs=(P("rhs", ("row", "col")), P("rhs", ("row", "col"))),
        check_vma=False,
    )
```

time: 1260 us -> 103 us (0.08)
  local copies, waits for them, and re-layouts: 439 us -> 4.85 us
  blocking collectives: 394 us -> 0 us
  waiting for transfers between devices: 317 us -> 17.5 us
  other arithmetic: 58.2 us -> 1.46 us
  Pallas kernels: 0 us -> 38.9 us
  starting transfers between devices: 0.12 us -> 38.1 us
  matrix products: 27.6 us -> 0 us
  between operations: 14.7 us -> 1.58 us
    gather x882 -> x0, local copies, waits for them, and re-layouts: 436 us -> none
    reduce_scatter x3 -> x0, waiting for transfers between devices: 317 us -> none  [per_device(): lax.psum_scatter(partial_sum.reshape(sketch, col_devices * rows_dev), 'co...]
    psum x5 -> x0, blocking collectives: 301 us -> none  [the longest x2 124 us: per_device(): curvature = lax.psum(gram_of(direction, image), ('row', 'col'))]
    all_gather x3 -> x0, blocking collectives: 93.3 us -> none  [per_device(): gathered = lax.all_gather(outgoing, 'row', axis=1, tiled=True)]
    pallas_call x0 -> x10, Pallas kernels: none -> 38.9 us  [the longest x2 10.3 us: per_device(): pl.pallas_call(functools.partial(step_kernel, pieces, iteration > 0), out...]
    ppermute x0 -> x32, starting transfers between devices: none -> 38.1 us  [the longest x28 37.4 us: around(): lax.ppermute(value, 'row', [(i, (i + k) % pieces) for i in range(pieces)])]
    another operation x25 -> x1, other arithmetic: 33.4 us -> 0.61 us  [per_device(): jnp.stack([lax.axis_index('row'), lax.axis_index('col')]).astype(jnp.int32)]
    dot_general x23 -> x0, matrix products: 25.8 us -> none  [the longest x9 17 us: add_rows(): jnp.einsum('gab,sgb->sga', tile_group, picked, preferred_element_type=jnp...]
  transfers between devices with their start and end apart: 3 -> 32, of which waited for: 3 -> 12; matrix products, arithmetic and copies ran while one was open for 1% -> 1% of each run, Pallas kernels for 0% -> 14%
where the time goes in v1:
time: 103 us; the launch traced here: 102 us
  Pallas kernels  38.9 us (38%)
  starting transfers between devices  38.1 us (37%)
  waiting for transfers between devices  17.5 us (17%)
  local copies, waits for them, and re-layouts  4.85 us (5%)
  between operations  1.58 us (2%)
  other arithmetic  1.46 us (1%)
    ppermute x28, starting transfers between devices, around(): lax.ppermute(value, 'row', [(i, (i + k) % pieces) for i in range(pieces)])  37.4 us
    ppermute x28, waiting for transfers between devices, around(): lax.ppermute(value, 'row', [(i, (i + k) % pieces) for i in range(pieces)])  13.1 us
    pallas_call x2, Pallas kernels, per_device(): pl.pallas_call(functools.partial(step_kernel, pieces, iteration > 0), out...  10.3 us
    pallas_call x1, Pallas kernels, per_device(): pl.pallas_call(functools.partial(dense_kernel, rows_dev, col_devices, pie...  10.2 us
    unnamed x66, local copies, waits for them, and re-layouts  4.85 us
    pallas_call x1, Pallas kernels, per_device(): pl.pallas_call(functools.partial(first_kernel, pieces), out_shape=(shape(...  4.64 us
    pallas_call x2, Pallas kernels, per_device(): pl.pallas_call(inverse_kernel, out_shape=small, in_specs=[VMEM], out_spec...  4.56 us
    ppermute x4, waiting for transfers between devices, across(): lax.ppermute(value, 'col', [(i, (i + 1) % col_devices) for i in range(col...  4.38 us
  transfers between devices with their start and end apart: 32, of which 12 were waited for; matrix products, arithmetic and copies ran while one was open for 1% of the time, Pallas kernels for 14%

profile of v1, /device:TPU:0, one launch (start us, length us, event | category | flops | bytes accessed | tf_op | source)
XLA Modules:
  0.0 102.4 jit_solution(14264817480404718470)
XLA Ops:
  0.6 0.8 multiply_multiply_fusion.refs_0_
  1.5 0.5 collective-permute-start.7
  1.9 5.6 %collective-permute-start.6 = (f32[32,256]{1,0:T(8,128)S(1)}, f32[32,256]{1,0:T(8,128)S(1)}, u32[]{:S(2)}, u32[]{:S(2)}) collective-permute-start(f32[32,256]{1,0:T(8,128)S(1)} %multiply_multiply_fusion.refs_0_), channel_id=1, source_target_pairs={{0,14},{2,0},{4,2},{6,4},{8,6},{10,8},{12,10},{14,12},{1,15},{3,1}... | collective-permute-start | bytes 98312 | tf_op jit(solution)/shard_map/ppermute | solution.py:257
  7.6 0.4 collective-permute-start.5
  8.0 0.0 collective-permute-start.4
  8.0 3.0 %collective-permute-start.3 = (f32[32,256]{1,0:T(8,128)S(1)}, f32[32,256]{1,0:T(8,128)S(1)}, u32[]{:S(2)}, u32[]{:S(2)}) collective-permute-start(f32[32,256]{1,0:T(8,128)S(1)} %multiply_multiply_fusion.refs_0_), channel_id=1, source_target_pairs={{0,8},{2,10},{4,12},{6,14},{8,0},{10,2},{12,4},{14,6},{1,9},{3,11}... | collective-permute-start | bytes 98312 | tf_op jit(solution)/shard_map/ppermute | solution.py:257
  11.0 0.0 collective-permute-done.6.refs_7_
  11.0 1.8 %collective-permute-start.1 = (f32[32,256]{1,0:T(8,128)S(1)}, f32[32,256]{1,0:T(8,128)S(1)}, u32[]{:S(2)}, u32[]{:S(2)}) collective-permute-start(f32[32,256]{1,0:T(8,128)S(1)} %multiply_multiply_fusion.refs_0_), channel_id=1, source_target_pairs={{0,4},{2,6},{4,8},{6,10},{8,12},{10,14},{12,0},{14,2},{1,5},{3,7},... | collective-permute-start | bytes 98312 | tf_op jit(solution)/shard_map/ppermute | solution.py:257
  12.9 0.0 collective-permute-done.5.refs_6_
  12.9 1.1 %collective-permute-start = (f32[32,256]{1,0:T(8,128)S(1)}, f32[32,256]{1,0:T(8,128)S(1)}, u32[]{:S(2)}, u32[]{:S(2)}) collective-permute-start(f32[32,256]{1,0:T(8,128)S(1)} %multiply_multiply_fusion.refs_0_), channel_id=1, source_target_pairs={{0,2},{2,4},{4,6},{6,8},{8,10},{10,12},{12,14},{14,0},{1,3},{3,5},... | collective-permute-start | bytes 98312 | tf_op jit(solution)/shard_map/ppermute | solution.py:257
  14.0 0.6 pad_add_fusion.place_ref
  15.3 10.2 %dense.1.refs_9_.refs_13_ = bf16[2,2048,512]{2,1,0:T(8,128)(2,1)} custom-call(s32[2]{0:T(128)} %pad_add_fusion.place_ref, s32[1]{0:T(128)S(6)} %copy.9.count_ref, s32[130]{0:T(256)} %rows_ref.1, s32[130]{0:T(256)} %cols_ref.1, bf16[130,128,128]{2,1,0:T(8,128)(2,1)} %tiles_ref.1), custom_call_target="tpu_custom_call" | custom-call | flops 8519680 | bytes 8519680 | tf_op jit(solution)/shard_map/dense/pallas_call | solution.py:270
  25.6 0.5 copy-done.21
  26.1 0.0 copy-done.22
  26.1 0.0 copy-done.23
  26.1 0.0 copy-done.24
  26.2 0.6 copy-done.25
  26.8 4.6 %first.1 = (f32[32,640]{1,0:T(8,128)}, f32[9,32,256]{2,1,0:T(8,128)}) custom-call(f32[32,256]{1,0:T(8,128)} %copy-done, f32[32,256]{1,0:T(8,128)} %copy-done.25, f32[32,256]{1,0:T(8,128)} %copy-done.24, f32[32,256]{1,0:T(8,128)} %copy-done.23, f32[32,256]{1,0:T(8,128)} %copy-done.22, f32[32,256]{1,0:T(8,128)} %copy-done.21, f32[32,256]{1,0:T(8,128)} %copy-done.20, ...), custom_call_target="tpu_custom_call" | custom-call | tf_op jit(solution)/shard_map/first/pallas_call | solution.py:288
  31.4 0.1 collective-permute-start.8
  31.5 1.5 %collective-permute-done.8.other_ref = f32[32,640]{1,0:T(8,128)S(1)} collective-permute-done((f32[32,640]{1,0:T(8,128)}, f32[32,640]{1,0:T(8,128)S(1)}, u32[]{:S(2)}, u32[]{:S(2)}) %collective-permute-start.8) | collective-permute-done | bytes 81952 | tf_op jit(solution)/shard_map/ppermute | solution.py:263
  33.0 0.6 copy-done.1
  33.6 2.2 %image.2 = (f32[32,384]{1,0:T(8,128)}, f32[32,256]{1,0:T(8,128)}, f32[32,128]{1,0:T(8,128)}) custom-call(f32[32,640]{1,0:T(8,128)} %get-tuple-element.21.mine_ref, f32[32,640]{1,0:T(8,128)} %copy-done.1, f32[9,32,256]{2,1,0:T(8,128)} %get-tuple-element.22.direction_ref.residual_ref.refs_9_.refs_10_, ...), custom_call_target="tpu_custom_call" | custom-call | tf_op jit(solution)/shard_map/image/pallas_call | solution.py:304
  35.8 1.8 %collective-permute-start.15 = (f32[32,384]{1,0:T(8,128)}, f32[32,384]{1,0:T(8,128)S(1)}, u32[]{:S(2)}, u32[]{:S(2)}) collective-permute-start(f32[32,384]{1,0:T(8,128)} %get-tuple-element.23.refs_0_), channel_id=1, source_target_pairs={{0,14},{2,0},{4,2},{6,4},{8,6},{10,8},{12,10},{14,12},{1,15},{3,1}... | collective-permute-start | bytes 147464 | tf_op jit(solution)/shard_map/ppermute | solution.py:257
  37.6 1.5 %collective-permute-start.14 = (f32[32,384]{1,0:T(8,128)}, f32[32,384]{1,0:T(8,128)S(1)}, u32[]{:S(2)}, u32[]{:S(2)}) collective-permute-start(f32[32,384]{1,0:T(8,128)} %get-tuple-element.23.refs_0_), channel_id=1, source_target_pairs={{0,12},{2,14},{4,0},{6,2},{8,4},{10,6},{12,8},{14,10},{1,13},{3,15... | collective-permute-start | bytes 147464 | tf_op jit(solution)/shard_map/ppermute | solution.py:257
  39.0 1.6 %collective-permute-start.12 = (f32[32,384]{1,0:T(8,128)}, f32[32,384]{1,0:T(8,128)S(1)}, u32[]{:S(2)}, u32[]{:S(2)}) collective-permute-start(f32[32,384]{1,0:T(8,128)} %get-tuple-element.23.refs_0_), channel_id=1, source_target_pairs={{0,8},{2,10},{4,12},{6,14},{8,0},{10,2},{12,4},{14,6},{1,9},{3,11}... | collective-permute-start | bytes 147464 | tf_op jit(solution)/shard_map/ppermute | solution.py:257
  40.6 1.4 %collective-permute-start.11 = (f32[32,384]{1,0:T(8,128)}, f32[32,384]{1,0:T(8,128)S(1)}, u32[]{:S(2)}, u32[]{:S(2)}) collective-permute-start(f32[32,384]{1,0:T(8,128)} %get-tuple-element.23.refs_0_), channel_id=1, source_target_pairs={{0,6},{2,8},{4,10},{6,12},{8,14},{10,0},{12,2},{14,4},{1,7},{3,9},... | collective-permute-start | bytes 147464 | tf_op jit(solution)/shard_map/ppermute | solution.py:257
  42.0 2.9 %collective-permute-start.10 = (f32[32,384]{1,0:T(8,128)}, f32[32,384]{1,0:T(8,128)S(1)}, u32[]{:S(2)}, u32[]{:S(2)}) collective-permute-start(f32[32,384]{1,0:T(8,128)} %get-tuple-element.23.refs_0_), channel_id=1, source_target_pairs={{0,4},{2,6},{4,8},{6,10},{8,12},{10,14},{12,0},{14,2},{1,5},{3,7},... | collective-permute-start | bytes 147464 | tf_op jit(solution)/shard_map/ppermute | solution.py:257
  44.9 2.3 %inverse.2.refs_12_ = f32[32,128]{1,0:T(8,128)} custom-call(f32[32,128]{1,0:T(8,128)} %get-tuple-element.25.norm_ref.refs_11_), custom_call_target="tpu_custom_call" | custom-call | tf_op jit(solution)/shard_map/inverse/pallas_call | solution.py:316
  47.2 0.1 collective-permute-done.12.refs_4_
  47.3 2.9 %collective-permute-done.11.refs_3_ = f32[32,384]{1,0:T(8,128)S(1)} collective-permute-done((f32[32,384]{1,0:T(8,128)}, f32[32,384]{1,0:T(8,128)S(1)}, u32[]{:S(2)}, u32[]{:S(2)}) %collective-permute-start.11) | collective-permute-done | bytes 49184 | tf_op jit(solution)/shard_map/ppermute | solution.py:257
  50.2 1.7 %collective-permute-done.9.refs_1_ = f32[32,384]{1,0:T(8,128)S(1)} collective-permute-done((f32[32,384]{1,0:T(8,128)}, f32[32,384]{1,0:T(8,128)S(1)}, u32[]{:S(2)}, u32[]{:S(2)}) %collective-permute-start.9) | collective-permute-done | bytes 49184 | tf_op jit(solution)/shard_map/ppermute | solution.py:257
  51.9 0.6 copy-done.17
  52.5 5.0 %step.2 = (f32[32,512]{1,0:T(8,128)}, f32[9,32,256]{2,1,0:T(8,128)}, f32[9,32,256]{2,1,0:T(8,128)}, f32[32,128]{1,0:T(8,128)}, f32[32,256]{1,0:T(8,128)}) custom-call(s32[2]{0:T(128)} %pad_add_fusion.place_ref, f32[32,384]{1,0:T(8,128)} %get-tuple-element.23.refs_0_, f32[32,384]{1,0:T(8,128)} %copy-done.17, f32[32,384]{1,0:T(8,128)} %copy-done.15, ...), custom_call_target="tpu_custom_call" | custom-call | tf_op jit(solution)/shard_map/step/pallas_call | solution.py:325
  57.5 0.1 collective-permute-start.16
  57.6 1.5 %collective-permute-done.16.other_ref = f32[32,512]{1,0:T(8,128)S(1)} collective-permute-done((f32[32,512]{1,0:T(8,128)}, f32[32,512]{1,0:T(8,128)S(1)}, u32[]{:S(2)}, u32[]{:S(2)}) %collective-permute-start.16) | collective-permute-done | bytes 65568 | tf_op jit(solution)/shard_map/ppermute | solution.py:263
  59.0 0.6 copy-done.3
  59.6 2.2 %image.3 = (f32[32,384]{1,0:T(8,128)}, f32[32,256]{1,0:T(8,128)}) custom-call(f32[32,512]{1,0:T(8,128)} %get-tuple-element.26.mine_ref, f32[32,512]{1,0:T(8,128)} %copy-done.3, f32[9,32,256]{2,1,0:T(8,128)} %get-tuple-element.27.direction_ref.refs_9_, f32[9,32,256]{2,1,0:T(8,128)} %get-tuple-element.28.residual_ref.refs_10_), custom_call_target="tpu_custom_call" | custom-call | tf_op jit(solution)/shard_map/image/pallas_call | solution.py:304
  61.8 0.1 collective-permute-start.23
  61.9 0.5 collective-permute-start.22
  62.4 1.2 %collective-permute-start.21 = (f32[32,384]{1,0:T(8,128)}, f32[32,384]{1,0:T(8,128)S(1)}, u32[]{:S(2)}, u32[]{:S(2)}) collective-permute-start(f32[32,384]{1,0:T(8,128)} %get-tuple-element.29.refs_0_), channel_id=1, source_target_pairs={{0,10},{2,12},{4,14},{6,0},{8,2},{10,4},{12,6},{14,8},{1,11},{3,13... | collective-permute-start | bytes 147464 | tf_op jit(solution)/shard_map/ppermute | solution.py:257
  63.6 2.6 %collective-permute-start.20 = (f32[32,384]{1,0:T(8,128)}, f32[32,384]{1,0:T(8,128)S(1)}, u32[]{:S(2)}, u32[]{:S(2)}) collective-permute-start(f32[32,384]{1,0:T(8,128)} %get-tuple-element.29.refs_0_), channel_id=1, source_target_pairs={{0,8},{2,10},{4,12},{6,14},{8,0},{10,2},{12,4},{14,6},{1,9},{3,11}... | collective-permute-start | bytes 147464 | tf_op jit(solution)/shard_map/ppermute | solution.py:257
  66.2 2.1 %collective-permute-start.18 = (f32[32,384]{1,0:T(8,128)}, f32[32,384]{1,0:T(8,128)S(1)}, u32[]{:S(2)}, u32[]{:S(2)}) collective-permute-start(f32[32,384]{1,0:T(8,128)} %get-tuple-element.29.refs_0_), channel_id=1, source_target_pairs={{0,4},{2,6},{4,8},{6,10},{8,12},{10,14},{12,0},{14,2},{1,5},{3,7},... | collective-permute-start | bytes 147464 | tf_op jit(solution)/shard_map/ppermute | solution.py:257
  68.3 1.4 %collective-permute-start.17 = (f32[32,384]{1,0:T(8,128)}, f32[32,384]{1,0:T(8,128)S(1)}, u32[]{:S(2)}, u32[]{:S(2)}) collective-permute-start(f32[32,384]{1,0:T(8,128)} %get-tuple-element.29.refs_0_), channel_id=1, source_target_pairs={{0,2},{2,4},{4,6},{6,8},{8,10},{10,12},{12,14},{14,0},{1,3},{3,5},... | collective-permute-start | bytes 147464 | tf_op jit(solution)/shard_map/ppermute | solution.py:257
  69.7 2.3 %inverse.3.refs_12_ = f32[32,128]{1,0:T(8,128)} custom-call(f32[32,128]{1,0:T(8,128)} %get-tuple-element.31.norm_ref.refs_11_), custom_call_target="tpu_custom_call" | custom-call | tf_op jit(solution)/shard_map/inverse/pallas_call | solution.py:316
  72.0 1.2 %collective-permute-done.20.refs_4_ = f32[32,384]{1,0:T(8,128)S(1)} collective-permute-done((f32[32,384]{1,0:T(8,128)}, f32[32,384]{1,0:T(8,128)S(1)}, u32[]{:S(2)}, u32[]{:S(2)}) %collective-permute-start.20) | collective-permute-done | bytes 49184 | tf_op jit(solution)/shard_map/ppermute | solution.py:257
  73.2 1.2 %collective-permute-done.19.refs_3_ = f32[32,384]{1,0:T(8,128)S(1)} collective-permute-done((f32[32,384]{1,0:T(8,128)}, f32[32,384]{1,0:T(8,128)S(1)}, u32[]{:S(2)}, u32[]{:S(2)}) %collective-permute-start.19) | collective-permute-done | bytes 49184 | tf_op jit(solution)/shard_map/ppermute | solution.py:257
  74.5 0.8 collective-permute-done.17.refs_1_
  75.3 0.6 copy-done.16
  75.9 5.3 %step.3 = (f32[32,512]{1,0:T(8,128)}, f32[9,32,256]{2,1,0:T(8,128)}, f32[9,32,256]{2,1,0:T(8,128)}, f32[32,128]{1,0:T(8,128)}, f32[32,256]{1,0:T(8,128)}) custom-call(s32[2]{0:T(128)} %pad_add_fusion.place_ref, f32[32,384]{1,0:T(8,128)} %get-tuple-element.29.refs_0_, f32[32,384]{1,0:T(8,128)} %copy-done.16, f32[32,384]{1,0:T(8,128)} %copy-done.14, ...), custom_call_target="tpu_custom_call" | custom-call | tf_op jit(solution)/shard_map/step/pallas_call | solution.py:325
  81.2 0.1 collective-permute-start.24
  81.3 1.5 %collective-permute-done.24.other_ref = f32[32,512]{1,0:T(8,128)S(1)} collective-permute-done((f32[32,512]{1,0:T(8,128)}, f32[32,512]{1,0:T(8,128)S(1)}, u32[]{:S(2)}, u32[]{:S(2)}) %collective-permute-start.24) | collective-permute-done | bytes 65568 | tf_op jit(solution)/shard_map/ppermute | solution.py:263
  82.7 0.6 copy-done.2
  83.3 1.9 %last_image.1 = (f32[32,256]{1,0:T(8,128)}, f32[32,128]{1,0:T(8,128)}) custom-call(f32[32,512]{1,0:T(8,128)} %get-tuple-element.33.mine_ref, f32[32,512]{1,0:T(8,128)} %copy-done.2, f32[9,32,256]{2,1,0:T(8,128)} %get-tuple-element.34.direction_ref.refs_9_), custom_call_target="tpu_custom_call" | custom-call | tf_op jit(solution)/shard_map/last_image/pallas_call | solution.py:335
  85.2 0.6 collective-permute-start.31
  85.8 2.0 %collective-permute-start.30 = (f32[32,128]{1,0:T(8,128)}, f32[32,128]{1,0:T(8,128)S(1)}, u32[]{:S(2)}, u32[]{:S(2)}) collective-permute-start(f32[32,128]{1,0:T(8,128)} %get-tuple-element.35.refs_0_), channel_id=1, source_target_pairs={{0,12},{2,14},{4,0},{6,2},{8,4},{10,6},{12,8},{14,10},{1,13},{3,15... | collective-permute-start | bytes 49160 | tf_op jit(solution)/shard_map/ppermute | solution.py:257
  87.8 2.9 %collective-permute-start.28 = (f32[32,128]{1,0:T(8,128)}, f32[32,128]{1,0:T(8,128)S(1)}, u32[]{:S(2)}, u32[]{:S(2)}) collective-permute-start(f32[32,128]{1,0:T(8,128)} %get-tuple-element.35.refs_0_), channel_id=1, source_target_pairs={{0,8},{2,10},{4,12},{6,14},{8,0},{10,2},{12,4},{14,6},{1,9},{3,11}... | collective-permute-start | bytes 49160 | tf_op jit(solution)/shard_map/ppermute | solution.py:257
  90.6 0.0 collective-permute-start.27
  90.7 1.5 %collective-permute-start.26 = (f32[32,128]{1,0:T(8,128)}, f32[32,128]{1,0:T(8,128)S(1)}, u32[]{:S(2)}, u32[]{:S(2)}) collective-permute-start(f32[32,128]{1,0:T(8,128)} %get-tuple-element.35.refs_0_), channel_id=1, source_target_pairs={{0,4},{2,6},{4,8},{6,10},{8,12},{10,14},{12,0},{14,2},{1,5},{3,7},... | collective-permute-start | bytes 49160 | tf_op jit(solution)/shard_map/ppermute | solution.py:257
  92.2 1.6 %collective-permute-start.25 = (f32[32,128]{1,0:T(8,128)}, f32[32,128]{1,0:T(8,128)S(1)}, u32[]{:S(2)}, u32[]{:S(2)}) collective-permute-start(f32[32,128]{1,0:T(8,128)} %get-tuple-element.35.refs_0_), channel_id=1, source_target_pairs={{0,2},{2,4},{4,6},{6,8},{8,10},{10,12},{12,14},{14,0},{1,3},{3,5},... | collective-permute-start | bytes 49160 | tf_op jit(solution)/shard_map/ppermute | solution.py:257
  93.7 2.6 %collective-permute-done.27.refs_3_ = f32[32,128]{1,0:T(8,128)S(1)} collective-permute-done((f32[32,128]{1,0:T(8,128)}, f32[32,128]{1,0:T(8,128)S(1)}, u32[]{:S(2)}, u32[]{:S(2)}) %collective-permute-start.27) | collective-permute-done | bytes 16416 | tf_op jit(solution)/shard_map/ppermute | solution.py:257
  96.4 0.1 collective-permute-done.26.refs_2_
  96.4 2.4 %collective-permute-done.25.refs_1_ = f32[32,128]{1,0:T(8,128)S(1)} collective-permute-done((f32[32,128]{1,0:T(8,128)}, f32[32,128]{1,0:T(8,128)S(1)}, u32[]{:S(2)}, u32[]{:S(2)}) %collective-permute-start.25) | collective-permute-done | bytes 16416 | tf_op jit(solution)/shard_map/ppermute | solution.py:257
  98.8 0.6 copy-done.32
  99.4 3.0 %last.1 = (f32[32,256]{1,0:T(8,128)}, f32[32,256]{1,0:T(8,128)}) custom-call(s32[2]{0:T(128)} %pad_add_fusion.place_ref, f32[32,128]{1,0:T(8,128)} %get-tuple-element.35.refs_0_, f32[32,128]{1,0:T(8,128)} %copy-done.32, f32[32,128]{1,0:T(8,128)} %copy-done.31, f32[32,128]{1,0:T(8,128)} %copy-done.30, f32[32,128]{1,0:T(8,128)} %copy-done.29, ...), custom_call_target="tpu_custom_call" | custom-call | tf_op jit(solution)/shard_map/last/pallas_call | solution.py:343
  (78 shorter events, 0.2 us)
Async XLA Ops:
  1.5 24.1 %copy-start = (f32[32,256]{1,0:T(8,128)}, f32[32,256]{1,0:T(8,128)S(1)}, u32[]{:S(2)}) copy-start(f32[32,256]{1,0:T(8,128)S(1)} %multiply_multiply_fusion.refs_0_) | copy-start | bytes 98308
  1.5 9.5 %collective-permute-start.7 = (f32[32,256]{1,0:T(8,128)S(1)}, f32[32,256]{1,0:T(8,128)S(1)}, u32[]{:S(2)}, u32[]{:S(2)}) collective-permute-start(f32[32,256]{1,0:T(8,128)S(1)} %multiply_multiply_fusion.refs_0_), channel_id=1, source_target_pairs={{0,1},{1,0},{2,3},{3,2},{4,5},{5,4},{6,7},{7,6},{8,9},{9,8},{10,11... | collective-permute-start | bytes 98312 | tf_op jit(solution)/shard_map/ppermute | solution.py:263
  1.9 9.1 %collective-permute-start.6 = (f32[32,256]{1,0:T(8,128)S(1)}, f32[32,256]{1,0:T(8,128)S(1)}, u32[]{:S(2)}, u32[]{:S(2)}) collective-permute-start(f32[32,256]{1,0:T(8,128)S(1)} %multiply_multiply_fusion.refs_0_), channel_id=1, source_target_pairs={{0,14},{2,0},{4,2},{6,4},{8,6},{10,8},{12,10},{14,12},{1,15},{3,1}... | collective-permute-start | bytes 98312 | tf_op jit(solution)/shard_map/ppermute | solution.py:257
  7.6 5.3 %collective-permute-start.5 = (f32[32,256]{1,0:T(8,128)S(1)}, f32[32,256]{1,0:T(8,128)S(1)}, u32[]{:S(2)}, u32[]{:S(2)}) collective-permute-start(f32[32,256]{1,0:T(8,128)S(1)} %multiply_multiply_fusion.refs_0_), channel_id=1, source_target_pairs={{0,12},{2,14},{4,0},{6,2},{8,4},{10,6},{12,8},{14,10},{1,13},{3,15... | collective-permute-start | bytes 98312 | tf_op jit(solution)/shard_map/ppermute | solution.py:257
  8.0 17.5 %collective-permute-start.4 = (f32[32,256]{1,0:T(8,128)S(1)}, f32[32,256]{1,0:T(8,128)S(1)}, u32[]{:S(2)}, u32[]{:S(2)}) collective-permute-start(f32[32,256]{1,0:T(8,128)S(1)} %multiply_multiply_fusion.refs_0_), channel_id=1, source_target_pairs={{0,10},{2,12},{4,14},{6,0},{8,2},{10,4},{12,6},{14,8},{1,11},{3,13... | collective-permute-start | bytes 98312 | tf_op jit(solution)/shard_map/ppermute | solution.py:257
  8.0 17.5 %collective-permute-start.3 = (f32[32,256]{1,0:T(8,128)S(1)}, f32[32,256]{1,0:T(8,128)S(1)}, u32[]{:S(2)}, u32[]{:S(2)}) collective-permute-start(f32[32,256]{1,0:T(8,128)S(1)} %multiply_multiply_fusion.refs_0_), channel_id=1, source_target_pairs={{0,8},{2,10},{4,12},{6,14},{8,0},{10,2},{12,4},{14,6},{1,9},{3,11}... | collective-permute-start | bytes 98312 | tf_op jit(solution)/shard_map/ppermute | solution.py:257
  11.0 14.6 %copy-start.18 = (f32[32,256]{1,0:T(8,128)}, f32[32,256]{1,0:T(8,128)S(1)}, u32[]{:S(2)}) copy-start(f32[32,256]{1,0:T(8,128)S(1)} %collective-permute-done.7.refs_8_) | copy-start | bytes 98308
  11.0 14.5 %collective-permute-start.2 = (f32[32,256]{1,0:T(8,128)S(1)}, f32[32,256]{1,0:T(8,128)S(1)}, u32[]{:S(2)}, u32[]{:S(2)}) collective-permute-start(f32[32,256]{1,0:T(8,128)S(1)} %multiply_multiply_fusion.refs_0_), channel_id=1, source_target_pairs={{0,6},{2,8},{4,10},{6,12},{8,14},{10,0},{12,2},{14,4},{1,7},{3,9},... | collective-permute-start | bytes 98312 | tf_op jit(solution)/shard_map/ppermute | solution.py:257
  11.0 14.6 %copy-start.19 = (f32[32,256]{1,0:T(8,128)}, f32[32,256]{1,0:T(8,128)S(1)}, u32[]{:S(2)}) copy-start(f32[32,256]{1,0:T(8,128)S(1)} %collective-permute-done.6.refs_7_) | copy-start | bytes 98308
  11.0 14.5 %collective-permute-start.1 = (f32[32,256]{1,0:T(8,128)S(1)}, f32[32,256]{1,0:T(8,128)S(1)}, u32[]{:S(2)}, u32[]{:S(2)}) collective-permute-start(f32[32,256]{1,0:T(8,128)S(1)} %multiply_multiply_fusion.refs_0_), channel_id=1, source_target_pairs={{0,4},{2,6},{4,8},{6,10},{8,12},{10,14},{12,0},{14,2},{1,5},{3,7},... | collective-permute-start | bytes 98312 | tf_op jit(solution)/shard_map/ppermute | solution.py:257
  12.9 12.7 %copy-start.20 = (f32[32,256]{1,0:T(8,128)}, f32[32,256]{1,0:T(8,128)S(1)}, u32[]{:S(2)}) copy-start(f32[32,256]{1,0:T(8,128)S(1)} %collective-permute-done.5.refs_6_) | copy-start | bytes 98308
  12.9 12.7 %collective-permute-start = (f32[32,256]{1,0:T(8,128)S(1)}, f32[32,256]{1,0:T(8,128)S(1)}, u32[]{:S(2)}, u32[]{:S(2)}) collective-permute-start(f32[32,256]{1,0:T(8,128)S(1)} %multiply_multiply_fusion.refs_0_), channel_id=1, source_target_pairs={{0,2},{2,4},{4,6},{6,8},{8,10},{10,12},{12,14},{14,0},{1,3},{3,5},... | collective-permute-start | bytes 98312 | tf_op jit(solution)/shard_map/ppermute | solution.py:257
  25.5 0.6 copy-start.21
  25.5 0.6 copy-start.22
  25.5 0.6 copy-start.23
  25.5 0.6 copy-start.24
  26.2 0.6 copy-start.25
  31.4 1.6 %collective-permute-start.8 = (f32[32,640]{1,0:T(8,128)}, f32[32,640]{1,0:T(8,128)S(1)}, u32[]{:S(2)}, u32[]{:S(2)}) collective-permute-start(f32[32,640]{1,0:T(8,128)} %get-tuple-element.21.mine_ref), channel_id=1, source_target_pairs={{0,1},{1,0},{2,3},{3,2},{4,5},{5,4},{6,7},{7,6},{8,9},{9,8},{10,11... | collective-permute-start | bytes 245768 | tf_op jit(solution)/shard_map/ppermute | solution.py:263
  33.0 0.6 copy-start.1
  35.8 6.2 %collective-permute-start.15 = (f32[32,384]{1,0:T(8,128)}, f32[32,384]{1,0:T(8,128)S(1)}, u32[]{:S(2)}, u32[]{:S(2)}) collective-permute-start(f32[32,384]{1,0:T(8,128)} %get-tuple-element.23.refs_0_), channel_id=1, source_target_pairs={{0,14},{2,0},{4,2},{6,4},{8,6},{10,8},{12,10},{14,12},{1,15},{3,1}... | collective-permute-start | bytes 147464 | tf_op jit(solution)/shard_map/ppermute | solution.py:257
  37.6 7.3 %collective-permute-start.14 = (f32[32,384]{1,0:T(8,128)}, f32[32,384]{1,0:T(8,128)S(1)}, u32[]{:S(2)}, u32[]{:S(2)}) collective-permute-start(f32[32,384]{1,0:T(8,128)} %get-tuple-element.23.refs_0_), channel_id=1, source_target_pairs={{0,12},{2,14},{4,0},{6,2},{8,4},{10,6},{12,8},{14,10},{1,13},{3,15... | collective-permute-start | bytes 147464 | tf_op jit(solution)/shard_map/ppermute | solution.py:257
  39.0 8.1 %collective-permute-start.13 = (f32[32,384]{1,0:T(8,128)}, f32[32,384]{1,0:T(8,128)S(1)}, u32[]{:S(2)}, u32[]{:S(2)}) collective-permute-start(f32[32,384]{1,0:T(8,128)} %get-tuple-element.23.refs_0_), channel_id=1, source_target_pairs={{0,10},{2,12},{4,14},{6,0},{8,2},{10,4},{12,6},{14,8},{1,11},{3,13... | collective-permute-start | bytes 147464 | tf_op jit(solution)/shard_map/ppermute | solution.py:257
  39.0 8.3 %collective-permute-start.12 = (f32[32,384]{1,0:T(8,128)}, f32[32,384]{1,0:T(8,128)S(1)}, u32[]{:S(2)}, u32[]{:S(2)}) collective-permute-start(f32[32,384]{1,0:T(8,128)} %get-tuple-element.23.refs_0_), channel_id=1, source_target_pairs={{0,8},{2,10},{4,12},{6,14},{8,0},{10,2},{12,4},{14,6},{1,9},{3,11}... | collective-permute-start | bytes 147464 | tf_op jit(solution)/shard_map/ppermute | solution.py:257
  40.6 9.6 %collective-permute-start.11 = (f32[32,384]{1,0:T(8,128)}, f32[32,384]{1,0:T(8,128)S(1)}, u32[]{:S(2)}, u32[]{:S(2)}) collective-permute-start(f32[32,384]{1,0:T(8,128)} %get-tuple-element.23.refs_0_), channel_id=1, source_target_pairs={{0,6},{2,8},{4,10},{6,12},{8,14},{10,0},{12,2},{14,4},{1,7},{3,9},... | collective-permute-start | bytes 147464 | tf_op jit(solution)/shard_map/ppermute | solution.py:257
  41.9 9.9 %copy-start.6 = (f32[32,384]{1,0:T(8,128)}, f32[32,384]{1,0:T(8,128)S(1)}, u32[]{:S(2)}) copy-start(f32[32,384]{1,0:T(8,128)S(1)} %collective-permute-done.15.refs_7_) | copy-start | bytes 147460
  42.0 8.2 %collective-permute-start.10 = (f32[32,384]{1,0:T(8,128)}, f32[32,384]{1,0:T(8,128)S(1)}, u32[]{:S(2)}, u32[]{:S(2)}) collective-permute-start(f32[32,384]{1,0:T(8,128)} %get-tuple-element.23.refs_0_), channel_id=1, source_target_pairs={{0,4},{2,6},{4,8},{6,10},{8,12},{10,14},{12,0},{14,2},{1,5},{3,7},... | collective-permute-start | bytes 147464 | tf_op jit(solution)/shard_map/ppermute | solution.py:257
  44.9 7.0 %copy-start.8 = (f32[32,384]{1,0:T(8,128)}, f32[32,384]{1,0:T(8,128)S(1)}, u32[]{:S(2)}) copy-start(f32[32,384]{1,0:T(8,128)S(1)} %collective-permute-done.14.refs_6_) | copy-start | bytes 147460
  44.9 7.0 %collective-permute-start.9 = (f32[32,384]{1,0:T(8,128)}, f32[32,384]{1,0:T(8,128)S(1)}, u32[]{:S(2)}, u32[]{:S(2)}) collective-permute-start(f32[32,384]{1,0:T(8,128)} %get-tuple-element.23.refs_0_), channel_id=1, source_target_pairs={{0,2},{2,4},{4,6},{6,8},{8,10},{10,12},{12,14},{14,0},{1,3},{3,5},... | collective-permute-start | bytes 147464 | tf_op jit(solution)/shard_map/ppermute | solution.py:257
  47.2 4.7 %copy-start.10 = (f32[32,384]{1,0:T(8,128)}, f32[32,384]{1,0:T(8,128)S(1)}, u32[]{:S(2)}) copy-start(f32[32,384]{1,0:T(8,128)S(1)} %collective-permute-done.13.refs_5_) | copy-start | bytes 147460
  47.3 4.6 %copy-start.12 = (f32[32,384]{1,0:T(8,128)}, f32[32,384]{1,0:T(8,128)S(1)}, u32[]{:S(2)}) copy-start(f32[32,384]{1,0:T(8,128)S(1)} %collective-permute-done.12.refs_4_) | copy-start | bytes 147460
  50.2 1.7 %copy-start.13 = (f32[32,384]{1,0:T(8,128)}, f32[32,384]{1,0:T(8,128)S(1)}, u32[]{:S(2)}) copy-start(f32[32,384]{1,0:T(8,128)S(1)} %collective-permute-done.11.refs_3_) | copy-start | bytes 147460
  50.2 1.7 %copy-start.15 = (f32[32,384]{1,0:T(8,128)}, f32[32,384]{1,0:T(8,128)S(1)}, u32[]{:S(2)}) copy-start(f32[32,384]{1,0:T(8,128)S(1)} %collective-permute-done.10.refs_2_) | copy-start | bytes 147460
  51.9 0.6 copy-start.17
  57.5 1.5 %collective-permute-start.16 = (f32[32,512]{1,0:T(8,128)}, f32[32,512]{1,0:T(8,128)S(1)}, u32[]{:S(2)}, u32[]{:S(2)}) collective-permute-start(f32[32,512]{1,0:T(8,128)} %get-tuple-element.26.mine_ref), channel_id=1, source_target_pairs={{0,1},{1,0},{2,3},{3,2},{4,5},{5,4},{6,7},{7,6},{8,9},{9,8},{10,11... | collective-permute-start | bytes 196616 | tf_op jit(solution)/shard_map/ppermute | solution.py:263
  59.0 0.6 copy-start.3
  61.8 4.4 %collective-permute-start.23 = (f32[32,384]{1,0:T(8,128)}, f32[32,384]{1,0:T(8,128)S(1)}, u32[]{:S(2)}, u32[]{:S(2)}) collective-permute-start(f32[32,384]{1,0:T(8,128)} %get-tuple-element.29.refs_0_), channel_id=1, source_target_pairs={{0,14},{2,0},{4,2},{6,4},{8,6},{10,8},{12,10},{14,12},{1,15},{3,1}... | collective-permute-start | bytes 147464 | tf_op jit(solution)/shard_map/ppermute | solution.py:257
  61.9 6.4 %collective-permute-start.22 = (f32[32,384]{1,0:T(8,128)}, f32[32,384]{1,0:T(8,128)S(1)}, u32[]{:S(2)}, u32[]{:S(2)}) collective-permute-start(f32[32,384]{1,0:T(8,128)} %get-tuple-element.29.refs_0_), channel_id=1, source_target_pairs={{0,12},{2,14},{4,0},{6,2},{8,4},{10,6},{12,8},{14,10},{1,13},{3,15... | collective-permute-start | bytes 147464 | tf_op jit(solution)/shard_map/ppermute | solution.py:257
  62.4 9.6 %collective-permute-start.21 = (f32[32,384]{1,0:T(8,128)}, f32[32,384]{1,0:T(8,128)S(1)}, u32[]{:S(2)}, u32[]{:S(2)}) collective-permute-start(f32[32,384]{1,0:T(8,128)} %get-tuple-element.29.refs_0_), channel_id=1, source_target_pairs={{0,10},{2,12},{4,14},{6,0},{8,2},{10,4},{12,6},{14,8},{1,11},{3,13... | collective-permute-start | bytes 147464 | tf_op jit(solution)/shard_map/ppermute | solution.py:257
  63.6 9.6 %collective-permute-start.20 = (f32[32,384]{1,0:T(8,128)}, f32[32,384]{1,0:T(8,128)S(1)}, u32[]{:S(2)}, u32[]{:S(2)}) collective-permute-start(f32[32,384]{1,0:T(8,128)} %get-tuple-element.29.refs_0_), channel_id=1, source_target_pairs={{0,8},{2,10},{4,12},{6,14},{8,0},{10,2},{12,4},{14,6},{1,9},{3,11}... | collective-permute-start | bytes 147464 | tf_op jit(solution)/shard_map/ppermute | solution.py:257
  66.2 8.3 %collective-permute-start.19 = (f32[32,384]{1,0:T(8,128)}, f32[32,384]{1,0:T(8,128)S(1)}, u32[]{:S(2)}, u32[]{:S(2)}) collective-permute-start(f32[32,384]{1,0:T(8,128)} %get-tuple-element.29.refs_0_), channel_id=1, source_target_pairs={{0,6},{2,8},{4,10},{6,12},{8,14},{10,0},{12,2},{14,4},{1,7},{3,9},... | collective-permute-start | bytes 147464 | tf_op jit(solution)/shard_map/ppermute | solution.py:257
  66.2 9.1 %copy-start.4 = (f32[32,384]{1,0:T(8,128)}, f32[32,384]{1,0:T(8,128)S(1)}, u32[]{:S(2)}) copy-start(f32[32,384]{1,0:T(8,128)S(1)} %collective-permute-done.23.refs_7_) | copy-start | bytes 147460
  66.2 8.3 %collective-permute-start.18 = (f32[32,384]{1,0:T(8,128)}, f32[32,384]{1,0:T(8,128)S(1)}, u32[]{:S(2)}, u32[]{:S(2)}) collective-permute-start(f32[32,384]{1,0:T(8,128)} %get-tuple-element.29.refs_0_), channel_id=1, source_target_pairs={{0,4},{2,6},{4,8},{6,10},{8,12},{10,14},{12,0},{14,2},{1,5},{3,7},... | collective-permute-start | bytes 147464 | tf_op jit(solution)/shard_map/ppermute | solution.py:257
  68.3 7.0 %copy-start.5 = (f32[32,384]{1,0:T(8,128)}, f32[32,384]{1,0:T(8,128)S(1)}, u32[]{:S(2)}) copy-start(f32[32,384]{1,0:T(8,128)S(1)} %collective-permute-done.22.refs_6_) | copy-start | bytes 147460
  68.3 7.0 %collective-permute-start.17 = (f32[32,384]{1,0:T(8,128)}, f32[32,384]{1,0:T(8,128)S(1)}, u32[]{:S(2)}, u32[]{:S(2)}) collective-permute-start(f32[32,384]{1,0:T(8,128)} %get-tuple-element.29.refs_0_), channel_id=1, source_target_pairs={{0,2},{2,4},{4,6},{6,8},{8,10},{10,12},{12,14},{14,0},{1,3},{3,5},... | collective-permute-start | bytes 147464 | tf_op jit(solution)/shard_map/ppermute | solution.py:257
  72.0 3.3 %copy-start.7 = (f32[32,384]{1,0:T(8,128)}, f32[32,384]{1,0:T(8,128)S(1)}, u32[]{:S(2)}) copy-start(f32[32,384]{1,0:T(8,128)S(1)} %collective-permute-done.21.refs_5_) | copy-start | bytes 147460
  73.2 2.1 %copy-start.9 = (f32[32,384]{1,0:T(8,128)}, f32[32,384]{1,0:T(8,128)S(1)}, u32[]{:S(2)}) copy-start(f32[32,384]{1,0:T(8,128)S(1)} %collective-permute-done.20.refs_4_) | copy-start | bytes 147460
  74.4 0.9 copy-start.11
  74.5 0.9 copy-start.14
  75.3 0.6 copy-start.16
  81.2 1.5 %collective-permute-start.24 = (f32[32,512]{1,0:T(8,128)}, f32[32,512]{1,0:T(8,128)S(1)}, u32[]{:S(2)}, u32[]{:S(2)}) collective-permute-start(f32[32,512]{1,0:T(8,128)} %get-tuple-element.33.mine_ref), channel_id=1, source_target_pairs={{0,1},{1,0},{2,3},{3,2},{4,5},{5,4},{6,7},{7,6},{8,9},{9,8},{10,11... | collective-permute-start | bytes 196616 | tf_op jit(solution)/shard_map/ppermute | solution.py:263
  82.7 0.6 copy-start.2
  85.2 5.5 %collective-permute-start.31 = (f32[32,128]{1,0:T(8,128)}, f32[32,128]{1,0:T(8,128)S(1)}, u32[]{:S(2)}, u32[]{:S(2)}) collective-permute-start(f32[32,128]{1,0:T(8,128)} %get-tuple-element.35.refs_0_), channel_id=1, source_target_pairs={{0,14},{2,0},{4,2},{6,4},{8,6},{10,8},{12,10},{14,12},{1,15},{3,1}... | collective-permute-start | bytes 49160 | tf_op jit(solution)/shard_map/ppermute | solution.py:257
  85.8 6.4 %collective-permute-start.30 = (f32[32,128]{1,0:T(8,128)}, f32[32,128]{1,0:T(8,128)S(1)}, u32[]{:S(2)}, u32[]{:S(2)}) collective-permute-start(f32[32,128]{1,0:T(8,128)} %get-tuple-element.35.refs_0_), channel_id=1, source_target_pairs={{0,12},{2,14},{4,0},{6,2},{8,4},{10,6},{12,8},{14,10},{1,13},{3,15... | collective-permute-start | bytes 49160 | tf_op jit(solution)/shard_map/ppermute | solution.py:257
  87.7 6.0 %collective-permute-start.29 = (f32[32,128]{1,0:T(8,128)}, f32[32,128]{1,0:T(8,128)S(1)}, u32[]{:S(2)}, u32[]{:S(2)}) collective-permute-start(f32[32,128]{1,0:T(8,128)} %get-tuple-element.35.refs_0_), channel_id=1, source_target_pairs={{0,10},{2,12},{4,14},{6,0},{8,2},{10,4},{12,6},{14,8},{1,11},{3,13... | collective-permute-start | bytes 49160 | tf_op jit(solution)/shard_map/ppermute | solution.py:257
  87.8 6.0 %collective-permute-start.28 = (f32[32,128]{1,0:T(8,128)}, f32[32,128]{1,0:T(8,128)S(1)}, u32[]{:S(2)}, u32[]{:S(2)}) collective-permute-start(f32[32,128]{1,0:T(8,128)} %get-tuple-element.35.refs_0_), channel_id=1, source_target_pairs={{0,8},{2,10},{4,12},{6,14},{8,0},{10,2},{12,4},{14,6},{1,9},{3,11}... | collective-permute-start | bytes 49160 | tf_op jit(solution)/shard_map/ppermute | solution.py:257
  90.6 5.7 %collective-permute-start.27 = (f32[32,128]{1,0:T(8,128)}, f32[32,128]{1,0:T(8,128)S(1)}, u32[]{:S(2)}, u32[]{:S(2)}) collective-permute-start(f32[32,128]{1,0:T(8,128)} %get-tuple-element.35.refs_0_), channel_id=1, source_target_pairs={{0,6},{2,8},{4,10},{6,12},{8,14},{10,0},{12,2},{14,4},{1,7},{3,9},... | collective-permute-start | bytes 49160 | tf_op jit(solution)/shard_map/ppermute | solution.py:257
  90.7 8.1 %copy-start.26 = (f32[32,128]{1,0:T(8,128)}, f32[32,128]{1,0:T(8,128)S(1)}, u32[]{:S(2)}) copy-start(f32[32,128]{1,0:T(8,128)S(1)} %collective-permute-done.31.refs_7_) | copy-start | bytes 49156
  90.7 5.8 %collective-permute-start.26 = (f32[32,128]{1,0:T(8,128)}, f32[32,128]{1,0:T(8,128)S(1)}, u32[]{:S(2)}, u32[]{:S(2)}) collective-permute-start(f32[32,128]{1,0:T(8,128)} %get-tuple-element.35.refs_0_), channel_id=1, source_target_pairs={{0,4},{2,6},{4,8},{6,10},{8,12},{10,14},{12,0},{14,2},{1,5},{3,7},... | collective-permute-start | bytes 49160 | tf_op jit(solution)/shard_map/ppermute | solution.py:257
  92.1 6.7 %copy-start.27 = (f32[32,128]{1,0:T(8,128)}, f32[32,128]{1,0:T(8,128)S(1)}, u32[]{:S(2)}) copy-start(f32[32,128]{1,0:T(8,128)S(1)} %collective-permute-done.30.refs_6_) | copy-start | bytes 49156
  92.2 6.6 %collective-permute-start.25 = (f32[32,128]{1,0:T(8,128)}, f32[32,128]{1,0:T(8,128)S(1)}, u32[]{:S(2)}, u32[]{:S(2)}) collective-permute-start(f32[32,128]{1,0:T(8,128)} %get-tuple-element.35.refs_0_), channel_id=1, source_target_pairs={{0,2},{2,4},{4,6},{6,8},{8,10},{10,12},{12,14},{14,0},{1,3},{3,5},... | collective-permute-start | bytes 49160 | tf_op jit(solution)/shard_map/ppermute | solution.py:257
  93.7 5.1 %copy-start.28 = (f32[32,128]{1,0:T(8,128)}, f32[32,128]{1,0:T(8,128)S(1)}, u32[]{:S(2)}) copy-start(f32[32,128]{1,0:T(8,128)S(1)} %collective-permute-done.29.refs_5_) | copy-start | bytes 49156
  93.7 5.1 %copy-start.29 = (f32[32,128]{1,0:T(8,128)}, f32[32,128]{1,0:T(8,128)S(1)}, u32[]{:S(2)}) copy-start(f32[32,128]{1,0:T(8,128)S(1)} %collective-permute-done.28.refs_4_) | copy-start | bytes 49156
  96.4 2.4 %copy-start.30 = (f32[32,128]{1,0:T(8,128)}, f32[32,128]{1,0:T(8,128)S(1)}, u32[]{:S(2)}) copy-start(f32[32,128]{1,0:T(8,128)S(1)} %collective-permute-done.27.refs_3_) | copy-start | bytes 49156
  96.4 2.4 %copy-start.31 = (f32[32,128]{1,0:T(8,128)}, f32[32,128]{1,0:T(8,128)S(1)}, u32[]{:S(2)}) copy-start(f32[32,128]{1,0:T(8,128)S(1)} %collective-permute-done.26.refs_2_) | copy-start | bytes 49156
  (1 other events, 0.6 us)

commit v2 on v1

v2 whole, which is shorter than its diff:
```python
import functools

import jax
import jax.numpy as jnp
from jax import lax
from jax.experimental import pallas as pl
from jax.experimental.pallas import tpu as pltpu
from jax.sharding import PartitionSpec as P

ITERS = 3
LANES = 128
PIVOTS = 8
F32 = jnp.float32
BF16 = jnp.bfloat16
SPARE_BYTES = 4 * 1024 * 1024

VMEM = pl.BlockSpec(memory_space=pltpu.VMEM)
SMEM = pl.BlockSpec(memory_space=pltpu.SMEM)


def params(*arrays):
    used = sum(a.size * jnp.dtype(a.dtype).itemsize for a in arrays)
    return pltpu.CompilerParams(vmem_limit_bytes=used + SPARE_BYTES)


def mul(left, right):
    return jnp.dot(left, right, precision=lax.Precision.HIGHEST, preferred_element_type=F32)


def mul_t(left, right):
    return lax.dot_general(
        left,
        right,
        (((1,), (1,)), ((), ())),
        precision=lax.Precision.HIGHEST,
        preferred_element_type=F32,
    )


def widen(matrix):
    rows, columns = matrix.shape
    return jnp.concatenate([matrix, jnp.zeros((rows, LANES - columns), F32)], axis=1)


def solve_wide(matrix, target):
    size = matrix.shape[0]
    row_ids = lax.broadcasted_iota(jnp.int32, (size, LANES), 0)
    lane_ids = lax.broadcasted_iota(jnp.int32, (size, LANES), 1)
    work = jnp.where(lane_ids < size, matrix, pltpu.roll(target, size, 1))
    for base in range(0, size, PIVOTS):
        columns = [
            jnp.broadcast_to(work[:, base + i : base + i + 1], (size, LANES))
            for i in range(PIVOTS)
        ]
        for i in range(PIVOTS):
            pivot = base + i
            here = row_ids == pivot
            inverse = 1.0 / columns[i][pivot : pivot + 1, :]
            row = work[pivot : pivot + 1, :] * inverse
            work = jnp.where(here, row, work - columns[i] * row)
            for later in range(i + 1, PIVOTS):
                entry = columns[later][pivot : pivot + 1, :] * inverse
                columns[later] = jnp.where(here, entry, columns[later] - columns[i] * entry)
    return pltpu.roll(work, LANES - size, 1)


def dense_kernel(
    rows_dev, col_devices, place_ref, count_ref, rows_ref, cols_ref, tiles_ref, out_ref, total
):
    tile = tiles_ref.shape[1]
    blocks = rows_dev // tile
    col_place = place_ref[1]
    col_blocks, row_blocks = total.shape[:2]

    def clear(index, carry):
        for b in range(row_blocks):
            total[index, b] = jnp.zeros((tile, tile), F32)
        return carry

    lax.fori_loop(0, col_blocks, clear, 0)

    def add(slot, carry):
        row = rows_ref[slot]
        column = cols_ref[slot]
        side = lax.rem(row // blocks + col_devices - col_place, col_devices)
        row_at = side * blocks + lax.rem(row, blocks)
        owner = column // (blocks * col_devices)
        column_at = owner * blocks + lax.rem(column, blocks)
        total[column_at, row_at] = total[column_at, row_at] + tiles_ref[slot].astype(F32)
        return carry

    lax.fori_loop(0, count_ref[0], add, 0)

    def split(index, carry):
        start = pl.multiple_of(index * tile, tile)
        for b in range(row_blocks):
            value = total[index, b].T
            high = value.astype(BF16)
            low = (value - high.astype(F32)).astype(BF16)
            out_ref[0, pl.ds(start, tile), pl.ds(b * tile, tile)] = high
            out_ref[1, pl.ds(start, tile), pl.ds(b * tile, tile)] = low
        return carry

    lax.fori_loop(0, col_blocks, split, 0)


def apply_dense(directions, matrix):
    width = directions[0].shape[1]
    total = None
    for k, direction in enumerate(directions):
        rounded = direction.astype(BF16)
        for part in range(2):
            term = jnp.dot(
                rounded,
                matrix[part, k * width : (k + 1) * width, :],
                preferred_element_type=F32,
            )
            total = term if total is None else total + term
    return total


def first_kernel(pieces, blocks_ref, far_ref, matrix, out_ref, state_ref):
    values = [blocks_ref[k] for k in range(pieces)] + [far_ref[...]]
    for k, value in enumerate(values):
        state_ref[k] = value
    half = mul_t(values[0], values[0])
    for value in values[1:pieces]:
        half = half + mul_t(value, value)
    rows = 2 * values[0].shape[1]
    out_ref[:, rows:] = widen(half)
    out_ref[:, :rows] = apply_dense(values[:pieces], matrix)


def image_kernel(first, place_ref, mine_ref, other_ref, direction_ref, residual_ref, *outs):
    out_ref, far_ref = outs[:2]
    here = place_ref[0]
    last = direction_ref.shape[0] - 1
    width = direction_ref.shape[2]
    near = mine_ref[:, :width] + other_ref[:, width : 2 * width]
    far = mine_ref[:, width : 2 * width] + other_ref[:, :width]
    far_ref[...] = far
    if first:
        outs[2][...] = mine_ref[:, 2 * width :] + other_ref[:, 2 * width :]
    image = jnp.concatenate([near, far], axis=1)
    direction = jnp.concatenate([direction_ref[here], direction_ref[last]], axis=1)
    curvature = 0.5 * (mul_t(image, direction) + mul_t(direction, image))
    residual = jnp.concatenate([residual_ref[here], residual_ref[last]], axis=1)
    size = curvature.shape[0]
    grams = [
        curvature,
        mul_t(image, residual),
        mul_t(image, image),
        jnp.zeros((size, LANES - 3 * size), F32),
    ]
    payload = jnp.concatenate([near] + grams, axis=1)
    for k in range(out_ref.shape[0]):
        out_ref[k] = payload


def inverse_kernel(norm_ref, out_ref):
    size = norm_ref.shape[0]
    norm = norm_ref[...]
    small = norm[:, :size]
    norm = widen(0.5 * (small + small.T))
    unit = lax.broadcasted_iota(jnp.int32, norm.shape, 0) == lax.broadcasted_iota(
        jnp.int32, norm.shape, 1
    )
    out_ref[...] = solve_wide(norm, jnp.where(unit, 1.0, 0.0))


def add_up(values):
    total = values[0]
    for value in values[1:]:
        total = total + value
    return total


def step_kernel(pieces, with_solution, place_ref, *refs):
    images_ref, far_ref, direction_ref, residual_ref, norm_ref, inverse_ref, matrix = refs[:7]
    refs = refs[7:]
    if with_solution:
        solution_ref, refs = refs[0], refs[1:]
    out_ref, new_direction, new_residual, new_norm, new_solution = refs
    size, width = far_ref.shape
    grams = add_up([images_ref[k, :, width:] for k in range(pieces)])
    norm = norm_ref[...]
    alpha = solve_wide(grams, norm)[:, :size]
    alpha_t = alpha.T
    image_residual = pltpu.roll(grams, LANES - size, 1)[:, :size]
    image_image = pltpu.roll(grams, LANES - 2 * size, 1)[:, :size]
    cross = mul(alpha_t, image_residual)
    next_norm = norm[:, :size] - (cross + cross.T) + mul(alpha_t, mul(image_image, alpha))
    new_norm[...] = widen(next_norm)
    beta_t = mul(next_norm, inverse_ref[:, :size])
    step = mul(alpha_t, direction_ref[place_ref[0]])
    new_solution[...] = solution_ref[...] + step if with_solution else step
    directions = []
    for k in range(pieces + 1):
        image = images_ref[k, :, :width] if k < pieces else far_ref[...]
        residual = residual_ref[k] - mul(alpha_t, image)
        direction = residual + mul(beta_t, direction_ref[k])
        new_residual[k] = residual
        new_direction[k] = direction
        directions.append(direction)
    out_ref[...] = apply_dense(directions[:pieces], matrix)


def last_image_kernel(place_ref, mine_ref, other_ref, direction_ref, near_ref, gram_ref):
    here = place_ref[0]
    last = direction_ref.shape[0] - 1
    width = direction_ref.shape[2]
    near = mine_ref[:, :width] + other_ref[:, width : 2 * width]
    far = mine_ref[:, width : 2 * width] + other_ref[:, :width]
    near_ref[...] = near
    image = jnp.concatenate([near, far], axis=1)
    direction = jnp.concatenate([direction_ref[here], direction_ref[last]], axis=1)
    gram = widen(0.5 * (mul_t(image, direction) + mul_t(direction, image)))
    for k in range(gram_ref.shape[0]):
        gram_ref[k] = gram


def last_kernel(
    pieces, place_ref, grams_ref, image_ref, direction_ref, residual_ref, norm_ref, solution_ref,
    new_solution, new_residual,
):
    here = place_ref[0]
    size = image_ref.shape[0]
    curvature = add_up([grams_ref[k] for k in range(pieces)])
    alpha_t = solve_wide(curvature, norm_ref[...])[:, :size].T
    new_solution[...] = solution_ref[...] + mul(alpha_t, direction_ref[here])
    new_residual[...] = residual_ref[here] - mul(alpha_t, image_ref[...])


def shape(*dims, dtype=F32):
    return jax.ShapeDtypeStruct(dims, dtype)


def per_device(tiles, tile_rows, tile_cols, tile_count, signs, vertex_weight, column_scale):
    sketch, rows_dev = signs.shape
    tile = tiles.shape[1]
    pieces = lax.axis_size("row")
    col_devices = lax.axis_size("col")
    group = col_devices * rows_dev
    depth = pieces * rows_dev
    place = jnp.stack([lax.axis_index("row"), lax.axis_index("col")]).astype(jnp.int32)

    def around(values):
        return lax.all_to_all(values, "row", 0, 0)

    def across(value):
        return lax.ppermute(
            value, "col", [(i, (i + 1) % col_devices) for i in range(col_devices)]
        )

    right_side = signs.astype(F32) * vertex_weight[None, :] * column_scale[:, None]
    far_side = across(right_side)
    blocks = around(jnp.broadcast_to(right_side[None], (pieces, sketch, rows_dev)))

    matrix = shape(2, depth, group, dtype=BF16)
    dense = pl.pallas_call(
        functools.partial(dense_kernel, rows_dev, col_devices),
        out_shape=matrix,
        in_specs=[SMEM, SMEM, SMEM, SMEM, VMEM],
        out_specs=VMEM,
        scratch_shapes=[pltpu.VMEM((depth // tile, group // tile, tile, tile), F32)],
        compiler_params=params(tiles, matrix, matrix),
        cost_estimate=pl.CostEstimate(
            flops=4 * tiles.size, bytes_accessed=4 * tiles.size, transcendentals=0
        ),
        name="dense",
    )(place, tile_count, tile_rows, tile_cols, tiles)

    state = shape(pieces + 1, sketch, rows_dev)
    small = shape(sketch, LANES)
    piece = shape(sketch, rows_dev)
    payload = shape(pieces, sketch, rows_dev + LANES)

    partial_sum, direction = pl.pallas_call(
        functools.partial(first_kernel, pieces),
        out_shape=(shape(sketch, group + LANES), state),
        in_specs=[VMEM] * 3,
        out_specs=(VMEM, VMEM),
        compiler_params=params(matrix, state, state),
        name="first",
    )(blocks, far_side, dense)
    residual = direction
    norm = None
    solution = None
    for iteration in range(ITERS - 1):
        first = iteration == 0
        outs = pl.pallas_call(
            functools.partial(image_kernel, first),
            out_shape=(payload, piece) + ((small,) if first else ()),
            in_specs=[SMEM] + [VMEM] * 4,
            out_specs=(VMEM,) * (3 if first else 2),
            compiler_params=params(payload, state, state),
            name="image",
        )(place, partial_sum, across(partial_sum), direction, residual)
        payloads, far = outs[:2]
        if first:
            norm = outs[2]
        inverse = pl.pallas_call(
            inverse_kernel,
            out_shape=small,
            in_specs=[VMEM],
            out_specs=VMEM,
            compiler_params=params(),
            name="inverse",
        )(norm)
        given = () if first else (solution,)
        partial_sum, direction, residual, norm, solution = pl.pallas_call(
            functools.partial(step_kernel, pieces, not first),
            out_shape=(shape(sketch, group), state, state, small, piece),
            in_specs=[SMEM] + [VMEM] * (7 + len(given)),
            out_specs=(VMEM,) * 5,
            compiler_params=params(payload, matrix, state, state, state, state),
            name="step",
        )(place, around(payloads), far, direction, residual, norm, inverse, dense, *given)
    image, grams = pl.pallas_call(
        last_image_kernel,
        out_shape=(piece, shape(pieces, sketch, LANES)),
        in_specs=[SMEM] + [VMEM] * 3,
        out_specs=(VMEM, VMEM),
        compiler_params=params(state),
        name="last_image",
    )(place, partial_sum, across(partial_sum), direction)
    return pl.pallas_call(
        functools.partial(last_kernel, pieces),
        out_shape=(piece, piece),
        in_specs=[SMEM] + [VMEM] * 6,
        out_specs=(VMEM, VMEM),
        compiler_params=params(payload, state, state),
        name="last",
    )(place, around(grams), image, direction, residual, norm, solution)


def solution(mesh):
    return jax.shard_map(
        per_device,
        mesh=mesh,
        in_specs=(
            P(("row", "col"), None, None),
            P(("row", "col")),
            P(("row", "col")),
            P(("row", "col")),
            P("rhs", ("row", "col")),
            P(("row", "col")),
            P("rhs"),
        ),
        out_specs=(P("rhs", ("row", "col")), P("rhs", ("row", "col"))),
        check_vma=False,
    )
```

time: 103 us -> 90 us (0.87)
  starting transfers between devices: 38.1 us -> 17.4 us
  Pallas kernels: 38.9 us -> 20.2 us
  blocking collectives: 0 us -> 10.8 us
  waiting for transfers between devices: 17.5 us -> 25.7 us
  local copies, waits for them, and re-layouts: 4.85 us -> 12.8 us
    ppermute x28 -> x0, starting transfers between devices: 37.4 us -> none  [around(): lax.ppermute(value, 'row', [(i, (i + k) % pieces) for i in range(pieces)])]
    all_to_all x0 -> x3, waiting for transfers between devices: none -> 22.3 us  [around(): return lax.all_to_all(values, 'row', 0, 0)]
    all_to_all x0 -> x3, starting transfers between devices: none -> 16.7 us  [around(): return lax.all_to_all(values, 'row', 0, 0)]
    ppermute x28 -> x0, waiting for transfers between devices: 13.1 us -> none  [around(): lax.ppermute(value, 'row', [(i, (i + k) % pieces) for i in range(pieces)])]
    pallas_call x6, Pallas kernels: 26.7 us -> 15 us  [the longest x2 6.02 us: per_device(): pl.pallas_call(functools.partial(step_kernel, pieces, not first), out_sha...]
    all_to_all x0 -> x1, blocking collectives: none -> 10.8 us  [around(): return lax.all_to_all(values, 'row', 0, 0)]
    unnamed x66 -> x14, local copies, waits for them, and re-layouts: 4.85 us -> 12.1 us
    pallas_call x1, Pallas kernels: 4.64 us -> 0.93 us  [per_device(): pl.pallas_call(functools.partial(first_kernel, pieces), out_shape=(shape(...]
  transfers between devices with their start and end apart: 32 -> 7, of which waited for: 12 -> 5; matrix products, arithmetic and copies ran while one was open for 1% -> 0% of each run, Pallas kernels for 14% -> 7%
where the time goes in v2:
time: 90 us; the launch traced here: 89.2 us
  waiting for transfers between devices  25.7 us (29%)
  Pallas kernels  20.2 us (22%)
  starting transfers between devices  17.4 us (19%)
  local copies, waits for them, and re-layouts  12.8 us (14%)
  blocking collectives  10.8 us (12%)
  between operations  1.37 us (2%)
  other arithmetic  0.92 us (1%)
    all_to_all x3, waiting for transfers between devices, around(): return lax.all_to_all(values, 'row', 0, 0)  22.3 us
    all_to_all x3, starting transfers between devices, around(): return lax.all_to_all(values, 'row', 0, 0)  16.7 us
    unnamed x14, local copies, waits for them, and re-layouts  12.1 us
    all_to_all x1, blocking collectives, around(): return lax.all_to_all(values, 'row', 0, 0)  10.8 us
    pallas_call x2, Pallas kernels, per_device(): pl.pallas_call(functools.partial(step_kernel, pieces, not first), out_sha...  6.02 us
    pallas_call x1, Pallas kernels, per_device(): pl.pallas_call(functools.partial(dense_kernel, rows_dev, col_devices), ou...  4.77 us
    pallas_call x2, Pallas kernels, per_device(): pl.pallas_call(functools.partial(image_kernel, first), out_shape=(payload...  3.45 us
    ppermute x4, waiting for transfers between devices, across(): lax.ppermute(value, 'col', [(i, (i + 1) % col_devices) for i in range(col...  3.41 us
  transfers between devices with their start and end apart: 7, of which 5 were waited for; matrix products, arithmetic and copies ran while one was open for 0% of the time, Pallas kernels for 7%

profile of v2, /device:TPU:0, one launch (start us, length us, event | category | flops | bytes accessed | tf_op | source)
XLA Modules:
  0.0 89.2 jit_solution(5294907409094211895)
XLA Ops:
  0.6 0.8 multiply_multiply_fusion
  1.5 0.7 broadcast_in_dim.2
  2.2 7.3 %all-to-all-start = ((f32[8,32,256]{2,1,0:T(8,128)}), f32[8,32,256]{2,1,0:T(8,128)S(1)}, u32[]{:S(2)}, u32[]{:S(2)}) async-start(f32[8,32,256]{2,1,0:T(8,128)} %broadcast_in_dim.2), calls=%async_computation | async-start | bytes 524288 | tf_op jit(solution)/shard_map/all_to_all | solution.py:248
  9.5 0.0 collective-permute-start
  9.5 0.1 pad_add_fusion.place_ref
  10.2 0.0 copy-start.4
  10.3 2.2 %copy-done.4 = bf16[130,128,128]{2,1,0:T(8,128)(2,1)S(1)} copy-done((bf16[130,128,128]{2,1,0:T(8,128)(2,1)S(1)}, bf16[130,128,128]{2,1,0:T(8,128)(2,1)}, u32[]{:S(2)}) %copy-start.4) | copy-done | bytes 4259864
  12.5 0.0 copy-start.5
  12.5 0.7 copy-done.5
  13.1 0.0 copy-start.6
  13.1 0.7 copy-done.6
  13.8 4.8 %dense.1.matrix.refs_6_ = bf16[2,2048,512]{2,1,0:T(8,128)(2,1)S(1)} custom-call(s32[2]{0:T(128)S(1)} %pad_add_fusion.place_ref, s32[1]{0:T(128)S(6)} %copy.9.count_ref, s32[130]{0:T(256)S(1)} %copy-done.5, s32[130]{0:T(256)S(1)} %copy-done.6, bf16[130,128,128]{2,1,0:T(8,128)(2,1)S(1)} %copy-done.4), custom_call_target="tpu_custom_call" | custom-call | flops 8519680 | bytes 8519680 | tf_op jit(solution)/shard_map/dense/pallas_call | solution.py:260
  18.6 0.0 copy-start
  18.6 1.9 %copy-done = bf16[2,2048,512]{2,1,0:T(8,128)(2,1)} copy-done((bf16[2,2048,512]{2,1,0:T(8,128)(2,1)}, bf16[2,2048,512]{2,1,0:T(8,128)(2,1)S(1)}, u32[]{:S(2)}) %copy-start) | copy-done | bytes 4194328
  20.5 0.0 collective-permute-done.far_ref
  20.5 0.0 all-to-all-done.blocks_ref
  20.5 0.0 copy-start.1
  20.5 2.2 %copy-done.1 = bf16[2,2048,512]{2,1,0:T(8,128)(2,1)S(1)} copy-done((bf16[2,2048,512]{2,1,0:T(8,128)(2,1)S(1)}, bf16[2,2048,512]{2,1,0:T(8,128)(2,1)}, u32[]{:S(2)}) %copy-start.1) | copy-done | bytes 4194328
  22.7 0.9 %first.1 = (f32[32,640]{1,0:T(8,128)S(1)}, f32[9,32,256]{2,1,0:T(8,128)S(1)}) custom-call(f32[8,32,256]{2,1,0:T(8,128)S(1)} %all-to-all-done.blocks_ref, f32[32,256]{1,0:T(8,128)S(1)} %collective-permute-done.far_ref, bf16[2,2048,512]{2,1,0:T(8,128)(2,1)S(1)} %copy-done.1), custom_call_target="tpu_custom_call" | custom-call | tf_op jit(solution)/shard_map/first/pallas_call | solution.py:278
  23.7 0.6 collective-permute-start.1
  24.2 0.9 %collective-permute-done.1.other_ref = f32[32,640]{1,0:T(8,128)S(1)} collective-permute-done((f32[32,640]{1,0:T(8,128)S(1)}, f32[32,640]{1,0:T(8,128)S(1)}, u32[]{:S(2)}, u32[]{:S(2)}) %collective-permute-start.1) | collective-permute-done | bytes 81952 | tf_op jit(solution)/shard_map/ppermute | solution.py:251
  25.2 1.7 %image.2 = (f32[8,32,384]{2,1,0:T(8,128)}, f32[32,256]{1,0:T(8,128)S(1)}, f32[32,128]{1,0:T(8,128)S(1)}) custom-call(s32[2]{0:T(128)S(1)} %pad_add_fusion.place_ref, f32[32,640]{1,0:T(8,128)S(1)} %get-tuple-element.21.mine_ref, f32[32,640]{1,0:T(8,128)S(1)} %collective-permute-done.1.other_ref, ...), custom_call_target="tpu_custom_call" | custom-call | tf_op jit(solution)/shard_map/image/pallas_call | solution.py:291
  26.9 5.8 %all-to-all-start.1 = ((f32[8,32,384]{2,1,0:T(8,128)}), f32[8,32,384]{2,1,0:T(8,128)S(1)}, u32[]{:S(2)}, u32[]{:S(2)}) async-start(f32[8,32,384]{2,1,0:T(8,128)} %get-tuple-element.23), calls=%async_computation.1 | async-start | bytes 786432 | tf_op jit(solution)/shard_map/all_to_all | solution.py:248
  32.7 0.9 %inverse.2.refs_5_ = f32[32,128]{1,0:T(8,128)S(1)} custom-call(f32[32,128]{1,0:T(8,128)S(1)} %get-tuple-element.25.norm_ref.refs_4_), custom_call_target="tpu_custom_call" | custom-call | tf_op jit(solution)/shard_map/inverse/pallas_call | solution.py:302
  33.6 11.2 %all-to-all-done.1.refs_0_ = f32[8,32,384]{2,1,0:T(8,128)S(1)} async-done(((f32[8,32,384]{2,1,0:T(8,128)}), f32[8,32,384]{2,1,0:T(8,128)S(1)}, u32[]{:S(2)}, u32[]{:S(2)}) %all-to-all-start.1) | async-done | bytes 393248 | tf_op jit(solution)/shard_map/all_to_all | solution.py:248
  44.9 0.0 copy-start.2
  44.9 2.2 %copy-done.2 = bf16[2,2048,512]{2,1,0:T(8,128)(2,1)S(1)} copy-done((bf16[2,2048,512]{2,1,0:T(8,128)(2,1)S(1)}, bf16[2,2048,512]{2,1,0:T(8,128)(2,1)}, u32[]{:S(2)}) %copy-start.2) | copy-done | bytes 4194328
  47.1 3.0 %step.2 = (f32[32,512]{1,0:T(8,128)S(1)}, f32[9,32,256]{2,1,0:T(8,128)S(1)}, f32[9,32,256]{2,1,0:T(8,128)S(1)}, f32[32,128]{1,0:T(8,128)S(1)}, f32[32,256]{1,0:T(8,128)S(1)}) custom-call(s32[2]{0:T(128)S(1)} %pad_add_fusion.place_ref, f32[8,32,384]{2,1,0:T(8,128)S(1)} %all-to-all-done.1.refs_0_, f32[32,256]{1,0:T(8,128)S(1)} %get-tuple-element.24.refs_1_, ...), custom_call_target="tpu_custom_call" | custom-call | tf_op jit(solution)/shard_map/step/pallas_call | solution.py:311
  50.1 0.1 collective-permute-start.2
  50.2 1.2 %collective-permute-done.2.other_ref = f32[32,512]{1,0:T(8,128)S(1)} collective-permute-done((f32[32,512]{1,0:T(8,128)S(1)}, f32[32,512]{1,0:T(8,128)S(1)}, u32[]{:S(2)}, u32[]{:S(2)}) %collective-permute-start.2) | collective-permute-done | bytes 65568 | tf_op jit(solution)/shard_map/ppermute | solution.py:251
  51.4 1.7 %image.3 = (f32[8,32,384]{2,1,0:T(8,128)}, f32[32,256]{1,0:T(8,128)S(1)}) custom-call(s32[2]{0:T(128)S(1)} %pad_add_fusion.place_ref, f32[32,512]{1,0:T(8,128)S(1)} %get-tuple-element.26.mine_ref, f32[32,512]{1,0:T(8,128)S(1)} %collective-permute-done.2.other_ref, f32[9,32,256]{2,1,0:T(8,128)S(1)} %get-tuple-element.27.direction_ref.refs_2_, ...), custom_call_target="tpu_custom_call" | custom-call | tf_op jit(solution)/shard_map/image/pallas_call | solution.py:291
  53.1 3.6 %all-to-all-start.2 = ((f32[8,32,384]{2,1,0:T(8,128)}), f32[8,32,384]{2,1,0:T(8,128)S(1)}, u32[]{:S(2)}, u32[]{:S(2)}) async-start(f32[8,32,384]{2,1,0:T(8,128)} %get-tuple-element.29), calls=%async_computation.2 | async-start | bytes 786432 | tf_op jit(solution)/shard_map/all_to_all | solution.py:248
  56.8 0.9 %inverse.3.refs_5_ = f32[32,128]{1,0:T(8,128)S(1)} custom-call(f32[32,128]{1,0:T(8,128)S(1)} %get-tuple-element.31.norm_ref.refs_4_), custom_call_target="tpu_custom_call" | custom-call | tf_op jit(solution)/shard_map/inverse/pallas_call | solution.py:302
  57.7 11.1 %all-to-all-done.2.refs_0_ = f32[8,32,384]{2,1,0:T(8,128)S(1)} async-done(((f32[8,32,384]{2,1,0:T(8,128)}), f32[8,32,384]{2,1,0:T(8,128)S(1)}, u32[]{:S(2)}, u32[]{:S(2)}) %all-to-all-start.2) | async-done | bytes 393248 | tf_op jit(solution)/shard_map/all_to_all | solution.py:248
  68.8 0.0 copy-start.3
  68.8 2.2 %copy-done.3 = bf16[2,2048,512]{2,1,0:T(8,128)(2,1)S(1)} copy-done((bf16[2,2048,512]{2,1,0:T(8,128)(2,1)S(1)}, bf16[2,2048,512]{2,1,0:T(8,128)(2,1)}, u32[]{:S(2)}) %copy-start.3) | copy-done | bytes 4194328
  71.0 3.0 %step.3 = (f32[32,512]{1,0:T(8,128)S(1)}, f32[9,32,256]{2,1,0:T(8,128)S(1)}, f32[9,32,256]{2,1,0:T(8,128)S(1)}, f32[32,128]{1,0:T(8,128)S(1)}, f32[32,256]{1,0:T(8,128)S(1)}) custom-call(s32[2]{0:T(128)S(1)} %pad_add_fusion.place_ref, f32[8,32,384]{2,1,0:T(8,128)S(1)} %all-to-all-done.2.refs_0_, f32[32,256]{1,0:T(8,128)S(1)} %get-tuple-element.30.refs_1_, ...), custom_call_target="tpu_custom_call" | custom-call | tf_op jit(solution)/shard_map/step/pallas_call | solution.py:311
  74.0 0.1 collective-permute-start.3
  74.1 1.2 %collective-permute-done.3.other_ref = f32[32,512]{1,0:T(8,128)S(1)} collective-permute-done((f32[32,512]{1,0:T(8,128)S(1)}, f32[32,512]{1,0:T(8,128)S(1)}, u32[]{:S(2)}, u32[]{:S(2)}) %collective-permute-start.3) | collective-permute-done | bytes 65568 | tf_op jit(solution)/shard_map/ppermute | solution.py:251
  75.3 0.8 last_image.1
  76.1 10.8 %all_to_all.20.grams_ref = f32[8,32,128]{2,1,0:T(8,128)S(1)} all-to-all(f32[8,32,128]{2,1,0:T(8,128)S(1)} %get-tuple-element.35), channel_id=1, replica_groups=mesh['rhs'=2,'row'=8,'col'=2] {'row'}, dimensions={0} | all-to-all | bytes 262144 | tf_op jit(solution)/shard_map/all_to_all | solution.py:248
  86.9 2.3 %last.1 = (f32[32,256]{1,0:T(8,128)}, f32[32,256]{1,0:T(8,128)}) custom-call(s32[2]{0:T(128)S(1)} %pad_add_fusion.place_ref, f32[8,32,128]{2,1,0:T(8,128)S(1)} %all_to_all.20.grams_ref, f32[32,256]{1,0:T(8,128)S(1)} %get-tuple-element.36.image_ref, f32[9,32,256]{2,1,0:T(8,128)S(1)} %get-tuple-element.34.direction_ref, ...), custom_call_target="tpu_custom_call" | custom-call | tf_op jit(solution)/shard_map/last/pallas_call | solution.py:327
Async XLA Ops:
  2.2 18.3 %all-to-all-start = ((f32[8,32,256]{2,1,0:T(8,128)}), f32[8,32,256]{2,1,0:T(8,128)S(1)}, u32[]{:S(2)}, u32[]{:S(2)}) async-start(f32[8,32,256]{2,1,0:T(8,128)} %broadcast_in_dim.2), calls=%async_computation | async-start | bytes 524288 | tf_op jit(solution)/shard_map/all_to_all | solution.py:248
  9.5 11.0 %collective-permute-start = (f32[32,256]{1,0:T(8,128)S(1)}, f32[32,256]{1,0:T(8,128)S(1)}, u32[]{:S(2)}, u32[]{:S(2)}) collective-permute-start(f32[32,256]{1,0:T(8,128)S(1)} %multiply_multiply_fusion), channel_id=1, source_target_pairs={{0,1},{1,0},{2,3},{3,2},{4,5},{5,4},{6,7},{7,6},{8,9},{9,8},{10,11... | collective-permute-start | bytes 98312 | tf_op jit(solution)/shard_map/ppermute | solution.py:251
  10.2 2.2 %copy-start.4 = (bf16[130,128,128]{2,1,0:T(8,128)(2,1)S(1)}, bf16[130,128,128]{2,1,0:T(8,128)(2,1)}, u32[]{:S(2)}) copy-start(bf16[130,128,128]{2,1,0:T(8,128)(2,1)} %tiles_ref.1) | copy-start | bytes 12779524
  12.5 0.7 copy-start.5
  13.1 0.7 copy-start.6
  18.6 1.9 %copy-start = (bf16[2,2048,512]{2,1,0:T(8,128)(2,1)}, bf16[2,2048,512]{2,1,0:T(8,128)(2,1)S(1)}, u32[]{:S(2)}) copy-start(bf16[2,2048,512]{2,1,0:T(8,128)(2,1)S(1)} %dense.1.matrix.refs_6_) | copy-start | bytes 12582916
  20.5 2.2 %copy-start.1 = (bf16[2,2048,512]{2,1,0:T(8,128)(2,1)S(1)}, bf16[2,2048,512]{2,1,0:T(8,128)(2,1)}, u32[]{:S(2)}) copy-start(bf16[2,2048,512]{2,1,0:T(8,128)(2,1)} %copy-done) | copy-start | bytes 12582916
  23.7 1.5 %collective-permute-start.1 = (f32[32,640]{1,0:T(8,128)S(1)}, f32[32,640]{1,0:T(8,128)S(1)}, u32[]{:S(2)}, u32[]{:S(2)}) collective-permute-start(f32[32,640]{1,0:T(8,128)S(1)} %get-tuple-element.21.mine_ref), channel_id=1, source_target_pairs={{0,1},{1,0},{2,3},{3,2},{4,5},{5,4},{6,7},{7,6},{8,9},{9,8},{10,11... | collective-permute-start | bytes 245768 | tf_op jit(solution)/shard_map/ppermute | solution.py:251
  26.9 18.0 %all-to-all-start.1 = ((f32[8,32,384]{2,1,0:T(8,128)}), f32[8,32,384]{2,1,0:T(8,128)S(1)}, u32[]{:S(2)}, u32[]{:S(2)}) async-start(f32[8,32,384]{2,1,0:T(8,128)} %get-tuple-element.23), calls=%async_computation.1 | async-start | bytes 786432 | tf_op jit(solution)/shard_map/all_to_all | solution.py:248
  44.9 2.2 %copy-start.2 = (bf16[2,2048,512]{2,1,0:T(8,128)(2,1)S(1)}, bf16[2,2048,512]{2,1,0:T(8,128)(2,1)}, u32[]{:S(2)}) copy-start(bf16[2,2048,512]{2,1,0:T(8,128)(2,1)} %copy-done) | copy-start | bytes 12582916
  50.1 1.3 %collective-permute-start.2 = (f32[32,512]{1,0:T(8,128)S(1)}, f32[32,512]{1,0:T(8,128)S(1)}, u32[]{:S(2)}, u32[]{:S(2)}) collective-permute-start(f32[32,512]{1,0:T(8,128)S(1)} %get-tuple-element.26.mine_ref), channel_id=1, source_target_pairs={{0,1},{1,0},{2,3},{3,2},{4,5},{5,4},{6,7},{7,6},{8,9},{9,8},{10,11... | collective-permute-start | bytes 196616 | tf_op jit(solution)/shard_map/ppermute | solution.py:251
  53.1 15.7 %all-to-all-start.2 = ((f32[8,32,384]{2,1,0:T(8,128)}), f32[8,32,384]{2,1,0:T(8,128)S(1)}, u32[]{:S(2)}, u32[]{:S(2)}) async-start(f32[8,32,384]{2,1,0:T(8,128)} %get-tuple-element.29), calls=%async_computation.2 | async-start | bytes 786432 | tf_op jit(solution)/shard_map/all_to_all | solution.py:248
  68.8 2.2 %copy-start.3 = (bf16[2,2048,512]{2,1,0:T(8,128)(2,1)S(1)}, bf16[2,2048,512]{2,1,0:T(8,128)(2,1)}, u32[]{:S(2)}) copy-start(bf16[2,2048,512]{2,1,0:T(8,128)(2,1)} %copy-done) | copy-start | bytes 12582916
  74.0 1.3 %collective-permute-start.3 = (f32[32,512]{1,0:T(8,128)S(1)}, f32[32,512]{1,0:T(8,128)S(1)}, u32[]{:S(2)}, u32[]{:S(2)}) collective-permute-start(f32[32,512]{1,0:T(8,128)S(1)} %get-tuple-element.33.mine_ref), channel_id=1, source_target_pairs={{0,1},{1,0},{2,3},{3,2},{4,5},{5,4},{6,7},{7,6},{8,9},{9,8},{10,11... | collective-permute-start | bytes 196616 | tf_op jit(solution)/shard_map/ppermute | solution.py:251

commit v3 on v2

v3 whole, which is shorter than its diff:
```python
import functools

import jax
import jax.numpy as jnp
from jax import lax
from jax.experimental import pallas as pl
from jax.experimental.pallas import tpu as pltpu
from jax.sharding import PartitionSpec as P

ITERS = 3
LANES = 128
PIVOTS = 8
CHUNKS = 5
F32 = jnp.float32
BF16 = jnp.bfloat16
SPARE_BYTES = 4 * 1024 * 1024

VMEM = pl.BlockSpec(memory_space=pltpu.VMEM)
SMEM = pl.BlockSpec(memory_space=pltpu.SMEM)
HBM = pl.BlockSpec(memory_space=pltpu.HBM)


def params(*arrays):
    used = sum(a.size * jnp.dtype(a.dtype).itemsize for a in arrays)
    return pltpu.CompilerParams(vmem_limit_bytes=used + SPARE_BYTES)


def split(value):
    high = value.astype(BF16)
    rest = value - high.astype(F32)
    middle = rest.astype(BF16)
    low = (rest - middle.astype(F32)).astype(BF16)
    return high, middle, low


def mul(left, right):
    return jnp.dot(left, right, precision=lax.Precision.HIGHEST, preferred_element_type=F32)


def factor(left):
    high, middle, low = split(left)
    return jnp.concatenate([high, high, middle, high, middle, low], axis=1)


def times(prepared, right):
    high, middle, low = split(right)
    stacked = jnp.concatenate([high, middle, high, low, middle, high], axis=0)
    return jnp.dot(prepared, stacked, preferred_element_type=F32)


def grams(left, rights):
    size = left.shape[0]
    parts = [split(right) for right in rights]
    parts = parts + [parts[0]] * (LANES // size - len(parts))
    stacked = jnp.concatenate([part[i] for i in range(3) for part in parts], axis=0)
    every = lax.dot_general(
        jnp.concatenate(split(left), axis=0),
        stacked,
        (((1,), (1,)), ((), ())),
        preferred_element_type=F32,
    )
    rows = every[2 * size :] + every[size : 2 * size] + every[:size]
    return rows[:, 2 * LANES :] + rows[:, LANES : 2 * LANES] + rows[:, :LANES]


def widen(matrix):
    rows, columns = matrix.shape
    return jnp.concatenate([matrix, jnp.zeros((rows, LANES - columns), F32)], axis=1)


def symmetric(matrix):
    return 0.5 * (matrix + matrix.T)


def solve_wide(matrix, target):
    size = matrix.shape[0]
    row_ids = lax.broadcasted_iota(jnp.int32, (size, LANES), 0)
    lane_ids = lax.broadcasted_iota(jnp.int32, (size, LANES), 1)
    work = jnp.where(lane_ids < size, matrix, pltpu.roll(target, size, 1))
    for base in range(0, size, PIVOTS):
        columns = [
            jnp.broadcast_to(work[:, base + i : base + i + 1], (size, LANES))
            for i in range(PIVOTS)
        ]
        for i in range(PIVOTS):
            pivot = base + i
            here = row_ids == pivot
            inverse = 1.0 / columns[i][pivot : pivot + 1, :]
            row = work[pivot : pivot + 1, :] * inverse
            work = jnp.where(here, row, work - columns[i] * row)
            for later in range(i + 1, PIVOTS):
                entry = columns[later][pivot : pivot + 1, :] * inverse
                columns[later] = jnp.where(here, entry, columns[later] - columns[i] * entry)
    return pltpu.roll(work, LANES - size, 1)


def add_up(values):
    values = list(values)
    while len(values) > 1:
        pairs = [values[i] + values[i + 1] for i in range(0, len(values) - 1, 2)]
        values = pairs + values[len(values) - len(values) % 2 :]
    return values[0]


def dense_kernel(rows_dev, col_devices, lists_ref, tiles_ref, out_ref, held, total, sems):
    slots, tile = tiles_ref.shape[:2]
    blocks = rows_dev // tile
    live = lists_ref[2 * slots]
    row_place = lists_ref[2 * slots + 1]
    col_place = lists_ref[2 * slots + 2]
    col_blocks, row_blocks = total.shape[:2]
    chunk = -(-slots // CHUNKS)
    copies = []
    for c in range(CHUNKS):
        part = pl.ds(c * chunk, min(chunk, slots - c * chunk))
        copies.append(pltpu.make_async_copy(tiles_ref.at[part], held.at[part], sems.at[c]))
        copies[c].start()

    def clear(index, carry):
        for b in range(row_blocks):
            total[index, b] = jnp.zeros((tile, tile), F32)
        return carry

    lax.fori_loop(0, col_blocks, clear, 0)

    def add(slot, carry):
        row = lists_ref[slot]
        column = lists_ref[slots + slot]
        side = lax.rem(row // blocks + col_devices - col_place, col_devices)
        row_at = side * blocks + lax.rem(row, blocks)
        owner = column // (blocks * col_devices)
        column_at = (owner ^ row_place) * blocks + lax.rem(column, blocks)
        total[column_at, row_at] = total[column_at, row_at] + held[slot].astype(F32)
        return carry

    for c in range(CHUNKS):
        copies[c].wait()
        lax.fori_loop(c * chunk, jnp.minimum(live, min((c + 1) * chunk, slots)), add, 0)

    def part(index, carry):
        start = pl.multiple_of(index * tile, tile)
        for b in range(row_blocks):
            value = total[index, b].T
            high = value.astype(BF16)
            low = (value - high.astype(F32)).astype(BF16)
            out_ref[0, pl.ds(start, tile), pl.ds(b * tile, tile)] = high
            out_ref[1, pl.ds(start, tile), pl.ds(b * tile, tile)] = low
        return carry

    lax.fori_loop(0, col_blocks, part, 0)


def apply_dense(directions, matrix):
    width = directions[0].shape[1]
    total = None
    for k, direction in enumerate(directions):
        rounded = direction.astype(BF16)
        for part in range(2):
            term = jnp.dot(
                rounded,
                matrix[part, k * width : (k + 1) * width, :],
                preferred_element_type=F32,
            )
            total = term if total is None else total + term
    return total


def first_kernel(pieces, *refs):
    values = [ref[...] for ref in refs[: pieces + 1]]
    matrix, out_ref, state_ref = refs[pieces + 1 :]
    for k, value in enumerate(values):
        state_ref[k] = value
    rows = 2 * values[0].shape[1]
    out_ref[:, rows:] = add_up([grams(value, [value]) for value in values[:pieces]])
    out_ref[:, :rows] = apply_dense(values[:pieces], matrix)


def add_halves(mine_ref, other_ref, width):
    near = mine_ref[:, :width] + other_ref[:, width : 2 * width]
    far = mine_ref[:, width : 2 * width] + other_ref[:, :width]
    return near, far


def image_kernel(first, mine_ref, other_ref, direction_ref, residual_ref, *outs):
    out_ref, far_ref = outs[:2]
    last = direction_ref.shape[0] - 1
    size, width = direction_ref.shape[1:]
    near, far = add_halves(mine_ref, other_ref, width)
    far_ref[...] = far
    if first:
        outs[2][...] = mine_ref[:, 2 * width :] + other_ref[:, 2 * width :]
    for i in range(width // LANES):
        out_ref[i * size : (i + 1) * size] = near[:, i * LANES : (i + 1) * LANES]
    near_part = grams(near, [direction_ref[0], residual_ref[0], near])
    far_part = grams(far, [direction_ref[last], residual_ref[last], far])
    out_ref[width // LANES * size :] = near_part + far_part


def inverse_kernel(norm_ref, out_ref):
    norm = widen(symmetric(norm_ref[:, : norm_ref.shape[0]]))
    unit = lax.broadcasted_iota(jnp.int32, norm.shape, 0) == lax.broadcasted_iota(
        jnp.int32, norm.shape, 1
    )
    out_ref[...] = solve_wide(norm, jnp.where(unit, 1.0, 0.0))


def step_kernel(pieces, with_solution, *refs):
    images = refs[:pieces]
    far_ref, direction_ref, residual_ref, norm_ref, inverse_ref, matrix = refs[pieces : pieces + 6]
    refs = refs[pieces + 6 :]
    if with_solution:
        solution_ref, refs = refs[0], refs[1:]
    out_ref, new_direction, new_residual, new_norm, new_solution = refs
    size, width = far_ref.shape
    parts = width // LANES
    products = add_up([ref[parts * size :] for ref in images])
    norm = norm_ref[...]
    alpha = solve_wide(widen(symmetric(products[:, :size])), norm)[:, :size]
    alpha_t = alpha.T
    image_residual = pltpu.roll(products, LANES - size, 1)[:, :size]
    image_image = pltpu.roll(products, LANES - 2 * size, 1)[:, :size]
    cross = mul(alpha_t, image_residual)
    next_norm = norm[:, :size] - (cross + cross.T) + mul(alpha_t, mul(image_image, alpha))
    new_norm[...] = widen(next_norm)
    beta_t = factor(mul(next_norm, inverse_ref[:, :size]))
    alpha_t = factor(alpha_t)
    step = times(alpha_t, direction_ref[0])
    new_solution[...] = solution_ref[...] + step if with_solution else step
    directions = []
    for k in range(pieces + 1):
        if k < pieces:
            image = jnp.concatenate(
                [images[k][i * size : (i + 1) * size] for i in range(parts)], axis=1
            )
        else:
            image = far_ref[...]
        residual = residual_ref[k] - times(alpha_t, image)
        direction = residual + times(beta_t, direction_ref[k])
        new_residual[k] = residual
        new_direction[k] = direction
        directions.append(direction)
    out_ref[...] = apply_dense(directions[:pieces], matrix)


def last_image_kernel(mine_ref, other_ref, direction_ref, near_ref, gram_ref):
    last = direction_ref.shape[0] - 1
    near, far = add_halves(mine_ref, other_ref, direction_ref.shape[2])
    near_ref[...] = near
    gram_ref[...] = grams(near, [direction_ref[0]]) + grams(far, [direction_ref[last]])


def last_kernel(pieces, *refs):
    image_ref, direction_ref, residual_ref, norm_ref, solution_ref = refs[pieces : pieces + 5]
    new_solution, new_residual = refs[pieces + 5 :]
    size = image_ref.shape[0]
    curvature = add_up([ref[:, :size] for ref in refs[:pieces]])
    alpha_t = factor(solve_wide(widen(symmetric(curvature)), norm_ref[...])[:, :size].T)
    new_solution[...] = solution_ref[...] + times(alpha_t, direction_ref[0])
    new_residual[...] = residual_ref[0] - times(alpha_t, image_ref[...])


def shape(*dims, dtype=F32):
    return jax.ShapeDtypeStruct(dims, dtype)


def per_device(tiles, tile_rows, tile_cols, tile_count, signs, vertex_weight, column_scale):
    sketch, rows_dev = signs.shape
    tile = tiles.shape[1]
    pieces = lax.axis_size("row")
    col_devices = lax.axis_size("col")
    group = col_devices * rows_dev
    depth = pieces * rows_dev

    def swap(value, mask):
        return lax.ppermute(value, "row", [(i, i ^ mask) for i in range(pieces)])

    def around(value, forward=True):
        if not forward:
            return [value] + [swap(value, k) for k in range(1, pieces)]
        even = [value] + [swap(value, k) for k in range(2, pieces, 2)]
        odd = [swap(piece, 1) for piece in even]
        return [piece for pair in zip(even, odd) for piece in pair]

    def across(value):
        return lax.ppermute(
            value, "col", [(i, (i + 1) % col_devices) for i in range(col_devices)]
        )

    right_side = signs.astype(F32) * vertex_weight[None, :] * column_scale[:, None]
    blocks = around(right_side, forward=False) + [across(right_side)]

    matrix = shape(2, depth, group, dtype=BF16)
    total = shape(depth // tile, group // tile, tile, tile)
    place = jnp.stack([lax.axis_index("row"), lax.axis_index("col")]).astype(jnp.int32)
    lists = jnp.concatenate([tile_rows, tile_cols, tile_count, place])
    dense = pl.pallas_call(
        functools.partial(dense_kernel, rows_dev, col_devices),
        out_shape=matrix,
        in_specs=[SMEM, HBM],
        out_specs=VMEM,
        scratch_shapes=[
            pltpu.VMEM(tiles.shape, BF16),
            pltpu.VMEM(total.shape, F32),
            pltpu.SemaphoreType.DMA((CHUNKS,)),
        ],
        compiler_params=params(tiles, total, matrix),
        cost_estimate=pl.CostEstimate(
            flops=4 * tiles.size, bytes_accessed=4 * tiles.size, transcendentals=0
        ),
        name="dense",
    )(lists, pltpu.with_memory_space_constraint(tiles, pltpu.HBM))

    state = shape(pieces + 1, sketch, rows_dev)
    small = shape(sketch, LANES)
    piece = shape(sketch, rows_dev)
    payload = shape(sketch * (rows_dev // LANES + 1), LANES)

    partial_sum, direction = pl.pallas_call(
        functools.partial(first_kernel, pieces),
        out_shape=(shape(sketch, group + LANES), state),
        in_specs=[VMEM] * (pieces + 2),
        out_specs=(VMEM, VMEM),
        compiler_params=params(matrix, state, state),
        name="first",
    )(*blocks, dense)
    residual = direction
    norm = None
    solution = None
    for iteration in range(ITERS - 1):
        first = iteration == 0
        outs = pl.pallas_call(
            functools.partial(image_kernel, first),
            out_shape=(payload, piece) + ((small,) if first else ()),
            in_specs=[VMEM] * 4,
            out_specs=(VMEM,) * (3 if first else 2),
            compiler_params=params(state, state),
            name="image",
        )(partial_sum, across(partial_sum), direction, residual)
        image, far = outs[:2]
        if first:
            norm = outs[2]
        inverse = pl.pallas_call(
            inverse_kernel,
            out_shape=small,
            in_specs=[VMEM],
            out_specs=VMEM,
            compiler_params=params(),
            name="inverse",
        )(norm)
        given = () if first else (solution,)
        partial_sum, direction, residual, norm, solution = pl.pallas_call(
            functools.partial(step_kernel, pieces, not first),
            out_shape=(shape(sketch, group), state, state, small, piece),
            in_specs=[VMEM] * (pieces + 6 + len(given)),
            out_specs=(VMEM,) * 5,
            compiler_params=params(matrix, state, state, state, state, state),
            name="step",
        )(*around(image), far, direction, residual, norm, inverse, dense, *given)
    image, gram = pl.pallas_call(
        last_image_kernel,
        out_shape=(piece, small),
        in_specs=[VMEM] * 3,
        out_specs=(VMEM, VMEM),
        compiler_params=params(state),
        name="last_image",
    )(partial_sum, across(partial_sum), direction)
    return pl.pallas_call(
        functools.partial(last_kernel, pieces),
        out_shape=(piece, piece),
        in_specs=[VMEM] * (pieces + 5),
        out_specs=(VMEM, VMEM),
        compiler_params=params(state, state, state),
        name="last",
    )(*around(gram), image, direction, residual, norm, solution)


def solution(mesh):
    return jax.shard_map(
        per_device,
        mesh=mesh,
        in_specs=(
            P(("row", "col"), None, None),
            P(("row", "col")),
            P(("row", "col")),
            P(("row", "col")),
            P("rhs", ("row", "col")),
            P(("row", "col")),
            P("rhs"),
        ),
        out_specs=(P("rhs", ("row", "col")), P("rhs", ("row", "col"))),
        check_vma=False,
    )
```

time: 90 us -> 73.1 us (0.81); the launches traced: 89.2 us -> 73.3 us
  starting transfers between devices: 17.4 us -> 38 us
  local copies, waits for them, and re-layouts: 12.8 us -> 0.77 us
  blocking collectives: 10.8 us -> 0 us
  waiting for transfers between devices: 25.7 us -> 16.1 us
  Pallas kernels: 20.2 us -> 16.2 us
    ppermute x0 -> x28, starting transfers between devices: none -> 37.5 us  [swap(): return lax.ppermute(value, 'row', [(i, i ^ mask) for i in range(pieces)])]
    all_to_all x3 -> x0, waiting for transfers between devices: 22.3 us -> none  [around(): return lax.all_to_all(values, 'row', 0, 0)]
    all_to_all x3 -> x0, starting transfers between devices: 16.7 us -> none  [around(): return lax.all_to_all(values, 'row', 0, 0)]
    ppermute x0 -> x28, waiting for transfers between devices: none -> 12.3 us  [swap(): return lax.ppermute(value, 'row', [(i, i ^ mask) for i in range(pieces)])]
    unnamed x14 -> x0, local copies, waits for them, and re-layouts: 12.1 us -> none
    all_to_all x1 -> x0, blocking collectives: 10.8 us -> none  [around(): return lax.all_to_all(values, 'row', 0, 0)]
    pallas_call x2, Pallas kernels: 3.45 us -> 0.49 us  [per_device(): pl.pallas_call(functools.partial(image_kernel, first), out_shape=(payload...]
    pallas_call x2, Pallas kernels: 6.02 us -> 4.93 us  [per_device(): pl.pallas_call(functools.partial(step_kernel, pieces, not first), out_sha...]
  transfers between devices with their start and end apart: 7 -> 32, of which waited for: 5 -> 15; matrix products, arithmetic and copies ran while one was open for 0% -> 1% of each run, Pallas kernels for 7% -> 10%
where the time goes in v3:
time: 73.1 us; the launch traced here: 73.3 us
  starting transfers between devices  38 us (52%)
  Pallas kernels  16.2 us (22%)
  waiting for transfers between devices  16.1 us (22%)
  between operations  1.41 us (2%)
  other arithmetic  0.85 us (1%)
  local copies, waits for them, and re-layouts  0.77 us (1%)
    ppermute x28, starting transfers between devices, swap(): return lax.ppermute(value, 'row', [(i, i ^ mask) for i in range(pieces)])  37.5 us
    ppermute x28, waiting for transfers between devices, swap(): return lax.ppermute(value, 'row', [(i, i ^ mask) for i in range(pieces)])  12.3 us
    pallas_call x1, Pallas kernels, per_device(): pl.pallas_call(functools.partial(dense_kernel, rows_dev, col_devices), ou...  5.57 us
    pallas_call x2, Pallas kernels, per_device(): pl.pallas_call(functools.partial(step_kernel, pieces, not first), out_sha...  4.93 us
    ppermute x4, waiting for transfers between devices, across(): lax.ppermute(value, 'col', [(i, (i + 1) % col_devices) for i in range(col...  3.79 us
    pallas_call x2, Pallas kernels, per_device(): pl.pallas_call(inverse_kernel, out_shape=small, in_specs=[VMEM], out_spec...  1.9 us
    pallas_call x1, Pallas kernels, per_device(): pl.pallas_call(functools.partial(last_kernel, pieces), out_shape=(piece,...  1.84 us
  transfers between devices with their start and end apart: 32, of which 15 were waited for; matrix products, arithmetic and copies ran while one was open for 1% of the time, Pallas kernels for 10%

profile of v3, /device:TPU:0, one launch (start us, length us, event | category | flops | bytes accessed | tf_op | source)
XLA Modules:
  0.0 73.3 jit_solution(17075231308479454127)
XLA Ops:
  0.6 0.8 %multiply_multiply_fusion.refs_0_ = f32[32,256]{1,0:T(8,128)S(1)} fusion(s32[32,256]{1,0:T(8,128)} %param.11, f32[32]{0:T(128)} %param.13, f32[256]{0:T(256)} %param.12), kind=kLoop, calls=%fused_computation | loop fusion | flops 24576 | bytes 66688 | tf_op jit(solution)/shard_map/mul | solution.py:289
  1.5 0.5 collective-permute-start.7
  1.9 5.6 %collective-permute-start.6 = (f32[32,256]{1,0:T(8,128)S(1)}, f32[32,256]{1,0:T(8,128)S(1)}, u32[]{:S(2)}, u32[]{:S(2)}) collective-permute-start(f32[32,256]{1,0:T(8,128)S(1)} %multiply_multiply_fusion.refs_0_), channel_id=1, source_target_pairs={{0,14},{2,12},{4,10},{6,8},{8,6},{10,4},{12,2},{14,0},{1,15},{3,13... | collective-permute-start | bytes 98312 | tf_op jit(solution)/shard_map/ppermute | solution.py:275
  7.6 0.2 collective-permute-start.5
  7.8 0.7 %collective-permute-start.4 = (f32[32,256]{1,0:T(8,128)S(1)}, f32[32,256]{1,0:T(8,128)S(1)}, u32[]{:S(2)}, u32[]{:S(2)}) collective-permute-start(f32[32,256]{1,0:T(8,128)S(1)} %multiply_multiply_fusion.refs_0_), channel_id=1, source_target_pairs={{0,10},{2,8},{4,14},{6,12},{8,2},{10,0},{12,6},{14,4},{1,11},{3,9}... | collective-permute-start | bytes 98312 | tf_op jit(solution)/shard_map/ppermute | solution.py:275
  8.5 2.1 %collective-permute-start.3 = (f32[32,256]{1,0:T(8,128)S(1)}, f32[32,256]{1,0:T(8,128)S(1)}, u32[]{:S(2)}, u32[]{:S(2)}) collective-permute-start(f32[32,256]{1,0:T(8,128)S(1)} %multiply_multiply_fusion.refs_0_), channel_id=1, source_target_pairs={{0,8},{2,10},{4,12},{6,14},{8,0},{10,2},{12,4},{14,6},{1,9},{3,11}... | collective-permute-start | bytes 98312 | tf_op jit(solution)/shard_map/ppermute | solution.py:275
  10.6 0.0 collective-permute-done.7.refs_8_
  10.6 2.3 %collective-permute-start.2 = (f32[32,256]{1,0:T(8,128)S(1)}, f32[32,256]{1,0:T(8,128)S(1)}, u32[]{:S(2)}, u32[]{:S(2)}) collective-permute-start(f32[32,256]{1,0:T(8,128)S(1)} %multiply_multiply_fusion.refs_0_), channel_id=1, source_target_pairs={{0,6},{2,4},{4,2},{6,0},{8,14},{10,12},{12,10},{14,8},{1,7},{3,5},... | collective-permute-start | bytes 98312 | tf_op jit(solution)/shard_map/ppermute | solution.py:275
  12.9 0.0 collective-permute-done.6.refs_7_
  12.9 0.8 %collective-permute-start.1 = (f32[32,256]{1,0:T(8,128)S(1)}, f32[32,256]{1,0:T(8,128)S(1)}, u32[]{:S(2)}, u32[]{:S(2)}) collective-permute-start(f32[32,256]{1,0:T(8,128)S(1)} %multiply_multiply_fusion.refs_0_), channel_id=1, source_target_pairs={{0,4},{2,6},{4,0},{6,2},{8,12},{10,14},{12,8},{14,10},{1,5},{3,7},... | collective-permute-start | bytes 98312 | tf_op jit(solution)/shard_map/ppermute | solution.py:275
  13.7 0.4 collective-permute-start
  14.7 0.8 %concatenate.3.lists_ref = s32[263]{0:T(512)S(1)} concatenate(s32[130]{0:T(256)} %param.8, s32[130]{0:T(256)} %param.9, s32[1]{0:T(128)S(6)} %copy.9, s32[1]{0:T(128)} %bitcast, s32[1]{0:T(128)} %bitcast.1), dimensions={0} | concatenate | bytes 2104 | tf_op jit(solution)/shard_map/concatenate | solution.py:295
  15.5 5.6 %dense.1.refs_9_.refs_13_ = bf16[2,2048,512]{2,1,0:T(8,128)(2,1)S(1)} custom-call(s32[263]{0:T(512)S(1)} %concatenate.3.lists_ref, bf16[130,128,128]{2,1,0:T(8,128)(2,1)} %tiles_ref.1), custom_call_target="tpu_custom_call" | custom-call | flops 8519680 | bytes 8519680 | tf_op jit(solution)/shard_map/dense/pallas_call | solution.py:296
  21.1 0.0 collective-permute-done.3.refs_4_
  21.1 0.0 collective-permute-done.2.refs_3_
  21.1 0.0 collective-permute-done.refs_1_
  21.1 1.2 %first.1 = (f32[32,640]{1,0:T(8,128)S(1)}, f32[9,32,256]{2,1,0:T(8,128)S(1)}) custom-call(f32[32,256]{1,0:T(8,128)S(1)} %multiply_multiply_fusion.refs_0_, f32[32,256]{1,0:T(8,128)S(1)} %collective-permute-done.refs_1_, f32[32,256]{1,0:T(8,128)S(1)} %collective-permute-done.1.refs_2_, f32[32,256]{1,0:T(8,128)S(1)} %collective-permute-done.2.refs_3_, ...), custom_call_target="tpu_custom_call" | custom-call | tf_op jit(solution)/shard_map/first/pallas_call | solution.py:318
  22.3 0.1 collective-permute-start.8
  22.4 1.3 %collective-permute-done.8.other_ref = f32[32,640]{1,0:T(8,128)S(1)} collective-permute-done((f32[32,640]{1,0:T(8,128)S(1)}, f32[32,640]{1,0:T(8,128)S(1)}, u32[]{:S(2)}, u32[]{:S(2)}) %collective-permute-start.8) | collective-permute-done | bytes 81952 | tf_op jit(solution)/shard_map/ppermute | solution.py:285
  23.7 0.2 image.2
  23.9 3.7 %collective-permute-start.14 = (f32[96,128]{1,0:T(8,128)S(1)}, f32[96,128]{1,0:T(8,128)S(1)}, u32[]{:S(2)}, u32[]{:S(2)}) collective-permute-start(f32[96,128]{1,0:T(8,128)S(1)} %get-tuple-element.23.refs_0_), channel_id=1, source_target_pairs={{0,12},{2,14},{4,8},{6,10},{8,4},{10,6},{12,0},{14,2},{1,13},{3,15... | collective-permute-start | bytes 147464 | tf_op jit(solution)/shard_map/ppermute | solution.py:275
  27.6 0.0 collective-permute-start.12
  27.6 0.8 %collective-permute-start.10 = (f32[96,128]{1,0:T(8,128)S(1)}, f32[96,128]{1,0:T(8,128)S(1)}, u32[]{:S(2)}, u32[]{:S(2)}) collective-permute-start(f32[96,128]{1,0:T(8,128)S(1)} %get-tuple-element.23.refs_0_), channel_id=1, source_target_pairs={{0,4},{2,6},{4,0},{6,2},{8,12},{10,14},{12,8},{14,10},{1,5},{3,7},... | collective-permute-start | bytes 147464 | tf_op jit(solution)/shard_map/ppermute | solution.py:275
  28.4 1.6 %collective-permute-start.9 = (f32[96,128]{1,0:T(8,128)S(1)}, f32[96,128]{1,0:T(8,128)S(1)}, u32[]{:S(2)}, u32[]{:S(2)}) collective-permute-start(f32[96,128]{1,0:T(8,128)S(1)} %get-tuple-element.23.refs_0_), channel_id=1, source_target_pairs={{0,2},{2,0},{4,6},{6,4},{8,10},{10,8},{12,14},{14,12},{1,3},{3,1},... | collective-permute-start | bytes 147464 | tf_op jit(solution)/shard_map/ppermute | solution.py:275
  30.0 0.2 collective-permute-done.14.refs_6_
  30.1 1.2 %collective-permute-start.15 = (f32[96,128]{1,0:T(8,128)S(1)}, f32[96,128]{1,0:T(8,128)S(1)}, u32[]{:S(2)}, u32[]{:S(2)}) collective-permute-start(f32[96,128]{1,0:T(8,128)S(1)} %collective-permute-done.14.refs_6_), channel_id=1, source_target_pairs={{0,2},{2,0},{4,6},{6,4},{8,10},{10,8},{12,14},{14,12},{1,3},{3,1},... | collective-permute-start | bytes 147464 | tf_op jit(solution)/shard_map/ppermute | solution.py:275
  31.4 1.3 %collective-permute-done.12.refs_4_ = f32[96,128]{1,0:T(8,128)S(1)} collective-permute-done((f32[96,128]{1,0:T(8,128)S(1)}, f32[96,128]{1,0:T(8,128)S(1)}, u32[]{:S(2)}, u32[]{:S(2)}) %collective-permute-start.12) | collective-permute-done | bytes 49184 | tf_op jit(solution)/shard_map/ppermute | solution.py:275
  32.7 1.7 %collective-permute-start.13 = (f32[96,128]{1,0:T(8,128)S(1)}, f32[96,128]{1,0:T(8,128)S(1)}, u32[]{:S(2)}, u32[]{:S(2)}) collective-permute-start(f32[96,128]{1,0:T(8,128)S(1)} %collective-permute-done.12.refs_4_), channel_id=1, source_target_pairs={{0,2},{2,0},{4,6},{6,4},{8,10},{10,8},{12,14},{14,12},{1,3},{3,1},... | collective-permute-start | bytes 147464 | tf_op jit(solution)/shard_map/ppermute | solution.py:275
  34.4 0.0 collective-permute-done.10.refs_2_
  34.4 0.3 collective-permute-start.11
  34.7 0.9 %inverse.2.refs_12_ = f32[32,128]{1,0:T(8,128)S(1)} custom-call(f32[32,128]{1,0:T(8,128)S(1)} %get-tuple-element.25.norm_ref.refs_11_), custom_call_target="tpu_custom_call" | custom-call | tf_op jit(solution)/shard_map/inverse/pallas_call | solution.py:342
  35.6 0.0 collective-permute-done.9.refs_1_
  35.6 0.0 collective-permute-done.15.refs_7_
  35.6 1.2 %collective-permute-done.13.refs_5_ = f32[96,128]{1,0:T(8,128)S(1)} collective-permute-done((f32[96,128]{1,0:T(8,128)S(1)}, f32[96,128]{1,0:T(8,128)S(1)}, u32[]{:S(2)}, u32[]{:S(2)}) %collective-permute-start.13) | collective-permute-done | bytes 49184 | tf_op jit(solution)/shard_map/ppermute | solution.py:275
  36.9 1.6 %collective-permute-done.11.refs_3_ = f32[96,128]{1,0:T(8,128)S(1)} collective-permute-done((f32[96,128]{1,0:T(8,128)S(1)}, f32[96,128]{1,0:T(8,128)S(1)}, u32[]{:S(2)}, u32[]{:S(2)}) %collective-permute-start.11) | collective-permute-done | bytes 49184 | tf_op jit(solution)/shard_map/ppermute | solution.py:275
  38.5 2.5 %step.2 = (f32[32,512]{1,0:T(8,128)S(1)}, f32[9,32,256]{2,1,0:T(8,128)S(1)}, f32[9,32,256]{2,1,0:T(8,128)S(1)}, f32[32,128]{1,0:T(8,128)S(1)}, f32[32,256]{1,0:T(8,128)S(1)}) custom-call(f32[96,128]{1,0:T(8,128)S(1)} %get-tuple-element.23.refs_0_, f32[96,128]{1,0:T(8,128)S(1)} %collective-permute-done.9.refs_1_, ...), custom_call_target="tpu_custom_call" | custom-call | tf_op jit(solution)/shard_map/step/pallas_call | solution.py:351
  41.0 0.0 collective-permute-start.16
  41.0 1.3 %collective-permute-done.16.other_ref = f32[32,512]{1,0:T(8,128)S(1)} collective-permute-done((f32[32,512]{1,0:T(8,128)S(1)}, f32[32,512]{1,0:T(8,128)S(1)}, u32[]{:S(2)}, u32[]{:S(2)}) %collective-permute-start.16) | collective-permute-done | bytes 65568 | tf_op jit(solution)/shard_map/ppermute | solution.py:285
  42.2 0.2 image.3
  42.5 2.9 %collective-permute-start.22 = (f32[96,128]{1,0:T(8,128)S(1)}, f32[96,128]{1,0:T(8,128)S(1)}, u32[]{:S(2)}, u32[]{:S(2)}) collective-permute-start(f32[96,128]{1,0:T(8,128)S(1)} %get-tuple-element.29.refs_0_), channel_id=1, source_target_pairs={{0,12},{2,14},{4,8},{6,10},{8,4},{10,6},{12,0},{14,2},{1,13},{3,15... | collective-permute-start | bytes 147464 | tf_op jit(solution)/shard_map/ppermute | solution.py:275
  45.4 1.5 %collective-permute-start.18 = (f32[96,128]{1,0:T(8,128)S(1)}, f32[96,128]{1,0:T(8,128)S(1)}, u32[]{:S(2)}, u32[]{:S(2)}) collective-permute-start(f32[96,128]{1,0:T(8,128)S(1)} %get-tuple-element.29.refs_0_), channel_id=1, source_target_pairs={{0,4},{2,6},{4,0},{6,2},{8,12},{10,14},{12,8},{14,10},{1,5},{3,7},... | collective-permute-start | bytes 147464 | tf_op jit(solution)/shard_map/ppermute | solution.py:275
  46.9 0.5 collective-permute-start.17
  47.5 1.5 %collective-permute-done.22.refs_6_ = f32[96,128]{1,0:T(8,128)S(1)} collective-permute-done((f32[96,128]{1,0:T(8,128)S(1)}, f32[96,128]{1,0:T(8,128)S(1)}, u32[]{:S(2)}, u32[]{:S(2)}) %collective-permute-start.22) | collective-permute-done | bytes 49184 | tf_op jit(solution)/shard_map/ppermute | solution.py:275
  49.0 0.1 collective-permute-start.23
  49.0 1.5 %collective-permute-done.20.refs_4_ = f32[96,128]{1,0:T(8,128)S(1)} collective-permute-done((f32[96,128]{1,0:T(8,128)S(1)}, f32[96,128]{1,0:T(8,128)S(1)}, u32[]{:S(2)}, u32[]{:S(2)}) %collective-permute-start.20) | collective-permute-done | bytes 49184 | tf_op jit(solution)/shard_map/ppermute | solution.py:275
  50.5 0.9 %collective-permute-start.21 = (f32[96,128]{1,0:T(8,128)S(1)}, f32[96,128]{1,0:T(8,128)S(1)}, u32[]{:S(2)}, u32[]{:S(2)}) collective-permute-start(f32[96,128]{1,0:T(8,128)S(1)} %collective-permute-done.20.refs_4_), channel_id=1, source_target_pairs={{0,2},{2,0},{4,6},{6,4},{8,10},{10,8},{12,14},{14,12},{1,3},{3,1},... | collective-permute-start | bytes 147464 | tf_op jit(solution)/shard_map/ppermute | solution.py:275
  51.4 1.2 %collective-permute-start.19 = (f32[96,128]{1,0:T(8,128)S(1)}, f32[96,128]{1,0:T(8,128)S(1)}, u32[]{:S(2)}, u32[]{:S(2)}) collective-permute-start(f32[96,128]{1,0:T(8,128)S(1)} %collective-permute-done.18.refs_2_), channel_id=1, source_target_pairs={{0,2},{2,0},{4,6},{6,4},{8,10},{10,8},{12,14},{14,12},{1,3},{3,1},... | collective-permute-start | bytes 147464 | tf_op jit(solution)/shard_map/ppermute | solution.py:275
  52.6 0.9 %inverse.3.refs_12_ = f32[32,128]{1,0:T(8,128)S(1)} custom-call(f32[32,128]{1,0:T(8,128)S(1)} %get-tuple-element.31.norm_ref.refs_11_), custom_call_target="tpu_custom_call" | custom-call | tf_op jit(solution)/shard_map/inverse/pallas_call | solution.py:342
  53.5 1.1 %collective-permute-done.21.refs_5_ = f32[96,128]{1,0:T(8,128)S(1)} collective-permute-done((f32[96,128]{1,0:T(8,128)S(1)}, f32[96,128]{1,0:T(8,128)S(1)}, u32[]{:S(2)}, u32[]{:S(2)}) %collective-permute-start.21) | collective-permute-done | bytes 49184 | tf_op jit(solution)/shard_map/ppermute | solution.py:275
  54.6 0.8 %collective-permute-done.19.refs_3_ = f32[96,128]{1,0:T(8,128)S(1)} collective-permute-done((f32[96,128]{1,0:T(8,128)S(1)}, f32[96,128]{1,0:T(8,128)S(1)}, u32[]{:S(2)}, u32[]{:S(2)}) %collective-permute-start.19) | collective-permute-done | bytes 49184 | tf_op jit(solution)/shard_map/ppermute | solution.py:275
  55.5 2.5 %step.3 = (f32[32,512]{1,0:T(8,128)S(1)}, f32[9,32,256]{2,1,0:T(8,128)S(1)}, f32[9,32,256]{2,1,0:T(8,128)S(1)}, f32[32,128]{1,0:T(8,128)S(1)}, f32[32,256]{1,0:T(8,128)S(1)}) custom-call(f32[96,128]{1,0:T(8,128)S(1)} %get-tuple-element.29.refs_0_, f32[96,128]{1,0:T(8,128)S(1)} %collective-permute-done.17.refs_1_, ...), custom_call_target="tpu_custom_call" | custom-call | tf_op jit(solution)/shard_map/step/pallas_call | solution.py:351
  57.9 1.3 %collective-permute-done.24.other_ref = f32[32,512]{1,0:T(8,128)S(1)} collective-permute-done((f32[32,512]{1,0:T(8,128)S(1)}, f32[32,512]{1,0:T(8,128)S(1)}, u32[]{:S(2)}, u32[]{:S(2)}) %collective-permute-start.24) | collective-permute-done | bytes 65568 | tf_op jit(solution)/shard_map/ppermute | solution.py:285
  59.2 0.2 last_image.1
  59.5 2.6 %collective-permute-start.30 = (f32[32,128]{1,0:T(8,128)S(1)}, f32[32,128]{1,0:T(8,128)S(1)}, u32[]{:S(2)}, u32[]{:S(2)}) collective-permute-start(f32[32,128]{1,0:T(8,128)S(1)} %get-tuple-element.35.refs_0_), channel_id=1, source_target_pairs={{0,12},{2,14},{4,8},{6,10},{8,4},{10,6},{12,0},{14,2},{1,13},{3,15... | collective-permute-start | bytes 49160 | tf_op jit(solution)/shard_map/ppermute | solution.py:275
  62.1 1.8 %collective-permute-start.26 = (f32[32,128]{1,0:T(8,128)S(1)}, f32[32,128]{1,0:T(8,128)S(1)}, u32[]{:S(2)}, u32[]{:S(2)}) collective-permute-start(f32[32,128]{1,0:T(8,128)S(1)} %get-tuple-element.35.refs_0_), channel_id=1, source_target_pairs={{0,4},{2,6},{4,0},{6,2},{8,12},{10,14},{12,8},{14,10},{1,5},{3,7},... | collective-permute-start | bytes 49160 | tf_op jit(solution)/shard_map/ppermute | solution.py:275
  63.9 1.2 %collective-permute-start.25 = (f32[32,128]{1,0:T(8,128)S(1)}, f32[32,128]{1,0:T(8,128)S(1)}, u32[]{:S(2)}, u32[]{:S(2)}) collective-permute-start(f32[32,128]{1,0:T(8,128)S(1)} %get-tuple-element.35.refs_0_), channel_id=1, source_target_pairs={{0,2},{2,0},{4,6},{6,4},{8,10},{10,8},{12,14},{14,12},{1,3},{3,1},... | collective-permute-start | bytes 49160 | tf_op jit(solution)/shard_map/ppermute | solution.py:275
  65.1 1.3 %collective-permute-start.31 = (f32[32,128]{1,0:T(8,128)S(1)}, f32[32,128]{1,0:T(8,128)S(1)}, u32[]{:S(2)}, u32[]{:S(2)}) collective-permute-start(f32[32,128]{1,0:T(8,128)S(1)} %collective-permute-done.30.refs_6_), channel_id=1, source_target_pairs={{0,2},{2,0},{4,6},{6,4},{8,10},{10,8},{12,14},{14,12},{1,3},{3,1},... | collective-permute-start | bytes 49160 | tf_op jit(solution)/shard_map/ppermute | solution.py:275
  66.4 0.3 collective-permute-done.28.refs_4_
  66.7 1.0 %collective-permute-start.29 = (f32[32,128]{1,0:T(8,128)S(1)}, f32[32,128]{1,0:T(8,128)S(1)}, u32[]{:S(2)}, u32[]{:S(2)}) collective-permute-start(f32[32,128]{1,0:T(8,128)S(1)} %collective-permute-done.28.refs_4_), channel_id=1, source_target_pairs={{0,2},{2,0},{4,6},{6,4},{8,10},{10,8},{12,14},{14,12},{1,3},{3,1},... | collective-permute-start | bytes 49160 | tf_op jit(solution)/shard_map/ppermute | solution.py:275
  67.7 1.0 %collective-permute-start.27 = (f32[32,128]{1,0:T(8,128)S(1)}, f32[32,128]{1,0:T(8,128)S(1)}, u32[]{:S(2)}, u32[]{:S(2)}) collective-permute-start(f32[32,128]{1,0:T(8,128)S(1)} %collective-permute-done.26.refs_2_), channel_id=1, source_target_pairs={{0,2},{2,0},{4,6},{6,4},{8,10},{10,8},{12,14},{14,12},{1,3},{3,1},... | collective-permute-start | bytes 49160 | tf_op jit(solution)/shard_map/ppermute | solution.py:275
  68.8 0.1 collective-permute-done.31.refs_7_
  68.9 1.6 %collective-permute-done.29.refs_5_ = f32[32,128]{1,0:T(8,128)S(1)} collective-permute-done((f32[32,128]{1,0:T(8,128)S(1)}, f32[32,128]{1,0:T(8,128)S(1)}, u32[]{:S(2)}, u32[]{:S(2)}) %collective-permute-start.29) | collective-permute-done | bytes 16416 | tf_op jit(solution)/shard_map/ppermute | solution.py:275
  70.5 1.0 %collective-permute-done.27.refs_3_ = f32[32,128]{1,0:T(8,128)S(1)} collective-permute-done((f32[32,128]{1,0:T(8,128)S(1)}, f32[32,128]{1,0:T(8,128)S(1)}, u32[]{:S(2)}, u32[]{:S(2)}) %collective-permute-start.27) | collective-permute-done | bytes 16416 | tf_op jit(solution)/shard_map/ppermute | solution.py:275
  71.5 1.8 %last.1 = (f32[32,256]{1,0:T(8,128)}, f32[32,256]{1,0:T(8,128)}) custom-call(f32[32,128]{1,0:T(8,128)S(1)} %get-tuple-element.35.refs_0_, f32[32,128]{1,0:T(8,128)S(1)} %collective-permute-done.25.refs_1_, f32[32,128]{1,0:T(8,128)S(1)} %collective-permute-done.26.refs_2_, f32[32,128]{1,0:T(8,128)S(1)} %collective-permute-done.27.refs_3_, ...), custom_call_target="tpu_custom_call" | custom-call | tf_op jit(solution)/shard_map/last/pallas_call | solution.py:367
  (12 shorter events, 0.0 us)
Async XLA Ops:
  1.5 9.1 %collective-permute-start.7 = (f32[32,256]{1,0:T(8,128)S(1)}, f32[32,256]{1,0:T(8,128)S(1)}, u32[]{:S(2)}, u32[]{:S(2)}) collective-permute-start(f32[32,256]{1,0:T(8,128)S(1)} %multiply_multiply_fusion.refs_0_), channel_id=1, source_target_pairs={{0,1},{1,0},{2,3},{3,2},{4,5},{5,4},{6,7},{7,6},{8,9},{9,8},{10,11... | collective-permute-start | bytes 98312 | tf_op jit(solution)/shard_map/ppermute | solution.py:285
  1.9 10.9 %collective-permute-start.6 = (f32[32,256]{1,0:T(8,128)S(1)}, f32[32,256]{1,0:T(8,128)S(1)}, u32[]{:S(2)}, u32[]{:S(2)}) collective-permute-start(f32[32,256]{1,0:T(8,128)S(1)} %multiply_multiply_fusion.refs_0_), channel_id=1, source_target_pairs={{0,14},{2,12},{4,10},{6,8},{8,6},{10,4},{12,2},{14,0},{1,15},{3,13... | collective-permute-start | bytes 98312 | tf_op jit(solution)/shard_map/ppermute | solution.py:275
  7.6 6.1 %collective-permute-start.5 = (f32[32,256]{1,0:T(8,128)S(1)}, f32[32,256]{1,0:T(8,128)S(1)}, u32[]{:S(2)}, u32[]{:S(2)}) collective-permute-start(f32[32,256]{1,0:T(8,128)S(1)} %multiply_multiply_fusion.refs_0_), channel_id=1, source_target_pairs={{0,12},{2,14},{4,8},{6,10},{8,4},{10,6},{12,0},{14,2},{1,13},{3,15... | collective-permute-start | bytes 98312 | tf_op jit(solution)/shard_map/ppermute | solution.py:275
  7.8 13.3 %collective-permute-start.4 = (f32[32,256]{1,0:T(8,128)S(1)}, f32[32,256]{1,0:T(8,128)S(1)}, u32[]{:S(2)}, u32[]{:S(2)}) collective-permute-start(f32[32,256]{1,0:T(8,128)S(1)} %multiply_multiply_fusion.refs_0_), channel_id=1, source_target_pairs={{0,10},{2,8},{4,14},{6,12},{8,2},{10,0},{12,6},{14,4},{1,11},{3,9}... | collective-permute-start | bytes 98312 | tf_op jit(solution)/shard_map/ppermute | solution.py:275
  8.5 12.6 %collective-permute-start.3 = (f32[32,256]{1,0:T(8,128)S(1)}, f32[32,256]{1,0:T(8,128)S(1)}, u32[]{:S(2)}, u32[]{:S(2)}) collective-permute-start(f32[32,256]{1,0:T(8,128)S(1)} %multiply_multiply_fusion.refs_0_), channel_id=1, source_target_pairs={{0,8},{2,10},{4,12},{6,14},{8,0},{10,2},{12,4},{14,6},{1,9},{3,11}... | collective-permute-start | bytes 98312 | tf_op jit(solution)/shard_map/ppermute | solution.py:275
  10.6 10.5 %collective-permute-start.2 = (f32[32,256]{1,0:T(8,128)S(1)}, f32[32,256]{1,0:T(8,128)S(1)}, u32[]{:S(2)}, u32[]{:S(2)}) collective-permute-start(f32[32,256]{1,0:T(8,128)S(1)} %multiply_multiply_fusion.refs_0_), channel_id=1, source_target_pairs={{0,6},{2,4},{4,2},{6,0},{8,14},{10,12},{12,10},{14,8},{1,7},{3,5},... | collective-permute-start | bytes 98312 | tf_op jit(solution)/shard_map/ppermute | solution.py:275
  12.9 8.3 %collective-permute-start.1 = (f32[32,256]{1,0:T(8,128)S(1)}, f32[32,256]{1,0:T(8,128)S(1)}, u32[]{:S(2)}, u32[]{:S(2)}) collective-permute-start(f32[32,256]{1,0:T(8,128)S(1)} %multiply_multiply_fusion.refs_0_), channel_id=1, source_target_pairs={{0,4},{2,6},{4,0},{6,2},{8,12},{10,14},{12,8},{14,10},{1,5},{3,7},... | collective-permute-start | bytes 98312 | tf_op jit(solution)/shard_map/ppermute | solution.py:275
  13.7 7.5 %collective-permute-start = (f32[32,256]{1,0:T(8,128)S(1)}, f32[32,256]{1,0:T(8,128)S(1)}, u32[]{:S(2)}, u32[]{:S(2)}) collective-permute-start(f32[32,256]{1,0:T(8,128)S(1)} %multiply_multiply_fusion.refs_0_), channel_id=1, source_target_pairs={{0,2},{2,0},{4,6},{6,4},{8,10},{10,8},{12,14},{14,12},{1,3},{3,1},... | collective-permute-start | bytes 98312 | tf_op jit(solution)/shard_map/ppermute | solution.py:275
  22.3 1.3 %collective-permute-start.8 = (f32[32,640]{1,0:T(8,128)S(1)}, f32[32,640]{1,0:T(8,128)S(1)}, u32[]{:S(2)}, u32[]{:S(2)}) collective-permute-start(f32[32,640]{1,0:T(8,128)S(1)} %get-tuple-element.21.mine_ref), channel_id=1, source_target_pairs={{0,1},{1,0},{2,3},{3,2},{4,5},{5,4},{6,7},{7,6},{8,9},{9,8},{10,11... | collective-permute-start | bytes 245768 | tf_op jit(solution)/shard_map/ppermute | solution.py:285
  23.9 6.2 %collective-permute-start.14 = (f32[96,128]{1,0:T(8,128)S(1)}, f32[96,128]{1,0:T(8,128)S(1)}, u32[]{:S(2)}, u32[]{:S(2)}) collective-permute-start(f32[96,128]{1,0:T(8,128)S(1)} %get-tuple-element.23.refs_0_), channel_id=1, source_target_pairs={{0,12},{2,14},{4,8},{6,10},{8,4},{10,6},{12,0},{14,2},{1,13},{3,15... | collective-permute-start | bytes 147464 | tf_op jit(solution)/shard_map/ppermute | solution.py:275
  27.6 5.0 %collective-permute-start.12 = (f32[96,128]{1,0:T(8,128)S(1)}, f32[96,128]{1,0:T(8,128)S(1)}, u32[]{:S(2)}, u32[]{:S(2)}) collective-permute-start(f32[96,128]{1,0:T(8,128)S(1)} %get-tuple-element.23.refs_0_), channel_id=1, source_target_pairs={{0,8},{2,10},{4,12},{6,14},{8,0},{10,2},{12,4},{14,6},{1,9},{3,11}... | collective-permute-start | bytes 147464 | tf_op jit(solution)/shard_map/ppermute | solution.py:275
  27.6 6.8 %collective-permute-start.10 = (f32[96,128]{1,0:T(8,128)S(1)}, f32[96,128]{1,0:T(8,128)S(1)}, u32[]{:S(2)}, u32[]{:S(2)}) collective-permute-start(f32[96,128]{1,0:T(8,128)S(1)} %get-tuple-element.23.refs_0_), channel_id=1, source_target_pairs={{0,4},{2,6},{4,0},{6,2},{8,12},{10,14},{12,8},{14,10},{1,5},{3,7},... | collective-permute-start | bytes 147464 | tf_op jit(solution)/shard_map/ppermute | solution.py:275
  28.4 7.2 %collective-permute-start.9 = (f32[96,128]{1,0:T(8,128)S(1)}, f32[96,128]{1,0:T(8,128)S(1)}, u32[]{:S(2)}, u32[]{:S(2)}) collective-permute-start(f32[96,128]{1,0:T(8,128)S(1)} %get-tuple-element.23.refs_0_), channel_id=1, source_target_pairs={{0,2},{2,0},{4,6},{6,4},{8,10},{10,8},{12,14},{14,12},{1,3},{3,1},... | collective-permute-start | bytes 147464 | tf_op jit(solution)/shard_map/ppermute | solution.py:275
  30.1 5.5 %collective-permute-start.15 = (f32[96,128]{1,0:T(8,128)S(1)}, f32[96,128]{1,0:T(8,128)S(1)}, u32[]{:S(2)}, u32[]{:S(2)}) collective-permute-start(f32[96,128]{1,0:T(8,128)S(1)} %collective-permute-done.14.refs_6_), channel_id=1, source_target_pairs={{0,2},{2,0},{4,6},{6,4},{8,10},{10,8},{12,14},{14,12},{1,3},{3,1},... | collective-permute-start | bytes 147464 | tf_op jit(solution)/shard_map/ppermute | solution.py:275
  32.7 4.2 %collective-permute-start.13 = (f32[96,128]{1,0:T(8,128)S(1)}, f32[96,128]{1,0:T(8,128)S(1)}, u32[]{:S(2)}, u32[]{:S(2)}) collective-permute-start(f32[96,128]{1,0:T(8,128)S(1)} %collective-permute-done.12.refs_4_), channel_id=1, source_target_pairs={{0,2},{2,0},{4,6},{6,4},{8,10},{10,8},{12,14},{14,12},{1,3},{3,1},... | collective-permute-start | bytes 147464 | tf_op jit(solution)/shard_map/ppermute | solution.py:275
  34.4 4.1 %collective-permute-start.11 = (f32[96,128]{1,0:T(8,128)S(1)}, f32[96,128]{1,0:T(8,128)S(1)}, u32[]{:S(2)}, u32[]{:S(2)}) collective-permute-start(f32[96,128]{1,0:T(8,128)S(1)} %collective-permute-done.10.refs_2_), channel_id=1, source_target_pairs={{0,2},{2,0},{4,6},{6,4},{8,10},{10,8},{12,14},{14,12},{1,3},{3,1},... | collective-permute-start | bytes 147464 | tf_op jit(solution)/shard_map/ppermute | solution.py:275
  41.0 1.3 %collective-permute-start.16 = (f32[32,512]{1,0:T(8,128)S(1)}, f32[32,512]{1,0:T(8,128)S(1)}, u32[]{:S(2)}, u32[]{:S(2)}) collective-permute-start(f32[32,512]{1,0:T(8,128)S(1)} %get-tuple-element.26.mine_ref), channel_id=1, source_target_pairs={{0,1},{1,0},{2,3},{3,2},{4,5},{5,4},{6,7},{7,6},{8,9},{9,8},{10,11... | collective-permute-start | bytes 196616 | tf_op jit(solution)/shard_map/ppermute | solution.py:285
  42.5 6.5 %collective-permute-start.22 = (f32[96,128]{1,0:T(8,128)S(1)}, f32[96,128]{1,0:T(8,128)S(1)}, u32[]{:S(2)}, u32[]{:S(2)}) collective-permute-start(f32[96,128]{1,0:T(8,128)S(1)} %get-tuple-element.29.refs_0_), channel_id=1, source_target_pairs={{0,12},{2,14},{4,8},{6,10},{8,4},{10,6},{12,0},{14,2},{1,13},{3,15... | collective-permute-start | bytes 147464 | tf_op jit(solution)/shard_map/ppermute | solution.py:275
  45.4 5.1 %collective-permute-start.20 = (f32[96,128]{1,0:T(8,128)S(1)}, f32[96,128]{1,0:T(8,128)S(1)}, u32[]{:S(2)}, u32[]{:S(2)}) collective-permute-start(f32[96,128]{1,0:T(8,128)S(1)} %get-tuple-element.29.refs_0_), channel_id=1, source_target_pairs={{0,8},{2,10},{4,12},{6,14},{8,0},{10,2},{12,4},{14,6},{1,9},{3,11}... | collective-permute-start | bytes 147464 | tf_op jit(solution)/shard_map/ppermute | solution.py:275
  45.4 6.0 %collective-permute-start.18 = (f32[96,128]{1,0:T(8,128)S(1)}, f32[96,128]{1,0:T(8,128)S(1)}, u32[]{:S(2)}, u32[]{:S(2)}) collective-permute-start(f32[96,128]{1,0:T(8,128)S(1)} %get-tuple-element.29.refs_0_), channel_id=1, source_target_pairs={{0,4},{2,6},{4,0},{6,2},{8,12},{10,14},{12,8},{14,10},{1,5},{3,7},... | collective-permute-start | bytes 147464 | tf_op jit(solution)/shard_map/ppermute | solution.py:275
  46.9 6.6 %collective-permute-start.17 = (f32[96,128]{1,0:T(8,128)S(1)}, f32[96,128]{1,0:T(8,128)S(1)}, u32[]{:S(2)}, u32[]{:S(2)}) collective-permute-start(f32[96,128]{1,0:T(8,128)S(1)} %get-tuple-element.29.refs_0_), channel_id=1, source_target_pairs={{0,2},{2,0},{4,6},{6,4},{8,10},{10,8},{12,14},{14,12},{1,3},{3,1},... | collective-permute-start | bytes 147464 | tf_op jit(solution)/shard_map/ppermute | solution.py:275
  49.0 4.6 %collective-permute-start.23 = (f32[96,128]{1,0:T(8,128)S(1)}, f32[96,128]{1,0:T(8,128)S(1)}, u32[]{:S(2)}, u32[]{:S(2)}) collective-permute-start(f32[96,128]{1,0:T(8,128)S(1)} %collective-permute-done.22.refs_6_), channel_id=1, source_target_pairs={{0,2},{2,0},{4,6},{6,4},{8,10},{10,8},{12,14},{14,12},{1,3},{3,1},... | collective-permute-start | bytes 147464 | tf_op jit(solution)/shard_map/ppermute | solution.py:275
  50.5 4.1 %collective-permute-start.21 = (f32[96,128]{1,0:T(8,128)S(1)}, f32[96,128]{1,0:T(8,128)S(1)}, u32[]{:S(2)}, u32[]{:S(2)}) collective-permute-start(f32[96,128]{1,0:T(8,128)S(1)} %collective-permute-done.20.refs_4_), channel_id=1, source_target_pairs={{0,2},{2,0},{4,6},{6,4},{8,10},{10,8},{12,14},{14,12},{1,3},{3,1},... | collective-permute-start | bytes 147464 | tf_op jit(solution)/shard_map/ppermute | solution.py:275
  51.4 4.1 %collective-permute-start.19 = (f32[96,128]{1,0:T(8,128)S(1)}, f32[96,128]{1,0:T(8,128)S(1)}, u32[]{:S(2)}, u32[]{:S(2)}) collective-permute-start(f32[96,128]{1,0:T(8,128)S(1)} %collective-permute-done.18.refs_2_), channel_id=1, source_target_pairs={{0,2},{2,0},{4,6},{6,4},{8,10},{10,8},{12,14},{14,12},{1,3},{3,1},... | collective-permute-start | bytes 147464 | tf_op jit(solution)/shard_map/ppermute | solution.py:275
  57.9 1.3 %collective-permute-start.24 = (f32[32,512]{1,0:T(8,128)S(1)}, f32[32,512]{1,0:T(8,128)S(1)}, u32[]{:S(2)}, u32[]{:S(2)}) collective-permute-start(f32[32,512]{1,0:T(8,128)S(1)} %get-tuple-element.33.mine_ref), channel_id=1, source_target_pairs={{0,1},{1,0},{2,3},{3,2},{4,5},{5,4},{6,7},{7,6},{8,9},{9,8},{10,11... | collective-permute-start | bytes 196616 | tf_op jit(solution)/shard_map/ppermute | solution.py:285
  59.5 5.6 %collective-permute-start.30 = (f32[32,128]{1,0:T(8,128)S(1)}, f32[32,128]{1,0:T(8,128)S(1)}, u32[]{:S(2)}, u32[]{:S(2)}) collective-permute-start(f32[32,128]{1,0:T(8,128)S(1)} %get-tuple-element.35.refs_0_), channel_id=1, source_target_pairs={{0,12},{2,14},{4,8},{6,10},{8,4},{10,6},{12,0},{14,2},{1,13},{3,15... | collective-permute-start | bytes 49160 | tf_op jit(solution)/shard_map/ppermute | solution.py:275
  62.1 4.6 %collective-permute-start.28 = (f32[32,128]{1,0:T(8,128)S(1)}, f32[32,128]{1,0:T(8,128)S(1)}, u32[]{:S(2)}, u32[]{:S(2)}) collective-permute-start(f32[32,128]{1,0:T(8,128)S(1)} %get-tuple-element.35.refs_0_), channel_id=1, source_target_pairs={{0,8},{2,10},{4,12},{6,14},{8,0},{10,2},{12,4},{14,6},{1,9},{3,11}... | collective-permute-start | bytes 49160 | tf_op jit(solution)/shard_map/ppermute | solution.py:275
  62.1 5.6 %collective-permute-start.26 = (f32[32,128]{1,0:T(8,128)S(1)}, f32[32,128]{1,0:T(8,128)S(1)}, u32[]{:S(2)}, u32[]{:S(2)}) collective-permute-start(f32[32,128]{1,0:T(8,128)S(1)} %get-tuple-element.35.refs_0_), channel_id=1, source_target_pairs={{0,4},{2,6},{4,0},{6,2},{8,12},{10,14},{12,8},{14,10},{1,5},{3,7},... | collective-permute-start | bytes 49160 | tf_op jit(solution)/shard_map/ppermute | solution.py:275
  63.9 4.9 %collective-permute-start.25 = (f32[32,128]{1,0:T(8,128)S(1)}, f32[32,128]{1,0:T(8,128)S(1)}, u32[]{:S(2)}, u32[]{:S(2)}) collective-permute-start(f32[32,128]{1,0:T(8,128)S(1)} %get-tuple-element.35.refs_0_), channel_id=1, source_target_pairs={{0,2},{2,0},{4,6},{6,4},{8,10},{10,8},{12,14},{14,12},{1,3},{3,1},... | collective-permute-start | bytes 49160 | tf_op jit(solution)/shard_map/ppermute | solution.py:275
  65.1 3.8 %collective-permute-start.31 = (f32[32,128]{1,0:T(8,128)S(1)}, f32[32,128]{1,0:T(8,128)S(1)}, u32[]{:S(2)}, u32[]{:S(2)}) collective-permute-start(f32[32,128]{1,0:T(8,128)S(1)} %collective-permute-done.30.refs_6_), channel_id=1, source_target_pairs={{0,2},{2,0},{4,6},{6,4},{8,10},{10,8},{12,14},{14,12},{1,3},{3,1},... | collective-permute-start | bytes 49160 | tf_op jit(solution)/shard_map/ppermute | solution.py:275
  66.7 3.7 %collective-permute-start.29 = (f32[32,128]{1,0:T(8,128)S(1)}, f32[32,128]{1,0:T(8,128)S(1)}, u32[]{:S(2)}, u32[]{:S(2)}) collective-permute-start(f32[32,128]{1,0:T(8,128)S(1)} %collective-permute-done.28.refs_4_), channel_id=1, source_target_pairs={{0,2},{2,0},{4,6},{6,4},{8,10},{10,8},{12,14},{14,12},{1,3},{3,1},... | collective-permute-start | bytes 49160 | tf_op jit(solution)/shard_map/ppermute | solution.py:275
  67.7 3.7 %collective-permute-start.27 = (f32[32,128]{1,0:T(8,128)S(1)}, f32[32,128]{1,0:T(8,128)S(1)}, u32[]{:S(2)}, u32[]{:S(2)}) collective-permute-start(f32[32,128]{1,0:T(8,128)S(1)} %collective-permute-done.26.refs_2_), channel_id=1, source_target_pairs={{0,2},{2,0},{4,6},{6,4},{8,10},{10,8},{12,14},{14,12},{1,3},{3,1},... | collective-permute-start | bytes 49160 | tf_op jit(solution)/shard_map/ppermute | solution.py:275

commit v4 on v3

--- a/solution.py
+++ b/solution.py
@@ -18,6 +18,7 @@
 VMEM = pl.BlockSpec(memory_space=pltpu.VMEM)
 SMEM = pl.BlockSpec(memory_space=pltpu.SMEM)
 HBM = pl.BlockSpec(memory_space=pltpu.HBM)
+ANY = pl.BlockSpec(memory_space=pl.ANY)
 
 
 def params(*arrays):
@@ -66,6 +67,23 @@
 def widen(matrix):
     rows, columns = matrix.shape
     return jnp.concatenate([matrix, jnp.zeros((rows, LANES - columns), F32)], axis=1)
+
+
+def pack(matrix):
+    rows = matrix.shape[0]
+    wide = widen(matrix)
+    folds = LANES // rows
+    height = rows // folds
+    total = wide[:height]
+    for i in range(1, folds):
+        total = total + pltpu.roll(wide[i * height : (i + 1) * height], i * rows, 1)
+    return total
+
+
+def unpack(folded, size):
+    folds = LANES // size
+    parts = [folded] + [pltpu.roll(folded, LANES - i * size, 1) for i in range(1, folds)]
+    return jnp.concatenate(parts, axis=0)[:, :size]
 
 
 def symmetric(matrix):
@@ -102,14 +120,21 @@
     return values[0]
 
 
-def dense_kernel(rows_dev, col_devices, lists_ref, tiles_ref, out_ref, held, total, sems):
+def gather_kernel(rows_dev, count_ref, rows_hbm, cols_hbm, tiles_ref, total, *scratch):
+    held, rows_ref, cols_ref, sems, list_sems = scratch
     slots, tile = tiles_ref.shape[:2]
     blocks = rows_dev // tile
-    live = lists_ref[2 * slots]
-    row_place = lists_ref[2 * slots + 1]
-    col_place = lists_ref[2 * slots + 2]
-    col_blocks, row_blocks = total.shape[:2]
+    row_place = lax.axis_index("row")
+    col_place = lax.axis_index("col")
+    col_devices = lax.axis_size("col")
+    row_blocks = col_devices * blocks
     chunk = -(-slots // CHUNKS)
+    lists = [
+        pltpu.make_async_copy(source, target, list_sems.at[i])
+        for i, (source, target) in enumerate(((rows_hbm, rows_ref), (cols_hbm, cols_ref)))
+    ]
+    for copy in lists:
+        copy.start()
     copies = []
     for c in range(CHUNKS):
         part = pl.ds(c * chunk, min(chunk, slots - c * chunk))
@@ -118,36 +143,49 @@
 
     def clear(index, carry):
         for b in range(row_blocks):
-            total[index, b] = jnp.zeros((tile, tile), F32)
+            total[index * row_blocks + b] = jnp.zeros((tile, tile), F32)
         return carry
 
-    lax.fori_loop(0, col_blocks, clear, 0)
+    lax.fori_loop(0, total.shape[0] // row_blocks, clear, 0)
+    for copy in lists:
+        copy.wait()
+    live = count_ref[0]
 
     def add(slot, carry):
-        row = lists_ref[slot]
-        column = lists_ref[slots + slot]
+        row = rows_ref[slot]
+        column = cols_ref[slot]
         side = lax.rem(row // blocks + col_devices - col_place, col_devices)
-        row_at = side * blocks + lax.rem(row, blocks)
         owner = column // (blocks * col_devices)
         column_at = (owner ^ row_place) * blocks + lax.rem(column, blocks)
-        total[column_at, row_at] = total[column_at, row_at] + held[slot].astype(F32)
+        at = column_at * row_blocks + side * blocks + lax.rem(row, blocks)
+        total[at] = total[at] + held[slot].astype(F32)
         return carry
 
     for c in range(CHUNKS):
         copies[c].wait()
         lax.fori_loop(c * chunk, jnp.minimum(live, min((c + 1) * chunk, slots)), add, 0)
 
+
+def dense_kernel(total, joined_ref, out_ref):
+    tile = total.shape[1]
+    row_blocks = out_ref.shape[2] // tile
+
     def part(index, carry):
         start = pl.multiple_of(index * tile, tile)
         for b in range(row_blocks):
-            value = total[index, b].T
+            value = total[index * row_blocks + b].T
             high = value.astype(BF16)
             low = (value - high.astype(F32)).astype(BF16)
             out_ref[0, pl.ds(start, tile), pl.ds(b * tile, tile)] = high
             out_ref[1, pl.ds(start, tile), pl.ds(b * tile, tile)] = low
         return carry
 
-    lax.fori_loop(0, col_blocks, part, 0)
+    lax.fori_loop(0, total.shape[0] // row_blocks, part, 0)
+
+
+def join_kernel(*refs):
+    for k, ref in enumerate(refs[:-2]):
+        refs[-1][k] = ref[...]
 
 
 def apply_dense(directions, matrix):
@@ -165,14 +203,14 @@
     return total
 
 
-def first_kernel(pieces, *refs):
-    values = [ref[...] for ref in refs[: pieces + 1]]
-    matrix, out_ref, state_ref = refs[pieces + 1 :]
-    for k, value in enumerate(values):
+def first_kernel(even_ref, odd_ref, far_ref, matrix, out_ref, state_ref):
+    pieces = 2 * even_ref.shape[0]
+    values = [(odd_ref if k % 2 else even_ref)[k // 2] for k in range(pieces)]
+    for k, value in enumerate(values + [far_ref[...]]):
         state_ref[k] = value
     rows = 2 * values[0].shape[1]
-    out_ref[:, rows:] = add_up([grams(value, [value]) for value in values[:pieces]])
-    out_ref[:, :rows] = apply_dense(values[:pieces], matrix)
+    out_ref[:, rows:] = add_up([grams(value, [value]) for value in values])
+    out_ref[:, :rows] = apply_dense(values, matrix)
 
 
 def add_halves(mine_ref, other_ref, width):
@@ -204,13 +242,13 @@
     out_ref[...] = solve_wide(norm, jnp.where(unit, 1.0, 0.0))
 
 
-def step_kernel(pieces, with_solution, *refs):
+def step_kernel(pieces, with_solution, last, *refs):
     images = refs[:pieces]
     far_ref, direction_ref, residual_ref, norm_ref, inverse_ref, matrix = refs[pieces : pieces + 6]
     refs = refs[pieces + 6 :]
     if with_solution:
         solution_ref, refs = refs[0], refs[1:]
-    out_ref, new_direction, new_residual, new_norm, new_solution = refs
+    out_ref, new_direction, new_residual, new_norm, new_solution = refs[:5]
     size, width = far_ref.shape
     parts = width // LANES
     products = add_up([ref[parts * size :] for ref in images])
@@ -236,27 +274,30 @@
             image = far_ref[...]
         residual = residual_ref[k] - times(alpha_t, image)
         direction = residual + times(beta_t, direction_ref[k])
-        new_residual[k] = residual
-        new_direction[k] = direction
+        if k < new_residual.shape[0]:
+            new_residual[k] = residual
+            new_direction[k] = direction
         directions.append(direction)
-    out_ref[...] = apply_dense(directions[:pieces], matrix)
-
-
-def last_image_kernel(mine_ref, other_ref, direction_ref, near_ref, gram_ref):
-    last = direction_ref.shape[0] - 1
-    near, far = add_halves(mine_ref, other_ref, direction_ref.shape[2])
-    near_ref[...] = near
-    gram_ref[...] = grams(near, [direction_ref[0]]) + grams(far, [direction_ref[last]])
-
-
-def last_kernel(pieces, *refs):
-    image_ref, direction_ref, residual_ref, norm_ref, solution_ref = refs[pieces : pieces + 5]
-    new_solution, new_residual = refs[pieces + 5 :]
-    size = image_ref.shape[0]
-    curvature = add_up([ref[:, :size] for ref in refs[:pieces]])
+    image = apply_dense(directions[:pieces], matrix)
+    out_ref[...] = image
+    if last:
+        near = grams(image[:, :width], [directions[0]])
+        far = grams(image[:, width:], [directions[pieces]])
+        gram = pack((near + far)[:, :size])
+        for k in range(refs[5].shape[0]):
+            refs[5][k] = gram
+
+
+def last_kernel(
+    grams_ref, mine_ref, other_ref, direction_ref, residual_ref, norm_ref, solution_ref,
+    new_solution, new_residual,
+):
+    size, width = solution_ref.shape
+    curvature = unpack(add_up([grams_ref[k] for k in range(grams_ref.shape[0])]), size)
     alpha_t = factor(solve_wide(widen(symmetric(curvature)), norm_ref[...])[:, :size].T)
     new_solution[...] = solution_ref[...] + times(alpha_t, direction_ref[0])
-    new_residual[...] = residual_ref[0] - times(alpha_t, image_ref[...])
+    image = mine_ref[:, :width] + other_ref[:, width:]
+    new_residual[...] = residual_ref[0] - times(alpha_t, image)
 
 
 def shape(*dims, dtype=F32):
@@ -274,9 +315,7 @@
     def swap(value, mask):
         return lax.ppermute(value, "row", [(i, i ^ mask) for i in range(pieces)])
 
-    def around(value, forward=True):
-        if not forward:
-            return [value] + [swap(value, k) for k in range(1, pieces)]
+    def around(value):
         even = [value] + [swap(value, k) for k in range(2, pieces, 2)]
         odd = [swap(piece, 1) for piece in even]
         return [piece for pair in zip(even, odd) for piece in pair]
@@ -287,28 +326,51 @@
         )
 
     right_side = signs.astype(F32) * vertex_weight[None, :] * column_scale[:, None]
-    blocks = around(right_side, forward=False) + [across(right_side)]
+    far_side = across(right_side)
+    even = [right_side] + [swap(right_side, k) for k in range(2, pieces, 2)]
 
     matrix = shape(2, depth, group, dtype=BF16)
-    total = shape(depth // tile, group // tile, tile, tile)
-    place = jnp.stack([lax.axis_index("row"), lax.axis_index("col")]).astype(jnp.int32)
-    lists = jnp.concatenate([tile_rows, tile_cols, tile_count, place])
-    dense = pl.pallas_call(
-        functools.partial(dense_kernel, rows_dev, col_devices),
-        out_shape=matrix,
-        in_specs=[SMEM, HBM],
+    total = shape(depth // tile * (group // tile), tile, tile)
+    lists = [tile_rows, tile_cols]
+    blocks_sum = pl.pallas_call(
+        functools.partial(gather_kernel, rows_dev),
+        out_shape=total,
+        in_specs=[SMEM] + [HBM] * 3,
         out_specs=VMEM,
         scratch_shapes=[
             pltpu.VMEM(tiles.shape, BF16),
-            pltpu.VMEM(total.shape, F32),
+            pltpu.SMEM(tile_rows.shape, jnp.int32),
+            pltpu.SMEM(tile_cols.shape, jnp.int32),
             pltpu.SemaphoreType.DMA((CHUNKS,)),
+            pltpu.SemaphoreType.DMA((len(lists),)),
         ],
-        compiler_params=params(tiles, total, matrix),
+        compiler_params=params(tiles, total),
+        cost_estimate=pl.CostEstimate(
+            flops=4 * tiles.size, bytes_accessed=4 * tiles.size, transcendentals=0
+        ),
+        name="gather",
+    )(tile_count, *[pltpu.with_memory_space_constraint(x, pltpu.HBM) for x in lists + [tiles]])
+    joined = shape(pieces // 2, sketch, rows_dev)
+    even = pl.pallas_call(
+        join_kernel,
+        out_shape=joined,
+        in_specs=[VMEM] * (pieces // 2) + [ANY],
+        out_specs=VMEM,
+        compiler_params=params(joined, joined),
+        name="join",
+    )(*even, blocks_sum)
+    odd = swap(even, 1)
+    dense = pl.pallas_call(
+        dense_kernel,
+        out_shape=matrix,
+        in_specs=[VMEM, ANY],
+        out_specs=VMEM,
+        compiler_params=params(total, matrix),
         cost_estimate=pl.CostEstimate(
             flops=4 * tiles.size, bytes_accessed=4 * tiles.size, transcendentals=0
         ),
         name="dense",
-    )(lists, pltpu.with_memory_space_constraint(tiles, pltpu.HBM))
+    )(blocks_sum, even)
 
     state = shape(pieces + 1, sketch, rows_dev)
     small = shape(sketch, LANES)
@@ -316,13 +378,13 @@
     payload = shape(sketch * (rows_dev // LANES + 1), LANES)
 
     partial_sum, direction = pl.pallas_call(
-        functools.partial(first_kernel, pieces),
+        first_kernel,
         out_shape=(shape(sketch, group + LANES), state),
-        in_specs=[VMEM] * (pieces + 2),
+        in_specs=[VMEM] * 4,
         out_specs=(VMEM, VMEM),
         compiler_params=params(matrix, state, state),
         name="first",
-    )(*blocks, dense)
+    )(even, odd, far_side, dense)
     residual = direction
     norm = None
     solution = None
@@ -347,31 +409,29 @@
             compiler_params=params(),
             name="inverse",
         )(norm)
+        last = iteration == ITERS - 2
         given = () if first else (solution,)
-        partial_sum, direction, residual, norm, solution = pl.pallas_call(
-            functools.partial(step_kernel, pieces, not first),
-            out_shape=(shape(sketch, group), state, state, small, piece),
+        kept = shape(1, sketch, rows_dev) if last else state
+        gram = shape(pieces * col_devices, sketch * sketch // LANES, LANES)
+        outs = pl.pallas_call(
+            functools.partial(step_kernel, pieces, not first, last),
+            out_shape=(shape(sketch, group), kept, kept, small, piece) + ((gram,) if last else ()),
             in_specs=[VMEM] * (pieces + 6 + len(given)),
-            out_specs=(VMEM,) * 5,
+            out_specs=(VMEM,) * (6 if last else 5),
             compiler_params=params(matrix, state, state, state, state, state),
             name="step",
         )(*around(image), far, direction, residual, norm, inverse, dense, *given)
-    image, gram = pl.pallas_call(
-        last_image_kernel,
-        out_shape=(piece, small),
-        in_specs=[VMEM] * 3,
+        partial_sum, direction, residual, norm, solution = outs[:5]
+    other = across(partial_sum)
+    every = lax.all_to_all(outs[5], ("row", "col"), 0, 0)
+    return pl.pallas_call(
+        last_kernel,
+        out_shape=(piece, piece),
+        in_specs=[VMEM] * 7,
         out_specs=(VMEM, VMEM),
-        compiler_params=params(state),
-        name="last_image",
-    )(partial_sum, across(partial_sum), direction)
-    return pl.pallas_call(
-        functools.partial(last_kernel, pieces),
-        out_shape=(piece, piece),
-        in_specs=[VMEM] * (pieces + 5),
-        out_specs=(VMEM, VMEM),
-        compiler_params=params(state, state, state),
+        compiler_params=params(state, state),
         name="last",
-    )(*around(gram), image, direction, residual, norm, solution)
+    )(every, partial_sum, other, direction, residual, norm, solution)
 
 
 def solution(mesh):

time: 73.1 us -> 66.8 us (0.914)
  starting transfers between devices: 38 us -> 29.9 us
  waiting for transfers between devices: 16.1 us -> 18.8 us
  local copies, waits for them, and re-layouts: 0.77 us -> 0 us
    ppermute x28 -> x18, starting transfers between devices: 37.5 us -> 25.4 us  [swap(): return lax.ppermute(value, 'row', [(i, i ^ mask) for i in range(pieces)])]
    all_to_all x0 -> x1, waiting for transfers between devices: none -> 5.58 us  [per_device(): every = lax.all_to_all(outs[5], ('row', 'col'), 0, 0)]
    all_to_all x0 -> x1, starting transfers between devices: none -> 3.99 us  [per_device(): every = lax.all_to_all(outs[5], ('row', 'col'), 0, 0)]
    ppermute x28 -> x18, waiting for transfers between devices: 12.3 us -> 9.76 us  [swap(): return lax.ppermute(value, 'row', [(i, i ^ mask) for i in range(pieces)])]
    concatenate x1 -> x0, local copies, waits for them, and re-layouts: 0.77 us -> none  [per_device(): lists = jnp.concatenate([tile_rows, tile_cols, tile_count, place])]
    pallas_call x6 -> x7, Pallas kernels: 13.8 us -> 13.8 us  [the longest x2 5.77 us: per_device(): pl.pallas_call(functools.partial(step_kernel, pieces, not first, last), o...]
  transfers between devices with their start and end apart: 32 -> 23, of which waited for: 15 -> 14; matrix products, arithmetic and copies ran while one was open for 1% -> 0% of each run, Pallas kernels for 10% -> 10%
where the time goes in v4:
time: 66.8 us; the launch traced here: 67.1 us
  starting transfers between devices  29.9 us (45%)
  waiting for transfers between devices  18.8 us (28%)
  Pallas kernels  16.2 us (24%)
  between operations  1.39 us (2%)
  other arithmetic  0.85 us (1%)
    ppermute x18, starting transfers between devices, swap(): return lax.ppermute(value, 'row', [(i, i ^ mask) for i in range(pieces)])  25.4 us
    ppermute x18, waiting for transfers between devices, swap(): return lax.ppermute(value, 'row', [(i, i ^ mask) for i in range(pieces)])  9.76 us
    pallas_call x2, Pallas kernels, per_device(): pl.pallas_call(functools.partial(step_kernel, pieces, not first, last), o...  5.77 us
    all_to_all x1, waiting for transfers between devices, per_device(): every = lax.all_to_all(outs[5], ('row', 'col'), 0, 0)  5.58 us
    all_to_all x1, starting transfers between devices, per_device(): every = lax.all_to_all(outs[5], ('row', 'col'), 0, 0)  3.99 us
    ppermute x4, waiting for transfers between devices, across(): lax.ppermute(value, 'col', [(i, (i + 1) % col_devices) for i in range(col...  3.44 us
    pallas_call x1, Pallas kernels, per_device(): pl.pallas_call(functools.partial(gather_kernel, rows_dev), out_shape=tota...  2.75 us
    pallas_call x1, Pallas kernels, per_device(): pl.pallas_call(dense_kernel, out_shape=matrix, in_specs=[VMEM, ANY], out_...  2.21 us
  transfers between devices with their start and end apart: 23, of which 14 were waited for; matrix products, arithmetic and copies ran while one was open for 0% of the time, Pallas kernels for 10%

profile of v4, /device:TPU:0, one launch (start us, length us, event | category | flops | bytes accessed | tf_op | source)
XLA Modules:
  0.0 67.1 jit_solution(10056477758831385700)
XLA Ops:
  0.6 0.8 %multiply_multiply_fusion.refs_0_ = f32[32,256]{1,0:T(8,128)S(1)} fusion(s32[32,256]{1,0:T(8,128)} %param.11, f32[32]{0:T(128)} %param.13, f32[256]{0:T(256)} %param.12), kind=kLoop, calls=%fused_computation | loop fusion | flops 24576 | bytes 66688 | tf_op jit(solution)/shard_map/mul | solution.py:328
  1.5 5.1 %collective-permute-start.2 = (f32[32,256]{1,0:T(8,128)S(1)}, f32[32,256]{1,0:T(8,128)S(1)}, u32[]{:S(2)}, u32[]{:S(2)}) collective-permute-start(f32[32,256]{1,0:T(8,128)S(1)} %multiply_multiply_fusion.refs_0_), channel_id=1, source_target_pairs={{0,12},{2,14},{4,8},{6,10},{8,4},{10,6},{12,0},{14,2},{1,13},{3,15... | collective-permute-start | bytes 98312 | tf_op jit(solution)/shard_map/ppermute | solution.py:316
  6.5 0.0 collective-permute-start.1
  6.5 0.6 collective-permute-start
  7.8 2.7 %gather.1.refs_4_.total = f32[64,128,128]{2,1,0:T(8,128)S(1)} custom-call(s32[1]{0:T(128)S(6)} %copy.9.count_ref, s32[130]{0:T(256)} %rows_hbm.1, s32[130]{0:T(256)} %cols_hbm.1, bf16[130,128,128]{2,1,0:T(8,128)(2,1)} %tiles_ref.1), custom_call_target="tpu_custom_call" | custom-call | flops 8519680 | bytes 8519680 | tf_op jit(solution)/shard_map/gather/pallas_call | solution.py:335
  10.6 0.0 collective-permute-done.2.refs_3_
  10.6 0.8 %collective-permute-done.1.refs_2_ = f32[32,256]{1,0:T(8,128)S(1)} collective-permute-done((f32[32,256]{1,0:T(8,128)S(1)}, f32[32,256]{1,0:T(8,128)S(1)}, u32[]{:S(2)}, u32[]{:S(2)}) %collective-permute-start.1) | collective-permute-done | bytes 32800 | tf_op jit(solution)/shard_map/ppermute | solution.py:316
  11.3 0.0 collective-permute-done.refs_1_
  11.4 1.6 %collective-permute-start.3 = (f32[4,32,256]{2,1,0:T(8,128)S(1)}, f32[4,32,256]{2,1,0:T(8,128)S(1)}, u32[]{:S(2)}, u32[]{:S(2)}) collective-permute-start(f32[4,32,256]{2,1,0:T(8,128)S(1)} %join.1.joined_ref.even_ref), channel_id=1, source_target_pairs={{0,2},{2,0},{4,6},{6,4},{8,10},{10,8},{12,14},{14,12},{1,3},{3,1},... | collective-permute-start | bytes 393224 | tf_op jit(solution)/shard_map/ppermute | solution.py:316
  12.9 0.0 collective-permute-start.4
  13.0 2.2 %dense.1.matrix.refs_13_ = bf16[2,2048,512]{2,1,0:T(8,128)(2,1)S(1)} custom-call(f32[64,128,128]{2,1,0:T(8,128)S(1)} %gather.1.refs_4_.total, f32[4,32,256]{2,1,0:T(8,128)S(1)} %join.1.joined_ref.even_ref), custom_call_target="tpu_custom_call" | custom-call | flops 8519680 | bytes 8519680 | tf_op jit(solution)/shard_map/dense/pallas_call | solution.py:363
  15.2 0.0 collective-permute-done.4.far_ref
  15.2 1.2 %collective-permute-done.3.odd_ref = f32[4,32,256]{2,1,0:T(8,128)S(1)} collective-permute-done((f32[4,32,256]{2,1,0:T(8,128)S(1)}, f32[4,32,256]{2,1,0:T(8,128)S(1)}, u32[]{:S(2)}, u32[]{:S(2)}) %collective-permute-start.3) | collective-permute-done | bytes 131104 | tf_op jit(solution)/shard_map/ppermute | solution.py:316
  16.4 1.2 %first.1 = (f32[32,640]{1,0:T(8,128)S(1)}, f32[9,32,256]{2,1,0:T(8,128)S(1)}) custom-call(f32[4,32,256]{2,1,0:T(8,128)S(1)} %join.1.joined_ref.even_ref, f32[4,32,256]{2,1,0:T(8,128)S(1)} %collective-permute-done.3.odd_ref, f32[32,256]{1,0:T(8,128)S(1)} %collective-permute-done.4.far_ref, bf16[2,2048,512]{2,1,0:T(8,128)(2,1)S(1)} %dense.1.matrix.refs_13_), custom_call_target="tpu_custom_call" | custom-call | tf_op jit(solution)/shard_map/first/pallas_call | solution.py:380
  17.6 0.1 collective-permute-start.5
  17.7 1.3 %collective-permute-done.5.other_ref = f32[32,640]{1,0:T(8,128)S(1)} collective-permute-done((f32[32,640]{1,0:T(8,128)S(1)}, f32[32,640]{1,0:T(8,128)S(1)}, u32[]{:S(2)}, u32[]{:S(2)}) %collective-permute-start.5) | collective-permute-done | bytes 81952 | tf_op jit(solution)/shard_map/ppermute | solution.py:324
  18.9 0.2 image.2
  19.2 4.8 %collective-permute-start.11 = (f32[96,128]{1,0:T(8,128)S(1)}, f32[96,128]{1,0:T(8,128)S(1)}, u32[]{:S(2)}, u32[]{:S(2)}) collective-permute-start(f32[96,128]{1,0:T(8,128)S(1)} %get-tuple-element.22.refs_0_), channel_id=1, source_target_pairs={{0,12},{2,14},{4,8},{6,10},{8,4},{10,6},{12,0},{14,2},{1,13},{3,15... | collective-permute-start | bytes 147464 | tf_op jit(solution)/shard_map/ppermute | solution.py:316
  24.0 0.0 collective-permute-start.9
  24.0 0.6 collective-permute-start.7
  24.6 0.5 collective-permute-start.6
  25.2 1.4 %collective-permute-done.11.refs_6_ = f32[96,128]{1,0:T(8,128)S(1)} collective-permute-done((f32[96,128]{1,0:T(8,128)S(1)}, f32[96,128]{1,0:T(8,128)S(1)}, u32[]{:S(2)}, u32[]{:S(2)}) %collective-permute-start.11) | collective-permute-done | bytes 49184 | tf_op jit(solution)/shard_map/ppermute | solution.py:316
  26.5 0.6 collective-permute-start.12
  27.1 1.8 %collective-permute-done.9.refs_4_ = f32[96,128]{1,0:T(8,128)S(1)} collective-permute-done((f32[96,128]{1,0:T(8,128)S(1)}, f32[96,128]{1,0:T(8,128)S(1)}, u32[]{:S(2)}, u32[]{:S(2)}) %collective-permute-start.9) | collective-permute-done | bytes 49184 | tf_op jit(solution)/shard_map/ppermute | solution.py:316
  29.0 0.1 collective-permute-start.10
  29.1 0.0 collective-permute-done.7.refs_2_
  29.1 2.0 %collective-permute-start.8 = (f32[96,128]{1,0:T(8,128)S(1)}, f32[96,128]{1,0:T(8,128)S(1)}, u32[]{:S(2)}, u32[]{:S(2)}) collective-permute-start(f32[96,128]{1,0:T(8,128)S(1)} %collective-permute-done.7.refs_2_), channel_id=1, source_target_pairs={{0,2},{2,0},{4,6},{6,4},{8,10},{10,8},{12,14},{14,12},{1,3},{3,1},... | collective-permute-start | bytes 147464 | tf_op jit(solution)/shard_map/ppermute | solution.py:316
  31.0 0.9 %inverse.2.refs_12_ = f32[32,128]{1,0:T(8,128)S(1)} custom-call(f32[32,128]{1,0:T(8,128)S(1)} %get-tuple-element.24.norm_ref.refs_11_), custom_call_target="tpu_custom_call" | custom-call | tf_op jit(solution)/shard_map/inverse/pallas_call | solution.py:404
  32.0 0.0 collective-permute-done.6.refs_1_
  32.0 0.0 collective-permute-done.12.refs_7_
  32.0 1.1 %collective-permute-done.10.refs_5_ = f32[96,128]{1,0:T(8,128)S(1)} collective-permute-done((f32[96,128]{1,0:T(8,128)S(1)}, f32[96,128]{1,0:T(8,128)S(1)}, u32[]{:S(2)}, u32[]{:S(2)}) %collective-permute-start.10) | collective-permute-done | bytes 49184 | tf_op jit(solution)/shard_map/ppermute | solution.py:316
  33.1 0.5 collective-permute-done.8.refs_3_
  33.6 2.5 %step.2 = (f32[32,512]{1,0:T(8,128)S(1)}, f32[9,32,256]{2,1,0:T(8,128)S(1)}, f32[9,32,256]{2,1,0:T(8,128)S(1)}, f32[32,128]{1,0:T(8,128)S(1)}, f32[32,256]{1,0:T(8,128)S(1)}) custom-call(f32[96,128]{1,0:T(8,128)S(1)} %get-tuple-element.22.refs_0_, f32[96,128]{1,0:T(8,128)S(1)} %collective-permute-done.6.refs_1_, ...), custom_call_target="tpu_custom_call" | custom-call | tf_op jit(solution)/shard_map/step/pallas_call | solution.py:416
  36.1 0.0 collective-permute-start.13
  36.1 1.3 %collective-permute-done.13.other_ref = f32[32,512]{1,0:T(8,128)S(1)} collective-permute-done((f32[32,512]{1,0:T(8,128)S(1)}, f32[32,512]{1,0:T(8,128)S(1)}, u32[]{:S(2)}, u32[]{:S(2)}) %collective-permute-start.13) | collective-permute-done | bytes 65568 | tf_op jit(solution)/shard_map/ppermute | solution.py:324
  37.3 0.2 image.3
  37.6 3.1 %collective-permute-start.19 = (f32[96,128]{1,0:T(8,128)S(1)}, f32[96,128]{1,0:T(8,128)S(1)}, u32[]{:S(2)}, u32[]{:S(2)}) collective-permute-start(f32[96,128]{1,0:T(8,128)S(1)} %get-tuple-element.28.refs_0_), channel_id=1, source_target_pairs={{0,12},{2,14},{4,8},{6,10},{8,4},{10,6},{12,0},{14,2},{1,13},{3,15... | collective-permute-start | bytes 147464 | tf_op jit(solution)/shard_map/ppermute | solution.py:316
  40.6 0.0 collective-permute-start.17
  40.6 1.4 %collective-permute-start.15 = (f32[96,128]{1,0:T(8,128)S(1)}, f32[96,128]{1,0:T(8,128)S(1)}, u32[]{:S(2)}, u32[]{:S(2)}) collective-permute-start(f32[96,128]{1,0:T(8,128)S(1)} %get-tuple-element.28.refs_0_), channel_id=1, source_target_pairs={{0,4},{2,6},{4,0},{6,2},{8,12},{10,14},{12,8},{14,10},{1,5},{3,7},... | collective-permute-start | bytes 147464 | tf_op jit(solution)/shard_map/ppermute | solution.py:316
  42.0 1.5 %collective-permute-start.14 = (f32[96,128]{1,0:T(8,128)S(1)}, f32[96,128]{1,0:T(8,128)S(1)}, u32[]{:S(2)}, u32[]{:S(2)}) collective-permute-start(f32[96,128]{1,0:T(8,128)S(1)} %get-tuple-element.28.refs_0_), channel_id=1, source_target_pairs={{0,2},{2,0},{4,6},{6,4},{8,10},{10,8},{12,14},{14,12},{1,3},{3,1},... | collective-permute-start | bytes 147464 | tf_op jit(solution)/shard_map/ppermute | solution.py:316
  43.5 0.3 collective-permute-done.19.refs_6_
  43.9 1.5 %collective-permute-start.20 = (f32[96,128]{1,0:T(8,128)S(1)}, f32[96,128]{1,0:T(8,128)S(1)}, u32[]{:S(2)}, u32[]{:S(2)}) collective-permute-start(f32[96,128]{1,0:T(8,128)S(1)} %collective-permute-done.19.refs_6_), channel_id=1, source_target_pairs={{0,2},{2,0},{4,6},{6,4},{8,10},{10,8},{12,14},{14,12},{1,3},{3,1},... | collective-permute-start | bytes 147464 | tf_op jit(solution)/shard_map/ppermute | solution.py:316
  45.4 0.3 collective-permute-done.17.refs_4_
  45.7 1.2 %collective-permute-start.18 = (f32[96,128]{1,0:T(8,128)S(1)}, f32[96,128]{1,0:T(8,128)S(1)}, u32[]{:S(2)}, u32[]{:S(2)}) collective-permute-start(f32[96,128]{1,0:T(8,128)S(1)} %collective-permute-done.17.refs_4_), channel_id=1, source_target_pairs={{0,2},{2,0},{4,6},{6,4},{8,10},{10,8},{12,14},{14,12},{1,3},{3,1},... | collective-permute-start | bytes 147464 | tf_op jit(solution)/shard_map/ppermute | solution.py:316
  46.9 0.0 collective-permute-done.15.refs_2_
  46.9 0.9 %collective-permute-start.16 = (f32[96,128]{1,0:T(8,128)S(1)}, f32[96,128]{1,0:T(8,128)S(1)}, u32[]{:S(2)}, u32[]{:S(2)}) collective-permute-start(f32[96,128]{1,0:T(8,128)S(1)} %collective-permute-done.15.refs_2_), channel_id=1, source_target_pairs={{0,2},{2,0},{4,6},{6,4},{8,10},{10,8},{12,14},{14,12},{1,3},{3,1},... | collective-permute-start | bytes 147464 | tf_op jit(solution)/shard_map/ppermute | solution.py:316
  47.7 0.9 %inverse.3.refs_12_ = f32[32,128]{1,0:T(8,128)S(1)} custom-call(f32[32,128]{1,0:T(8,128)S(1)} %get-tuple-element.30.norm_ref.refs_11_), custom_call_target="tpu_custom_call" | custom-call | tf_op jit(solution)/shard_map/inverse/pallas_call | solution.py:404
  48.7 0.0 collective-permute-done.14.refs_1_
  48.7 0.0 collective-permute-done.20.refs_7_
  48.7 1.6 %collective-permute-done.18.refs_5_ = f32[96,128]{1,0:T(8,128)S(1)} collective-permute-done((f32[96,128]{1,0:T(8,128)S(1)}, f32[96,128]{1,0:T(8,128)S(1)}, u32[]{:S(2)}, u32[]{:S(2)}) %collective-permute-start.18) | collective-permute-done | bytes 49184 | tf_op jit(solution)/shard_map/ppermute | solution.py:316
  50.2 0.7 %collective-permute-done.16.refs_3_ = f32[96,128]{1,0:T(8,128)S(1)} collective-permute-done((f32[96,128]{1,0:T(8,128)S(1)}, f32[96,128]{1,0:T(8,128)S(1)}, u32[]{:S(2)}, u32[]{:S(2)}) %collective-permute-start.16) | collective-permute-done | bytes 49184 | tf_op jit(solution)/shard_map/ppermute | solution.py:316
  51.0 3.3 %step.3 = (f32[32,512]{1,0:T(8,128)S(1)}, f32[1,32,256]{2,1,0:T(8,128)S(1)}, f32[1,32,256]{2,1,0:T(8,128)S(1)}, f32[32,128]{1,0:T(8,128)S(1)}, f32[32,256]{1,0:T(8,128)S(1)}, /*index=5*/f32[16,8,128]{2,1,0:T(8,128)}) custom-call(f32[96,128]{1,0:T(8,128)S(1)} %get-tuple-element.28.refs_0_, f32[96,128]{1,0:T(8,128)S(1)} %collective-permute-done.14.refs_1_, ...), custom_call_target="tpu_custom_call" | custom-call | tf_op jit(solution)/shard_map/step/pallas_call | solution.py:416
  54.3 4.0 %all-to-all-start = ((f32[16,8,128]{2,1,0:T(8,128)}), f32[16,8,128]{2,1,0:T(8,128)S(1)}, u32[]{:S(2)}, u32[]{:S(2)}) async-start(f32[16,8,128]{2,1,0:T(8,128)} %get-tuple-element.32), calls=%async_computation | async-start | bytes 131072 | tf_op jit(solution)/shard_map/all_to_all | solution.py:426
  58.3 0.4 collective-permute-start.21
  58.7 0.9 %collective-permute-done.21.other_ref = f32[32,512]{1,0:T(8,128)S(1)} collective-permute-done((f32[32,512]{1,0:T(8,128)S(1)}, f32[32,512]{1,0:T(8,128)S(1)}, u32[]{:S(2)}, u32[]{:S(2)}) %collective-permute-start.21) | collective-permute-done | bytes 65568 | tf_op jit(solution)/shard_map/ppermute | solution.py:324
  59.6 5.6 %all-to-all-done.grams_ref = f32[16,8,128]{2,1,0:T(8,128)S(1)} async-done(((f32[16,8,128]{2,1,0:T(8,128)}), f32[16,8,128]{2,1,0:T(8,128)S(1)}, u32[]{:S(2)}, u32[]{:S(2)}) %all-to-all-start) | async-done | bytes 65568 | tf_op jit(solution)/shard_map/all_to_all | solution.py:426
  65.2 1.9 %last.1 = (f32[32,256]{1,0:T(8,128)}, f32[32,256]{1,0:T(8,128)}) custom-call(f32[16,8,128]{2,1,0:T(8,128)S(1)} %all-to-all-done.grams_ref, f32[32,512]{1,0:T(8,128)S(1)} %get-tuple-element.33.mine_ref, f32[32,512]{1,0:T(8,128)S(1)} %collective-permute-done.21.other_ref, f32[1,32,256]{2,1,0:T(8,128)S(1)} %get-tuple-element.34.direction_ref, ...), custom_call_target="tpu_custom_call" | custom-call | tf_op jit(solution)/shard_map/last/pallas_call | solution.py:427
  (1 shorter events, 0.0 us)
Async XLA Ops:
  1.5 9.1 %collective-permute-start.2 = (f32[32,256]{1,0:T(8,128)S(1)}, f32[32,256]{1,0:T(8,128)S(1)}, u32[]{:S(2)}, u32[]{:S(2)}) collective-permute-start(f32[32,256]{1,0:T(8,128)S(1)} %multiply_multiply_fusion.refs_0_), channel_id=1, source_target_pairs={{0,12},{2,14},{4,8},{6,10},{8,4},{10,6},{12,0},{14,2},{1,13},{3,15... | collective-permute-start | bytes 98312 | tf_op jit(solution)/shard_map/ppermute | solution.py:316
  6.5 4.8 %collective-permute-start.1 = (f32[32,256]{1,0:T(8,128)S(1)}, f32[32,256]{1,0:T(8,128)S(1)}, u32[]{:S(2)}, u32[]{:S(2)}) collective-permute-start(f32[32,256]{1,0:T(8,128)S(1)} %multiply_multiply_fusion.refs_0_), channel_id=1, source_target_pairs={{0,8},{2,10},{4,12},{6,14},{8,0},{10,2},{12,4},{14,6},{1,9},{3,11}... | collective-permute-start | bytes 98312 | tf_op jit(solution)/shard_map/ppermute | solution.py:316
  6.5 4.8 %collective-permute-start = (f32[32,256]{1,0:T(8,128)S(1)}, f32[32,256]{1,0:T(8,128)S(1)}, u32[]{:S(2)}, u32[]{:S(2)}) collective-permute-start(f32[32,256]{1,0:T(8,128)S(1)} %multiply_multiply_fusion.refs_0_), channel_id=1, source_target_pairs={{0,4},{2,6},{4,0},{6,2},{8,12},{10,14},{12,8},{14,10},{1,5},{3,7},... | collective-permute-start | bytes 98312 | tf_op jit(solution)/shard_map/ppermute | solution.py:316
  11.4 5.0 %collective-permute-start.3 = (f32[4,32,256]{2,1,0:T(8,128)S(1)}, f32[4,32,256]{2,1,0:T(8,128)S(1)}, u32[]{:S(2)}, u32[]{:S(2)}) collective-permute-start(f32[4,32,256]{2,1,0:T(8,128)S(1)} %join.1.joined_ref.even_ref), channel_id=1, source_target_pairs={{0,2},{2,0},{4,6},{6,4},{8,10},{10,8},{12,14},{14,12},{1,3},{3,1},... | collective-permute-start | bytes 393224 | tf_op jit(solution)/shard_map/ppermute | solution.py:316
  12.9 2.2 %collective-permute-start.4 = (f32[32,256]{1,0:T(8,128)S(1)}, f32[32,256]{1,0:T(8,128)S(1)}, u32[]{:S(2)}, u32[]{:S(2)}) collective-permute-start(f32[32,256]{1,0:T(8,128)S(1)} %multiply_multiply_fusion.refs_0_), channel_id=1, source_target_pairs={{0,1},{1,0},{2,3},{3,2},{4,5},{5,4},{6,7},{7,6},{8,9},{9,8},{10,11... | collective-permute-start | bytes 98312 | tf_op jit(solution)/shard_map/ppermute | solution.py:324
  17.6 1.3 %collective-permute-start.5 = (f32[32,640]{1,0:T(8,128)S(1)}, f32[32,640]{1,0:T(8,128)S(1)}, u32[]{:S(2)}, u32[]{:S(2)}) collective-permute-start(f32[32,640]{1,0:T(8,128)S(1)} %get-tuple-element.20.mine_ref), channel_id=1, source_target_pairs={{0,1},{1,0},{2,3},{3,2},{4,5},{5,4},{6,7},{7,6},{8,9},{9,8},{10,11... | collective-permute-start | bytes 245768 | tf_op jit(solution)/shard_map/ppermute | solution.py:324
  19.2 7.3 %collective-permute-start.11 = (f32[96,128]{1,0:T(8,128)S(1)}, f32[96,128]{1,0:T(8,128)S(1)}, u32[]{:S(2)}, u32[]{:S(2)}) collective-permute-start(f32[96,128]{1,0:T(8,128)S(1)} %get-tuple-element.22.refs_0_), channel_id=1, source_target_pairs={{0,12},{2,14},{4,8},{6,10},{8,4},{10,6},{12,0},{14,2},{1,13},{3,15... | collective-permute-start | bytes 147464 | tf_op jit(solution)/shard_map/ppermute | solution.py:316
  24.0 5.0 %collective-permute-start.9 = (f32[96,128]{1,0:T(8,128)S(1)}, f32[96,128]{1,0:T(8,128)S(1)}, u32[]{:S(2)}, u32[]{:S(2)}) collective-permute-start(f32[96,128]{1,0:T(8,128)S(1)} %get-tuple-element.22.refs_0_), channel_id=1, source_target_pairs={{0,8},{2,10},{4,12},{6,14},{8,0},{10,2},{12,4},{14,6},{1,9},{3,11}... | collective-permute-start | bytes 147464 | tf_op jit(solution)/shard_map/ppermute | solution.py:316
  24.0 5.1 %collective-permute-start.7 = (f32[96,128]{1,0:T(8,128)S(1)}, f32[96,128]{1,0:T(8,128)S(1)}, u32[]{:S(2)}, u32[]{:S(2)}) collective-permute-start(f32[96,128]{1,0:T(8,128)S(1)} %get-tuple-element.22.refs_0_), channel_id=1, source_target_pairs={{0,4},{2,6},{4,0},{6,2},{8,12},{10,14},{12,8},{14,10},{1,5},{3,7},... | collective-permute-start | bytes 147464 | tf_op jit(solution)/shard_map/ppermute | solution.py:316
  24.6 7.3 %collective-permute-start.6 = (f32[96,128]{1,0:T(8,128)S(1)}, f32[96,128]{1,0:T(8,128)S(1)}, u32[]{:S(2)}, u32[]{:S(2)}) collective-permute-start(f32[96,128]{1,0:T(8,128)S(1)} %get-tuple-element.22.refs_0_), channel_id=1, source_target_pairs={{0,2},{2,0},{4,6},{6,4},{8,10},{10,8},{12,14},{14,12},{1,3},{3,1},... | collective-permute-start | bytes 147464 | tf_op jit(solution)/shard_map/ppermute | solution.py:316
  26.5 5.4 %collective-permute-start.12 = (f32[96,128]{1,0:T(8,128)S(1)}, f32[96,128]{1,0:T(8,128)S(1)}, u32[]{:S(2)}, u32[]{:S(2)}) collective-permute-start(f32[96,128]{1,0:T(8,128)S(1)} %collective-permute-done.11.refs_6_), channel_id=1, source_target_pairs={{0,2},{2,0},{4,6},{6,4},{8,10},{10,8},{12,14},{14,12},{1,3},{3,1},... | collective-permute-start | bytes 147464 | tf_op jit(solution)/shard_map/ppermute | solution.py:316
  29.0 4.1 %collective-permute-start.10 = (f32[96,128]{1,0:T(8,128)S(1)}, f32[96,128]{1,0:T(8,128)S(1)}, u32[]{:S(2)}, u32[]{:S(2)}) collective-permute-start(f32[96,128]{1,0:T(8,128)S(1)} %collective-permute-done.9.refs_4_), channel_id=1, source_target_pairs={{0,2},{2,0},{4,6},{6,4},{8,10},{10,8},{12,14},{14,12},{1,3},{3,1},... | collective-permute-start | bytes 147464 | tf_op jit(solution)/shard_map/ppermute | solution.py:316
  29.1 4.5 %collective-permute-start.8 = (f32[96,128]{1,0:T(8,128)S(1)}, f32[96,128]{1,0:T(8,128)S(1)}, u32[]{:S(2)}, u32[]{:S(2)}) collective-permute-start(f32[96,128]{1,0:T(8,128)S(1)} %collective-permute-done.7.refs_2_), channel_id=1, source_target_pairs={{0,2},{2,0},{4,6},{6,4},{8,10},{10,8},{12,14},{14,12},{1,3},{3,1},... | collective-permute-start | bytes 147464 | tf_op jit(solution)/shard_map/ppermute | solution.py:316
  36.1 1.3 %collective-permute-start.13 = (f32[32,512]{1,0:T(8,128)S(1)}, f32[32,512]{1,0:T(8,128)S(1)}, u32[]{:S(2)}, u32[]{:S(2)}) collective-permute-start(f32[32,512]{1,0:T(8,128)S(1)} %get-tuple-element.25.mine_ref), channel_id=1, source_target_pairs={{0,1},{1,0},{2,3},{3,2},{4,5},{5,4},{6,7},{7,6},{8,9},{9,8},{10,11... | collective-permute-start | bytes 196616 | tf_op jit(solution)/shard_map/ppermute | solution.py:324
  37.6 6.3 %collective-permute-start.19 = (f32[96,128]{1,0:T(8,128)S(1)}, f32[96,128]{1,0:T(8,128)S(1)}, u32[]{:S(2)}, u32[]{:S(2)}) collective-permute-start(f32[96,128]{1,0:T(8,128)S(1)} %get-tuple-element.28.refs_0_), channel_id=1, source_target_pairs={{0,12},{2,14},{4,8},{6,10},{8,4},{10,6},{12,0},{14,2},{1,13},{3,15... | collective-permute-start | bytes 147464 | tf_op jit(solution)/shard_map/ppermute | solution.py:316
  40.6 5.0 %collective-permute-start.17 = (f32[96,128]{1,0:T(8,128)S(1)}, f32[96,128]{1,0:T(8,128)S(1)}, u32[]{:S(2)}, u32[]{:S(2)}) collective-permute-start(f32[96,128]{1,0:T(8,128)S(1)} %get-tuple-element.28.refs_0_), channel_id=1, source_target_pairs={{0,8},{2,10},{4,12},{6,14},{8,0},{10,2},{12,4},{14,6},{1,9},{3,11}... | collective-permute-start | bytes 147464 | tf_op jit(solution)/shard_map/ppermute | solution.py:316
  40.6 6.2 %collective-permute-start.15 = (f32[96,128]{1,0:T(8,128)S(1)}, f32[96,128]{1,0:T(8,128)S(1)}, u32[]{:S(2)}, u32[]{:S(2)}) collective-permute-start(f32[96,128]{1,0:T(8,128)S(1)} %get-tuple-element.28.refs_0_), channel_id=1, source_target_pairs={{0,4},{2,6},{4,0},{6,2},{8,12},{10,14},{12,8},{14,10},{1,5},{3,7},... | collective-permute-start | bytes 147464 | tf_op jit(solution)/shard_map/ppermute | solution.py:316
  42.0 6.6 %collective-permute-start.14 = (f32[96,128]{1,0:T(8,128)S(1)}, f32[96,128]{1,0:T(8,128)S(1)}, u32[]{:S(2)}, u32[]{:S(2)}) collective-permute-start(f32[96,128]{1,0:T(8,128)S(1)} %get-tuple-element.28.refs_0_), channel_id=1, source_target_pairs={{0,2},{2,0},{4,6},{6,4},{8,10},{10,8},{12,14},{14,12},{1,3},{3,1},... | collective-permute-start | bytes 147464 | tf_op jit(solution)/shard_map/ppermute | solution.py:316
  43.9 4.8 %collective-permute-start.20 = (f32[96,128]{1,0:T(8,128)S(1)}, f32[96,128]{1,0:T(8,128)S(1)}, u32[]{:S(2)}, u32[]{:S(2)}) collective-permute-start(f32[96,128]{1,0:T(8,128)S(1)} %collective-permute-done.19.refs_6_), channel_id=1, source_target_pairs={{0,2},{2,0},{4,6},{6,4},{8,10},{10,8},{12,14},{14,12},{1,3},{3,1},... | collective-permute-start | bytes 147464 | tf_op jit(solution)/shard_map/ppermute | solution.py:316
  45.7 4.6 %collective-permute-start.18 = (f32[96,128]{1,0:T(8,128)S(1)}, f32[96,128]{1,0:T(8,128)S(1)}, u32[]{:S(2)}, u32[]{:S(2)}) collective-permute-start(f32[96,128]{1,0:T(8,128)S(1)} %collective-permute-done.17.refs_4_), channel_id=1, source_target_pairs={{0,2},{2,0},{4,6},{6,4},{8,10},{10,8},{12,14},{14,12},{1,3},{3,1},... | collective-permute-start | bytes 147464 | tf_op jit(solution)/shard_map/ppermute | solution.py:316
  46.9 4.1 %collective-permute-start.16 = (f32[96,128]{1,0:T(8,128)S(1)}, f32[96,128]{1,0:T(8,128)S(1)}, u32[]{:S(2)}, u32[]{:S(2)}) collective-permute-start(f32[96,128]{1,0:T(8,128)S(1)} %collective-permute-done.15.refs_2_), channel_id=1, source_target_pairs={{0,2},{2,0},{4,6},{6,4},{8,10},{10,8},{12,14},{14,12},{1,3},{3,1},... | collective-permute-start | bytes 147464 | tf_op jit(solution)/shard_map/ppermute | solution.py:316
  54.3 10.9 %all-to-all-start = ((f32[16,8,128]{2,1,0:T(8,128)}), f32[16,8,128]{2,1,0:T(8,128)S(1)}, u32[]{:S(2)}, u32[]{:S(2)}) async-start(f32[16,8,128]{2,1,0:T(8,128)} %get-tuple-element.32), calls=%async_computation | async-start | bytes 131072 | tf_op jit(solution)/shard_map/all_to_all | solution.py:426
  58.3 1.3 %collective-permute-start.21 = (f32[32,512]{1,0:T(8,128)S(1)}, f32[32,512]{1,0:T(8,128)S(1)}, u32[]{:S(2)}, u32[]{:S(2)}) collective-permute-start(f32[32,512]{1,0:T(8,128)S(1)} %get-tuple-element.33.mine_ref), channel_id=1, source_target_pairs={{0,1},{1,0},{2,3},{3,2},{4,5},{5,4},{6,7},{7,6},{8,9},{9,8},{10,11... | collective-permute-start | bytes 196616 | tf_op jit(solution)/shard_map/ppermute | solution.py:324

commit v5 on v4

--- a/solution.py
+++ b/solution.py
@@ -135,11 +135,15 @@
     ]
     for copy in lists:
         copy.start()
+    live = count_ref[0]
     copies = []
     for c in range(CHUNKS):
         part = pl.ds(c * chunk, min(chunk, slots - c * chunk))
         copies.append(pltpu.make_async_copy(tiles_ref.at[part], held.at[part], sems.at[c]))
-        copies[c].start()
+
+        @pl.when(c * chunk < live)
+        def _():
+            copies[c].start()
 
     def clear(index, carry):
         for b in range(row_blocks):
@@ -149,21 +153,29 @@
     lax.fori_loop(0, total.shape[0] // row_blocks, clear, 0)
     for copy in lists:
         copy.wait()
-    live = count_ref[0]
-
-    def add(slot, carry):
+
+    def place(slot):
         row = rows_ref[slot]
         column = cols_ref[slot]
         side = lax.rem(row // blocks + col_devices - col_place, col_devices)
         owner = column // (blocks * col_devices)
         column_at = (owner ^ row_place) * blocks + lax.rem(column, blocks)
-        at = column_at * row_blocks + side * blocks + lax.rem(row, blocks)
-        total[at] = total[at] + held[slot].astype(F32)
-        return carry
-
+        return column_at * row_blocks + side * blocks + lax.rem(row, blocks)
+
+    def add(slot, at):
+        value = total[at] + held[slot].astype(F32)
+        following = place(jnp.minimum(slot + 1, slots - 1))
+        total[at] = value
+        return following
+
+    at = place(0)
     for c in range(CHUNKS):
-        copies[c].wait()
-        lax.fori_loop(c * chunk, jnp.minimum(live, min((c + 1) * chunk, slots)), add, 0)
+
+        @pl.when(c * chunk < live)
+        def _():
+            copies[c].wait()
+
+        at = lax.fori_loop(c * chunk, jnp.minimum(live, min((c + 1) * chunk, slots)), add, at)
 
 
 def dense_kernel(total, joined_ref, out_ref):
@@ -219,7 +231,7 @@
     return near, far
 
 
-def image_kernel(first, mine_ref, other_ref, direction_ref, residual_ref, *outs):
+def image_kernel(first, mine_ref, other_ref, direction_ref, *outs):
     out_ref, far_ref = outs[:2]
     last = direction_ref.shape[0] - 1
     size, width = direction_ref.shape[1:]
@@ -229,9 +241,8 @@
         outs[2][...] = mine_ref[:, 2 * width :] + other_ref[:, 2 * width :]
     for i in range(width // LANES):
         out_ref[i * size : (i + 1) * size] = near[:, i * LANES : (i + 1) * LANES]
-    near_part = grams(near, [direction_ref[0], residual_ref[0], near])
-    far_part = grams(far, [direction_ref[last], residual_ref[last], far])
-    out_ref[width // LANES * size :] = near_part + far_part
+    product = grams(near, [direction_ref[0]]) + grams(far, [direction_ref[last]])
+    out_ref[width // LANES * size :] = pack(product[:, :size])
 
 
 def inverse_kernel(norm_ref, out_ref):
@@ -242,29 +253,19 @@
     out_ref[...] = solve_wide(norm, jnp.where(unit, 1.0, 0.0))
 
 
-def step_kernel(pieces, with_solution, last, *refs):
+def residual_kernel(pieces, with_solution, last, *refs):
     images = refs[:pieces]
-    far_ref, direction_ref, residual_ref, norm_ref, inverse_ref, matrix = refs[pieces : pieces + 6]
-    refs = refs[pieces + 6 :]
+    far_ref, direction_ref, residual_ref, norm_ref = refs[pieces : pieces + 4]
+    refs = refs[pieces + 4 :]
     if with_solution:
         solution_ref, refs = refs[0], refs[1:]
-    out_ref, new_direction, new_residual, new_norm, new_solution = refs[:5]
+    new_residual, half_ref, new_solution = refs[:3]
     size, width = far_ref.shape
     parts = width // LANES
-    products = add_up([ref[parts * size :] for ref in images])
-    norm = norm_ref[...]
-    alpha = solve_wide(widen(symmetric(products[:, :size])), norm)[:, :size]
-    alpha_t = alpha.T
-    image_residual = pltpu.roll(products, LANES - size, 1)[:, :size]
-    image_image = pltpu.roll(products, LANES - 2 * size, 1)[:, :size]
-    cross = mul(alpha_t, image_residual)
-    next_norm = norm[:, :size] - (cross + cross.T) + mul(alpha_t, mul(image_image, alpha))
-    new_norm[...] = widen(next_norm)
-    beta_t = factor(mul(next_norm, inverse_ref[:, :size]))
-    alpha_t = factor(alpha_t)
-    step = times(alpha_t, direction_ref[0])
-    new_solution[...] = solution_ref[...] + step if with_solution else step
-    directions = []
+    curvature = unpack(add_up([ref[parts * size :] for ref in images]), size)
+    alpha = solve_wide(widen(symmetric(curvature)), norm_ref[...])[:, :size]
+    alpha_t = factor(alpha.T)
+    products = []
     for k in range(pieces + 1):
         if k < pieces:
             image = jnp.concatenate(
@@ -273,9 +274,28 @@
         else:
             image = far_ref[...]
         residual = residual_ref[k] - times(alpha_t, image)
-        direction = residual + times(beta_t, direction_ref[k])
-        if k < new_residual.shape[0]:
-            new_residual[k] = residual
+        new_residual[k] = residual
+        if last and k == 0:
+            refs[3][...] = residual
+        if k < pieces:
+            products.append(grams(residual, [residual]))
+    half_ref[...] = pack(add_up(products)[:, :size])
+    step = times(alpha_t, direction_ref[0])
+    new_solution[...] = solution_ref[...] + step if with_solution else step
+
+
+def direction_kernel(
+    pieces, last, mine_ref, other_ref, inverse_ref, residual_ref, direction_ref, matrix, *outs
+):
+    out_ref, new_direction, new_norm = outs[:3]
+    size, width = residual_ref.shape[1:]
+    next_norm = unpack(mine_ref[...] + other_ref[...], size)
+    new_norm[...] = widen(next_norm)
+    beta_t = factor(mul(next_norm, inverse_ref[:, :size]))
+    directions = []
+    for k in range(pieces + 1):
+        direction = residual_ref[k] + times(beta_t, direction_ref[k])
+        if k < new_direction.shape[0]:
             new_direction[k] = direction
         directions.append(direction)
     image = apply_dense(directions[:pieces], matrix)
@@ -284,8 +304,8 @@
         near = grams(image[:, :width], [directions[0]])
         far = grams(image[:, width:], [directions[pieces]])
         gram = pack((near + far)[:, :size])
-        for k in range(refs[5].shape[0]):
-            refs[5][k] = gram
+        for k in range(outs[3].shape[0]):
+            outs[3][k] = gram
 
 
 def last_kernel(
@@ -297,7 +317,7 @@
     alpha_t = factor(solve_wide(widen(symmetric(curvature)), norm_ref[...])[:, :size].T)
     new_solution[...] = solution_ref[...] + times(alpha_t, direction_ref[0])
     image = mine_ref[:, :width] + other_ref[:, width:]
-    new_residual[...] = residual_ref[0] - times(alpha_t, image)
+    new_residual[...] = residual_ref[...] - times(alpha_t, image)
 
 
 def shape(*dims, dtype=F32):
@@ -316,9 +336,15 @@
         return lax.ppermute(value, "row", [(i, i ^ mask) for i in range(pieces)])
 
     def around(value):
-        even = [value] + [swap(value, k) for k in range(2, pieces, 2)]
-        odd = [swap(piece, 1) for piece in even]
-        return [piece for pair in zip(even, odd) for piece in pair]
+        got = {0: value}
+        half = pieces // 2
+        for k in (*range(2, half), 1, half, half - 1):
+            if k not in got:
+                got[k] = swap(value, k)
+        for k in range(half + 1, pieces):
+            mask = half if k == pieces - 1 else k - half
+            got[k] = swap(got[k ^ mask], mask)
+        return [got[k] for k in range(pieces)]
 
     def across(value):
         return lax.ppermute(
@@ -375,7 +401,8 @@
     state = shape(pieces + 1, sketch, rows_dev)
     small = shape(sketch, LANES)
     piece = shape(sketch, rows_dev)
-    payload = shape(sketch * (rows_dev // LANES + 1), LANES)
+    packed = shape(sketch * sketch // LANES, LANES)
+    payload = shape(sketch * (rows_dev // LANES) + packed.shape[0], LANES)
 
     partial_sum, direction = pl.pallas_call(
         first_kernel,
@@ -390,14 +417,15 @@
     solution = None
     for iteration in range(ITERS - 1):
         first = iteration == 0
+        last = iteration == ITERS - 2
         outs = pl.pallas_call(
             functools.partial(image_kernel, first),
             out_shape=(payload, piece) + ((small,) if first else ()),
-            in_specs=[VMEM] * 4,
+            in_specs=[VMEM] * 3,
             out_specs=(VMEM,) * (3 if first else 2),
             compiler_params=params(state, state),
             name="image",
-        )(partial_sum, across(partial_sum), direction, residual)
+        )(partial_sum, across(partial_sum), direction)
         image, far = outs[:2]
         if first:
             norm = outs[2]
@@ -409,21 +437,28 @@
             compiler_params=params(),
             name="inverse",
         )(norm)
-        last = iteration == ITERS - 2
         given = () if first else (solution,)
+        residual, half, solution, *own = pl.pallas_call(
+            functools.partial(residual_kernel, pieces, not first, last),
+            out_shape=(state, packed, piece) + ((piece,) if last else ()),
+            in_specs=[VMEM] * (pieces + 4 + len(given)),
+            out_specs=(VMEM,) * (4 if last else 3),
+            compiler_params=params(state, state, state, state),
+            name="residual",
+        )(*around(image), far, direction, residual, norm, *given)
         kept = shape(1, sketch, rows_dev) if last else state
-        gram = shape(pieces * col_devices, sketch * sketch // LANES, LANES)
+        gram = shape(pieces * col_devices, *packed.shape)
         outs = pl.pallas_call(
-            functools.partial(step_kernel, pieces, not first, last),
-            out_shape=(shape(sketch, group), kept, kept, small, piece) + ((gram,) if last else ()),
-            in_specs=[VMEM] * (pieces + 6 + len(given)),
-            out_specs=(VMEM,) * (6 if last else 5),
-            compiler_params=params(matrix, state, state, state, state, state),
-            name="step",
-        )(*around(image), far, direction, residual, norm, inverse, dense, *given)
-        partial_sum, direction, residual, norm, solution = outs[:5]
+            functools.partial(direction_kernel, pieces, last),
+            out_shape=(shape(sketch, group), kept, small) + ((gram,) if last else ()),
+            in_specs=[VMEM] * 6,
+            out_specs=(VMEM,) * (4 if last else 3),
+            compiler_params=params(matrix, state, state, state),
+            name="direction",
+        )(half, across(half), inverse, residual, direction, dense)
+        partial_sum, direction, norm = outs[:3]
     other = across(partial_sum)
-    every = lax.all_to_all(outs[5], ("row", "col"), 0, 0)
+    every = lax.all_to_all(outs[3], ("row", "col"), 0, 0)
     return pl.pallas_call(
         last_kernel,
         out_shape=(piece, piece),
@@ -431,7 +466,7 @@
         out_specs=(VMEM, VMEM),
         compiler_params=params(state, state),
         name="last",
-    )(every, partial_sum, other, direction, residual, norm, solution)
+    )(every, partial_sum, other, direction, *own, norm, solution)
 
 
 def solution(mesh):

time: 66.8 us -> 71.4 us (1.069)
  Pallas kernels: 16.2 us -> 19.2 us
  starting transfers between devices: 29.9 us -> 31.9 us
    pallas_call x2 -> x4, Pallas kernels: 5.77 us -> 8.87 us  [the longest x2 5.76 us: per_device(): pl.pallas_call(functools.partial(residual_kernel, pieces, not first, last...]
    ppermute x18, starting transfers between devices: 25.4 us -> 26.4 us  [swap(): return lax.ppermute(value, 'row', [(i, i ^ mask) for i in range(pieces)])]
    ppermute x4 -> x6, waiting for transfers between devices: 3.44 us -> 3.53 us  [across(): lax.ppermute(value, 'col', [(i, (i + 1) % col_devices) for i in range(col...]
  transfers between devices with their start and end apart: 23 -> 25, of which waited for: 14 -> 13; matrix products, arithmetic and copies ran while one was open for 0% -> 0% of each run, Pallas kernels for 10% -> 9%
where the time goes in v5:
time: 71.4 us; the launch traced here: 71.5 us
  starting transfers between devices  31.9 us (45%)
  Pallas kernels  19.2 us (27%)
  waiting for transfers between devices  18.2 us (25%)
  between operations  1.39 us (2%)
  other arithmetic  0.85 us (1%)
    ppermute x18, starting transfers between devices, swap(): return lax.ppermute(value, 'row', [(i, i ^ mask) for i in range(pieces)])  26.4 us
    ppermute x18, waiting for transfers between devices, swap(): return lax.ppermute(value, 'row', [(i, i ^ mask) for i in range(pieces)])  9.11 us
    pallas_call x2, Pallas kernels, per_device(): pl.pallas_call(functools.partial(residual_kernel, pieces, not first, last...  5.76 us
    all_to_all x1, waiting for transfers between devices, per_device(): every = lax.all_to_all(outs[3], ('row', 'col'), 0, 0)  5.58 us
    all_to_all x1, starting transfers between devices, per_device(): every = lax.all_to_all(outs[3], ('row', 'col'), 0, 0)  4.56 us
    ppermute x6, waiting for transfers between devices, across(): lax.ppermute(value, 'col', [(i, (i + 1) % col_devices) for i in range(col...  3.53 us
    pallas_call x2, Pallas kernels, per_device(): pl.pallas_call(functools.partial(direction_kernel, pieces, last), out_sha...  3.11 us
    pallas_call x1, Pallas kernels, per_device(): pl.pallas_call(functools.partial(gather_kernel, rows_dev), out_shape=tota...  2.49 us
  transfers between devices with their start and end apart: 25, of which 13 were waited for; matrix products, arithmetic and copies ran while one was open for 0% of the time, Pallas kernels for 9%

profile of v5, /device:TPU:0, one launch (start us, length us, event | category | flops | bytes accessed | tf_op | source)
XLA Modules:
  0.0 71.5 jit_solution(17821647789706551987)
XLA Ops:
  0.6 0.8 %multiply_multiply_fusion.refs_0_ = f32[32,256]{1,0:T(8,128)S(1)} fusion(s32[32,256]{1,0:T(8,128)} %param.11, f32[32]{0:T(128)} %param.13, f32[256]{0:T(256)} %param.12), kind=kLoop, calls=%fused_computation | loop fusion | flops 24576 | bytes 66688 | tf_op jit(solution)/shard_map/mul | solution.py:354
  1.5 5.1 %collective-permute-start.2 = (f32[32,256]{1,0:T(8,128)S(1)}, f32[32,256]{1,0:T(8,128)S(1)}, u32[]{:S(2)}, u32[]{:S(2)}) collective-permute-start(f32[32,256]{1,0:T(8,128)S(1)} %multiply_multiply_fusion.refs_0_), channel_id=1, source_target_pairs={{0,12},{2,14},{4,8},{6,10},{8,4},{10,6},{12,0},{14,2},{1,13},{3,15... | collective-permute-start | bytes 98312 | tf_op jit(solution)/shard_map/ppermute | solution.py:336
  6.5 0.0 collective-permute-start.1
  6.5 0.6 collective-permute-start
  7.8 2.5 %gather.1.refs_4_.total = f32[64,128,128]{2,1,0:T(8,128)S(1)} custom-call(s32[1]{0:T(128)S(6)} %copy.9.count_ref, s32[130]{0:T(256)} %rows_hbm.1, s32[130]{0:T(256)} %cols_hbm.1, bf16[130,128,128]{2,1,0:T(8,128)(2,1)} %tiles_ref.1), custom_call_target="tpu_custom_call" | custom-call | flops 8519680 | bytes 8519680 | tf_op jit(solution)/shard_map/gather/pallas_call | solution.py:361
  10.3 0.0 collective-permute-done.2.refs_3_
  10.3 1.0 %collective-permute-done.1.refs_2_ = f32[32,256]{1,0:T(8,128)S(1)} collective-permute-done((f32[32,256]{1,0:T(8,128)S(1)}, f32[32,256]{1,0:T(8,128)S(1)}, u32[]{:S(2)}, u32[]{:S(2)}) %collective-permute-start.1) | collective-permute-done | bytes 32800 | tf_op jit(solution)/shard_map/ppermute | solution.py:336
  11.3 0.0 collective-permute-done.refs_1_
  11.4 1.6 %collective-permute-start.3 = (f32[4,32,256]{2,1,0:T(8,128)S(1)}, f32[4,32,256]{2,1,0:T(8,128)S(1)}, u32[]{:S(2)}, u32[]{:S(2)}) collective-permute-start(f32[4,32,256]{2,1,0:T(8,128)S(1)} %join.1.joined_ref.even_ref), channel_id=1, source_target_pairs={{0,2},{2,0},{4,6},{6,4},{8,10},{10,8},{12,14},{14,12},{1,3},{3,1},... | collective-permute-start | bytes 393224 | tf_op jit(solution)/shard_map/ppermute | solution.py:336
  12.9 0.0 collective-permute-start.4
  13.0 2.2 %dense.1.matrix = bf16[2,2048,512]{2,1,0:T(8,128)(2,1)S(1)} custom-call(f32[64,128,128]{2,1,0:T(8,128)S(1)} %gather.1.refs_4_.total, f32[4,32,256]{2,1,0:T(8,128)S(1)} %join.1.joined_ref.even_ref), custom_call_target="tpu_custom_call" | custom-call | flops 8519680 | bytes 8519680 | tf_op jit(solution)/shard_map/dense/pallas_call | solution.py:389
  15.2 0.0 collective-permute-done.4.far_ref
  15.2 1.2 %collective-permute-done.3.odd_ref = f32[4,32,256]{2,1,0:T(8,128)S(1)} collective-permute-done((f32[4,32,256]{2,1,0:T(8,128)S(1)}, f32[4,32,256]{2,1,0:T(8,128)S(1)}, u32[]{:S(2)}, u32[]{:S(2)}) %collective-permute-start.3) | collective-permute-done | bytes 131104 | tf_op jit(solution)/shard_map/ppermute | solution.py:336
  16.4 1.2 %first.1 = (f32[32,640]{1,0:T(8,128)S(1)}, f32[9,32,256]{2,1,0:T(8,128)S(1)}) custom-call(f32[4,32,256]{2,1,0:T(8,128)S(1)} %join.1.joined_ref.even_ref, f32[4,32,256]{2,1,0:T(8,128)S(1)} %collective-permute-done.3.odd_ref, f32[32,256]{1,0:T(8,128)S(1)} %collective-permute-done.4.far_ref, bf16[2,2048,512]{2,1,0:T(8,128)(2,1)S(1)} %dense.1.matrix), custom_call_target="tpu_custom_call" | custom-call | tf_op jit(solution)/shard_map/first/pallas_call | solution.py:407
  17.6 0.1 collective-permute-start.5
  17.7 1.3 %collective-permute-done.5.other_ref = f32[32,640]{1,0:T(8,128)S(1)} collective-permute-done((f32[32,640]{1,0:T(8,128)S(1)}, f32[32,640]{1,0:T(8,128)S(1)}, u32[]{:S(2)}, u32[]{:S(2)}) %collective-permute-start.5) | collective-permute-done | bytes 81952 | tf_op jit(solution)/shard_map/ppermute | solution.py:350
  18.9 0.3 image.2
  19.3 2.0 %collective-permute-start.9 = (f32[72,128]{1,0:T(8,128)S(1)}, f32[72,128]{1,0:T(8,128)S(1)}, u32[]{:S(2)}, u32[]{:S(2)}) collective-permute-start(f32[72,128]{1,0:T(8,128)S(1)} %get-tuple-element.25.refs_0_), channel_id=1, source_target_pairs={{0,8},{2,10},{4,12},{6,14},{8,0},{10,2},{12,4},{14,6},{1,9},{3,11}... | collective-permute-start | bytes 110600 | tf_op jit(solution)/shard_map/ppermute | solution.py:336
  21.3 3.9 %collective-permute-start.8 = (f32[72,128]{1,0:T(8,128)S(1)}, f32[72,128]{1,0:T(8,128)S(1)}, u32[]{:S(2)}, u32[]{:S(2)}) collective-permute-start(f32[72,128]{1,0:T(8,128)S(1)} %get-tuple-element.25.refs_0_), channel_id=1, source_target_pairs={{0,6},{2,4},{4,2},{6,0},{8,14},{10,12},{12,10},{14,8},{1,7},{3,5},... | collective-permute-start | bytes 110600 | tf_op jit(solution)/shard_map/ppermute | solution.py:336
  25.2 0.0 collective-permute-start.7
  25.2 0.6 collective-permute-start.6
  25.8 0.0 collective-permute-done.9.refs_4_
  25.8 1.5 %collective-permute-start.11 = (f32[72,128]{1,0:T(8,128)S(1)}, f32[72,128]{1,0:T(8,128)S(1)}, u32[]{:S(2)}, u32[]{:S(2)}) collective-permute-start(f32[72,128]{1,0:T(8,128)S(1)} %collective-permute-done.9.refs_4_), channel_id=1, source_target_pairs={{0,4},{2,6},{4,0},{6,2},{8,12},{10,14},{12,8},{14,10},{1,5},{3,7},... | collective-permute-start | bytes 110600 | tf_op jit(solution)/shard_map/ppermute | solution.py:336
  27.2 2.0 %collective-permute-start.10 = (f32[72,128]{1,0:T(8,128)S(1)}, f32[72,128]{1,0:T(8,128)S(1)}, u32[]{:S(2)}, u32[]{:S(2)}) collective-permute-start(f32[72,128]{1,0:T(8,128)S(1)} %collective-permute-done.9.refs_4_), channel_id=1, source_target_pairs={{0,2},{2,0},{4,6},{6,4},{8,10},{10,8},{12,14},{14,12},{1,3},{3,1},... | collective-permute-start | bytes 110600 | tf_op jit(solution)/shard_map/ppermute | solution.py:336
  29.2 0.0 collective-permute-done.8.refs_3_
  29.3 1.4 %collective-permute-start.12 = (f32[72,128]{1,0:T(8,128)S(1)}, f32[72,128]{1,0:T(8,128)S(1)}, u32[]{:S(2)}, u32[]{:S(2)}) collective-permute-start(f32[72,128]{1,0:T(8,128)S(1)} %collective-permute-done.8.refs_3_), channel_id=1, source_target_pairs={{0,8},{2,10},{4,12},{6,14},{8,0},{10,2},{12,4},{14,6},{1,9},{3,11}... | collective-permute-start | bytes 110600 | tf_op jit(solution)/shard_map/ppermute | solution.py:336
  30.6 0.0 collective-permute-done.7.refs_2_
  30.6 0.0 collective-permute-done.6.refs_1_
  30.6 0.0 collective-permute-done.11.refs_6_
  30.7 0.5 collective-permute-done.10.refs_5_
  31.2 2.9 %collective-permute-done.12.refs_7_ = f32[72,128]{1,0:T(8,128)S(1)} collective-permute-done((f32[72,128]{1,0:T(8,128)S(1)}, f32[72,128]{1,0:T(8,128)S(1)}, u32[]{:S(2)}, u32[]{:S(2)}) %collective-permute-start.12) | collective-permute-done | bytes 36896 | tf_op jit(solution)/shard_map/ppermute | solution.py:336
  34.1 2.9 %residual.2 = (f32[9,32,256]{2,1,0:T(8,128)S(1)}, f32[8,128]{1,0:T(8,128)S(1)}, f32[32,256]{1,0:T(8,128)S(1)}) custom-call(f32[72,128]{1,0:T(8,128)S(1)} %get-tuple-element.25.refs_0_, f32[72,128]{1,0:T(8,128)S(1)} %collective-permute-done.6.refs_1_, f32[72,128]{1,0:T(8,128)S(1)} %collective-permute-done.7.refs_2_, ...), custom_call_target="tpu_custom_call" | custom-call | tf_op jit(solution)/shard_map/residual/pallas_call | solution.py:441
  37.0 0.0 collective-permute-start.13
  37.0 0.9 %inverse.2.inverse_ref = f32[32,128]{1,0:T(8,128)S(1)} custom-call(f32[32,128]{1,0:T(8,128)S(1)} %get-tuple-element.27.refs_11_.norm_ref), custom_call_target="tpu_custom_call" | custom-call | tf_op jit(solution)/shard_map/inverse/pallas_call | solution.py:432
  38.0 0.2 collective-permute-done.13.other_ref
  38.2 1.1 %direction.2 = (f32[32,512]{1,0:T(8,128)S(1)}, f32[9,32,256]{2,1,0:T(8,128)S(1)}, f32[32,128]{1,0:T(8,128)S(1)}) custom-call(f32[8,128]{1,0:T(8,128)S(1)} %get-tuple-element.28.mine_ref, f32[8,128]{1,0:T(8,128)S(1)} %collective-permute-done.13.other_ref, f32[32,128]{1,0:T(8,128)S(1)} %inverse.2.inverse_ref, ...), custom_call_target="tpu_custom_call" | custom-call | tf_op jit(solution)/shard_map/direction/pallas_call | solution.py:451
  39.3 0.4 collective-permute-start.14
  39.6 1.0 %collective-permute-done.14.other_ref = f32[32,512]{1,0:T(8,128)S(1)} collective-permute-done((f32[32,512]{1,0:T(8,128)S(1)}, f32[32,512]{1,0:T(8,128)S(1)}, u32[]{:S(2)}, u32[]{:S(2)}) %collective-permute-start.14) | collective-permute-done | bytes 65568 | tf_op jit(solution)/shard_map/ppermute | solution.py:350
  40.6 0.3 image.3
  40.9 1.4 %collective-permute-start.18 = (f32[72,128]{1,0:T(8,128)S(1)}, f32[72,128]{1,0:T(8,128)S(1)}, u32[]{:S(2)}, u32[]{:S(2)}) collective-permute-start(f32[72,128]{1,0:T(8,128)S(1)} %get-tuple-element.32.refs_0_), channel_id=1, source_target_pairs={{0,8},{2,10},{4,12},{6,14},{8,0},{10,2},{12,4},{14,6},{1,9},{3,11}... | collective-permute-start | bytes 110600 | tf_op jit(solution)/shard_map/ppermute | solution.py:336
  42.3 0.0 collective-permute-start.17
  42.3 1.5 %collective-permute-start.16 = (f32[72,128]{1,0:T(8,128)S(1)}, f32[72,128]{1,0:T(8,128)S(1)}, u32[]{:S(2)}, u32[]{:S(2)}) collective-permute-start(f32[72,128]{1,0:T(8,128)S(1)} %get-tuple-element.32.refs_0_), channel_id=1, source_target_pairs={{0,4},{2,6},{4,0},{6,2},{8,12},{10,14},{12,8},{14,10},{1,5},{3,7},... | collective-permute-start | bytes 110600 | tf_op jit(solution)/shard_map/ppermute | solution.py:336
  43.9 1.9 %collective-permute-start.15 = (f32[72,128]{1,0:T(8,128)S(1)}, f32[72,128]{1,0:T(8,128)S(1)}, u32[]{:S(2)}, u32[]{:S(2)}) collective-permute-start(f32[72,128]{1,0:T(8,128)S(1)} %get-tuple-element.32.refs_0_), channel_id=1, source_target_pairs={{0,2},{2,0},{4,6},{6,4},{8,10},{10,8},{12,14},{14,12},{1,3},{3,1},... | collective-permute-start | bytes 110600 | tf_op jit(solution)/shard_map/ppermute | solution.py:336
  45.8 0.1 collective-permute-done.18.refs_4_
  45.9 0.0 collective-permute-start.20
  45.9 1.3 %collective-permute-start.19 = (f32[72,128]{1,0:T(8,128)S(1)}, f32[72,128]{1,0:T(8,128)S(1)}, u32[]{:S(2)}, u32[]{:S(2)}) collective-permute-start(f32[72,128]{1,0:T(8,128)S(1)} %collective-permute-done.18.refs_4_), channel_id=1, source_target_pairs={{0,2},{2,0},{4,6},{6,4},{8,10},{10,8},{12,14},{14,12},{1,3},{3,1},... | collective-permute-start | bytes 110600 | tf_op jit(solution)/shard_map/ppermute | solution.py:336
  47.2 0.0 collective-permute-done.17.refs_3_
  47.2 1.6 %collective-permute-start.21 = (f32[72,128]{1,0:T(8,128)S(1)}, f32[72,128]{1,0:T(8,128)S(1)}, u32[]{:S(2)}, u32[]{:S(2)}) collective-permute-start(f32[72,128]{1,0:T(8,128)S(1)} %collective-permute-done.17.refs_3_), channel_id=1, source_target_pairs={{0,8},{2,10},{4,12},{6,14},{8,0},{10,2},{12,4},{14,6},{1,9},{3,11}... | collective-permute-start | bytes 110600 | tf_op jit(solution)/shard_map/ppermute | solution.py:336
  48.8 0.0 collective-permute-done.16.refs_2_
  48.8 0.0 collective-permute-done.15.refs_1_
  48.8 1.5 %collective-permute-done.20.refs_6_ = f32[72,128]{1,0:T(8,128)S(1)} collective-permute-done((f32[72,128]{1,0:T(8,128)S(1)}, f32[72,128]{1,0:T(8,128)S(1)}, u32[]{:S(2)}, u32[]{:S(2)}) %collective-permute-start.20) | collective-permute-done | bytes 36896 | tf_op jit(solution)/shard_map/ppermute | solution.py:336
  50.3 0.0 collective-permute-done.19.refs_5_
  50.3 1.8 %collective-permute-done.21.refs_7_ = f32[72,128]{1,0:T(8,128)S(1)} collective-permute-done((f32[72,128]{1,0:T(8,128)S(1)}, f32[72,128]{1,0:T(8,128)S(1)}, u32[]{:S(2)}, u32[]{:S(2)}) %collective-permute-start.21) | collective-permute-done | bytes 36896 | tf_op jit(solution)/shard_map/ppermute | solution.py:336
  52.1 2.9 %residual.3 = (f32[9,32,256]{2,1,0:T(8,128)S(1)}, f32[8,128]{1,0:T(8,128)S(1)}, f32[32,256]{1,0:T(8,128)S(1)}, f32[32,256]{1,0:T(8,128)S(1)}) custom-call(f32[72,128]{1,0:T(8,128)S(1)} %get-tuple-element.32.refs_0_, f32[72,128]{1,0:T(8,128)S(1)} %collective-permute-done.15.refs_1_, f32[72,128]{1,0:T(8,128)S(1)} %collective-permute-done.16.refs_2_, ...), custom_call_target="tpu_custom_call" | custom-call | tf_op jit(solution)/shard_map/residual/pallas_call | solution.py:441
  55.0 0.0 collective-permute-start.22
  55.0 0.9 %inverse.3.inverse_ref = f32[32,128]{1,0:T(8,128)S(1)} custom-call(f32[32,128]{1,0:T(8,128)S(1)} %get-tuple-element.34.refs_11_.norm_ref), custom_call_target="tpu_custom_call" | custom-call | tf_op jit(solution)/shard_map/inverse/pallas_call | solution.py:432
  55.9 0.2 collective-permute-done.22.other_ref
  56.1 2.0 %direction.3 = (f32[32,512]{1,0:T(8,128)S(1)}, f32[1,32,256]{2,1,0:T(8,128)S(1)}, f32[32,128]{1,0:T(8,128)S(1)}, f32[16,8,128]{2,1,0:T(8,128)}) custom-call(f32[8,128]{1,0:T(8,128)S(1)} %get-tuple-element.36.mine_ref, f32[8,128]{1,0:T(8,128)S(1)} %collective-permute-done.22.other_ref, f32[32,128]{1,0:T(8,128)S(1)} %inverse.3.inverse_ref, ...), custom_call_target="tpu_custom_call" | custom-call | tf_op jit(solution)/shard_map/direction/pallas_call | solution.py:451
  58.2 4.6 %all-to-all-start = ((f32[16,8,128]{2,1,0:T(8,128)}), f32[16,8,128]{2,1,0:T(8,128)S(1)}, u32[]{:S(2)}, u32[]{:S(2)}) async-start(f32[16,8,128]{2,1,0:T(8,128)} %get-tuple-element.38), calls=%async_computation | async-start | bytes 131072 | tf_op jit(solution)/shard_map/all_to_all | solution.py:461
  62.7 0.4 collective-permute-start.23
  63.1 0.9 %collective-permute-done.23.other_ref = f32[32,512]{1,0:T(8,128)S(1)} collective-permute-done((f32[32,512]{1,0:T(8,128)S(1)}, f32[32,512]{1,0:T(8,128)S(1)}, u32[]{:S(2)}, u32[]{:S(2)}) %collective-permute-start.23) | collective-permute-done | bytes 65568 | tf_op jit(solution)/shard_map/ppermute | solution.py:350
  64.1 5.6 %all-to-all-done.grams_ref = f32[16,8,128]{2,1,0:T(8,128)S(1)} async-done(((f32[16,8,128]{2,1,0:T(8,128)}), f32[16,8,128]{2,1,0:T(8,128)S(1)}, u32[]{:S(2)}, u32[]{:S(2)}) %all-to-all-start) | async-done | bytes 65568 | tf_op jit(solution)/shard_map/all_to_all | solution.py:461
  69.6 1.9 %last.1 = (f32[32,256]{1,0:T(8,128)}, f32[32,256]{1,0:T(8,128)}) custom-call(f32[16,8,128]{2,1,0:T(8,128)S(1)} %all-to-all-done.grams_ref, f32[32,512]{1,0:T(8,128)S(1)} %get-tuple-element.39.mine_ref, f32[32,512]{1,0:T(8,128)S(1)} %collective-permute-done.23.other_ref, f32[1,32,256]{2,1,0:T(8,128)S(1)} %get-tuple-element.40.direction_ref, ...), custom_call_target="tpu_custom_call" | custom-call | tf_op jit(solution)/shard_map/last/pallas_call | solution.py:462
  (1 shorter events, 0.0 us)
Async XLA Ops:
  1.5 8.8 %collective-permute-start.2 = (f32[32,256]{1,0:T(8,128)S(1)}, f32[32,256]{1,0:T(8,128)S(1)}, u32[]{:S(2)}, u32[]{:S(2)}) collective-permute-start(f32[32,256]{1,0:T(8,128)S(1)} %multiply_multiply_fusion.refs_0_), channel_id=1, source_target_pairs={{0,12},{2,14},{4,8},{6,10},{8,4},{10,6},{12,0},{14,2},{1,13},{3,15... | collective-permute-start | bytes 98312 | tf_op jit(solution)/shard_map/ppermute | solution.py:336
  6.5 4.8 %collective-permute-start.1 = (f32[32,256]{1,0:T(8,128)S(1)}, f32[32,256]{1,0:T(8,128)S(1)}, u32[]{:S(2)}, u32[]{:S(2)}) collective-permute-start(f32[32,256]{1,0:T(8,128)S(1)} %multiply_multiply_fusion.refs_0_), channel_id=1, source_target_pairs={{0,8},{2,10},{4,12},{6,14},{8,0},{10,2},{12,4},{14,6},{1,9},{3,11}... | collective-permute-start | bytes 98312 | tf_op jit(solution)/shard_map/ppermute | solution.py:336
  6.5 4.8 %collective-permute-start = (f32[32,256]{1,0:T(8,128)S(1)}, f32[32,256]{1,0:T(8,128)S(1)}, u32[]{:S(2)}, u32[]{:S(2)}) collective-permute-start(f32[32,256]{1,0:T(8,128)S(1)} %multiply_multiply_fusion.refs_0_), channel_id=1, source_target_pairs={{0,4},{2,6},{4,0},{6,2},{8,12},{10,14},{12,8},{14,10},{1,5},{3,7},... | collective-permute-start | bytes 98312 | tf_op jit(solution)/shard_map/ppermute | solution.py:336
  11.4 5.0 %collective-permute-start.3 = (f32[4,32,256]{2,1,0:T(8,128)S(1)}, f32[4,32,256]{2,1,0:T(8,128)S(1)}, u32[]{:S(2)}, u32[]{:S(2)}) collective-permute-start(f32[4,32,256]{2,1,0:T(8,128)S(1)} %join.1.joined_ref.even_ref), channel_id=1, source_target_pairs={{0,2},{2,0},{4,6},{6,4},{8,10},{10,8},{12,14},{14,12},{1,3},{3,1},... | collective-permute-start | bytes 393224 | tf_op jit(solution)/shard_map/ppermute | solution.py:336
  12.9 2.2 %collective-permute-start.4 = (f32[32,256]{1,0:T(8,128)S(1)}, f32[32,256]{1,0:T(8,128)S(1)}, u32[]{:S(2)}, u32[]{:S(2)}) collective-permute-start(f32[32,256]{1,0:T(8,128)S(1)} %multiply_multiply_fusion.refs_0_), channel_id=1, source_target_pairs={{0,1},{1,0},{2,3},{3,2},{4,5},{5,4},{6,7},{7,6},{8,9},{9,8},{10,11... | collective-permute-start | bytes 98312 | tf_op jit(solution)/shard_map/ppermute | solution.py:350
  17.6 1.3 %collective-permute-start.5 = (f32[32,640]{1,0:T(8,128)S(1)}, f32[32,640]{1,0:T(8,128)S(1)}, u32[]{:S(2)}, u32[]{:S(2)}) collective-permute-start(f32[32,640]{1,0:T(8,128)S(1)} %get-tuple-element.23.mine_ref), channel_id=1, source_target_pairs={{0,1},{1,0},{2,3},{3,2},{4,5},{5,4},{6,7},{7,6},{8,9},{9,8},{10,11... | collective-permute-start | bytes 245768 | tf_op jit(solution)/shard_map/ppermute | solution.py:350
  19.3 6.5 %collective-permute-start.9 = (f32[72,128]{1,0:T(8,128)S(1)}, f32[72,128]{1,0:T(8,128)S(1)}, u32[]{:S(2)}, u32[]{:S(2)}) collective-permute-start(f32[72,128]{1,0:T(8,128)S(1)} %get-tuple-element.25.refs_0_), channel_id=1, source_target_pairs={{0,8},{2,10},{4,12},{6,14},{8,0},{10,2},{12,4},{14,6},{1,9},{3,11}... | collective-permute-start | bytes 110600 | tf_op jit(solution)/shard_map/ppermute | solution.py:336
  21.3 8.0 %collective-permute-start.8 = (f32[72,128]{1,0:T(8,128)S(1)}, f32[72,128]{1,0:T(8,128)S(1)}, u32[]{:S(2)}, u32[]{:S(2)}) collective-permute-start(f32[72,128]{1,0:T(8,128)S(1)} %get-tuple-element.25.refs_0_), channel_id=1, source_target_pairs={{0,6},{2,4},{4,2},{6,0},{8,14},{10,12},{12,10},{14,8},{1,7},{3,5},... | collective-permute-start | bytes 110600 | tf_op jit(solution)/shard_map/ppermute | solution.py:336
  25.2 5.5 %collective-permute-start.7 = (f32[72,128]{1,0:T(8,128)S(1)}, f32[72,128]{1,0:T(8,128)S(1)}, u32[]{:S(2)}, u32[]{:S(2)}) collective-permute-start(f32[72,128]{1,0:T(8,128)S(1)} %get-tuple-element.25.refs_0_), channel_id=1, source_target_pairs={{0,4},{2,6},{4,0},{6,2},{8,12},{10,14},{12,8},{14,10},{1,5},{3,7},... | collective-permute-start | bytes 110600 | tf_op jit(solution)/shard_map/ppermute | solution.py:336
  25.2 5.5 %collective-permute-start.6 = (f32[72,128]{1,0:T(8,128)S(1)}, f32[72,128]{1,0:T(8,128)S(1)}, u32[]{:S(2)}, u32[]{:S(2)}) collective-permute-start(f32[72,128]{1,0:T(8,128)S(1)} %get-tuple-element.25.refs_0_), channel_id=1, source_target_pairs={{0,2},{2,0},{4,6},{6,4},{8,10},{10,8},{12,14},{14,12},{1,3},{3,1},... | collective-permute-start | bytes 110600 | tf_op jit(solution)/shard_map/ppermute | solution.py:336
  25.8 4.9 %collective-permute-start.11 = (f32[72,128]{1,0:T(8,128)S(1)}, f32[72,128]{1,0:T(8,128)S(1)}, u32[]{:S(2)}, u32[]{:S(2)}) collective-permute-start(f32[72,128]{1,0:T(8,128)S(1)} %collective-permute-done.9.refs_4_), channel_id=1, source_target_pairs={{0,4},{2,6},{4,0},{6,2},{8,12},{10,14},{12,8},{14,10},{1,5},{3,7},... | collective-permute-start | bytes 110600 | tf_op jit(solution)/shard_map/ppermute | solution.py:336
  27.2 4.0 %collective-permute-start.10 = (f32[72,128]{1,0:T(8,128)S(1)}, f32[72,128]{1,0:T(8,128)S(1)}, u32[]{:S(2)}, u32[]{:S(2)}) collective-permute-start(f32[72,128]{1,0:T(8,128)S(1)} %collective-permute-done.9.refs_4_), channel_id=1, source_target_pairs={{0,2},{2,0},{4,6},{6,4},{8,10},{10,8},{12,14},{14,12},{1,3},{3,1},... | collective-permute-start | bytes 110600 | tf_op jit(solution)/shard_map/ppermute | solution.py:336
  29.3 4.9 %collective-permute-start.12 = (f32[72,128]{1,0:T(8,128)S(1)}, f32[72,128]{1,0:T(8,128)S(1)}, u32[]{:S(2)}, u32[]{:S(2)}) collective-permute-start(f32[72,128]{1,0:T(8,128)S(1)} %collective-permute-done.8.refs_3_), channel_id=1, source_target_pairs={{0,8},{2,10},{4,12},{6,14},{8,0},{10,2},{12,4},{14,6},{1,9},{3,11}... | collective-permute-start | bytes 110600 | tf_op jit(solution)/shard_map/ppermute | solution.py:336
  37.0 1.2 %collective-permute-start.13 = (f32[8,128]{1,0:T(8,128)S(1)}, f32[8,128]{1,0:T(8,128)S(1)}, u32[]{:S(2)}, u32[]{:S(2)}) collective-permute-start(f32[8,128]{1,0:T(8,128)S(1)} %get-tuple-element.28.mine_ref), channel_id=1, source_target_pairs={{0,1},{1,0},{2,3},{3,2},{4,5},{5,4},{6,7},{7,6},{8,9},{9,8},{10,11... | collective-permute-start | bytes 12296 | tf_op jit(solution)/shard_map/ppermute | solution.py:350
  39.3 1.3 %collective-permute-start.14 = (f32[32,512]{1,0:T(8,128)S(1)}, f32[32,512]{1,0:T(8,128)S(1)}, u32[]{:S(2)}, u32[]{:S(2)}) collective-permute-start(f32[32,512]{1,0:T(8,128)S(1)} %get-tuple-element.30.mine_ref), channel_id=1, source_target_pairs={{0,1},{1,0},{2,3},{3,2},{4,5},{5,4},{6,7},{7,6},{8,9},{9,8},{10,11... | collective-permute-start | bytes 196616 | tf_op jit(solution)/shard_map/ppermute | solution.py:350
  40.9 5.0 %collective-permute-start.18 = (f32[72,128]{1,0:T(8,128)S(1)}, f32[72,128]{1,0:T(8,128)S(1)}, u32[]{:S(2)}, u32[]{:S(2)}) collective-permute-start(f32[72,128]{1,0:T(8,128)S(1)} %get-tuple-element.32.refs_0_), channel_id=1, source_target_pairs={{0,8},{2,10},{4,12},{6,14},{8,0},{10,2},{12,4},{14,6},{1,9},{3,11}... | collective-permute-start | bytes 110600 | tf_op jit(solution)/shard_map/ppermute | solution.py:336
  42.3 4.9 %collective-permute-start.17 = (f32[72,128]{1,0:T(8,128)S(1)}, f32[72,128]{1,0:T(8,128)S(1)}, u32[]{:S(2)}, u32[]{:S(2)}) collective-permute-start(f32[72,128]{1,0:T(8,128)S(1)} %get-tuple-element.32.refs_0_), channel_id=1, source_target_pairs={{0,6},{2,4},{4,2},{6,0},{8,14},{10,12},{12,10},{14,8},{1,7},{3,5},... | collective-permute-start | bytes 110600 | tf_op jit(solution)/shard_map/ppermute | solution.py:336
  42.3 6.5 %collective-permute-start.16 = (f32[72,128]{1,0:T(8,128)S(1)}, f32[72,128]{1,0:T(8,128)S(1)}, u32[]{:S(2)}, u32[]{:S(2)}) collective-permute-start(f32[72,128]{1,0:T(8,128)S(1)} %get-tuple-element.32.refs_0_), channel_id=1, source_target_pairs={{0,4},{2,6},{4,0},{6,2},{8,12},{10,14},{12,8},{14,10},{1,5},{3,7},... | collective-permute-start | bytes 110600 | tf_op jit(solution)/shard_map/ppermute | solution.py:336
  43.9 5.0 %collective-permute-start.15 = (f32[72,128]{1,0:T(8,128)S(1)}, f32[72,128]{1,0:T(8,128)S(1)}, u32[]{:S(2)}, u32[]{:S(2)}) collective-permute-start(f32[72,128]{1,0:T(8,128)S(1)} %get-tuple-element.32.refs_0_), channel_id=1, source_target_pairs={{0,2},{2,0},{4,6},{6,4},{8,10},{10,8},{12,14},{14,12},{1,3},{3,1},... | collective-permute-start | bytes 110600 | tf_op jit(solution)/shard_map/ppermute | solution.py:336
  45.9 4.4 %collective-permute-start.20 = (f32[72,128]{1,0:T(8,128)S(1)}, f32[72,128]{1,0:T(8,128)S(1)}, u32[]{:S(2)}, u32[]{:S(2)}) collective-permute-start(f32[72,128]{1,0:T(8,128)S(1)} %collective-permute-done.18.refs_4_), channel_id=1, source_target_pairs={{0,4},{2,6},{4,0},{6,2},{8,12},{10,14},{12,8},{14,10},{1,5},{3,7},... | collective-permute-start | bytes 110600 | tf_op jit(solution)/shard_map/ppermute | solution.py:336
  45.9 4.4 %collective-permute-start.19 = (f32[72,128]{1,0:T(8,128)S(1)}, f32[72,128]{1,0:T(8,128)S(1)}, u32[]{:S(2)}, u32[]{:S(2)}) collective-permute-start(f32[72,128]{1,0:T(8,128)S(1)} %collective-permute-done.18.refs_4_), channel_id=1, source_target_pairs={{0,2},{2,0},{4,6},{6,4},{8,10},{10,8},{12,14},{14,12},{1,3},{3,1},... | collective-permute-start | bytes 110600 | tf_op jit(solution)/shard_map/ppermute | solution.py:336
  47.2 4.9 %collective-permute-start.21 = (f32[72,128]{1,0:T(8,128)S(1)}, f32[72,128]{1,0:T(8,128)S(1)}, u32[]{:S(2)}, u32[]{:S(2)}) collective-permute-start(f32[72,128]{1,0:T(8,128)S(1)} %collective-permute-done.17.refs_3_), channel_id=1, source_target_pairs={{0,8},{2,10},{4,12},{6,14},{8,0},{10,2},{12,4},{14,6},{1,9},{3,11}... | collective-permute-start | bytes 110600 | tf_op jit(solution)/shard_map/ppermute | solution.py:336
  55.0 1.2 %collective-permute-start.22 = (f32[8,128]{1,0:T(8,128)S(1)}, f32[8,128]{1,0:T(8,128)S(1)}, u32[]{:S(2)}, u32[]{:S(2)}) collective-permute-start(f32[8,128]{1,0:T(8,128)S(1)} %get-tuple-element.36.mine_ref), channel_id=1, source_target_pairs={{0,1},{1,0},{2,3},{3,2},{4,5},{5,4},{6,7},{7,6},{8,9},{9,8},{10,11... | collective-permute-start | bytes 12296 | tf_op jit(solution)/shard_map/ppermute | solution.py:350
  58.2 11.5 %all-to-all-start = ((f32[16,8,128]{2,1,0:T(8,128)}), f32[16,8,128]{2,1,0:T(8,128)S(1)}, u32[]{:S(2)}, u32[]{:S(2)}) async-start(f32[16,8,128]{2,1,0:T(8,128)} %get-tuple-element.38), calls=%async_computation | async-start | bytes 131072 | tf_op jit(solution)/shard_map/all_to_all | solution.py:461
  62.7 1.3 %collective-permute-start.23 = (f32[32,512]{1,0:T(8,128)S(1)}, f32[32,512]{1,0:T(8,128)S(1)}, u32[]{:S(2)}, u32[]{:S(2)}) collective-permute-start(f32[32,512]{1,0:T(8,128)S(1)} %get-tuple-element.39.mine_ref), channel_id=1, source_target_pairs={{0,1},{1,0},{2,3},{3,2},{4,5},{5,4},{6,7},{7,6},{8,9},{9,8},{10,11... | collective-permute-start | bytes 196616 | tf_op jit(solution)/shard_map/ppermute | solution.py:350

commit v6 on v5

--- a/solution.py
+++ b/solution.py
@@ -38,66 +38,75 @@
     return jnp.dot(left, right, precision=lax.Precision.HIGHEST, preferred_element_type=F32)
 
 
-def factor(left):
+def stack(left):
     high, middle, low = split(left)
-    return jnp.concatenate([high, high, middle, high, middle, low], axis=1)
-
-
-def times(prepared, right):
+    return jnp.concatenate([high, high, middle, high, middle, low], axis=0)
+
+
+def times(stacked, right):
     high, middle, low = split(right)
-    stacked = jnp.concatenate([high, middle, high, low, middle, high], axis=0)
-    return jnp.dot(prepared, stacked, preferred_element_type=F32)
-
-
-def grams(left, rights):
-    size = left.shape[0]
-    parts = [split(right) for right in rights]
-    parts = parts + [parts[0]] * (LANES // size - len(parts))
-    stacked = jnp.concatenate([part[i] for i in range(3) for part in parts], axis=0)
+    return lax.dot_general(
+        stacked,
+        jnp.concatenate([high, middle, high, low, middle, high], axis=0),
+        (((0,), (0,)), ((), ())),
+        preferred_element_type=F32,
+    )
+
+
+def gram_parts(left, right):
+    size, width = left.shape
+    filler = jnp.zeros((LANES - 3 * size, width), BF16)
     every = lax.dot_general(
         jnp.concatenate(split(left), axis=0),
-        stacked,
+        jnp.concatenate([*split(right), filler], axis=0),
         (((1,), (1,)), ((), ())),
         preferred_element_type=F32,
     )
-    rows = every[2 * size :] + every[size : 2 * size] + every[:size]
-    return rows[:, 2 * LANES :] + rows[:, LANES : 2 * LANES] + rows[:, :LANES]
-
-
-def widen(matrix):
-    rows, columns = matrix.shape
-    return jnp.concatenate([matrix, jnp.zeros((rows, LANES - columns), F32)], axis=1)
-
-
-def pack(matrix):
-    rows = matrix.shape[0]
-    wide = widen(matrix)
+    return every[2 * size :] + every[size : 2 * size] + every[:size]
+
+
+def symmetric_parts(left, right):
+    return 0.5 * (gram_parts(left, right) + gram_parts(right, left))
+
+
+def finish(parts, place=0):
+    size = parts.shape[0]
+
+    def block(index):
+        shift = (place - index) * size % LANES
+        return pltpu.roll(parts, shift, 1) if shift else parts
+
+    return block(2) + block(1) + block(0)
+
+
+def pack(wide):
+    rows = wide.shape[0]
     folds = LANES // rows
     height = rows // folds
+    lanes = lax.broadcasted_iota(jnp.int32, wide.shape, 1)
+    wide = jnp.where(lanes < rows, wide, 0.0)
     total = wide[:height]
     for i in range(1, folds):
         total = total + pltpu.roll(wide[i * height : (i + 1) * height], i * rows, 1)
     return total
 
 
-def unpack(folded, size):
-    folds = LANES // size
-    parts = [folded] + [pltpu.roll(folded, LANES - i * size, 1) for i in range(1, folds)]
-    return jnp.concatenate(parts, axis=0)[:, :size]
-
-
-def symmetric(matrix):
-    return 0.5 * (matrix + matrix.T)
-
-
-def solve_wide(matrix, target):
+def unpack(folded, size, place=0):
+    parts = []
+    for i in range(LANES // size):
+        shift = (place - i) * size % LANES
+        parts.append(pltpu.roll(folded, shift, 1) if shift else folded)
+    return jnp.concatenate(parts, axis=0)
+
+
+def solve_wide(target, matrix):
     size = matrix.shape[0]
     row_ids = lax.broadcasted_iota(jnp.int32, (size, LANES), 0)
     lane_ids = lax.broadcasted_iota(jnp.int32, (size, LANES), 1)
-    work = jnp.where(lane_ids < size, matrix, pltpu.roll(target, size, 1))
+    work = jnp.where(lane_ids < size, target, matrix)
     for base in range(0, size, PIVOTS):
         columns = [
-            jnp.broadcast_to(work[:, base + i : base + i + 1], (size, LANES))
+            jnp.broadcast_to(work[:, size + base + i : size + base + i + 1], (size, LANES))
             for i in range(PIVOTS)
         ]
         for i in range(PIVOTS):
@@ -109,7 +118,7 @@
             for later in range(i + 1, PIVOTS):
                 entry = columns[later][pivot : pivot + 1, :] * inverse
                 columns[later] = jnp.where(here, entry, columns[later] - columns[i] * entry)
-    return pltpu.roll(work, LANES - size, 1)
+    return work
 
 
 def add_up(values):
@@ -221,7 +230,8 @@
     for k, value in enumerate(values + [far_ref[...]]):
         state_ref[k] = value
     rows = 2 * values[0].shape[1]
-    out_ref[:, rows:] = add_up([grams(value, [value]) for value in values])
+    joined = jnp.concatenate(values, axis=1)
+    out_ref[:, rows:] = gram_parts(joined, joined)
     out_ref[:, :rows] = apply_dense(values, matrix)
 
 
@@ -238,23 +248,33 @@
     near, far = add_halves(mine_ref, other_ref, width)
     far_ref[...] = far
     if first:
-        outs[2][...] = mine_ref[:, 2 * width :] + other_ref[:, 2 * width :]
+        outs[2][...] = finish(mine_ref[:, 2 * width :] + other_ref[:, 2 * width :])
     for i in range(width // LANES):
         out_ref[i * size : (i + 1) * size] = near[:, i * LANES : (i + 1) * LANES]
-    product = grams(near, [direction_ref[0]]) + grams(far, [direction_ref[last]])
-    out_ref[width // LANES * size :] = pack(product[:, :size])
+    out_ref[width // LANES * size :] = symmetric_parts(near, direction_ref[0]) + symmetric_parts(
+        far, direction_ref[last]
+    )
 
 
 def inverse_kernel(norm_ref, out_ref):
-    norm = widen(symmetric(norm_ref[:, : norm_ref.shape[0]]))
+    norm = norm_ref[...]
+    size = norm.shape[0]
+    norm = 0.5 * (norm + jnp.concatenate([norm[:, :size].T, norm[:, size:]], axis=1))
     unit = lax.broadcasted_iota(jnp.int32, norm.shape, 0) == lax.broadcasted_iota(
         jnp.int32, norm.shape, 1
     )
-    out_ref[...] = solve_wide(norm, jnp.where(unit, 1.0, 0.0))
+    out_ref[...] = solve_wide(jnp.where(unit, 1.0, 0.0), pltpu.roll(norm, size, 1))
+
+
+def arrivals(pieces):
+    half = pieces // 2
+    forwarded = [*range(half + 1, pieces - 1), pieces - 1]
+    own = [k for k in range(1, half - 1)] + [half, half - 1]
+    return [0, *forwarded, *own]
 
 
 def residual_kernel(pieces, with_solution, last, *refs):
-    images = refs[:pieces]
+    images = [refs[arrivals(pieces).index(k)] for k in range(pieces)]
     far_ref, direction_ref, residual_ref, norm_ref = refs[pieces : pieces + 4]
     refs = refs[pieces + 4 :]
     if with_solution:
@@ -262,10 +282,9 @@
     new_residual, half_ref, new_solution = refs[:3]
     size, width = far_ref.shape
     parts = width // LANES
-    curvature = unpack(add_up([ref[parts * size :] for ref in images]), size)
-    alpha = solve_wide(widen(symmetric(curvature)), norm_ref[...])[:, :size]
-    alpha_t = factor(alpha.T)
-    products = []
+    curvature = finish(add_up([ref[parts * size :] for ref in images]), 1)
+    alpha = stack(solve_wide(norm_ref[...], curvature)[:, :size])
+    residuals = []
     for k in range(pieces + 1):
         if k < pieces:
             image = jnp.concatenate(
@@ -273,14 +292,15 @@
             )
         else:
             image = far_ref[...]
-        residual = residual_ref[k] - times(alpha_t, image)
+        residual = residual_ref[k] - times(alpha, image)
         new_residual[k] = residual
         if last and k == 0:
             refs[3][...] = residual
         if k < pieces:
-            products.append(grams(residual, [residual]))
-    half_ref[...] = pack(add_up(products)[:, :size])
-    step = times(alpha_t, direction_ref[0])
+            residuals.append(residual)
+    joined = jnp.concatenate(residuals, axis=1)
+    half_ref[...] = gram_parts(joined, joined)
+    step = times(alpha, direction_ref[0])
     new_solution[...] = solution_ref[...] + step if with_solution else step
 
 
@@ -289,21 +309,21 @@
 ):
     out_ref, new_direction, new_norm = outs[:3]
     size, width = residual_ref.shape[1:]
-    next_norm = unpack(mine_ref[...] + other_ref[...], size)
-    new_norm[...] = widen(next_norm)
-    beta_t = factor(mul(next_norm, inverse_ref[:, :size]))
+    next_norm = finish(mine_ref[...] + other_ref[...])
+    new_norm[...] = next_norm
+    beta = stack(mul(inverse_ref[:, :size], next_norm[:, :size]))
     directions = []
     for k in range(pieces + 1):
-        direction = residual_ref[k] + times(beta_t, direction_ref[k])
+        direction = residual_ref[k] + times(beta, direction_ref[k])
         if k < new_direction.shape[0]:
             new_direction[k] = direction
         directions.append(direction)
     image = apply_dense(directions[:pieces], matrix)
     out_ref[...] = image
     if last:
-        near = grams(image[:, :width], [directions[0]])
-        far = grams(image[:, width:], [directions[pieces]])
-        gram = pack((near + far)[:, :size])
+        near = symmetric_parts(image[:, :width], directions[0])
+        far = symmetric_parts(image[:, width:], directions[pieces])
+        gram = pack(finish(near + far))
         for k in range(outs[3].shape[0]):
             outs[3][k] = gram
 
@@ -313,11 +333,11 @@
     new_solution, new_residual,
 ):
     size, width = solution_ref.shape
-    curvature = unpack(add_up([grams_ref[k] for k in range(grams_ref.shape[0])]), size)
-    alpha_t = factor(solve_wide(widen(symmetric(curvature)), norm_ref[...])[:, :size].T)
-    new_solution[...] = solution_ref[...] + times(alpha_t, direction_ref[0])
+    curvature = unpack(add_up([grams_ref[k] for k in range(grams_ref.shape[0])]), size, 1)
+    alpha = stack(solve_wide(norm_ref[...], curvature)[:, :size])
+    new_solution[...] = solution_ref[...] + times(alpha, direction_ref[0])
     image = mine_ref[:, :width] + other_ref[:, width:]
-    new_residual[...] = residual_ref[...] - times(alpha_t, image)
+    new_residual[...] = residual_ref[...] - times(alpha, image)
 
 
 def shape(*dims, dtype=F32):
@@ -401,8 +421,7 @@
     state = shape(pieces + 1, sketch, rows_dev)
     small = shape(sketch, LANES)
     piece = shape(sketch, rows_dev)
-    packed = shape(sketch * sketch // LANES, LANES)
-    payload = shape(sketch * (rows_dev // LANES) + packed.shape[0], LANES)
+    payload = shape(sketch * (rows_dev // LANES + 1), LANES)
 
     partial_sum, direction = pl.pallas_call(
         first_kernel,
@@ -437,17 +456,18 @@
             compiler_params=params(),
             name="inverse",
         )(norm)
+        images = around(image)
         given = () if first else (solution,)
         residual, half, solution, *own = pl.pallas_call(
             functools.partial(residual_kernel, pieces, not first, last),
-            out_shape=(state, packed, piece) + ((piece,) if last else ()),
+            out_shape=(state, small, piece) + ((piece,) if last else ()),
             in_specs=[VMEM] * (pieces + 4 + len(given)),
             out_specs=(VMEM,) * (4 if last else 3),
             compiler_params=params(state, state, state, state),
             name="residual",
-        )(*around(image), far, direction, residual, norm, *given)
+        )(*[images[k] for k in arrivals(pieces)], far, direction, residual, norm, *given)
         kept = shape(1, sketch, rows_dev) if last else state
-        gram = shape(pieces * col_devices, *packed.shape)
+        gram = shape(pieces * col_devices, sketch * sketch // LANES, LANES)
         outs = pl.pallas_call(
             functools.partial(direction_kernel, pieces, last),
             out_shape=(shape(sketch, group), kept, small) + ((gram,) if last else ()),

time: 71.4 us -> 66.9 us (0.937)
  starting transfers between devices: 31.9 us -> 27.2 us
  waiting for transfers between devices: 18.2 us -> 20.5 us
  Pallas kernels: 19.2 us -> 17.1 us
    ppermute x18, starting transfers between devices: 26.4 us -> 21.8 us  [swap(): return lax.ppermute(value, 'row', [(i, i ^ mask) for i in range(pieces)])]
    pallas_call x2, Pallas kernels: 5.76 us -> 2.81 us  [per_device(): pl.pallas_call(functools.partial(residual_kernel, pieces, not first, last...]
    ppermute x18, waiting for transfers between devices: 9.11 us -> 11.3 us  [swap(): return lax.ppermute(value, 'row', [(i, i ^ mask) for i in range(pieces)])]
    pallas_call x1, Pallas kernels: 2.49 us -> 4.14 us  [per_device(): pl.pallas_call(functools.partial(gather_kernel, rows_dev), out_shape=tota...]
  transfers between devices with their start and end apart: 25 -> 25, of which waited for: 13 -> 15; matrix products, arithmetic and copies ran while one was open for 0% -> 0% of each run, Pallas kernels for 9% -> 12%
where the time goes in v6:
time: 66.9 us; the launch traced here: 67.1 us
  starting transfers between devices  27.2 us (41%)
  waiting for transfers between devices  20.5 us (31%)
  Pallas kernels  17.1 us (26%)
  between operations  1.4 us (2%)
  other arithmetic  0.85 us (1%)
    ppermute x18, starting transfers between devices, swap(): return lax.ppermute(value, 'row', [(i, i ^ mask) for i in range(pieces)])  21.8 us
    ppermute x18, waiting for transfers between devices, swap(): return lax.ppermute(value, 'row', [(i, i ^ mask) for i in range(pieces)])  11.3 us
    all_to_all x1, waiting for transfers between devices, per_device(): every = lax.all_to_all(outs[3], ('row', 'col'), 0, 0)  5.58 us
    all_to_all x1, starting transfers between devices, per_device(): every = lax.all_to_all(outs[3], ('row', 'col'), 0, 0)  4.51 us
    pallas_call x1, Pallas kernels, per_device(): pl.pallas_call(functools.partial(gather_kernel, rows_dev), out_shape=tota...  4.14 us
    ppermute x6, waiting for transfers between devices, across(): lax.ppermute(value, 'col', [(i, (i + 1) % col_devices) for i in range(col...  3.66 us
    pallas_call x2, Pallas kernels, per_device(): pl.pallas_call(functools.partial(direction_kernel, pieces, last), out_sha...  3.13 us
    pallas_call x2, Pallas kernels, per_device(): pl.pallas_call(functools.partial(residual_kernel, pieces, not first, last...  2.81 us
  transfers between devices with their start and end apart: 25, of which 15 were waited for; matrix products, arithmetic and copies ran while one was open for 0% of the time, Pallas kernels for 12%

profile of v6, /device:TPU:0, one launch (start us, length us, event | category | flops | bytes accessed | tf_op | source)
XLA Modules:
  0.0 67.1 jit_solution(12014777823722799407)
XLA Ops:
  0.6 0.8 %multiply_multiply_fusion.refs_0_ = f32[32,256]{1,0:T(8,128)S(1)} fusion(s32[32,256]{1,0:T(8,128)} %param.11, f32[32]{0:T(128)} %param.13, f32[256]{0:T(256)} %param.12), kind=kLoop, calls=%fused_computation | loop fusion | flops 24576 | bytes 66688 | tf_op jit(solution)/shard_map/mul | solution.py:374
  1.5 5.1 %collective-permute-start.2 = (f32[32,256]{1,0:T(8,128)S(1)}, f32[32,256]{1,0:T(8,128)S(1)}, u32[]{:S(2)}, u32[]{:S(2)}) collective-permute-start(f32[32,256]{1,0:T(8,128)S(1)} %multiply_multiply_fusion.refs_0_), channel_id=1, source_target_pairs={{0,12},{2,14},{4,8},{6,10},{8,4},{10,6},{12,0},{14,2},{1,13},{3,15... | collective-permute-start | bytes 98312 | tf_op jit(solution)/shard_map/ppermute | solution.py:356
  6.5 0.0 collective-permute-start.1
  6.5 0.6 collective-permute-start
  7.8 4.1 %gather.1.refs_4_.total = f32[64,128,128]{2,1,0:T(8,128)S(1)} custom-call(s32[1]{0:T(128)S(6)} %copy.9.count_ref, s32[130]{0:T(256)} %rows_hbm.1, s32[130]{0:T(256)} %cols_hbm.1, bf16[130,128,128]{2,1,0:T(8,128)(2,1)} %tiles_ref.1), custom_call_target="tpu_custom_call" | custom-call | flops 8519680 | bytes 8519680 | tf_op jit(solution)/shard_map/gather/pallas_call | solution.py:381
  12.0 0.0 collective-permute-done.2.refs_3_
  12.0 0.0 collective-permute-done.1.refs_2_
  12.0 0.0 collective-permute-done.refs_1_
  12.0 0.9 %collective-permute-start.3 = (f32[4,32,256]{2,1,0:T(8,128)S(1)}, f32[4,32,256]{2,1,0:T(8,128)S(1)}, u32[]{:S(2)}, u32[]{:S(2)}) collective-permute-start(f32[4,32,256]{2,1,0:T(8,128)S(1)} %join.1.joined_ref.even_ref), channel_id=1, source_target_pairs={{0,2},{2,0},{4,6},{6,4},{8,10},{10,8},{12,14},{14,12},{1,3},{3,1},... | collective-permute-start | bytes 393224 | tf_op jit(solution)/shard_map/ppermute | solution.py:356
  12.9 0.0 collective-permute-start.4
  13.0 2.2 %dense.1.matrix = bf16[2,2048,512]{2,1,0:T(8,128)(2,1)S(1)} custom-call(f32[64,128,128]{2,1,0:T(8,128)S(1)} %gather.1.refs_4_.total, f32[4,32,256]{2,1,0:T(8,128)S(1)} %join.1.joined_ref.even_ref), custom_call_target="tpu_custom_call" | custom-call | flops 8519680 | bytes 8519680 | tf_op jit(solution)/shard_map/dense/pallas_call | solution.py:409
  15.2 0.0 collective-permute-done.4.far_ref
  15.2 1.9 %collective-permute-done.3.odd_ref = f32[4,32,256]{2,1,0:T(8,128)S(1)} collective-permute-done((f32[4,32,256]{2,1,0:T(8,128)S(1)}, f32[4,32,256]{2,1,0:T(8,128)S(1)}, u32[]{:S(2)}, u32[]{:S(2)}) %collective-permute-start.3) | collective-permute-done | bytes 131104 | tf_op jit(solution)/shard_map/ppermute | solution.py:356
  17.1 0.9 %first.1 = (f32[32,640]{1,0:T(8,128)S(1)}, f32[9,32,256]{2,1,0:T(8,128)S(1)}) custom-call(f32[4,32,256]{2,1,0:T(8,128)S(1)} %join.1.joined_ref.even_ref, f32[4,32,256]{2,1,0:T(8,128)S(1)} %collective-permute-done.3.odd_ref, f32[32,256]{1,0:T(8,128)S(1)} %collective-permute-done.4.far_ref, bf16[2,2048,512]{2,1,0:T(8,128)(2,1)S(1)} %dense.1.matrix), custom_call_target="tpu_custom_call" | custom-call | tf_op jit(solution)/shard_map/first/pallas_call | solution.py:426
  17.9 0.1 collective-permute-start.5
  18.0 1.3 %collective-permute-done.5.other_ref = f32[32,640]{1,0:T(8,128)S(1)} collective-permute-done((f32[32,640]{1,0:T(8,128)S(1)}, f32[32,640]{1,0:T(8,128)S(1)}, u32[]{:S(2)}, u32[]{:S(2)}) %collective-permute-start.5) | collective-permute-done | bytes 81952 | tf_op jit(solution)/shard_map/ppermute | solution.py:370
  19.3 0.2 image.2
  19.5 0.6 collective-permute-start.9
  20.1 3.0 %collective-permute-start.6 = (f32[96,128]{1,0:T(8,128)S(1)}, f32[96,128]{1,0:T(8,128)S(1)}, u32[]{:S(2)}, u32[]{:S(2)}) collective-permute-start(f32[96,128]{1,0:T(8,128)S(1)} %get-tuple-element.25.refs_0_), channel_id=1, source_target_pairs={{0,8},{2,10},{4,12},{6,14},{8,0},{10,2},{12,4},{14,6},{1,9},{3,11}... | collective-permute-start | bytes 147464 | tf_op jit(solution)/shard_map/ppermute | solution.py:356
  23.1 0.8 %collective-permute-start.12 = (f32[96,128]{1,0:T(8,128)S(1)}, f32[96,128]{1,0:T(8,128)S(1)}, u32[]{:S(2)}, u32[]{:S(2)}) collective-permute-start(f32[96,128]{1,0:T(8,128)S(1)} %get-tuple-element.25.refs_0_), channel_id=1, source_target_pairs={{0,4},{2,6},{4,0},{6,2},{8,12},{10,14},{12,8},{14,10},{1,5},{3,7},... | collective-permute-start | bytes 147464 | tf_op jit(solution)/shard_map/ppermute | solution.py:356
  23.8 0.5 collective-permute-start.11
  24.3 1.2 %collective-permute-done.9.refs_7_ = f32[96,128]{1,0:T(8,128)S(1)} collective-permute-done((f32[96,128]{1,0:T(8,128)S(1)}, f32[96,128]{1,0:T(8,128)S(1)}, u32[]{:S(2)}, u32[]{:S(2)}) %collective-permute-start.9) | collective-permute-done | bytes 49184 | tf_op jit(solution)/shard_map/ppermute | solution.py:356
  25.5 0.5 collective-permute-start.10
  26.0 0.0 collective-permute-done.6.refs_6_
  26.0 2.1 %collective-permute-start.8 = (f32[96,128]{1,0:T(8,128)S(1)}, f32[96,128]{1,0:T(8,128)S(1)}, u32[]{:S(2)}, u32[]{:S(2)}) collective-permute-start(f32[96,128]{1,0:T(8,128)S(1)} %collective-permute-done.6.refs_6_), channel_id=1, source_target_pairs={{0,4},{2,6},{4,0},{6,2},{8,12},{10,14},{12,8},{14,10},{1,5},{3,7},... | collective-permute-start | bytes 147464 | tf_op jit(solution)/shard_map/ppermute | solution.py:356
  28.1 1.3 %collective-permute-start.7 = (f32[96,128]{1,0:T(8,128)S(1)}, f32[96,128]{1,0:T(8,128)S(1)}, u32[]{:S(2)}, u32[]{:S(2)}) collective-permute-start(f32[96,128]{1,0:T(8,128)S(1)} %collective-permute-done.6.refs_6_), channel_id=1, source_target_pairs={{0,2},{2,0},{4,6},{6,4},{8,10},{10,8},{12,14},{14,12},{1,3},{3,1},... | collective-permute-start | bytes 147464 | tf_op jit(solution)/shard_map/ppermute | solution.py:356
  29.4 0.0 collective-permute-done.12.refs_5_
  29.4 0.0 collective-permute-done.11.refs_4_
  29.4 1.4 %collective-permute-done.10.refs_3_ = f32[96,128]{1,0:T(8,128)S(1)} collective-permute-done((f32[96,128]{1,0:T(8,128)S(1)}, f32[96,128]{1,0:T(8,128)S(1)}, u32[]{:S(2)}, u32[]{:S(2)}) %collective-permute-start.10) | collective-permute-done | bytes 49184 | tf_op jit(solution)/shard_map/ppermute | solution.py:356
  30.8 0.0 collective-permute-done.8.refs_2_
  30.8 1.3 %collective-permute-done.7.refs_1_ = f32[96,128]{1,0:T(8,128)S(1)} collective-permute-done((f32[96,128]{1,0:T(8,128)S(1)}, f32[96,128]{1,0:T(8,128)S(1)}, u32[]{:S(2)}, u32[]{:S(2)}) %collective-permute-start.7) | collective-permute-done | bytes 49184 | tf_op jit(solution)/shard_map/ppermute | solution.py:356
  32.2 1.4 %residual.2 = (f32[9,32,256]{2,1,0:T(8,128)S(1)}, f32[32,128]{1,0:T(8,128)S(1)}, f32[32,256]{1,0:T(8,128)S(1)}) custom-call(f32[96,128]{1,0:T(8,128)S(1)} %get-tuple-element.25.refs_0_, f32[96,128]{1,0:T(8,128)S(1)} %collective-permute-done.7.refs_1_, f32[96,128]{1,0:T(8,128)S(1)} %collective-permute-done.8.refs_2_, ...), custom_call_target="tpu_custom_call" | custom-call | tf_op jit(solution)/shard_map/residual/pallas_call | solution.py:461
  33.6 0.0 collective-permute-start.13
  33.6 1.0 %inverse.2.inverse_ref = f32[32,128]{1,0:T(8,128)S(1)} custom-call(f32[32,128]{1,0:T(8,128)S(1)} %get-tuple-element.27.refs_11_.norm_ref), custom_call_target="tpu_custom_call" | custom-call | tf_op jit(solution)/shard_map/inverse/pallas_call | solution.py:451
  34.6 0.2 collective-permute-done.13.other_ref
  34.8 1.1 %direction.2 = (f32[32,512]{1,0:T(8,128)S(1)}, f32[9,32,256]{2,1,0:T(8,128)S(1)}, f32[32,128]{1,0:T(8,128)S(1)}) custom-call(f32[32,128]{1,0:T(8,128)S(1)} %get-tuple-element.28.mine_ref, f32[32,128]{1,0:T(8,128)S(1)} %collective-permute-done.13.other_ref, f32[32,128]{1,0:T(8,128)S(1)} %inverse.2.inverse_ref, ...), custom_call_target="tpu_custom_call" | custom-call | tf_op jit(solution)/shard_map/direction/pallas_call | solution.py:471
  35.9 0.3 collective-permute-start.14
  36.2 1.0 %collective-permute-done.14.other_ref = f32[32,512]{1,0:T(8,128)S(1)} collective-permute-done((f32[32,512]{1,0:T(8,128)S(1)}, f32[32,512]{1,0:T(8,128)S(1)}, u32[]{:S(2)}, u32[]{:S(2)}) %collective-permute-start.14) | collective-permute-done | bytes 65568 | tf_op jit(solution)/shard_map/ppermute | solution.py:370
  37.2 0.2 image.3
  37.4 1.3 %collective-permute-start.18 = (f32[96,128]{1,0:T(8,128)S(1)}, f32[96,128]{1,0:T(8,128)S(1)}, u32[]{:S(2)}, u32[]{:S(2)}) collective-permute-start(f32[96,128]{1,0:T(8,128)S(1)} %get-tuple-element.32.refs_0_), channel_id=1, source_target_pairs={{0,6},{2,4},{4,2},{6,0},{8,14},{10,12},{12,10},{14,8},{1,7},{3,5},... | collective-permute-start | bytes 147464 | tf_op jit(solution)/shard_map/ppermute | solution.py:356
  38.7 0.9 %collective-permute-start.15 = (f32[96,128]{1,0:T(8,128)S(1)}, f32[96,128]{1,0:T(8,128)S(1)}, u32[]{:S(2)}, u32[]{:S(2)}) collective-permute-start(f32[96,128]{1,0:T(8,128)S(1)} %get-tuple-element.32.refs_0_), channel_id=1, source_target_pairs={{0,8},{2,10},{4,12},{6,14},{8,0},{10,2},{12,4},{14,6},{1,9},{3,11}... | collective-permute-start | bytes 147464 | tf_op jit(solution)/shard_map/ppermute | solution.py:356
  39.6 1.2 %collective-permute-start.21 = (f32[96,128]{1,0:T(8,128)S(1)}, f32[96,128]{1,0:T(8,128)S(1)}, u32[]{:S(2)}, u32[]{:S(2)}) collective-permute-start(f32[96,128]{1,0:T(8,128)S(1)} %get-tuple-element.32.refs_0_), channel_id=1, source_target_pairs={{0,4},{2,6},{4,0},{6,2},{8,12},{10,14},{12,8},{14,10},{1,5},{3,7},... | collective-permute-start | bytes 147464 | tf_op jit(solution)/shard_map/ppermute | solution.py:356
  40.8 1.0 %collective-permute-start.20 = (f32[96,128]{1,0:T(8,128)S(1)}, f32[96,128]{1,0:T(8,128)S(1)}, u32[]{:S(2)}, u32[]{:S(2)}) collective-permute-start(f32[96,128]{1,0:T(8,128)S(1)} %get-tuple-element.32.refs_0_), channel_id=1, source_target_pairs={{0,2},{2,0},{4,6},{6,4},{8,10},{10,8},{12,14},{14,12},{1,3},{3,1},... | collective-permute-start | bytes 147464 | tf_op jit(solution)/shard_map/ppermute | solution.py:356
  41.9 1.7 %collective-permute-done.18.refs_7_ = f32[96,128]{1,0:T(8,128)S(1)} collective-permute-done((f32[96,128]{1,0:T(8,128)S(1)}, f32[96,128]{1,0:T(8,128)S(1)}, u32[]{:S(2)}, u32[]{:S(2)}) %collective-permute-start.18) | collective-permute-done | bytes 49184 | tf_op jit(solution)/shard_map/ppermute | solution.py:356
  43.6 0.2 collective-permute-start.19
  43.8 0.4 collective-permute-done.15.refs_6_
  44.2 1.0 %collective-permute-start.17 = (f32[96,128]{1,0:T(8,128)S(1)}, f32[96,128]{1,0:T(8,128)S(1)}, u32[]{:S(2)}, u32[]{:S(2)}) collective-permute-start(f32[96,128]{1,0:T(8,128)S(1)} %collective-permute-done.15.refs_6_), channel_id=1, source_target_pairs={{0,4},{2,6},{4,0},{6,2},{8,12},{10,14},{12,8},{14,10},{1,5},{3,7},... | collective-permute-start | bytes 147464 | tf_op jit(solution)/shard_map/ppermute | solution.py:356
  45.2 0.7 %collective-permute-start.16 = (f32[96,128]{1,0:T(8,128)S(1)}, f32[96,128]{1,0:T(8,128)S(1)}, u32[]{:S(2)}, u32[]{:S(2)}) collective-permute-start(f32[96,128]{1,0:T(8,128)S(1)} %collective-permute-done.15.refs_6_), channel_id=1, source_target_pairs={{0,2},{2,0},{4,6},{6,4},{8,10},{10,8},{12,14},{14,12},{1,3},{3,1},... | collective-permute-start | bytes 147464 | tf_op jit(solution)/shard_map/ppermute | solution.py:356
  46.0 0.0 collective-permute-done.21.refs_5_
  46.0 0.0 collective-permute-done.20.refs_4_
  46.0 2.7 %collective-permute-done.19.refs_3_ = f32[96,128]{1,0:T(8,128)S(1)} collective-permute-done((f32[96,128]{1,0:T(8,128)S(1)}, f32[96,128]{1,0:T(8,128)S(1)}, u32[]{:S(2)}, u32[]{:S(2)}) %collective-permute-start.19) | collective-permute-done | bytes 49184 | tf_op jit(solution)/shard_map/ppermute | solution.py:356
  48.7 0.1 collective-permute-done.17.refs_2_
  48.8 0.5 collective-permute-done.16.refs_1_
  49.3 1.4 %residual.3 = (f32[9,32,256]{2,1,0:T(8,128)S(1)}, f32[32,128]{1,0:T(8,128)S(1)}, f32[32,256]{1,0:T(8,128)S(1)}, f32[32,256]{1,0:T(8,128)S(1)}) custom-call(f32[96,128]{1,0:T(8,128)S(1)} %get-tuple-element.32.refs_0_, f32[96,128]{1,0:T(8,128)S(1)} %collective-permute-done.16.refs_1_, f32[96,128]{1,0:T(8,128)S(1)} %collective-permute-done.17.refs_2_, ...), custom_call_target="tpu_custom_call" | custom-call | tf_op jit(solution)/shard_map/residual/pallas_call | solution.py:461
  50.7 0.0 collective-permute-start.22
  50.7 0.9 %inverse.3.inverse_ref = f32[32,128]{1,0:T(8,128)S(1)} custom-call(f32[32,128]{1,0:T(8,128)S(1)} %get-tuple-element.34.refs_11_.norm_ref), custom_call_target="tpu_custom_call" | custom-call | tf_op jit(solution)/shard_map/inverse/pallas_call | solution.py:451
  51.7 0.2 collective-permute-done.22.other_ref
  51.9 2.1 %direction.3 = (f32[32,512]{1,0:T(8,128)S(1)}, f32[1,32,256]{2,1,0:T(8,128)S(1)}, f32[32,128]{1,0:T(8,128)S(1)}, f32[16,8,128]{2,1,0:T(8,128)}) custom-call(f32[32,128]{1,0:T(8,128)S(1)} %get-tuple-element.36.mine_ref, f32[32,128]{1,0:T(8,128)S(1)} %collective-permute-done.22.other_ref, f32[32,128]{1,0:T(8,128)S(1)} %inverse.3.inverse_ref, ...), custom_call_target="tpu_custom_call" | custom-call | tf_op jit(solution)/shard_map/direction/pallas_call | solution.py:471
  54.0 4.5 %all-to-all-start = ((f32[16,8,128]{2,1,0:T(8,128)}), f32[16,8,128]{2,1,0:T(8,128)S(1)}, u32[]{:S(2)}, u32[]{:S(2)}) async-start(f32[16,8,128]{2,1,0:T(8,128)} %get-tuple-element.38), calls=%async_computation | async-start | bytes 131072 | tf_op jit(solution)/shard_map/all_to_all | solution.py:481
  58.5 0.4 collective-permute-start.23
  58.9 0.9 %collective-permute-done.23.other_ref = f32[32,512]{1,0:T(8,128)S(1)} collective-permute-done((f32[32,512]{1,0:T(8,128)S(1)}, f32[32,512]{1,0:T(8,128)S(1)}, u32[]{:S(2)}, u32[]{:S(2)}) %collective-permute-start.23) | collective-permute-done | bytes 65568 | tf_op jit(solution)/shard_map/ppermute | solution.py:370
  59.8 5.6 %all-to-all-done.grams_ref = f32[16,8,128]{2,1,0:T(8,128)S(1)} async-done(((f32[16,8,128]{2,1,0:T(8,128)}), f32[16,8,128]{2,1,0:T(8,128)S(1)}, u32[]{:S(2)}, u32[]{:S(2)}) %all-to-all-start) | async-done | bytes 65568 | tf_op jit(solution)/shard_map/all_to_all | solution.py:481
  65.4 1.7 %last.1 = (f32[32,256]{1,0:T(8,128)}, f32[32,256]{1,0:T(8,128)}) custom-call(f32[16,8,128]{2,1,0:T(8,128)S(1)} %all-to-all-done.grams_ref, f32[32,512]{1,0:T(8,128)S(1)} %get-tuple-element.39.mine_ref, f32[32,512]{1,0:T(8,128)S(1)} %collective-permute-done.23.other_ref, f32[1,32,256]{2,1,0:T(8,128)S(1)} %get-tuple-element.40.direction_ref, ...), custom_call_target="tpu_custom_call" | custom-call | tf_op jit(solution)/shard_map/last/pallas_call | solution.py:482
  (1 shorter events, 0.0 us)
Async XLA Ops:
  1.5 10.5 %collective-permute-start.2 = (f32[32,256]{1,0:T(8,128)S(1)}, f32[32,256]{1,0:T(8,128)S(1)}, u32[]{:S(2)}, u32[]{:S(2)}) collective-permute-start(f32[32,256]{1,0:T(8,128)S(1)} %multiply_multiply_fusion.refs_0_), channel_id=1, source_target_pairs={{0,12},{2,14},{4,8},{6,10},{8,4},{10,6},{12,0},{14,2},{1,13},{3,15... | collective-permute-start | bytes 98312 | tf_op jit(solution)/shard_map/ppermute | solution.py:356
  6.5 5.5 %collective-permute-start.1 = (f32[32,256]{1,0:T(8,128)S(1)}, f32[32,256]{1,0:T(8,128)S(1)}, u32[]{:S(2)}, u32[]{:S(2)}) collective-permute-start(f32[32,256]{1,0:T(8,128)S(1)} %multiply_multiply_fusion.refs_0_), channel_id=1, source_target_pairs={{0,8},{2,10},{4,12},{6,14},{8,0},{10,2},{12,4},{14,6},{1,9},{3,11}... | collective-permute-start | bytes 98312 | tf_op jit(solution)/shard_map/ppermute | solution.py:356
  6.5 5.5 %collective-permute-start = (f32[32,256]{1,0:T(8,128)S(1)}, f32[32,256]{1,0:T(8,128)S(1)}, u32[]{:S(2)}, u32[]{:S(2)}) collective-permute-start(f32[32,256]{1,0:T(8,128)S(1)} %multiply_multiply_fusion.refs_0_), channel_id=1, source_target_pairs={{0,4},{2,6},{4,0},{6,2},{8,12},{10,14},{12,8},{14,10},{1,5},{3,7},... | collective-permute-start | bytes 98312 | tf_op jit(solution)/shard_map/ppermute | solution.py:356
  12.0 5.0 %collective-permute-start.3 = (f32[4,32,256]{2,1,0:T(8,128)S(1)}, f32[4,32,256]{2,1,0:T(8,128)S(1)}, u32[]{:S(2)}, u32[]{:S(2)}) collective-permute-start(f32[4,32,256]{2,1,0:T(8,128)S(1)} %join.1.joined_ref.even_ref), channel_id=1, source_target_pairs={{0,2},{2,0},{4,6},{6,4},{8,10},{10,8},{12,14},{14,12},{1,3},{3,1},... | collective-permute-start | bytes 393224 | tf_op jit(solution)/shard_map/ppermute | solution.py:356
  12.9 2.2 %collective-permute-start.4 = (f32[32,256]{1,0:T(8,128)S(1)}, f32[32,256]{1,0:T(8,128)S(1)}, u32[]{:S(2)}, u32[]{:S(2)}) collective-permute-start(f32[32,256]{1,0:T(8,128)S(1)} %multiply_multiply_fusion.refs_0_), channel_id=1, source_target_pairs={{0,1},{1,0},{2,3},{3,2},{4,5},{5,4},{6,7},{7,6},{8,9},{9,8},{10,11... | collective-permute-start | bytes 98312 | tf_op jit(solution)/shard_map/ppermute | solution.py:370
  17.9 1.4 %collective-permute-start.5 = (f32[32,640]{1,0:T(8,128)S(1)}, f32[32,640]{1,0:T(8,128)S(1)}, u32[]{:S(2)}, u32[]{:S(2)}) collective-permute-start(f32[32,640]{1,0:T(8,128)S(1)} %get-tuple-element.23.mine_ref), channel_id=1, source_target_pairs={{0,1},{1,0},{2,3},{3,2},{4,5},{5,4},{6,7},{7,6},{8,9},{9,8},{10,11... | collective-permute-start | bytes 245768 | tf_op jit(solution)/shard_map/ppermute | solution.py:370
  19.5 6.0 %collective-permute-start.9 = (f32[96,128]{1,0:T(8,128)S(1)}, f32[96,128]{1,0:T(8,128)S(1)}, u32[]{:S(2)}, u32[]{:S(2)}) collective-permute-start(f32[96,128]{1,0:T(8,128)S(1)} %get-tuple-element.25.refs_0_), channel_id=1, source_target_pairs={{0,6},{2,4},{4,2},{6,0},{8,14},{10,12},{12,10},{14,8},{1,7},{3,5},... | collective-permute-start | bytes 147464 | tf_op jit(solution)/shard_map/ppermute | solution.py:356
  20.1 5.9 %collective-permute-start.6 = (f32[96,128]{1,0:T(8,128)S(1)}, f32[96,128]{1,0:T(8,128)S(1)}, u32[]{:S(2)}, u32[]{:S(2)}) collective-permute-start(f32[96,128]{1,0:T(8,128)S(1)} %get-tuple-element.25.refs_0_), channel_id=1, source_target_pairs={{0,8},{2,10},{4,12},{6,14},{8,0},{10,2},{12,4},{14,6},{1,9},{3,11}... | collective-permute-start | bytes 147464 | tf_op jit(solution)/shard_map/ppermute | solution.py:356
  23.1 6.3 %collective-permute-start.12 = (f32[96,128]{1,0:T(8,128)S(1)}, f32[96,128]{1,0:T(8,128)S(1)}, u32[]{:S(2)}, u32[]{:S(2)}) collective-permute-start(f32[96,128]{1,0:T(8,128)S(1)} %get-tuple-element.25.refs_0_), channel_id=1, source_target_pairs={{0,4},{2,6},{4,0},{6,2},{8,12},{10,14},{12,8},{14,10},{1,5},{3,7},... | collective-permute-start | bytes 147464 | tf_op jit(solution)/shard_map/ppermute | solution.py:356
  23.8 5.6 %collective-permute-start.11 = (f32[96,128]{1,0:T(8,128)S(1)}, f32[96,128]{1,0:T(8,128)S(1)}, u32[]{:S(2)}, u32[]{:S(2)}) collective-permute-start(f32[96,128]{1,0:T(8,128)S(1)} %get-tuple-element.25.refs_0_), channel_id=1, source_target_pairs={{0,2},{2,0},{4,6},{6,4},{8,10},{10,8},{12,14},{14,12},{1,3},{3,1},... | collective-permute-start | bytes 147464 | tf_op jit(solution)/shard_map/ppermute | solution.py:356
  25.5 5.3 %collective-permute-start.10 = (f32[96,128]{1,0:T(8,128)S(1)}, f32[96,128]{1,0:T(8,128)S(1)}, u32[]{:S(2)}, u32[]{:S(2)}) collective-permute-start(f32[96,128]{1,0:T(8,128)S(1)} %collective-permute-done.9.refs_7_), channel_id=1, source_target_pairs={{0,8},{2,10},{4,12},{6,14},{8,0},{10,2},{12,4},{14,6},{1,9},{3,11}... | collective-permute-start | bytes 147464 | tf_op jit(solution)/shard_map/ppermute | solution.py:356
  26.0 4.9 %collective-permute-start.8 = (f32[96,128]{1,0:T(8,128)S(1)}, f32[96,128]{1,0:T(8,128)S(1)}, u32[]{:S(2)}, u32[]{:S(2)}) collective-permute-start(f32[96,128]{1,0:T(8,128)S(1)} %collective-permute-done.6.refs_6_), channel_id=1, source_target_pairs={{0,4},{2,6},{4,0},{6,2},{8,12},{10,14},{12,8},{14,10},{1,5},{3,7},... | collective-permute-start | bytes 147464 | tf_op jit(solution)/shard_map/ppermute | solution.py:356
  28.1 4.1 %collective-permute-start.7 = (f32[96,128]{1,0:T(8,128)S(1)}, f32[96,128]{1,0:T(8,128)S(1)}, u32[]{:S(2)}, u32[]{:S(2)}) collective-permute-start(f32[96,128]{1,0:T(8,128)S(1)} %collective-permute-done.6.refs_6_), channel_id=1, source_target_pairs={{0,2},{2,0},{4,6},{6,4},{8,10},{10,8},{12,14},{14,12},{1,3},{3,1},... | collective-permute-start | bytes 147464 | tf_op jit(solution)/shard_map/ppermute | solution.py:356
  33.6 1.2 %collective-permute-start.13 = (f32[32,128]{1,0:T(8,128)S(1)}, f32[32,128]{1,0:T(8,128)S(1)}, u32[]{:S(2)}, u32[]{:S(2)}) collective-permute-start(f32[32,128]{1,0:T(8,128)S(1)} %get-tuple-element.28.mine_ref), channel_id=1, source_target_pairs={{0,1},{1,0},{2,3},{3,2},{4,5},{5,4},{6,7},{7,6},{8,9},{9,8},{10,11... | collective-permute-start | bytes 49160 | tf_op jit(solution)/shard_map/ppermute | solution.py:370
  35.9 1.3 %collective-permute-start.14 = (f32[32,512]{1,0:T(8,128)S(1)}, f32[32,512]{1,0:T(8,128)S(1)}, u32[]{:S(2)}, u32[]{:S(2)}) collective-permute-start(f32[32,512]{1,0:T(8,128)S(1)} %get-tuple-element.30.mine_ref), channel_id=1, source_target_pairs={{0,1},{1,0},{2,3},{3,2},{4,5},{5,4},{6,7},{7,6},{8,9},{9,8},{10,11... | collective-permute-start | bytes 196616 | tf_op jit(solution)/shard_map/ppermute | solution.py:370
  37.4 6.2 %collective-permute-start.18 = (f32[96,128]{1,0:T(8,128)S(1)}, f32[96,128]{1,0:T(8,128)S(1)}, u32[]{:S(2)}, u32[]{:S(2)}) collective-permute-start(f32[96,128]{1,0:T(8,128)S(1)} %get-tuple-element.32.refs_0_), channel_id=1, source_target_pairs={{0,6},{2,4},{4,2},{6,0},{8,14},{10,12},{12,10},{14,8},{1,7},{3,5},... | collective-permute-start | bytes 147464 | tf_op jit(solution)/shard_map/ppermute | solution.py:356
  38.7 5.5 %collective-permute-start.15 = (f32[96,128]{1,0:T(8,128)S(1)}, f32[96,128]{1,0:T(8,128)S(1)}, u32[]{:S(2)}, u32[]{:S(2)}) collective-permute-start(f32[96,128]{1,0:T(8,128)S(1)} %get-tuple-element.32.refs_0_), channel_id=1, source_target_pairs={{0,8},{2,10},{4,12},{6,14},{8,0},{10,2},{12,4},{14,6},{1,9},{3,11}... | collective-permute-start | bytes 147464 | tf_op jit(solution)/shard_map/ppermute | solution.py:356
  39.6 6.4 %collective-permute-start.21 = (f32[96,128]{1,0:T(8,128)S(1)}, f32[96,128]{1,0:T(8,128)S(1)}, u32[]{:S(2)}, u32[]{:S(2)}) collective-permute-start(f32[96,128]{1,0:T(8,128)S(1)} %get-tuple-element.32.refs_0_), channel_id=1, source_target_pairs={{0,4},{2,6},{4,0},{6,2},{8,12},{10,14},{12,8},{14,10},{1,5},{3,7},... | collective-permute-start | bytes 147464 | tf_op jit(solution)/shard_map/ppermute | solution.py:356
  40.8 5.1 %collective-permute-start.20 = (f32[96,128]{1,0:T(8,128)S(1)}, f32[96,128]{1,0:T(8,128)S(1)}, u32[]{:S(2)}, u32[]{:S(2)}) collective-permute-start(f32[96,128]{1,0:T(8,128)S(1)} %get-tuple-element.32.refs_0_), channel_id=1, source_target_pairs={{0,2},{2,0},{4,6},{6,4},{8,10},{10,8},{12,14},{14,12},{1,3},{3,1},... | collective-permute-start | bytes 147464 | tf_op jit(solution)/shard_map/ppermute | solution.py:356
  43.6 5.1 %collective-permute-start.19 = (f32[96,128]{1,0:T(8,128)S(1)}, f32[96,128]{1,0:T(8,128)S(1)}, u32[]{:S(2)}, u32[]{:S(2)}) collective-permute-start(f32[96,128]{1,0:T(8,128)S(1)} %collective-permute-done.18.refs_7_), channel_id=1, source_target_pairs={{0,8},{2,10},{4,12},{6,14},{8,0},{10,2},{12,4},{14,6},{1,9},{3,11}... | collective-permute-start | bytes 147464 | tf_op jit(solution)/shard_map/ppermute | solution.py:356
  44.2 4.6 %collective-permute-start.17 = (f32[96,128]{1,0:T(8,128)S(1)}, f32[96,128]{1,0:T(8,128)S(1)}, u32[]{:S(2)}, u32[]{:S(2)}) collective-permute-start(f32[96,128]{1,0:T(8,128)S(1)} %collective-permute-done.15.refs_6_), channel_id=1, source_target_pairs={{0,4},{2,6},{4,0},{6,2},{8,12},{10,14},{12,8},{14,10},{1,5},{3,7},... | collective-permute-start | bytes 147464 | tf_op jit(solution)/shard_map/ppermute | solution.py:356
  45.2 4.1 %collective-permute-start.16 = (f32[96,128]{1,0:T(8,128)S(1)}, f32[96,128]{1,0:T(8,128)S(1)}, u32[]{:S(2)}, u32[]{:S(2)}) collective-permute-start(f32[96,128]{1,0:T(8,128)S(1)} %collective-permute-done.15.refs_6_), channel_id=1, source_target_pairs={{0,2},{2,0},{4,6},{6,4},{8,10},{10,8},{12,14},{14,12},{1,3},{3,1},... | collective-permute-start | bytes 147464 | tf_op jit(solution)/shard_map/ppermute | solution.py:356
  50.7 1.2 %collective-permute-start.22 = (f32[32,128]{1,0:T(8,128)S(1)}, f32[32,128]{1,0:T(8,128)S(1)}, u32[]{:S(2)}, u32[]{:S(2)}) collective-permute-start(f32[32,128]{1,0:T(8,128)S(1)} %get-tuple-element.36.mine_ref), channel_id=1, source_target_pairs={{0,1},{1,0},{2,3},{3,2},{4,5},{5,4},{6,7},{7,6},{8,9},{9,8},{10,11... | collective-permute-start | bytes 49160 | tf_op jit(solution)/shard_map/ppermute | solution.py:370
  54.0 11.4 %all-to-all-start = ((f32[16,8,128]{2,1,0:T(8,128)}), f32[16,8,128]{2,1,0:T(8,128)S(1)}, u32[]{:S(2)}, u32[]{:S(2)}) async-start(f32[16,8,128]{2,1,0:T(8,128)} %get-tuple-element.38), calls=%async_computation | async-start | bytes 131072 | tf_op jit(solution)/shard_map/all_to_all | solution.py:481
  58.5 1.3 %collective-permute-start.23 = (f32[32,512]{1,0:T(8,128)S(1)}, f32[32,512]{1,0:T(8,128)S(1)}, u32[]{:S(2)}, u32[]{:S(2)}) collective-permute-start(f32[32,512]{1,0:T(8,128)S(1)} %get-tuple-element.39.mine_ref), channel_id=1, source_target_pairs={{0,1},{1,0},{2,3},{3,2},{4,5},{5,4},{6,7},{7,6},{8,9},{9,8},{10,11... | collective-permute-start | bytes 196616 | tf_op jit(solution)/shard_map/ppermute | solution.py:370

commit v7 on v6

v7 whole, which is shorter than its diff:
```python
import functools

import jax
import jax.numpy as jnp
from jax import lax
from jax.experimental import pallas as pl
from jax.experimental.pallas import tpu as pltpu
from jax.sharding import PartitionSpec as P

ITERS = 3
LANES = 128
PIVOTS = 8
CHUNKS = 5
F32 = jnp.float32
BF16 = jnp.bfloat16
SPARE_BYTES = 4 * 1024 * 1024

VMEM = pl.BlockSpec(memory_space=pltpu.VMEM)
SMEM = pl.BlockSpec(memory_space=pltpu.SMEM)
HBM = pl.BlockSpec(memory_space=pltpu.HBM)
ANY = pl.BlockSpec(memory_space=pl.ANY)


def params(*arrays):
    used = sum(a.size * jnp.dtype(a.dtype).itemsize for a in arrays)
    return pltpu.CompilerParams(vmem_limit_bytes=used + SPARE_BYTES)


def split(value):
    high = value.astype(BF16)
    rest = value - high.astype(F32)
    middle = rest.astype(BF16)
    low = (rest - middle.astype(F32)).astype(BF16)
    return high, middle, low


def mul(left, right):
    return jnp.dot(left, right, precision=lax.Precision.HIGHEST, preferred_element_type=F32)


def stack(left):
    high, middle, low = split(left)
    return jnp.concatenate([high, high, middle, high, middle, low], axis=0)


def times(stacked, right):
    high, middle, low = split(right)
    return lax.dot_general(
        stacked,
        jnp.concatenate([high, middle, high, low, middle, high], axis=0),
        (((0,), (0,)), ((), ())),
        preferred_element_type=F32,
    )


def gram_parts(left, right):
    size, width = left.shape
    filler = jnp.zeros((LANES - 3 * size, width), BF16)
    every = lax.dot_general(
        jnp.concatenate(split(left), axis=0),
        jnp.concatenate([*split(right), filler], axis=0),
        (((1,), (1,)), ((), ())),
        preferred_element_type=F32,
    )
    return every[2 * size :] + every[size : 2 * size] + every[:size]


def symmetric_parts(left, right):
    return 0.5 * (gram_parts(left, right) + gram_parts(right, left))


def finish(parts, place=0):
    size = parts.shape[0]

    def block(index):
        shift = (place - index) * size % LANES
        return pltpu.roll(parts, shift, 1) if shift else parts

    return block(2) + block(1) + block(0)


def pack(wide):
    rows = wide.shape[0]
    folds = LANES // rows
    height = rows // folds
    lanes = lax.broadcasted_iota(jnp.int32, wide.shape, 1)
    wide = jnp.where(lanes < rows, wide, 0.0)
    total = wide[:height]
    for i in range(1, folds):
        total = total + pltpu.roll(wide[i * height : (i + 1) * height], i * rows, 1)
    return total


def unpack(folded, size, place=0):
    parts = []
    for i in range(LANES // size):
        shift = (place - i) * size % LANES
        parts.append(pltpu.roll(folded, shift, 1) if shift else folded)
    return jnp.concatenate(parts, axis=0)


def solve_wide(target, matrix):
    size = matrix.shape[0]
    row_ids = lax.broadcasted_iota(jnp.int32, (size, LANES), 0)
    lane_ids = lax.broadcasted_iota(jnp.int32, (size, LANES), 1)
    work = jnp.where(lane_ids < size, target, matrix)
    for base in range(0, size, PIVOTS):
        columns = [
            jnp.broadcast_to(work[:, size + base + i : size + base + i + 1], (size, LANES))
            for i in range(PIVOTS)
        ]
        for i in range(PIVOTS):
            pivot = base + i
            here = row_ids == pivot
            inverse = 1.0 / columns[i][pivot : pivot + 1, :]
            row = work[pivot : pivot + 1, :] * inverse
            work = jnp.where(here, row, work - columns[i] * row)
            for later in range(i + 1, PIVOTS):
                entry = columns[later][pivot : pivot + 1, :] * inverse
                columns[later] = jnp.where(here, entry, columns[later] - columns[i] * entry)
    return work


def add_up(values):
    values = list(values)
    while len(values) > 1:
        pairs = [values[i] + values[i + 1] for i in range(0, len(values) - 1, 2)]
        values = pairs + values[len(values) - len(values) % 2 :]
    return values[0]


def add_tiles(rows_dev, lists, tiles, first_tile, start, stop, total):
    rows_ref, cols_ref = lists
    tile = total.shape[1]
    slots = rows_ref.shape[0]
    blocks = rows_dev // tile
    row_place = lax.axis_index("row")
    col_place = lax.axis_index("col")
    col_devices = lax.axis_size("col")
    row_blocks = col_devices * blocks

    def place(slot):
        row = rows_ref[slot]
        column = cols_ref[slot]
        side = lax.rem(row // blocks + col_devices - col_place, col_devices)
        owner = column // (blocks * col_devices)
        column_at = (owner ^ row_place) * blocks + lax.rem(column, blocks)
        return column_at * row_blocks + side * blocks + lax.rem(row, blocks)

    def add(slot, at):
        value = total[at] + tiles[slot - first_tile].astype(F32)
        following = place(jnp.minimum(slot + 1, slots - 1))
        total[at] = value
        return following

    lax.fori_loop(start, stop, add, place(start))


def copy_lists(hbm_refs, smem_refs, sems):
    copies = [
        pltpu.make_async_copy(source, target, sems.at[i])
        for i, (source, target) in enumerate(zip(hbm_refs, smem_refs))
    ]
    for copy in copies:
        copy.start()
    return copies


def gather_kernel(rows_dev, count_ref, rows_hbm, cols_hbm, tiles_ref, total, rest, *scratch):
    held, rows_ref, cols_ref, sems, list_sems = scratch
    live = count_ref[0]
    half = held.shape[0]
    slots, tile = tiles_ref.shape[:2]
    chunk = -(-half // CHUNKS)
    lists = copy_lists((rows_hbm, cols_hbm), (rows_ref, cols_ref), list_sems)
    copies = []
    for c in range(CHUNKS):
        part = pl.ds(c * chunk, min(chunk, half - c * chunk))
        copies.append(pltpu.make_async_copy(tiles_ref.at[part], held.at[part], sems.at[c]))

        @pl.when(c * chunk < live)
        def _():
            copies[c].start()

    last = pltpu.make_async_copy(tiles_ref.at[pl.ds(half, slots - half)], rest, sems.at[CHUNKS])

    @pl.when(half < live)
    def _():
        last.start()

    def clear(index, carry):
        total[index] = jnp.zeros((tile, tile), F32)
        return carry

    lax.fori_loop(0, total.shape[0], clear, 0, unroll=4)
    for copy in lists:
        copy.wait()
    for c in range(CHUNKS):
        start, stop = c * chunk, min((c + 1) * chunk, half)

        @pl.when(start < live)
        def _():
            copies[c].wait()
            add_tiles(
                rows_dev, (rows_ref, cols_ref), held, 0, start, jnp.minimum(live, stop), total
            )

    @pl.when(half < live)
    def _():
        last.wait()


def dense_kernel(
    rows_dev, count_ref, rows_hbm, cols_hbm, rest, total_in, joined_ref, out_ref, total, *scratch
):
    rows_ref, cols_ref, list_sems = scratch
    live = count_ref[0]
    half = rows_ref.shape[0] - rest.shape[0]
    tile = total.shape[1]
    row_blocks = out_ref.shape[2] // tile

    @pl.when(half < live)
    def _():
        lists = copy_lists((rows_hbm, cols_hbm), (rows_ref, cols_ref), list_sems)
        for copy in lists:
            copy.wait()
        add_tiles(rows_dev, (rows_ref, cols_ref), rest, half, half, live, total)

    def part(index, carry):
        start = pl.multiple_of(index * tile, tile)
        for b in range(row_blocks):
            value = total[index * row_blocks + b].T
            high = value.astype(BF16)
            low = (value - high.astype(F32)).astype(BF16)
            out_ref[0, pl.ds(start, tile), pl.ds(b * tile, tile)] = high
            out_ref[1, pl.ds(start, tile), pl.ds(b * tile, tile)] = low
        return carry

    lax.fori_loop(0, total.shape[0] // row_blocks, part, 0)


def join_kernel(*refs):
    for k, ref in enumerate(refs[:-2]):
        refs[-1][k] = ref[...]


def apply_dense(directions, matrix):
    width = directions[0].shape[1]
    total = None
    for k, direction in enumerate(directions):
        rounded = direction.astype(BF16)
        for part in range(2):
            term = jnp.dot(
                rounded,
                matrix[part, k * width : (k + 1) * width, :],
                preferred_element_type=F32,
            )
            total = term if total is None else total + term
    return total


def first_kernel(even_ref, odd_ref, matrix, out_ref, blocks_ref):
    pieces = blocks_ref.shape[0]
    values = [(odd_ref if k % 2 else even_ref)[k // 2] for k in range(pieces)]
    for k, value in enumerate(values):
        blocks_ref[k] = value
    rows = 2 * values[0].shape[1]
    joined = jnp.concatenate(values, axis=1)
    out_ref[:, rows:] = gram_parts(joined, joined)
    out_ref[:, :rows] = apply_dense(values, matrix)


def collect_kernel(near_ref, far_ref, residual_ref, direction_ref):
    pieces = near_ref.shape[0]
    for k in range(pieces):
        residual_ref[0, k] = near_ref[k]
        residual_ref[1, k] = far_ref[k]
        direction_ref[k] = near_ref[k]
    direction_ref[pieces] = far_ref[0]


def add_halves(mine_ref, other_ref, width):
    near = mine_ref[:, :width] + other_ref[:, width : 2 * width]
    far = mine_ref[:, width : 2 * width] + other_ref[:, :width]
    return near, far


def image_kernel(first, mine_ref, other_ref, near_ref, far_ref, out_ref, *norm_ref):
    core = lax.axis_index("col")
    size, width = near_ref.shape[1:]
    near, far = add_halves(mine_ref, other_ref, width)
    if first:
        norm_ref[0][...] = finish(mine_ref[:, 2 * width :] + other_ref[:, 2 * width :])
    parts = width // LANES
    for i in range(parts):
        lanes = slice(i * LANES, (i + 1) * LANES)
        for place, half in ((core, near), (1 - core, far)):
            at = pl.multiple_of((place * parts + i) * size, size)
            out_ref[pl.ds(at, size)] = half[:, lanes]
    out_ref[2 * parts * size :] = symmetric_parts(near, near_ref[0]) + symmetric_parts(
        far, far_ref[far_ref.shape[0] - 1]
    )


def inverse_kernel(norm_ref, out_ref):
    norm = norm_ref[...]
    size = norm.shape[0]
    norm = 0.5 * (norm + jnp.concatenate([norm[:, :size].T, norm[:, size:]], axis=1))
    unit = lax.broadcasted_iota(jnp.int32, norm.shape, 0) == lax.broadcasted_iota(
        jnp.int32, norm.shape, 1
    )
    out_ref[...] = solve_wide(jnp.where(unit, 1.0, 0.0), pltpu.roll(norm, size, 1))


def pick(refs, places, core, rows):
    if places[0] == places[1]:
        return refs[places[0]][rows]
    return jnp.where(core == 0, refs[places[0]][rows], refs[places[1]][rows])


def step_kernel(places, with_solution, last, *refs):
    used = 1 + max(max(pair) for pair in places)
    images, refs = refs[:used], refs[used:]
    direction_ref, residual_ref, norm_ref, inverse_ref, matrix = refs[:5]
    refs = refs[5:]
    if with_solution:
        solution_ref, refs = refs[0], refs[1:]
    out_ref, new_direction, new_residual, new_norm, new_solution = refs
    core = lax.axis_index("col")
    pieces = len(places)
    size, width = direction_ref.shape[1:]
    parts = width // LANES

    def image(k, half):
        found = []
        for i in range(parts):
            at = pl.multiple_of((half * parts + i) * size, size)
            found.append(pick(images, places[k], core, pl.ds(at, size)))
        return jnp.concatenate(found, axis=1)

    behind = slice(2 * parts * size, None)
    products = add_up([pick(images, pair, core, behind) for pair in places])
    alpha = stack(solve_wide(norm_ref[...], finish(products, 1))[:, :size])
    residuals = [
        [residual_ref[side, k] - times(alpha, image(k, half)) for k in range(pieces)]
        for side, half in enumerate((core, 1 - core))
    ]
    joined = [jnp.concatenate(values, axis=1) for values in residuals]
    next_norm = finish(gram_parts(joined[0], joined[0]) + gram_parts(joined[1], joined[1]))
    new_norm[...] = next_norm
    step = times(alpha, direction_ref[0])
    new_solution[...] = solution_ref[...] + step if with_solution else step
    beta = stack(mul(inverse_ref[:, :size], next_norm[:, :size]))
    directions = [
        residual + times(beta, direction_ref[k])
        for k, residual in enumerate(residuals[0] + residuals[1][:1])
    ]
    if last:
        new_residual[...] = residuals[0][0]
        new_direction[0] = directions[0]
        new_direction[1] = directions[pieces]
    else:
        for k in range(pieces):
            new_residual[0, k] = residuals[0][k]
            new_residual[1, k] = residuals[1][k]
        for k in range(pieces + 1):
            new_direction[k] = directions[k]
    out_ref[...] = apply_dense(directions[:pieces], matrix)


def last_image_kernel(mine_ref, other_ref, direction_ref, near_ref, gram_ref):
    near, far = add_halves(mine_ref, other_ref, direction_ref.shape[2])
    near_ref[...] = near
    gram_ref[...] = symmetric_parts(near, direction_ref[0]) + symmetric_parts(
        far, direction_ref[1]
    )


def last_kernel(places, *refs):
    used = 1 + max(max(pair) for pair in places)
    image_ref, direction_ref, residual_ref, norm_ref, solution_ref = refs[used:-2]
    new_solution, new_residual = refs[-2:]
    core = lax.axis_index("col")
    size = image_ref.shape[0]
    products = add_up([pick(refs, pair, core, slice(None)) for pair in places])
    alpha = stack(solve_wide(norm_ref[...], finish(products, 1))[:, :size])
    new_solution[...] = solution_ref[...] + times(alpha, direction_ref[0])
    new_residual[...] = residual_ref[...] - times(alpha, image_ref[...])


def shape(*dims, dtype=F32):
    return jax.ShapeDtypeStruct(dims, dtype)


def per_device(tiles, tile_rows, tile_cols, tile_count, signs, vertex_weight, column_scale):
    sketch, rows_dev = signs.shape
    tile = tiles.shape[1]
    pieces = lax.axis_size("row")
    col_devices = lax.axis_size("col")
    group = col_devices * rows_dev
    depth = pieces * rows_dev

    def swap(value, mask):
        return lax.ppermute(value, "row", [(i, i ^ mask) for i in range(pieces)])

    def across(value):
        return lax.ppermute(
            value, "col", [(i, (i + 1) % col_devices) for i in range(col_devices)]
        )

    def exchange(value):
        if pieces != 8:
            found = [value] + [swap(value, k) for k in range(1, pieces)]
            return found, [(k, k) for k in range(pieces)]
        shares = ((7, 4), (3, 5), (2, 6), (1, 0))
        fetched = []
        passed = []
        places = {0: (0, 0)}
        for turn, masks in enumerate(shares, 1):
            pairs = [
                (i * 2 + core, (i ^ mask) * 2 + core)
                for core, mask in enumerate(masks)
                if mask
                for i in range(pieces)
            ]
            fetched.append(lax.ppermute(value, ("row", "col"), pairs))
            pairs = [(core, 1 - core) for core, mask in enumerate(masks) if mask]
            passed.append(lax.ppermute(fetched[-1], "col", pairs))
            for core, mask in enumerate(masks):
                if mask:
                    here = (turn, turn + len(shares))
                    places[mask] = here if core == 0 else here[::-1]
        return [value, *fetched, *passed], [places[k] for k in range(pieces)]

    right_side = signs.astype(F32) * vertex_weight[None, :] * column_scale[:, None]
    far_side = across(right_side)[None]
    even = [right_side] + [swap(right_side, k) for k in range(2, pieces, 2)]

    matrix = shape(2, depth, group, dtype=BF16)
    total = shape(depth // tile * (group // tile), tile, tile)
    slots = tiles.shape[0]
    half = slots // 2
    rest = shape(slots - half, tile, tile, dtype=BF16)
    lists = [pltpu.with_memory_space_constraint(x, pltpu.HBM) for x in (tile_rows, tile_cols)]
    lists_scratch = [pltpu.SMEM(x.shape, jnp.int32) for x in lists]
    cost = pl.CostEstimate(
        flops=4 * tiles.size, bytes_accessed=4 * tiles.size, transcendentals=0
    )
    blocks_sum, others = pl.pallas_call(
        functools.partial(gather_kernel, rows_dev),
        out_shape=(total, rest),
        in_specs=[SMEM] + [HBM] * 3,
        out_specs=(VMEM, VMEM),
        scratch_shapes=[
            pltpu.VMEM((half, tile, tile), BF16),
            *lists_scratch,
            pltpu.SemaphoreType.DMA((CHUNKS + 1,)),
            pltpu.SemaphoreType.DMA((len(lists),)),
        ],
        compiler_params=params(tiles, total),
        cost_estimate=cost,
        name="gather",
    )(tile_count, *lists, pltpu.with_memory_space_constraint(tiles, pltpu.HBM))
    joined = shape(pieces // 2, sketch, rows_dev)
    even = pl.pallas_call(
        join_kernel,
        out_shape=joined,
        in_specs=[VMEM] * (pieces // 2) + [ANY],
        out_specs=VMEM,
        compiler_params=params(joined, joined),
        name="join",
    )(*even, blocks_sum)
    odd = swap(even, 1)
    dense, _ = pl.pallas_call(
        functools.partial(dense_kernel, rows_dev),
        out_shape=(matrix, total),
        in_specs=[SMEM] + [HBM] * 2 + [VMEM, VMEM, ANY],
        out_specs=(VMEM, VMEM),
        scratch_shapes=[*lists_scratch, pltpu.SemaphoreType.DMA((len(lists),))],
        input_output_aliases={4: 1},
        compiler_params=params(rest, total, total, matrix),
        cost_estimate=cost,
        name="dense",
    )(tile_count, *lists, others, blocks_sum, even)

    held = shape(2, pieces, sketch, rows_dev)
    state = shape(pieces + 1, sketch, rows_dev)
    small = shape(sketch, LANES)
    piece = shape(sketch, rows_dev)
    payload = shape(sketch * (2 * (rows_dev // LANES) + 1), LANES)

    partial_sum, blocks = pl.pallas_call(
        first_kernel,
        out_shape=(shape(sketch, group + LANES), shape(pieces, sketch, rows_dev)),
        in_specs=[VMEM] * 3,
        out_specs=(VMEM, VMEM),
        compiler_params=params(matrix, state, state),
        name="first",
    )(even, odd, dense)
    residual, direction = pl.pallas_call(
        collect_kernel,
        out_shape=(held, state),
        in_specs=[VMEM] * 2,
        out_specs=(VMEM, VMEM),
        compiler_params=params(held, held, state),
        name="collect",
    )(blocks, across(blocks))
    norm = None
    solution = None
    for iteration in range(ITERS - 1):
        first = iteration == 0
        last = iteration == ITERS - 2
        outs = pl.pallas_call(
            functools.partial(image_kernel, first),
            out_shape=(payload,) + ((small,) if first else ()),
            in_specs=[VMEM] * 4,
            out_specs=(VMEM,) * (2 if first else 1),
            compiler_params=params(state, payload),
            name="image",
        )(partial_sum, across(partial_sum), *((even, far_side) if first else (direction,) * 2))
        if first:
            norm = outs[1]
        found, places = exchange(outs[0])
        inverse = pl.pallas_call(
            inverse_kernel,
            out_shape=small,
            in_specs=[VMEM],
            out_specs=VMEM,
            compiler_params=params(),
            name="inverse",
        )(norm)
        given = () if first else (solution,)
        partial_sum, direction, residual, norm, solution = pl.pallas_call(
            functools.partial(step_kernel, places, not first, last),
            out_shape=(
                shape(sketch, group),
                shape(2, sketch, rows_dev) if last else state,
                piece if last else held,
                small,
                piece,
            ),
            in_specs=[VMEM] * (len(found) + 5 + len(given)),
            out_specs=(VMEM,) * 5,
            compiler_params=params(matrix, held, held, held, held, state),
            name="step",
        )(*found, direction, residual, norm, inverse, dense, *given)
    near, gram = pl.pallas_call(
        last_image_kernel,
        out_shape=(piece, small),
        in_specs=[VMEM] * 3,
        out_specs=(VMEM, VMEM),
        compiler_params=params(state),
        name="last_image",
    )(partial_sum, across(partial_sum), direction)
    found, places = exchange(gram)
    return pl.pallas_call(
        functools.partial(last_kernel, places),
        out_shape=(piece, piece),
        in_specs=[VMEM] * (len(found) + 5),
        out_specs=(VMEM, VMEM),
        compiler_params=params(state, state),
        name="last",
    )(*found, near, direction, residual, norm, solution)


def solution(mesh):
    return jax.shard_map(
        per_device,
        mesh=mesh,
        in_specs=(
            P(("row", "col"), None, None),
            P(("row", "col")),
            P(("row", "col")),
            P(("row", "col")),
            P("rhs", ("row", "col")),
            P(("row", "col")),
            P("rhs"),
        ),
        out_specs=(P("rhs", ("row", "col")), P("rhs", ("row", "col"))),
        check_vma=False,
    )
```

time: 66.9 us -> 72 us (1.076)
  starting transfers between devices: 27.2 us -> 39.1 us
  waiting for transfers between devices: 20.5 us -> 14.1 us
  Pallas kernels: 17.1 us -> 15.9 us
    ppermute x0 -> x24, starting transfers between devices: none -> 30.7 us  [the longest x12 24.5 us: exchange(): fetched.append(lax.ppermute(value, ('row', 'col'), pairs))]
    ppermute x18 -> x4, starting transfers between devices: 21.8 us -> 7.2 us  [swap(): return lax.ppermute(value, 'row', [(i, i ^ mask) for i in range(pieces)])]
    ppermute x18 -> x4, waiting for transfers between devices: 11.3 us -> 3.61 us  [swap(): return lax.ppermute(value, 'row', [(i, i ^ mask) for i in range(pieces)])]
    ppermute x0 -> x24, waiting for transfers between devices: none -> 7.31 us  [the longest x12 6.49 us: exchange(): fetched.append(lax.ppermute(value, ('row', 'col'), pairs))]
    all_to_all x1 -> x0, waiting for transfers between devices: 5.58 us -> none  [per_device(): every = lax.all_to_all(outs[3], ('row', 'col'), 0, 0)]
    all_to_all x1 -> x0, starting transfers between devices: 4.51 us -> none  [per_device(): every = lax.all_to_all(outs[3], ('row', 'col'), 0, 0)]
    pallas_call x8, Pallas kernels: 14.8 us -> 13.7 us  [the longest x2 6.04 us: per_device(): pl.pallas_call(functools.partial(step_kernel, places, not first, last), o...]
    ppermute x6 -> x5, waiting for transfers between devices: 3.66 us -> 3.17 us  [across(): lax.ppermute(value, 'col', [(i, (i + 1) % col_devices) for i in range(col...]
  transfers between devices with their start and end apart: 25 -> 33, of which waited for: 15 -> 12; matrix products, arithmetic and copies ran while one was open for 0% -> 0% of each run, Pallas kernels for 12% -> 10%
where the time goes in v7:
time: 72 us; the launch traced here: 71.6 us
  starting transfers between devices  39.1 us (54%)
  Pallas kernels  15.9 us (22%)
  waiting for transfers between devices  14.1 us (20%)
  between operations  1.57 us (2%)
  other arithmetic  0.85 us (1%)
    ppermute x12, starting transfers between devices, exchange(): fetched.append(lax.ppermute(value, ('row', 'col'), pairs))  24.5 us
    ppermute x4, starting transfers between devices, swap(): return lax.ppermute(value, 'row', [(i, i ^ mask) for i in range(pieces)])  7.2 us
    ppermute x12, waiting for transfers between devices, exchange(): fetched.append(lax.ppermute(value, ('row', 'col'), pairs))  6.49 us
    ppermute x12, starting transfers between devices, exchange(): passed.append(lax.ppermute(fetched[-1], 'col', pairs))  6.13 us
    pallas_call x2, Pallas kernels, per_device(): pl.pallas_call(functools.partial(step_kernel, places, not first, last), o...  6.04 us
    ppermute x4, waiting for transfers between devices, swap(): return lax.ppermute(value, 'row', [(i, i ^ mask) for i in range(pieces)])  3.61 us
    ppermute x5, waiting for transfers between devices, across(): lax.ppermute(value, 'col', [(i, (i + 1) % col_devices) for i in range(col...  3.17 us
    pallas_call x1, Pallas kernels, per_device(): pl.pallas_call(functools.partial(gather_kernel, rows_dev), out_shape=(tot...  2.63 us
  transfers between devices with their start and end apart: 33, of which 12 were waited for; matrix products, arithmetic and copies ran while one was open for 0% of the time, Pallas kernels for 10%

profile of v7, /device:TPU:0, one launch (start us, length us, event | category | flops | bytes accessed | tf_op | source)
XLA Modules:
  0.0 71.6 jit_solution(2433888750477296621)
XLA Ops:
  0.6 0.8 %multiply_multiply_fusion.refs_0_ = f32[32,256]{1,0:T(8,128)S(1)} fusion(s32[32,256]{1,0:T(8,128)} %param.11, f32[32]{0:T(128)} %param.13, f32[256]{0:T(256)} %param.12), kind=kLoop, calls=%fused_computation | loop fusion | flops 24576 | bytes 66688 | tf_op jit(solution)/shard_map/mul | solution.py:435
  1.5 3.0 %collective-permute-start = (f32[32,256]{1,0:T(8,128)S(1)}, f32[32,256]{1,0:T(8,128)S(1)}, u32[]{:S(2)}, u32[]{:S(2)}) collective-permute-start(f32[32,256]{1,0:T(8,128)S(1)} %multiply_multiply_fusion.refs_0_), channel_id=1, source_target_pairs={{0,4},{2,6},{4,0},{6,2},{8,12},{10,14},{12,8},{14,10},{1,5},{3,7},... | collective-permute-start | bytes 98312 | tf_op jit(solution)/shard_map/ppermute | solution.py:404
  4.5 2.6 %collective-permute-start.1 = (f32[32,256]{1,0:T(8,128)S(1)}, f32[32,256]{1,0:T(8,128)S(1)}, u32[]{:S(2)}, u32[]{:S(2)}) collective-permute-start(f32[32,256]{1,0:T(8,128)S(1)} %multiply_multiply_fusion.refs_0_), channel_id=1, source_target_pairs={{0,8},{2,10},{4,12},{6,14},{8,0},{10,2},{12,4},{14,6},{1,9},{3,11}... | collective-permute-start | bytes 98312 | tf_op jit(solution)/shard_map/ppermute | solution.py:404
  7.8 2.6 %gather.1 = (f32[64,128,128]{2,1,0:T(8,128)S(1)}, bf16[65,128,128]{2,1,0:T(8,128)(2,1)S(1)}) custom-call(s32[1]{0:T(128)S(6)} %copy.11.count_ref, s32[130]{0:T(256)} %rows_hbm.3, s32[130]{0:T(256)} %cols_hbm.3, bf16[130,128,128]{2,1,0:T(8,128)(2,1)} %tiles_ref.1), custom_call_target="tpu_custom_call" | custom-call | flops 8519680 | bytes 8519680 | tf_op jit(solution)/shard_map/gather/pallas_call | solution.py:449
  10.4 2.4 %collective-permute-done.2.refs_3_ = f32[32,256]{1,0:T(8,128)S(1)} collective-permute-done((f32[32,256]{1,0:T(8,128)S(1)}, f32[32,256]{1,0:T(8,128)S(1)}, u32[]{:S(2)}, u32[]{:S(2)}) %collective-permute-start.2) | collective-permute-done | bytes 32800 | tf_op jit(solution)/shard_map/ppermute | solution.py:404
  12.8 1.6 %collective-permute-start.3 = (f32[4,32,256]{2,1,0:T(8,128)S(1)}, f32[4,32,256]{2,1,0:T(8,128)S(1)}, u32[]{:S(2)}, u32[]{:S(2)}) collective-permute-start(f32[4,32,256]{2,1,0:T(8,128)S(1)} %join.1.joined_ref.even_ref.near_ref), channel_id=1, source_target_pairs={{0,2},{2,0},{4,6},{6,4},{8,10},{10,8},{12,14},{14,12},{1,3},{3,1},... | collective-permute-start | bytes 393224 | tf_op jit(solution)/shard_map/ppermute | solution.py:404
  14.4 2.2 %dense.1 = (bf16[2,2048,512]{2,1,0:T(8,128)(2,1)S(1)}, f32[64,128,128]{2,1,0:T(8,128)S(1)}) custom-call(s32[1]{0:T(128)S(6)} %copy.11.count_ref, s32[130]{0:T(256)} %rows_hbm.3, s32[130]{0:T(256)} %cols_hbm.3, bf16[65,128,128]{2,1,0:T(8,128)(2,1)S(1)} %get-tuple-element.24.rest, ...), custom_call_target="tpu_custom_call", output_to_operand_aliasing={{1}: (4, {})} | custom-call | flops 8519680 | bytes 8519680 | tf_op jit(solution)/shard_map/dense/pallas_call | solution.py:474
  16.6 1.2 %collective-permute-done.3.odd_ref = f32[4,32,256]{2,1,0:T(8,128)S(1)} collective-permute-done((f32[4,32,256]{2,1,0:T(8,128)S(1)}, f32[4,32,256]{2,1,0:T(8,128)S(1)}, u32[]{:S(2)}, u32[]{:S(2)}) %collective-permute-start.3) | collective-permute-done | bytes 131104 | tf_op jit(solution)/shard_map/ppermute | solution.py:404
  17.9 0.9 %first.1 = (f32[32,640]{1,0:T(8,128)S(1)}, f32[8,32,256]{2,1,0:T(8,128)S(1)}) custom-call(f32[4,32,256]{2,1,0:T(8,128)S(1)} %join.1.joined_ref.even_ref.near_ref, f32[4,32,256]{2,1,0:T(8,128)S(1)} %collective-permute-done.3.odd_ref, bf16[2,2048,512]{2,1,0:T(8,128)(2,1)S(1)} %get-tuple-element.25.matrix.refs_13_), custom_call_target="tpu_custom_call" | custom-call | tf_op jit(solution)/shard_map/first/pallas_call | solution.py:492
  18.7 0.1 collective-permute-start.14
  18.8 0.5 collective-permute-start.4
  19.3 0.1 collective-permute-start.5
  19.4 1.1 %collective-permute-done.5 = f32[32,256]{1,0:T(8,128)S(1)} collective-permute-done((f32[32,256]{1,0:T(8,128)S(1)}, f32[32,256]{1,0:T(8,128)S(1)}, u32[]{:S(2)}, u32[]{:S(2)}) %collective-permute-start.5) | collective-permute-done | bytes 32800 | tf_op jit(solution)/shard_map/ppermute | solution.py:407
  20.5 0.0 collective-permute-done.4.other_ref
  20.5 0.2 image.2
  20.7 2.3 %collective-permute-start.6 = (f32[160,128]{1,0:T(8,128)S(1)}, f32[160,128]{1,0:T(8,128)S(1)}, u32[]{:S(2)}, u32[]{:S(2)}) collective-permute-start(f32[160,128]{1,0:T(8,128)S(1)} %get-tuple-element.27.refs_0_), channel_id=1, source_target_pairs={{0,14},{2,12},{4,10},{6,8},{8,6},{10,4},{12,2},{14,0},{1,9},{3,11}... | collective-permute-start | bytes 245768 | tf_op jit(solution)/shard_map/ppermute | solution.py:426
  23.0 0.0 collective-permute-start.7
  23.0 2.1 %collective-permute-start.8 = (f32[160,128]{1,0:T(8,128)S(1)}, f32[160,128]{1,0:T(8,128)S(1)}, u32[]{:S(2)}, u32[]{:S(2)}) collective-permute-start(f32[160,128]{1,0:T(8,128)S(1)} %get-tuple-element.27.refs_0_), channel_id=1, source_target_pairs={{0,4},{2,6},{4,0},{6,2},{8,12},{10,14},{12,8},{14,10},{1,13},{3,15... | collective-permute-start | bytes 245768 | tf_op jit(solution)/shard_map/ppermute | solution.py:426
  25.1 3.3 %collective-permute-start.9 = (f32[160,128]{1,0:T(8,128)S(1)}, f32[160,128]{1,0:T(8,128)S(1)}, u32[]{:S(2)}, u32[]{:S(2)}) collective-permute-start(f32[160,128]{1,0:T(8,128)S(1)} %get-tuple-element.27.refs_0_), channel_id=1, source_target_pairs={{0,2},{2,0},{4,6},{6,4},{8,10},{10,8},{12,14},{14,12},{16,18},{18,... | collective-permute-start | bytes 245768 | tf_op jit(solution)/shard_map/ppermute | solution.py:426
  28.4 0.0 collective-permute-done.6.refs_1_
  28.4 0.1 collective-permute-start.10
  28.5 2.0 %collective-permute-done.7.refs_2_ = f32[160,128]{1,0:T(8,128)S(1)} collective-permute-done((f32[160,128]{1,0:T(8,128)S(1)}, f32[160,128]{1,0:T(8,128)S(1)}, u32[]{:S(2)}, u32[]{:S(2)}) %collective-permute-start.7) | collective-permute-done | bytes 81952 | tf_op jit(solution)/shard_map/ppermute | solution.py:426
  30.5 0.0 collective-permute-start.11
  30.5 0.5 collective-permute-start.12
  31.0 0.4 collective-permute-done.9.refs_4_
  31.4 1.5 %collective-permute-start.13 = (f32[160,128]{1,0:T(8,128)S(1)}, f32[160,128]{1,0:T(8,128)S(1)}, u32[]{:S(2)}, u32[]{:S(2)}) collective-permute-start(f32[160,128]{1,0:T(8,128)S(1)} %collective-permute-done.9.refs_4_), channel_id=1, source_target_pairs={{0,1},{2,3},{4,5},{6,7},{8,9},{10,11},{12,13},{14,15},{16,17},{18,... | collective-permute-start | bytes 245768 | tf_op jit(solution)/shard_map/ppermute | solution.py:428
  32.9 0.9 %inverse.2.refs_12_ = f32[32,128]{1,0:T(8,128)S(1)} custom-call(f32[32,128]{1,0:T(8,128)S(1)} %get-tuple-element.31.norm_ref.refs_11_), custom_call_target="tpu_custom_call" | custom-call | tf_op jit(solution)/shard_map/inverse/pallas_call | solution.py:524
  33.9 0.0 collective-permute-done.14.far_ref
  33.9 0.1 collect.1
  34.0 0.0 collective-permute-done.12.refs_7_
  34.0 0.0 collective-permute-done.13.refs_8_
  34.0 3.0 %step.2 = (f32[32,512]{1,0:T(8,128)S(1)}, f32[9,32,256]{2,1,0:T(8,128)S(1)}, f32[2,8,32,256]{3,2,1,0:T(8,128)S(1)}, f32[32,128]{1,0:T(8,128)S(1)}, f32[32,256]{1,0:T(8,128)S(1)}) custom-call(f32[160,128]{1,0:T(8,128)S(1)} %get-tuple-element.27.refs_0_, f32[160,128]{1,0:T(8,128)S(1)} %collective-permute-done.6.refs_1_, ...), custom_call_target="tpu_custom_call" | custom-call | tf_op jit(solution)/shard_map/step/pallas_call | solution.py:533
  37.0 0.3 collective-permute-start.15
  37.3 1.1 %collective-permute-done.15.other_ref = f32[32,512]{1,0:T(8,128)S(1)} collective-permute-done((f32[32,512]{1,0:T(8,128)S(1)}, f32[32,512]{1,0:T(8,128)S(1)}, u32[]{:S(2)}, u32[]{:S(2)}) %collective-permute-start.15) | collective-permute-done | bytes 65568 | tf_op jit(solution)/shard_map/ppermute | solution.py:407
  38.3 0.2 image.3.refs_0_
  38.5 3.1 %collective-permute-start.16 = (f32[160,128]{1,0:T(8,128)S(1)}, f32[160,128]{1,0:T(8,128)S(1)}, u32[]{:S(2)}, u32[]{:S(2)}) collective-permute-start(f32[160,128]{1,0:T(8,128)S(1)} %image.3.refs_0_), channel_id=1, source_target_pairs={{0,14},{2,12},{4,10},{6,8},{8,6},{10,4},{12,2},{14,0},{1,9},{3,11}... | collective-permute-start | bytes 245768 | tf_op jit(solution)/shard_map/ppermute | solution.py:426
  41.7 0.0 collective-permute-start.17
  41.7 2.0 %collective-permute-start.18 = (f32[160,128]{1,0:T(8,128)S(1)}, f32[160,128]{1,0:T(8,128)S(1)}, u32[]{:S(2)}, u32[]{:S(2)}) collective-permute-start(f32[160,128]{1,0:T(8,128)S(1)} %image.3.refs_0_), channel_id=1, source_target_pairs={{0,4},{2,6},{4,0},{6,2},{8,12},{10,14},{12,8},{14,10},{1,13},{3,15... | collective-permute-start | bytes 245768 | tf_op jit(solution)/shard_map/ppermute | solution.py:426
  43.6 3.4 %collective-permute-start.19 = (f32[160,128]{1,0:T(8,128)S(1)}, f32[160,128]{1,0:T(8,128)S(1)}, u32[]{:S(2)}, u32[]{:S(2)}) collective-permute-start(f32[160,128]{1,0:T(8,128)S(1)} %image.3.refs_0_), channel_id=1, source_target_pairs={{0,2},{2,0},{4,6},{6,4},{8,10},{10,8},{12,14},{14,12},{16,18},{18,... | collective-permute-start | bytes 245768 | tf_op jit(solution)/shard_map/ppermute | solution.py:426
  47.1 0.1 collective-permute-start.20
  47.1 2.0 %collective-permute-done.17.refs_2_ = f32[160,128]{1,0:T(8,128)S(1)} collective-permute-done((f32[160,128]{1,0:T(8,128)S(1)}, f32[160,128]{1,0:T(8,128)S(1)}, u32[]{:S(2)}, u32[]{:S(2)}) %collective-permute-start.17) | collective-permute-done | bytes 81952 | tf_op jit(solution)/shard_map/ppermute | solution.py:426
  49.1 0.1 collective-permute-done.18.refs_3_
  49.2 0.5 collective-permute-start.22
  49.7 0.4 collective-permute-done.19.refs_4_
  50.0 1.6 %collective-permute-start.23 = (f32[160,128]{1,0:T(8,128)S(1)}, f32[160,128]{1,0:T(8,128)S(1)}, u32[]{:S(2)}, u32[]{:S(2)}) collective-permute-start(f32[160,128]{1,0:T(8,128)S(1)} %collective-permute-done.19.refs_4_), channel_id=1, source_target_pairs={{0,1},{2,3},{4,5},{6,7},{8,9},{10,11},{12,13},{14,15},{16,17},{18,... | collective-permute-start | bytes 245768 | tf_op jit(solution)/shard_map/ppermute | solution.py:428
  51.6 0.9 %inverse.3.refs_12_ = f32[32,128]{1,0:T(8,128)S(1)} custom-call(f32[32,128]{1,0:T(8,128)S(1)} %get-tuple-element.35.norm_ref.refs_11_), custom_call_target="tpu_custom_call" | custom-call | tf_op jit(solution)/shard_map/inverse/pallas_call | solution.py:524
  52.6 0.0 collective-permute-done.21.refs_6_
  52.6 0.0 collective-permute-done.22.refs_7_
  52.6 3.0 %step.3 = (f32[32,512]{1,0:T(8,128)S(1)}, f32[2,32,256]{2,1,0:T(8,128)S(1)}, f32[32,256]{1,0:T(8,128)S(1)}, f32[32,128]{1,0:T(8,128)S(1)}, f32[32,256]{1,0:T(8,128)S(1)}) custom-call(f32[160,128]{1,0:T(8,128)S(1)} %image.3.refs_0_, f32[160,128]{1,0:T(8,128)S(1)} %collective-permute-done.16.refs_1_, f32[160,128]{1,0:T(8,128)S(1)} %collective-permute-done.17.refs_2_, ...), custom_call_target="tpu_custom_call" | custom-call | tf_op jit(solution)/shard_map/step/pallas_call | solution.py:533
  55.6 0.3 collective-permute-start.24
  55.9 1.0 %collective-permute-done.24.other_ref = f32[32,512]{1,0:T(8,128)S(1)} collective-permute-done((f32[32,512]{1,0:T(8,128)S(1)}, f32[32,512]{1,0:T(8,128)S(1)}, u32[]{:S(2)}, u32[]{:S(2)}) %collective-permute-start.24) | collective-permute-done | bytes 65568 | tf_op jit(solution)/shard_map/ppermute | solution.py:407
  56.9 0.2 last_image.1
  57.1 2.9 %collective-permute-start.25 = (f32[32,128]{1,0:T(8,128)S(1)}, f32[32,128]{1,0:T(8,128)S(1)}, u32[]{:S(2)}, u32[]{:S(2)}) collective-permute-start(f32[32,128]{1,0:T(8,128)S(1)} %get-tuple-element.39.refs_0_), channel_id=1, source_target_pairs={{0,14},{2,12},{4,10},{6,8},{8,6},{10,4},{12,2},{14,0},{1,9},{3,11}... | collective-permute-start | bytes 49160 | tf_op jit(solution)/shard_map/ppermute | solution.py:426
  60.0 0.0 collective-permute-start.26
  60.0 2.1 %collective-permute-start.27 = (f32[32,128]{1,0:T(8,128)S(1)}, f32[32,128]{1,0:T(8,128)S(1)}, u32[]{:S(2)}, u32[]{:S(2)}) collective-permute-start(f32[32,128]{1,0:T(8,128)S(1)} %get-tuple-element.39.refs_0_), channel_id=1, source_target_pairs={{0,4},{2,6},{4,0},{6,2},{8,12},{10,14},{12,8},{14,10},{1,13},{3,15... | collective-permute-start | bytes 49160 | tf_op jit(solution)/shard_map/ppermute | solution.py:426
  62.2 3.3 %collective-permute-start.28 = (f32[32,128]{1,0:T(8,128)S(1)}, f32[32,128]{1,0:T(8,128)S(1)}, u32[]{:S(2)}, u32[]{:S(2)}) collective-permute-start(f32[32,128]{1,0:T(8,128)S(1)} %get-tuple-element.39.refs_0_), channel_id=1, source_target_pairs={{0,2},{2,0},{4,6},{6,4},{8,10},{10,8},{12,14},{14,12},{16,18},{18,... | collective-permute-start | bytes 49160 | tf_op jit(solution)/shard_map/ppermute | solution.py:426
  65.4 0.0 collective-permute-done.25.refs_1_
  65.4 0.1 collective-permute-start.29
  65.5 0.5 collective-permute-start.30
  66.0 0.1 collective-permute-start.31
  66.1 1.7 %collective-permute-done.28.refs_4_ = f32[32,128]{1,0:T(8,128)S(1)} collective-permute-done((f32[32,128]{1,0:T(8,128)S(1)}, f32[32,128]{1,0:T(8,128)S(1)}, u32[]{:S(2)}, u32[]{:S(2)}) %collective-permute-start.28) | collective-permute-done | bytes 16416 | tf_op jit(solution)/shard_map/ppermute | solution.py:426
  67.8 1.3 %collective-permute-start.32 = (f32[32,128]{1,0:T(8,128)S(1)}, f32[32,128]{1,0:T(8,128)S(1)}, u32[]{:S(2)}, u32[]{:S(2)}) collective-permute-start(f32[32,128]{1,0:T(8,128)S(1)} %collective-permute-done.28.refs_4_), channel_id=1, source_target_pairs={{0,1},{2,3},{4,5},{6,7},{8,9},{10,11},{12,13},{14,15},{16,17},{18,... | collective-permute-start | bytes 49160 | tf_op jit(solution)/shard_map/ppermute | solution.py:428
  69.1 0.8 %collective-permute-done.32.refs_8_ = f32[32,128]{1,0:T(8,128)S(1)} collective-permute-done((f32[32,128]{1,0:T(8,128)S(1)}, f32[32,128]{1,0:T(8,128)S(1)}, u32[]{:S(2)}, u32[]{:S(2)}) %collective-permute-start.32) | collective-permute-done | bytes 16416 | tf_op jit(solution)/shard_map/ppermute | solution.py:428
  69.9 1.7 %last.1 = (f32[32,256]{1,0:T(8,128)}, f32[32,256]{1,0:T(8,128)}) custom-call(f32[32,128]{1,0:T(8,128)S(1)} %get-tuple-element.39.refs_0_, f32[32,128]{1,0:T(8,128)S(1)} %collective-permute-done.25.refs_1_, f32[32,128]{1,0:T(8,128)S(1)} %collective-permute-done.26.refs_2_, f32[32,128]{1,0:T(8,128)S(1)} %collective-permute-done.27.refs_3_, ...), custom_call_target="tpu_custom_call" | custom-call | tf_op jit(solution)/shard_map/last/pallas_call | solution.py:556
  (16 shorter events, 0.0 us)
Async XLA Ops:
  1.5 8.9 %collective-permute-start = (f32[32,256]{1,0:T(8,128)S(1)}, f32[32,256]{1,0:T(8,128)S(1)}, u32[]{:S(2)}, u32[]{:S(2)}) collective-permute-start(f32[32,256]{1,0:T(8,128)S(1)} %multiply_multiply_fusion.refs_0_), channel_id=1, source_target_pairs={{0,4},{2,6},{4,0},{6,2},{8,12},{10,14},{12,8},{14,10},{1,5},{3,7},... | collective-permute-start | bytes 98312 | tf_op jit(solution)/shard_map/ppermute | solution.py:404
  4.5 5.9 %collective-permute-start.1 = (f32[32,256]{1,0:T(8,128)S(1)}, f32[32,256]{1,0:T(8,128)S(1)}, u32[]{:S(2)}, u32[]{:S(2)}) collective-permute-start(f32[32,256]{1,0:T(8,128)S(1)} %multiply_multiply_fusion.refs_0_), channel_id=1, source_target_pairs={{0,8},{2,10},{4,12},{6,14},{8,0},{10,2},{12,4},{14,6},{1,9},{3,11}... | collective-permute-start | bytes 98312 | tf_op jit(solution)/shard_map/ppermute | solution.py:404
  7.1 5.7 %collective-permute-start.2 = (f32[32,256]{1,0:T(8,128)S(1)}, f32[32,256]{1,0:T(8,128)S(1)}, u32[]{:S(2)}, u32[]{:S(2)}) collective-permute-start(f32[32,256]{1,0:T(8,128)S(1)} %multiply_multiply_fusion.refs_0_), channel_id=1, source_target_pairs={{0,12},{2,14},{4,8},{6,10},{8,4},{10,6},{12,0},{14,2},{1,13},{3,15... | collective-permute-start | bytes 98312 | tf_op jit(solution)/shard_map/ppermute | solution.py:404
  12.8 5.0 %collective-permute-start.3 = (f32[4,32,256]{2,1,0:T(8,128)S(1)}, f32[4,32,256]{2,1,0:T(8,128)S(1)}, u32[]{:S(2)}, u32[]{:S(2)}) collective-permute-start(f32[4,32,256]{2,1,0:T(8,128)S(1)} %join.1.joined_ref.even_ref.near_ref), channel_id=1, source_target_pairs={{0,2},{2,0},{4,6},{6,4},{8,10},{10,8},{12,14},{14,12},{1,3},{3,1},... | collective-permute-start | bytes 393224 | tf_op jit(solution)/shard_map/ppermute | solution.py:404
  18.7 15.1 %collective-permute-start.14 = (f32[8,32,256]{2,1,0:T(8,128)S(1)}, f32[8,32,256]{2,1,0:T(8,128)S(1)}, u32[]{:S(2)}, u32[]{:S(2)}) collective-permute-start(f32[8,32,256]{2,1,0:T(8,128)S(1)} %get-tuple-element.28.near_ref), channel_id=1, source_target_pairs={{0,1},{1,0},{2,3},{3,2},{4,5},{5,4},{6,7},{7,6},{8,9},{9,8},{10,11... | collective-permute-start | bytes 786440 | tf_op jit(solution)/shard_map/ppermute | solution.py:407
  18.8 1.7 %collective-permute-start.4 = (f32[32,640]{1,0:T(8,128)S(1)}, f32[32,640]{1,0:T(8,128)S(1)}, u32[]{:S(2)}, u32[]{:S(2)}) collective-permute-start(f32[32,640]{1,0:T(8,128)S(1)} %get-tuple-element.26.mine_ref), channel_id=1, source_target_pairs={{0,1},{1,0},{2,3},{3,2},{4,5},{5,4},{6,7},{7,6},{8,9},{9,8},{10,11... | collective-permute-start | bytes 245768 | tf_op jit(solution)/shard_map/ppermute | solution.py:407
  19.3 1.2 %collective-permute-start.5 = (f32[32,256]{1,0:T(8,128)S(1)}, f32[32,256]{1,0:T(8,128)S(1)}, u32[]{:S(2)}, u32[]{:S(2)}) collective-permute-start(f32[32,256]{1,0:T(8,128)S(1)} %multiply_multiply_fusion.refs_0_), channel_id=1, source_target_pairs={{0,1},{1,0},{2,3},{3,2},{4,5},{5,4},{6,7},{7,6},{8,9},{9,8},{10,11... | collective-permute-start | bytes 98312 | tf_op jit(solution)/shard_map/ppermute | solution.py:407
  20.7 7.7 %collective-permute-start.6 = (f32[160,128]{1,0:T(8,128)S(1)}, f32[160,128]{1,0:T(8,128)S(1)}, u32[]{:S(2)}, u32[]{:S(2)}) collective-permute-start(f32[160,128]{1,0:T(8,128)S(1)} %get-tuple-element.27.refs_0_), channel_id=1, source_target_pairs={{0,14},{2,12},{4,10},{6,8},{8,6},{10,4},{12,2},{14,0},{1,9},{3,11}... | collective-permute-start | bytes 245768 | tf_op jit(solution)/shard_map/ppermute | solution.py:426
  23.0 7.4 %collective-permute-start.7 = (f32[160,128]{1,0:T(8,128)S(1)}, f32[160,128]{1,0:T(8,128)S(1)}, u32[]{:S(2)}, u32[]{:S(2)}) collective-permute-start(f32[160,128]{1,0:T(8,128)S(1)} %get-tuple-element.27.refs_0_), channel_id=1, source_target_pairs={{0,6},{2,4},{4,2},{6,0},{8,14},{10,12},{12,10},{14,8},{1,11},{3,9}... | collective-permute-start | bytes 245768 | tf_op jit(solution)/shard_map/ppermute | solution.py:426
  23.0 7.5 %collective-permute-start.8 = (f32[160,128]{1,0:T(8,128)S(1)}, f32[160,128]{1,0:T(8,128)S(1)}, u32[]{:S(2)}, u32[]{:S(2)}) collective-permute-start(f32[160,128]{1,0:T(8,128)S(1)} %get-tuple-element.27.refs_0_), channel_id=1, source_target_pairs={{0,4},{2,6},{4,0},{6,2},{8,12},{10,14},{12,8},{14,10},{1,13},{3,15... | collective-permute-start | bytes 245768 | tf_op jit(solution)/shard_map/ppermute | solution.py:426
  25.1 6.3 %collective-permute-start.9 = (f32[160,128]{1,0:T(8,128)S(1)}, f32[160,128]{1,0:T(8,128)S(1)}, u32[]{:S(2)}, u32[]{:S(2)}) collective-permute-start(f32[160,128]{1,0:T(8,128)S(1)} %get-tuple-element.27.refs_0_), channel_id=1, source_target_pairs={{0,2},{2,0},{4,6},{6,4},{8,10},{10,8},{12,14},{14,12},{16,18},{18,... | collective-permute-start | bytes 245768 | tf_op jit(solution)/shard_map/ppermute | solution.py:426
  28.4 5.5 %collective-permute-start.10 = (f32[160,128]{1,0:T(8,128)S(1)}, f32[160,128]{1,0:T(8,128)S(1)}, u32[]{:S(2)}, u32[]{:S(2)}) collective-permute-start(f32[160,128]{1,0:T(8,128)S(1)} %collective-permute-done.6.refs_1_), channel_id=1, source_target_pairs={{0,1},{1,0},{2,3},{3,2},{4,5},{5,4},{6,7},{7,6},{8,9},{9,8},{10,11... | collective-permute-start | bytes 245768 | tf_op jit(solution)/shard_map/ppermute | solution.py:428
  30.5 3.5 %collective-permute-start.11 = (f32[160,128]{1,0:T(8,128)S(1)}, f32[160,128]{1,0:T(8,128)S(1)}, u32[]{:S(2)}, u32[]{:S(2)}) collective-permute-start(f32[160,128]{1,0:T(8,128)S(1)} %collective-permute-done.7.refs_2_), channel_id=1, source_target_pairs={{0,1},{1,0},{2,3},{3,2},{4,5},{5,4},{6,7},{7,6},{8,9},{9,8},{10,11... | collective-permute-start | bytes 245768 | tf_op jit(solution)/shard_map/ppermute | solution.py:428
  30.5 3.5 %collective-permute-start.12 = (f32[160,128]{1,0:T(8,128)S(1)}, f32[160,128]{1,0:T(8,128)S(1)}, u32[]{:S(2)}, u32[]{:S(2)}) collective-permute-start(f32[160,128]{1,0:T(8,128)S(1)} %collective-permute-done.8.refs_3_), channel_id=1, source_target_pairs={{0,1},{1,0},{2,3},{3,2},{4,5},{5,4},{6,7},{7,6},{8,9},{9,8},{10,11... | collective-permute-start | bytes 245768 | tf_op jit(solution)/shard_map/ppermute | solution.py:428
  31.4 2.5 %collective-permute-start.13 = (f32[160,128]{1,0:T(8,128)S(1)}, f32[160,128]{1,0:T(8,128)S(1)}, u32[]{:S(2)}, u32[]{:S(2)}) collective-permute-start(f32[160,128]{1,0:T(8,128)S(1)} %collective-permute-done.9.refs_4_), channel_id=1, source_target_pairs={{0,1},{2,3},{4,5},{6,7},{8,9},{10,11},{12,13},{14,15},{16,17},{18,... | collective-permute-start | bytes 245768 | tf_op jit(solution)/shard_map/ppermute | solution.py:428
  37.0 1.3 %collective-permute-start.15 = (f32[32,512]{1,0:T(8,128)S(1)}, f32[32,512]{1,0:T(8,128)S(1)}, u32[]{:S(2)}, u32[]{:S(2)}) collective-permute-start(f32[32,512]{1,0:T(8,128)S(1)} %get-tuple-element.32.mine_ref), channel_id=1, source_target_pairs={{0,1},{1,0},{2,3},{3,2},{4,5},{5,4},{6,7},{7,6},{8,9},{9,8},{10,11... | collective-permute-start | bytes 196616 | tf_op jit(solution)/shard_map/ppermute | solution.py:407
  38.5 8.5 %collective-permute-start.16 = (f32[160,128]{1,0:T(8,128)S(1)}, f32[160,128]{1,0:T(8,128)S(1)}, u32[]{:S(2)}, u32[]{:S(2)}) collective-permute-start(f32[160,128]{1,0:T(8,128)S(1)} %image.3.refs_0_), channel_id=1, source_target_pairs={{0,14},{2,12},{4,10},{6,8},{8,6},{10,4},{12,2},{14,0},{1,9},{3,11}... | collective-permute-start | bytes 245768 | tf_op jit(solution)/shard_map/ppermute | solution.py:426
  41.7 7.5 %collective-permute-start.17 = (f32[160,128]{1,0:T(8,128)S(1)}, f32[160,128]{1,0:T(8,128)S(1)}, u32[]{:S(2)}, u32[]{:S(2)}) collective-permute-start(f32[160,128]{1,0:T(8,128)S(1)} %image.3.refs_0_), channel_id=1, source_target_pairs={{0,6},{2,4},{4,2},{6,0},{8,14},{10,12},{12,10},{14,8},{1,11},{3,9}... | collective-permute-start | bytes 245768 | tf_op jit(solution)/shard_map/ppermute | solution.py:426
  41.7 7.5 %collective-permute-start.18 = (f32[160,128]{1,0:T(8,128)S(1)}, f32[160,128]{1,0:T(8,128)S(1)}, u32[]{:S(2)}, u32[]{:S(2)}) collective-permute-start(f32[160,128]{1,0:T(8,128)S(1)} %image.3.refs_0_), channel_id=1, source_target_pairs={{0,4},{2,6},{4,0},{6,2},{8,12},{10,14},{12,8},{14,10},{1,13},{3,15... | collective-permute-start | bytes 245768 | tf_op jit(solution)/shard_map/ppermute | solution.py:426
  43.6 6.4 %collective-permute-start.19 = (f32[160,128]{1,0:T(8,128)S(1)}, f32[160,128]{1,0:T(8,128)S(1)}, u32[]{:S(2)}, u32[]{:S(2)}) collective-permute-start(f32[160,128]{1,0:T(8,128)S(1)} %image.3.refs_0_), channel_id=1, source_target_pairs={{0,2},{2,0},{4,6},{6,4},{8,10},{10,8},{12,14},{14,12},{16,18},{18,... | collective-permute-start | bytes 245768 | tf_op jit(solution)/shard_map/ppermute | solution.py:426
  47.1 5.5 %collective-permute-start.20 = (f32[160,128]{1,0:T(8,128)S(1)}, f32[160,128]{1,0:T(8,128)S(1)}, u32[]{:S(2)}, u32[]{:S(2)}) collective-permute-start(f32[160,128]{1,0:T(8,128)S(1)} %collective-permute-done.16.refs_1_), channel_id=1, source_target_pairs={{0,1},{1,0},{2,3},{3,2},{4,5},{5,4},{6,7},{7,6},{8,9},{9,8},{10,11... | collective-permute-start | bytes 245768 | tf_op jit(solution)/shard_map/ppermute | solution.py:428
  49.1 3.4 %collective-permute-start.21 = (f32[160,128]{1,0:T(8,128)S(1)}, f32[160,128]{1,0:T(8,128)S(1)}, u32[]{:S(2)}, u32[]{:S(2)}) collective-permute-start(f32[160,128]{1,0:T(8,128)S(1)} %collective-permute-done.17.refs_2_), channel_id=1, source_target_pairs={{0,1},{1,0},{2,3},{3,2},{4,5},{5,4},{6,7},{7,6},{8,9},{9,8},{10,11... | collective-permute-start | bytes 245768 | tf_op jit(solution)/shard_map/ppermute | solution.py:428
  49.2 3.4 %collective-permute-start.22 = (f32[160,128]{1,0:T(8,128)S(1)}, f32[160,128]{1,0:T(8,128)S(1)}, u32[]{:S(2)}, u32[]{:S(2)}) collective-permute-start(f32[160,128]{1,0:T(8,128)S(1)} %collective-permute-done.18.refs_3_), channel_id=1, source_target_pairs={{0,1},{1,0},{2,3},{3,2},{4,5},{5,4},{6,7},{7,6},{8,9},{9,8},{10,11... | collective-permute-start | bytes 245768 | tf_op jit(solution)/shard_map/ppermute | solution.py:428
  50.0 2.6 %collective-permute-start.23 = (f32[160,128]{1,0:T(8,128)S(1)}, f32[160,128]{1,0:T(8,128)S(1)}, u32[]{:S(2)}, u32[]{:S(2)}) collective-permute-start(f32[160,128]{1,0:T(8,128)S(1)} %collective-permute-done.19.refs_4_), channel_id=1, source_target_pairs={{0,1},{2,3},{4,5},{6,7},{8,9},{10,11},{12,13},{14,15},{16,17},{18,... | collective-permute-start | bytes 245768 | tf_op jit(solution)/shard_map/ppermute | solution.py:428
  55.6 1.3 %collective-permute-start.24 = (f32[32,512]{1,0:T(8,128)S(1)}, f32[32,512]{1,0:T(8,128)S(1)}, u32[]{:S(2)}, u32[]{:S(2)}) collective-permute-start(f32[32,512]{1,0:T(8,128)S(1)} %get-tuple-element.37.mine_ref), channel_id=1, source_target_pairs={{0,1},{1,0},{2,3},{3,2},{4,5},{5,4},{6,7},{7,6},{8,9},{9,8},{10,11... | collective-permute-start | bytes 196616 | tf_op jit(solution)/shard_map/ppermute | solution.py:407
  57.1 8.3 %collective-permute-start.25 = (f32[32,128]{1,0:T(8,128)S(1)}, f32[32,128]{1,0:T(8,128)S(1)}, u32[]{:S(2)}, u32[]{:S(2)}) collective-permute-start(f32[32,128]{1,0:T(8,128)S(1)} %get-tuple-element.39.refs_0_), channel_id=1, source_target_pairs={{0,14},{2,12},{4,10},{6,8},{8,6},{10,4},{12,2},{14,0},{1,9},{3,11}... | collective-permute-start | bytes 49160 | tf_op jit(solution)/shard_map/ppermute | solution.py:426
  60.0 5.5 %collective-permute-start.26 = (f32[32,128]{1,0:T(8,128)S(1)}, f32[32,128]{1,0:T(8,128)S(1)}, u32[]{:S(2)}, u32[]{:S(2)}) collective-permute-start(f32[32,128]{1,0:T(8,128)S(1)} %get-tuple-element.39.refs_0_), channel_id=1, source_target_pairs={{0,6},{2,4},{4,2},{6,0},{8,14},{10,12},{12,10},{14,8},{1,11},{3,9}... | collective-permute-start | bytes 49160 | tf_op jit(solution)/shard_map/ppermute | solution.py:426
  60.0 6.0 %collective-permute-start.27 = (f32[32,128]{1,0:T(8,128)S(1)}, f32[32,128]{1,0:T(8,128)S(1)}, u32[]{:S(2)}, u32[]{:S(2)}) collective-permute-start(f32[32,128]{1,0:T(8,128)S(1)} %get-tuple-element.39.refs_0_), channel_id=1, source_target_pairs={{0,4},{2,6},{4,0},{6,2},{8,12},{10,14},{12,8},{14,10},{1,13},{3,15... | collective-permute-start | bytes 49160 | tf_op jit(solution)/shard_map/ppermute | solution.py:426
  62.2 5.6 %collective-permute-start.28 = (f32[32,128]{1,0:T(8,128)S(1)}, f32[32,128]{1,0:T(8,128)S(1)}, u32[]{:S(2)}, u32[]{:S(2)}) collective-permute-start(f32[32,128]{1,0:T(8,128)S(1)} %get-tuple-element.39.refs_0_), channel_id=1, source_target_pairs={{0,2},{2,0},{4,6},{6,4},{8,10},{10,8},{12,14},{14,12},{16,18},{18,... | collective-permute-start | bytes 49160 | tf_op jit(solution)/shard_map/ppermute | solution.py:426
  65.4 3.6 %collective-permute-start.29 = (f32[32,128]{1,0:T(8,128)S(1)}, f32[32,128]{1,0:T(8,128)S(1)}, u32[]{:S(2)}, u32[]{:S(2)}) collective-permute-start(f32[32,128]{1,0:T(8,128)S(1)} %collective-permute-done.25.refs_1_), channel_id=1, source_target_pairs={{0,1},{1,0},{2,3},{3,2},{4,5},{5,4},{6,7},{7,6},{8,9},{9,8},{10,11... | collective-permute-start | bytes 49160 | tf_op jit(solution)/shard_map/ppermute | solution.py:428
  65.5 3.5 %collective-permute-start.30 = (f32[32,128]{1,0:T(8,128)S(1)}, f32[32,128]{1,0:T(8,128)S(1)}, u32[]{:S(2)}, u32[]{:S(2)}) collective-permute-start(f32[32,128]{1,0:T(8,128)S(1)} %collective-permute-done.26.refs_2_), channel_id=1, source_target_pairs={{0,1},{1,0},{2,3},{3,2},{4,5},{5,4},{6,7},{7,6},{8,9},{9,8},{10,11... | collective-permute-start | bytes 49160 | tf_op jit(solution)/shard_map/ppermute | solution.py:428
  66.0 3.1 %collective-permute-start.31 = (f32[32,128]{1,0:T(8,128)S(1)}, f32[32,128]{1,0:T(8,128)S(1)}, u32[]{:S(2)}, u32[]{:S(2)}) collective-permute-start(f32[32,128]{1,0:T(8,128)S(1)} %collective-permute-done.27.refs_3_), channel_id=1, source_target_pairs={{0,1},{1,0},{2,3},{3,2},{4,5},{5,4},{6,7},{7,6},{8,9},{9,8},{10,11... | collective-permute-start | bytes 49160 | tf_op jit(solution)/shard_map/ppermute | solution.py:428
  67.8 2.1 %collective-permute-start.32 = (f32[32,128]{1,0:T(8,128)S(1)}, f32[32,128]{1,0:T(8,128)S(1)}, u32[]{:S(2)}, u32[]{:S(2)}) collective-permute-start(f32[32,128]{1,0:T(8,128)S(1)} %collective-permute-done.28.refs_4_), channel_id=1, source_target_pairs={{0,1},{2,3},{4,5},{6,7},{8,9},{10,11},{12,13},{14,15},{16,17},{18,... | collective-permute-start | bytes 49160 | tf_op jit(solution)/shard_map/ppermute | solution.py:428

commit v8 on v7

--- a/solution.py
+++ b/solution.py
@@ -285,12 +285,13 @@
     return near, far
 
 
-def image_kernel(first, mine_ref, other_ref, near_ref, far_ref, out_ref, *norm_ref):
+def image_kernel(first, mine_ref, other_ref, near_ref, far_ref, *refs):
+    out_ref, norm_ref = refs[1:3] if first else (refs[0], None)
     core = lax.axis_index("col")
     size, width = near_ref.shape[1:]
     near, far = add_halves(mine_ref, other_ref, width)
     if first:
-        norm_ref[0][...] = finish(mine_ref[:, 2 * width :] + other_ref[:, 2 * width :])
+        norm_ref[...] = finish(mine_ref[:, 2 * width :] + other_ref[:, 2 * width :])
     parts = width // LANES
     for i in range(parts):
         lanes = slice(i * LANES, (i + 1) * LANES)
@@ -412,7 +413,7 @@
         if pieces != 8:
             found = [value] + [swap(value, k) for k in range(1, pieces)]
             return found, [(k, k) for k in range(pieces)]
-        shares = ((7, 4), (3, 5), (2, 6), (1, 0))
+        shares = ((7, 4), (3, 5), (2, 6), (1, 1))
         fetched = []
         passed = []
         places = {0: (0, 0)}
@@ -420,16 +421,15 @@
             pairs = [
                 (i * 2 + core, (i ^ mask) * 2 + core)
                 for core, mask in enumerate(masks)
-                if mask
                 for i in range(pieces)
             ]
             fetched.append(lax.ppermute(value, ("row", "col"), pairs))
-            pairs = [(core, 1 - core) for core, mask in enumerate(masks) if mask]
-            passed.append(lax.ppermute(fetched[-1], "col", pairs))
-            for core, mask in enumerate(masks):
-                if mask:
-                    here = (turn, turn + len(shares))
-                    places[mask] = here if core == 0 else here[::-1]
+            if masks[0] == masks[1]:
+                places[masks[0]] = (turn, turn)
+            else:
+                passed.append(across(fetched[-1]))
+                places[masks[0]] = (turn, turn + len(shares))
+                places[masks[1]] = (turn + len(shares), turn)
         return [value, *fetched, *passed], [places[k] for k in range(pieces)]
 
     right_side = signs.astype(F32) * vertex_weight[None, :] * column_scale[:, None]
@@ -497,29 +497,33 @@
         compiler_params=params(matrix, state, state),
         name="first",
     )(even, odd, dense)
-    residual, direction = pl.pallas_call(
-        collect_kernel,
-        out_shape=(held, state),
-        in_specs=[VMEM] * 2,
-        out_specs=(VMEM, VMEM),
-        compiler_params=params(held, held, state),
-        name="collect",
-    )(blocks, across(blocks))
     norm = None
     solution = None
+    direction = None
     for iteration in range(ITERS - 1):
         first = iteration == 0
         last = iteration == ITERS - 2
+        sums = (partial_sum, across(partial_sum))
+        given = (even, far_side, blocks) if first else (direction, direction)
         outs = pl.pallas_call(
             functools.partial(image_kernel, first),
-            out_shape=(payload,) + ((small,) if first else ()),
-            in_specs=[VMEM] * 4,
-            out_specs=(VMEM,) * (2 if first else 1),
+            out_shape=(payload, small, blocks) if first else (payload,),
+            in_specs=[VMEM] * 4 + [ANY] * (len(given) - 2),
+            out_specs=(VMEM, VMEM, ANY) if first else (VMEM,),
+            input_output_aliases={4: 2} if first else {},
             compiler_params=params(state, payload),
             name="image",
-        )(partial_sum, across(partial_sum), *((even, far_side) if first else (direction,) * 2))
+        )(*sums, *given)
         if first:
-            norm = outs[1]
+            norm, blocks = outs[1:]
+            residual, direction = pl.pallas_call(
+                collect_kernel,
+                out_shape=(held, state),
+                in_specs=[VMEM] * 2,
+                out_specs=(VMEM, VMEM),
+                compiler_params=params(held, held, state),
+                name="collect",
+            )(blocks, across(blocks))
         found, places = exchange(outs[0])
         inverse = pl.pallas_call(
             inverse_kernel,

time: 72 us -> 63.7 us (0.88)
  starting transfers between devices: 39.1 us -> 27.2 us
  waiting for transfers between devices: 14.1 us -> 18.3 us
    ppermute x12, starting transfers between devices: 24.5 us -> 17.1 us  [exchange(): fetched.append(lax.ppermute(value, ('row', 'col'), pairs))]
    ppermute x12 -> x0, starting transfers between devices: 6.13 us -> none  [exchange(): passed.append(lax.ppermute(fetched[-1], 'col', pairs))]
    ppermute x12, waiting for transfers between devices: 6.49 us -> 11.5 us  [exchange(): fetched.append(lax.ppermute(value, ('row', 'col'), pairs))]
    ppermute x5 -> x14, starting transfers between devices: 1.26 us -> 2.95 us  [across(): lax.ppermute(value, 'col', [(i, (i + 1) % col_devices) for i in range(col...]
    ppermute x12 -> x0, waiting for transfers between devices: 0.82 us -> none  [exchange(): passed.append(lax.ppermute(fetched[-1], 'col', pairs))]
    ppermute x5 -> x14, waiting for transfers between devices: 3.17 us -> 3.05 us  [across(): lax.ppermute(value, 'col', [(i, (i + 1) % col_devices) for i in range(col...]
  transfers between devices with their start and end apart: 33 -> 30, of which waited for: 12 -> 14; matrix products, arithmetic and copies ran while one was open for 0% -> 0% of each run, Pallas kernels for 10% -> 10%
where the time goes in v8:
time: 63.7 us; the launch traced here: 63.6 us
  starting transfers between devices  27.2 us (43%)
  waiting for transfers between devices  18.3 us (29%)
  Pallas kernels  15.8 us (25%)
  between operations  1.45 us (2%)
  other arithmetic  0.85 us (1%)
    ppermute x12, starting transfers between devices, exchange(): fetched.append(lax.ppermute(value, ('row', 'col'), pairs))  17.1 us
    ppermute x12, waiting for transfers between devices, exchange(): fetched.append(lax.ppermute(value, ('row', 'col'), pairs))  11.5 us
    ppermute x4, starting transfers between devices, swap(): return lax.ppermute(value, 'row', [(i, i ^ mask) for i in range(pieces)])  7.2 us
    pallas_call x2, Pallas kernels, per_device(): pl.pallas_call(functools.partial(step_kernel, places, not first, last), o...  6.04 us
    ppermute x4, waiting for transfers between devices, swap(): return lax.ppermute(value, 'row', [(i, i ^ mask) for i in range(pieces)])  3.72 us
    ppermute x14, waiting for transfers between devices, across(): lax.ppermute(value, 'col', [(i, (i + 1) % col_devices) for i in range(col...  3.05 us
    ppermute x14, starting transfers between devices, across(): lax.ppermute(value, 'col', [(i, (i + 1) % col_devices) for i in range(col...  2.95 us
    pallas_call x1, Pallas kernels, per_device(): pl.pallas_call(functools.partial(gather_kernel, rows_dev), out_shape=(tot...  2.52 us
  transfers between devices with their start and end apart: 30, of which 14 were waited for; matrix products, arithmetic and copies ran while one was open for 0% of the time, Pallas kernels for 10%

profile of v8, /device:TPU:0, one launch (start us, length us, event | category | flops | bytes accessed | tf_op | source)
XLA Modules:
  0.0 63.6 jit_solution(7812071651984958752)
XLA Ops:
  0.6 0.8 %multiply_multiply_fusion.refs_0_ = f32[32,256]{1,0:T(8,128)S(1)} fusion(s32[32,256]{1,0:T(8,128)} %param.11, f32[32]{0:T(128)} %param.13, f32[256]{0:T(256)} %param.12), kind=kLoop, calls=%fused_computation | loop fusion | flops 24576 | bytes 66688 | tf_op jit(solution)/shard_map/mul | solution.py:435
  1.5 3.0 %collective-permute-start = (f32[32,256]{1,0:T(8,128)S(1)}, f32[32,256]{1,0:T(8,128)S(1)}, u32[]{:S(2)}, u32[]{:S(2)}) collective-permute-start(f32[32,256]{1,0:T(8,128)S(1)} %multiply_multiply_fusion.refs_0_), channel_id=1, source_target_pairs={{0,4},{2,6},{4,0},{6,2},{8,12},{10,14},{12,8},{14,10},{1,5},{3,7},... | collective-permute-start | bytes 98312 | tf_op jit(solution)/shard_map/ppermute | solution.py:405
  4.5 2.6 %collective-permute-start.1 = (f32[32,256]{1,0:T(8,128)S(1)}, f32[32,256]{1,0:T(8,128)S(1)}, u32[]{:S(2)}, u32[]{:S(2)}) collective-permute-start(f32[32,256]{1,0:T(8,128)S(1)} %multiply_multiply_fusion.refs_0_), channel_id=1, source_target_pairs={{0,8},{2,10},{4,12},{6,14},{8,0},{10,2},{12,4},{14,6},{1,9},{3,11}... | collective-permute-start | bytes 98312 | tf_op jit(solution)/shard_map/ppermute | solution.py:405
  7.1 0.0 collective-permute-start.2
  7.8 2.5 %gather.1 = (f32[64,128,128]{2,1,0:T(8,128)S(1)}, bf16[65,128,128]{2,1,0:T(8,128)(2,1)S(1)}) custom-call(s32[1]{0:T(128)S(6)} %copy.13.count_ref, s32[130]{0:T(256)} %rows_hbm.3, s32[130]{0:T(256)} %cols_hbm.3, bf16[130,128,128]{2,1,0:T(8,128)(2,1)} %tiles_ref.1), custom_call_target="tpu_custom_call" | custom-call | flops 8519680 | bytes 8519680 | tf_op jit(solution)/shard_map/gather/pallas_call | solution.py:449
  10.3 0.0 collective-permute-done.refs_1_
  10.3 0.0 collective-permute-done.1.refs_2_
  10.3 2.5 %collective-permute-done.2.refs_3_ = f32[32,256]{1,0:T(8,128)S(1)} collective-permute-done((f32[32,256]{1,0:T(8,128)S(1)}, f32[32,256]{1,0:T(8,128)S(1)}, u32[]{:S(2)}, u32[]{:S(2)}) %collective-permute-start.2) | collective-permute-done | bytes 32800 | tf_op jit(solution)/shard_map/ppermute | solution.py:405
  12.8 1.6 %collective-permute-start.3 = (f32[4,32,256]{2,1,0:T(8,128)S(1)}, f32[4,32,256]{2,1,0:T(8,128)S(1)}, u32[]{:S(2)}, u32[]{:S(2)}) collective-permute-start(f32[4,32,256]{2,1,0:T(8,128)S(1)} %join.1.joined_ref.even_ref.near_ref), channel_id=1, source_target_pairs={{0,2},{2,0},{4,6},{6,4},{8,10},{10,8},{12,14},{14,12},{1,3},{3,1},... | collective-permute-start | bytes 393224 | tf_op jit(solution)/shard_map/ppermute | solution.py:405
  14.4 2.2 %dense.1 = (bf16[2,2048,512]{2,1,0:T(8,128)(2,1)S(1)}, f32[64,128,128]{2,1,0:T(8,128)S(1)}) custom-call(s32[1]{0:T(128)S(6)} %copy.13.count_ref, s32[130]{0:T(256)} %rows_hbm.3, s32[130]{0:T(256)} %cols_hbm.3, bf16[65,128,128]{2,1,0:T(8,128)(2,1)S(1)} %get-tuple-element.25.rest, ...), custom_call_target="tpu_custom_call", output_to_operand_aliasing={{1}: (4, {})} | custom-call | flops 8519680 | bytes 8519680 | tf_op jit(solution)/shard_map/dense/pallas_call | solution.py:474
  16.6 1.2 %collective-permute-done.3.odd_ref = f32[4,32,256]{2,1,0:T(8,128)S(1)} collective-permute-done((f32[4,32,256]{2,1,0:T(8,128)S(1)}, f32[4,32,256]{2,1,0:T(8,128)S(1)}, u32[]{:S(2)}, u32[]{:S(2)}) %collective-permute-start.3) | collective-permute-done | bytes 131104 | tf_op jit(solution)/shard_map/ppermute | solution.py:405
  17.9 0.9 %first.1 = (f32[32,640]{1,0:T(8,128)S(1)}, f32[8,32,256]{2,1,0:T(8,128)S(1)}) custom-call(f32[4,32,256]{2,1,0:T(8,128)S(1)} %join.1.joined_ref.even_ref.near_ref, f32[4,32,256]{2,1,0:T(8,128)S(1)} %collective-permute-done.3.odd_ref, bf16[2,2048,512]{2,1,0:T(8,128)(2,1)S(1)} %get-tuple-element.26.matrix.refs_12_), custom_call_target="tpu_custom_call" | custom-call | tf_op jit(solution)/shard_map/first/pallas_call | solution.py:492
  18.7 0.1 collective-permute-start.4
  18.8 0.5 collective-permute-start.5
  19.3 0.9 %collective-permute-done.5 = f32[32,256]{1,0:T(8,128)S(1)} collective-permute-done((f32[32,256]{1,0:T(8,128)S(1)}, f32[32,256]{1,0:T(8,128)S(1)}, u32[]{:S(2)}, u32[]{:S(2)}) %collective-permute-start.5) | collective-permute-done | bytes 32800 | tf_op jit(solution)/shard_map/ppermute | solution.py:408
  20.2 0.0 collective-permute-done.4.other_ref
  20.2 0.2 image.2
  20.4 0.4 collective-permute-start.13
  20.7 2.4 %collective-permute-start.6 = (f32[160,128]{1,0:T(8,128)S(1)}, f32[160,128]{1,0:T(8,128)S(1)}, u32[]{:S(2)}, u32[]{:S(2)}) collective-permute-start(f32[160,128]{1,0:T(8,128)S(1)} %get-tuple-element.29.refs_0_), channel_id=1, source_target_pairs={{0,14},{2,12},{4,10},{6,8},{8,6},{10,4},{12,2},{14,0},{1,9},{3,11}... | collective-permute-start | bytes 245768 | tf_op jit(solution)/shard_map/ppermute | solution.py:426
  23.1 0.0 collective-permute-start.7
  23.1 2.9 %collective-permute-start.8 = (f32[160,128]{1,0:T(8,128)S(1)}, f32[160,128]{1,0:T(8,128)S(1)}, u32[]{:S(2)}, u32[]{:S(2)}) collective-permute-start(f32[160,128]{1,0:T(8,128)S(1)} %get-tuple-element.29.refs_0_), channel_id=1, source_target_pairs={{0,4},{2,6},{4,0},{6,2},{8,12},{10,14},{12,8},{14,10},{1,13},{3,15... | collective-permute-start | bytes 245768 | tf_op jit(solution)/shard_map/ppermute | solution.py:426
  26.1 0.6 collective-permute-start.9
  26.6 2.0 %collective-permute-done.6.refs_1_ = f32[160,128]{1,0:T(8,128)S(1)} collective-permute-done((f32[160,128]{1,0:T(8,128)S(1)}, f32[160,128]{1,0:T(8,128)S(1)}, u32[]{:S(2)}, u32[]{:S(2)}) %collective-permute-start.6) | collective-permute-done | bytes 81952 | tf_op jit(solution)/shard_map/ppermute | solution.py:426
  28.6 0.0 collective-permute-start.10
  28.6 0.5 collective-permute-done.7.refs_2_
  29.1 0.0 collective-permute-start.11
  29.1 2.4 %collective-permute-done.8.refs_3_ = f32[160,128]{1,0:T(8,128)S(1)} collective-permute-done((f32[160,128]{1,0:T(8,128)S(1)}, f32[160,128]{1,0:T(8,128)S(1)}, u32[]{:S(2)}, u32[]{:S(2)}) %collective-permute-start.8) | collective-permute-done | bytes 81952 | tf_op jit(solution)/shard_map/ppermute | solution.py:426
  31.4 0.0 collective-permute-start.12
  31.5 0.9 %inverse.2.refs_11_ = f32[32,128]{1,0:T(8,128)S(1)} custom-call(f32[32,128]{1,0:T(8,128)S(1)} %get-tuple-element.33.norm_ref.refs_10_), custom_call_target="tpu_custom_call" | custom-call | tf_op jit(solution)/shard_map/inverse/pallas_call | solution.py:528
  32.4 0.0 collective-permute-done.13.far_ref
  32.4 0.1 collect.1
  32.5 0.0 collective-permute-done.9.refs_4_
  32.5 0.0 collective-permute-done.11.refs_6_
  32.5 0.2 collective-permute-done.12.refs_7_
  32.7 3.0 %step.2 = (f32[32,512]{1,0:T(8,128)S(1)}, f32[9,32,256]{2,1,0:T(8,128)S(1)}, f32[2,8,32,256]{3,2,1,0:T(8,128)S(1)}, f32[32,128]{1,0:T(8,128)S(1)}, f32[32,256]{1,0:T(8,128)S(1)}) custom-call(f32[160,128]{1,0:T(8,128)S(1)} %get-tuple-element.29.refs_0_, f32[160,128]{1,0:T(8,128)S(1)} %collective-permute-done.6.refs_1_, ...), custom_call_target="tpu_custom_call" | custom-call | tf_op jit(solution)/shard_map/step/pallas_call | solution.py:537
  35.7 0.3 collective-permute-start.14
  36.1 1.0 %collective-permute-done.14.other_ref = f32[32,512]{1,0:T(8,128)S(1)} collective-permute-done((f32[32,512]{1,0:T(8,128)S(1)}, f32[32,512]{1,0:T(8,128)S(1)}, u32[]{:S(2)}, u32[]{:S(2)}) %collective-permute-start.14) | collective-permute-done | bytes 65568 | tf_op jit(solution)/shard_map/ppermute | solution.py:408
  37.1 0.2 image.3.refs_0_
  37.3 2.0 %collective-permute-start.15 = (f32[160,128]{1,0:T(8,128)S(1)}, f32[160,128]{1,0:T(8,128)S(1)}, u32[]{:S(2)}, u32[]{:S(2)}) collective-permute-start(f32[160,128]{1,0:T(8,128)S(1)} %image.3.refs_0_), channel_id=1, source_target_pairs={{0,14},{2,12},{4,10},{6,8},{8,6},{10,4},{12,2},{14,0},{1,9},{3,11}... | collective-permute-start | bytes 245768 | tf_op jit(solution)/shard_map/ppermute | solution.py:426
  39.3 2.1 %collective-permute-start.17 = (f32[160,128]{1,0:T(8,128)S(1)}, f32[160,128]{1,0:T(8,128)S(1)}, u32[]{:S(2)}, u32[]{:S(2)}) collective-permute-start(f32[160,128]{1,0:T(8,128)S(1)} %image.3.refs_0_), channel_id=1, source_target_pairs={{0,4},{2,6},{4,0},{6,2},{8,12},{10,14},{12,8},{14,10},{1,13},{3,15... | collective-permute-start | bytes 245768 | tf_op jit(solution)/shard_map/ppermute | solution.py:426
  41.4 1.4 %collective-permute-start.18 = (f32[160,128]{1,0:T(8,128)S(1)}, f32[160,128]{1,0:T(8,128)S(1)}, u32[]{:S(2)}, u32[]{:S(2)}) collective-permute-start(f32[160,128]{1,0:T(8,128)S(1)} %image.3.refs_0_), channel_id=1, source_target_pairs={{0,2},{2,0},{4,6},{6,4},{8,10},{10,8},{12,14},{14,12},{1,3},{3,1},... | collective-permute-start | bytes 245768 | tf_op jit(solution)/shard_map/ppermute | solution.py:426
  42.8 2.1 %collective-permute-done.15.refs_1_ = f32[160,128]{1,0:T(8,128)S(1)} collective-permute-done((f32[160,128]{1,0:T(8,128)S(1)}, f32[160,128]{1,0:T(8,128)S(1)}, u32[]{:S(2)}, u32[]{:S(2)}) %collective-permute-start.15) | collective-permute-done | bytes 81952 | tf_op jit(solution)/shard_map/ppermute | solution.py:426
  44.9 2.5 %collective-permute-done.16.refs_2_ = f32[160,128]{1,0:T(8,128)S(1)} collective-permute-done((f32[160,128]{1,0:T(8,128)S(1)}, f32[160,128]{1,0:T(8,128)S(1)}, u32[]{:S(2)}, u32[]{:S(2)}) %collective-permute-start.16) | collective-permute-done | bytes 81952 | tf_op jit(solution)/shard_map/ppermute | solution.py:426
  47.3 0.0 collective-permute-start.20
  47.3 0.5 collective-permute-start.21
  47.8 0.9 %inverse.3.refs_11_ = f32[32,128]{1,0:T(8,128)S(1)} custom-call(f32[32,128]{1,0:T(8,128)S(1)} %get-tuple-element.37.norm_ref.refs_10_), custom_call_target="tpu_custom_call" | custom-call | tf_op jit(solution)/shard_map/inverse/pallas_call | solution.py:528
  48.8 0.0 collective-permute-done.18.refs_4_
  48.8 0.0 collective-permute-done.19.refs_5_
  48.8 0.0 collective-permute-done.21.refs_7_
  48.8 3.0 %step.3 = (f32[32,512]{1,0:T(8,128)S(1)}, f32[2,32,256]{2,1,0:T(8,128)S(1)}, f32[32,256]{1,0:T(8,128)S(1)}, f32[32,128]{1,0:T(8,128)S(1)}, f32[32,256]{1,0:T(8,128)S(1)}) custom-call(f32[160,128]{1,0:T(8,128)S(1)} %image.3.refs_0_, f32[160,128]{1,0:T(8,128)S(1)} %collective-permute-done.15.refs_1_, f32[160,128]{1,0:T(8,128)S(1)} %collective-permute-done.16.refs_2_, ...), custom_call_target="tpu_custom_call" | custom-call | tf_op jit(solution)/shard_map/step/pallas_call | solution.py:537
  51.8 0.4 collective-permute-start.22
  52.2 1.0 %collective-permute-done.22.other_ref = f32[32,512]{1,0:T(8,128)S(1)} collective-permute-done((f32[32,512]{1,0:T(8,128)S(1)}, f32[32,512]{1,0:T(8,128)S(1)}, u32[]{:S(2)}, u32[]{:S(2)}) %collective-permute-start.22) | collective-permute-done | bytes 65568 | tf_op jit(solution)/shard_map/ppermute | solution.py:408
  53.1 0.2 last_image.1
  53.3 2.2 %collective-permute-start.23 = (f32[32,128]{1,0:T(8,128)S(1)}, f32[32,128]{1,0:T(8,128)S(1)}, u32[]{:S(2)}, u32[]{:S(2)}) collective-permute-start(f32[32,128]{1,0:T(8,128)S(1)} %get-tuple-element.41.refs_0_), channel_id=1, source_target_pairs={{0,14},{2,12},{4,10},{6,8},{8,6},{10,4},{12,2},{14,0},{1,9},{3,11}... | collective-permute-start | bytes 49160 | tf_op jit(solution)/shard_map/ppermute | solution.py:426
  55.5 2.7 %collective-permute-start.25 = (f32[32,128]{1,0:T(8,128)S(1)}, f32[32,128]{1,0:T(8,128)S(1)}, u32[]{:S(2)}, u32[]{:S(2)}) collective-permute-start(f32[32,128]{1,0:T(8,128)S(1)} %get-tuple-element.41.refs_0_), channel_id=1, source_target_pairs={{0,4},{2,6},{4,0},{6,2},{8,12},{10,14},{12,8},{14,10},{1,13},{3,15... | collective-permute-start | bytes 49160 | tf_op jit(solution)/shard_map/ppermute | solution.py:426
  58.2 0.8 %collective-permute-start.26 = (f32[32,128]{1,0:T(8,128)S(1)}, f32[32,128]{1,0:T(8,128)S(1)}, u32[]{:S(2)}, u32[]{:S(2)}) collective-permute-start(f32[32,128]{1,0:T(8,128)S(1)} %get-tuple-element.41.refs_0_), channel_id=1, source_target_pairs={{0,2},{2,0},{4,6},{6,4},{8,10},{10,8},{12,14},{14,12},{1,3},{3,1},... | collective-permute-start | bytes 49160 | tf_op jit(solution)/shard_map/ppermute | solution.py:426
  59.0 0.9 %collective-permute-done.23.refs_1_ = f32[32,128]{1,0:T(8,128)S(1)} collective-permute-done((f32[32,128]{1,0:T(8,128)S(1)}, f32[32,128]{1,0:T(8,128)S(1)}, u32[]{:S(2)}, u32[]{:S(2)}) %collective-permute-start.23) | collective-permute-done | bytes 16416 | tf_op jit(solution)/shard_map/ppermute | solution.py:426
  60.0 0.0 collective-permute-start.27
  60.0 0.2 collective-permute-done.24.refs_2_
  60.2 0.3 collective-permute-start.28
  60.5 0.0 collective-permute-done.25.refs_3_
  60.5 0.5 collective-permute-start.29
  60.9 1.0 %collective-permute-done.26.refs_4_ = f32[32,128]{1,0:T(8,128)S(1)} collective-permute-done((f32[32,128]{1,0:T(8,128)S(1)}, f32[32,128]{1,0:T(8,128)S(1)}, u32[]{:S(2)}, u32[]{:S(2)}) %collective-permute-start.26) | collective-permute-done | bytes 16416 | tf_op jit(solution)/shard_map/ppermute | solution.py:426
  62.0 1.7 %last.1 = (f32[32,256]{1,0:T(8,128)}, f32[32,256]{1,0:T(8,128)}) custom-call(f32[32,128]{1,0:T(8,128)S(1)} %get-tuple-element.41.refs_0_, f32[32,128]{1,0:T(8,128)S(1)} %collective-permute-done.23.refs_1_, f32[32,128]{1,0:T(8,128)S(1)} %collective-permute-done.24.refs_2_, f32[32,128]{1,0:T(8,128)S(1)} %collective-permute-done.25.refs_3_, ...), custom_call_target="tpu_custom_call" | custom-call | tf_op jit(solution)/shard_map/last/pallas_call | solution.py:560
  (10 shorter events, 0.0 us)
Async XLA Ops:
  1.5 8.8 %collective-permute-start = (f32[32,256]{1,0:T(8,128)S(1)}, f32[32,256]{1,0:T(8,128)S(1)}, u32[]{:S(2)}, u32[]{:S(2)}) collective-permute-start(f32[32,256]{1,0:T(8,128)S(1)} %multiply_multiply_fusion.refs_0_), channel_id=1, source_target_pairs={{0,4},{2,6},{4,0},{6,2},{8,12},{10,14},{12,8},{14,10},{1,5},{3,7},... | collective-permute-start | bytes 98312 | tf_op jit(solution)/shard_map/ppermute | solution.py:405
  4.5 5.8 %collective-permute-start.1 = (f32[32,256]{1,0:T(8,128)S(1)}, f32[32,256]{1,0:T(8,128)S(1)}, u32[]{:S(2)}, u32[]{:S(2)}) collective-permute-start(f32[32,256]{1,0:T(8,128)S(1)} %multiply_multiply_fusion.refs_0_), channel_id=1, source_target_pairs={{0,8},{2,10},{4,12},{6,14},{8,0},{10,2},{12,4},{14,6},{1,9},{3,11}... | collective-permute-start | bytes 98312 | tf_op jit(solution)/shard_map/ppermute | solution.py:405
  7.1 5.7 %collective-permute-start.2 = (f32[32,256]{1,0:T(8,128)S(1)}, f32[32,256]{1,0:T(8,128)S(1)}, u32[]{:S(2)}, u32[]{:S(2)}) collective-permute-start(f32[32,256]{1,0:T(8,128)S(1)} %multiply_multiply_fusion.refs_0_), channel_id=1, source_target_pairs={{0,12},{2,14},{4,8},{6,10},{8,4},{10,6},{12,0},{14,2},{1,13},{3,15... | collective-permute-start | bytes 98312 | tf_op jit(solution)/shard_map/ppermute | solution.py:405
  12.8 5.0 %collective-permute-start.3 = (f32[4,32,256]{2,1,0:T(8,128)S(1)}, f32[4,32,256]{2,1,0:T(8,128)S(1)}, u32[]{:S(2)}, u32[]{:S(2)}) collective-permute-start(f32[4,32,256]{2,1,0:T(8,128)S(1)} %join.1.joined_ref.even_ref.near_ref), channel_id=1, source_target_pairs={{0,2},{2,0},{4,6},{6,4},{8,10},{10,8},{12,14},{14,12},{1,3},{3,1},... | collective-permute-start | bytes 393224 | tf_op jit(solution)/shard_map/ppermute | solution.py:405
  18.7 1.5 %collective-permute-start.4 = (f32[32,640]{1,0:T(8,128)S(1)}, f32[32,640]{1,0:T(8,128)S(1)}, u32[]{:S(2)}, u32[]{:S(2)}) collective-permute-start(f32[32,640]{1,0:T(8,128)S(1)} %get-tuple-element.27.mine_ref), channel_id=1, source_target_pairs={{0,1},{1,0},{2,3},{3,2},{4,5},{5,4},{6,7},{7,6},{8,9},{9,8},{10,11... | collective-permute-start | bytes 245768 | tf_op jit(solution)/shard_map/ppermute | solution.py:408
  18.8 1.4 %collective-permute-start.5 = (f32[32,256]{1,0:T(8,128)S(1)}, f32[32,256]{1,0:T(8,128)S(1)}, u32[]{:S(2)}, u32[]{:S(2)}) collective-permute-start(f32[32,256]{1,0:T(8,128)S(1)} %multiply_multiply_fusion.refs_0_), channel_id=1, source_target_pairs={{0,1},{1,0},{2,3},{3,2},{4,5},{5,4},{6,7},{7,6},{8,9},{9,8},{10,11... | collective-permute-start | bytes 98312 | tf_op jit(solution)/shard_map/ppermute | solution.py:408
  20.4 12.0 %collective-permute-start.13 = (f32[8,32,256]{2,1,0:T(8,128)S(1)}, f32[8,32,256]{2,1,0:T(8,128)S(1)}, u32[]{:S(2)}, u32[]{:S(2)}) collective-permute-start(f32[8,32,256]{2,1,0:T(8,128)S(1)} %get-tuple-element.30.near_ref), channel_id=1, source_target_pairs={{0,1},{1,0},{2,3},{3,2},{4,5},{5,4},{6,7},{7,6},{8,9},{9,8},{10,11... | collective-permute-start | bytes 786440 | tf_op jit(solution)/shard_map/ppermute | solution.py:408
  20.7 7.8 %collective-permute-start.6 = (f32[160,128]{1,0:T(8,128)S(1)}, f32[160,128]{1,0:T(8,128)S(1)}, u32[]{:S(2)}, u32[]{:S(2)}) collective-permute-start(f32[160,128]{1,0:T(8,128)S(1)} %get-tuple-element.29.refs_0_), channel_id=1, source_target_pairs={{0,14},{2,12},{4,10},{6,8},{8,6},{10,4},{12,2},{14,0},{1,9},{3,11}... | collective-permute-start | bytes 245768 | tf_op jit(solution)/shard_map/ppermute | solution.py:426
  23.1 5.9 %collective-permute-start.7 = (f32[160,128]{1,0:T(8,128)S(1)}, f32[160,128]{1,0:T(8,128)S(1)}, u32[]{:S(2)}, u32[]{:S(2)}) collective-permute-start(f32[160,128]{1,0:T(8,128)S(1)} %get-tuple-element.29.refs_0_), channel_id=1, source_target_pairs={{0,6},{2,4},{4,2},{6,0},{8,14},{10,12},{12,10},{14,8},{1,11},{3,9}... | collective-permute-start | bytes 245768 | tf_op jit(solution)/shard_map/ppermute | solution.py:426
  23.1 8.3 %collective-permute-start.8 = (f32[160,128]{1,0:T(8,128)S(1)}, f32[160,128]{1,0:T(8,128)S(1)}, u32[]{:S(2)}, u32[]{:S(2)}) collective-permute-start(f32[160,128]{1,0:T(8,128)S(1)} %get-tuple-element.29.refs_0_), channel_id=1, source_target_pairs={{0,4},{2,6},{4,0},{6,2},{8,12},{10,14},{12,8},{14,10},{1,13},{3,15... | collective-permute-start | bytes 245768 | tf_op jit(solution)/shard_map/ppermute | solution.py:426
  26.1 6.4 %collective-permute-start.9 = (f32[160,128]{1,0:T(8,128)S(1)}, f32[160,128]{1,0:T(8,128)S(1)}, u32[]{:S(2)}, u32[]{:S(2)}) collective-permute-start(f32[160,128]{1,0:T(8,128)S(1)} %get-tuple-element.29.refs_0_), channel_id=1, source_target_pairs={{0,2},{2,0},{4,6},{6,4},{8,10},{10,8},{12,14},{14,12},{1,3},{3,1},... | collective-permute-start | bytes 245768 | tf_op jit(solution)/shard_map/ppermute | solution.py:426
  28.6 3.9 %collective-permute-start.10 = (f32[160,128]{1,0:T(8,128)S(1)}, f32[160,128]{1,0:T(8,128)S(1)}, u32[]{:S(2)}, u32[]{:S(2)}) collective-permute-start(f32[160,128]{1,0:T(8,128)S(1)} %collective-permute-done.6.refs_1_), channel_id=1, source_target_pairs={{0,1},{1,0},{2,3},{3,2},{4,5},{5,4},{6,7},{7,6},{8,9},{9,8},{10,11... | collective-permute-start | bytes 245768 | tf_op jit(solution)/shard_map/ppermute | solution.py:408
  29.1 3.4 %collective-permute-start.11 = (f32[160,128]{1,0:T(8,128)S(1)}, f32[160,128]{1,0:T(8,128)S(1)}, u32[]{:S(2)}, u32[]{:S(2)}) collective-permute-start(f32[160,128]{1,0:T(8,128)S(1)} %collective-permute-done.7.refs_2_), channel_id=1, source_target_pairs={{0,1},{1,0},{2,3},{3,2},{4,5},{5,4},{6,7},{7,6},{8,9},{9,8},{10,11... | collective-permute-start | bytes 245768 | tf_op jit(solution)/shard_map/ppermute | solution.py:408
  31.4 1.3 %collective-permute-start.12 = (f32[160,128]{1,0:T(8,128)S(1)}, f32[160,128]{1,0:T(8,128)S(1)}, u32[]{:S(2)}, u32[]{:S(2)}) collective-permute-start(f32[160,128]{1,0:T(8,128)S(1)} %collective-permute-done.8.refs_3_), channel_id=1, source_target_pairs={{0,1},{1,0},{2,3},{3,2},{4,5},{5,4},{6,7},{7,6},{8,9},{9,8},{10,11... | collective-permute-start | bytes 245768 | tf_op jit(solution)/shard_map/ppermute | solution.py:408
  35.7 1.3 %collective-permute-start.14 = (f32[32,512]{1,0:T(8,128)S(1)}, f32[32,512]{1,0:T(8,128)S(1)}, u32[]{:S(2)}, u32[]{:S(2)}) collective-permute-start(f32[32,512]{1,0:T(8,128)S(1)} %get-tuple-element.34.mine_ref), channel_id=1, source_target_pairs={{0,1},{1,0},{2,3},{3,2},{4,5},{5,4},{6,7},{7,6},{8,9},{9,8},{10,11... | collective-permute-start | bytes 196616 | tf_op jit(solution)/shard_map/ppermute | solution.py:408
  37.3 7.6 %collective-permute-start.15 = (f32[160,128]{1,0:T(8,128)S(1)}, f32[160,128]{1,0:T(8,128)S(1)}, u32[]{:S(2)}, u32[]{:S(2)}) collective-permute-start(f32[160,128]{1,0:T(8,128)S(1)} %image.3.refs_0_), channel_id=1, source_target_pairs={{0,14},{2,12},{4,10},{6,8},{8,6},{10,4},{12,2},{14,0},{1,9},{3,11}... | collective-permute-start | bytes 245768 | tf_op jit(solution)/shard_map/ppermute | solution.py:426
  39.3 8.1 %collective-permute-start.16 = (f32[160,128]{1,0:T(8,128)S(1)}, f32[160,128]{1,0:T(8,128)S(1)}, u32[]{:S(2)}, u32[]{:S(2)}) collective-permute-start(f32[160,128]{1,0:T(8,128)S(1)} %image.3.refs_0_), channel_id=1, source_target_pairs={{0,6},{2,4},{4,2},{6,0},{8,14},{10,12},{12,10},{14,8},{1,11},{3,9}... | collective-permute-start | bytes 245768 | tf_op jit(solution)/shard_map/ppermute | solution.py:426
  39.3 8.1 %collective-permute-start.17 = (f32[160,128]{1,0:T(8,128)S(1)}, f32[160,128]{1,0:T(8,128)S(1)}, u32[]{:S(2)}, u32[]{:S(2)}) collective-permute-start(f32[160,128]{1,0:T(8,128)S(1)} %image.3.refs_0_), channel_id=1, source_target_pairs={{0,4},{2,6},{4,0},{6,2},{8,12},{10,14},{12,8},{14,10},{1,13},{3,15... | collective-permute-start | bytes 245768 | tf_op jit(solution)/shard_map/ppermute | solution.py:426
  41.4 7.4 %collective-permute-start.18 = (f32[160,128]{1,0:T(8,128)S(1)}, f32[160,128]{1,0:T(8,128)S(1)}, u32[]{:S(2)}, u32[]{:S(2)}) collective-permute-start(f32[160,128]{1,0:T(8,128)S(1)} %image.3.refs_0_), channel_id=1, source_target_pairs={{0,2},{2,0},{4,6},{6,4},{8,10},{10,8},{12,14},{14,12},{1,3},{3,1},... | collective-permute-start | bytes 245768 | tf_op jit(solution)/shard_map/ppermute | solution.py:426
  44.9 3.9 %collective-permute-start.19 = (f32[160,128]{1,0:T(8,128)S(1)}, f32[160,128]{1,0:T(8,128)S(1)}, u32[]{:S(2)}, u32[]{:S(2)}) collective-permute-start(f32[160,128]{1,0:T(8,128)S(1)} %collective-permute-done.15.refs_1_), channel_id=1, source_target_pairs={{0,1},{1,0},{2,3},{3,2},{4,5},{5,4},{6,7},{7,6},{8,9},{9,8},{10,11... | collective-permute-start | bytes 245768 | tf_op jit(solution)/shard_map/ppermute | solution.py:408
  47.3 1.5 %collective-permute-start.20 = (f32[160,128]{1,0:T(8,128)S(1)}, f32[160,128]{1,0:T(8,128)S(1)}, u32[]{:S(2)}, u32[]{:S(2)}) collective-permute-start(f32[160,128]{1,0:T(8,128)S(1)} %collective-permute-done.16.refs_2_), channel_id=1, source_target_pairs={{0,1},{1,0},{2,3},{3,2},{4,5},{5,4},{6,7},{7,6},{8,9},{9,8},{10,11... | collective-permute-start | bytes 245768 | tf_op jit(solution)/shard_map/ppermute | solution.py:408
  47.3 1.5 %collective-permute-start.21 = (f32[160,128]{1,0:T(8,128)S(1)}, f32[160,128]{1,0:T(8,128)S(1)}, u32[]{:S(2)}, u32[]{:S(2)}) collective-permute-start(f32[160,128]{1,0:T(8,128)S(1)} %collective-permute-done.17.refs_3_), channel_id=1, source_target_pairs={{0,1},{1,0},{2,3},{3,2},{4,5},{5,4},{6,7},{7,6},{8,9},{9,8},{10,11... | collective-permute-start | bytes 245768 | tf_op jit(solution)/shard_map/ppermute | solution.py:408
  51.8 1.3 %collective-permute-start.22 = (f32[32,512]{1,0:T(8,128)S(1)}, f32[32,512]{1,0:T(8,128)S(1)}, u32[]{:S(2)}, u32[]{:S(2)}) collective-permute-start(f32[32,512]{1,0:T(8,128)S(1)} %get-tuple-element.39.mine_ref), channel_id=1, source_target_pairs={{0,1},{1,0},{2,3},{3,2},{4,5},{5,4},{6,7},{7,6},{8,9},{9,8},{10,11... | collective-permute-start | bytes 196616 | tf_op jit(solution)/shard_map/ppermute | solution.py:408
  53.3 6.6 %collective-permute-start.23 = (f32[32,128]{1,0:T(8,128)S(1)}, f32[32,128]{1,0:T(8,128)S(1)}, u32[]{:S(2)}, u32[]{:S(2)}) collective-permute-start(f32[32,128]{1,0:T(8,128)S(1)} %get-tuple-element.41.refs_0_), channel_id=1, source_target_pairs={{0,14},{2,12},{4,10},{6,8},{8,6},{10,4},{12,2},{14,0},{1,9},{3,11}... | collective-permute-start | bytes 49160 | tf_op jit(solution)/shard_map/ppermute | solution.py:426
  55.5 4.6 %collective-permute-start.24 = (f32[32,128]{1,0:T(8,128)S(1)}, f32[32,128]{1,0:T(8,128)S(1)}, u32[]{:S(2)}, u32[]{:S(2)}) collective-permute-start(f32[32,128]{1,0:T(8,128)S(1)} %get-tuple-element.41.refs_0_), channel_id=1, source_target_pairs={{0,6},{2,4},{4,2},{6,0},{8,14},{10,12},{12,10},{14,8},{1,11},{3,9}... | collective-permute-start | bytes 49160 | tf_op jit(solution)/shard_map/ppermute | solution.py:426
  55.5 4.9 %collective-permute-start.25 = (f32[32,128]{1,0:T(8,128)S(1)}, f32[32,128]{1,0:T(8,128)S(1)}, u32[]{:S(2)}, u32[]{:S(2)}) collective-permute-start(f32[32,128]{1,0:T(8,128)S(1)} %get-tuple-element.41.refs_0_), channel_id=1, source_target_pairs={{0,4},{2,6},{4,0},{6,2},{8,12},{10,14},{12,8},{14,10},{1,13},{3,15... | collective-permute-start | bytes 49160 | tf_op jit(solution)/shard_map/ppermute | solution.py:426
  58.2 3.7 %collective-permute-start.26 = (f32[32,128]{1,0:T(8,128)S(1)}, f32[32,128]{1,0:T(8,128)S(1)}, u32[]{:S(2)}, u32[]{:S(2)}) collective-permute-start(f32[32,128]{1,0:T(8,128)S(1)} %get-tuple-element.41.refs_0_), channel_id=1, source_target_pairs={{0,2},{2,0},{4,6},{6,4},{8,10},{10,8},{12,14},{14,12},{1,3},{3,1},... | collective-permute-start | bytes 49160 | tf_op jit(solution)/shard_map/ppermute | solution.py:426
  60.0 2.0 %collective-permute-start.27 = (f32[32,128]{1,0:T(8,128)S(1)}, f32[32,128]{1,0:T(8,128)S(1)}, u32[]{:S(2)}, u32[]{:S(2)}) collective-permute-start(f32[32,128]{1,0:T(8,128)S(1)} %collective-permute-done.23.refs_1_), channel_id=1, source_target_pairs={{0,1},{1,0},{2,3},{3,2},{4,5},{5,4},{6,7},{7,6},{8,9},{9,8},{10,11... | collective-permute-start | bytes 49160 | tf_op jit(solution)/shard_map/ppermute | solution.py:408
  60.2 1.8 %collective-permute-start.28 = (f32[32,128]{1,0:T(8,128)S(1)}, f32[32,128]{1,0:T(8,128)S(1)}, u32[]{:S(2)}, u32[]{:S(2)}) collective-permute-start(f32[32,128]{1,0:T(8,128)S(1)} %collective-permute-done.24.refs_2_), channel_id=1, source_target_pairs={{0,1},{1,0},{2,3},{3,2},{4,5},{5,4},{6,7},{7,6},{8,9},{9,8},{10,11... | collective-permute-start | bytes 49160 | tf_op jit(solution)/shard_map/ppermute | solution.py:408
  60.5 1.5 %collective-permute-start.29 = (f32[32,128]{1,0:T(8,128)S(1)}, f32[32,128]{1,0:T(8,128)S(1)}, u32[]{:S(2)}, u32[]{:S(2)}) collective-permute-start(f32[32,128]{1,0:T(8,128)S(1)} %collective-permute-done.25.refs_3_), channel_id=1, source_target_pairs={{0,1},{1,0},{2,3},{3,2},{4,5},{5,4},{6,7},{7,6},{8,9},{9,8},{10,11... | collective-permute-start | bytes 49160 | tf_op jit(solution)/shard_map/ppermute | solution.py:408

commit v9 on v8

--- a/solution.py
+++ b/solution.py
@@ -39,18 +39,15 @@
 
 
 def stack(left):
-    high, middle, low = split(left)
-    return jnp.concatenate([high, high, middle, high, middle, low], axis=0)
+    high, middle, low = [part.astype(F32) for part in split(left)]
+    parts = jnp.concatenate([high, high, middle, high, middle, low], axis=0)
+    return parts.T.astype(BF16)
 
 
 def times(stacked, right):
     high, middle, low = split(right)
-    return lax.dot_general(
-        stacked,
-        jnp.concatenate([high, middle, high, low, middle, high], axis=0),
-        (((0,), (0,)), ((), ())),
-        preferred_element_type=F32,
-    )
+    parts = jnp.concatenate([high, middle, high, low, middle, high], axis=0)
+    return jnp.dot(stacked, parts, preferred_element_type=F32)
 
 
 def gram_parts(left, right):
@@ -240,23 +237,16 @@
 
 
 def join_kernel(*refs):
-    for k, ref in enumerate(refs[:-2]):
+    for k, ref in enumerate(reversed(refs[:-2])):
         refs[-1][k] = ref[...]
 
 
 def apply_dense(directions, matrix):
-    width = directions[0].shape[1]
-    total = None
-    for k, direction in enumerate(directions):
-        rounded = direction.astype(BF16)
-        for part in range(2):
-            term = jnp.dot(
-                rounded,
-                matrix[part, k * width : (k + 1) * width, :],
-                preferred_element_type=F32,
-            )
-            total = term if total is None else total + term
-    return total
+    rounded = jnp.concatenate([direction.astype(BF16) for direction in directions], axis=1)
+    high, low = [
+        jnp.dot(rounded, matrix[part], preferred_element_type=F32) for part in range(2)
+    ]
+    return high + low
 
 
 def first_kernel(even_ref, odd_ref, matrix, out_ref, blocks_ref):
@@ -298,9 +288,10 @@
         for place, half in ((core, near), (1 - core, far)):
             at = pl.multiple_of((place * parts + i) * size, size)
             out_ref[pl.ds(at, size)] = half[:, lanes]
-    out_ref[2 * parts * size :] = symmetric_parts(near, near_ref[0]) + symmetric_parts(
+    products = symmetric_parts(near, near_ref[0]) + symmetric_parts(
         far, far_ref[far_ref.shape[0] - 1]
     )
+    out_ref[2 * parts * size :] = pack(finish(products))
 
 
 def inverse_kernel(norm_ref, out_ref):
@@ -341,7 +332,7 @@
 
     behind = slice(2 * parts * size, None)
     products = add_up([pick(images, pair, core, behind) for pair in places])
-    alpha = stack(solve_wide(norm_ref[...], finish(products, 1))[:, :size])
+    alpha = stack(solve_wide(norm_ref[...], unpack(products, size, 1))[:, :size])
     residuals = [
         [residual_ref[side, k] - times(alpha, image(k, half)) for k in range(pieces)]
         for side, half in enumerate((core, 1 - core))
@@ -372,9 +363,8 @@
 def last_image_kernel(mine_ref, other_ref, direction_ref, near_ref, gram_ref):
     near, far = add_halves(mine_ref, other_ref, direction_ref.shape[2])
     near_ref[...] = near
-    gram_ref[...] = symmetric_parts(near, direction_ref[0]) + symmetric_parts(
-        far, direction_ref[1]
-    )
+    products = symmetric_parts(near, direction_ref[0]) + symmetric_parts(far, direction_ref[1])
+    gram_ref[...] = pack(finish(products))
 
 
 def last_kernel(places, *refs):
@@ -384,7 +374,7 @@
     core = lax.axis_index("col")
     size = image_ref.shape[0]
     products = add_up([pick(refs, pair, core, slice(None)) for pair in places])
-    alpha = stack(solve_wide(norm_ref[...], finish(products, 1))[:, :size])
+    alpha = stack(solve_wide(norm_ref[...], unpack(products, size, 1))[:, :size])
     new_solution[...] = solution_ref[...] + times(alpha, direction_ref[0])
     new_residual[...] = residual_ref[...] - times(alpha, image_ref[...])
 
@@ -469,7 +459,7 @@
         out_specs=VMEM,
         compiler_params=params(joined, joined),
         name="join",
-    )(*even, blocks_sum)
+    )(*reversed(even), blocks_sum)
     odd = swap(even, 1)
     dense, _ = pl.pallas_call(
         functools.partial(dense_kernel, rows_dev),
@@ -487,7 +477,8 @@
     state = shape(pieces + 1, sketch, rows_dev)
     small = shape(sketch, LANES)
     piece = shape(sketch, rows_dev)
-    payload = shape(sketch * (2 * (rows_dev // LANES) + 1), LANES)
+    packed = shape(sketch * sketch // LANES, LANES)
+    payload = shape(2 * sketch * (rows_dev // LANES) + packed.shape[0], LANES)
 
     partial_sum, blocks = pl.pallas_call(
         first_kernel,
@@ -550,7 +541,7 @@
         )(*found, direction, residual, norm, inverse, dense, *given)
     near, gram = pl.pallas_call(
         last_image_kernel,
-        out_shape=(piece, small),
+        out_shape=(piece, packed),
         in_specs=[VMEM] * 3,
         out_specs=(VMEM, VMEM),
         compiler_params=params(state),

time: 63.7 us -> 62.3 us (0.978)
  waiting for transfers between devices: 18.3 us -> 13.2 us
  starting transfers between devices: 27.2 us -> 30.2 us
    ppermute x12, waiting for transfers between devices: 11.5 us -> 8.14 us  [exchange(): fetched.append(lax.ppermute(value, ('row', 'col'), pairs))]
    ppermute x12, starting transfers between devices: 17.1 us -> 19.9 us  [exchange(): fetched.append(lax.ppermute(value, ('row', 'col'), pairs))]
    ppermute x4, waiting for transfers between devices: 3.72 us -> 2.17 us  [swap(): return lax.ppermute(value, 'row', [(i, i ^ mask) for i in range(pieces)])]
  transfers between devices with their start and end apart: 30 -> 30, of which waited for: 14 -> 10; matrix products, arithmetic and copies ran while one was open for 0% -> 0% of each run, Pallas kernels for 10% -> 11%
where the time goes in v9:
time: 62.3 us; the launch traced here: 62.1 us
  starting transfers between devices  30.2 us (48%)
  Pallas kernels  16.4 us (26%)
  waiting for transfers between devices  13.2 us (21%)
  between operations  1.44 us (2%)
  other arithmetic  0.85 us (1%)
    ppermute x12, starting transfers between devices, exchange(): fetched.append(lax.ppermute(value, ('row', 'col'), pairs))  19.9 us
    ppermute x12, waiting for transfers between devices, exchange(): fetched.append(lax.ppermute(value, ('row', 'col'), pairs))  8.14 us
    ppermute x4, starting transfers between devices, swap(): return lax.ppermute(value, 'row', [(i, i ^ mask) for i in range(pieces)])  7.28 us
    pallas_call x2, Pallas kernels, per_device(): pl.pallas_call(functools.partial(step_kernel, places, not first, last), o...  6.11 us
    ppermute x14, starting transfers between devices, across(): lax.ppermute(value, 'col', [(i, (i + 1) % col_devices) for i in range(col...  2.97 us
    ppermute x14, waiting for transfers between devices, across(): lax.ppermute(value, 'col', [(i, (i + 1) % col_devices) for i in range(col...  2.91 us
    pallas_call x1, Pallas kernels, per_device(): pl.pallas_call(functools.partial(gather_kernel, rows_dev), out_shape=(tot...  2.54 us
    pallas_call x1, Pallas kernels, per_device(): pl.pallas_call(functools.partial(dense_kernel, rows_dev), out_shape=(matr...  2.23 us
  transfers between devices with their start and end apart: 30, of which 10 were waited for; matrix products, arithmetic and copies ran while one was open for 0% of the time, Pallas kernels for 11%

profile of v9, /device:TPU:0, one launch (start us, length us, event | category | flops | bytes accessed | tf_op | source)
XLA Modules:
  0.0 62.1 jit_solution(8428894950196529040)
XLA Ops:
  0.6 0.8 %multiply_multiply_fusion.refs_3_ = f32[32,256]{1,0:T(8,128)S(1)} fusion(s32[32,256]{1,0:T(8,128)} %param.11, f32[32]{0:T(128)} %param.13, f32[256]{0:T(256)} %param.12), kind=kLoop, calls=%fused_computation | loop fusion | flops 24576 | bytes 66688 | tf_op jit(solution)/shard_map/mul | solution.py:425
  1.5 5.1 %collective-permute-start = (f32[32,256]{1,0:T(8,128)S(1)}, f32[32,256]{1,0:T(8,128)S(1)}, u32[]{:S(2)}, u32[]{:S(2)}) collective-permute-start(f32[32,256]{1,0:T(8,128)S(1)} %multiply_multiply_fusion.refs_3_), channel_id=1, source_target_pairs={{0,12},{2,14},{4,8},{6,10},{8,4},{10,6},{12,0},{14,2},{1,13},{3,15... | collective-permute-start | bytes 98312 | tf_op jit(solution)/shard_map/ppermute | solution.py:395
  6.5 0.6 %collective-permute-start.2 = (f32[32,256]{1,0:T(8,128)S(1)}, f32[32,256]{1,0:T(8,128)S(1)}, u32[]{:S(2)}, u32[]{:S(2)}) collective-permute-start(f32[32,256]{1,0:T(8,128)S(1)} %multiply_multiply_fusion.refs_3_), channel_id=1, source_target_pairs={{0,4},{2,6},{4,0},{6,2},{8,12},{10,14},{12,8},{14,10},{1,5},{3,7},... | collective-permute-start | bytes 98312 | tf_op jit(solution)/shard_map/ppermute | solution.py:395
  7.8 2.5 %gather.1 = (f32[64,128,128]{2,1,0:T(8,128)S(1)}, bf16[65,128,128]{2,1,0:T(8,128)(2,1)S(1)}) custom-call(s32[1]{0:T(128)S(6)} %copy.13.count_ref, s32[130]{0:T(256)} %rows_hbm.3, s32[130]{0:T(256)} %cols_hbm.3, bf16[130,128,128]{2,1,0:T(8,128)(2,1)} %tiles_ref.1), custom_call_target="tpu_custom_call" | custom-call | flops 8519680 | bytes 8519680 | tf_op jit(solution)/shard_map/gather/pallas_call | solution.py:439
  10.4 1.0 %collective-permute-done.1.refs_1_ = f32[32,256]{1,0:T(8,128)S(1)} collective-permute-done((f32[32,256]{1,0:T(8,128)S(1)}, f32[32,256]{1,0:T(8,128)S(1)}, u32[]{:S(2)}, u32[]{:S(2)}) %collective-permute-start.1) | collective-permute-done | bytes 32800 | tf_op jit(solution)/shard_map/ppermute | solution.py:395
  11.3 0.0 collective-permute-done.2.refs_2_
  11.4 1.6 %collective-permute-start.3 = (f32[4,32,256]{2,1,0:T(8,128)S(1)}, f32[4,32,256]{2,1,0:T(8,128)S(1)}, u32[]{:S(2)}, u32[]{:S(2)}) collective-permute-start(f32[4,32,256]{2,1,0:T(8,128)S(1)} %join.1.joined_ref.even_ref.near_ref), channel_id=1, source_target_pairs={{0,2},{2,0},{4,6},{6,4},{8,10},{10,8},{12,14},{14,12},{1,3},{3,1},... | collective-permute-start | bytes 393224 | tf_op jit(solution)/shard_map/ppermute | solution.py:395
  12.9 2.2 %dense.1 = (bf16[2,2048,512]{2,1,0:T(8,128)(2,1)S(1)}, f32[64,128,128]{2,1,0:T(8,128)S(1)}) custom-call(s32[1]{0:T(128)S(6)} %copy.13.count_ref, s32[130]{0:T(256)} %rows_hbm.3, s32[130]{0:T(256)} %cols_hbm.3, bf16[65,128,128]{2,1,0:T(8,128)(2,1)S(1)} %get-tuple-element.25.rest, ...), custom_call_target="tpu_custom_call", output_to_operand_aliasing={{1}: (4, {})} | custom-call | flops 8519680 | bytes 8519680 | tf_op jit(solution)/shard_map/dense/pallas_call | solution.py:464
  15.2 1.2 %collective-permute-done.3.odd_ref = f32[4,32,256]{2,1,0:T(8,128)S(1)} collective-permute-done((f32[4,32,256]{2,1,0:T(8,128)S(1)}, f32[4,32,256]{2,1,0:T(8,128)S(1)}, u32[]{:S(2)}, u32[]{:S(2)}) %collective-permute-start.3) | collective-permute-done | bytes 131104 | tf_op jit(solution)/shard_map/ppermute | solution.py:395
  16.4 0.9 %first.1 = (f32[32,640]{1,0:T(8,128)S(1)}, f32[8,32,256]{2,1,0:T(8,128)S(1)}) custom-call(f32[4,32,256]{2,1,0:T(8,128)S(1)} %join.1.joined_ref.even_ref.near_ref, f32[4,32,256]{2,1,0:T(8,128)S(1)} %collective-permute-done.3.odd_ref, bf16[2,2048,512]{2,1,0:T(8,128)(2,1)S(1)} %get-tuple-element.26.matrix.refs_12_), custom_call_target="tpu_custom_call" | custom-call | tf_op jit(solution)/shard_map/first/pallas_call | solution.py:483
  17.3 0.0 collective-permute-start.4
  17.3 0.5 collective-permute-start.5
  17.8 0.9 %collective-permute-done.5 = f32[32,256]{1,0:T(8,128)S(1)} collective-permute-done((f32[32,256]{1,0:T(8,128)S(1)}, f32[32,256]{1,0:T(8,128)S(1)}, u32[]{:S(2)}, u32[]{:S(2)}) %collective-permute-start.5) | collective-permute-done | bytes 32800 | tf_op jit(solution)/shard_map/ppermute | solution.py:398
  18.7 0.0 collective-permute-done.4.other_ref
  18.7 0.3 image.2
  19.0 0.4 collective-permute-start.13
  19.4 3.8 %collective-permute-start.6 = (f32[136,128]{1,0:T(8,128)S(1)}, f32[136,128]{1,0:T(8,128)S(1)}, u32[]{:S(2)}, u32[]{:S(2)}) collective-permute-start(f32[136,128]{1,0:T(8,128)S(1)} %get-tuple-element.29.refs_0_), channel_id=1, source_target_pairs={{0,14},{2,12},{4,10},{6,8},{8,6},{10,4},{12,2},{14,0},{1,9},{3,11}... | collective-permute-start | bytes 208904 | tf_op jit(solution)/shard_map/ppermute | solution.py:416
  23.2 0.6 %collective-permute-start.7 = (f32[136,128]{1,0:T(8,128)S(1)}, f32[136,128]{1,0:T(8,128)S(1)}, u32[]{:S(2)}, u32[]{:S(2)}) collective-permute-start(f32[136,128]{1,0:T(8,128)S(1)} %get-tuple-element.29.refs_0_), channel_id=1, source_target_pairs={{0,6},{2,4},{4,2},{6,0},{8,14},{10,12},{12,10},{14,8},{1,11},{3,9}... | collective-permute-start | bytes 208904 | tf_op jit(solution)/shard_map/ppermute | solution.py:416
  23.9 1.1 %collective-permute-start.8 = (f32[136,128]{1,0:T(8,128)S(1)}, f32[136,128]{1,0:T(8,128)S(1)}, u32[]{:S(2)}, u32[]{:S(2)}) collective-permute-start(f32[136,128]{1,0:T(8,128)S(1)} %get-tuple-element.29.refs_0_), channel_id=1, source_target_pairs={{0,4},{2,6},{4,0},{6,2},{8,12},{10,14},{12,8},{14,10},{1,13},{3,15... | collective-permute-start | bytes 208904 | tf_op jit(solution)/shard_map/ppermute | solution.py:416
  25.0 1.7 %collective-permute-start.9 = (f32[136,128]{1,0:T(8,128)S(1)}, f32[136,128]{1,0:T(8,128)S(1)}, u32[]{:S(2)}, u32[]{:S(2)}) collective-permute-start(f32[136,128]{1,0:T(8,128)S(1)} %get-tuple-element.29.refs_0_), channel_id=1, source_target_pairs={{0,2},{2,0},{4,6},{6,4},{8,10},{10,8},{12,14},{14,12},{1,3},{3,1},... | collective-permute-start | bytes 208904 | tf_op jit(solution)/shard_map/ppermute | solution.py:416
  26.7 0.0 collective-permute-done.6.refs_1_
  26.7 0.0 collective-permute-start.10
  26.7 3.2 %collective-permute-done.7.refs_2_ = f32[136,128]{1,0:T(8,128)S(1)} collective-permute-done((f32[136,128]{1,0:T(8,128)S(1)}, f32[136,128]{1,0:T(8,128)S(1)}, u32[]{:S(2)}, u32[]{:S(2)}) %collective-permute-start.7) | collective-permute-done | bytes 69664 | tf_op jit(solution)/shard_map/ppermute | solution.py:416
  29.9 0.0 collective-permute-start.11
  29.9 0.0 collective-permute-done.8.refs_3_
  29.9 0.5 collective-permute-start.12
  30.5 0.9 %inverse.2.refs_11_ = f32[32,128]{1,0:T(8,128)S(1)} custom-call(f32[32,128]{1,0:T(8,128)S(1)} %get-tuple-element.33.norm_ref.refs_10_), custom_call_target="tpu_custom_call" | custom-call | tf_op jit(solution)/shard_map/inverse/pallas_call | solution.py:519
  31.4 0.1 collect.1
  31.5 0.0 collective-permute-done.10.refs_5_
  31.5 0.0 collective-permute-done.11.refs_6_
  31.5 3.1 %step.2 = (f32[32,512]{1,0:T(8,128)S(1)}, f32[9,32,256]{2,1,0:T(8,128)S(1)}, f32[2,8,32,256]{3,2,1,0:T(8,128)S(1)}, f32[32,128]{1,0:T(8,128)S(1)}, f32[32,256]{1,0:T(8,128)S(1)}) custom-call(f32[136,128]{1,0:T(8,128)S(1)} %get-tuple-element.29.refs_0_, f32[136,128]{1,0:T(8,128)S(1)} %collective-permute-done.6.refs_1_, ...), custom_call_target="tpu_custom_call" | custom-call | tf_op jit(solution)/shard_map/step/pallas_call | solution.py:528
  34.6 0.2 collective-permute-start.14
  34.8 1.0 %collective-permute-done.14.other_ref = f32[32,512]{1,0:T(8,128)S(1)} collective-permute-done((f32[32,512]{1,0:T(8,128)S(1)}, f32[32,512]{1,0:T(8,128)S(1)}, u32[]{:S(2)}, u32[]{:S(2)}) %collective-permute-start.14) | collective-permute-done | bytes 65568 | tf_op jit(solution)/shard_map/ppermute | solution.py:398
  35.8 0.3 image.3.refs_0_
  36.2 2.5 %collective-permute-start.15 = (f32[136,128]{1,0:T(8,128)S(1)}, f32[136,128]{1,0:T(8,128)S(1)}, u32[]{:S(2)}, u32[]{:S(2)}) collective-permute-start(f32[136,128]{1,0:T(8,128)S(1)} %image.3.refs_0_), channel_id=1, source_target_pairs={{0,14},{2,12},{4,10},{6,8},{8,6},{10,4},{12,2},{14,0},{1,9},{3,11}... | collective-permute-start | bytes 208904 | tf_op jit(solution)/shard_map/ppermute | solution.py:416
  38.7 0.0 collective-permute-start.16
  38.7 2.2 %collective-permute-start.17 = (f32[136,128]{1,0:T(8,128)S(1)}, f32[136,128]{1,0:T(8,128)S(1)}, u32[]{:S(2)}, u32[]{:S(2)}) collective-permute-start(f32[136,128]{1,0:T(8,128)S(1)} %image.3.refs_0_), channel_id=1, source_target_pairs={{0,4},{2,6},{4,0},{6,2},{8,12},{10,14},{12,8},{14,10},{1,13},{3,15... | collective-permute-start | bytes 208904 | tf_op jit(solution)/shard_map/ppermute | solution.py:416
  40.9 1.3 %collective-permute-start.18 = (f32[136,128]{1,0:T(8,128)S(1)}, f32[136,128]{1,0:T(8,128)S(1)}, u32[]{:S(2)}, u32[]{:S(2)}) collective-permute-start(f32[136,128]{1,0:T(8,128)S(1)} %image.3.refs_0_), channel_id=1, source_target_pairs={{0,2},{2,0},{4,6},{6,4},{8,10},{10,8},{12,14},{14,12},{1,3},{3,1},... | collective-permute-start | bytes 208904 | tf_op jit(solution)/shard_map/ppermute | solution.py:416
  42.2 1.9 %collective-permute-done.15.refs_1_ = f32[136,128]{1,0:T(8,128)S(1)} collective-permute-done((f32[136,128]{1,0:T(8,128)S(1)}, f32[136,128]{1,0:T(8,128)S(1)}, u32[]{:S(2)}, u32[]{:S(2)}) %collective-permute-start.15) | collective-permute-done | bytes 69664 | tf_op jit(solution)/shard_map/ppermute | solution.py:416
  44.1 0.0 collective-permute-start.19
  44.1 0.9 %collective-permute-done.16.refs_2_ = f32[136,128]{1,0:T(8,128)S(1)} collective-permute-done((f32[136,128]{1,0:T(8,128)S(1)}, f32[136,128]{1,0:T(8,128)S(1)}, u32[]{:S(2)}, u32[]{:S(2)}) %collective-permute-start.16) | collective-permute-done | bytes 69664 | tf_op jit(solution)/shard_map/ppermute | solution.py:416
  45.0 0.5 collective-permute-start.21
  45.5 0.9 %inverse.3.refs_11_ = f32[32,128]{1,0:T(8,128)S(1)} custom-call(f32[32,128]{1,0:T(8,128)S(1)} %get-tuple-element.37.norm_ref.refs_10_), custom_call_target="tpu_custom_call" | custom-call | tf_op jit(solution)/shard_map/inverse/pallas_call | solution.py:519
  46.4 0.0 collective-permute-done.18.refs_4_
  46.4 0.0 collective-permute-done.19.refs_5_
  46.5 0.0 collective-permute-done.21.refs_7_
  46.5 3.1 %step.3 = (f32[32,512]{1,0:T(8,128)S(1)}, f32[2,32,256]{2,1,0:T(8,128)S(1)}, f32[32,256]{1,0:T(8,128)S(1)}, f32[32,128]{1,0:T(8,128)S(1)}, f32[32,256]{1,0:T(8,128)S(1)}) custom-call(f32[136,128]{1,0:T(8,128)S(1)} %image.3.refs_0_, f32[136,128]{1,0:T(8,128)S(1)} %collective-permute-done.15.refs_1_, f32[136,128]{1,0:T(8,128)S(1)} %collective-permute-done.16.refs_2_, ...), custom_call_target="tpu_custom_call" | custom-call | tf_op jit(solution)/shard_map/step/pallas_call | solution.py:528
  49.5 0.3 collective-permute-start.22
  49.8 1.0 %collective-permute-done.22.other_ref = f32[32,512]{1,0:T(8,128)S(1)} collective-permute-done((f32[32,512]{1,0:T(8,128)S(1)}, f32[32,512]{1,0:T(8,128)S(1)}, u32[]{:S(2)}, u32[]{:S(2)}) %collective-permute-start.22) | collective-permute-done | bytes 65568 | tf_op jit(solution)/shard_map/ppermute | solution.py:398
  50.8 0.3 last_image.1
  51.1 3.2 %collective-permute-start.23 = (f32[8,128]{1,0:T(8,128)S(1)}, f32[8,128]{1,0:T(8,128)S(1)}, u32[]{:S(2)}, u32[]{:S(2)}) collective-permute-start(f32[8,128]{1,0:T(8,128)S(1)} %get-tuple-element.41.refs_0_), channel_id=1, source_target_pairs={{0,14},{2,12},{4,10},{6,8},{8,6},{10,4},{12,2},{14,0},{1,9},{3,11}... | collective-permute-start | bytes 12296 | tf_op jit(solution)/shard_map/ppermute | solution.py:416
  54.3 0.0 collective-permute-start.24
  54.3 2.5 %collective-permute-start.25 = (f32[8,128]{1,0:T(8,128)S(1)}, f32[8,128]{1,0:T(8,128)S(1)}, u32[]{:S(2)}, u32[]{:S(2)}) collective-permute-start(f32[8,128]{1,0:T(8,128)S(1)} %get-tuple-element.41.refs_0_), channel_id=1, source_target_pairs={{0,4},{2,6},{4,0},{6,2},{8,12},{10,14},{12,8},{14,10},{1,13},{3,15... | collective-permute-start | bytes 12296 | tf_op jit(solution)/shard_map/ppermute | solution.py:416
  56.8 1.0 %collective-permute-start.26 = (f32[8,128]{1,0:T(8,128)S(1)}, f32[8,128]{1,0:T(8,128)S(1)}, u32[]{:S(2)}, u32[]{:S(2)}) collective-permute-start(f32[8,128]{1,0:T(8,128)S(1)} %get-tuple-element.41.refs_0_), channel_id=1, source_target_pairs={{0,2},{2,0},{4,6},{6,4},{8,10},{10,8},{12,14},{14,12},{1,3},{3,1},... | collective-permute-start | bytes 12296 | tf_op jit(solution)/shard_map/ppermute | solution.py:416
  57.8 0.0 collective-permute-done.23.refs_1_
  57.8 0.0 collective-permute-start.27
  57.8 1.0 %collective-permute-done.24.refs_2_ = f32[8,128]{1,0:T(8,128)S(1)} collective-permute-done((f32[8,128]{1,0:T(8,128)S(1)}, f32[8,128]{1,0:T(8,128)S(1)}, u32[]{:S(2)}, u32[]{:S(2)}) %collective-permute-start.24) | collective-permute-done | bytes 4128 | tf_op jit(solution)/shard_map/ppermute | solution.py:416
  58.8 0.0 collective-permute-done.25.refs_3_
  58.8 0.5 collective-permute-start.29
  59.3 1.1 %collective-permute-done.26.refs_4_ = f32[8,128]{1,0:T(8,128)S(1)} collective-permute-done((f32[8,128]{1,0:T(8,128)S(1)}, f32[8,128]{1,0:T(8,128)S(1)}, u32[]{:S(2)}, u32[]{:S(2)}) %collective-permute-start.26) | collective-permute-done | bytes 4128 | tf_op jit(solution)/shard_map/ppermute | solution.py:416
  60.4 0.0 collective-permute-done.27.refs_5_
  60.4 0.0 collective-permute-done.28.refs_6_
  60.4 0.0 collective-permute-done.29.refs_7_
  60.4 1.7 %last.1 = (f32[32,256]{1,0:T(8,128)}, f32[32,256]{1,0:T(8,128)}) custom-call(f32[8,128]{1,0:T(8,128)S(1)} %get-tuple-element.41.refs_0_, f32[8,128]{1,0:T(8,128)S(1)} %collective-permute-done.23.refs_1_, f32[8,128]{1,0:T(8,128)S(1)} %collective-permute-done.24.refs_2_, f32[8,128]{1,0:T(8,128)S(1)} %collective-permute-done.25.refs_3_, ...), custom_call_target="tpu_custom_call" | custom-call | tf_op jit(solution)/shard_map/last/pallas_call | solution.py:551
  (10 shorter events, 0.0 us)
Async XLA Ops:
  1.5 8.9 %collective-permute-start = (f32[32,256]{1,0:T(8,128)S(1)}, f32[32,256]{1,0:T(8,128)S(1)}, u32[]{:S(2)}, u32[]{:S(2)}) collective-permute-start(f32[32,256]{1,0:T(8,128)S(1)} %multiply_multiply_fusion.refs_3_), channel_id=1, source_target_pairs={{0,12},{2,14},{4,8},{6,10},{8,4},{10,6},{12,0},{14,2},{1,13},{3,15... | collective-permute-start | bytes 98312 | tf_op jit(solution)/shard_map/ppermute | solution.py:395
  6.5 4.8 %collective-permute-start.1 = (f32[32,256]{1,0:T(8,128)S(1)}, f32[32,256]{1,0:T(8,128)S(1)}, u32[]{:S(2)}, u32[]{:S(2)}) collective-permute-start(f32[32,256]{1,0:T(8,128)S(1)} %multiply_multiply_fusion.refs_3_), channel_id=1, source_target_pairs={{0,8},{2,10},{4,12},{6,14},{8,0},{10,2},{12,4},{14,6},{1,9},{3,11}... | collective-permute-start | bytes 98312 | tf_op jit(solution)/shard_map/ppermute | solution.py:395
  6.5 4.8 %collective-permute-start.2 = (f32[32,256]{1,0:T(8,128)S(1)}, f32[32,256]{1,0:T(8,128)S(1)}, u32[]{:S(2)}, u32[]{:S(2)}) collective-permute-start(f32[32,256]{1,0:T(8,128)S(1)} %multiply_multiply_fusion.refs_3_), channel_id=1, source_target_pairs={{0,4},{2,6},{4,0},{6,2},{8,12},{10,14},{12,8},{14,10},{1,5},{3,7},... | collective-permute-start | bytes 98312 | tf_op jit(solution)/shard_map/ppermute | solution.py:395
  11.4 5.0 %collective-permute-start.3 = (f32[4,32,256]{2,1,0:T(8,128)S(1)}, f32[4,32,256]{2,1,0:T(8,128)S(1)}, u32[]{:S(2)}, u32[]{:S(2)}) collective-permute-start(f32[4,32,256]{2,1,0:T(8,128)S(1)} %join.1.joined_ref.even_ref.near_ref), channel_id=1, source_target_pairs={{0,2},{2,0},{4,6},{6,4},{8,10},{10,8},{12,14},{14,12},{1,3},{3,1},... | collective-permute-start | bytes 393224 | tf_op jit(solution)/shard_map/ppermute | solution.py:395
  17.3 1.4 %collective-permute-start.4 = (f32[32,640]{1,0:T(8,128)S(1)}, f32[32,640]{1,0:T(8,128)S(1)}, u32[]{:S(2)}, u32[]{:S(2)}) collective-permute-start(f32[32,640]{1,0:T(8,128)S(1)} %get-tuple-element.27.mine_ref), channel_id=1, source_target_pairs={{0,1},{1,0},{2,3},{3,2},{4,5},{5,4},{6,7},{7,6},{8,9},{9,8},{10,11... | collective-permute-start | bytes 245768 | tf_op jit(solution)/shard_map/ppermute | solution.py:398
  17.3 1.4 %collective-permute-start.5 = (f32[32,256]{1,0:T(8,128)S(1)}, f32[32,256]{1,0:T(8,128)S(1)}, u32[]{:S(2)}, u32[]{:S(2)}) collective-permute-start(f32[32,256]{1,0:T(8,128)S(1)} %multiply_multiply_fusion.refs_3_), channel_id=1, source_target_pairs={{0,1},{1,0},{2,3},{3,2},{4,5},{5,4},{6,7},{7,6},{8,9},{9,8},{10,11... | collective-permute-start | bytes 98312 | tf_op jit(solution)/shard_map/ppermute | solution.py:398
  19.0 12.3 %collective-permute-start.13 = (f32[8,32,256]{2,1,0:T(8,128)S(1)}, f32[8,32,256]{2,1,0:T(8,128)S(1)}, u32[]{:S(2)}, u32[]{:S(2)}) collective-permute-start(f32[8,32,256]{2,1,0:T(8,128)S(1)} %get-tuple-element.30.near_ref), channel_id=1, source_target_pairs={{0,1},{1,0},{2,3},{3,2},{4,5},{5,4},{6,7},{7,6},{8,9},{9,8},{10,11... | collective-permute-start | bytes 786440 | tf_op jit(solution)/shard_map/ppermute | solution.py:398
  19.4 7.3 %collective-permute-start.6 = (f32[136,128]{1,0:T(8,128)S(1)}, f32[136,128]{1,0:T(8,128)S(1)}, u32[]{:S(2)}, u32[]{:S(2)}) collective-permute-start(f32[136,128]{1,0:T(8,128)S(1)} %get-tuple-element.29.refs_0_), channel_id=1, source_target_pairs={{0,14},{2,12},{4,10},{6,8},{8,6},{10,4},{12,2},{14,0},{1,9},{3,11}... | collective-permute-start | bytes 208904 | tf_op jit(solution)/shard_map/ppermute | solution.py:416
  23.2 6.7 %collective-permute-start.7 = (f32[136,128]{1,0:T(8,128)S(1)}, f32[136,128]{1,0:T(8,128)S(1)}, u32[]{:S(2)}, u32[]{:S(2)}) collective-permute-start(f32[136,128]{1,0:T(8,128)S(1)} %get-tuple-element.29.refs_0_), channel_id=1, source_target_pairs={{0,6},{2,4},{4,2},{6,0},{8,14},{10,12},{12,10},{14,8},{1,11},{3,9}... | collective-permute-start | bytes 208904 | tf_op jit(solution)/shard_map/ppermute | solution.py:416
  23.9 6.1 %collective-permute-start.8 = (f32[136,128]{1,0:T(8,128)S(1)}, f32[136,128]{1,0:T(8,128)S(1)}, u32[]{:S(2)}, u32[]{:S(2)}) collective-permute-start(f32[136,128]{1,0:T(8,128)S(1)} %get-tuple-element.29.refs_0_), channel_id=1, source_target_pairs={{0,4},{2,6},{4,0},{6,2},{8,12},{10,14},{12,8},{14,10},{1,13},{3,15... | collective-permute-start | bytes 208904 | tf_op jit(solution)/shard_map/ppermute | solution.py:416
  25.0 6.4 %collective-permute-start.9 = (f32[136,128]{1,0:T(8,128)S(1)}, f32[136,128]{1,0:T(8,128)S(1)}, u32[]{:S(2)}, u32[]{:S(2)}) collective-permute-start(f32[136,128]{1,0:T(8,128)S(1)} %get-tuple-element.29.refs_0_), channel_id=1, source_target_pairs={{0,2},{2,0},{4,6},{6,4},{8,10},{10,8},{12,14},{14,12},{1,3},{3,1},... | collective-permute-start | bytes 208904 | tf_op jit(solution)/shard_map/ppermute | solution.py:416
  26.7 4.8 %collective-permute-start.10 = (f32[136,128]{1,0:T(8,128)S(1)}, f32[136,128]{1,0:T(8,128)S(1)}, u32[]{:S(2)}, u32[]{:S(2)}) collective-permute-start(f32[136,128]{1,0:T(8,128)S(1)} %collective-permute-done.6.refs_1_), channel_id=1, source_target_pairs={{0,1},{1,0},{2,3},{3,2},{4,5},{5,4},{6,7},{7,6},{8,9},{9,8},{10,11... | collective-permute-start | bytes 208904 | tf_op jit(solution)/shard_map/ppermute | solution.py:398
  29.9 1.5 %collective-permute-start.11 = (f32[136,128]{1,0:T(8,128)S(1)}, f32[136,128]{1,0:T(8,128)S(1)}, u32[]{:S(2)}, u32[]{:S(2)}) collective-permute-start(f32[136,128]{1,0:T(8,128)S(1)} %collective-permute-done.7.refs_2_), channel_id=1, source_target_pairs={{0,1},{1,0},{2,3},{3,2},{4,5},{5,4},{6,7},{7,6},{8,9},{9,8},{10,11... | collective-permute-start | bytes 208904 | tf_op jit(solution)/shard_map/ppermute | solution.py:398
  29.9 1.5 %collective-permute-start.12 = (f32[136,128]{1,0:T(8,128)S(1)}, f32[136,128]{1,0:T(8,128)S(1)}, u32[]{:S(2)}, u32[]{:S(2)}) collective-permute-start(f32[136,128]{1,0:T(8,128)S(1)} %collective-permute-done.8.refs_3_), channel_id=1, source_target_pairs={{0,1},{1,0},{2,3},{3,2},{4,5},{5,4},{6,7},{7,6},{8,9},{9,8},{10,11... | collective-permute-start | bytes 208904 | tf_op jit(solution)/shard_map/ppermute | solution.py:398
  34.6 1.3 %collective-permute-start.14 = (f32[32,512]{1,0:T(8,128)S(1)}, f32[32,512]{1,0:T(8,128)S(1)}, u32[]{:S(2)}, u32[]{:S(2)}) collective-permute-start(f32[32,512]{1,0:T(8,128)S(1)} %get-tuple-element.34.mine_ref), channel_id=1, source_target_pairs={{0,1},{1,0},{2,3},{3,2},{4,5},{5,4},{6,7},{7,6},{8,9},{9,8},{10,11... | collective-permute-start | bytes 196616 | tf_op jit(solution)/shard_map/ppermute | solution.py:398
  36.2 7.9 %collective-permute-start.15 = (f32[136,128]{1,0:T(8,128)S(1)}, f32[136,128]{1,0:T(8,128)S(1)}, u32[]{:S(2)}, u32[]{:S(2)}) collective-permute-start(f32[136,128]{1,0:T(8,128)S(1)} %image.3.refs_0_), channel_id=1, source_target_pairs={{0,14},{2,12},{4,10},{6,8},{8,6},{10,4},{12,2},{14,0},{1,9},{3,11}... | collective-permute-start | bytes 208904 | tf_op jit(solution)/shard_map/ppermute | solution.py:416
  38.7 6.3 %collective-permute-start.16 = (f32[136,128]{1,0:T(8,128)S(1)}, f32[136,128]{1,0:T(8,128)S(1)}, u32[]{:S(2)}, u32[]{:S(2)}) collective-permute-start(f32[136,128]{1,0:T(8,128)S(1)} %image.3.refs_0_), channel_id=1, source_target_pairs={{0,6},{2,4},{4,2},{6,0},{8,14},{10,12},{12,10},{14,8},{1,11},{3,9}... | collective-permute-start | bytes 208904 | tf_op jit(solution)/shard_map/ppermute | solution.py:416
  38.7 6.3 %collective-permute-start.17 = (f32[136,128]{1,0:T(8,128)S(1)}, f32[136,128]{1,0:T(8,128)S(1)}, u32[]{:S(2)}, u32[]{:S(2)}) collective-permute-start(f32[136,128]{1,0:T(8,128)S(1)} %image.3.refs_0_), channel_id=1, source_target_pairs={{0,4},{2,6},{4,0},{6,2},{8,12},{10,14},{12,8},{14,10},{1,13},{3,15... | collective-permute-start | bytes 208904 | tf_op jit(solution)/shard_map/ppermute | solution.py:416
  40.9 5.6 %collective-permute-start.18 = (f32[136,128]{1,0:T(8,128)S(1)}, f32[136,128]{1,0:T(8,128)S(1)}, u32[]{:S(2)}, u32[]{:S(2)}) collective-permute-start(f32[136,128]{1,0:T(8,128)S(1)} %image.3.refs_0_), channel_id=1, source_target_pairs={{0,2},{2,0},{4,6},{6,4},{8,10},{10,8},{12,14},{14,12},{1,3},{3,1},... | collective-permute-start | bytes 208904 | tf_op jit(solution)/shard_map/ppermute | solution.py:416
  44.1 2.4 %collective-permute-start.19 = (f32[136,128]{1,0:T(8,128)S(1)}, f32[136,128]{1,0:T(8,128)S(1)}, u32[]{:S(2)}, u32[]{:S(2)}) collective-permute-start(f32[136,128]{1,0:T(8,128)S(1)} %collective-permute-done.15.refs_1_), channel_id=1, source_target_pairs={{0,1},{1,0},{2,3},{3,2},{4,5},{5,4},{6,7},{7,6},{8,9},{9,8},{10,11... | collective-permute-start | bytes 208904 | tf_op jit(solution)/shard_map/ppermute | solution.py:398
  45.0 1.5 %collective-permute-start.20 = (f32[136,128]{1,0:T(8,128)S(1)}, f32[136,128]{1,0:T(8,128)S(1)}, u32[]{:S(2)}, u32[]{:S(2)}) collective-permute-start(f32[136,128]{1,0:T(8,128)S(1)} %collective-permute-done.16.refs_2_), channel_id=1, source_target_pairs={{0,1},{1,0},{2,3},{3,2},{4,5},{5,4},{6,7},{7,6},{8,9},{9,8},{10,11... | collective-permute-start | bytes 208904 | tf_op jit(solution)/shard_map/ppermute | solution.py:398
  45.0 1.5 %collective-permute-start.21 = (f32[136,128]{1,0:T(8,128)S(1)}, f32[136,128]{1,0:T(8,128)S(1)}, u32[]{:S(2)}, u32[]{:S(2)}) collective-permute-start(f32[136,128]{1,0:T(8,128)S(1)} %collective-permute-done.17.refs_3_), channel_id=1, source_target_pairs={{0,1},{1,0},{2,3},{3,2},{4,5},{5,4},{6,7},{7,6},{8,9},{9,8},{10,11... | collective-permute-start | bytes 208904 | tf_op jit(solution)/shard_map/ppermute | solution.py:398
  49.5 1.3 %collective-permute-start.22 = (f32[32,512]{1,0:T(8,128)S(1)}, f32[32,512]{1,0:T(8,128)S(1)}, u32[]{:S(2)}, u32[]{:S(2)}) collective-permute-start(f32[32,512]{1,0:T(8,128)S(1)} %get-tuple-element.39.mine_ref), channel_id=1, source_target_pairs={{0,1},{1,0},{2,3},{3,2},{4,5},{5,4},{6,7},{7,6},{8,9},{9,8},{10,11... | collective-permute-start | bytes 196616 | tf_op jit(solution)/shard_map/ppermute | solution.py:398
  51.1 6.6 %collective-permute-start.23 = (f32[8,128]{1,0:T(8,128)S(1)}, f32[8,128]{1,0:T(8,128)S(1)}, u32[]{:S(2)}, u32[]{:S(2)}) collective-permute-start(f32[8,128]{1,0:T(8,128)S(1)} %get-tuple-element.41.refs_0_), channel_id=1, source_target_pairs={{0,14},{2,12},{4,10},{6,8},{8,6},{10,4},{12,2},{14,0},{1,9},{3,11}... | collective-permute-start | bytes 12296 | tf_op jit(solution)/shard_map/ppermute | solution.py:416
  54.3 4.5 %collective-permute-start.24 = (f32[8,128]{1,0:T(8,128)S(1)}, f32[8,128]{1,0:T(8,128)S(1)}, u32[]{:S(2)}, u32[]{:S(2)}) collective-permute-start(f32[8,128]{1,0:T(8,128)S(1)} %get-tuple-element.41.refs_0_), channel_id=1, source_target_pairs={{0,6},{2,4},{4,2},{6,0},{8,14},{10,12},{12,10},{14,8},{1,11},{3,9}... | collective-permute-start | bytes 12296 | tf_op jit(solution)/shard_map/ppermute | solution.py:416
  54.3 4.5 %collective-permute-start.25 = (f32[8,128]{1,0:T(8,128)S(1)}, f32[8,128]{1,0:T(8,128)S(1)}, u32[]{:S(2)}, u32[]{:S(2)}) collective-permute-start(f32[8,128]{1,0:T(8,128)S(1)} %get-tuple-element.41.refs_0_), channel_id=1, source_target_pairs={{0,4},{2,6},{4,0},{6,2},{8,12},{10,14},{12,8},{14,10},{1,13},{3,15... | collective-permute-start | bytes 12296 | tf_op jit(solution)/shard_map/ppermute | solution.py:416
  56.8 3.6 %collective-permute-start.26 = (f32[8,128]{1,0:T(8,128)S(1)}, f32[8,128]{1,0:T(8,128)S(1)}, u32[]{:S(2)}, u32[]{:S(2)}) collective-permute-start(f32[8,128]{1,0:T(8,128)S(1)} %get-tuple-element.41.refs_0_), channel_id=1, source_target_pairs={{0,2},{2,0},{4,6},{6,4},{8,10},{10,8},{12,14},{14,12},{1,3},{3,1},... | collective-permute-start | bytes 12296 | tf_op jit(solution)/shard_map/ppermute | solution.py:416
  57.8 2.6 %collective-permute-start.27 = (f32[8,128]{1,0:T(8,128)S(1)}, f32[8,128]{1,0:T(8,128)S(1)}, u32[]{:S(2)}, u32[]{:S(2)}) collective-permute-start(f32[8,128]{1,0:T(8,128)S(1)} %collective-permute-done.23.refs_1_), channel_id=1, source_target_pairs={{0,1},{1,0},{2,3},{3,2},{4,5},{5,4},{6,7},{7,6},{8,9},{9,8},{10,11... | collective-permute-start | bytes 12296 | tf_op jit(solution)/shard_map/ppermute | solution.py:398
  58.8 1.6 %collective-permute-start.28 = (f32[8,128]{1,0:T(8,128)S(1)}, f32[8,128]{1,0:T(8,128)S(1)}, u32[]{:S(2)}, u32[]{:S(2)}) collective-permute-start(f32[8,128]{1,0:T(8,128)S(1)} %collective-permute-done.24.refs_2_), channel_id=1, source_target_pairs={{0,1},{1,0},{2,3},{3,2},{4,5},{5,4},{6,7},{7,6},{8,9},{9,8},{10,11... | collective-permute-start | bytes 12296 | tf_op jit(solution)/shard_map/ppermute | solution.py:398
  58.8 1.6 %collective-permute-start.29 = (f32[8,128]{1,0:T(8,128)S(1)}, f32[8,128]{1,0:T(8,128)S(1)}, u32[]{:S(2)}, u32[]{:S(2)}) collective-permute-start(f32[8,128]{1,0:T(8,128)S(1)} %collective-permute-done.25.refs_3_), channel_id=1, source_target_pairs={{0,1},{1,0},{2,3},{3,2},{4,5},{5,4},{6,7},{7,6},{8,9},{9,8},{10,11... | collective-permute-start | bytes 12296 | tf_op jit(solution)/shard_map/ppermute | solution.py:398

commit v10 on v9

--- a/solution.py
+++ b/solution.py
@@ -9,6 +9,7 @@
 
 ITERS = 3
 LANES = 128
+SUBLANES = 8
 PIVOTS = 8
 CHUNKS = 5
 F32 = jnp.float32
@@ -98,24 +99,34 @@
 
 def solve_wide(target, matrix):
     size = matrix.shape[0]
-    row_ids = lax.broadcasted_iota(jnp.int32, (size, LANES), 0)
+    groups = (size // SUBLANES, SUBLANES, LANES)
+    row_ids = (
+        lax.broadcasted_iota(jnp.int32, groups, 0) * SUBLANES
+        + lax.broadcasted_iota(jnp.int32, groups, 1)
+    )
     lane_ids = lax.broadcasted_iota(jnp.int32, (size, LANES), 1)
-    work = jnp.where(lane_ids < size, target, matrix)
-    for base in range(0, size, PIVOTS):
+    work = jnp.where(lane_ids < size, target, matrix).reshape(groups)
+    scale = jnp.zeros(groups, F32)
+
+    def spread(value, row):
+        at = row % SUBLANES
+        return jnp.broadcast_to(value[row // SUBLANES, at : at + 1], (SUBLANES, LANES))
+
+    for base in range(size, 2 * size, PIVOTS):
         columns = [
-            jnp.broadcast_to(work[:, size + base + i : size + base + i + 1], (size, LANES))
-            for i in range(PIVOTS)
+            jnp.broadcast_to(work[:, :, base + i : base + i + 1], groups) for i in range(PIVOTS)
         ]
         for i in range(PIVOTS):
-            pivot = base + i
+            pivot = base - size + i
             here = row_ids == pivot
-            inverse = 1.0 / columns[i][pivot : pivot + 1, :]
-            row = work[pivot : pivot + 1, :] * inverse
-            work = jnp.where(here, row, work - columns[i] * row)
+            inverse = pltpu.reciprocal(spread(columns[i], pivot), full_range=False)
+            factors = jnp.where(here, 0.0, columns[i])
+            work = work - factors * (spread(work, pivot) * inverse)[None]
+            scale = jnp.where(here, inverse[None], scale)
             for later in range(i + 1, PIVOTS):
-                entry = columns[later][pivot : pivot + 1, :] * inverse
-                columns[later] = jnp.where(here, entry, columns[later] - columns[i] * entry)
-    return work
+                entry = spread(columns[later], pivot) * inverse
+                columns[later] = columns[later] - factors * entry[None]
+    return (work * scale).reshape(size, LANES)
 
 
 def add_up(values):
@@ -403,7 +414,7 @@
         if pieces != 8:
             found = [value] + [swap(value, k) for k in range(1, pieces)]
             return found, [(k, k) for k in range(pieces)]
-        shares = ((7, 4), (3, 5), (2, 6), (1, 1))
+        shares = ((7, 5), (3, 6), (2, 4), (1, 1))
         fetched = []
         passed = []
         places = {0: (0, 0)}

time: 62.3 us -> 62.3 us (level)
  Pallas kernels: 16.4 us -> 17.7 us
  waiting for transfers between devices: 13.2 us -> 11.9 us
    ppermute x4, waiting for transfers between devices: 2.17 us -> 1.29 us  [swap(): return lax.ppermute(value, 'row', [(i, i ^ mask) for i in range(pieces)])]
    pallas_call x1, Pallas kernels: 2.23 us -> 3.02 us  [per_device(): pl.pallas_call(functools.partial(dense_kernel, rows_dev), out_shape=(matr...]
  transfers between devices with their start and end apart: 30 -> 30, of which waited for: 10 -> 14; matrix products, arithmetic and copies ran while one was open for 0% -> 0% of each run, Pallas kernels for 11% -> 13%
where the time goes in v10:
time: 62.3 us; the launch traced here: 62.1 us
  starting transfers between devices  30.2 us (48%)
  Pallas kernels  17.7 us (28%)
  waiting for transfers between devices  11.9 us (19%)
  between operations  1.43 us (2%)
  other arithmetic  0.85 us (1%)
    ppermute x12, starting transfers between devices, exchange(): fetched.append(lax.ppermute(value, ('row', 'col'), pairs))  19.7 us
    ppermute x12, waiting for transfers between devices, exchange(): fetched.append(lax.ppermute(value, ('row', 'col'), pairs))  7.75 us
    ppermute x4, starting transfers between devices, swap(): return lax.ppermute(value, 'row', [(i, i ^ mask) for i in range(pieces)])  7.28 us
    pallas_call x2, Pallas kernels, per_device(): pl.pallas_call(functools.partial(step_kernel, places, not first, last), o...  6.24 us
    ppermute x14, starting transfers between devices, across(): lax.ppermute(value, 'col', [(i, (i + 1) % col_devices) for i in range(col...  3.17 us
    pallas_call x1, Pallas kernels, per_device(): pl.pallas_call(functools.partial(dense_kernel, rows_dev), out_shape=(matr...  3.02 us
    ppermute x14, waiting for transfers between devices, across(): lax.ppermute(value, 'col', [(i, (i + 1) % col_devices) for i in range(col...  2.88 us
    pallas_call x1, Pallas kernels, per_device(): pl.pallas_call(functools.partial(gather_kernel, rows_dev), out_shape=(tot...  2.64 us
  transfers between devices with their start and end apart: 30, of which 14 were waited for; matrix products, arithmetic and copies ran while one was open for 0% of the time, Pallas kernels for 13%

profile of v10, /device:TPU:0, one launch (start us, length us, event | category | flops | bytes accessed | tf_op | source)
XLA Modules:
  0.0 62.1 jit_solution(299926173842922789)
XLA Ops:
  0.6 0.8 %multiply_multiply_fusion.refs_3_ = f32[32,256]{1,0:T(8,128)S(1)} fusion(s32[32,256]{1,0:T(8,128)} %param.11, f32[32]{0:T(128)} %param.13, f32[256]{0:T(256)} %param.12), kind=kLoop, calls=%fused_computation | loop fusion | flops 24576 | bytes 66688 | tf_op jit(solution)/shard_map/mul | solution.py:436
  1.5 5.1 %collective-permute-start = (f32[32,256]{1,0:T(8,128)S(1)}, f32[32,256]{1,0:T(8,128)S(1)}, u32[]{:S(2)}, u32[]{:S(2)}) collective-permute-start(f32[32,256]{1,0:T(8,128)S(1)} %multiply_multiply_fusion.refs_3_), channel_id=1, source_target_pairs={{0,12},{2,14},{4,8},{6,10},{8,4},{10,6},{12,0},{14,2},{1,13},{3,15... | collective-permute-start | bytes 98312 | tf_op jit(solution)/shard_map/ppermute | solution.py:406
  6.5 0.0 collective-permute-start.1
  6.5 0.6 %collective-permute-start.2 = (f32[32,256]{1,0:T(8,128)S(1)}, f32[32,256]{1,0:T(8,128)S(1)}, u32[]{:S(2)}, u32[]{:S(2)}) collective-permute-start(f32[32,256]{1,0:T(8,128)S(1)} %multiply_multiply_fusion.refs_3_), channel_id=1, source_target_pairs={{0,4},{2,6},{4,0},{6,2},{8,12},{10,14},{12,8},{14,10},{1,5},{3,7},... | collective-permute-start | bytes 98312 | tf_op jit(solution)/shard_map/ppermute | solution.py:406
  7.8 2.6 %gather.1 = (f32[64,128,128]{2,1,0:T(8,128)S(1)}, bf16[65,128,128]{2,1,0:T(8,128)(2,1)S(1)}) custom-call(s32[1]{0:T(128)S(6)} %copy.13.count_ref, s32[130]{0:T(256)} %rows_hbm.3, s32[130]{0:T(256)} %cols_hbm.3, bf16[130,128,128]{2,1,0:T(8,128)(2,1)} %tiles_ref.1), custom_call_target="tpu_custom_call" | custom-call | flops 8519680 | bytes 8519680 | tf_op jit(solution)/shard_map/gather/pallas_call | solution.py:450
  10.5 0.0 collective-permute-done.refs_0_
  10.5 0.9 %collective-permute-done.1.refs_1_ = f32[32,256]{1,0:T(8,128)S(1)} collective-permute-done((f32[32,256]{1,0:T(8,128)S(1)}, f32[32,256]{1,0:T(8,128)S(1)}, u32[]{:S(2)}, u32[]{:S(2)}) %collective-permute-start.1) | collective-permute-done | bytes 32800 | tf_op jit(solution)/shard_map/ppermute | solution.py:406
  11.3 0.0 collective-permute-done.2.refs_2_
  11.4 1.6 %collective-permute-start.3 = (f32[4,32,256]{2,1,0:T(8,128)S(1)}, f32[4,32,256]{2,1,0:T(8,128)S(1)}, u32[]{:S(2)}, u32[]{:S(2)}) collective-permute-start(f32[4,32,256]{2,1,0:T(8,128)S(1)} %join.1.joined_ref.even_ref.near_ref), channel_id=1, source_target_pairs={{0,2},{2,0},{4,6},{6,4},{8,10},{10,8},{12,14},{14,12},{1,3},{3,1},... | collective-permute-start | bytes 393224 | tf_op jit(solution)/shard_map/ppermute | solution.py:406
  12.9 3.0 %dense.1 = (bf16[2,2048,512]{2,1,0:T(8,128)(2,1)S(1)}, f32[64,128,128]{2,1,0:T(8,128)S(1)}) custom-call(s32[1]{0:T(128)S(6)} %copy.13.count_ref, s32[130]{0:T(256)} %rows_hbm.3, s32[130]{0:T(256)} %cols_hbm.3, bf16[65,128,128]{2,1,0:T(8,128)(2,1)S(1)} %get-tuple-element.25.rest, ...), custom_call_target="tpu_custom_call", output_to_operand_aliasing={{1}: (4, {})} | custom-call | flops 8519680 | bytes 8519680 | tf_op jit(solution)/shard_map/dense/pallas_call | solution.py:475
  16.0 0.4 collective-permute-done.3.odd_ref
  16.4 0.9 %first.1 = (f32[32,640]{1,0:T(8,128)S(1)}, f32[8,32,256]{2,1,0:T(8,128)S(1)}) custom-call(f32[4,32,256]{2,1,0:T(8,128)S(1)} %join.1.joined_ref.even_ref.near_ref, f32[4,32,256]{2,1,0:T(8,128)S(1)} %collective-permute-done.3.odd_ref, bf16[2,2048,512]{2,1,0:T(8,128)(2,1)S(1)} %get-tuple-element.26.matrix.refs_12_), custom_call_target="tpu_custom_call" | custom-call | tf_op jit(solution)/shard_map/first/pallas_call | solution.py:494
  17.3 0.0 collective-permute-start.4
  17.3 0.5 collective-permute-start.5
  17.8 0.9 %collective-permute-done.5 = f32[32,256]{1,0:T(8,128)S(1)} collective-permute-done((f32[32,256]{1,0:T(8,128)S(1)}, f32[32,256]{1,0:T(8,128)S(1)}, u32[]{:S(2)}, u32[]{:S(2)}) %collective-permute-start.5) | collective-permute-done | bytes 32800 | tf_op jit(solution)/shard_map/ppermute | solution.py:409
  18.7 0.0 collective-permute-done.4.other_ref
  18.7 0.3 image.2
  19.0 0.4 collective-permute-start.13
  19.4 3.8 %collective-permute-start.6 = (f32[136,128]{1,0:T(8,128)S(1)}, f32[136,128]{1,0:T(8,128)S(1)}, u32[]{:S(2)}, u32[]{:S(2)}) collective-permute-start(f32[136,128]{1,0:T(8,128)S(1)} %get-tuple-element.29.refs_0_), channel_id=1, source_target_pairs={{0,14},{2,12},{4,10},{6,8},{8,6},{10,4},{12,2},{14,0},{1,11},{3,9}... | collective-permute-start | bytes 208904 | tf_op jit(solution)/shard_map/ppermute | solution.py:427
  23.2 0.0 collective-permute-start.7
  23.3 1.9 %collective-permute-start.8 = (f32[136,128]{1,0:T(8,128)S(1)}, f32[136,128]{1,0:T(8,128)S(1)}, u32[]{:S(2)}, u32[]{:S(2)}) collective-permute-start(f32[136,128]{1,0:T(8,128)S(1)} %get-tuple-element.29.refs_0_), channel_id=1, source_target_pairs={{0,4},{2,6},{4,0},{6,2},{8,12},{10,14},{12,8},{14,10},{1,9},{3,11}... | collective-permute-start | bytes 208904 | tf_op jit(solution)/shard_map/ppermute | solution.py:427
  25.1 1.6 %collective-permute-start.9 = (f32[136,128]{1,0:T(8,128)S(1)}, f32[136,128]{1,0:T(8,128)S(1)}, u32[]{:S(2)}, u32[]{:S(2)}) collective-permute-start(f32[136,128]{1,0:T(8,128)S(1)} %get-tuple-element.29.refs_0_), channel_id=1, source_target_pairs={{0,2},{2,0},{4,6},{6,4},{8,10},{10,8},{12,14},{14,12},{1,3},{3,1},... | collective-permute-start | bytes 208904 | tf_op jit(solution)/shard_map/ppermute | solution.py:427
  26.7 0.0 collective-permute-done.6.refs_1_
  26.7 0.3 collective-permute-start.10
  27.0 1.7 %collective-permute-done.7.refs_2_ = f32[136,128]{1,0:T(8,128)S(1)} collective-permute-done((f32[136,128]{1,0:T(8,128)S(1)}, f32[136,128]{1,0:T(8,128)S(1)}, u32[]{:S(2)}, u32[]{:S(2)}) %collective-permute-start.7) | collective-permute-done | bytes 69664 | tf_op jit(solution)/shard_map/ppermute | solution.py:427
  28.7 0.0 collective-permute-start.11
  28.7 0.8 %collective-permute-done.8.refs_3_ = f32[136,128]{1,0:T(8,128)S(1)} collective-permute-done((f32[136,128]{1,0:T(8,128)S(1)}, f32[136,128]{1,0:T(8,128)S(1)}, u32[]{:S(2)}, u32[]{:S(2)}) %collective-permute-start.8) | collective-permute-done | bytes 69664 | tf_op jit(solution)/shard_map/ppermute | solution.py:427
  29.5 0.1 collective-permute-start.12
  29.6 1.0 %inverse.2.refs_11_ = f32[32,128]{1,0:T(8,128)S(1)} custom-call(f32[32,128]{1,0:T(8,128)S(1)} %get-tuple-element.33.norm_ref.refs_10_), custom_call_target="tpu_custom_call" | custom-call | tf_op jit(solution)/shard_map/inverse/pallas_call | solution.py:530
  30.6 0.0 collective-permute-done.13.far_ref
  30.6 0.1 collect.1
  30.7 0.0 collective-permute-done.10.refs_5_
  30.7 0.0 collective-permute-done.11.refs_6_
  30.7 0.0 collective-permute-done.12.refs_7_
  30.7 3.1 %step.2 = (f32[32,512]{1,0:T(8,128)S(1)}, f32[9,32,256]{2,1,0:T(8,128)S(1)}, f32[2,8,32,256]{3,2,1,0:T(8,128)S(1)}, f32[32,128]{1,0:T(8,128)S(1)}, f32[32,256]{1,0:T(8,128)S(1)}) custom-call(f32[136,128]{1,0:T(8,128)S(1)} %get-tuple-element.29.refs_0_, f32[136,128]{1,0:T(8,128)S(1)} %collective-permute-done.6.refs_1_, ...), custom_call_target="tpu_custom_call" | custom-call | tf_op jit(solution)/shard_map/step/pallas_call | solution.py:539
  33.9 0.4 collective-permute-start.14
  34.3 0.9 %collective-permute-done.14.other_ref = f32[32,512]{1,0:T(8,128)S(1)} collective-permute-done((f32[32,512]{1,0:T(8,128)S(1)}, f32[32,512]{1,0:T(8,128)S(1)}, u32[]{:S(2)}, u32[]{:S(2)}) %collective-permute-start.14) | collective-permute-done | bytes 65568 | tf_op jit(solution)/shard_map/ppermute | solution.py:409
  35.2 0.3 image.3.refs_0_
  35.5 3.0 %collective-permute-start.15 = (f32[136,128]{1,0:T(8,128)S(1)}, f32[136,128]{1,0:T(8,128)S(1)}, u32[]{:S(2)}, u32[]{:S(2)}) collective-permute-start(f32[136,128]{1,0:T(8,128)S(1)} %image.3.refs_0_), channel_id=1, source_target_pairs={{0,14},{2,12},{4,10},{6,8},{8,6},{10,4},{12,2},{14,0},{1,11},{3,9}... | collective-permute-start | bytes 208904 | tf_op jit(solution)/shard_map/ppermute | solution.py:427
  38.5 0.0 collective-permute-start.16
  38.5 2.9 %collective-permute-start.17 = (f32[136,128]{1,0:T(8,128)S(1)}, f32[136,128]{1,0:T(8,128)S(1)}, u32[]{:S(2)}, u32[]{:S(2)}) collective-permute-start(f32[136,128]{1,0:T(8,128)S(1)} %image.3.refs_0_), channel_id=1, source_target_pairs={{0,4},{2,6},{4,0},{6,2},{8,12},{10,14},{12,8},{14,10},{1,9},{3,11}... | collective-permute-start | bytes 208904 | tf_op jit(solution)/shard_map/ppermute | solution.py:427
  41.5 0.5 collective-permute-start.18
  42.0 0.8 %collective-permute-done.15.refs_1_ = f32[136,128]{1,0:T(8,128)S(1)} collective-permute-done((f32[136,128]{1,0:T(8,128)S(1)}, f32[136,128]{1,0:T(8,128)S(1)}, u32[]{:S(2)}, u32[]{:S(2)}) %collective-permute-start.15) | collective-permute-done | bytes 69664 | tf_op jit(solution)/shard_map/ppermute | solution.py:427
  42.8 0.6 collective-permute-start.19
  43.4 1.0 %collective-permute-done.16.refs_2_ = f32[136,128]{1,0:T(8,128)S(1)} collective-permute-done((f32[136,128]{1,0:T(8,128)S(1)}, f32[136,128]{1,0:T(8,128)S(1)}, u32[]{:S(2)}, u32[]{:S(2)}) %collective-permute-start.16) | collective-permute-done | bytes 69664 | tf_op jit(solution)/shard_map/ppermute | solution.py:427
  44.4 1.2 %collective-permute-done.17.refs_3_ = f32[136,128]{1,0:T(8,128)S(1)} collective-permute-done((f32[136,128]{1,0:T(8,128)S(1)}, f32[136,128]{1,0:T(8,128)S(1)}, u32[]{:S(2)}, u32[]{:S(2)}) %collective-permute-start.17) | collective-permute-done | bytes 69664 | tf_op jit(solution)/shard_map/ppermute | solution.py:427
  45.7 1.0 %inverse.3.refs_11_ = f32[32,128]{1,0:T(8,128)S(1)} custom-call(f32[32,128]{1,0:T(8,128)S(1)} %get-tuple-element.37.norm_ref.refs_10_), custom_call_target="tpu_custom_call" | custom-call | tf_op jit(solution)/shard_map/inverse/pallas_call | solution.py:530
  46.7 0.0 collective-permute-done.18.refs_4_
  46.7 0.0 collective-permute-done.20.refs_6_
  46.7 0.2 collective-permute-done.21.refs_7_
  46.9 3.1 %step.3 = (f32[32,512]{1,0:T(8,128)S(1)}, f32[2,32,256]{2,1,0:T(8,128)S(1)}, f32[32,256]{1,0:T(8,128)S(1)}, f32[32,128]{1,0:T(8,128)S(1)}, f32[32,256]{1,0:T(8,128)S(1)}) custom-call(f32[136,128]{1,0:T(8,128)S(1)} %image.3.refs_0_, f32[136,128]{1,0:T(8,128)S(1)} %collective-permute-done.15.refs_1_, f32[136,128]{1,0:T(8,128)S(1)} %collective-permute-done.16.refs_2_, ...), custom_call_target="tpu_custom_call" | custom-call | tf_op jit(solution)/shard_map/step/pallas_call | solution.py:539
  50.0 0.4 collective-permute-start.22
  50.4 0.9 %collective-permute-done.22.other_ref = f32[32,512]{1,0:T(8,128)S(1)} collective-permute-done((f32[32,512]{1,0:T(8,128)S(1)}, f32[32,512]{1,0:T(8,128)S(1)}, u32[]{:S(2)}, u32[]{:S(2)}) %collective-permute-start.22) | collective-permute-done | bytes 65568 | tf_op jit(solution)/shard_map/ppermute | solution.py:409
  51.3 0.3 last_image.1
  51.6 2.4 %collective-permute-start.23 = (f32[8,128]{1,0:T(8,128)S(1)}, f32[8,128]{1,0:T(8,128)S(1)}, u32[]{:S(2)}, u32[]{:S(2)}) collective-permute-start(f32[8,128]{1,0:T(8,128)S(1)} %get-tuple-element.41.refs_0_), channel_id=1, source_target_pairs={{0,14},{2,12},{4,10},{6,8},{8,6},{10,4},{12,2},{14,0},{1,11},{3,9}... | collective-permute-start | bytes 12296 | tf_op jit(solution)/shard_map/ppermute | solution.py:427
  54.1 0.0 collective-permute-start.24
  54.1 2.6 %collective-permute-start.25 = (f32[8,128]{1,0:T(8,128)S(1)}, f32[8,128]{1,0:T(8,128)S(1)}, u32[]{:S(2)}, u32[]{:S(2)}) collective-permute-start(f32[8,128]{1,0:T(8,128)S(1)} %get-tuple-element.41.refs_0_), channel_id=1, source_target_pairs={{0,4},{2,6},{4,0},{6,2},{8,12},{10,14},{12,8},{14,10},{1,9},{3,11}... | collective-permute-start | bytes 12296 | tf_op jit(solution)/shard_map/ppermute | solution.py:427
  56.7 0.9 %collective-permute-start.26 = (f32[8,128]{1,0:T(8,128)S(1)}, f32[8,128]{1,0:T(8,128)S(1)}, u32[]{:S(2)}, u32[]{:S(2)}) collective-permute-start(f32[8,128]{1,0:T(8,128)S(1)} %get-tuple-element.41.refs_0_), channel_id=1, source_target_pairs={{0,2},{2,0},{4,6},{6,4},{8,10},{10,8},{12,14},{14,12},{1,3},{3,1},... | collective-permute-start | bytes 12296 | tf_op jit(solution)/shard_map/ppermute | solution.py:427
  57.6 0.4 collective-permute-done.23.refs_1_
  58.0 0.6 %collective-permute-done.24.refs_2_ = f32[8,128]{1,0:T(8,128)S(1)} collective-permute-done((f32[8,128]{1,0:T(8,128)S(1)}, f32[8,128]{1,0:T(8,128)S(1)}, u32[]{:S(2)}, u32[]{:S(2)}) %collective-permute-start.24) | collective-permute-done | bytes 4128 | tf_op jit(solution)/shard_map/ppermute | solution.py:427
  58.6 0.0 collective-permute-done.25.refs_3_
  58.6 0.5 collective-permute-start.29
  59.1 1.2 %collective-permute-done.26.refs_4_ = f32[8,128]{1,0:T(8,128)S(1)} collective-permute-done((f32[8,128]{1,0:T(8,128)S(1)}, f32[8,128]{1,0:T(8,128)S(1)}, u32[]{:S(2)}, u32[]{:S(2)}) %collective-permute-start.26) | collective-permute-done | bytes 4128 | tf_op jit(solution)/shard_map/ppermute | solution.py:427
  60.3 1.7 %last.1 = (f32[32,256]{1,0:T(8,128)}, f32[32,256]{1,0:T(8,128)}) custom-call(f32[8,128]{1,0:T(8,128)S(1)} %get-tuple-element.41.refs_0_, f32[8,128]{1,0:T(8,128)S(1)} %collective-permute-done.23.refs_1_, f32[8,128]{1,0:T(8,128)S(1)} %collective-permute-done.24.refs_2_, f32[8,128]{1,0:T(8,128)S(1)} %collective-permute-done.25.refs_3_, ...), custom_call_target="tpu_custom_call" | custom-call | tf_op jit(solution)/shard_map/last/pallas_call | solution.py:562
  (10 shorter events, 0.0 us)
Async XLA Ops:
  1.5 9.0 %collective-permute-start = (f32[32,256]{1,0:T(8,128)S(1)}, f32[32,256]{1,0:T(8,128)S(1)}, u32[]{:S(2)}, u32[]{:S(2)}) collective-permute-start(f32[32,256]{1,0:T(8,128)S(1)} %multiply_multiply_fusion.refs_3_), channel_id=1, source_target_pairs={{0,12},{2,14},{4,8},{6,10},{8,4},{10,6},{12,0},{14,2},{1,13},{3,15... | collective-permute-start | bytes 98312 | tf_op jit(solution)/shard_map/ppermute | solution.py:406
  6.5 4.8 %collective-permute-start.1 = (f32[32,256]{1,0:T(8,128)S(1)}, f32[32,256]{1,0:T(8,128)S(1)}, u32[]{:S(2)}, u32[]{:S(2)}) collective-permute-start(f32[32,256]{1,0:T(8,128)S(1)} %multiply_multiply_fusion.refs_3_), channel_id=1, source_target_pairs={{0,8},{2,10},{4,12},{6,14},{8,0},{10,2},{12,4},{14,6},{1,9},{3,11}... | collective-permute-start | bytes 98312 | tf_op jit(solution)/shard_map/ppermute | solution.py:406
  6.5 4.8 %collective-permute-start.2 = (f32[32,256]{1,0:T(8,128)S(1)}, f32[32,256]{1,0:T(8,128)S(1)}, u32[]{:S(2)}, u32[]{:S(2)}) collective-permute-start(f32[32,256]{1,0:T(8,128)S(1)} %multiply_multiply_fusion.refs_3_), channel_id=1, source_target_pairs={{0,4},{2,6},{4,0},{6,2},{8,12},{10,14},{12,8},{14,10},{1,5},{3,7},... | collective-permute-start | bytes 98312 | tf_op jit(solution)/shard_map/ppermute | solution.py:406
  11.4 5.0 %collective-permute-start.3 = (f32[4,32,256]{2,1,0:T(8,128)S(1)}, f32[4,32,256]{2,1,0:T(8,128)S(1)}, u32[]{:S(2)}, u32[]{:S(2)}) collective-permute-start(f32[4,32,256]{2,1,0:T(8,128)S(1)} %join.1.joined_ref.even_ref.near_ref), channel_id=1, source_target_pairs={{0,2},{2,0},{4,6},{6,4},{8,10},{10,8},{12,14},{14,12},{1,3},{3,1},... | collective-permute-start | bytes 393224 | tf_op jit(solution)/shard_map/ppermute | solution.py:406
  17.3 1.4 %collective-permute-start.4 = (f32[32,640]{1,0:T(8,128)S(1)}, f32[32,640]{1,0:T(8,128)S(1)}, u32[]{:S(2)}, u32[]{:S(2)}) collective-permute-start(f32[32,640]{1,0:T(8,128)S(1)} %get-tuple-element.27.mine_ref), channel_id=1, source_target_pairs={{0,1},{1,0},{2,3},{3,2},{4,5},{5,4},{6,7},{7,6},{8,9},{9,8},{10,11... | collective-permute-start | bytes 245768 | tf_op jit(solution)/shard_map/ppermute | solution.py:409
  17.3 1.4 %collective-permute-start.5 = (f32[32,256]{1,0:T(8,128)S(1)}, f32[32,256]{1,0:T(8,128)S(1)}, u32[]{:S(2)}, u32[]{:S(2)}) collective-permute-start(f32[32,256]{1,0:T(8,128)S(1)} %multiply_multiply_fusion.refs_3_), channel_id=1, source_target_pairs={{0,1},{1,0},{2,3},{3,2},{4,5},{5,4},{6,7},{7,6},{8,9},{9,8},{10,11... | collective-permute-start | bytes 98312 | tf_op jit(solution)/shard_map/ppermute | solution.py:409
  19.0 11.6 %collective-permute-start.13 = (f32[8,32,256]{2,1,0:T(8,128)S(1)}, f32[8,32,256]{2,1,0:T(8,128)S(1)}, u32[]{:S(2)}, u32[]{:S(2)}) collective-permute-start(f32[8,32,256]{2,1,0:T(8,128)S(1)} %get-tuple-element.30.near_ref), channel_id=1, source_target_pairs={{0,1},{1,0},{2,3},{3,2},{4,5},{5,4},{6,7},{7,6},{8,9},{9,8},{10,11... | collective-permute-start | bytes 786440 | tf_op jit(solution)/shard_map/ppermute | solution.py:409
  19.4 7.3 %collective-permute-start.6 = (f32[136,128]{1,0:T(8,128)S(1)}, f32[136,128]{1,0:T(8,128)S(1)}, u32[]{:S(2)}, u32[]{:S(2)}) collective-permute-start(f32[136,128]{1,0:T(8,128)S(1)} %get-tuple-element.29.refs_0_), channel_id=1, source_target_pairs={{0,14},{2,12},{4,10},{6,8},{8,6},{10,4},{12,2},{14,0},{1,11},{3,9}... | collective-permute-start | bytes 208904 | tf_op jit(solution)/shard_map/ppermute | solution.py:427
  23.2 5.5 %collective-permute-start.7 = (f32[136,128]{1,0:T(8,128)S(1)}, f32[136,128]{1,0:T(8,128)S(1)}, u32[]{:S(2)}, u32[]{:S(2)}) collective-permute-start(f32[136,128]{1,0:T(8,128)S(1)} %get-tuple-element.29.refs_0_), channel_id=1, source_target_pairs={{0,6},{2,4},{4,2},{6,0},{8,14},{10,12},{12,10},{14,8},{1,13},{3,15... | collective-permute-start | bytes 208904 | tf_op jit(solution)/shard_map/ppermute | solution.py:427
  23.3 6.2 %collective-permute-start.8 = (f32[136,128]{1,0:T(8,128)S(1)}, f32[136,128]{1,0:T(8,128)S(1)}, u32[]{:S(2)}, u32[]{:S(2)}) collective-permute-start(f32[136,128]{1,0:T(8,128)S(1)} %get-tuple-element.29.refs_0_), channel_id=1, source_target_pairs={{0,4},{2,6},{4,0},{6,2},{8,12},{10,14},{12,8},{14,10},{1,9},{3,11}... | collective-permute-start | bytes 208904 | tf_op jit(solution)/shard_map/ppermute | solution.py:427
  25.1 5.5 %collective-permute-start.9 = (f32[136,128]{1,0:T(8,128)S(1)}, f32[136,128]{1,0:T(8,128)S(1)}, u32[]{:S(2)}, u32[]{:S(2)}) collective-permute-start(f32[136,128]{1,0:T(8,128)S(1)} %get-tuple-element.29.refs_0_), channel_id=1, source_target_pairs={{0,2},{2,0},{4,6},{6,4},{8,10},{10,8},{12,14},{14,12},{1,3},{3,1},... | collective-permute-start | bytes 208904 | tf_op jit(solution)/shard_map/ppermute | solution.py:427
  26.7 4.0 %collective-permute-start.10 = (f32[136,128]{1,0:T(8,128)S(1)}, f32[136,128]{1,0:T(8,128)S(1)}, u32[]{:S(2)}, u32[]{:S(2)}) collective-permute-start(f32[136,128]{1,0:T(8,128)S(1)} %collective-permute-done.6.refs_1_), channel_id=1, source_target_pairs={{0,1},{1,0},{2,3},{3,2},{4,5},{5,4},{6,7},{7,6},{8,9},{9,8},{10,11... | collective-permute-start | bytes 208904 | tf_op jit(solution)/shard_map/ppermute | solution.py:409
  28.7 2.0 %collective-permute-start.11 = (f32[136,128]{1,0:T(8,128)S(1)}, f32[136,128]{1,0:T(8,128)S(1)}, u32[]{:S(2)}, u32[]{:S(2)}) collective-permute-start(f32[136,128]{1,0:T(8,128)S(1)} %collective-permute-done.7.refs_2_), channel_id=1, source_target_pairs={{0,1},{1,0},{2,3},{3,2},{4,5},{5,4},{6,7},{7,6},{8,9},{9,8},{10,11... | collective-permute-start | bytes 208904 | tf_op jit(solution)/shard_map/ppermute | solution.py:409
  29.5 1.3 %collective-permute-start.12 = (f32[136,128]{1,0:T(8,128)S(1)}, f32[136,128]{1,0:T(8,128)S(1)}, u32[]{:S(2)}, u32[]{:S(2)}) collective-permute-start(f32[136,128]{1,0:T(8,128)S(1)} %collective-permute-done.8.refs_3_), channel_id=1, source_target_pairs={{0,1},{1,0},{2,3},{3,2},{4,5},{5,4},{6,7},{7,6},{8,9},{9,8},{10,11... | collective-permute-start | bytes 208904 | tf_op jit(solution)/shard_map/ppermute | solution.py:409
  33.9 1.3 %collective-permute-start.14 = (f32[32,512]{1,0:T(8,128)S(1)}, f32[32,512]{1,0:T(8,128)S(1)}, u32[]{:S(2)}, u32[]{:S(2)}) collective-permute-start(f32[32,512]{1,0:T(8,128)S(1)} %get-tuple-element.34.mine_ref), channel_id=1, source_target_pairs={{0,1},{1,0},{2,3},{3,2},{4,5},{5,4},{6,7},{7,6},{8,9},{9,8},{10,11... | collective-permute-start | bytes 196616 | tf_op jit(solution)/shard_map/ppermute | solution.py:409
  35.5 7.3 %collective-permute-start.15 = (f32[136,128]{1,0:T(8,128)S(1)}, f32[136,128]{1,0:T(8,128)S(1)}, u32[]{:S(2)}, u32[]{:S(2)}) collective-permute-start(f32[136,128]{1,0:T(8,128)S(1)} %image.3.refs_0_), channel_id=1, source_target_pairs={{0,14},{2,12},{4,10},{6,8},{8,6},{10,4},{12,2},{14,0},{1,11},{3,9}... | collective-permute-start | bytes 208904 | tf_op jit(solution)/shard_map/ppermute | solution.py:427
  38.5 5.9 %collective-permute-start.16 = (f32[136,128]{1,0:T(8,128)S(1)}, f32[136,128]{1,0:T(8,128)S(1)}, u32[]{:S(2)}, u32[]{:S(2)}) collective-permute-start(f32[136,128]{1,0:T(8,128)S(1)} %image.3.refs_0_), channel_id=1, source_target_pairs={{0,6},{2,4},{4,2},{6,0},{8,14},{10,12},{12,10},{14,8},{1,13},{3,15... | collective-permute-start | bytes 208904 | tf_op jit(solution)/shard_map/ppermute | solution.py:427
  38.5 7.1 %collective-permute-start.17 = (f32[136,128]{1,0:T(8,128)S(1)}, f32[136,128]{1,0:T(8,128)S(1)}, u32[]{:S(2)}, u32[]{:S(2)}) collective-permute-start(f32[136,128]{1,0:T(8,128)S(1)} %image.3.refs_0_), channel_id=1, source_target_pairs={{0,4},{2,6},{4,0},{6,2},{8,12},{10,14},{12,8},{14,10},{1,9},{3,11}... | collective-permute-start | bytes 208904 | tf_op jit(solution)/shard_map/ppermute | solution.py:427
  41.5 5.2 %collective-permute-start.18 = (f32[136,128]{1,0:T(8,128)S(1)}, f32[136,128]{1,0:T(8,128)S(1)}, u32[]{:S(2)}, u32[]{:S(2)}) collective-permute-start(f32[136,128]{1,0:T(8,128)S(1)} %image.3.refs_0_), channel_id=1, source_target_pairs={{0,2},{2,0},{4,6},{6,4},{8,10},{10,8},{12,14},{14,12},{1,3},{3,1},... | collective-permute-start | bytes 208904 | tf_op jit(solution)/shard_map/ppermute | solution.py:427
  42.8 3.9 %collective-permute-start.19 = (f32[136,128]{1,0:T(8,128)S(1)}, f32[136,128]{1,0:T(8,128)S(1)}, u32[]{:S(2)}, u32[]{:S(2)}) collective-permute-start(f32[136,128]{1,0:T(8,128)S(1)} %collective-permute-done.15.refs_1_), channel_id=1, source_target_pairs={{0,1},{1,0},{2,3},{3,2},{4,5},{5,4},{6,7},{7,6},{8,9},{9,8},{10,11... | collective-permute-start | bytes 208904 | tf_op jit(solution)/shard_map/ppermute | solution.py:409
  44.4 2.3 %collective-permute-start.20 = (f32[136,128]{1,0:T(8,128)S(1)}, f32[136,128]{1,0:T(8,128)S(1)}, u32[]{:S(2)}, u32[]{:S(2)}) collective-permute-start(f32[136,128]{1,0:T(8,128)S(1)} %collective-permute-done.16.refs_2_), channel_id=1, source_target_pairs={{0,1},{1,0},{2,3},{3,2},{4,5},{5,4},{6,7},{7,6},{8,9},{9,8},{10,11... | collective-permute-start | bytes 208904 | tf_op jit(solution)/shard_map/ppermute | solution.py:409
  45.7 1.3 %collective-permute-start.21 = (f32[136,128]{1,0:T(8,128)S(1)}, f32[136,128]{1,0:T(8,128)S(1)}, u32[]{:S(2)}, u32[]{:S(2)}) collective-permute-start(f32[136,128]{1,0:T(8,128)S(1)} %collective-permute-done.17.refs_3_), channel_id=1, source_target_pairs={{0,1},{1,0},{2,3},{3,2},{4,5},{5,4},{6,7},{7,6},{8,9},{9,8},{10,11... | collective-permute-start | bytes 208904 | tf_op jit(solution)/shard_map/ppermute | solution.py:409
  50.0 1.3 %collective-permute-start.22 = (f32[32,512]{1,0:T(8,128)S(1)}, f32[32,512]{1,0:T(8,128)S(1)}, u32[]{:S(2)}, u32[]{:S(2)}) collective-permute-start(f32[32,512]{1,0:T(8,128)S(1)} %get-tuple-element.39.mine_ref), channel_id=1, source_target_pairs={{0,1},{1,0},{2,3},{3,2},{4,5},{5,4},{6,7},{7,6},{8,9},{9,8},{10,11... | collective-permute-start | bytes 196616 | tf_op jit(solution)/shard_map/ppermute | solution.py:409
  51.6 6.3 %collective-permute-start.23 = (f32[8,128]{1,0:T(8,128)S(1)}, f32[8,128]{1,0:T(8,128)S(1)}, u32[]{:S(2)}, u32[]{:S(2)}) collective-permute-start(f32[8,128]{1,0:T(8,128)S(1)} %get-tuple-element.41.refs_0_), channel_id=1, source_target_pairs={{0,14},{2,12},{4,10},{6,8},{8,6},{10,4},{12,2},{14,0},{1,11},{3,9}... | collective-permute-start | bytes 12296 | tf_op jit(solution)/shard_map/ppermute | solution.py:427
  54.1 4.5 %collective-permute-start.24 = (f32[8,128]{1,0:T(8,128)S(1)}, f32[8,128]{1,0:T(8,128)S(1)}, u32[]{:S(2)}, u32[]{:S(2)}) collective-permute-start(f32[8,128]{1,0:T(8,128)S(1)} %get-tuple-element.41.refs_0_), channel_id=1, source_target_pairs={{0,6},{2,4},{4,2},{6,0},{8,14},{10,12},{12,10},{14,8},{1,13},{3,15... | collective-permute-start | bytes 12296 | tf_op jit(solution)/shard_map/ppermute | solution.py:427
  54.1 4.5 %collective-permute-start.25 = (f32[8,128]{1,0:T(8,128)S(1)}, f32[8,128]{1,0:T(8,128)S(1)}, u32[]{:S(2)}, u32[]{:S(2)}) collective-permute-start(f32[8,128]{1,0:T(8,128)S(1)} %get-tuple-element.41.refs_0_), channel_id=1, source_target_pairs={{0,4},{2,6},{4,0},{6,2},{8,12},{10,14},{12,8},{14,10},{1,9},{3,11}... | collective-permute-start | bytes 12296 | tf_op jit(solution)/shard_map/ppermute | solution.py:427
  56.7 3.6 %collective-permute-start.26 = (f32[8,128]{1,0:T(8,128)S(1)}, f32[8,128]{1,0:T(8,128)S(1)}, u32[]{:S(2)}, u32[]{:S(2)}) collective-permute-start(f32[8,128]{1,0:T(8,128)S(1)} %get-tuple-element.41.refs_0_), channel_id=1, source_target_pairs={{0,2},{2,0},{4,6},{6,4},{8,10},{10,8},{12,14},{14,12},{1,3},{3,1},... | collective-permute-start | bytes 12296 | tf_op jit(solution)/shard_map/ppermute | solution.py:427
  58.0 2.4 %collective-permute-start.27 = (f32[8,128]{1,0:T(8,128)S(1)}, f32[8,128]{1,0:T(8,128)S(1)}, u32[]{:S(2)}, u32[]{:S(2)}) collective-permute-start(f32[8,128]{1,0:T(8,128)S(1)} %collective-permute-done.23.refs_1_), channel_id=1, source_target_pairs={{0,1},{1,0},{2,3},{3,2},{4,5},{5,4},{6,7},{7,6},{8,9},{9,8},{10,11... | collective-permute-start | bytes 12296 | tf_op jit(solution)/shard_map/ppermute | solution.py:409
  58.6 1.7 %collective-permute-start.28 = (f32[8,128]{1,0:T(8,128)S(1)}, f32[8,128]{1,0:T(8,128)S(1)}, u32[]{:S(2)}, u32[]{:S(2)}) collective-permute-start(f32[8,128]{1,0:T(8,128)S(1)} %collective-permute-done.24.refs_2_), channel_id=1, source_target_pairs={{0,1},{1,0},{2,3},{3,2},{4,5},{5,4},{6,7},{7,6},{8,9},{9,8},{10,11... | collective-permute-start | bytes 12296 | tf_op jit(solution)/shard_map/ppermute | solution.py:409
  58.6 1.7 %collective-permute-start.29 = (f32[8,128]{1,0:T(8,128)S(1)}, f32[8,128]{1,0:T(8,128)S(1)}, u32[]{:S(2)}, u32[]{:S(2)}) collective-permute-start(f32[8,128]{1,0:T(8,128)S(1)} %collective-permute-done.25.refs_3_), channel_id=1, source_target_pairs={{0,1},{1,0},{2,3},{3,2},{4,5},{5,4},{6,7},{7,6},{8,9},{9,8},{10,11... | collective-permute-start | bytes 12296 | tf_op jit(solution)/shard_map/ppermute | solution.py:409

commit v11 on v9

--- a/solution.py
+++ b/solution.py
@@ -109,7 +109,7 @@
         for i in range(PIVOTS):
             pivot = base + i
             here = row_ids == pivot
-            inverse = 1.0 / columns[i][pivot : pivot + 1, :]
+            inverse = pltpu.reciprocal(columns[i][pivot : pivot + 1, :], full_range=False)
             row = work[pivot : pivot + 1, :] * inverse
             work = jnp.where(here, row, work - columns[i] * row)
             for later in range(i + 1, PIVOTS):
@@ -144,13 +144,22 @@
         column_at = (owner ^ row_place) * blocks + lax.rem(column, blocks)
         return column_at * row_blocks + side * blocks + lax.rem(row, blocks)
 
-    def add(slot, at):
-        value = total[at] + tiles[slot - first_tile].astype(F32)
-        following = place(jnp.minimum(slot + 1, slots - 1))
-        total[at] = value
+    def after(slot):
+        return place(jnp.minimum(slot, slots - 1))
+
+    def add(turn, places):
+        slot = start + 2 * turn
+        values = [tiles[slot + i - first_tile].astype(F32) for i in range(2)]
+        following = (after(slot + 2), after(slot + 3))
+        for at, value in zip(places, values):
+            total[at] = total[at] + value
         return following
 
-    lax.fori_loop(start, stop, add, place(start))
+    places = lax.fori_loop(0, (stop - start) // 2, add, (after(start), after(start + 1)))
+
+    @pl.when(lax.rem(stop - start, 2) == 1)
+    def _():
+        total[places[0]] = total[places[0]] + tiles[stop - 1 - first_tile].astype(F32)
 
 
 def copy_lists(hbm_refs, smem_refs, sems):
@@ -403,7 +412,7 @@
         if pieces != 8:
             found = [value] + [swap(value, k) for k in range(1, pieces)]
             return found, [(k, k) for k in range(pieces)]
-        shares = ((7, 4), (3, 5), (2, 6), (1, 1))
+        shares = ((7, 5), (3, 6), (2, 4), (1, 1))
         fetched = []
         passed = []
         places = {0: (0, 0)}

time: 62.3 us -> 61.5 us (0.987)
  starting transfers between devices: 30.2 us -> 28.6 us
  waiting for transfers between devices: 13.2 us -> 14.5 us
    ppermute x12, starting transfers between devices: 19.9 us -> 18.8 us  [exchange(): fetched.append(lax.ppermute(value, ('row', 'col'), pairs))]
  transfers between devices with their start and end apart: 30 -> 30, of which waited for: 10 -> 16; matrix products, arithmetic and copies ran while one was open for 0% -> 0% of each run, Pallas kernels for 11% -> 10%
where the time goes in v11:
time: 61.5 us; the launch traced here: 61.4 us
  starting transfers between devices  28.6 us (47%)
  Pallas kernels  16.1 us (26%)
  waiting for transfers between devices  14.5 us (24%)
  between operations  1.43 us (2%)
  other arithmetic  0.85 us (1%)
    ppermute x12, starting transfers between devices, exchange(): fetched.append(lax.ppermute(value, ('row', 'col'), pairs))  18.8 us
    ppermute x12, waiting for transfers between devices, exchange(): fetched.append(lax.ppermute(value, ('row', 'col'), pairs))  8.61 us
    ppermute x4, starting transfers between devices, swap(): return lax.ppermute(value, 'row', [(i, i ^ mask) for i in range(pieces)])  7.28 us
    pallas_call x2, Pallas kernels, per_device(): pl.pallas_call(functools.partial(step_kernel, places, not first, last), o...  6.1 us
    ppermute x14, waiting for transfers between devices, across(): lax.ppermute(value, 'col', [(i, (i + 1) % col_devices) for i in range(col...  3.37 us
    ppermute x14, starting transfers between devices, across(): lax.ppermute(value, 'col', [(i, (i + 1) % col_devices) for i in range(col...  2.5 us
    ppermute x4, waiting for transfers between devices, swap(): return lax.ppermute(value, 'row', [(i, i ^ mask) for i in range(pieces)])  2.48 us
    pallas_call x1, Pallas kernels, per_device(): pl.pallas_call(functools.partial(gather_kernel, rows_dev), out_shape=(tot...  2.23 us
  transfers between devices with their start and end apart: 30, of which 16 were waited for; matrix products, arithmetic and copies ran while one was open for 0% of the time, Pallas kernels for 10%

profile of v11, /device:TPU:0, one launch (start us, length us, event | category | flops | bytes accessed | tf_op | source)
XLA Modules:
  0.0 61.4 jit_solution(945523435516063980)
XLA Ops:
  0.6 0.8 %multiply_multiply_fusion.refs_3_ = f32[32,256]{1,0:T(8,128)S(1)} fusion(s32[32,256]{1,0:T(8,128)} %param.11, f32[32]{0:T(128)} %param.13, f32[256]{0:T(256)} %param.12), kind=kLoop, calls=%fused_computation | loop fusion | flops 24576 | bytes 66688 | tf_op jit(solution)/shard_map/mul | solution.py:434
  1.5 5.1 %collective-permute-start = (f32[32,256]{1,0:T(8,128)S(1)}, f32[32,256]{1,0:T(8,128)S(1)}, u32[]{:S(2)}, u32[]{:S(2)}) collective-permute-start(f32[32,256]{1,0:T(8,128)S(1)} %multiply_multiply_fusion.refs_3_), channel_id=1, source_target_pairs={{0,12},{2,14},{4,8},{6,10},{8,4},{10,6},{12,0},{14,2},{1,13},{3,15... | collective-permute-start | bytes 98312 | tf_op jit(solution)/shard_map/ppermute | solution.py:404
  6.5 0.0 collective-permute-start.1
  6.5 0.6 %collective-permute-start.2 = (f32[32,256]{1,0:T(8,128)S(1)}, f32[32,256]{1,0:T(8,128)S(1)}, u32[]{:S(2)}, u32[]{:S(2)}) collective-permute-start(f32[32,256]{1,0:T(8,128)S(1)} %multiply_multiply_fusion.refs_3_), channel_id=1, source_target_pairs={{0,4},{2,6},{4,0},{6,2},{8,12},{10,14},{12,8},{14,10},{1,5},{3,7},... | collective-permute-start | bytes 98312 | tf_op jit(solution)/shard_map/ppermute | solution.py:404
  7.8 2.2 %gather.1 = (f32[64,128,128]{2,1,0:T(8,128)S(1)}, bf16[65,128,128]{2,1,0:T(8,128)(2,1)S(1)}) custom-call(s32[1]{0:T(128)S(6)} %copy.13.count_ref, s32[130]{0:T(256)} %rows_hbm.3, s32[130]{0:T(256)} %cols_hbm.3, bf16[130,128,128]{2,1,0:T(8,128)(2,1)} %tiles_ref.1), custom_call_target="tpu_custom_call" | custom-call | flops 8519680 | bytes 8519680 | tf_op jit(solution)/shard_map/gather/pallas_call | solution.py:448
  10.1 0.0 collective-permute-done.refs_0_
  10.1 1.3 %collective-permute-done.1.refs_1_ = f32[32,256]{1,0:T(8,128)S(1)} collective-permute-done((f32[32,256]{1,0:T(8,128)S(1)}, f32[32,256]{1,0:T(8,128)S(1)}, u32[]{:S(2)}, u32[]{:S(2)}) %collective-permute-start.1) | collective-permute-done | bytes 32800 | tf_op jit(solution)/shard_map/ppermute | solution.py:404
  11.3 0.0 collective-permute-done.2.refs_2_
  11.4 1.6 %collective-permute-start.3 = (f32[4,32,256]{2,1,0:T(8,128)S(1)}, f32[4,32,256]{2,1,0:T(8,128)S(1)}, u32[]{:S(2)}, u32[]{:S(2)}) collective-permute-start(f32[4,32,256]{2,1,0:T(8,128)S(1)} %join.1.joined_ref.even_ref.near_ref), channel_id=1, source_target_pairs={{0,2},{2,0},{4,6},{6,4},{8,10},{10,8},{12,14},{14,12},{1,3},{3,1},... | collective-permute-start | bytes 393224 | tf_op jit(solution)/shard_map/ppermute | solution.py:404
  12.9 2.2 %dense.1 = (bf16[2,2048,512]{2,1,0:T(8,128)(2,1)S(1)}, f32[64,128,128]{2,1,0:T(8,128)S(1)}) custom-call(s32[1]{0:T(128)S(6)} %copy.13.count_ref, s32[130]{0:T(256)} %rows_hbm.3, s32[130]{0:T(256)} %cols_hbm.3, bf16[65,128,128]{2,1,0:T(8,128)(2,1)S(1)} %get-tuple-element.25.rest, ...), custom_call_target="tpu_custom_call", output_to_operand_aliasing={{1}: (4, {})} | custom-call | flops 8519680 | bytes 8519680 | tf_op jit(solution)/shard_map/dense/pallas_call | solution.py:473
  15.2 1.2 %collective-permute-done.3.odd_ref = f32[4,32,256]{2,1,0:T(8,128)S(1)} collective-permute-done((f32[4,32,256]{2,1,0:T(8,128)S(1)}, f32[4,32,256]{2,1,0:T(8,128)S(1)}, u32[]{:S(2)}, u32[]{:S(2)}) %collective-permute-start.3) | collective-permute-done | bytes 131104 | tf_op jit(solution)/shard_map/ppermute | solution.py:404
  16.4 0.9 %first.1 = (f32[32,640]{1,0:T(8,128)S(1)}, f32[8,32,256]{2,1,0:T(8,128)S(1)}) custom-call(f32[4,32,256]{2,1,0:T(8,128)S(1)} %join.1.joined_ref.even_ref.near_ref, f32[4,32,256]{2,1,0:T(8,128)S(1)} %collective-permute-done.3.odd_ref, bf16[2,2048,512]{2,1,0:T(8,128)(2,1)S(1)} %get-tuple-element.26.matrix.refs_12_), custom_call_target="tpu_custom_call" | custom-call | tf_op jit(solution)/shard_map/first/pallas_call | solution.py:492
  17.3 0.0 collective-permute-start.4
  17.3 0.5 collective-permute-start.5
  17.8 0.9 %collective-permute-done.5 = f32[32,256]{1,0:T(8,128)S(1)} collective-permute-done((f32[32,256]{1,0:T(8,128)S(1)}, f32[32,256]{1,0:T(8,128)S(1)}, u32[]{:S(2)}, u32[]{:S(2)}) %collective-permute-start.5) | collective-permute-done | bytes 32800 | tf_op jit(solution)/shard_map/ppermute | solution.py:407
  18.7 0.3 image.2
  19.0 0.4 collective-permute-start.13
  19.4 3.5 %collective-permute-start.6 = (f32[136,128]{1,0:T(8,128)S(1)}, f32[136,128]{1,0:T(8,128)S(1)}, u32[]{:S(2)}, u32[]{:S(2)}) collective-permute-start(f32[136,128]{1,0:T(8,128)S(1)} %get-tuple-element.29.refs_0_), channel_id=1, source_target_pairs={{0,14},{2,12},{4,10},{6,8},{8,6},{10,4},{12,2},{14,0},{1,11},{3,9}... | collective-permute-start | bytes 208904 | tf_op jit(solution)/shard_map/ppermute | solution.py:425
  22.9 0.0 collective-permute-start.7
  22.9 2.0 %collective-permute-start.8 = (f32[136,128]{1,0:T(8,128)S(1)}, f32[136,128]{1,0:T(8,128)S(1)}, u32[]{:S(2)}, u32[]{:S(2)}) collective-permute-start(f32[136,128]{1,0:T(8,128)S(1)} %get-tuple-element.29.refs_0_), channel_id=1, source_target_pairs={{0,4},{2,6},{4,0},{6,2},{8,12},{10,14},{12,8},{14,10},{1,9},{3,11}... | collective-permute-start | bytes 208904 | tf_op jit(solution)/shard_map/ppermute | solution.py:425
  24.9 1.5 %collective-permute-start.9 = (f32[136,128]{1,0:T(8,128)S(1)}, f32[136,128]{1,0:T(8,128)S(1)}, u32[]{:S(2)}, u32[]{:S(2)}) collective-permute-start(f32[136,128]{1,0:T(8,128)S(1)} %get-tuple-element.29.refs_0_), channel_id=1, source_target_pairs={{0,2},{2,0},{4,6},{6,4},{8,10},{10,8},{12,14},{14,12},{1,3},{3,1},... | collective-permute-start | bytes 208904 | tf_op jit(solution)/shard_map/ppermute | solution.py:425
  26.4 0.1 collective-permute-done.6.refs_1_
  26.5 0.5 collective-permute-start.10
  27.0 1.5 %collective-permute-done.7.refs_2_ = f32[136,128]{1,0:T(8,128)S(1)} collective-permute-done((f32[136,128]{1,0:T(8,128)S(1)}, f32[136,128]{1,0:T(8,128)S(1)}, u32[]{:S(2)}, u32[]{:S(2)}) %collective-permute-start.7) | collective-permute-done | bytes 69664 | tf_op jit(solution)/shard_map/ppermute | solution.py:425
  28.5 0.0 collective-permute-start.11
  28.5 1.1 %collective-permute-done.8.refs_3_ = f32[136,128]{1,0:T(8,128)S(1)} collective-permute-done((f32[136,128]{1,0:T(8,128)S(1)}, f32[136,128]{1,0:T(8,128)S(1)}, u32[]{:S(2)}, u32[]{:S(2)}) %collective-permute-start.8) | collective-permute-done | bytes 69664 | tf_op jit(solution)/shard_map/ppermute | solution.py:425
  29.6 0.9 %inverse.2.refs_11_ = f32[32,128]{1,0:T(8,128)S(1)} custom-call(f32[32,128]{1,0:T(8,128)S(1)} %get-tuple-element.33.norm_ref.refs_10_), custom_call_target="tpu_custom_call" | custom-call | tf_op jit(solution)/shard_map/inverse/pallas_call | solution.py:528
  30.5 0.1 collect.1
  30.6 0.0 collective-permute-done.10.refs_5_
  30.6 0.0 collective-permute-done.11.refs_6_
  30.6 0.2 collective-permute-done.12.refs_7_
  30.8 3.1 %step.2 = (f32[32,512]{1,0:T(8,128)S(1)}, f32[9,32,256]{2,1,0:T(8,128)S(1)}, f32[2,8,32,256]{3,2,1,0:T(8,128)S(1)}, f32[32,128]{1,0:T(8,128)S(1)}, f32[32,256]{1,0:T(8,128)S(1)}) custom-call(f32[136,128]{1,0:T(8,128)S(1)} %get-tuple-element.29.refs_0_, f32[136,128]{1,0:T(8,128)S(1)} %collective-permute-done.6.refs_1_, ...), custom_call_target="tpu_custom_call" | custom-call | tf_op jit(solution)/shard_map/step/pallas_call | solution.py:537
  33.9 0.3 collective-permute-start.14
  34.2 1.0 %collective-permute-done.14.other_ref = f32[32,512]{1,0:T(8,128)S(1)} collective-permute-done((f32[32,512]{1,0:T(8,128)S(1)}, f32[32,512]{1,0:T(8,128)S(1)}, u32[]{:S(2)}, u32[]{:S(2)}) %collective-permute-start.14) | collective-permute-done | bytes 65568 | tf_op jit(solution)/shard_map/ppermute | solution.py:407
  35.2 0.3 image.3.refs_0_
  35.5 2.5 %collective-permute-start.15 = (f32[136,128]{1,0:T(8,128)S(1)}, f32[136,128]{1,0:T(8,128)S(1)}, u32[]{:S(2)}, u32[]{:S(2)}) collective-permute-start(f32[136,128]{1,0:T(8,128)S(1)} %image.3.refs_0_), channel_id=1, source_target_pairs={{0,14},{2,12},{4,10},{6,8},{8,6},{10,4},{12,2},{14,0},{1,11},{3,9}... | collective-permute-start | bytes 208904 | tf_op jit(solution)/shard_map/ppermute | solution.py:425
  38.0 0.3 collective-permute-start.16
  38.3 2.8 %collective-permute-start.17 = (f32[136,128]{1,0:T(8,128)S(1)}, f32[136,128]{1,0:T(8,128)S(1)}, u32[]{:S(2)}, u32[]{:S(2)}) collective-permute-start(f32[136,128]{1,0:T(8,128)S(1)} %image.3.refs_0_), channel_id=1, source_target_pairs={{0,4},{2,6},{4,0},{6,2},{8,12},{10,14},{12,8},{14,10},{1,9},{3,11}... | collective-permute-start | bytes 208904 | tf_op jit(solution)/shard_map/ppermute | solution.py:425
  41.1 0.5 collective-permute-start.18
  41.5 1.6 %collective-permute-done.15.refs_1_ = f32[136,128]{1,0:T(8,128)S(1)} collective-permute-done((f32[136,128]{1,0:T(8,128)S(1)}, f32[136,128]{1,0:T(8,128)S(1)}, u32[]{:S(2)}, u32[]{:S(2)}) %collective-permute-start.15) | collective-permute-done | bytes 69664 | tf_op jit(solution)/shard_map/ppermute | solution.py:425
  43.1 0.0 collective-permute-start.19
  43.1 1.0 %collective-permute-done.16.refs_2_ = f32[136,128]{1,0:T(8,128)S(1)} collective-permute-done((f32[136,128]{1,0:T(8,128)S(1)}, f32[136,128]{1,0:T(8,128)S(1)}, u32[]{:S(2)}, u32[]{:S(2)}) %collective-permute-start.16) | collective-permute-done | bytes 69664 | tf_op jit(solution)/shard_map/ppermute | solution.py:425
  44.1 0.0 collective-permute-start.20
  44.1 1.3 %collective-permute-done.17.refs_3_ = f32[136,128]{1,0:T(8,128)S(1)} collective-permute-done((f32[136,128]{1,0:T(8,128)S(1)}, f32[136,128]{1,0:T(8,128)S(1)}, u32[]{:S(2)}, u32[]{:S(2)}) %collective-permute-start.17) | collective-permute-done | bytes 69664 | tf_op jit(solution)/shard_map/ppermute | solution.py:425
  45.4 0.9 %inverse.3.refs_11_ = f32[32,128]{1,0:T(8,128)S(1)} custom-call(f32[32,128]{1,0:T(8,128)S(1)} %get-tuple-element.37.norm_ref.refs_10_), custom_call_target="tpu_custom_call" | custom-call | tf_op jit(solution)/shard_map/inverse/pallas_call | solution.py:528
  46.4 0.0 collective-permute-done.19.refs_5_
  46.4 0.0 collective-permute-done.20.refs_6_
  46.4 0.3 collective-permute-done.21.refs_7_
  46.7 3.0 %step.3 = (f32[32,512]{1,0:T(8,128)S(1)}, f32[2,32,256]{2,1,0:T(8,128)S(1)}, f32[32,256]{1,0:T(8,128)S(1)}, f32[32,128]{1,0:T(8,128)S(1)}, f32[32,256]{1,0:T(8,128)S(1)}) custom-call(f32[136,128]{1,0:T(8,128)S(1)} %image.3.refs_0_, f32[136,128]{1,0:T(8,128)S(1)} %collective-permute-done.15.refs_1_, f32[136,128]{1,0:T(8,128)S(1)} %collective-permute-done.16.refs_2_, ...), custom_call_target="tpu_custom_call" | custom-call | tf_op jit(solution)/shard_map/step/pallas_call | solution.py:537
  49.7 0.2 collective-permute-start.22
  50.0 1.0 %collective-permute-done.22.other_ref = f32[32,512]{1,0:T(8,128)S(1)} collective-permute-done((f32[32,512]{1,0:T(8,128)S(1)}, f32[32,512]{1,0:T(8,128)S(1)}, u32[]{:S(2)}, u32[]{:S(2)}) %collective-permute-start.22) | collective-permute-done | bytes 65568 | tf_op jit(solution)/shard_map/ppermute | solution.py:407
  51.0 0.3 last_image.1
  51.4 2.3 %collective-permute-start.23 = (f32[8,128]{1,0:T(8,128)S(1)}, f32[8,128]{1,0:T(8,128)S(1)}, u32[]{:S(2)}, u32[]{:S(2)}) collective-permute-start(f32[8,128]{1,0:T(8,128)S(1)} %get-tuple-element.41.refs_0_), channel_id=1, source_target_pairs={{0,14},{2,12},{4,10},{6,8},{8,6},{10,4},{12,2},{14,0},{1,11},{3,9}... | collective-permute-start | bytes 12296 | tf_op jit(solution)/shard_map/ppermute | solution.py:425
  53.7 0.0 collective-permute-start.24
  53.7 2.4 %collective-permute-start.25 = (f32[8,128]{1,0:T(8,128)S(1)}, f32[8,128]{1,0:T(8,128)S(1)}, u32[]{:S(2)}, u32[]{:S(2)}) collective-permute-start(f32[8,128]{1,0:T(8,128)S(1)} %get-tuple-element.41.refs_0_), channel_id=1, source_target_pairs={{0,4},{2,6},{4,0},{6,2},{8,12},{10,14},{12,8},{14,10},{1,9},{3,11}... | collective-permute-start | bytes 12296 | tf_op jit(solution)/shard_map/ppermute | solution.py:425
  56.1 1.0 %collective-permute-start.26 = (f32[8,128]{1,0:T(8,128)S(1)}, f32[8,128]{1,0:T(8,128)S(1)}, u32[]{:S(2)}, u32[]{:S(2)}) collective-permute-start(f32[8,128]{1,0:T(8,128)S(1)} %get-tuple-element.41.refs_0_), channel_id=1, source_target_pairs={{0,2},{2,0},{4,6},{6,4},{8,10},{10,8},{12,14},{14,12},{1,3},{3,1},... | collective-permute-start | bytes 12296 | tf_op jit(solution)/shard_map/ppermute | solution.py:425
  57.1 0.5 collective-permute-done.23.refs_1_
  57.7 0.0 collective-permute-start.27
  57.7 0.5 collective-permute-done.24.refs_2_
  58.2 0.0 collective-permute-start.28
  58.2 0.0 collective-permute-done.25.refs_3_
  58.2 0.5 collective-permute-start.29
  58.7 1.0 %collective-permute-done.26.refs_4_ = f32[8,128]{1,0:T(8,128)S(1)} collective-permute-done((f32[8,128]{1,0:T(8,128)S(1)}, f32[8,128]{1,0:T(8,128)S(1)}, u32[]{:S(2)}, u32[]{:S(2)}) %collective-permute-start.26) | collective-permute-done | bytes 4128 | tf_op jit(solution)/shard_map/ppermute | solution.py:425
  59.7 1.7 %last.1 = (f32[32,256]{1,0:T(8,128)}, f32[32,256]{1,0:T(8,128)}) custom-call(f32[8,128]{1,0:T(8,128)S(1)} %get-tuple-element.41.refs_0_, f32[8,128]{1,0:T(8,128)S(1)} %collective-permute-done.23.refs_1_, f32[8,128]{1,0:T(8,128)S(1)} %collective-permute-done.24.refs_2_, f32[8,128]{1,0:T(8,128)S(1)} %collective-permute-done.25.refs_3_, ...), custom_call_target="tpu_custom_call" | custom-call | tf_op jit(solution)/shard_map/last/pallas_call | solution.py:560
  (10 shorter events, 0.0 us)
Async XLA Ops:
  1.5 8.6 %collective-permute-start = (f32[32,256]{1,0:T(8,128)S(1)}, f32[32,256]{1,0:T(8,128)S(1)}, u32[]{:S(2)}, u32[]{:S(2)}) collective-permute-start(f32[32,256]{1,0:T(8,128)S(1)} %multiply_multiply_fusion.refs_3_), channel_id=1, source_target_pairs={{0,12},{2,14},{4,8},{6,10},{8,4},{10,6},{12,0},{14,2},{1,13},{3,15... | collective-permute-start | bytes 98312 | tf_op jit(solution)/shard_map/ppermute | solution.py:404
  6.5 4.8 %collective-permute-start.1 = (f32[32,256]{1,0:T(8,128)S(1)}, f32[32,256]{1,0:T(8,128)S(1)}, u32[]{:S(2)}, u32[]{:S(2)}) collective-permute-start(f32[32,256]{1,0:T(8,128)S(1)} %multiply_multiply_fusion.refs_3_), channel_id=1, source_target_pairs={{0,8},{2,10},{4,12},{6,14},{8,0},{10,2},{12,4},{14,6},{1,9},{3,11}... | collective-permute-start | bytes 98312 | tf_op jit(solution)/shard_map/ppermute | solution.py:404
  6.5 4.8 %collective-permute-start.2 = (f32[32,256]{1,0:T(8,128)S(1)}, f32[32,256]{1,0:T(8,128)S(1)}, u32[]{:S(2)}, u32[]{:S(2)}) collective-permute-start(f32[32,256]{1,0:T(8,128)S(1)} %multiply_multiply_fusion.refs_3_), channel_id=1, source_target_pairs={{0,4},{2,6},{4,0},{6,2},{8,12},{10,14},{12,8},{14,10},{1,5},{3,7},... | collective-permute-start | bytes 98312 | tf_op jit(solution)/shard_map/ppermute | solution.py:404
  11.4 5.0 %collective-permute-start.3 = (f32[4,32,256]{2,1,0:T(8,128)S(1)}, f32[4,32,256]{2,1,0:T(8,128)S(1)}, u32[]{:S(2)}, u32[]{:S(2)}) collective-permute-start(f32[4,32,256]{2,1,0:T(8,128)S(1)} %join.1.joined_ref.even_ref.near_ref), channel_id=1, source_target_pairs={{0,2},{2,0},{4,6},{6,4},{8,10},{10,8},{12,14},{14,12},{1,3},{3,1},... | collective-permute-start | bytes 393224 | tf_op jit(solution)/shard_map/ppermute | solution.py:404
  17.3 1.4 %collective-permute-start.4 = (f32[32,640]{1,0:T(8,128)S(1)}, f32[32,640]{1,0:T(8,128)S(1)}, u32[]{:S(2)}, u32[]{:S(2)}) collective-permute-start(f32[32,640]{1,0:T(8,128)S(1)} %get-tuple-element.27.mine_ref), channel_id=1, source_target_pairs={{0,1},{1,0},{2,3},{3,2},{4,5},{5,4},{6,7},{7,6},{8,9},{9,8},{10,11... | collective-permute-start | bytes 245768 | tf_op jit(solution)/shard_map/ppermute | solution.py:407
  17.3 1.4 %collective-permute-start.5 = (f32[32,256]{1,0:T(8,128)S(1)}, f32[32,256]{1,0:T(8,128)S(1)}, u32[]{:S(2)}, u32[]{:S(2)}) collective-permute-start(f32[32,256]{1,0:T(8,128)S(1)} %multiply_multiply_fusion.refs_3_), channel_id=1, source_target_pairs={{0,1},{1,0},{2,3},{3,2},{4,5},{5,4},{6,7},{7,6},{8,9},{9,8},{10,11... | collective-permute-start | bytes 98312 | tf_op jit(solution)/shard_map/ppermute | solution.py:407
  19.0 11.5 %collective-permute-start.13 = (f32[8,32,256]{2,1,0:T(8,128)S(1)}, f32[8,32,256]{2,1,0:T(8,128)S(1)}, u32[]{:S(2)}, u32[]{:S(2)}) collective-permute-start(f32[8,32,256]{2,1,0:T(8,128)S(1)} %get-tuple-element.30.near_ref), channel_id=1, source_target_pairs={{0,1},{1,0},{2,3},{3,2},{4,5},{5,4},{6,7},{7,6},{8,9},{9,8},{10,11... | collective-permute-start | bytes 786440 | tf_op jit(solution)/shard_map/ppermute | solution.py:407
  19.4 7.1 %collective-permute-start.6 = (f32[136,128]{1,0:T(8,128)S(1)}, f32[136,128]{1,0:T(8,128)S(1)}, u32[]{:S(2)}, u32[]{:S(2)}) collective-permute-start(f32[136,128]{1,0:T(8,128)S(1)} %get-tuple-element.29.refs_0_), channel_id=1, source_target_pairs={{0,14},{2,12},{4,10},{6,8},{8,6},{10,4},{12,2},{14,0},{1,11},{3,9}... | collective-permute-start | bytes 208904 | tf_op jit(solution)/shard_map/ppermute | solution.py:425
  22.9 5.6 %collective-permute-start.7 = (f32[136,128]{1,0:T(8,128)S(1)}, f32[136,128]{1,0:T(8,128)S(1)}, u32[]{:S(2)}, u32[]{:S(2)}) collective-permute-start(f32[136,128]{1,0:T(8,128)S(1)} %get-tuple-element.29.refs_0_), channel_id=1, source_target_pairs={{0,6},{2,4},{4,2},{6,0},{8,14},{10,12},{12,10},{14,8},{1,13},{3,15... | collective-permute-start | bytes 208904 | tf_op jit(solution)/shard_map/ppermute | solution.py:425
  22.9 6.7 %collective-permute-start.8 = (f32[136,128]{1,0:T(8,128)S(1)}, f32[136,128]{1,0:T(8,128)S(1)}, u32[]{:S(2)}, u32[]{:S(2)}) collective-permute-start(f32[136,128]{1,0:T(8,128)S(1)} %get-tuple-element.29.refs_0_), channel_id=1, source_target_pairs={{0,4},{2,6},{4,0},{6,2},{8,12},{10,14},{12,8},{14,10},{1,9},{3,11}... | collective-permute-start | bytes 208904 | tf_op jit(solution)/shard_map/ppermute | solution.py:425
  24.9 5.7 %collective-permute-start.9 = (f32[136,128]{1,0:T(8,128)S(1)}, f32[136,128]{1,0:T(8,128)S(1)}, u32[]{:S(2)}, u32[]{:S(2)}) collective-permute-start(f32[136,128]{1,0:T(8,128)S(1)} %get-tuple-element.29.refs_0_), channel_id=1, source_target_pairs={{0,2},{2,0},{4,6},{6,4},{8,10},{10,8},{12,14},{14,12},{1,3},{3,1},... | collective-permute-start | bytes 208904 | tf_op jit(solution)/shard_map/ppermute | solution.py:425
  26.5 4.1 %collective-permute-start.10 = (f32[136,128]{1,0:T(8,128)S(1)}, f32[136,128]{1,0:T(8,128)S(1)}, u32[]{:S(2)}, u32[]{:S(2)}) collective-permute-start(f32[136,128]{1,0:T(8,128)S(1)} %collective-permute-done.6.refs_1_), channel_id=1, source_target_pairs={{0,1},{1,0},{2,3},{3,2},{4,5},{5,4},{6,7},{7,6},{8,9},{9,8},{10,11... | collective-permute-start | bytes 208904 | tf_op jit(solution)/shard_map/ppermute | solution.py:407
  28.5 2.1 %collective-permute-start.11 = (f32[136,128]{1,0:T(8,128)S(1)}, f32[136,128]{1,0:T(8,128)S(1)}, u32[]{:S(2)}, u32[]{:S(2)}) collective-permute-start(f32[136,128]{1,0:T(8,128)S(1)} %collective-permute-done.7.refs_2_), channel_id=1, source_target_pairs={{0,1},{1,0},{2,3},{3,2},{4,5},{5,4},{6,7},{7,6},{8,9},{9,8},{10,11... | collective-permute-start | bytes 208904 | tf_op jit(solution)/shard_map/ppermute | solution.py:407
  29.6 1.3 %collective-permute-start.12 = (f32[136,128]{1,0:T(8,128)S(1)}, f32[136,128]{1,0:T(8,128)S(1)}, u32[]{:S(2)}, u32[]{:S(2)}) collective-permute-start(f32[136,128]{1,0:T(8,128)S(1)} %collective-permute-done.8.refs_3_), channel_id=1, source_target_pairs={{0,1},{1,0},{2,3},{3,2},{4,5},{5,4},{6,7},{7,6},{8,9},{9,8},{10,11... | collective-permute-start | bytes 208904 | tf_op jit(solution)/shard_map/ppermute | solution.py:407
  33.9 1.3 %collective-permute-start.14 = (f32[32,512]{1,0:T(8,128)S(1)}, f32[32,512]{1,0:T(8,128)S(1)}, u32[]{:S(2)}, u32[]{:S(2)}) collective-permute-start(f32[32,512]{1,0:T(8,128)S(1)} %get-tuple-element.34.mine_ref), channel_id=1, source_target_pairs={{0,1},{1,0},{2,3},{3,2},{4,5},{5,4},{6,7},{7,6},{8,9},{9,8},{10,11... | collective-permute-start | bytes 196616 | tf_op jit(solution)/shard_map/ppermute | solution.py:407
  35.5 7.6 %collective-permute-start.15 = (f32[136,128]{1,0:T(8,128)S(1)}, f32[136,128]{1,0:T(8,128)S(1)}, u32[]{:S(2)}, u32[]{:S(2)}) collective-permute-start(f32[136,128]{1,0:T(8,128)S(1)} %image.3.refs_0_), channel_id=1, source_target_pairs={{0,14},{2,12},{4,10},{6,8},{8,6},{10,4},{12,2},{14,0},{1,11},{3,9}... | collective-permute-start | bytes 208904 | tf_op jit(solution)/shard_map/ppermute | solution.py:425
  38.0 6.1 %collective-permute-start.16 = (f32[136,128]{1,0:T(8,128)S(1)}, f32[136,128]{1,0:T(8,128)S(1)}, u32[]{:S(2)}, u32[]{:S(2)}) collective-permute-start(f32[136,128]{1,0:T(8,128)S(1)} %image.3.refs_0_), channel_id=1, source_target_pairs={{0,6},{2,4},{4,2},{6,0},{8,14},{10,12},{12,10},{14,8},{1,13},{3,15... | collective-permute-start | bytes 208904 | tf_op jit(solution)/shard_map/ppermute | solution.py:425
  38.3 7.1 %collective-permute-start.17 = (f32[136,128]{1,0:T(8,128)S(1)}, f32[136,128]{1,0:T(8,128)S(1)}, u32[]{:S(2)}, u32[]{:S(2)}) collective-permute-start(f32[136,128]{1,0:T(8,128)S(1)} %image.3.refs_0_), channel_id=1, source_target_pairs={{0,4},{2,6},{4,0},{6,2},{8,12},{10,14},{12,8},{14,10},{1,9},{3,11}... | collective-permute-start | bytes 208904 | tf_op jit(solution)/shard_map/ppermute | solution.py:425
  41.1 5.3 %collective-permute-start.18 = (f32[136,128]{1,0:T(8,128)S(1)}, f32[136,128]{1,0:T(8,128)S(1)}, u32[]{:S(2)}, u32[]{:S(2)}) collective-permute-start(f32[136,128]{1,0:T(8,128)S(1)} %image.3.refs_0_), channel_id=1, source_target_pairs={{0,2},{2,0},{4,6},{6,4},{8,10},{10,8},{12,14},{14,12},{1,3},{3,1},... | collective-permute-start | bytes 208904 | tf_op jit(solution)/shard_map/ppermute | solution.py:425
  43.1 3.3 %collective-permute-start.19 = (f32[136,128]{1,0:T(8,128)S(1)}, f32[136,128]{1,0:T(8,128)S(1)}, u32[]{:S(2)}, u32[]{:S(2)}) collective-permute-start(f32[136,128]{1,0:T(8,128)S(1)} %collective-permute-done.15.refs_1_), channel_id=1, source_target_pairs={{0,1},{1,0},{2,3},{3,2},{4,5},{5,4},{6,7},{7,6},{8,9},{9,8},{10,11... | collective-permute-start | bytes 208904 | tf_op jit(solution)/shard_map/ppermute | solution.py:407
  44.1 2.3 %collective-permute-start.20 = (f32[136,128]{1,0:T(8,128)S(1)}, f32[136,128]{1,0:T(8,128)S(1)}, u32[]{:S(2)}, u32[]{:S(2)}) collective-permute-start(f32[136,128]{1,0:T(8,128)S(1)} %collective-permute-done.16.refs_2_), channel_id=1, source_target_pairs={{0,1},{1,0},{2,3},{3,2},{4,5},{5,4},{6,7},{7,6},{8,9},{9,8},{10,11... | collective-permute-start | bytes 208904 | tf_op jit(solution)/shard_map/ppermute | solution.py:407
  45.4 1.3 %collective-permute-start.21 = (f32[136,128]{1,0:T(8,128)S(1)}, f32[136,128]{1,0:T(8,128)S(1)}, u32[]{:S(2)}, u32[]{:S(2)}) collective-permute-start(f32[136,128]{1,0:T(8,128)S(1)} %collective-permute-done.17.refs_3_), channel_id=1, source_target_pairs={{0,1},{1,0},{2,3},{3,2},{4,5},{5,4},{6,7},{7,6},{8,9},{9,8},{10,11... | collective-permute-start | bytes 208904 | tf_op jit(solution)/shard_map/ppermute | solution.py:407
  49.7 1.3 %collective-permute-start.22 = (f32[32,512]{1,0:T(8,128)S(1)}, f32[32,512]{1,0:T(8,128)S(1)}, u32[]{:S(2)}, u32[]{:S(2)}) collective-permute-start(f32[32,512]{1,0:T(8,128)S(1)} %get-tuple-element.39.mine_ref), channel_id=1, source_target_pairs={{0,1},{1,0},{2,3},{3,2},{4,5},{5,4},{6,7},{7,6},{8,9},{9,8},{10,11... | collective-permute-start | bytes 196616 | tf_op jit(solution)/shard_map/ppermute | solution.py:407
  51.4 6.3 %collective-permute-start.23 = (f32[8,128]{1,0:T(8,128)S(1)}, f32[8,128]{1,0:T(8,128)S(1)}, u32[]{:S(2)}, u32[]{:S(2)}) collective-permute-start(f32[8,128]{1,0:T(8,128)S(1)} %get-tuple-element.41.refs_0_), channel_id=1, source_target_pairs={{0,14},{2,12},{4,10},{6,8},{8,6},{10,4},{12,2},{14,0},{1,11},{3,9}... | collective-permute-start | bytes 12296 | tf_op jit(solution)/shard_map/ppermute | solution.py:425
  53.7 4.5 %collective-permute-start.24 = (f32[8,128]{1,0:T(8,128)S(1)}, f32[8,128]{1,0:T(8,128)S(1)}, u32[]{:S(2)}, u32[]{:S(2)}) collective-permute-start(f32[8,128]{1,0:T(8,128)S(1)} %get-tuple-element.41.refs_0_), channel_id=1, source_target_pairs={{0,6},{2,4},{4,2},{6,0},{8,14},{10,12},{12,10},{14,8},{1,13},{3,15... | collective-permute-start | bytes 12296 | tf_op jit(solution)/shard_map/ppermute | solution.py:425
  53.7 4.5 %collective-permute-start.25 = (f32[8,128]{1,0:T(8,128)S(1)}, f32[8,128]{1,0:T(8,128)S(1)}, u32[]{:S(2)}, u32[]{:S(2)}) collective-permute-start(f32[8,128]{1,0:T(8,128)S(1)} %get-tuple-element.41.refs_0_), channel_id=1, source_target_pairs={{0,4},{2,6},{4,0},{6,2},{8,12},{10,14},{12,8},{14,10},{1,9},{3,11}... | collective-permute-start | bytes 12296 | tf_op jit(solution)/shard_map/ppermute | solution.py:425
  56.1 3.6 %collective-permute-start.26 = (f32[8,128]{1,0:T(8,128)S(1)}, f32[8,128]{1,0:T(8,128)S(1)}, u32[]{:S(2)}, u32[]{:S(2)}) collective-permute-start(f32[8,128]{1,0:T(8,128)S(1)} %get-tuple-element.41.refs_0_), channel_id=1, source_target_pairs={{0,2},{2,0},{4,6},{6,4},{8,10},{10,8},{12,14},{14,12},{1,3},{3,1},... | collective-permute-start | bytes 12296 | tf_op jit(solution)/shard_map/ppermute | solution.py:425
  57.7 2.0 %collective-permute-start.27 = (f32[8,128]{1,0:T(8,128)S(1)}, f32[8,128]{1,0:T(8,128)S(1)}, u32[]{:S(2)}, u32[]{:S(2)}) collective-permute-start(f32[8,128]{1,0:T(8,128)S(1)} %collective-permute-done.23.refs_1_), channel_id=1, source_target_pairs={{0,1},{1,0},{2,3},{3,2},{4,5},{5,4},{6,7},{7,6},{8,9},{9,8},{10,11... | collective-permute-start | bytes 12296 | tf_op jit(solution)/shard_map/ppermute | solution.py:407
  58.2 1.6 %collective-permute-start.28 = (f32[8,128]{1,0:T(8,128)S(1)}, f32[8,128]{1,0:T(8,128)S(1)}, u32[]{:S(2)}, u32[]{:S(2)}) collective-permute-start(f32[8,128]{1,0:T(8,128)S(1)} %collective-permute-done.24.refs_2_), channel_id=1, source_target_pairs={{0,1},{1,0},{2,3},{3,2},{4,5},{5,4},{6,7},{7,6},{8,9},{9,8},{10,11... | collective-permute-start | bytes 12296 | tf_op jit(solution)/shard_map/ppermute | solution.py:407
  58.2 1.5 %collective-permute-start.29 = (f32[8,128]{1,0:T(8,128)S(1)}, f32[8,128]{1,0:T(8,128)S(1)}, u32[]{:S(2)}, u32[]{:S(2)}) collective-permute-start(f32[8,128]{1,0:T(8,128)S(1)} %collective-permute-done.25.refs_3_), channel_id=1, source_target_pairs={{0,1},{1,0},{2,3},{3,2},{4,5},{5,4},{6,7},{7,6},{8,9},{9,8},{10,11... | collective-permute-start | bytes 12296 | tf_op jit(solution)/shard_map/ppermute | solution.py:407

commit v12 on v11

--- a/solution.py
+++ b/solution.py
@@ -245,8 +245,8 @@
     lax.fori_loop(0, total.shape[0] // row_blocks, part, 0)
 
 
-def join_kernel(*refs):
-    for k, ref in enumerate(reversed(refs[:-2])):
+def join_kernel(order, *refs):
+    for k, ref in zip(order, refs):
         refs[-1][k] = ref[...]
 
 
@@ -285,7 +285,7 @@
 
 
 def image_kernel(first, mine_ref, other_ref, near_ref, far_ref, *refs):
-    out_ref, norm_ref = refs[1:3] if first else (refs[0], None)
+    out_ref, norm_ref = refs if first else (refs[0], None)
     core = lax.axis_index("col")
     size, width = near_ref.shape[1:]
     near, far = add_halves(mine_ref, other_ref, width)
@@ -319,8 +319,7 @@
     return jnp.where(core == 0, refs[places[0]][rows], refs[places[1]][rows])
 
 
-def step_kernel(places, with_solution, last, *refs):
-    used = 1 + max(max(pair) for pair in places)
+def step_kernel(used, places, with_solution, last, *refs):
     images, refs = refs[:used], refs[used:]
     direction_ref, residual_ref, norm_ref, inverse_ref, matrix = refs[:5]
     refs = refs[5:]
@@ -376,8 +375,7 @@
     gram_ref[...] = pack(finish(products))
 
 
-def last_kernel(places, *refs):
-    used = 1 + max(max(pair) for pair in places)
+def last_kernel(used, places, *refs):
     image_ref, direction_ref, residual_ref, norm_ref, solution_ref = refs[used:-2]
     new_solution, new_residual = refs[-2:]
     core = lax.axis_index("col")
@@ -412,24 +410,21 @@
         if pieces != 8:
             found = [value] + [swap(value, k) for k in range(1, pieces)]
             return found, [(k, k) for k in range(pieces)]
-        shares = ((7, 5), (3, 6), (2, 4), (1, 1))
-        fetched = []
-        passed = []
-        places = {0: (0, 0)}
-        for turn, masks in enumerate(shares, 1):
+        turns = ((2, 4), (7, 6), (1, 2))
+
+        def fetch(source, masks):
             pairs = [
                 (i * 2 + core, (i ^ mask) * 2 + core)
                 for core, mask in enumerate(masks)
                 for i in range(pieces)
             ]
-            fetched.append(lax.ppermute(value, ("row", "col"), pairs))
-            if masks[0] == masks[1]:
-                places[masks[0]] = (turn, turn)
-            else:
-                passed.append(across(fetched[-1]))
-                places[masks[0]] = (turn, turn + len(shares))
-                places[masks[1]] = (turn + len(shares), turn)
-        return [value, *fetched, *passed], [places[k] for k in range(pieces)]
+            return lax.ppermute(source, ("row", "col"), pairs)
+
+        fetched = [fetch(value, masks) for masks in turns]
+        fetched.append(fetch(fetched[0], (1, 1)))
+        found = [value, *fetched, *map(across, fetched)]
+        places = [(0, 0), (3, 7), (1, 5), (4, 8), (5, 1), (8, 4), (6, 2), (2, 6)]
+        return found, places
 
     right_side = signs.astype(F32) * vertex_weight[None, :] * column_scale[:, None]
     far_side = across(right_side)[None]
@@ -461,14 +456,15 @@
         name="gather",
     )(tile_count, *lists, pltpu.with_memory_space_constraint(tiles, pltpu.HBM))
     joined = shape(pieces // 2, sketch, rows_dev)
+    order = [*range(pieces // 4, pieces // 2), *range(1, pieces // 4), 0]
     even = pl.pallas_call(
-        join_kernel,
+        functools.partial(join_kernel, order),
         out_shape=joined,
         in_specs=[VMEM] * (pieces // 2) + [ANY],
         out_specs=VMEM,
         compiler_params=params(joined, joined),
         name="join",
-    )(*reversed(even), blocks_sum)
+    )(*[even[k] for k in order], blocks_sum)
     odd = swap(even, 1)
     dense, _ = pl.pallas_call(
         functools.partial(dense_kernel, rows_dev),
@@ -504,18 +500,18 @@
         first = iteration == 0
         last = iteration == ITERS - 2
         sums = (partial_sum, across(partial_sum))
-        given = (even, far_side, blocks) if first else (direction, direction)
+        given = (even, far_side) if first else (direction, direction)
         outs = pl.pallas_call(
             functools.partial(image_kernel, first),
-            out_shape=(payload, small, blocks) if first else (payload,),
-            in_specs=[VMEM] * 4 + [ANY] * (len(given) - 2),
-            out_specs=(VMEM, VMEM, ANY) if first else (VMEM,),
-            input_output_aliases={4: 2} if first else {},
+            out_shape=(payload, small) if first else (payload,),
+            in_specs=[VMEM] * 4,
+            out_specs=(VMEM, VMEM) if first else (VMEM,),
             compiler_params=params(state, payload),
             name="image",
         )(*sums, *given)
+        found, places = exchange(outs[0])
         if first:
-            norm, blocks = outs[1:]
+            norm = outs[1]
             residual, direction = pl.pallas_call(
                 collect_kernel,
                 out_shape=(held, state),
@@ -524,7 +520,6 @@
                 compiler_params=params(held, held, state),
                 name="collect",
             )(blocks, across(blocks))
-        found, places = exchange(outs[0])
         inverse = pl.pallas_call(
             inverse_kernel,
             out_shape=small,
@@ -535,7 +530,7 @@
         )(norm)
         given = () if first else (solution,)
         partial_sum, direction, residual, norm, solution = pl.pallas_call(
-            functools.partial(step_kernel, places, not first, last),
+            functools.partial(step_kernel, len(found), places, not first, last),
             out_shape=(
                 shape(sketch, group),
                 shape(2, sketch, rows_dev) if last else state,
@@ -558,7 +553,7 @@
     )(partial_sum, across(partial_sum), direction)
     found, places = exchange(gram)
     return pl.pallas_call(
-        functools.partial(last_kernel, places),
+        functools.partial(last_kernel, len(found), places),
         out_shape=(piece, piece),
         in_specs=[VMEM] * (len(found) + 5),
         out_specs=(VMEM, VMEM),

time: 61.5 us -> 62 us (level); the launches traced: 61.4 us -> 61.2 us
  starting transfers between devices: 28.6 us -> 25.5 us
  waiting for transfers between devices: 14.5 us -> 17.3 us
    ppermute x12, starting transfers between devices: 18.8 us -> 15.7 us  [fetch(): return lax.ppermute(source, ('row', 'col'), pairs)]
    ppermute x12, waiting for transfers between devices: 8.61 us -> 10.1 us  [fetch(): return lax.ppermute(source, ('row', 'col'), pairs)]
    ppermute x14 -> x17, waiting for transfers between devices: 3.37 us -> 4.81 us  [across(): lax.ppermute(value, 'col', [(i, (i + 1) % col_devices) for i in range(col...]
    ppermute x14 -> x17, starting transfers between devices: 2.5 us -> 2.56 us  [across(): lax.ppermute(value, 'col', [(i, (i + 1) % col_devices) for i in range(col...]
  transfers between devices with their start and end apart: 30 -> 33, of which waited for: 16 -> 19; matrix products, arithmetic and copies ran while one was open for 0% -> 0% of each run, Pallas kernels for 10% -> 11%
where the time goes in v12:
time: 62 us; the launch traced here: 61.2 us
  starting transfers between devices  25.5 us (41%)
  waiting for transfers between devices  17.3 us (28%)
  Pallas kernels  16.1 us (26%)
  between operations  1.43 us (2%)
  other arithmetic  0.85 us (1%)
    ppermute x12, starting transfers between devices, fetch(): return lax.ppermute(source, ('row', 'col'), pairs)  15.7 us
    ppermute x12, waiting for transfers between devices, fetch(): return lax.ppermute(source, ('row', 'col'), pairs)  10.1 us
    ppermute x4, starting transfers between devices, swap(): return lax.ppermute(value, 'row', [(i, i ^ mask) for i in range(pieces)])  7.2 us
    pallas_call x2, Pallas kernels, per_device(): pl.pallas_call(functools.partial(step_kernel, len(found), places, not fir...  6.12 us
    ppermute x17, waiting for transfers between devices, across(): lax.ppermute(value, 'col', [(i, (i + 1) % col_devices) for i in range(col...  4.81 us
    ppermute x17, starting transfers between devices, across(): lax.ppermute(value, 'col', [(i, (i + 1) % col_devices) for i in range(col...  2.56 us
    ppermute x4, waiting for transfers between devices, swap(): return lax.ppermute(value, 'row', [(i, i ^ mask) for i in range(pieces)])  2.41 us
    pallas_call x1, Pallas kernels, per_device(): pl.pallas_call(functools.partial(gather_kernel, rows_dev), out_shape=(tot...  2.27 us
  transfers between devices with their start and end apart: 33, of which 19 were waited for; matrix products, arithmetic and copies ran while one was open for 0% of the time, Pallas kernels for 11%

profile of v12, /device:TPU:0, one launch (start us, length us, event | category | flops | bytes accessed | tf_op | source)
XLA Modules:
  0.0 61.2 jit_solution(15872641854966914419)
XLA Ops:
  0.6 0.8 %multiply_multiply_fusion.refs_3_ = f32[32,256]{1,0:T(8,128)S(1)} fusion(s32[32,256]{1,0:T(8,128)} %param.11, f32[32]{0:T(128)} %param.13, f32[256]{0:T(256)} %param.12), kind=kLoop, calls=%fused_computation | loop fusion | flops 24576 | bytes 66688 | tf_op jit(solution)/shard_map/mul | solution.py:429
  1.5 4.0 %collective-permute-start = (f32[32,256]{1,0:T(8,128)S(1)}, f32[32,256]{1,0:T(8,128)S(1)}, u32[]{:S(2)}, u32[]{:S(2)}) collective-permute-start(f32[32,256]{1,0:T(8,128)S(1)} %multiply_multiply_fusion.refs_3_), channel_id=1, source_target_pairs={{0,8},{2,10},{4,12},{6,14},{8,0},{10,2},{12,4},{14,6},{1,9},{3,11}... | collective-permute-start | bytes 98312 | tf_op jit(solution)/shard_map/ppermute | solution.py:402
  5.5 1.3 %collective-permute-start.1 = (f32[32,256]{1,0:T(8,128)S(1)}, f32[32,256]{1,0:T(8,128)S(1)}, u32[]{:S(2)}, u32[]{:S(2)}) collective-permute-start(f32[32,256]{1,0:T(8,128)S(1)} %multiply_multiply_fusion.refs_3_), channel_id=1, source_target_pairs={{0,12},{2,14},{4,8},{6,10},{8,4},{10,6},{12,0},{14,2},{1,13},{3,15... | collective-permute-start | bytes 98312 | tf_op jit(solution)/shard_map/ppermute | solution.py:402
  6.9 0.2 collective-permute-start.2
  7.8 2.3 %gather.1 = (f32[64,128,128]{2,1,0:T(8,128)S(1)}, bf16[65,128,128]{2,1,0:T(8,128)(2,1)S(1)}) custom-call(s32[1]{0:T(128)S(6)} %copy.11.count_ref, s32[130]{0:T(256)} %rows_hbm.3, s32[130]{0:T(256)} %cols_hbm.3, bf16[130,128,128]{2,1,0:T(8,128)(2,1)} %tiles_ref.1), custom_call_target="tpu_custom_call" | custom-call | flops 8519680 | bytes 8519680 | tf_op jit(solution)/shard_map/gather/pallas_call | solution.py:443
  10.0 0.0 collective-permute-done.refs_0_
  10.0 1.2 %collective-permute-done.1.refs_1_ = f32[32,256]{1,0:T(8,128)S(1)} collective-permute-done((f32[32,256]{1,0:T(8,128)S(1)}, f32[32,256]{1,0:T(8,128)S(1)}, u32[]{:S(2)}, u32[]{:S(2)}) %collective-permute-start.1) | collective-permute-done | bytes 32800 | tf_op jit(solution)/shard_map/ppermute | solution.py:402
  11.2 0.0 collective-permute-done.2.refs_2_
  11.2 1.6 %collective-permute-start.3 = (f32[4,32,256]{2,1,0:T(8,128)S(1)}, f32[4,32,256]{2,1,0:T(8,128)S(1)}, u32[]{:S(2)}, u32[]{:S(2)}) collective-permute-start(f32[4,32,256]{2,1,0:T(8,128)S(1)} %join.1.joined_ref.even_ref.near_ref), channel_id=1, source_target_pairs={{0,2},{2,0},{4,6},{6,4},{8,10},{10,8},{12,14},{14,12},{1,3},{3,1},... | collective-permute-start | bytes 393224 | tf_op jit(solution)/shard_map/ppermute | solution.py:402
  12.8 2.2 %dense.1 = (bf16[2,2048,512]{2,1,0:T(8,128)(2,1)S(1)}, f32[64,128,128]{2,1,0:T(8,128)S(1)}) custom-call(s32[1]{0:T(128)S(6)} %copy.11.count_ref, s32[130]{0:T(256)} %rows_hbm.3, s32[130]{0:T(256)} %cols_hbm.3, bf16[65,128,128]{2,1,0:T(8,128)(2,1)S(1)} %get-tuple-element.24.rest, ...), custom_call_target="tpu_custom_call", output_to_operand_aliasing={{1}: (4, {})} | custom-call | flops 8519680 | bytes 8519680 | tf_op jit(solution)/shard_map/dense/pallas_call | solution.py:469
  15.1 1.2 %collective-permute-done.3.odd_ref = f32[4,32,256]{2,1,0:T(8,128)S(1)} collective-permute-done((f32[4,32,256]{2,1,0:T(8,128)S(1)}, f32[4,32,256]{2,1,0:T(8,128)S(1)}, u32[]{:S(2)}, u32[]{:S(2)}) %collective-permute-start.3) | collective-permute-done | bytes 131104 | tf_op jit(solution)/shard_map/ppermute | solution.py:402
  16.3 0.9 %first.1 = (f32[32,640]{1,0:T(8,128)S(1)}, f32[8,32,256]{2,1,0:T(8,128)S(1)}) custom-call(f32[4,32,256]{2,1,0:T(8,128)S(1)} %join.1.joined_ref.even_ref.near_ref, f32[4,32,256]{2,1,0:T(8,128)S(1)} %collective-permute-done.3.odd_ref, bf16[2,2048,512]{2,1,0:T(8,128)(2,1)S(1)} %get-tuple-element.25.matrix.refs_13_), custom_call_target="tpu_custom_call" | custom-call | tf_op jit(solution)/shard_map/first/pallas_call | solution.py:488
  17.2 0.0 collective-permute-start.4
  17.2 0.5 collective-permute-start.14
  17.7 0.1 collective-permute-start.5
  17.8 1.1 %collective-permute-done.5 = f32[32,256]{1,0:T(8,128)S(1)} collective-permute-done((f32[32,256]{1,0:T(8,128)S(1)}, f32[32,256]{1,0:T(8,128)S(1)}, u32[]{:S(2)}, u32[]{:S(2)}) %collective-permute-start.5) | collective-permute-done | bytes 32800 | tf_op jit(solution)/shard_map/ppermute | solution.py:405
  18.9 0.0 collective-permute-done.4.other_ref
  18.9 0.3 image.2
  19.3 0.6 collective-permute-start.6
  19.9 3.6 %collective-permute-start.7 = (f32[136,128]{1,0:T(8,128)S(1)}, f32[136,128]{1,0:T(8,128)S(1)}, u32[]{:S(2)}, u32[]{:S(2)}) collective-permute-start(f32[136,128]{1,0:T(8,128)S(1)} %get-tuple-element.27.refs_0_), channel_id=1, source_target_pairs={{0,14},{2,12},{4,10},{6,8},{8,6},{10,4},{12,2},{14,0},{1,13},{3,15... | collective-permute-start | bytes 208904 | tf_op jit(solution)/shard_map/ppermute | solution.py:421
  23.4 0.5 collective-permute-start.8
  23.9 1.5 %collective-permute-start.9 = (f32[136,128]{1,0:T(8,128)S(1)}, f32[136,128]{1,0:T(8,128)S(1)}, u32[]{:S(2)}, u32[]{:S(2)}) collective-permute-start(f32[136,128]{1,0:T(8,128)S(1)} %collective-permute-done.6.refs_1_), channel_id=1, source_target_pairs={{0,2},{2,0},{4,6},{6,4},{8,10},{10,8},{12,14},{14,12},{1,3},{3,1},... | collective-permute-start | bytes 208904 | tf_op jit(solution)/shard_map/ppermute | solution.py:421
  25.5 0.6 %collective-permute-start.10 = (f32[136,128]{1,0:T(8,128)S(1)}, f32[136,128]{1,0:T(8,128)S(1)}, u32[]{:S(2)}, u32[]{:S(2)}) collective-permute-start(f32[136,128]{1,0:T(8,128)S(1)} %collective-permute-done.6.refs_1_), channel_id=1, source_target_pairs={{0,1},{1,0},{2,3},{3,2},{4,5},{5,4},{6,7},{7,6},{8,9},{9,8},{10,11... | collective-permute-start | bytes 208904 | tf_op jit(solution)/shard_map/ppermute | solution.py:405
  26.1 1.3 %collective-permute-done.7.refs_2_ = f32[136,128]{1,0:T(8,128)S(1)} collective-permute-done((f32[136,128]{1,0:T(8,128)S(1)}, f32[136,128]{1,0:T(8,128)S(1)}, u32[]{:S(2)}, u32[]{:S(2)}) %collective-permute-start.7) | collective-permute-done | bytes 69664 | tf_op jit(solution)/shard_map/ppermute | solution.py:421
  27.4 1.2 %collective-permute-done.8.refs_3_ = f32[136,128]{1,0:T(8,128)S(1)} collective-permute-done((f32[136,128]{1,0:T(8,128)S(1)}, f32[136,128]{1,0:T(8,128)S(1)}, u32[]{:S(2)}, u32[]{:S(2)}) %collective-permute-start.8) | collective-permute-done | bytes 69664 | tf_op jit(solution)/shard_map/ppermute | solution.py:421
  28.6 0.9 %collective-permute-done.9.refs_4_ = f32[136,128]{1,0:T(8,128)S(1)} collective-permute-done((f32[136,128]{1,0:T(8,128)S(1)}, f32[136,128]{1,0:T(8,128)S(1)}, u32[]{:S(2)}, u32[]{:S(2)}) %collective-permute-start.9) | collective-permute-done | bytes 69664 | tf_op jit(solution)/shard_map/ppermute | solution.py:421
  29.4 0.0 collective-permute-start.13
  29.5 0.9 %inverse.2.refs_12_ = f32[32,128]{1,0:T(8,128)S(1)} custom-call(f32[32,128]{1,0:T(8,128)S(1)} %get-tuple-element.31.norm_ref.refs_11_), custom_call_target="tpu_custom_call" | custom-call | tf_op jit(solution)/shard_map/inverse/pallas_call | solution.py:523
  30.4 0.0 collective-permute-done.14.far_ref
  30.4 0.1 collect.1
  30.5 0.0 collective-permute-done.10.refs_5_
  30.5 0.0 collective-permute-done.11.refs_6_
  30.5 0.2 collective-permute-done.13.refs_8_
  30.7 3.1 %step.2 = (f32[32,512]{1,0:T(8,128)S(1)}, f32[9,32,256]{2,1,0:T(8,128)S(1)}, f32[2,8,32,256]{3,2,1,0:T(8,128)S(1)}, f32[32,128]{1,0:T(8,128)S(1)}, f32[32,256]{1,0:T(8,128)S(1)}) custom-call(f32[136,128]{1,0:T(8,128)S(1)} %get-tuple-element.27.refs_0_, f32[136,128]{1,0:T(8,128)S(1)} %collective-permute-done.6.refs_1_, ...), custom_call_target="tpu_custom_call" | custom-call | tf_op jit(solution)/shard_map/step/pallas_call | solution.py:532
  33.8 0.3 collective-permute-start.15
  34.1 1.0 %collective-permute-done.15.other_ref = f32[32,512]{1,0:T(8,128)S(1)} collective-permute-done((f32[32,512]{1,0:T(8,128)S(1)}, f32[32,512]{1,0:T(8,128)S(1)}, u32[]{:S(2)}, u32[]{:S(2)}) %collective-permute-start.15) | collective-permute-done | bytes 65568 | tf_op jit(solution)/shard_map/ppermute | solution.py:405
  35.1 0.3 image.3.refs_0_
  35.4 0.0 collective-permute-start.16
  35.4 2.7 %collective-permute-start.17 = (f32[136,128]{1,0:T(8,128)S(1)}, f32[136,128]{1,0:T(8,128)S(1)}, u32[]{:S(2)}, u32[]{:S(2)}) collective-permute-start(f32[136,128]{1,0:T(8,128)S(1)} %image.3.refs_0_), channel_id=1, source_target_pairs={{0,14},{2,12},{4,10},{6,8},{8,6},{10,4},{12,2},{14,0},{1,13},{3,15... | collective-permute-start | bytes 208904 | tf_op jit(solution)/shard_map/ppermute | solution.py:421
  38.1 1.1 %collective-permute-start.18 = (f32[136,128]{1,0:T(8,128)S(1)}, f32[136,128]{1,0:T(8,128)S(1)}, u32[]{:S(2)}, u32[]{:S(2)}) collective-permute-start(f32[136,128]{1,0:T(8,128)S(1)} %image.3.refs_0_), channel_id=1, source_target_pairs={{0,2},{2,0},{4,6},{6,4},{8,10},{10,8},{12,14},{14,12},{1,5},{3,7},... | collective-permute-start | bytes 208904 | tf_op jit(solution)/shard_map/ppermute | solution.py:421
  39.2 1.5 %collective-permute-done.16.refs_1_ = f32[136,128]{1,0:T(8,128)S(1)} collective-permute-done((f32[136,128]{1,0:T(8,128)S(1)}, f32[136,128]{1,0:T(8,128)S(1)}, u32[]{:S(2)}, u32[]{:S(2)}) %collective-permute-start.16) | collective-permute-done | bytes 69664 | tf_op jit(solution)/shard_map/ppermute | solution.py:421
  40.7 1.0 %collective-permute-start.19 = (f32[136,128]{1,0:T(8,128)S(1)}, f32[136,128]{1,0:T(8,128)S(1)}, u32[]{:S(2)}, u32[]{:S(2)}) collective-permute-start(f32[136,128]{1,0:T(8,128)S(1)} %collective-permute-done.16.refs_1_), channel_id=1, source_target_pairs={{0,2},{2,0},{4,6},{6,4},{8,10},{10,8},{12,14},{14,12},{1,3},{3,1},... | collective-permute-start | bytes 208904 | tf_op jit(solution)/shard_map/ppermute | solution.py:421
  41.8 1.4 %collective-permute-done.17.refs_2_ = f32[136,128]{1,0:T(8,128)S(1)} collective-permute-done((f32[136,128]{1,0:T(8,128)S(1)}, f32[136,128]{1,0:T(8,128)S(1)}, u32[]{:S(2)}, u32[]{:S(2)}) %collective-permute-start.17) | collective-permute-done | bytes 69664 | tf_op jit(solution)/shard_map/ppermute | solution.py:421
  43.2 0.0 collective-permute-start.21
  43.2 0.3 collective-permute-done.18.refs_3_
  43.5 0.2 collective-permute-start.22
  43.7 1.3 %collective-permute-done.19.refs_4_ = f32[136,128]{1,0:T(8,128)S(1)} collective-permute-done((f32[136,128]{1,0:T(8,128)S(1)}, f32[136,128]{1,0:T(8,128)S(1)}, u32[]{:S(2)}, u32[]{:S(2)}) %collective-permute-start.19) | collective-permute-done | bytes 69664 | tf_op jit(solution)/shard_map/ppermute | solution.py:421
  45.1 0.9 %inverse.3.refs_12_ = f32[32,128]{1,0:T(8,128)S(1)} custom-call(f32[32,128]{1,0:T(8,128)S(1)} %get-tuple-element.35.norm_ref.refs_11_), custom_call_target="tpu_custom_call" | custom-call | tf_op jit(solution)/shard_map/inverse/pallas_call | solution.py:523
  46.0 0.3 collective-permute-done.23.refs_8_
  46.3 3.1 %step.3 = (f32[32,512]{1,0:T(8,128)S(1)}, f32[2,32,256]{2,1,0:T(8,128)S(1)}, f32[32,256]{1,0:T(8,128)S(1)}, f32[32,128]{1,0:T(8,128)S(1)}, f32[32,256]{1,0:T(8,128)S(1)}) custom-call(f32[136,128]{1,0:T(8,128)S(1)} %image.3.refs_0_, f32[136,128]{1,0:T(8,128)S(1)} %collective-permute-done.16.refs_1_, f32[136,128]{1,0:T(8,128)S(1)} %collective-permute-done.17.refs_2_, ...), custom_call_target="tpu_custom_call" | custom-call | tf_op jit(solution)/shard_map/step/pallas_call | solution.py:532
  49.4 0.2 collective-permute-start.24
  49.6 1.0 %collective-permute-done.24.other_ref = f32[32,512]{1,0:T(8,128)S(1)} collective-permute-done((f32[32,512]{1,0:T(8,128)S(1)}, f32[32,512]{1,0:T(8,128)S(1)}, u32[]{:S(2)}, u32[]{:S(2)}) %collective-permute-start.24) | collective-permute-done | bytes 65568 | tf_op jit(solution)/shard_map/ppermute | solution.py:405
  50.6 0.3 last_image.1
  51.0 0.3 collective-permute-start.25
  51.3 2.3 %collective-permute-start.26 = (f32[8,128]{1,0:T(8,128)S(1)}, f32[8,128]{1,0:T(8,128)S(1)}, u32[]{:S(2)}, u32[]{:S(2)}) collective-permute-start(f32[8,128]{1,0:T(8,128)S(1)} %get-tuple-element.39.refs_0_), channel_id=1, source_target_pairs={{0,14},{2,12},{4,10},{6,8},{8,6},{10,4},{12,2},{14,0},{1,13},{3,15... | collective-permute-start | bytes 12296 | tf_op jit(solution)/shard_map/ppermute | solution.py:421
  53.7 1.1 %collective-permute-start.27 = (f32[8,128]{1,0:T(8,128)S(1)}, f32[8,128]{1,0:T(8,128)S(1)}, u32[]{:S(2)}, u32[]{:S(2)}) collective-permute-start(f32[8,128]{1,0:T(8,128)S(1)} %get-tuple-element.39.refs_0_), channel_id=1, source_target_pairs={{0,2},{2,0},{4,6},{6,4},{8,10},{10,8},{12,14},{14,12},{1,5},{3,7},... | collective-permute-start | bytes 12296 | tf_op jit(solution)/shard_map/ppermute | solution.py:421
  54.7 1.0 %collective-permute-start.28 = (f32[8,128]{1,0:T(8,128)S(1)}, f32[8,128]{1,0:T(8,128)S(1)}, u32[]{:S(2)}, u32[]{:S(2)}) collective-permute-start(f32[8,128]{1,0:T(8,128)S(1)} %collective-permute-done.25.refs_1_), channel_id=1, source_target_pairs={{0,2},{2,0},{4,6},{6,4},{8,10},{10,8},{12,14},{14,12},{1,3},{3,1},... | collective-permute-start | bytes 12296 | tf_op jit(solution)/shard_map/ppermute | solution.py:421
  55.7 1.9 %collective-permute-done.26.refs_2_ = f32[8,128]{1,0:T(8,128)S(1)} collective-permute-done((f32[8,128]{1,0:T(8,128)S(1)}, f32[8,128]{1,0:T(8,128)S(1)}, u32[]{:S(2)}, u32[]{:S(2)}) %collective-permute-start.26) | collective-permute-done | bytes 4128 | tf_op jit(solution)/shard_map/ppermute | solution.py:421
  57.6 0.5 collective-permute-start.31
  58.1 0.2 collective-permute-done.28.refs_4_
  58.3 0.5 collective-permute-done.30.refs_6_
  58.8 0.2 collective-permute-done.31.refs_7_
  59.0 0.5 collective-permute-done.32.refs_8_
  59.5 1.7 %last.1 = (f32[32,256]{1,0:T(8,128)}, f32[32,256]{1,0:T(8,128)}) custom-call(f32[8,128]{1,0:T(8,128)S(1)} %get-tuple-element.39.refs_0_, f32[8,128]{1,0:T(8,128)S(1)} %collective-permute-done.25.refs_1_, f32[8,128]{1,0:T(8,128)S(1)} %collective-permute-done.26.refs_2_, f32[8,128]{1,0:T(8,128)S(1)} %collective-permute-done.27.refs_3_, ...), custom_call_target="tpu_custom_call" | custom-call | tf_op jit(solution)/shard_map/last/pallas_call | solution.py:555
  (16 shorter events, 0.0 us)
Async XLA Ops:
  1.5 8.6 %collective-permute-start = (f32[32,256]{1,0:T(8,128)S(1)}, f32[32,256]{1,0:T(8,128)S(1)}, u32[]{:S(2)}, u32[]{:S(2)}) collective-permute-start(f32[32,256]{1,0:T(8,128)S(1)} %multiply_multiply_fusion.refs_3_), channel_id=1, source_target_pairs={{0,8},{2,10},{4,12},{6,14},{8,0},{10,2},{12,4},{14,6},{1,9},{3,11}... | collective-permute-start | bytes 98312 | tf_op jit(solution)/shard_map/ppermute | solution.py:402
  5.5 5.7 %collective-permute-start.1 = (f32[32,256]{1,0:T(8,128)S(1)}, f32[32,256]{1,0:T(8,128)S(1)}, u32[]{:S(2)}, u32[]{:S(2)}) collective-permute-start(f32[32,256]{1,0:T(8,128)S(1)} %multiply_multiply_fusion.refs_3_), channel_id=1, source_target_pairs={{0,12},{2,14},{4,8},{6,10},{8,4},{10,6},{12,0},{14,2},{1,13},{3,15... | collective-permute-start | bytes 98312 | tf_op jit(solution)/shard_map/ppermute | solution.py:402
  6.9 4.4 %collective-permute-start.2 = (f32[32,256]{1,0:T(8,128)S(1)}, f32[32,256]{1,0:T(8,128)S(1)}, u32[]{:S(2)}, u32[]{:S(2)}) collective-permute-start(f32[32,256]{1,0:T(8,128)S(1)} %multiply_multiply_fusion.refs_3_), channel_id=1, source_target_pairs={{0,4},{2,6},{4,0},{6,2},{8,12},{10,14},{12,8},{14,10},{1,5},{3,7},... | collective-permute-start | bytes 98312 | tf_op jit(solution)/shard_map/ppermute | solution.py:402
  11.2 5.0 %collective-permute-start.3 = (f32[4,32,256]{2,1,0:T(8,128)S(1)}, f32[4,32,256]{2,1,0:T(8,128)S(1)}, u32[]{:S(2)}, u32[]{:S(2)}) collective-permute-start(f32[4,32,256]{2,1,0:T(8,128)S(1)} %join.1.joined_ref.even_ref.near_ref), channel_id=1, source_target_pairs={{0,2},{2,0},{4,6},{6,4},{8,10},{10,8},{12,14},{14,12},{1,3},{3,1},... | collective-permute-start | bytes 393224 | tf_op jit(solution)/shard_map/ppermute | solution.py:402
  17.2 1.8 %collective-permute-start.4 = (f32[32,640]{1,0:T(8,128)S(1)}, f32[32,640]{1,0:T(8,128)S(1)}, u32[]{:S(2)}, u32[]{:S(2)}) collective-permute-start(f32[32,640]{1,0:T(8,128)S(1)} %get-tuple-element.26.mine_ref), channel_id=1, source_target_pairs={{0,1},{1,0},{2,3},{3,2},{4,5},{5,4},{6,7},{7,6},{8,9},{9,8},{10,11... | collective-permute-start | bytes 245768 | tf_op jit(solution)/shard_map/ppermute | solution.py:405
  17.2 13.2 %collective-permute-start.14 = (f32[8,32,256]{2,1,0:T(8,128)S(1)}, f32[8,32,256]{2,1,0:T(8,128)S(1)}, u32[]{:S(2)}, u32[]{:S(2)}) collective-permute-start(f32[8,32,256]{2,1,0:T(8,128)S(1)} %get-tuple-element.28.near_ref), channel_id=1, source_target_pairs={{0,1},{1,0},{2,3},{3,2},{4,5},{5,4},{6,7},{7,6},{8,9},{9,8},{10,11... | collective-permute-start | bytes 786440 | tf_op jit(solution)/shard_map/ppermute | solution.py:405
  17.7 1.2 %collective-permute-start.5 = (f32[32,256]{1,0:T(8,128)S(1)}, f32[32,256]{1,0:T(8,128)S(1)}, u32[]{:S(2)}, u32[]{:S(2)}) collective-permute-start(f32[32,256]{1,0:T(8,128)S(1)} %multiply_multiply_fusion.refs_3_), channel_id=1, source_target_pairs={{0,1},{1,0},{2,3},{3,2},{4,5},{5,4},{6,7},{7,6},{8,9},{9,8},{10,11... | collective-permute-start | bytes 98312 | tf_op jit(solution)/shard_map/ppermute | solution.py:405
  19.3 4.7 %collective-permute-start.6 = (f32[136,128]{1,0:T(8,128)S(1)}, f32[136,128]{1,0:T(8,128)S(1)}, u32[]{:S(2)}, u32[]{:S(2)}) collective-permute-start(f32[136,128]{1,0:T(8,128)S(1)} %get-tuple-element.27.refs_0_), channel_id=1, source_target_pairs={{0,4},{2,6},{4,0},{6,2},{8,12},{10,14},{12,8},{14,10},{1,9},{3,11}... | collective-permute-start | bytes 208904 | tf_op jit(solution)/shard_map/ppermute | solution.py:421
  19.9 7.6 %collective-permute-start.7 = (f32[136,128]{1,0:T(8,128)S(1)}, f32[136,128]{1,0:T(8,128)S(1)}, u32[]{:S(2)}, u32[]{:S(2)}) collective-permute-start(f32[136,128]{1,0:T(8,128)S(1)} %get-tuple-element.27.refs_0_), channel_id=1, source_target_pairs={{0,14},{2,12},{4,10},{6,8},{8,6},{10,4},{12,2},{14,0},{1,13},{3,15... | collective-permute-start | bytes 208904 | tf_op jit(solution)/shard_map/ppermute | solution.py:421
  23.4 5.2 %collective-permute-start.8 = (f32[136,128]{1,0:T(8,128)S(1)}, f32[136,128]{1,0:T(8,128)S(1)}, u32[]{:S(2)}, u32[]{:S(2)}) collective-permute-start(f32[136,128]{1,0:T(8,128)S(1)} %get-tuple-element.27.refs_0_), channel_id=1, source_target_pairs={{0,2},{2,0},{4,6},{6,4},{8,10},{10,8},{12,14},{14,12},{1,5},{3,7},... | collective-permute-start | bytes 208904 | tf_op jit(solution)/shard_map/ppermute | solution.py:421
  23.9 5.5 %collective-permute-start.9 = (f32[136,128]{1,0:T(8,128)S(1)}, f32[136,128]{1,0:T(8,128)S(1)}, u32[]{:S(2)}, u32[]{:S(2)}) collective-permute-start(f32[136,128]{1,0:T(8,128)S(1)} %collective-permute-done.6.refs_1_), channel_id=1, source_target_pairs={{0,2},{2,0},{4,6},{6,4},{8,10},{10,8},{12,14},{14,12},{1,3},{3,1},... | collective-permute-start | bytes 208904 | tf_op jit(solution)/shard_map/ppermute | solution.py:421
  25.5 5.0 %collective-permute-start.10 = (f32[136,128]{1,0:T(8,128)S(1)}, f32[136,128]{1,0:T(8,128)S(1)}, u32[]{:S(2)}, u32[]{:S(2)}) collective-permute-start(f32[136,128]{1,0:T(8,128)S(1)} %collective-permute-done.6.refs_1_), channel_id=1, source_target_pairs={{0,1},{1,0},{2,3},{3,2},{4,5},{5,4},{6,7},{7,6},{8,9},{9,8},{10,11... | collective-permute-start | bytes 208904 | tf_op jit(solution)/shard_map/ppermute | solution.py:405
  27.4 3.0 %collective-permute-start.11 = (f32[136,128]{1,0:T(8,128)S(1)}, f32[136,128]{1,0:T(8,128)S(1)}, u32[]{:S(2)}, u32[]{:S(2)}) collective-permute-start(f32[136,128]{1,0:T(8,128)S(1)} %collective-permute-done.7.refs_2_), channel_id=1, source_target_pairs={{0,1},{1,0},{2,3},{3,2},{4,5},{5,4},{6,7},{7,6},{8,9},{9,8},{10,11... | collective-permute-start | bytes 208904 | tf_op jit(solution)/shard_map/ppermute | solution.py:405
  28.6 1.9 %collective-permute-start.12 = (f32[136,128]{1,0:T(8,128)S(1)}, f32[136,128]{1,0:T(8,128)S(1)}, u32[]{:S(2)}, u32[]{:S(2)}) collective-permute-start(f32[136,128]{1,0:T(8,128)S(1)} %collective-permute-done.8.refs_3_), channel_id=1, source_target_pairs={{0,1},{1,0},{2,3},{3,2},{4,5},{5,4},{6,7},{7,6},{8,9},{9,8},{10,11... | collective-permute-start | bytes 208904 | tf_op jit(solution)/shard_map/ppermute | solution.py:405
  29.4 1.3 %collective-permute-start.13 = (f32[136,128]{1,0:T(8,128)S(1)}, f32[136,128]{1,0:T(8,128)S(1)}, u32[]{:S(2)}, u32[]{:S(2)}) collective-permute-start(f32[136,128]{1,0:T(8,128)S(1)} %collective-permute-done.9.refs_4_), channel_id=1, source_target_pairs={{0,1},{1,0},{2,3},{3,2},{4,5},{5,4},{6,7},{7,6},{8,9},{9,8},{10,11... | collective-permute-start | bytes 208904 | tf_op jit(solution)/shard_map/ppermute | solution.py:405
  33.8 1.3 %collective-permute-start.15 = (f32[32,512]{1,0:T(8,128)S(1)}, f32[32,512]{1,0:T(8,128)S(1)}, u32[]{:S(2)}, u32[]{:S(2)}) collective-permute-start(f32[32,512]{1,0:T(8,128)S(1)} %get-tuple-element.32.mine_ref), channel_id=1, source_target_pairs={{0,1},{1,0},{2,3},{3,2},{4,5},{5,4},{6,7},{7,6},{8,9},{9,8},{10,11... | collective-permute-start | bytes 196616 | tf_op jit(solution)/shard_map/ppermute | solution.py:405
  35.4 5.3 %collective-permute-start.16 = (f32[136,128]{1,0:T(8,128)S(1)}, f32[136,128]{1,0:T(8,128)S(1)}, u32[]{:S(2)}, u32[]{:S(2)}) collective-permute-start(f32[136,128]{1,0:T(8,128)S(1)} %image.3.refs_0_), channel_id=1, source_target_pairs={{0,4},{2,6},{4,0},{6,2},{8,12},{10,14},{12,8},{14,10},{1,9},{3,11}... | collective-permute-start | bytes 208904 | tf_op jit(solution)/shard_map/ppermute | solution.py:421
  35.4 7.8 %collective-permute-start.17 = (f32[136,128]{1,0:T(8,128)S(1)}, f32[136,128]{1,0:T(8,128)S(1)}, u32[]{:S(2)}, u32[]{:S(2)}) collective-permute-start(f32[136,128]{1,0:T(8,128)S(1)} %image.3.refs_0_), channel_id=1, source_target_pairs={{0,14},{2,12},{4,10},{6,8},{8,6},{10,4},{12,2},{14,0},{1,13},{3,15... | collective-permute-start | bytes 208904 | tf_op jit(solution)/shard_map/ppermute | solution.py:421
  38.1 5.4 %collective-permute-start.18 = (f32[136,128]{1,0:T(8,128)S(1)}, f32[136,128]{1,0:T(8,128)S(1)}, u32[]{:S(2)}, u32[]{:S(2)}) collective-permute-start(f32[136,128]{1,0:T(8,128)S(1)} %image.3.refs_0_), channel_id=1, source_target_pairs={{0,2},{2,0},{4,6},{6,4},{8,10},{10,8},{12,14},{14,12},{1,5},{3,7},... | collective-permute-start | bytes 208904 | tf_op jit(solution)/shard_map/ppermute | solution.py:421
  40.7 4.3 %collective-permute-start.19 = (f32[136,128]{1,0:T(8,128)S(1)}, f32[136,128]{1,0:T(8,128)S(1)}, u32[]{:S(2)}, u32[]{:S(2)}) collective-permute-start(f32[136,128]{1,0:T(8,128)S(1)} %collective-permute-done.16.refs_1_), channel_id=1, source_target_pairs={{0,2},{2,0},{4,6},{6,4},{8,10},{10,8},{12,14},{14,12},{1,3},{3,1},... | collective-permute-start | bytes 208904 | tf_op jit(solution)/shard_map/ppermute | solution.py:421
  41.8 4.2 %collective-permute-start.20 = (f32[136,128]{1,0:T(8,128)S(1)}, f32[136,128]{1,0:T(8,128)S(1)}, u32[]{:S(2)}, u32[]{:S(2)}) collective-permute-start(f32[136,128]{1,0:T(8,128)S(1)} %collective-permute-done.16.refs_1_), channel_id=1, source_target_pairs={{0,1},{1,0},{2,3},{3,2},{4,5},{5,4},{6,7},{7,6},{8,9},{9,8},{10,11... | collective-permute-start | bytes 208904 | tf_op jit(solution)/shard_map/ppermute | solution.py:405
  43.2 2.8 %collective-permute-start.21 = (f32[136,128]{1,0:T(8,128)S(1)}, f32[136,128]{1,0:T(8,128)S(1)}, u32[]{:S(2)}, u32[]{:S(2)}) collective-permute-start(f32[136,128]{1,0:T(8,128)S(1)} %collective-permute-done.17.refs_2_), channel_id=1, source_target_pairs={{0,1},{1,0},{2,3},{3,2},{4,5},{5,4},{6,7},{7,6},{8,9},{9,8},{10,11... | collective-permute-start | bytes 208904 | tf_op jit(solution)/shard_map/ppermute | solution.py:405
  43.5 2.5 %collective-permute-start.22 = (f32[136,128]{1,0:T(8,128)S(1)}, f32[136,128]{1,0:T(8,128)S(1)}, u32[]{:S(2)}, u32[]{:S(2)}) collective-permute-start(f32[136,128]{1,0:T(8,128)S(1)} %collective-permute-done.18.refs_3_), channel_id=1, source_target_pairs={{0,1},{1,0},{2,3},{3,2},{4,5},{5,4},{6,7},{7,6},{8,9},{9,8},{10,11... | collective-permute-start | bytes 208904 | tf_op jit(solution)/shard_map/ppermute | solution.py:405
  45.0 1.3 %collective-permute-start.23 = (f32[136,128]{1,0:T(8,128)S(1)}, f32[136,128]{1,0:T(8,128)S(1)}, u32[]{:S(2)}, u32[]{:S(2)}) collective-permute-start(f32[136,128]{1,0:T(8,128)S(1)} %collective-permute-done.19.refs_4_), channel_id=1, source_target_pairs={{0,1},{1,0},{2,3},{3,2},{4,5},{5,4},{6,7},{7,6},{8,9},{9,8},{10,11... | collective-permute-start | bytes 208904 | tf_op jit(solution)/shard_map/ppermute | solution.py:405
  49.4 1.3 %collective-permute-start.24 = (f32[32,512]{1,0:T(8,128)S(1)}, f32[32,512]{1,0:T(8,128)S(1)}, u32[]{:S(2)}, u32[]{:S(2)}) collective-permute-start(f32[32,512]{1,0:T(8,128)S(1)} %get-tuple-element.37.mine_ref), channel_id=1, source_target_pairs={{0,1},{1,0},{2,3},{3,2},{4,5},{5,4},{6,7},{7,6},{8,9},{9,8},{10,11... | collective-permute-start | bytes 196616 | tf_op jit(solution)/shard_map/ppermute | solution.py:405
  51.0 3.7 %collective-permute-start.25 = (f32[8,128]{1,0:T(8,128)S(1)}, f32[8,128]{1,0:T(8,128)S(1)}, u32[]{:S(2)}, u32[]{:S(2)}) collective-permute-start(f32[8,128]{1,0:T(8,128)S(1)} %get-tuple-element.39.refs_0_), channel_id=1, source_target_pairs={{0,4},{2,6},{4,0},{6,2},{8,12},{10,14},{12,8},{14,10},{1,9},{3,11}... | collective-permute-start | bytes 12296 | tf_op jit(solution)/shard_map/ppermute | solution.py:421
  51.3 6.3 %collective-permute-start.26 = (f32[8,128]{1,0:T(8,128)S(1)}, f32[8,128]{1,0:T(8,128)S(1)}, u32[]{:S(2)}, u32[]{:S(2)}) collective-permute-start(f32[8,128]{1,0:T(8,128)S(1)} %get-tuple-element.39.refs_0_), channel_id=1, source_target_pairs={{0,14},{2,12},{4,10},{6,8},{8,6},{10,4},{12,2},{14,0},{1,13},{3,15... | collective-permute-start | bytes 12296 | tf_op jit(solution)/shard_map/ppermute | solution.py:421
  53.7 4.0 %collective-permute-start.27 = (f32[8,128]{1,0:T(8,128)S(1)}, f32[8,128]{1,0:T(8,128)S(1)}, u32[]{:S(2)}, u32[]{:S(2)}) collective-permute-start(f32[8,128]{1,0:T(8,128)S(1)} %get-tuple-element.39.refs_0_), channel_id=1, source_target_pairs={{0,2},{2,0},{4,6},{6,4},{8,10},{10,8},{12,14},{14,12},{1,5},{3,7},... | collective-permute-start | bytes 12296 | tf_op jit(solution)/shard_map/ppermute | solution.py:421
  54.7 3.6 %collective-permute-start.28 = (f32[8,128]{1,0:T(8,128)S(1)}, f32[8,128]{1,0:T(8,128)S(1)}, u32[]{:S(2)}, u32[]{:S(2)}) collective-permute-start(f32[8,128]{1,0:T(8,128)S(1)} %collective-permute-done.25.refs_1_), channel_id=1, source_target_pairs={{0,2},{2,0},{4,6},{6,4},{8,10},{10,8},{12,14},{14,12},{1,3},{3,1},... | collective-permute-start | bytes 12296 | tf_op jit(solution)/shard_map/ppermute | solution.py:421
  55.7 2.6 %collective-permute-start.29 = (f32[8,128]{1,0:T(8,128)S(1)}, f32[8,128]{1,0:T(8,128)S(1)}, u32[]{:S(2)}, u32[]{:S(2)}) collective-permute-start(f32[8,128]{1,0:T(8,128)S(1)} %collective-permute-done.25.refs_1_), channel_id=1, source_target_pairs={{0,1},{1,0},{2,3},{3,2},{4,5},{5,4},{6,7},{7,6},{8,9},{9,8},{10,11... | collective-permute-start | bytes 12296 | tf_op jit(solution)/shard_map/ppermute | solution.py:405
  57.6 1.2 %collective-permute-start.30 = (f32[8,128]{1,0:T(8,128)S(1)}, f32[8,128]{1,0:T(8,128)S(1)}, u32[]{:S(2)}, u32[]{:S(2)}) collective-permute-start(f32[8,128]{1,0:T(8,128)S(1)} %collective-permute-done.26.refs_2_), channel_id=1, source_target_pairs={{0,1},{1,0},{2,3},{3,2},{4,5},{5,4},{6,7},{7,6},{8,9},{9,8},{10,11... | collective-permute-start | bytes 12296 | tf_op jit(solution)/shard_map/ppermute | solution.py:405
  57.6 1.3 %collective-permute-start.31 = (f32[8,128]{1,0:T(8,128)S(1)}, f32[8,128]{1,0:T(8,128)S(1)}, u32[]{:S(2)}, u32[]{:S(2)}) collective-permute-start(f32[8,128]{1,0:T(8,128)S(1)} %collective-permute-done.27.refs_3_), channel_id=1, source_target_pairs={{0,1},{1,0},{2,3},{3,2},{4,5},{5,4},{6,7},{7,6},{8,9},{9,8},{10,11... | collective-permute-start | bytes 12296 | tf_op jit(solution)/shard_map/ppermute | solution.py:405
  58.3 1.2 %collective-permute-start.32 = (f32[8,128]{1,0:T(8,128)S(1)}, f32[8,128]{1,0:T(8,128)S(1)}, u32[]{:S(2)}, u32[]{:S(2)}) collective-permute-start(f32[8,128]{1,0:T(8,128)S(1)} %collective-permute-done.28.refs_4_), channel_id=1, source_target_pairs={{0,1},{1,0},{2,3},{3,2},{4,5},{5,4},{6,7},{7,6},{8,9},{9,8},{10,11... | collective-permute-start | bytes 12296 | tf_op jit(solution)/shard_map/ppermute | solution.py:405

commit v13 on v12

--- a/solution.py
+++ b/solution.py
@@ -101,20 +101,30 @@
     row_ids = lax.broadcasted_iota(jnp.int32, (size, LANES), 0)
     lane_ids = lax.broadcasted_iota(jnp.int32, (size, LANES), 1)
     work = jnp.where(lane_ids < size, target, matrix)
+    work = work * pltpu.reciprocal(work[:1, size : size + 1], full_range=False)
     for base in range(0, size, PIVOTS):
         columns = [
             jnp.broadcast_to(work[:, size + base + i : size + base + i + 1], (size, LANES))
             for i in range(PIVOTS)
         ]
-        for i in range(PIVOTS):
-            pivot = base + i
-            here = row_ids == pivot
-            inverse = pltpu.reciprocal(columns[i][pivot : pivot + 1, :], full_range=False)
-            row = work[pivot : pivot + 1, :] * inverse
-            work = jnp.where(here, row, work - columns[i] * row)
-            for later in range(i + 1, PIVOTS):
-                entry = columns[later][pivot : pivot + 1, :] * inverse
-                columns[later] = jnp.where(here, entry, columns[later] - columns[i] * entry)
+        for i in range(0, PIVOTS, 2):
+            first = base + i
+            one, two = columns[i : i + 2]
+            here = row_ids == first
+            below = row_ids == first + 1
+            row, next_row = slice(first, first + 1), slice(first + 1, first + 2)
+            a, b, c, d = one[row], two[row], one[next_row], two[next_row]
+            inverse = pltpu.reciprocal(a * d - b * c, full_range=False)
+
+            def eliminate(value):
+                up, low = value[row], value[next_row]
+                up, low = (d * up - b * low) * inverse, (a * low - c * up) * inverse
+                rest = value - one * up - two * low
+                return jnp.where(here, up, jnp.where(below, low, rest))
+
+            work = eliminate(work)
+            for later in range(i + 2, PIVOTS):
+                columns[later] = eliminate(columns[later])
     return work
 
 
@@ -410,21 +420,24 @@
         if pieces != 8:
             found = [value] + [swap(value, k) for k in range(1, pieces)]
             return found, [(k, k) for k in range(pieces)]
-        turns = ((2, 4), (7, 6), (1, 2))
-
-        def fetch(source, masks):
+        turns = ((7, 5), (3, 6), (2, 4), (1, 1))
+        fetched = []
+        passed = []
+        places = {0: (0, 0)}
+        for turn, masks in enumerate(turns, 1):
             pairs = [
                 (i * 2 + core, (i ^ mask) * 2 + core)
                 for core, mask in enumerate(masks)
                 for i in range(pieces)
             ]
-            return lax.ppermute(source, ("row", "col"), pairs)
-
-        fetched = [fetch(value, masks) for masks in turns]
-        fetched.append(fetch(fetched[0], (1, 1)))
-        found = [value, *fetched, *map(across, fetched)]
-        places = [(0, 0), (3, 7), (1, 5), (4, 8), (5, 1), (8, 4), (6, 2), (2, 6)]
-        return found, places
+            fetched.append(lax.ppermute(value, ("row", "col"), pairs))
+            if masks[0] == masks[1]:
+                places[masks[0]] = (turn, turn)
+            else:
+                passed.append(across(fetched[-1]))
+                places[masks[0]] = (turn, turn + len(turns))
+                places[masks[1]] = (turn + len(turns), turn)
+        return [value, *fetched, *passed], [places[k] for k in range(pieces)]
 
     right_side = signs.astype(F32) * vertex_weight[None, :] * column_scale[:, None]
     far_side = across(right_side)[None]

time: 62 us -> 61.4 us (level); the launches traced: 61.2 us -> 61.2 us
  waiting for transfers between devices: 17.3 us -> 13.8 us
  Pallas kernels: 16.1 us -> 18.5 us
  starting transfers between devices: 25.5 us -> 26.6 us
    pallas_call x1, Pallas kernels: 2.23 us -> 4.11 us  [per_device(): pl.pallas_call(functools.partial(dense_kernel, rows_dev), out_shape=(matr...]
    ppermute x17 -> x14, waiting for transfers between devices: 4.81 us -> 3.42 us  [across(): lax.ppermute(value, 'col', [(i, (i + 1) % col_devices) for i in range(col...]
    ppermute x12, starting transfers between devices: 15.7 us -> 17 us  [exchange(): fetched.append(lax.ppermute(value, ('row', 'col'), pairs))]
    ppermute x4, waiting for transfers between devices: 2.41 us -> 1.13 us  [swap(): return lax.ppermute(value, 'row', [(i, i ^ mask) for i in range(pieces)])]
    ppermute x12, waiting for transfers between devices: 10.1 us -> 9.25 us  [exchange(): fetched.append(lax.ppermute(value, ('row', 'col'), pairs))]
    ppermute x17 -> x14, starting transfers between devices: 2.56 us -> 2.31 us  [across(): lax.ppermute(value, 'col', [(i, (i + 1) % col_devices) for i in range(col...]
  transfers between devices with their start and end apart: 33 -> 30, of which waited for: 19 -> 14; matrix products, arithmetic and copies ran while one was open for 0% -> 0% of each run, Pallas kernels for 11% -> 15%
where the time goes in v13:
time: 61.4 us; the launch traced here: 61.2 us
  starting transfers between devices  26.6 us (43%)
  Pallas kernels  18.5 us (30%)
  waiting for transfers between devices  13.8 us (22%)
  between operations  1.44 us (2%)
  other arithmetic  0.85 us (1%)
    ppermute x12, starting transfers between devices, exchange(): fetched.append(lax.ppermute(value, ('row', 'col'), pairs))  17 us
    ppermute x12, waiting for transfers between devices, exchange(): fetched.append(lax.ppermute(value, ('row', 'col'), pairs))  9.25 us
    ppermute x4, starting transfers between devices, swap(): return lax.ppermute(value, 'row', [(i, i ^ mask) for i in range(pieces)])  7.2 us
    pallas_call x2, Pallas kernels, per_device(): pl.pallas_call(functools.partial(step_kernel, len(found), places, not fir...  6.28 us
    pallas_call x1, Pallas kernels, per_device(): pl.pallas_call(functools.partial(dense_kernel, rows_dev), out_shape=(matr...  4.11 us
    ppermute x14, waiting for transfers between devices, across(): lax.ppermute(value, 'col', [(i, (i + 1) % col_devices) for i in range(col...  3.42 us
    pallas_call x1, Pallas kernels, per_device(): pl.pallas_call(functools.partial(gather_kernel, rows_dev), out_shape=(tot...  2.34 us
    ppermute x14, starting transfers between devices, across(): lax.ppermute(value, 'col', [(i, (i + 1) % col_devices) for i in range(col...  2.31 us
  transfers between devices with their start and end apart: 30, of which 14 were waited for; matrix products, arithmetic and copies ran while one was open for 0% of the time, Pallas kernels for 15%

profile of v13, /device:TPU:0, one launch (start us, length us, event | category | flops | bytes accessed | tf_op | source)
XLA Modules:
  0.0 61.2 jit_solution(3259850849565990952)
XLA Ops:
  0.6 0.8 %multiply_multiply_fusion.refs_3_ = f32[32,256]{1,0:T(8,128)S(1)} fusion(s32[32,256]{1,0:T(8,128)} %param.11, f32[32]{0:T(128)} %param.13, f32[256]{0:T(256)} %param.12), kind=kLoop, calls=%fused_computation | loop fusion | flops 24576 | bytes 66688 | tf_op jit(solution)/shard_map/mul | solution.py:442
  1.5 4.0 %collective-permute-start = (f32[32,256]{1,0:T(8,128)S(1)}, f32[32,256]{1,0:T(8,128)S(1)}, u32[]{:S(2)}, u32[]{:S(2)}) collective-permute-start(f32[32,256]{1,0:T(8,128)S(1)} %multiply_multiply_fusion.refs_3_), channel_id=1, source_target_pairs={{0,8},{2,10},{4,12},{6,14},{8,0},{10,2},{12,4},{14,6},{1,9},{3,11}... | collective-permute-start | bytes 98312 | tf_op jit(solution)/shard_map/ppermute | solution.py:412
  5.5 1.3 %collective-permute-start.1 = (f32[32,256]{1,0:T(8,128)S(1)}, f32[32,256]{1,0:T(8,128)S(1)}, u32[]{:S(2)}, u32[]{:S(2)}) collective-permute-start(f32[32,256]{1,0:T(8,128)S(1)} %multiply_multiply_fusion.refs_3_), channel_id=1, source_target_pairs={{0,12},{2,14},{4,8},{6,10},{8,4},{10,6},{12,0},{14,2},{1,13},{3,15... | collective-permute-start | bytes 98312 | tf_op jit(solution)/shard_map/ppermute | solution.py:412
  6.9 0.2 collective-permute-start.2
  7.8 2.3 %gather.1 = (f32[64,128,128]{2,1,0:T(8,128)S(1)}, bf16[65,128,128]{2,1,0:T(8,128)(2,1)S(1)}) custom-call(s32[1]{0:T(128)S(6)} %copy.11.count_ref, s32[130]{0:T(256)} %rows_hbm.3, s32[130]{0:T(256)} %cols_hbm.3, bf16[130,128,128]{2,1,0:T(8,128)(2,1)} %tiles_ref.1), custom_call_target="tpu_custom_call" | custom-call | flops 8519680 | bytes 8519680 | tf_op jit(solution)/shard_map/gather/pallas_call | solution.py:456
  10.1 0.0 collective-permute-done.refs_0_
  10.1 1.1 %collective-permute-done.1.refs_1_ = f32[32,256]{1,0:T(8,128)S(1)} collective-permute-done((f32[32,256]{1,0:T(8,128)S(1)}, f32[32,256]{1,0:T(8,128)S(1)}, u32[]{:S(2)}, u32[]{:S(2)}) %collective-permute-start.1) | collective-permute-done | bytes 32800 | tf_op jit(solution)/shard_map/ppermute | solution.py:412
  11.2 0.0 collective-permute-done.2.refs_2_
  11.2 1.6 %collective-permute-start.3 = (f32[4,32,256]{2,1,0:T(8,128)S(1)}, f32[4,32,256]{2,1,0:T(8,128)S(1)}, u32[]{:S(2)}, u32[]{:S(2)}) collective-permute-start(f32[4,32,256]{2,1,0:T(8,128)S(1)} %join.1.joined_ref.even_ref.near_ref), channel_id=1, source_target_pairs={{0,2},{2,0},{4,6},{6,4},{8,10},{10,8},{12,14},{14,12},{1,3},{3,1},... | collective-permute-start | bytes 393224 | tf_op jit(solution)/shard_map/ppermute | solution.py:412
  12.8 4.1 %dense.1 = (bf16[2,2048,512]{2,1,0:T(8,128)(2,1)S(1)}, f32[64,128,128]{2,1,0:T(8,128)S(1)}) custom-call(s32[1]{0:T(128)S(6)} %copy.11.count_ref, s32[130]{0:T(256)} %rows_hbm.3, s32[130]{0:T(256)} %cols_hbm.3, bf16[65,128,128]{2,1,0:T(8,128)(2,1)S(1)} %get-tuple-element.24.rest, ...), custom_call_target="tpu_custom_call", output_to_operand_aliasing={{1}: (4, {})} | custom-call | flops 8519680 | bytes 8519680 | tf_op jit(solution)/shard_map/dense/pallas_call | solution.py:482
  17.0 0.0 collective-permute-done.3.odd_ref
  17.0 0.9 %first.1 = (f32[32,640]{1,0:T(8,128)S(1)}, f32[8,32,256]{2,1,0:T(8,128)S(1)}) custom-call(f32[4,32,256]{2,1,0:T(8,128)S(1)} %join.1.joined_ref.even_ref.near_ref, f32[4,32,256]{2,1,0:T(8,128)S(1)} %collective-permute-done.3.odd_ref, bf16[2,2048,512]{2,1,0:T(8,128)(2,1)S(1)} %get-tuple-element.25.matrix.refs_12_), custom_call_target="tpu_custom_call" | custom-call | tf_op jit(solution)/shard_map/first/pallas_call | solution.py:501
  17.9 0.0 collective-permute-start.13
  17.9 0.5 collective-permute-start.4
  18.4 0.1 collective-permute-start.5
  18.5 1.1 %collective-permute-done.5 = f32[32,256]{1,0:T(8,128)S(1)} collective-permute-done((f32[32,256]{1,0:T(8,128)S(1)}, f32[32,256]{1,0:T(8,128)S(1)}, u32[]{:S(2)}, u32[]{:S(2)}) %collective-permute-start.5) | collective-permute-done | bytes 32800 | tf_op jit(solution)/shard_map/ppermute | solution.py:415
  19.6 0.0 collective-permute-done.4.other_ref
  19.6 0.3 image.2
  20.0 2.3 %collective-permute-start.6 = (f32[136,128]{1,0:T(8,128)S(1)}, f32[136,128]{1,0:T(8,128)S(1)}, u32[]{:S(2)}, u32[]{:S(2)}) collective-permute-start(f32[136,128]{1,0:T(8,128)S(1)} %get-tuple-element.27.refs_0_), channel_id=1, source_target_pairs={{0,14},{2,12},{4,10},{6,8},{8,6},{10,4},{12,2},{14,0},{1,11},{3,9}... | collective-permute-start | bytes 208904 | tf_op jit(solution)/shard_map/ppermute | solution.py:433
  22.3 0.2 collective-permute-start.7
  22.5 1.8 %collective-permute-start.8 = (f32[136,128]{1,0:T(8,128)S(1)}, f32[136,128]{1,0:T(8,128)S(1)}, u32[]{:S(2)}, u32[]{:S(2)}) collective-permute-start(f32[136,128]{1,0:T(8,128)S(1)} %get-tuple-element.27.refs_0_), channel_id=1, source_target_pairs={{0,4},{2,6},{4,0},{6,2},{8,12},{10,14},{12,8},{14,10},{1,9},{3,11}... | collective-permute-start | bytes 208904 | tf_op jit(solution)/shard_map/ppermute | solution.py:433
  24.2 1.5 %collective-permute-start.9 = (f32[136,128]{1,0:T(8,128)S(1)}, f32[136,128]{1,0:T(8,128)S(1)}, u32[]{:S(2)}, u32[]{:S(2)}) collective-permute-start(f32[136,128]{1,0:T(8,128)S(1)} %get-tuple-element.27.refs_0_), channel_id=1, source_target_pairs={{0,2},{2,0},{4,6},{6,4},{8,10},{10,8},{12,14},{14,12},{1,3},{3,1},... | collective-permute-start | bytes 208904 | tf_op jit(solution)/shard_map/ppermute | solution.py:433
  25.8 2.1 %collective-permute-done.6.refs_1_ = f32[136,128]{1,0:T(8,128)S(1)} collective-permute-done((f32[136,128]{1,0:T(8,128)S(1)}, f32[136,128]{1,0:T(8,128)S(1)}, u32[]{:S(2)}, u32[]{:S(2)}) %collective-permute-start.6) | collective-permute-done | bytes 69664 | tf_op jit(solution)/shard_map/ppermute | solution.py:433
  27.9 0.0 collective-permute-start.10
  27.9 0.7 %collective-permute-done.7.refs_2_ = f32[136,128]{1,0:T(8,128)S(1)} collective-permute-done((f32[136,128]{1,0:T(8,128)S(1)}, f32[136,128]{1,0:T(8,128)S(1)}, u32[]{:S(2)}, u32[]{:S(2)}) %collective-permute-start.7) | collective-permute-done | bytes 69664 | tf_op jit(solution)/shard_map/ppermute | solution.py:433
  28.6 0.0 collective-permute-start.11
  28.6 0.3 collective-permute-done.8.refs_3_
  28.9 0.7 %collective-permute-start.12 = (f32[136,128]{1,0:T(8,128)S(1)}, f32[136,128]{1,0:T(8,128)S(1)}, u32[]{:S(2)}, u32[]{:S(2)}) collective-permute-start(f32[136,128]{1,0:T(8,128)S(1)} %collective-permute-done.8.refs_3_), channel_id=1, source_target_pairs={{0,1},{1,0},{2,3},{3,2},{4,5},{5,4},{6,7},{7,6},{8,9},{9,8},{10,11... | collective-permute-start | bytes 208904 | tf_op jit(solution)/shard_map/ppermute | solution.py:415
  29.6 1.0 %inverse.2.refs_11_ = f32[32,128]{1,0:T(8,128)S(1)} custom-call(f32[32,128]{1,0:T(8,128)S(1)} %get-tuple-element.31.norm_ref.refs_10_), custom_call_target="tpu_custom_call" | custom-call | tf_op jit(solution)/shard_map/inverse/pallas_call | solution.py:536
  30.6 0.1 collect.1
  30.7 0.0 collective-permute-done.10.refs_5_
  30.7 0.0 collective-permute-done.11.refs_6_
  30.7 3.2 %step.2 = (f32[32,512]{1,0:T(8,128)S(1)}, f32[9,32,256]{2,1,0:T(8,128)S(1)}, f32[2,8,32,256]{3,2,1,0:T(8,128)S(1)}, f32[32,128]{1,0:T(8,128)S(1)}, f32[32,256]{1,0:T(8,128)S(1)}) custom-call(f32[136,128]{1,0:T(8,128)S(1)} %get-tuple-element.27.refs_0_, f32[136,128]{1,0:T(8,128)S(1)} %collective-permute-done.6.refs_1_, ...), custom_call_target="tpu_custom_call" | custom-call | tf_op jit(solution)/shard_map/step/pallas_call | solution.py:545
  33.9 0.1 collective-permute-start.14
  34.0 1.2 %collective-permute-done.14.other_ref = f32[32,512]{1,0:T(8,128)S(1)} collective-permute-done((f32[32,512]{1,0:T(8,128)S(1)}, f32[32,512]{1,0:T(8,128)S(1)}, u32[]{:S(2)}, u32[]{:S(2)}) %collective-permute-start.14) | collective-permute-done | bytes 65568 | tf_op jit(solution)/shard_map/ppermute | solution.py:415
  35.2 0.3 image.3.refs_0_
  35.5 2.1 %collective-permute-start.15 = (f32[136,128]{1,0:T(8,128)S(1)}, f32[136,128]{1,0:T(8,128)S(1)}, u32[]{:S(2)}, u32[]{:S(2)}) collective-permute-start(f32[136,128]{1,0:T(8,128)S(1)} %image.3.refs_0_), channel_id=1, source_target_pairs={{0,14},{2,12},{4,10},{6,8},{8,6},{10,4},{12,2},{14,0},{1,11},{3,9}... | collective-permute-start | bytes 208904 | tf_op jit(solution)/shard_map/ppermute | solution.py:433
  37.6 0.4 collective-permute-start.16
  38.0 2.6 %collective-permute-start.17 = (f32[136,128]{1,0:T(8,128)S(1)}, f32[136,128]{1,0:T(8,128)S(1)}, u32[]{:S(2)}, u32[]{:S(2)}) collective-permute-start(f32[136,128]{1,0:T(8,128)S(1)} %image.3.refs_0_), channel_id=1, source_target_pairs={{0,4},{2,6},{4,0},{6,2},{8,12},{10,14},{12,8},{14,10},{1,9},{3,11}... | collective-permute-start | bytes 208904 | tf_op jit(solution)/shard_map/ppermute | solution.py:433
  40.6 0.5 collective-permute-start.18
  41.1 2.3 %collective-permute-done.15.refs_1_ = f32[136,128]{1,0:T(8,128)S(1)} collective-permute-done((f32[136,128]{1,0:T(8,128)S(1)}, f32[136,128]{1,0:T(8,128)S(1)}, u32[]{:S(2)}, u32[]{:S(2)}) %collective-permute-start.15) | collective-permute-done | bytes 69664 | tf_op jit(solution)/shard_map/ppermute | solution.py:433
  43.4 0.0 collective-permute-start.19
  43.4 0.8 %collective-permute-done.16.refs_2_ = f32[136,128]{1,0:T(8,128)S(1)} collective-permute-done((f32[136,128]{1,0:T(8,128)S(1)}, f32[136,128]{1,0:T(8,128)S(1)}, u32[]{:S(2)}, u32[]{:S(2)}) %collective-permute-start.16) | collective-permute-done | bytes 69664 | tf_op jit(solution)/shard_map/ppermute | solution.py:433
  44.2 0.0 collective-permute-start.20
  44.2 1.1 %collective-permute-done.17.refs_3_ = f32[136,128]{1,0:T(8,128)S(1)} collective-permute-done((f32[136,128]{1,0:T(8,128)S(1)}, f32[136,128]{1,0:T(8,128)S(1)}, u32[]{:S(2)}, u32[]{:S(2)}) %collective-permute-start.17) | collective-permute-done | bytes 69664 | tf_op jit(solution)/shard_map/ppermute | solution.py:433
  45.3 0.0 collective-permute-start.21
  45.3 1.0 %inverse.3.refs_11_ = f32[32,128]{1,0:T(8,128)S(1)} custom-call(f32[32,128]{1,0:T(8,128)S(1)} %get-tuple-element.35.norm_ref.refs_10_), custom_call_target="tpu_custom_call" | custom-call | tf_op jit(solution)/shard_map/inverse/pallas_call | solution.py:536
  46.4 0.0 collective-permute-done.20.refs_6_
  46.4 0.2 collective-permute-done.21.refs_7_
  46.6 3.1 %step.3 = (f32[32,512]{1,0:T(8,128)S(1)}, f32[2,32,256]{2,1,0:T(8,128)S(1)}, f32[32,256]{1,0:T(8,128)S(1)}, f32[32,128]{1,0:T(8,128)S(1)}, f32[32,256]{1,0:T(8,128)S(1)}) custom-call(f32[136,128]{1,0:T(8,128)S(1)} %image.3.refs_0_, f32[136,128]{1,0:T(8,128)S(1)} %collective-permute-done.15.refs_1_, f32[136,128]{1,0:T(8,128)S(1)} %collective-permute-done.16.refs_2_, ...), custom_call_target="tpu_custom_call" | custom-call | tf_op jit(solution)/shard_map/step/pallas_call | solution.py:545
  49.7 0.4 collective-permute-start.22
  50.0 0.9 %collective-permute-done.22.other_ref = f32[32,512]{1,0:T(8,128)S(1)} collective-permute-done((f32[32,512]{1,0:T(8,128)S(1)}, f32[32,512]{1,0:T(8,128)S(1)}, u32[]{:S(2)}, u32[]{:S(2)}) %collective-permute-start.22) | collective-permute-done | bytes 65568 | tf_op jit(solution)/shard_map/ppermute | solution.py:415
  51.0 0.3 last_image.1
  51.3 2.2 %collective-permute-start.23 = (f32[8,128]{1,0:T(8,128)S(1)}, f32[8,128]{1,0:T(8,128)S(1)}, u32[]{:S(2)}, u32[]{:S(2)}) collective-permute-start(f32[8,128]{1,0:T(8,128)S(1)} %get-tuple-element.39.refs_0_), channel_id=1, source_target_pairs={{0,14},{2,12},{4,10},{6,8},{8,6},{10,4},{12,2},{14,0},{1,11},{3,9}... | collective-permute-start | bytes 12296 | tf_op jit(solution)/shard_map/ppermute | solution.py:433
  53.5 0.0 collective-permute-start.24
  53.5 2.3 %collective-permute-start.25 = (f32[8,128]{1,0:T(8,128)S(1)}, f32[8,128]{1,0:T(8,128)S(1)}, u32[]{:S(2)}, u32[]{:S(2)}) collective-permute-start(f32[8,128]{1,0:T(8,128)S(1)} %get-tuple-element.39.refs_0_), channel_id=1, source_target_pairs={{0,4},{2,6},{4,0},{6,2},{8,12},{10,14},{12,8},{14,10},{1,9},{3,11}... | collective-permute-start | bytes 12296 | tf_op jit(solution)/shard_map/ppermute | solution.py:433
  55.8 1.2 %collective-permute-start.26 = (f32[8,128]{1,0:T(8,128)S(1)}, f32[8,128]{1,0:T(8,128)S(1)}, u32[]{:S(2)}, u32[]{:S(2)}) collective-permute-start(f32[8,128]{1,0:T(8,128)S(1)} %get-tuple-element.39.refs_0_), channel_id=1, source_target_pairs={{0,2},{2,0},{4,6},{6,4},{8,10},{10,8},{12,14},{14,12},{1,3},{3,1},... | collective-permute-start | bytes 12296 | tf_op jit(solution)/shard_map/ppermute | solution.py:433
  57.0 0.6 %collective-permute-done.23.refs_1_ = f32[8,128]{1,0:T(8,128)S(1)} collective-permute-done((f32[8,128]{1,0:T(8,128)S(1)}, f32[8,128]{1,0:T(8,128)S(1)}, u32[]{:S(2)}, u32[]{:S(2)}) %collective-permute-start.23) | collective-permute-done | bytes 4128 | tf_op jit(solution)/shard_map/ppermute | solution.py:433
  57.6 0.4 collective-permute-done.24.refs_2_
  58.0 0.1 collective-permute-start.28
  58.1 0.4 collective-permute-start.29
  58.5 0.9 %collective-permute-done.26.refs_4_ = f32[8,128]{1,0:T(8,128)S(1)} collective-permute-done((f32[8,128]{1,0:T(8,128)S(1)}, f32[8,128]{1,0:T(8,128)S(1)}, u32[]{:S(2)}, u32[]{:S(2)}) %collective-permute-start.26) | collective-permute-done | bytes 4128 | tf_op jit(solution)/shard_map/ppermute | solution.py:433
  59.4 0.0 collective-permute-done.29.refs_7_
  59.4 1.8 %last.1 = (f32[32,256]{1,0:T(8,128)}, f32[32,256]{1,0:T(8,128)}) custom-call(f32[8,128]{1,0:T(8,128)S(1)} %get-tuple-element.39.refs_0_, f32[8,128]{1,0:T(8,128)S(1)} %collective-permute-done.23.refs_1_, f32[8,128]{1,0:T(8,128)S(1)} %collective-permute-done.24.refs_2_, f32[8,128]{1,0:T(8,128)S(1)} %collective-permute-done.25.refs_3_, ...), custom_call_target="tpu_custom_call" | custom-call | tf_op jit(solution)/shard_map/last/pallas_call | solution.py:568
  (10 shorter events, 0.0 us)
Async XLA Ops:
  1.5 8.6 %collective-permute-start = (f32[32,256]{1,0:T(8,128)S(1)}, f32[32,256]{1,0:T(8,128)S(1)}, u32[]{:S(2)}, u32[]{:S(2)}) collective-permute-start(f32[32,256]{1,0:T(8,128)S(1)} %multiply_multiply_fusion.refs_3_), channel_id=1, source_target_pairs={{0,8},{2,10},{4,12},{6,14},{8,0},{10,2},{12,4},{14,6},{1,9},{3,11}... | collective-permute-start | bytes 98312 | tf_op jit(solution)/shard_map/ppermute | solution.py:412
  5.5 5.7 %collective-permute-start.1 = (f32[32,256]{1,0:T(8,128)S(1)}, f32[32,256]{1,0:T(8,128)S(1)}, u32[]{:S(2)}, u32[]{:S(2)}) collective-permute-start(f32[32,256]{1,0:T(8,128)S(1)} %multiply_multiply_fusion.refs_3_), channel_id=1, source_target_pairs={{0,12},{2,14},{4,8},{6,10},{8,4},{10,6},{12,0},{14,2},{1,13},{3,15... | collective-permute-start | bytes 98312 | tf_op jit(solution)/shard_map/ppermute | solution.py:412
  6.9 4.4 %collective-permute-start.2 = (f32[32,256]{1,0:T(8,128)S(1)}, f32[32,256]{1,0:T(8,128)S(1)}, u32[]{:S(2)}, u32[]{:S(2)}) collective-permute-start(f32[32,256]{1,0:T(8,128)S(1)} %multiply_multiply_fusion.refs_3_), channel_id=1, source_target_pairs={{0,4},{2,6},{4,0},{6,2},{8,12},{10,14},{12,8},{14,10},{1,5},{3,7},... | collective-permute-start | bytes 98312 | tf_op jit(solution)/shard_map/ppermute | solution.py:412
  11.2 5.7 %collective-permute-start.3 = (f32[4,32,256]{2,1,0:T(8,128)S(1)}, f32[4,32,256]{2,1,0:T(8,128)S(1)}, u32[]{:S(2)}, u32[]{:S(2)}) collective-permute-start(f32[4,32,256]{2,1,0:T(8,128)S(1)} %join.1.joined_ref.even_ref.near_ref), channel_id=1, source_target_pairs={{0,2},{2,0},{4,6},{6,4},{8,10},{10,8},{12,14},{14,12},{1,3},{3,1},... | collective-permute-start | bytes 393224 | tf_op jit(solution)/shard_map/ppermute | solution.py:412
  17.9 12.8 %collective-permute-start.13 = (f32[8,32,256]{2,1,0:T(8,128)S(1)}, f32[8,32,256]{2,1,0:T(8,128)S(1)}, u32[]{:S(2)}, u32[]{:S(2)}) collective-permute-start(f32[8,32,256]{2,1,0:T(8,128)S(1)} %get-tuple-element.28.near_ref), channel_id=1, source_target_pairs={{0,1},{1,0},{2,3},{3,2},{4,5},{5,4},{6,7},{7,6},{8,9},{9,8},{10,11... | collective-permute-start | bytes 786440 | tf_op jit(solution)/shard_map/ppermute | solution.py:415
  17.9 1.7 %collective-permute-start.4 = (f32[32,640]{1,0:T(8,128)S(1)}, f32[32,640]{1,0:T(8,128)S(1)}, u32[]{:S(2)}, u32[]{:S(2)}) collective-permute-start(f32[32,640]{1,0:T(8,128)S(1)} %get-tuple-element.26.mine_ref), channel_id=1, source_target_pairs={{0,1},{1,0},{2,3},{3,2},{4,5},{5,4},{6,7},{7,6},{8,9},{9,8},{10,11... | collective-permute-start | bytes 245768 | tf_op jit(solution)/shard_map/ppermute | solution.py:415
  18.4 1.2 %collective-permute-start.5 = (f32[32,256]{1,0:T(8,128)S(1)}, f32[32,256]{1,0:T(8,128)S(1)}, u32[]{:S(2)}, u32[]{:S(2)}) collective-permute-start(f32[32,256]{1,0:T(8,128)S(1)} %multiply_multiply_fusion.refs_3_), channel_id=1, source_target_pairs={{0,1},{1,0},{2,3},{3,2},{4,5},{5,4},{6,7},{7,6},{8,9},{9,8},{10,11... | collective-permute-start | bytes 98312 | tf_op jit(solution)/shard_map/ppermute | solution.py:415
  20.0 7.9 %collective-permute-start.6 = (f32[136,128]{1,0:T(8,128)S(1)}, f32[136,128]{1,0:T(8,128)S(1)}, u32[]{:S(2)}, u32[]{:S(2)}) collective-permute-start(f32[136,128]{1,0:T(8,128)S(1)} %get-tuple-element.27.refs_0_), channel_id=1, source_target_pairs={{0,14},{2,12},{4,10},{6,8},{8,6},{10,4},{12,2},{14,0},{1,11},{3,9}... | collective-permute-start | bytes 208904 | tf_op jit(solution)/shard_map/ppermute | solution.py:433
  22.3 6.3 %collective-permute-start.7 = (f32[136,128]{1,0:T(8,128)S(1)}, f32[136,128]{1,0:T(8,128)S(1)}, u32[]{:S(2)}, u32[]{:S(2)}) collective-permute-start(f32[136,128]{1,0:T(8,128)S(1)} %get-tuple-element.27.refs_0_), channel_id=1, source_target_pairs={{0,6},{2,4},{4,2},{6,0},{8,14},{10,12},{12,10},{14,8},{1,13},{3,15... | collective-permute-start | bytes 208904 | tf_op jit(solution)/shard_map/ppermute | solution.py:433
  22.5 6.4 %collective-permute-start.8 = (f32[136,128]{1,0:T(8,128)S(1)}, f32[136,128]{1,0:T(8,128)S(1)}, u32[]{:S(2)}, u32[]{:S(2)}) collective-permute-start(f32[136,128]{1,0:T(8,128)S(1)} %get-tuple-element.27.refs_0_), channel_id=1, source_target_pairs={{0,4},{2,6},{4,0},{6,2},{8,12},{10,14},{12,8},{14,10},{1,9},{3,11}... | collective-permute-start | bytes 208904 | tf_op jit(solution)/shard_map/ppermute | solution.py:433
  24.2 6.5 %collective-permute-start.9 = (f32[136,128]{1,0:T(8,128)S(1)}, f32[136,128]{1,0:T(8,128)S(1)}, u32[]{:S(2)}, u32[]{:S(2)}) collective-permute-start(f32[136,128]{1,0:T(8,128)S(1)} %get-tuple-element.27.refs_0_), channel_id=1, source_target_pairs={{0,2},{2,0},{4,6},{6,4},{8,10},{10,8},{12,14},{14,12},{1,3},{3,1},... | collective-permute-start | bytes 208904 | tf_op jit(solution)/shard_map/ppermute | solution.py:433
  27.9 2.8 %collective-permute-start.10 = (f32[136,128]{1,0:T(8,128)S(1)}, f32[136,128]{1,0:T(8,128)S(1)}, u32[]{:S(2)}, u32[]{:S(2)}) collective-permute-start(f32[136,128]{1,0:T(8,128)S(1)} %collective-permute-done.6.refs_1_), channel_id=1, source_target_pairs={{0,1},{1,0},{2,3},{3,2},{4,5},{5,4},{6,7},{7,6},{8,9},{9,8},{10,11... | collective-permute-start | bytes 208904 | tf_op jit(solution)/shard_map/ppermute | solution.py:415
  28.6 2.1 %collective-permute-start.11 = (f32[136,128]{1,0:T(8,128)S(1)}, f32[136,128]{1,0:T(8,128)S(1)}, u32[]{:S(2)}, u32[]{:S(2)}) collective-permute-start(f32[136,128]{1,0:T(8,128)S(1)} %collective-permute-done.7.refs_2_), channel_id=1, source_target_pairs={{0,1},{1,0},{2,3},{3,2},{4,5},{5,4},{6,7},{7,6},{8,9},{9,8},{10,11... | collective-permute-start | bytes 208904 | tf_op jit(solution)/shard_map/ppermute | solution.py:415
  28.9 1.8 %collective-permute-start.12 = (f32[136,128]{1,0:T(8,128)S(1)}, f32[136,128]{1,0:T(8,128)S(1)}, u32[]{:S(2)}, u32[]{:S(2)}) collective-permute-start(f32[136,128]{1,0:T(8,128)S(1)} %collective-permute-done.8.refs_3_), channel_id=1, source_target_pairs={{0,1},{1,0},{2,3},{3,2},{4,5},{5,4},{6,7},{7,6},{8,9},{9,8},{10,11... | collective-permute-start | bytes 208904 | tf_op jit(solution)/shard_map/ppermute | solution.py:415
  33.9 1.3 %collective-permute-start.14 = (f32[32,512]{1,0:T(8,128)S(1)}, f32[32,512]{1,0:T(8,128)S(1)}, u32[]{:S(2)}, u32[]{:S(2)}) collective-permute-start(f32[32,512]{1,0:T(8,128)S(1)} %get-tuple-element.32.mine_ref), channel_id=1, source_target_pairs={{0,1},{1,0},{2,3},{3,2},{4,5},{5,4},{6,7},{7,6},{8,9},{9,8},{10,11... | collective-permute-start | bytes 196616 | tf_op jit(solution)/shard_map/ppermute | solution.py:415
  35.5 7.9 %collective-permute-start.15 = (f32[136,128]{1,0:T(8,128)S(1)}, f32[136,128]{1,0:T(8,128)S(1)}, u32[]{:S(2)}, u32[]{:S(2)}) collective-permute-start(f32[136,128]{1,0:T(8,128)S(1)} %image.3.refs_0_), channel_id=1, source_target_pairs={{0,14},{2,12},{4,10},{6,8},{8,6},{10,4},{12,2},{14,0},{1,11},{3,9}... | collective-permute-start | bytes 208904 | tf_op jit(solution)/shard_map/ppermute | solution.py:433
  37.6 6.6 %collective-permute-start.16 = (f32[136,128]{1,0:T(8,128)S(1)}, f32[136,128]{1,0:T(8,128)S(1)}, u32[]{:S(2)}, u32[]{:S(2)}) collective-permute-start(f32[136,128]{1,0:T(8,128)S(1)} %image.3.refs_0_), channel_id=1, source_target_pairs={{0,6},{2,4},{4,2},{6,0},{8,14},{10,12},{12,10},{14,8},{1,13},{3,15... | collective-permute-start | bytes 208904 | tf_op jit(solution)/shard_map/ppermute | solution.py:433
  38.0 7.3 %collective-permute-start.17 = (f32[136,128]{1,0:T(8,128)S(1)}, f32[136,128]{1,0:T(8,128)S(1)}, u32[]{:S(2)}, u32[]{:S(2)}) collective-permute-start(f32[136,128]{1,0:T(8,128)S(1)} %image.3.refs_0_), channel_id=1, source_target_pairs={{0,4},{2,6},{4,0},{6,2},{8,12},{10,14},{12,8},{14,10},{1,9},{3,11}... | collective-permute-start | bytes 208904 | tf_op jit(solution)/shard_map/ppermute | solution.py:433
  40.6 5.8 %collective-permute-start.18 = (f32[136,128]{1,0:T(8,128)S(1)}, f32[136,128]{1,0:T(8,128)S(1)}, u32[]{:S(2)}, u32[]{:S(2)}) collective-permute-start(f32[136,128]{1,0:T(8,128)S(1)} %image.3.refs_0_), channel_id=1, source_target_pairs={{0,2},{2,0},{4,6},{6,4},{8,10},{10,8},{12,14},{14,12},{1,3},{3,1},... | collective-permute-start | bytes 208904 | tf_op jit(solution)/shard_map/ppermute | solution.py:433
  43.4 2.9 %collective-permute-start.19 = (f32[136,128]{1,0:T(8,128)S(1)}, f32[136,128]{1,0:T(8,128)S(1)}, u32[]{:S(2)}, u32[]{:S(2)}) collective-permute-start(f32[136,128]{1,0:T(8,128)S(1)} %collective-permute-done.15.refs_1_), channel_id=1, source_target_pairs={{0,1},{1,0},{2,3},{3,2},{4,5},{5,4},{6,7},{7,6},{8,9},{9,8},{10,11... | collective-permute-start | bytes 208904 | tf_op jit(solution)/shard_map/ppermute | solution.py:415
  44.2 2.2 %collective-permute-start.20 = (f32[136,128]{1,0:T(8,128)S(1)}, f32[136,128]{1,0:T(8,128)S(1)}, u32[]{:S(2)}, u32[]{:S(2)}) collective-permute-start(f32[136,128]{1,0:T(8,128)S(1)} %collective-permute-done.16.refs_2_), channel_id=1, source_target_pairs={{0,1},{1,0},{2,3},{3,2},{4,5},{5,4},{6,7},{7,6},{8,9},{9,8},{10,11... | collective-permute-start | bytes 208904 | tf_op jit(solution)/shard_map/ppermute | solution.py:415
  45.3 1.3 %collective-permute-start.21 = (f32[136,128]{1,0:T(8,128)S(1)}, f32[136,128]{1,0:T(8,128)S(1)}, u32[]{:S(2)}, u32[]{:S(2)}) collective-permute-start(f32[136,128]{1,0:T(8,128)S(1)} %collective-permute-done.17.refs_3_), channel_id=1, source_target_pairs={{0,1},{1,0},{2,3},{3,2},{4,5},{5,4},{6,7},{7,6},{8,9},{9,8},{10,11... | collective-permute-start | bytes 208904 | tf_op jit(solution)/shard_map/ppermute | solution.py:415
  49.7 1.3 %collective-permute-start.22 = (f32[32,512]{1,0:T(8,128)S(1)}, f32[32,512]{1,0:T(8,128)S(1)}, u32[]{:S(2)}, u32[]{:S(2)}) collective-permute-start(f32[32,512]{1,0:T(8,128)S(1)} %get-tuple-element.37.mine_ref), channel_id=1, source_target_pairs={{0,1},{1,0},{2,3},{3,2},{4,5},{5,4},{6,7},{7,6},{8,9},{9,8},{10,11... | collective-permute-start | bytes 196616 | tf_op jit(solution)/shard_map/ppermute | solution.py:415
  51.3 6.3 %collective-permute-start.23 = (f32[8,128]{1,0:T(8,128)S(1)}, f32[8,128]{1,0:T(8,128)S(1)}, u32[]{:S(2)}, u32[]{:S(2)}) collective-permute-start(f32[8,128]{1,0:T(8,128)S(1)} %get-tuple-element.39.refs_0_), channel_id=1, source_target_pairs={{0,14},{2,12},{4,10},{6,8},{8,6},{10,4},{12,2},{14,0},{1,11},{3,9}... | collective-permute-start | bytes 12296 | tf_op jit(solution)/shard_map/ppermute | solution.py:433
  53.5 4.5 %collective-permute-start.24 = (f32[8,128]{1,0:T(8,128)S(1)}, f32[8,128]{1,0:T(8,128)S(1)}, u32[]{:S(2)}, u32[]{:S(2)}) collective-permute-start(f32[8,128]{1,0:T(8,128)S(1)} %get-tuple-element.39.refs_0_), channel_id=1, source_target_pairs={{0,6},{2,4},{4,2},{6,0},{8,14},{10,12},{12,10},{14,8},{1,13},{3,15... | collective-permute-start | bytes 12296 | tf_op jit(solution)/shard_map/ppermute | solution.py:433
  53.5 4.6 %collective-permute-start.25 = (f32[8,128]{1,0:T(8,128)S(1)}, f32[8,128]{1,0:T(8,128)S(1)}, u32[]{:S(2)}, u32[]{:S(2)}) collective-permute-start(f32[8,128]{1,0:T(8,128)S(1)} %get-tuple-element.39.refs_0_), channel_id=1, source_target_pairs={{0,4},{2,6},{4,0},{6,2},{8,12},{10,14},{12,8},{14,10},{1,9},{3,11}... | collective-permute-start | bytes 12296 | tf_op jit(solution)/shard_map/ppermute | solution.py:433
  55.8 3.6 %collective-permute-start.26 = (f32[8,128]{1,0:T(8,128)S(1)}, f32[8,128]{1,0:T(8,128)S(1)}, u32[]{:S(2)}, u32[]{:S(2)}) collective-permute-start(f32[8,128]{1,0:T(8,128)S(1)} %get-tuple-element.39.refs_0_), channel_id=1, source_target_pairs={{0,2},{2,0},{4,6},{6,4},{8,10},{10,8},{12,14},{14,12},{1,3},{3,1},... | collective-permute-start | bytes 12296 | tf_op jit(solution)/shard_map/ppermute | solution.py:433
  57.6 1.8 %collective-permute-start.27 = (f32[8,128]{1,0:T(8,128)S(1)}, f32[8,128]{1,0:T(8,128)S(1)}, u32[]{:S(2)}, u32[]{:S(2)}) collective-permute-start(f32[8,128]{1,0:T(8,128)S(1)} %collective-permute-done.23.refs_1_), channel_id=1, source_target_pairs={{0,1},{1,0},{2,3},{3,2},{4,5},{5,4},{6,7},{7,6},{8,9},{9,8},{10,11... | collective-permute-start | bytes 12296 | tf_op jit(solution)/shard_map/ppermute | solution.py:415
  58.0 1.4 %collective-permute-start.28 = (f32[8,128]{1,0:T(8,128)S(1)}, f32[8,128]{1,0:T(8,128)S(1)}, u32[]{:S(2)}, u32[]{:S(2)}) collective-permute-start(f32[8,128]{1,0:T(8,128)S(1)} %collective-permute-done.24.refs_2_), channel_id=1, source_target_pairs={{0,1},{1,0},{2,3},{3,2},{4,5},{5,4},{6,7},{7,6},{8,9},{9,8},{10,11... | collective-permute-start | bytes 12296 | tf_op jit(solution)/shard_map/ppermute | solution.py:415
  58.1 1.3 %collective-permute-start.29 = (f32[8,128]{1,0:T(8,128)S(1)}, f32[8,128]{1,0:T(8,128)S(1)}, u32[]{:S(2)}, u32[]{:S(2)}) collective-permute-start(f32[8,128]{1,0:T(8,128)S(1)} %collective-permute-done.25.refs_3_), channel_id=1, source_target_pairs={{0,1},{1,0},{2,3},{3,2},{4,5},{5,4},{6,7},{7,6},{8,9},{9,8},{10,11... | collective-permute-start | bytes 12296 | tf_op jit(solution)/shard_map/ppermute | solution.py:415

commit v14 on v12

--- a/solution.py
+++ b/solution.py
@@ -410,21 +410,24 @@
         if pieces != 8:
             found = [value] + [swap(value, k) for k in range(1, pieces)]
             return found, [(k, k) for k in range(pieces)]
-        turns = ((2, 4), (7, 6), (1, 2))
-
-        def fetch(source, masks):
+        turns = ((7, 5), (3, 6), (2, 4), (1, 1))
+        fetched = []
+        passed = []
+        places = {0: (0, 0)}
+        for turn, masks in enumerate(turns, 1):
             pairs = [
                 (i * 2 + core, (i ^ mask) * 2 + core)
                 for core, mask in enumerate(masks)
                 for i in range(pieces)
             ]
-            return lax.ppermute(source, ("row", "col"), pairs)
-
-        fetched = [fetch(value, masks) for masks in turns]
-        fetched.append(fetch(fetched[0], (1, 1)))
-        found = [value, *fetched, *map(across, fetched)]
-        places = [(0, 0), (3, 7), (1, 5), (4, 8), (5, 1), (8, 4), (6, 2), (2, 6)]
-        return found, places
+            fetched.append(lax.ppermute(value, ("row", "col"), pairs))
+            if masks[0] == masks[1]:
+                places[masks[0]] = (turn, turn)
+            else:
+                passed.append(across(fetched[-1]))
+                places[masks[0]] = (turn, turn + len(turns))
+                places[masks[1]] = (turn + len(turns), turn)
+        return [value, *fetched, *passed], [places[k] for k in range(pieces)]
 
     right_side = signs.astype(F32) * vertex_weight[None, :] * column_scale[:, None]
     far_side = across(right_side)[None]
@@ -433,7 +436,7 @@
     matrix = shape(2, depth, group, dtype=BF16)
     total = shape(depth // tile * (group // tile), tile, tile)
     slots = tiles.shape[0]
-    half = slots // 2
+    half = slots * 3 // 8
     rest = shape(slots - half, tile, tile, dtype=BF16)
     lists = [pltpu.with_memory_space_constraint(x, pltpu.HBM) for x in (tile_rows, tile_cols)]
     lists_scratch = [pltpu.SMEM(x.shape, jnp.int32) for x in lists]

time: 62 us -> 61.2 us (0.987); the launches traced: 61.2 us -> 61.2 us
  waiting for transfers between devices: 17.3 us -> 12.7 us
  starting transfers between devices: 25.5 us -> 29.1 us
  Pallas kernels: 16.1 us -> 17.2 us
    ppermute x12, starting transfers between devices: 15.7 us -> 18.4 us  [exchange(): fetched.append(lax.ppermute(value, ('row', 'col'), pairs))]
    ppermute x12, waiting for transfers between devices: 10.1 us -> 8.18 us  [exchange(): fetched.append(lax.ppermute(value, ('row', 'col'), pairs))]
    ppermute x17 -> x14, waiting for transfers between devices: 4.81 us -> 3.17 us  [across(): lax.ppermute(value, 'col', [(i, (i + 1) % col_devices) for i in range(col...]
    ppermute x4, waiting for transfers between devices: 2.41 us -> 1.35 us  [swap(): return lax.ppermute(value, 'row', [(i, i ^ mask) for i in range(pieces)])]
    pallas_call x1, Pallas kernels: 2.23 us -> 3.23 us  [per_device(): pl.pallas_call(functools.partial(dense_kernel, rows_dev), out_shape=(matr...]
    ppermute x17 -> x14, starting transfers between devices: 2.56 us -> 3.41 us  [across(): lax.ppermute(value, 'col', [(i, (i + 1) % col_devices) for i in range(col...]
  transfers between devices with their start and end apart: 33 -> 30, of which waited for: 19 -> 13; matrix products, arithmetic and copies ran while one was open for 0% -> 0% of each run, Pallas kernels for 11% -> 13%
where the time goes in v14:
time: 61.2 us
  starting transfers between devices  29.1 us (48%)
  Pallas kernels  17.2 us (28%)
  waiting for transfers between devices  12.7 us (21%)
  between operations  1.44 us (2%)
  other arithmetic  0.85 us (1%)
    ppermute x12, starting transfers between devices, exchange(): fetched.append(lax.ppermute(value, ('row', 'col'), pairs))  18.4 us
    ppermute x12, waiting for transfers between devices, exchange(): fetched.append(lax.ppermute(value, ('row', 'col'), pairs))  8.18 us
    ppermute x4, starting transfers between devices, swap(): return lax.ppermute(value, 'row', [(i, i ^ mask) for i in range(pieces)])  7.2 us
    pallas_call x2, Pallas kernels, per_device(): pl.pallas_call(functools.partial(step_kernel, len(found), places, not fir...  6.12 us
    ppermute x14, starting transfers between devices, across(): lax.ppermute(value, 'col', [(i, (i + 1) % col_devices) for i in range(col...  3.41 us
    pallas_call x1, Pallas kernels, per_device(): pl.pallas_call(functools.partial(dense_kernel, rows_dev), out_shape=(matr...  3.23 us
    ppermute x14, waiting for transfers between devices, across(): lax.ppermute(value, 'col', [(i, (i + 1) % col_devices) for i in range(col...  3.17 us
    pallas_call x1, Pallas kernels, per_device(): pl.pallas_call(functools.partial(gather_kernel, rows_dev), out_shape=(tot...  2.33 us
  transfers between devices with their start and end apart: 30, of which 13 were waited for; matrix products, arithmetic and copies ran while one was open for 0% of the time, Pallas kernels for 13%

profile of v14, /device:TPU:0, one launch (start us, length us, event | category | flops | bytes accessed | tf_op | source)
XLA Modules:
  0.0 61.2 jit_solution(5208435269800635946)
XLA Ops:
  0.6 0.8 %multiply_multiply_fusion.refs_3_ = f32[32,256]{1,0:T(8,128)S(1)} fusion(s32[32,256]{1,0:T(8,128)} %param.11, f32[32]{0:T(128)} %param.13, f32[256]{0:T(256)} %param.12), kind=kLoop, calls=%fused_computation | loop fusion | flops 24576 | bytes 66688 | tf_op jit(solution)/shard_map/mul | solution.py:432
  1.5 4.0 %collective-permute-start = (f32[32,256]{1,0:T(8,128)S(1)}, f32[32,256]{1,0:T(8,128)S(1)}, u32[]{:S(2)}, u32[]{:S(2)}) collective-permute-start(f32[32,256]{1,0:T(8,128)S(1)} %multiply_multiply_fusion.refs_3_), channel_id=1, source_target_pairs={{0,8},{2,10},{4,12},{6,14},{8,0},{10,2},{12,4},{14,6},{1,9},{3,11}... | collective-permute-start | bytes 98312 | tf_op jit(solution)/shard_map/ppermute | solution.py:402
  5.5 1.3 %collective-permute-start.1 = (f32[32,256]{1,0:T(8,128)S(1)}, f32[32,256]{1,0:T(8,128)S(1)}, u32[]{:S(2)}, u32[]{:S(2)}) collective-permute-start(f32[32,256]{1,0:T(8,128)S(1)} %multiply_multiply_fusion.refs_3_), channel_id=1, source_target_pairs={{0,12},{2,14},{4,8},{6,10},{8,4},{10,6},{12,0},{14,2},{1,13},{3,15... | collective-permute-start | bytes 98312 | tf_op jit(solution)/shard_map/ppermute | solution.py:402
  6.9 0.2 collective-permute-start.2
  7.8 2.3 %gather.1 = (f32[64,128,128]{2,1,0:T(8,128)S(1)}, bf16[82,128,128]{2,1,0:T(8,128)(2,1)S(1)}) custom-call(s32[1]{0:T(128)S(6)} %copy.11.count_ref, s32[130]{0:T(256)} %rows_hbm.3, s32[130]{0:T(256)} %cols_hbm.3, bf16[130,128,128]{2,1,0:T(8,128)(2,1)} %tiles_ref.1), custom_call_target="tpu_custom_call" | custom-call | flops 8519680 | bytes 8519680 | tf_op jit(solution)/shard_map/gather/pallas_call | solution.py:446
  10.1 0.0 collective-permute-done.refs_0_
  10.1 1.1 %collective-permute-done.1.refs_1_ = f32[32,256]{1,0:T(8,128)S(1)} collective-permute-done((f32[32,256]{1,0:T(8,128)S(1)}, f32[32,256]{1,0:T(8,128)S(1)}, u32[]{:S(2)}, u32[]{:S(2)}) %collective-permute-start.1) | collective-permute-done | bytes 32800 | tf_op jit(solution)/shard_map/ppermute | solution.py:402
  11.2 0.0 collective-permute-done.2.refs_2_
  11.2 1.6 %collective-permute-start.3 = (f32[4,32,256]{2,1,0:T(8,128)S(1)}, f32[4,32,256]{2,1,0:T(8,128)S(1)}, u32[]{:S(2)}, u32[]{:S(2)}) collective-permute-start(f32[4,32,256]{2,1,0:T(8,128)S(1)} %join.1.joined_ref.even_ref.near_ref), channel_id=1, source_target_pairs={{0,2},{2,0},{4,6},{6,4},{8,10},{10,8},{12,14},{14,12},{1,3},{3,1},... | collective-permute-start | bytes 393224 | tf_op jit(solution)/shard_map/ppermute | solution.py:402
  12.8 3.2 %dense.1 = (bf16[2,2048,512]{2,1,0:T(8,128)(2,1)S(1)}, f32[64,128,128]{2,1,0:T(8,128)S(1)}) custom-call(s32[1]{0:T(128)S(6)} %copy.11.count_ref, s32[130]{0:T(256)} %rows_hbm.3, s32[130]{0:T(256)} %cols_hbm.3, bf16[82,128,128]{2,1,0:T(8,128)(2,1)S(1)} %get-tuple-element.24.rest, ...), custom_call_target="tpu_custom_call", output_to_operand_aliasing={{1}: (4, {})} | custom-call | flops 8519680 | bytes 8519680 | tf_op jit(solution)/shard_map/dense/pallas_call | solution.py:472
  16.1 0.2 collective-permute-done.3.odd_ref
  16.3 0.9 %first.1 = (f32[32,640]{1,0:T(8,128)S(1)}, f32[8,32,256]{2,1,0:T(8,128)S(1)}) custom-call(f32[4,32,256]{2,1,0:T(8,128)S(1)} %join.1.joined_ref.even_ref.near_ref, f32[4,32,256]{2,1,0:T(8,128)S(1)} %collective-permute-done.3.odd_ref, bf16[2,2048,512]{2,1,0:T(8,128)(2,1)S(1)} %get-tuple-element.25.matrix.refs_12_), custom_call_target="tpu_custom_call" | custom-call | tf_op jit(solution)/shard_map/first/pallas_call | solution.py:491
  17.2 0.0 collective-permute-start.13
  17.2 0.5 collective-permute-start.4
  17.7 0.1 collective-permute-start.5
  17.8 1.1 %collective-permute-done.5 = f32[32,256]{1,0:T(8,128)S(1)} collective-permute-done((f32[32,256]{1,0:T(8,128)S(1)}, f32[32,256]{1,0:T(8,128)S(1)}, u32[]{:S(2)}, u32[]{:S(2)}) %collective-permute-start.5) | collective-permute-done | bytes 32800 | tf_op jit(solution)/shard_map/ppermute | solution.py:405
  18.9 0.0 collective-permute-done.4.other_ref
  18.9 0.3 image.2
  19.3 3.0 %collective-permute-start.6 = (f32[136,128]{1,0:T(8,128)S(1)}, f32[136,128]{1,0:T(8,128)S(1)}, u32[]{:S(2)}, u32[]{:S(2)}) collective-permute-start(f32[136,128]{1,0:T(8,128)S(1)} %get-tuple-element.27.refs_0_), channel_id=1, source_target_pairs={{0,14},{2,12},{4,10},{6,8},{8,6},{10,4},{12,2},{14,0},{1,11},{3,9}... | collective-permute-start | bytes 208904 | tf_op jit(solution)/shard_map/ppermute | solution.py:423
  22.3 1.2 %collective-permute-start.7 = (f32[136,128]{1,0:T(8,128)S(1)}, f32[136,128]{1,0:T(8,128)S(1)}, u32[]{:S(2)}, u32[]{:S(2)}) collective-permute-start(f32[136,128]{1,0:T(8,128)S(1)} %get-tuple-element.27.refs_0_), channel_id=1, source_target_pairs={{0,6},{2,4},{4,2},{6,0},{8,14},{10,12},{12,10},{14,8},{1,13},{3,15... | collective-permute-start | bytes 208904 | tf_op jit(solution)/shard_map/ppermute | solution.py:423
  23.5 0.8 %collective-permute-start.8 = (f32[136,128]{1,0:T(8,128)S(1)}, f32[136,128]{1,0:T(8,128)S(1)}, u32[]{:S(2)}, u32[]{:S(2)}) collective-permute-start(f32[136,128]{1,0:T(8,128)S(1)} %get-tuple-element.27.refs_0_), channel_id=1, source_target_pairs={{0,4},{2,6},{4,0},{6,2},{8,12},{10,14},{12,8},{14,10},{1,9},{3,11}... | collective-permute-start | bytes 208904 | tf_op jit(solution)/shard_map/ppermute | solution.py:423
  24.2 1.5 %collective-permute-start.9 = (f32[136,128]{1,0:T(8,128)S(1)}, f32[136,128]{1,0:T(8,128)S(1)}, u32[]{:S(2)}, u32[]{:S(2)}) collective-permute-start(f32[136,128]{1,0:T(8,128)S(1)} %get-tuple-element.27.refs_0_), channel_id=1, source_target_pairs={{0,2},{2,0},{4,6},{6,4},{8,10},{10,8},{12,14},{14,12},{1,3},{3,1},... | collective-permute-start | bytes 208904 | tf_op jit(solution)/shard_map/ppermute | solution.py:423
  25.8 0.7 %collective-permute-done.6.refs_1_ = f32[136,128]{1,0:T(8,128)S(1)} collective-permute-done((f32[136,128]{1,0:T(8,128)S(1)}, f32[136,128]{1,0:T(8,128)S(1)}, u32[]{:S(2)}, u32[]{:S(2)}) %collective-permute-start.6) | collective-permute-done | bytes 69664 | tf_op jit(solution)/shard_map/ppermute | solution.py:423
  26.4 0.2 collective-permute-start.10
  26.6 1.7 %collective-permute-done.7.refs_2_ = f32[136,128]{1,0:T(8,128)S(1)} collective-permute-done((f32[136,128]{1,0:T(8,128)S(1)}, f32[136,128]{1,0:T(8,128)S(1)}, u32[]{:S(2)}, u32[]{:S(2)}) %collective-permute-start.7) | collective-permute-done | bytes 69664 | tf_op jit(solution)/shard_map/ppermute | solution.py:423
  28.4 0.0 collective-permute-start.11
  28.4 0.5 collective-permute-done.8.refs_3_
  28.9 0.8 %collective-permute-start.12 = (f32[136,128]{1,0:T(8,128)S(1)}, f32[136,128]{1,0:T(8,128)S(1)}, u32[]{:S(2)}, u32[]{:S(2)}) collective-permute-start(f32[136,128]{1,0:T(8,128)S(1)} %collective-permute-done.8.refs_3_), channel_id=1, source_target_pairs={{0,1},{1,0},{2,3},{3,2},{4,5},{5,4},{6,7},{7,6},{8,9},{9,8},{10,11... | collective-permute-start | bytes 208904 | tf_op jit(solution)/shard_map/ppermute | solution.py:405
  29.7 0.9 %inverse.2.refs_11_ = f32[32,128]{1,0:T(8,128)S(1)} custom-call(f32[32,128]{1,0:T(8,128)S(1)} %get-tuple-element.31.norm_ref.refs_10_), custom_call_target="tpu_custom_call" | custom-call | tf_op jit(solution)/shard_map/inverse/pallas_call | solution.py:526
  30.6 0.0 collective-permute-done.13.far_ref
  30.6 0.1 collect.1
  30.7 0.0 collective-permute-done.11.refs_6_
  30.7 3.1 %step.2 = (f32[32,512]{1,0:T(8,128)S(1)}, f32[9,32,256]{2,1,0:T(8,128)S(1)}, f32[2,8,32,256]{3,2,1,0:T(8,128)S(1)}, f32[32,128]{1,0:T(8,128)S(1)}, f32[32,256]{1,0:T(8,128)S(1)}) custom-call(f32[136,128]{1,0:T(8,128)S(1)} %get-tuple-element.27.refs_0_, f32[136,128]{1,0:T(8,128)S(1)} %collective-permute-done.6.refs_1_, ...), custom_call_target="tpu_custom_call" | custom-call | tf_op jit(solution)/shard_map/step/pallas_call | solution.py:535
  33.8 0.2 collective-permute-start.14
  34.0 1.0 %collective-permute-done.14.other_ref = f32[32,512]{1,0:T(8,128)S(1)} collective-permute-done((f32[32,512]{1,0:T(8,128)S(1)}, f32[32,512]{1,0:T(8,128)S(1)}, u32[]{:S(2)}, u32[]{:S(2)}) %collective-permute-start.14) | collective-permute-done | bytes 65568 | tf_op jit(solution)/shard_map/ppermute | solution.py:405
  35.1 0.3 image.3.refs_0_
  35.4 2.3 %collective-permute-start.15 = (f32[136,128]{1,0:T(8,128)S(1)}, f32[136,128]{1,0:T(8,128)S(1)}, u32[]{:S(2)}, u32[]{:S(2)}) collective-permute-start(f32[136,128]{1,0:T(8,128)S(1)} %image.3.refs_0_), channel_id=1, source_target_pairs={{0,14},{2,12},{4,10},{6,8},{8,6},{10,4},{12,2},{14,0},{1,11},{3,9}... | collective-permute-start | bytes 208904 | tf_op jit(solution)/shard_map/ppermute | solution.py:423
  37.8 0.0 collective-permute-start.16
  37.8 2.6 %collective-permute-start.17 = (f32[136,128]{1,0:T(8,128)S(1)}, f32[136,128]{1,0:T(8,128)S(1)}, u32[]{:S(2)}, u32[]{:S(2)}) collective-permute-start(f32[136,128]{1,0:T(8,128)S(1)} %image.3.refs_0_), channel_id=1, source_target_pairs={{0,4},{2,6},{4,0},{6,2},{8,12},{10,14},{12,8},{14,10},{1,9},{3,11}... | collective-permute-start | bytes 208904 | tf_op jit(solution)/shard_map/ppermute | solution.py:423
  40.4 0.9 %collective-permute-start.18 = (f32[136,128]{1,0:T(8,128)S(1)}, f32[136,128]{1,0:T(8,128)S(1)}, u32[]{:S(2)}, u32[]{:S(2)}) collective-permute-start(f32[136,128]{1,0:T(8,128)S(1)} %image.3.refs_0_), channel_id=1, source_target_pairs={{0,2},{2,0},{4,6},{6,4},{8,10},{10,8},{12,14},{14,12},{1,3},{3,1},... | collective-permute-start | bytes 208904 | tf_op jit(solution)/shard_map/ppermute | solution.py:423
  41.3 2.1 %collective-permute-done.15.refs_1_ = f32[136,128]{1,0:T(8,128)S(1)} collective-permute-done((f32[136,128]{1,0:T(8,128)S(1)}, f32[136,128]{1,0:T(8,128)S(1)}, u32[]{:S(2)}, u32[]{:S(2)}) %collective-permute-start.15) | collective-permute-done | bytes 69664 | tf_op jit(solution)/shard_map/ppermute | solution.py:423
  43.4 0.0 collective-permute-start.19
  43.4 0.8 %collective-permute-done.16.refs_2_ = f32[136,128]{1,0:T(8,128)S(1)} collective-permute-done((f32[136,128]{1,0:T(8,128)S(1)}, f32[136,128]{1,0:T(8,128)S(1)}, u32[]{:S(2)}, u32[]{:S(2)}) %collective-permute-start.16) | collective-permute-done | bytes 69664 | tf_op jit(solution)/shard_map/ppermute | solution.py:423
  44.2 0.7 %collective-permute-start.21 = (f32[136,128]{1,0:T(8,128)S(1)}, f32[136,128]{1,0:T(8,128)S(1)}, u32[]{:S(2)}, u32[]{:S(2)}) collective-permute-start(f32[136,128]{1,0:T(8,128)S(1)} %collective-permute-done.17.refs_3_), channel_id=1, source_target_pairs={{0,1},{1,0},{2,3},{3,2},{4,5},{5,4},{6,7},{7,6},{8,9},{9,8},{10,11... | collective-permute-start | bytes 208904 | tf_op jit(solution)/shard_map/ppermute | solution.py:405
  44.9 0.9 %inverse.3.refs_11_ = f32[32,128]{1,0:T(8,128)S(1)} custom-call(f32[32,128]{1,0:T(8,128)S(1)} %get-tuple-element.35.norm_ref.refs_10_), custom_call_target="tpu_custom_call" | custom-call | tf_op jit(solution)/shard_map/inverse/pallas_call | solution.py:526
  45.8 0.0 collective-permute-done.19.refs_5_
  45.8 3.1 %step.3 = (f32[32,512]{1,0:T(8,128)S(1)}, f32[2,32,256]{2,1,0:T(8,128)S(1)}, f32[32,256]{1,0:T(8,128)S(1)}, f32[32,128]{1,0:T(8,128)S(1)}, f32[32,256]{1,0:T(8,128)S(1)}) custom-call(f32[136,128]{1,0:T(8,128)S(1)} %image.3.refs_0_, f32[136,128]{1,0:T(8,128)S(1)} %collective-permute-done.15.refs_1_, f32[136,128]{1,0:T(8,128)S(1)} %collective-permute-done.16.refs_2_, ...), custom_call_target="tpu_custom_call" | custom-call | tf_op jit(solution)/shard_map/step/pallas_call | solution.py:535
  48.9 0.3 collective-permute-start.22
  49.2 1.0 %collective-permute-done.22.other_ref = f32[32,512]{1,0:T(8,128)S(1)} collective-permute-done((f32[32,512]{1,0:T(8,128)S(1)}, f32[32,512]{1,0:T(8,128)S(1)}, u32[]{:S(2)}, u32[]{:S(2)}) %collective-permute-start.22) | collective-permute-done | bytes 65568 | tf_op jit(solution)/shard_map/ppermute | solution.py:405
  50.2 0.3 last_image.1
  50.5 2.6 %collective-permute-start.23 = (f32[8,128]{1,0:T(8,128)S(1)}, f32[8,128]{1,0:T(8,128)S(1)}, u32[]{:S(2)}, u32[]{:S(2)}) collective-permute-start(f32[8,128]{1,0:T(8,128)S(1)} %get-tuple-element.39.refs_0_), channel_id=1, source_target_pairs={{0,14},{2,12},{4,10},{6,8},{8,6},{10,4},{12,2},{14,0},{1,11},{3,9}... | collective-permute-start | bytes 12296 | tf_op jit(solution)/shard_map/ppermute | solution.py:423
  53.1 0.1 collective-permute-start.24
  53.3 2.7 %collective-permute-start.25 = (f32[8,128]{1,0:T(8,128)S(1)}, f32[8,128]{1,0:T(8,128)S(1)}, u32[]{:S(2)}, u32[]{:S(2)}) collective-permute-start(f32[8,128]{1,0:T(8,128)S(1)} %get-tuple-element.39.refs_0_), channel_id=1, source_target_pairs={{0,4},{2,6},{4,0},{6,2},{8,12},{10,14},{12,8},{14,10},{1,9},{3,11}... | collective-permute-start | bytes 12296 | tf_op jit(solution)/shard_map/ppermute | solution.py:423
  55.9 0.7 %collective-permute-start.26 = (f32[8,128]{1,0:T(8,128)S(1)}, f32[8,128]{1,0:T(8,128)S(1)}, u32[]{:S(2)}, u32[]{:S(2)}) collective-permute-start(f32[8,128]{1,0:T(8,128)S(1)} %get-tuple-element.39.refs_0_), channel_id=1, source_target_pairs={{0,2},{2,0},{4,6},{6,4},{8,10},{10,8},{12,14},{14,12},{1,3},{3,1},... | collective-permute-start | bytes 12296 | tf_op jit(solution)/shard_map/ppermute | solution.py:423
  56.6 0.2 collective-permute-done.23.refs_1_
  56.8 0.0 collective-permute-start.27
  56.8 0.8 %collective-permute-done.24.refs_2_ = f32[8,128]{1,0:T(8,128)S(1)} collective-permute-done((f32[8,128]{1,0:T(8,128)S(1)}, f32[8,128]{1,0:T(8,128)S(1)}, u32[]{:S(2)}, u32[]{:S(2)}) %collective-permute-start.24) | collective-permute-done | bytes 4128 | tf_op jit(solution)/shard_map/ppermute | solution.py:423
  57.7 0.0 collective-permute-start.28
  57.7 0.0 collective-permute-done.25.refs_3_
  57.7 0.5 collective-permute-start.29
  58.2 1.4 %collective-permute-done.26.refs_4_ = f32[8,128]{1,0:T(8,128)S(1)} collective-permute-done((f32[8,128]{1,0:T(8,128)S(1)}, f32[8,128]{1,0:T(8,128)S(1)}, u32[]{:S(2)}, u32[]{:S(2)}) %collective-permute-start.26) | collective-permute-done | bytes 4128 | tf_op jit(solution)/shard_map/ppermute | solution.py:423
  59.5 0.0 collective-permute-done.28.refs_6_
  59.6 0.0 collective-permute-done.29.refs_7_
  59.6 1.7 %last.1 = (f32[32,256]{1,0:T(8,128)}, f32[32,256]{1,0:T(8,128)}) custom-call(f32[8,128]{1,0:T(8,128)S(1)} %get-tuple-element.39.refs_0_, f32[8,128]{1,0:T(8,128)S(1)} %collective-permute-done.23.refs_1_, f32[8,128]{1,0:T(8,128)S(1)} %collective-permute-done.24.refs_2_, f32[8,128]{1,0:T(8,128)S(1)} %collective-permute-done.25.refs_3_, ...), custom_call_target="tpu_custom_call" | custom-call | tf_op jit(solution)/shard_map/last/pallas_call | solution.py:558
  (10 shorter events, 0.0 us)
Async XLA Ops:
  1.5 8.6 %collective-permute-start = (f32[32,256]{1,0:T(8,128)S(1)}, f32[32,256]{1,0:T(8,128)S(1)}, u32[]{:S(2)}, u32[]{:S(2)}) collective-permute-start(f32[32,256]{1,0:T(8,128)S(1)} %multiply_multiply_fusion.refs_3_), channel_id=1, source_target_pairs={{0,8},{2,10},{4,12},{6,14},{8,0},{10,2},{12,4},{14,6},{1,9},{3,11}... | collective-permute-start | bytes 98312 | tf_op jit(solution)/shard_map/ppermute | solution.py:402
  5.5 5.7 %collective-permute-start.1 = (f32[32,256]{1,0:T(8,128)S(1)}, f32[32,256]{1,0:T(8,128)S(1)}, u32[]{:S(2)}, u32[]{:S(2)}) collective-permute-start(f32[32,256]{1,0:T(8,128)S(1)} %multiply_multiply_fusion.refs_3_), channel_id=1, source_target_pairs={{0,12},{2,14},{4,8},{6,10},{8,4},{10,6},{12,0},{14,2},{1,13},{3,15... | collective-permute-start | bytes 98312 | tf_op jit(solution)/shard_map/ppermute | solution.py:402
  6.9 4.4 %collective-permute-start.2 = (f32[32,256]{1,0:T(8,128)S(1)}, f32[32,256]{1,0:T(8,128)S(1)}, u32[]{:S(2)}, u32[]{:S(2)}) collective-permute-start(f32[32,256]{1,0:T(8,128)S(1)} %multiply_multiply_fusion.refs_3_), channel_id=1, source_target_pairs={{0,4},{2,6},{4,0},{6,2},{8,12},{10,14},{12,8},{14,10},{1,5},{3,7},... | collective-permute-start | bytes 98312 | tf_op jit(solution)/shard_map/ppermute | solution.py:402
  11.2 5.0 %collective-permute-start.3 = (f32[4,32,256]{2,1,0:T(8,128)S(1)}, f32[4,32,256]{2,1,0:T(8,128)S(1)}, u32[]{:S(2)}, u32[]{:S(2)}) collective-permute-start(f32[4,32,256]{2,1,0:T(8,128)S(1)} %join.1.joined_ref.even_ref.near_ref), channel_id=1, source_target_pairs={{0,2},{2,0},{4,6},{6,4},{8,10},{10,8},{12,14},{14,12},{1,3},{3,1},... | collective-permute-start | bytes 393224 | tf_op jit(solution)/shard_map/ppermute | solution.py:402
  17.2 13.5 %collective-permute-start.13 = (f32[8,32,256]{2,1,0:T(8,128)S(1)}, f32[8,32,256]{2,1,0:T(8,128)S(1)}, u32[]{:S(2)}, u32[]{:S(2)}) collective-permute-start(f32[8,32,256]{2,1,0:T(8,128)S(1)} %get-tuple-element.28.near_ref), channel_id=1, source_target_pairs={{0,1},{1,0},{2,3},{3,2},{4,5},{5,4},{6,7},{7,6},{8,9},{9,8},{10,11... | collective-permute-start | bytes 786440 | tf_op jit(solution)/shard_map/ppermute | solution.py:405
  17.2 1.7 %collective-permute-start.4 = (f32[32,640]{1,0:T(8,128)S(1)}, f32[32,640]{1,0:T(8,128)S(1)}, u32[]{:S(2)}, u32[]{:S(2)}) collective-permute-start(f32[32,640]{1,0:T(8,128)S(1)} %get-tuple-element.26.mine_ref), channel_id=1, source_target_pairs={{0,1},{1,0},{2,3},{3,2},{4,5},{5,4},{6,7},{7,6},{8,9},{9,8},{10,11... | collective-permute-start | bytes 245768 | tf_op jit(solution)/shard_map/ppermute | solution.py:405
  17.7 1.2 %collective-permute-start.5 = (f32[32,256]{1,0:T(8,128)S(1)}, f32[32,256]{1,0:T(8,128)S(1)}, u32[]{:S(2)}, u32[]{:S(2)}) collective-permute-start(f32[32,256]{1,0:T(8,128)S(1)} %multiply_multiply_fusion.refs_3_), channel_id=1, source_target_pairs={{0,1},{1,0},{2,3},{3,2},{4,5},{5,4},{6,7},{7,6},{8,9},{9,8},{10,11... | collective-permute-start | bytes 98312 | tf_op jit(solution)/shard_map/ppermute | solution.py:405
  19.3 7.1 %collective-permute-start.6 = (f32[136,128]{1,0:T(8,128)S(1)}, f32[136,128]{1,0:T(8,128)S(1)}, u32[]{:S(2)}, u32[]{:S(2)}) collective-permute-start(f32[136,128]{1,0:T(8,128)S(1)} %get-tuple-element.27.refs_0_), channel_id=1, source_target_pairs={{0,14},{2,12},{4,10},{6,8},{8,6},{10,4},{12,2},{14,0},{1,11},{3,9}... | collective-permute-start | bytes 208904 | tf_op jit(solution)/shard_map/ppermute | solution.py:423
  22.3 6.1 %collective-permute-start.7 = (f32[136,128]{1,0:T(8,128)S(1)}, f32[136,128]{1,0:T(8,128)S(1)}, u32[]{:S(2)}, u32[]{:S(2)}) collective-permute-start(f32[136,128]{1,0:T(8,128)S(1)} %get-tuple-element.27.refs_0_), channel_id=1, source_target_pairs={{0,6},{2,4},{4,2},{6,0},{8,14},{10,12},{12,10},{14,8},{1,13},{3,15... | collective-permute-start | bytes 208904 | tf_op jit(solution)/shard_map/ppermute | solution.py:423
  23.5 5.4 %collective-permute-start.8 = (f32[136,128]{1,0:T(8,128)S(1)}, f32[136,128]{1,0:T(8,128)S(1)}, u32[]{:S(2)}, u32[]{:S(2)}) collective-permute-start(f32[136,128]{1,0:T(8,128)S(1)} %get-tuple-element.27.refs_0_), channel_id=1, source_target_pairs={{0,4},{2,6},{4,0},{6,2},{8,12},{10,14},{12,8},{14,10},{1,9},{3,11}... | collective-permute-start | bytes 208904 | tf_op jit(solution)/shard_map/ppermute | solution.py:423
  24.2 6.5 %collective-permute-start.9 = (f32[136,128]{1,0:T(8,128)S(1)}, f32[136,128]{1,0:T(8,128)S(1)}, u32[]{:S(2)}, u32[]{:S(2)}) collective-permute-start(f32[136,128]{1,0:T(8,128)S(1)} %get-tuple-element.27.refs_0_), channel_id=1, source_target_pairs={{0,2},{2,0},{4,6},{6,4},{8,10},{10,8},{12,14},{14,12},{1,3},{3,1},... | collective-permute-start | bytes 208904 | tf_op jit(solution)/shard_map/ppermute | solution.py:423
  26.4 4.3 %collective-permute-start.10 = (f32[136,128]{1,0:T(8,128)S(1)}, f32[136,128]{1,0:T(8,128)S(1)}, u32[]{:S(2)}, u32[]{:S(2)}) collective-permute-start(f32[136,128]{1,0:T(8,128)S(1)} %collective-permute-done.6.refs_1_), channel_id=1, source_target_pairs={{0,1},{1,0},{2,3},{3,2},{4,5},{5,4},{6,7},{7,6},{8,9},{9,8},{10,11... | collective-permute-start | bytes 208904 | tf_op jit(solution)/shard_map/ppermute | solution.py:405
  28.4 2.4 %collective-permute-start.11 = (f32[136,128]{1,0:T(8,128)S(1)}, f32[136,128]{1,0:T(8,128)S(1)}, u32[]{:S(2)}, u32[]{:S(2)}) collective-permute-start(f32[136,128]{1,0:T(8,128)S(1)} %collective-permute-done.7.refs_2_), channel_id=1, source_target_pairs={{0,1},{1,0},{2,3},{3,2},{4,5},{5,4},{6,7},{7,6},{8,9},{9,8},{10,11... | collective-permute-start | bytes 208904 | tf_op jit(solution)/shard_map/ppermute | solution.py:405
  28.9 1.8 %collective-permute-start.12 = (f32[136,128]{1,0:T(8,128)S(1)}, f32[136,128]{1,0:T(8,128)S(1)}, u32[]{:S(2)}, u32[]{:S(2)}) collective-permute-start(f32[136,128]{1,0:T(8,128)S(1)} %collective-permute-done.8.refs_3_), channel_id=1, source_target_pairs={{0,1},{1,0},{2,3},{3,2},{4,5},{5,4},{6,7},{7,6},{8,9},{9,8},{10,11... | collective-permute-start | bytes 208904 | tf_op jit(solution)/shard_map/ppermute | solution.py:405
  33.8 1.3 %collective-permute-start.14 = (f32[32,512]{1,0:T(8,128)S(1)}, f32[32,512]{1,0:T(8,128)S(1)}, u32[]{:S(2)}, u32[]{:S(2)}) collective-permute-start(f32[32,512]{1,0:T(8,128)S(1)} %get-tuple-element.32.mine_ref), channel_id=1, source_target_pairs={{0,1},{1,0},{2,3},{3,2},{4,5},{5,4},{6,7},{7,6},{8,9},{9,8},{10,11... | collective-permute-start | bytes 196616 | tf_op jit(solution)/shard_map/ppermute | solution.py:405
  35.4 7.9 %collective-permute-start.15 = (f32[136,128]{1,0:T(8,128)S(1)}, f32[136,128]{1,0:T(8,128)S(1)}, u32[]{:S(2)}, u32[]{:S(2)}) collective-permute-start(f32[136,128]{1,0:T(8,128)S(1)} %image.3.refs_0_), channel_id=1, source_target_pairs={{0,14},{2,12},{4,10},{6,8},{8,6},{10,4},{12,2},{14,0},{1,11},{3,9}... | collective-permute-start | bytes 208904 | tf_op jit(solution)/shard_map/ppermute | solution.py:423
  37.8 6.4 %collective-permute-start.16 = (f32[136,128]{1,0:T(8,128)S(1)}, f32[136,128]{1,0:T(8,128)S(1)}, u32[]{:S(2)}, u32[]{:S(2)}) collective-permute-start(f32[136,128]{1,0:T(8,128)S(1)} %image.3.refs_0_), channel_id=1, source_target_pairs={{0,6},{2,4},{4,2},{6,0},{8,14},{10,12},{12,10},{14,8},{1,13},{3,15... | collective-permute-start | bytes 208904 | tf_op jit(solution)/shard_map/ppermute | solution.py:423
  37.8 6.4 %collective-permute-start.17 = (f32[136,128]{1,0:T(8,128)S(1)}, f32[136,128]{1,0:T(8,128)S(1)}, u32[]{:S(2)}, u32[]{:S(2)}) collective-permute-start(f32[136,128]{1,0:T(8,128)S(1)} %image.3.refs_0_), channel_id=1, source_target_pairs={{0,4},{2,6},{4,0},{6,2},{8,12},{10,14},{12,8},{14,10},{1,9},{3,11}... | collective-permute-start | bytes 208904 | tf_op jit(solution)/shard_map/ppermute | solution.py:423
  40.4 5.4 %collective-permute-start.18 = (f32[136,128]{1,0:T(8,128)S(1)}, f32[136,128]{1,0:T(8,128)S(1)}, u32[]{:S(2)}, u32[]{:S(2)}) collective-permute-start(f32[136,128]{1,0:T(8,128)S(1)} %image.3.refs_0_), channel_id=1, source_target_pairs={{0,2},{2,0},{4,6},{6,4},{8,10},{10,8},{12,14},{14,12},{1,3},{3,1},... | collective-permute-start | bytes 208904 | tf_op jit(solution)/shard_map/ppermute | solution.py:423
  43.4 2.5 %collective-permute-start.19 = (f32[136,128]{1,0:T(8,128)S(1)}, f32[136,128]{1,0:T(8,128)S(1)}, u32[]{:S(2)}, u32[]{:S(2)}) collective-permute-start(f32[136,128]{1,0:T(8,128)S(1)} %collective-permute-done.15.refs_1_), channel_id=1, source_target_pairs={{0,1},{1,0},{2,3},{3,2},{4,5},{5,4},{6,7},{7,6},{8,9},{9,8},{10,11... | collective-permute-start | bytes 208904 | tf_op jit(solution)/shard_map/ppermute | solution.py:405
  44.2 1.7 %collective-permute-start.20 = (f32[136,128]{1,0:T(8,128)S(1)}, f32[136,128]{1,0:T(8,128)S(1)}, u32[]{:S(2)}, u32[]{:S(2)}) collective-permute-start(f32[136,128]{1,0:T(8,128)S(1)} %collective-permute-done.16.refs_2_), channel_id=1, source_target_pairs={{0,1},{1,0},{2,3},{3,2},{4,5},{5,4},{6,7},{7,6},{8,9},{9,8},{10,11... | collective-permute-start | bytes 208904 | tf_op jit(solution)/shard_map/ppermute | solution.py:405
  44.2 1.7 %collective-permute-start.21 = (f32[136,128]{1,0:T(8,128)S(1)}, f32[136,128]{1,0:T(8,128)S(1)}, u32[]{:S(2)}, u32[]{:S(2)}) collective-permute-start(f32[136,128]{1,0:T(8,128)S(1)} %collective-permute-done.17.refs_3_), channel_id=1, source_target_pairs={{0,1},{1,0},{2,3},{3,2},{4,5},{5,4},{6,7},{7,6},{8,9},{9,8},{10,11... | collective-permute-start | bytes 208904 | tf_op jit(solution)/shard_map/ppermute | solution.py:405
  48.9 1.3 %collective-permute-start.22 = (f32[32,512]{1,0:T(8,128)S(1)}, f32[32,512]{1,0:T(8,128)S(1)}, u32[]{:S(2)}, u32[]{:S(2)}) collective-permute-start(f32[32,512]{1,0:T(8,128)S(1)} %get-tuple-element.37.mine_ref), channel_id=1, source_target_pairs={{0,1},{1,0},{2,3},{3,2},{4,5},{5,4},{6,7},{7,6},{8,9},{9,8},{10,11... | collective-permute-start | bytes 196616 | tf_op jit(solution)/shard_map/ppermute | solution.py:405
  50.5 6.3 %collective-permute-start.23 = (f32[8,128]{1,0:T(8,128)S(1)}, f32[8,128]{1,0:T(8,128)S(1)}, u32[]{:S(2)}, u32[]{:S(2)}) collective-permute-start(f32[8,128]{1,0:T(8,128)S(1)} %get-tuple-element.39.refs_0_), channel_id=1, source_target_pairs={{0,14},{2,12},{4,10},{6,8},{8,6},{10,4},{12,2},{14,0},{1,11},{3,9}... | collective-permute-start | bytes 12296 | tf_op jit(solution)/shard_map/ppermute | solution.py:423
  53.1 4.5 %collective-permute-start.24 = (f32[8,128]{1,0:T(8,128)S(1)}, f32[8,128]{1,0:T(8,128)S(1)}, u32[]{:S(2)}, u32[]{:S(2)}) collective-permute-start(f32[8,128]{1,0:T(8,128)S(1)} %get-tuple-element.39.refs_0_), channel_id=1, source_target_pairs={{0,6},{2,4},{4,2},{6,0},{8,14},{10,12},{12,10},{14,8},{1,13},{3,15... | collective-permute-start | bytes 12296 | tf_op jit(solution)/shard_map/ppermute | solution.py:423
  53.3 4.4 %collective-permute-start.25 = (f32[8,128]{1,0:T(8,128)S(1)}, f32[8,128]{1,0:T(8,128)S(1)}, u32[]{:S(2)}, u32[]{:S(2)}) collective-permute-start(f32[8,128]{1,0:T(8,128)S(1)} %get-tuple-element.39.refs_0_), channel_id=1, source_target_pairs={{0,4},{2,6},{4,0},{6,2},{8,12},{10,14},{12,8},{14,10},{1,9},{3,11}... | collective-permute-start | bytes 12296 | tf_op jit(solution)/shard_map/ppermute | solution.py:423
  55.9 3.6 %collective-permute-start.26 = (f32[8,128]{1,0:T(8,128)S(1)}, f32[8,128]{1,0:T(8,128)S(1)}, u32[]{:S(2)}, u32[]{:S(2)}) collective-permute-start(f32[8,128]{1,0:T(8,128)S(1)} %get-tuple-element.39.refs_0_), channel_id=1, source_target_pairs={{0,2},{2,0},{4,6},{6,4},{8,10},{10,8},{12,14},{14,12},{1,3},{3,1},... | collective-permute-start | bytes 12296 | tf_op jit(solution)/shard_map/ppermute | solution.py:423
  56.8 2.7 %collective-permute-start.27 = (f32[8,128]{1,0:T(8,128)S(1)}, f32[8,128]{1,0:T(8,128)S(1)}, u32[]{:S(2)}, u32[]{:S(2)}) collective-permute-start(f32[8,128]{1,0:T(8,128)S(1)} %collective-permute-done.23.refs_1_), channel_id=1, source_target_pairs={{0,1},{1,0},{2,3},{3,2},{4,5},{5,4},{6,7},{7,6},{8,9},{9,8},{10,11... | collective-permute-start | bytes 12296 | tf_op jit(solution)/shard_map/ppermute | solution.py:405
  57.7 1.9 %collective-permute-start.28 = (f32[8,128]{1,0:T(8,128)S(1)}, f32[8,128]{1,0:T(8,128)S(1)}, u32[]{:S(2)}, u32[]{:S(2)}) collective-permute-start(f32[8,128]{1,0:T(8,128)S(1)} %collective-permute-done.24.refs_2_), channel_id=1, source_target_pairs={{0,1},{1,0},{2,3},{3,2},{4,5},{5,4},{6,7},{7,6},{8,9},{9,8},{10,11... | collective-permute-start | bytes 12296 | tf_op jit(solution)/shard_map/ppermute | solution.py:405
  57.7 1.9 %collective-permute-start.29 = (f32[8,128]{1,0:T(8,128)S(1)}, f32[8,128]{1,0:T(8,128)S(1)}, u32[]{:S(2)}, u32[]{:S(2)}) collective-permute-start(f32[8,128]{1,0:T(8,128)S(1)} %collective-permute-done.25.refs_3_), channel_id=1, source_target_pairs={{0,1},{1,0},{2,3},{3,2},{4,5},{5,4},{6,7},{7,6},{8,9},{9,8},{10,11... | collective-permute-start | bytes 12296 | tf_op jit(solution)/shard_map/ppermute | solution.py:405

commit v15 on v12

--- a/solution.py
+++ b/solution.py
@@ -188,11 +188,21 @@
         def _():
             copies[c].start()
 
-    last = pltpu.make_async_copy(tiles_ref.at[pl.ds(half, slots - half)], rest, sems.at[CHUNKS])
-
-    @pl.when(half < live)
-    def _():
-        last.start()
+    chunk_rest = -(-rest.shape[0] // CHUNKS)
+    rest_copies = []
+    for c in range(CHUNKS):
+        start = c * chunk_rest
+        length = min(chunk_rest, rest.shape[0] - start)
+        copy = pltpu.make_async_copy(
+            tiles_ref.at[pl.ds(half + start, length)],
+            rest.at[pl.ds(start, length)],
+            sems.at[CHUNKS + c],
+        )
+        rest_copies.append((half + start, copy))
+
+        @pl.when(half + start < live)
+        def _():
+            copy.start()
 
     def clear(index, carry):
         total[index] = jnp.zeros((tile, tile), F32)
@@ -211,9 +221,11 @@
                 rows_dev, (rows_ref, cols_ref), held, 0, start, jnp.minimum(live, stop), total
             )
 
-    @pl.when(half < live)
-    def _():
-        last.wait()
+    for start, copy in rest_copies:
+
+        @pl.when(start < live)
+        def _():
+            copy.wait()
 
 
 def dense_kernel(
@@ -410,7 +422,6 @@
         if pieces != 8:
             found = [value] + [swap(value, k) for k in range(1, pieces)]
             return found, [(k, k) for k in range(pieces)]
-        turns = ((2, 4), (7, 6), (1, 2))
 
         def fetch(source, masks):
             pairs = [
@@ -420,11 +431,10 @@
             ]
             return lax.ppermute(source, ("row", "col"), pairs)
 
-        fetched = [fetch(value, masks) for masks in turns]
-        fetched.append(fetch(fetched[0], (1, 1)))
+        fetched = [fetch(value, masks) for masks in ((1, 4), (3, 6), (2, 1))]
+        fetched.append(fetch(fetched[0], (6, 1)))
         found = [value, *fetched, *map(across, fetched)]
-        places = [(0, 0), (3, 7), (1, 5), (4, 8), (5, 1), (8, 4), (6, 2), (2, 6)]
-        return found, places
+        return found, [(0, 0), (1, 3), (3, 7), (2, 6), (5, 1), (8, 4), (6, 2), (4, 8)]
 
     right_side = signs.astype(F32) * vertex_weight[None, :] * column_scale[:, None]
     far_side = across(right_side)[None]
@@ -433,7 +443,7 @@
     matrix = shape(2, depth, group, dtype=BF16)
     total = shape(depth // tile * (group // tile), tile, tile)
     slots = tiles.shape[0]
-    half = slots // 2
+    half = slots * 3 // 8
     rest = shape(slots - half, tile, tile, dtype=BF16)
     lists = [pltpu.with_memory_space_constraint(x, pltpu.HBM) for x in (tile_rows, tile_cols)]
     lists_scratch = [pltpu.SMEM(x.shape, jnp.int32) for x in lists]
@@ -448,7 +458,7 @@
         scratch_shapes=[
             pltpu.VMEM((half, tile, tile), BF16),
             *lists_scratch,
-            pltpu.SemaphoreType.DMA((CHUNKS + 1,)),
+            pltpu.SemaphoreType.DMA((2 * CHUNKS,)),
             pltpu.SemaphoreType.DMA((len(lists),)),
         ],
         compiler_params=params(tiles, total),

time: 62 us -> 64.1 us (1.034)
  starting transfers between devices: 25.5 us -> 26.6 us
  Pallas kernels: 16.1 us -> 17 us
  waiting for transfers between devices: 17.3 us -> 18 us
    ppermute x12, waiting for transfers between devices: 10.1 us -> 11.7 us  [fetch(): return lax.ppermute(source, ('row', 'col'), pairs)]
    pallas_call x1, Pallas kernels: 2.23 us -> 3.27 us  [per_device(): pl.pallas_call(functools.partial(dense_kernel, rows_dev), out_shape=(matr...]
    ppermute x4, waiting for transfers between devices: 2.41 us -> 1.52 us  [swap(): return lax.ppermute(value, 'row', [(i, i ^ mask) for i in range(pieces)])]
    ppermute x12, starting transfers between devices: 15.7 us -> 16.6 us  [fetch(): return lax.ppermute(source, ('row', 'col'), pairs)]
  transfers between devices with their start and end apart: 33 -> 33, of which waited for: 19 -> 18; matrix products, arithmetic and copies ran while one was open for 0% -> 0% of each run, Pallas kernels for 11% -> 12%
where the time goes in v15:
time: 64.1 us; the launch traced here: 63.9 us
  starting transfers between devices  26.6 us (41%)
  waiting for transfers between devices  18 us (28%)
  Pallas kernels  17 us (27%)
  between operations  1.44 us (2%)
  other arithmetic  0.85 us (1%)
    ppermute x12, starting transfers between devices, fetch(): return lax.ppermute(source, ('row', 'col'), pairs)  16.6 us
    ppermute x12, waiting for transfers between devices, fetch(): return lax.ppermute(source, ('row', 'col'), pairs)  11.7 us
    ppermute x4, starting transfers between devices, swap(): return lax.ppermute(value, 'row', [(i, i ^ mask) for i in range(pieces)])  7.2 us
    pallas_call x2, Pallas kernels, per_device(): pl.pallas_call(functools.partial(step_kernel, len(found), places, not fir...  6.12 us
    ppermute x17, waiting for transfers between devices, across(): lax.ppermute(value, 'col', [(i, (i + 1) % col_devices) for i in range(col...  4.79 us
    pallas_call x1, Pallas kernels, per_device(): pl.pallas_call(functools.partial(dense_kernel, rows_dev), out_shape=(matr...  3.27 us
    ppermute x17, starting transfers between devices, across(): lax.ppermute(value, 'col', [(i, (i + 1) % col_devices) for i in range(col...  2.82 us
    pallas_call x1, Pallas kernels, per_device(): pl.pallas_call(functools.partial(gather_kernel, rows_dev), out_shape=(tot...  2.12 us
  transfers between devices with their start and end apart: 33, of which 18 were waited for; matrix products, arithmetic and copies ran while one was open for 0% of the time, Pallas kernels for 12%

profile of v15, /device:TPU:0, one launch (start us, length us, event | category | flops | bytes accessed | tf_op | source)
XLA Modules:
  0.0 63.9 jit_solution(13469594076513877541)
XLA Ops:
  0.6 0.8 %multiply_multiply_fusion.refs_3_ = f32[32,256]{1,0:T(8,128)S(1)} fusion(s32[32,256]{1,0:T(8,128)} %param.11, f32[32]{0:T(128)} %param.13, f32[256]{0:T(256)} %param.12), kind=kLoop, calls=%fused_computation | loop fusion | flops 24576 | bytes 66688 | tf_op jit(solution)/shard_map/mul | solution.py:439
  1.5 4.0 %collective-permute-start = (f32[32,256]{1,0:T(8,128)S(1)}, f32[32,256]{1,0:T(8,128)S(1)}, u32[]{:S(2)}, u32[]{:S(2)}) collective-permute-start(f32[32,256]{1,0:T(8,128)S(1)} %multiply_multiply_fusion.refs_3_), channel_id=1, source_target_pairs={{0,8},{2,10},{4,12},{6,14},{8,0},{10,2},{12,4},{14,6},{1,9},{3,11}... | collective-permute-start | bytes 98312 | tf_op jit(solution)/shard_map/ppermute | solution.py:414
  5.5 1.3 %collective-permute-start.1 = (f32[32,256]{1,0:T(8,128)S(1)}, f32[32,256]{1,0:T(8,128)S(1)}, u32[]{:S(2)}, u32[]{:S(2)}) collective-permute-start(f32[32,256]{1,0:T(8,128)S(1)} %multiply_multiply_fusion.refs_3_), channel_id=1, source_target_pairs={{0,12},{2,14},{4,8},{6,10},{8,4},{10,6},{12,0},{14,2},{1,13},{3,15... | collective-permute-start | bytes 98312 | tf_op jit(solution)/shard_map/ppermute | solution.py:414
  6.9 0.2 collective-permute-start.2
  7.8 2.1 %gather.1 = (f32[64,128,128]{2,1,0:T(8,128)S(1)}, bf16[82,128,128]{2,1,0:T(8,128)(2,1)S(1)}) custom-call(s32[1]{0:T(128)S(6)} %copy.11.count_ref, s32[130]{0:T(256)} %rows_hbm.3, s32[130]{0:T(256)} %cols_hbm.3, bf16[130,128,128]{2,1,0:T(8,128)(2,1)} %tiles_ref.1), custom_call_target="tpu_custom_call" | custom-call | flops 8519680 | bytes 8519680 | tf_op jit(solution)/shard_map/gather/pallas_call | solution.py:453
  9.9 0.0 collective-permute-done.refs_0_
  9.9 1.3 %collective-permute-done.1.refs_1_ = f32[32,256]{1,0:T(8,128)S(1)} collective-permute-done((f32[32,256]{1,0:T(8,128)S(1)}, f32[32,256]{1,0:T(8,128)S(1)}, u32[]{:S(2)}, u32[]{:S(2)}) %collective-permute-start.1) | collective-permute-done | bytes 32800 | tf_op jit(solution)/shard_map/ppermute | solution.py:414
  11.2 0.0 collective-permute-done.2.refs_2_
  11.2 1.6 %collective-permute-start.3 = (f32[4,32,256]{2,1,0:T(8,128)S(1)}, f32[4,32,256]{2,1,0:T(8,128)S(1)}, u32[]{:S(2)}, u32[]{:S(2)}) collective-permute-start(f32[4,32,256]{2,1,0:T(8,128)S(1)} %join.1.joined_ref.even_ref.near_ref), channel_id=1, source_target_pairs={{0,2},{2,0},{4,6},{6,4},{8,10},{10,8},{12,14},{14,12},{1,3},{3,1},... | collective-permute-start | bytes 393224 | tf_op jit(solution)/shard_map/ppermute | solution.py:414
  12.8 3.3 %dense.1 = (bf16[2,2048,512]{2,1,0:T(8,128)(2,1)S(1)}, f32[64,128,128]{2,1,0:T(8,128)S(1)}) custom-call(s32[1]{0:T(128)S(6)} %copy.11.count_ref, s32[130]{0:T(256)} %rows_hbm.3, s32[130]{0:T(256)} %cols_hbm.3, bf16[82,128,128]{2,1,0:T(8,128)(2,1)S(1)} %get-tuple-element.24.rest, ...), custom_call_target="tpu_custom_call", output_to_operand_aliasing={{1}: (4, {})} | custom-call | flops 8519680 | bytes 8519680 | tf_op jit(solution)/shard_map/dense/pallas_call | solution.py:479
  16.1 0.2 collective-permute-done.3.odd_ref
  16.3 0.9 %first.1 = (f32[32,640]{1,0:T(8,128)S(1)}, f32[8,32,256]{2,1,0:T(8,128)S(1)}) custom-call(f32[4,32,256]{2,1,0:T(8,128)S(1)} %join.1.joined_ref.even_ref.near_ref, f32[4,32,256]{2,1,0:T(8,128)S(1)} %collective-permute-done.3.odd_ref, bf16[2,2048,512]{2,1,0:T(8,128)(2,1)S(1)} %get-tuple-element.25.matrix.refs_13_), custom_call_target="tpu_custom_call" | custom-call | tf_op jit(solution)/shard_map/first/pallas_call | solution.py:498
  17.2 0.0 collective-permute-start.4
  17.2 0.5 collective-permute-start.14
  17.7 0.1 collective-permute-start.5
  17.8 1.1 %collective-permute-done.5 = f32[32,256]{1,0:T(8,128)S(1)} collective-permute-done((f32[32,256]{1,0:T(8,128)S(1)}, f32[32,256]{1,0:T(8,128)S(1)}, u32[]{:S(2)}, u32[]{:S(2)}) %collective-permute-start.5) | collective-permute-done | bytes 32800 | tf_op jit(solution)/shard_map/ppermute | solution.py:417
  18.9 0.3 image.2
  19.3 1.5 %collective-permute-start.6 = (f32[136,128]{1,0:T(8,128)S(1)}, f32[136,128]{1,0:T(8,128)S(1)}, u32[]{:S(2)}, u32[]{:S(2)}) collective-permute-start(f32[136,128]{1,0:T(8,128)S(1)} %get-tuple-element.27.refs_0_), channel_id=1, source_target_pairs={{0,2},{2,0},{4,6},{6,4},{8,10},{10,8},{12,14},{14,12},{1,9},{3,11}... | collective-permute-start | bytes 208904 | tf_op jit(solution)/shard_map/ppermute | solution.py:432
  20.8 0.4 collective-permute-start.7
  21.2 1.6 %collective-permute-start.8 = (f32[136,128]{1,0:T(8,128)S(1)}, f32[136,128]{1,0:T(8,128)S(1)}, u32[]{:S(2)}, u32[]{:S(2)}) collective-permute-start(f32[136,128]{1,0:T(8,128)S(1)} %get-tuple-element.27.refs_0_), channel_id=1, source_target_pairs={{0,4},{2,6},{4,0},{6,2},{8,12},{10,14},{12,8},{14,10},{1,3},{3,1},... | collective-permute-start | bytes 208904 | tf_op jit(solution)/shard_map/ppermute | solution.py:432
  22.8 0.8 %collective-permute-done.6.refs_1_ = f32[136,128]{1,0:T(8,128)S(1)} collective-permute-done((f32[136,128]{1,0:T(8,128)S(1)}, f32[136,128]{1,0:T(8,128)S(1)}, u32[]{:S(2)}, u32[]{:S(2)}) %collective-permute-start.6) | collective-permute-done | bytes 69664 | tf_op jit(solution)/shard_map/ppermute | solution.py:432
  23.6 2.0 %collective-permute-start.9 = (f32[136,128]{1,0:T(8,128)S(1)}, f32[136,128]{1,0:T(8,128)S(1)}, u32[]{:S(2)}, u32[]{:S(2)}) collective-permute-start(f32[136,128]{1,0:T(8,128)S(1)} %collective-permute-done.6.refs_1_), channel_id=1, source_target_pairs={{0,12},{2,14},{4,8},{6,10},{8,4},{10,6},{12,0},{14,2},{1,3},{3,1},... | collective-permute-start | bytes 208904 | tf_op jit(solution)/shard_map/ppermute | solution.py:432
  25.6 0.3 collective-permute-start.10
  25.9 0.4 collective-permute-done.7.refs_2_
  26.3 0.3 collective-permute-start.11
  26.6 0.2 collective-permute-done.8.refs_3_
  26.8 0.0 collective-permute-start.12
  26.8 2.9 %collective-permute-done.9.refs_4_ = f32[136,128]{1,0:T(8,128)S(1)} collective-permute-done((f32[136,128]{1,0:T(8,128)S(1)}, f32[136,128]{1,0:T(8,128)S(1)}, u32[]{:S(2)}, u32[]{:S(2)}) %collective-permute-start.9) | collective-permute-done | bytes 69664 | tf_op jit(solution)/shard_map/ppermute | solution.py:432
  29.7 0.0 collective-permute-start.13
  29.7 0.9 %inverse.2.refs_12_ = f32[32,128]{1,0:T(8,128)S(1)} custom-call(f32[32,128]{1,0:T(8,128)S(1)} %get-tuple-element.31.norm_ref.refs_11_), custom_call_target="tpu_custom_call" | custom-call | tf_op jit(solution)/shard_map/inverse/pallas_call | solution.py:533
  30.7 0.0 collective-permute-done.14.far_ref
  30.7 0.1 collect.1
  30.7 0.0 collective-permute-done.10.refs_5_
  30.8 0.2 collective-permute-done.13.refs_8_
  31.0 3.1 %step.2 = (f32[32,512]{1,0:T(8,128)S(1)}, f32[9,32,256]{2,1,0:T(8,128)S(1)}, f32[2,8,32,256]{3,2,1,0:T(8,128)S(1)}, f32[32,128]{1,0:T(8,128)S(1)}, f32[32,256]{1,0:T(8,128)S(1)}) custom-call(f32[136,128]{1,0:T(8,128)S(1)} %get-tuple-element.27.refs_0_, f32[136,128]{1,0:T(8,128)S(1)} %collective-permute-done.6.refs_1_, ...), custom_call_target="tpu_custom_call" | custom-call | tf_op jit(solution)/shard_map/step/pallas_call | solution.py:542
  34.0 0.3 collective-permute-start.15
  34.4 0.9 %collective-permute-done.15.other_ref = f32[32,512]{1,0:T(8,128)S(1)} collective-permute-done((f32[32,512]{1,0:T(8,128)S(1)}, f32[32,512]{1,0:T(8,128)S(1)}, u32[]{:S(2)}, u32[]{:S(2)}) %collective-permute-start.15) | collective-permute-done | bytes 65568 | tf_op jit(solution)/shard_map/ppermute | solution.py:417
  35.3 0.3 image.3.refs_0_
  35.7 1.5 %collective-permute-start.16 = (f32[136,128]{1,0:T(8,128)S(1)}, f32[136,128]{1,0:T(8,128)S(1)}, u32[]{:S(2)}, u32[]{:S(2)}) collective-permute-start(f32[136,128]{1,0:T(8,128)S(1)} %image.3.refs_0_), channel_id=1, source_target_pairs={{0,2},{2,0},{4,6},{6,4},{8,10},{10,8},{12,14},{14,12},{1,9},{3,11}... | collective-permute-start | bytes 208904 | tf_op jit(solution)/shard_map/ppermute | solution.py:432
  37.2 0.0 collective-permute-start.17
  37.2 2.0 %collective-permute-start.18 = (f32[136,128]{1,0:T(8,128)S(1)}, f32[136,128]{1,0:T(8,128)S(1)}, u32[]{:S(2)}, u32[]{:S(2)}) collective-permute-start(f32[136,128]{1,0:T(8,128)S(1)} %image.3.refs_0_), channel_id=1, source_target_pairs={{0,4},{2,6},{4,0},{6,2},{8,12},{10,14},{12,8},{14,10},{1,3},{3,1},... | collective-permute-start | bytes 208904 | tf_op jit(solution)/shard_map/ppermute | solution.py:432
  39.2 0.8 %collective-permute-done.16.refs_1_ = f32[136,128]{1,0:T(8,128)S(1)} collective-permute-done((f32[136,128]{1,0:T(8,128)S(1)}, f32[136,128]{1,0:T(8,128)S(1)}, u32[]{:S(2)}, u32[]{:S(2)}) %collective-permute-start.16) | collective-permute-done | bytes 69664 | tf_op jit(solution)/shard_map/ppermute | solution.py:432
  40.0 2.0 %collective-permute-start.19 = (f32[136,128]{1,0:T(8,128)S(1)}, f32[136,128]{1,0:T(8,128)S(1)}, u32[]{:S(2)}, u32[]{:S(2)}) collective-permute-start(f32[136,128]{1,0:T(8,128)S(1)} %collective-permute-done.16.refs_1_), channel_id=1, source_target_pairs={{0,12},{2,14},{4,8},{6,10},{8,4},{10,6},{12,0},{14,2},{1,3},{3,1},... | collective-permute-start | bytes 208904 | tf_op jit(solution)/shard_map/ppermute | solution.py:432
  42.0 1.0 %collective-permute-done.17.refs_2_ = f32[136,128]{1,0:T(8,128)S(1)} collective-permute-done((f32[136,128]{1,0:T(8,128)S(1)}, f32[136,128]{1,0:T(8,128)S(1)}, u32[]{:S(2)}, u32[]{:S(2)}) %collective-permute-start.17) | collective-permute-done | bytes 69664 | tf_op jit(solution)/shard_map/ppermute | solution.py:432
  43.0 0.0 collective-permute-start.21
  43.0 0.0 collective-permute-done.18.refs_3_
  43.0 0.5 collective-permute-start.22
  43.5 2.5 %collective-permute-done.19.refs_4_ = f32[136,128]{1,0:T(8,128)S(1)} collective-permute-done((f32[136,128]{1,0:T(8,128)S(1)}, f32[136,128]{1,0:T(8,128)S(1)}, u32[]{:S(2)}, u32[]{:S(2)}) %collective-permute-start.19) | collective-permute-done | bytes 69664 | tf_op jit(solution)/shard_map/ppermute | solution.py:432
  46.1 0.9 %inverse.3.refs_12_ = f32[32,128]{1,0:T(8,128)S(1)} custom-call(f32[32,128]{1,0:T(8,128)S(1)} %get-tuple-element.35.norm_ref.refs_11_), custom_call_target="tpu_custom_call" | custom-call | tf_op jit(solution)/shard_map/inverse/pallas_call | solution.py:533
  47.1 0.3 collective-permute-done.23.refs_8_
  47.4 3.1 %step.3 = (f32[32,512]{1,0:T(8,128)S(1)}, f32[2,32,256]{2,1,0:T(8,128)S(1)}, f32[32,256]{1,0:T(8,128)S(1)}, f32[32,128]{1,0:T(8,128)S(1)}, f32[32,256]{1,0:T(8,128)S(1)}) custom-call(f32[136,128]{1,0:T(8,128)S(1)} %image.3.refs_0_, f32[136,128]{1,0:T(8,128)S(1)} %collective-permute-done.16.refs_1_, f32[136,128]{1,0:T(8,128)S(1)} %collective-permute-done.17.refs_2_, ...), custom_call_target="tpu_custom_call" | custom-call | tf_op jit(solution)/shard_map/step/pallas_call | solution.py:542
  50.4 0.2 collective-permute-start.24
  50.7 1.0 %collective-permute-done.24.other_ref = f32[32,512]{1,0:T(8,128)S(1)} collective-permute-done((f32[32,512]{1,0:T(8,128)S(1)}, f32[32,512]{1,0:T(8,128)S(1)}, u32[]{:S(2)}, u32[]{:S(2)}) %collective-permute-start.24) | collective-permute-done | bytes 65568 | tf_op jit(solution)/shard_map/ppermute | solution.py:417
  51.7 0.3 last_image.1
  52.0 1.5 %collective-permute-start.25 = (f32[8,128]{1,0:T(8,128)S(1)}, f32[8,128]{1,0:T(8,128)S(1)}, u32[]{:S(2)}, u32[]{:S(2)}) collective-permute-start(f32[8,128]{1,0:T(8,128)S(1)} %get-tuple-element.39.refs_0_), channel_id=1, source_target_pairs={{0,2},{2,0},{4,6},{6,4},{8,10},{10,8},{12,14},{14,12},{1,9},{3,11}... | collective-permute-start | bytes 12296 | tf_op jit(solution)/shard_map/ppermute | solution.py:432
  53.6 2.0 %collective-permute-start.27 = (f32[8,128]{1,0:T(8,128)S(1)}, f32[8,128]{1,0:T(8,128)S(1)}, u32[]{:S(2)}, u32[]{:S(2)}) collective-permute-start(f32[8,128]{1,0:T(8,128)S(1)} %get-tuple-element.39.refs_0_), channel_id=1, source_target_pairs={{0,4},{2,6},{4,0},{6,2},{8,12},{10,14},{12,8},{14,10},{1,3},{3,1},... | collective-permute-start | bytes 12296 | tf_op jit(solution)/shard_map/ppermute | solution.py:432
  55.5 0.1 collective-permute-done.25.refs_1_
  55.6 2.0 %collective-permute-start.28 = (f32[8,128]{1,0:T(8,128)S(1)}, f32[8,128]{1,0:T(8,128)S(1)}, u32[]{:S(2)}, u32[]{:S(2)}) collective-permute-start(f32[8,128]{1,0:T(8,128)S(1)} %collective-permute-done.25.refs_1_), channel_id=1, source_target_pairs={{0,12},{2,14},{4,8},{6,10},{8,4},{10,6},{12,0},{14,2},{1,3},{3,1},... | collective-permute-start | bytes 12296 | tf_op jit(solution)/shard_map/ppermute | solution.py:432
  57.7 0.4 collective-permute-done.26.refs_2_
  58.1 0.1 collective-permute-start.30
  58.2 0.4 collective-permute-start.31
  58.6 2.5 %collective-permute-done.28.refs_4_ = f32[8,128]{1,0:T(8,128)S(1)} collective-permute-done((f32[8,128]{1,0:T(8,128)S(1)}, f32[8,128]{1,0:T(8,128)S(1)}, u32[]{:S(2)}, u32[]{:S(2)}) %collective-permute-start.28) | collective-permute-done | bytes 4128 | tf_op jit(solution)/shard_map/ppermute | solution.py:432
  61.1 1.1 %collective-permute-done.32.refs_8_ = f32[8,128]{1,0:T(8,128)S(1)} collective-permute-done((f32[8,128]{1,0:T(8,128)S(1)}, f32[8,128]{1,0:T(8,128)S(1)}, u32[]{:S(2)}, u32[]{:S(2)}) %collective-permute-start.32) | collective-permute-done | bytes 4128 | tf_op jit(solution)/shard_map/ppermute | solution.py:417
  62.2 1.7 %last.1 = (f32[32,256]{1,0:T(8,128)}, f32[32,256]{1,0:T(8,128)}) custom-call(f32[8,128]{1,0:T(8,128)S(1)} %get-tuple-element.39.refs_0_, f32[8,128]{1,0:T(8,128)S(1)} %collective-permute-done.25.refs_1_, f32[8,128]{1,0:T(8,128)S(1)} %collective-permute-done.26.refs_2_, f32[8,128]{1,0:T(8,128)S(1)} %collective-permute-done.27.refs_3_, ...), custom_call_target="tpu_custom_call" | custom-call | tf_op jit(solution)/shard_map/last/pallas_call | solution.py:565
  (16 shorter events, 0.0 us)
Async XLA Ops:
  1.5 8.4 %collective-permute-start = (f32[32,256]{1,0:T(8,128)S(1)}, f32[32,256]{1,0:T(8,128)S(1)}, u32[]{:S(2)}, u32[]{:S(2)}) collective-permute-start(f32[32,256]{1,0:T(8,128)S(1)} %multiply_multiply_fusion.refs_3_), channel_id=1, source_target_pairs={{0,8},{2,10},{4,12},{6,14},{8,0},{10,2},{12,4},{14,6},{1,9},{3,11}... | collective-permute-start | bytes 98312 | tf_op jit(solution)/shard_map/ppermute | solution.py:414
  5.5 5.7 %collective-permute-start.1 = (f32[32,256]{1,0:T(8,128)S(1)}, f32[32,256]{1,0:T(8,128)S(1)}, u32[]{:S(2)}, u32[]{:S(2)}) collective-permute-start(f32[32,256]{1,0:T(8,128)S(1)} %multiply_multiply_fusion.refs_3_), channel_id=1, source_target_pairs={{0,12},{2,14},{4,8},{6,10},{8,4},{10,6},{12,0},{14,2},{1,13},{3,15... | collective-permute-start | bytes 98312 | tf_op jit(solution)/shard_map/ppermute | solution.py:414
  6.9 4.4 %collective-permute-start.2 = (f32[32,256]{1,0:T(8,128)S(1)}, f32[32,256]{1,0:T(8,128)S(1)}, u32[]{:S(2)}, u32[]{:S(2)}) collective-permute-start(f32[32,256]{1,0:T(8,128)S(1)} %multiply_multiply_fusion.refs_3_), channel_id=1, source_target_pairs={{0,4},{2,6},{4,0},{6,2},{8,12},{10,14},{12,8},{14,10},{1,5},{3,7},... | collective-permute-start | bytes 98312 | tf_op jit(solution)/shard_map/ppermute | solution.py:414
  11.2 5.0 %collective-permute-start.3 = (f32[4,32,256]{2,1,0:T(8,128)S(1)}, f32[4,32,256]{2,1,0:T(8,128)S(1)}, u32[]{:S(2)}, u32[]{:S(2)}) collective-permute-start(f32[4,32,256]{2,1,0:T(8,128)S(1)} %join.1.joined_ref.even_ref.near_ref), channel_id=1, source_target_pairs={{0,2},{2,0},{4,6},{6,4},{8,10},{10,8},{12,14},{14,12},{1,3},{3,1},... | collective-permute-start | bytes 393224 | tf_op jit(solution)/shard_map/ppermute | solution.py:414
  17.2 1.8 %collective-permute-start.4 = (f32[32,640]{1,0:T(8,128)S(1)}, f32[32,640]{1,0:T(8,128)S(1)}, u32[]{:S(2)}, u32[]{:S(2)}) collective-permute-start(f32[32,640]{1,0:T(8,128)S(1)} %get-tuple-element.26.mine_ref), channel_id=1, source_target_pairs={{0,1},{1,0},{2,3},{3,2},{4,5},{5,4},{6,7},{7,6},{8,9},{9,8},{10,11... | collective-permute-start | bytes 245768 | tf_op jit(solution)/shard_map/ppermute | solution.py:417
  17.2 13.4 %collective-permute-start.14 = (f32[8,32,256]{2,1,0:T(8,128)S(1)}, f32[8,32,256]{2,1,0:T(8,128)S(1)}, u32[]{:S(2)}, u32[]{:S(2)}) collective-permute-start(f32[8,32,256]{2,1,0:T(8,128)S(1)} %get-tuple-element.28.near_ref), channel_id=1, source_target_pairs={{0,1},{1,0},{2,3},{3,2},{4,5},{5,4},{6,7},{7,6},{8,9},{9,8},{10,11... | collective-permute-start | bytes 786440 | tf_op jit(solution)/shard_map/ppermute | solution.py:417
  17.7 1.2 %collective-permute-start.5 = (f32[32,256]{1,0:T(8,128)S(1)}, f32[32,256]{1,0:T(8,128)S(1)}, u32[]{:S(2)}, u32[]{:S(2)}) collective-permute-start(f32[32,256]{1,0:T(8,128)S(1)} %multiply_multiply_fusion.refs_3_), channel_id=1, source_target_pairs={{0,1},{1,0},{2,3},{3,2},{4,5},{5,4},{6,7},{7,6},{8,9},{9,8},{10,11... | collective-permute-start | bytes 98312 | tf_op jit(solution)/shard_map/ppermute | solution.py:417
  19.3 4.3 %collective-permute-start.6 = (f32[136,128]{1,0:T(8,128)S(1)}, f32[136,128]{1,0:T(8,128)S(1)}, u32[]{:S(2)}, u32[]{:S(2)}) collective-permute-start(f32[136,128]{1,0:T(8,128)S(1)} %get-tuple-element.27.refs_0_), channel_id=1, source_target_pairs={{0,2},{2,0},{4,6},{6,4},{8,10},{10,8},{12,14},{14,12},{1,9},{3,11}... | collective-permute-start | bytes 208904 | tf_op jit(solution)/shard_map/ppermute | solution.py:432
  20.8 5.5 %collective-permute-start.7 = (f32[136,128]{1,0:T(8,128)S(1)}, f32[136,128]{1,0:T(8,128)S(1)}, u32[]{:S(2)}, u32[]{:S(2)}) collective-permute-start(f32[136,128]{1,0:T(8,128)S(1)} %get-tuple-element.27.refs_0_), channel_id=1, source_target_pairs={{0,6},{2,4},{4,2},{6,0},{8,14},{10,12},{12,10},{14,8},{1,13},{3,15... | collective-permute-start | bytes 208904 | tf_op jit(solution)/shard_map/ppermute | solution.py:432
  21.2 5.6 %collective-permute-start.8 = (f32[136,128]{1,0:T(8,128)S(1)}, f32[136,128]{1,0:T(8,128)S(1)}, u32[]{:S(2)}, u32[]{:S(2)}) collective-permute-start(f32[136,128]{1,0:T(8,128)S(1)} %get-tuple-element.27.refs_0_), channel_id=1, source_target_pairs={{0,4},{2,6},{4,0},{6,2},{8,12},{10,14},{12,8},{14,10},{1,3},{3,1},... | collective-permute-start | bytes 208904 | tf_op jit(solution)/shard_map/ppermute | solution.py:432
  23.6 6.1 %collective-permute-start.9 = (f32[136,128]{1,0:T(8,128)S(1)}, f32[136,128]{1,0:T(8,128)S(1)}, u32[]{:S(2)}, u32[]{:S(2)}) collective-permute-start(f32[136,128]{1,0:T(8,128)S(1)} %collective-permute-done.6.refs_1_), channel_id=1, source_target_pairs={{0,12},{2,14},{4,8},{6,10},{8,4},{10,6},{12,0},{14,2},{1,3},{3,1},... | collective-permute-start | bytes 208904 | tf_op jit(solution)/shard_map/ppermute | solution.py:432
  25.6 5.1 %collective-permute-start.10 = (f32[136,128]{1,0:T(8,128)S(1)}, f32[136,128]{1,0:T(8,128)S(1)}, u32[]{:S(2)}, u32[]{:S(2)}) collective-permute-start(f32[136,128]{1,0:T(8,128)S(1)} %collective-permute-done.6.refs_1_), channel_id=1, source_target_pairs={{0,1},{1,0},{2,3},{3,2},{4,5},{5,4},{6,7},{7,6},{8,9},{9,8},{10,11... | collective-permute-start | bytes 208904 | tf_op jit(solution)/shard_map/ppermute | solution.py:417
  26.3 4.4 %collective-permute-start.11 = (f32[136,128]{1,0:T(8,128)S(1)}, f32[136,128]{1,0:T(8,128)S(1)}, u32[]{:S(2)}, u32[]{:S(2)}) collective-permute-start(f32[136,128]{1,0:T(8,128)S(1)} %collective-permute-done.7.refs_2_), channel_id=1, source_target_pairs={{0,1},{1,0},{2,3},{3,2},{4,5},{5,4},{6,7},{7,6},{8,9},{9,8},{10,11... | collective-permute-start | bytes 208904 | tf_op jit(solution)/shard_map/ppermute | solution.py:417
  26.8 3.9 %collective-permute-start.12 = (f32[136,128]{1,0:T(8,128)S(1)}, f32[136,128]{1,0:T(8,128)S(1)}, u32[]{:S(2)}, u32[]{:S(2)}) collective-permute-start(f32[136,128]{1,0:T(8,128)S(1)} %collective-permute-done.8.refs_3_), channel_id=1, source_target_pairs={{0,1},{1,0},{2,3},{3,2},{4,5},{5,4},{6,7},{7,6},{8,9},{9,8},{10,11... | collective-permute-start | bytes 208904 | tf_op jit(solution)/shard_map/ppermute | solution.py:417
  29.7 1.3 %collective-permute-start.13 = (f32[136,128]{1,0:T(8,128)S(1)}, f32[136,128]{1,0:T(8,128)S(1)}, u32[]{:S(2)}, u32[]{:S(2)}) collective-permute-start(f32[136,128]{1,0:T(8,128)S(1)} %collective-permute-done.9.refs_4_), channel_id=1, source_target_pairs={{0,1},{1,0},{2,3},{3,2},{4,5},{5,4},{6,7},{7,6},{8,9},{9,8},{10,11... | collective-permute-start | bytes 208904 | tf_op jit(solution)/shard_map/ppermute | solution.py:417
  34.0 1.3 %collective-permute-start.15 = (f32[32,512]{1,0:T(8,128)S(1)}, f32[32,512]{1,0:T(8,128)S(1)}, u32[]{:S(2)}, u32[]{:S(2)}) collective-permute-start(f32[32,512]{1,0:T(8,128)S(1)} %get-tuple-element.32.mine_ref), channel_id=1, source_target_pairs={{0,1},{1,0},{2,3},{3,2},{4,5},{5,4},{6,7},{7,6},{8,9},{9,8},{10,11... | collective-permute-start | bytes 196616 | tf_op jit(solution)/shard_map/ppermute | solution.py:417
  35.7 4.3 %collective-permute-start.16 = (f32[136,128]{1,0:T(8,128)S(1)}, f32[136,128]{1,0:T(8,128)S(1)}, u32[]{:S(2)}, u32[]{:S(2)}) collective-permute-start(f32[136,128]{1,0:T(8,128)S(1)} %image.3.refs_0_), channel_id=1, source_target_pairs={{0,2},{2,0},{4,6},{6,4},{8,10},{10,8},{12,14},{14,12},{1,9},{3,11}... | collective-permute-start | bytes 208904 | tf_op jit(solution)/shard_map/ppermute | solution.py:432
  37.2 5.8 %collective-permute-start.17 = (f32[136,128]{1,0:T(8,128)S(1)}, f32[136,128]{1,0:T(8,128)S(1)}, u32[]{:S(2)}, u32[]{:S(2)}) collective-permute-start(f32[136,128]{1,0:T(8,128)S(1)} %image.3.refs_0_), channel_id=1, source_target_pairs={{0,6},{2,4},{4,2},{6,0},{8,14},{10,12},{12,10},{14,8},{1,13},{3,15... | collective-permute-start | bytes 208904 | tf_op jit(solution)/shard_map/ppermute | solution.py:432
  37.2 5.8 %collective-permute-start.18 = (f32[136,128]{1,0:T(8,128)S(1)}, f32[136,128]{1,0:T(8,128)S(1)}, u32[]{:S(2)}, u32[]{:S(2)}) collective-permute-start(f32[136,128]{1,0:T(8,128)S(1)} %image.3.refs_0_), channel_id=1, source_target_pairs={{0,4},{2,6},{4,0},{6,2},{8,12},{10,14},{12,8},{14,10},{1,3},{3,1},... | collective-permute-start | bytes 208904 | tf_op jit(solution)/shard_map/ppermute | solution.py:432
  40.0 6.1 %collective-permute-start.19 = (f32[136,128]{1,0:T(8,128)S(1)}, f32[136,128]{1,0:T(8,128)S(1)}, u32[]{:S(2)}, u32[]{:S(2)}) collective-permute-start(f32[136,128]{1,0:T(8,128)S(1)} %collective-permute-done.16.refs_1_), channel_id=1, source_target_pairs={{0,12},{2,14},{4,8},{6,10},{8,4},{10,6},{12,0},{14,2},{1,3},{3,1},... | collective-permute-start | bytes 208904 | tf_op jit(solution)/shard_map/ppermute | solution.py:432
  42.0 5.0 %collective-permute-start.20 = (f32[136,128]{1,0:T(8,128)S(1)}, f32[136,128]{1,0:T(8,128)S(1)}, u32[]{:S(2)}, u32[]{:S(2)}) collective-permute-start(f32[136,128]{1,0:T(8,128)S(1)} %collective-permute-done.16.refs_1_), channel_id=1, source_target_pairs={{0,1},{1,0},{2,3},{3,2},{4,5},{5,4},{6,7},{7,6},{8,9},{9,8},{10,11... | collective-permute-start | bytes 208904 | tf_op jit(solution)/shard_map/ppermute | solution.py:417
  43.0 4.0 %collective-permute-start.21 = (f32[136,128]{1,0:T(8,128)S(1)}, f32[136,128]{1,0:T(8,128)S(1)}, u32[]{:S(2)}, u32[]{:S(2)}) collective-permute-start(f32[136,128]{1,0:T(8,128)S(1)} %collective-permute-done.17.refs_2_), channel_id=1, source_target_pairs={{0,1},{1,0},{2,3},{3,2},{4,5},{5,4},{6,7},{7,6},{8,9},{9,8},{10,11... | collective-permute-start | bytes 208904 | tf_op jit(solution)/shard_map/ppermute | solution.py:417
  43.0 4.0 %collective-permute-start.22 = (f32[136,128]{1,0:T(8,128)S(1)}, f32[136,128]{1,0:T(8,128)S(1)}, u32[]{:S(2)}, u32[]{:S(2)}) collective-permute-start(f32[136,128]{1,0:T(8,128)S(1)} %collective-permute-done.18.refs_3_), channel_id=1, source_target_pairs={{0,1},{1,0},{2,3},{3,2},{4,5},{5,4},{6,7},{7,6},{8,9},{9,8},{10,11... | collective-permute-start | bytes 208904 | tf_op jit(solution)/shard_map/ppermute | solution.py:417
  46.1 1.3 %collective-permute-start.23 = (f32[136,128]{1,0:T(8,128)S(1)}, f32[136,128]{1,0:T(8,128)S(1)}, u32[]{:S(2)}, u32[]{:S(2)}) collective-permute-start(f32[136,128]{1,0:T(8,128)S(1)} %collective-permute-done.19.refs_4_), channel_id=1, source_target_pairs={{0,1},{1,0},{2,3},{3,2},{4,5},{5,4},{6,7},{7,6},{8,9},{9,8},{10,11... | collective-permute-start | bytes 208904 | tf_op jit(solution)/shard_map/ppermute | solution.py:417
  50.4 1.3 %collective-permute-start.24 = (f32[32,512]{1,0:T(8,128)S(1)}, f32[32,512]{1,0:T(8,128)S(1)}, u32[]{:S(2)}, u32[]{:S(2)}) collective-permute-start(f32[32,512]{1,0:T(8,128)S(1)} %get-tuple-element.37.mine_ref), channel_id=1, source_target_pairs={{0,1},{1,0},{2,3},{3,2},{4,5},{5,4},{6,7},{7,6},{8,9},{9,8},{10,11... | collective-permute-start | bytes 196616 | tf_op jit(solution)/shard_map/ppermute | solution.py:417
  52.0 3.6 %collective-permute-start.25 = (f32[8,128]{1,0:T(8,128)S(1)}, f32[8,128]{1,0:T(8,128)S(1)}, u32[]{:S(2)}, u32[]{:S(2)}) collective-permute-start(f32[8,128]{1,0:T(8,128)S(1)} %get-tuple-element.39.refs_0_), channel_id=1, source_target_pairs={{0,2},{2,0},{4,6},{6,4},{8,10},{10,8},{12,14},{14,12},{1,9},{3,11}... | collective-permute-start | bytes 12296 | tf_op jit(solution)/shard_map/ppermute | solution.py:432
  53.6 4.5 %collective-permute-start.26 = (f32[8,128]{1,0:T(8,128)S(1)}, f32[8,128]{1,0:T(8,128)S(1)}, u32[]{:S(2)}, u32[]{:S(2)}) collective-permute-start(f32[8,128]{1,0:T(8,128)S(1)} %get-tuple-element.39.refs_0_), channel_id=1, source_target_pairs={{0,6},{2,4},{4,2},{6,0},{8,14},{10,12},{12,10},{14,8},{1,13},{3,15... | collective-permute-start | bytes 12296 | tf_op jit(solution)/shard_map/ppermute | solution.py:432
  53.6 4.6 %collective-permute-start.27 = (f32[8,128]{1,0:T(8,128)S(1)}, f32[8,128]{1,0:T(8,128)S(1)}, u32[]{:S(2)}, u32[]{:S(2)}) collective-permute-start(f32[8,128]{1,0:T(8,128)S(1)} %get-tuple-element.39.refs_0_), channel_id=1, source_target_pairs={{0,4},{2,6},{4,0},{6,2},{8,12},{10,14},{12,8},{14,10},{1,3},{3,1},... | collective-permute-start | bytes 12296 | tf_op jit(solution)/shard_map/ppermute | solution.py:432
  55.6 5.4 %collective-permute-start.28 = (f32[8,128]{1,0:T(8,128)S(1)}, f32[8,128]{1,0:T(8,128)S(1)}, u32[]{:S(2)}, u32[]{:S(2)}) collective-permute-start(f32[8,128]{1,0:T(8,128)S(1)} %collective-permute-done.25.refs_1_), channel_id=1, source_target_pairs={{0,12},{2,14},{4,8},{6,10},{8,4},{10,6},{12,0},{14,2},{1,3},{3,1},... | collective-permute-start | bytes 12296 | tf_op jit(solution)/shard_map/ppermute | solution.py:432
  57.7 3.4 %collective-permute-start.29 = (f32[8,128]{1,0:T(8,128)S(1)}, f32[8,128]{1,0:T(8,128)S(1)}, u32[]{:S(2)}, u32[]{:S(2)}) collective-permute-start(f32[8,128]{1,0:T(8,128)S(1)} %collective-permute-done.25.refs_1_), channel_id=1, source_target_pairs={{0,1},{1,0},{2,3},{3,2},{4,5},{5,4},{6,7},{7,6},{8,9},{9,8},{10,11... | collective-permute-start | bytes 12296 | tf_op jit(solution)/shard_map/ppermute | solution.py:417
  58.1 3.0 %collective-permute-start.30 = (f32[8,128]{1,0:T(8,128)S(1)}, f32[8,128]{1,0:T(8,128)S(1)}, u32[]{:S(2)}, u32[]{:S(2)}) collective-permute-start(f32[8,128]{1,0:T(8,128)S(1)} %collective-permute-done.26.refs_2_), channel_id=1, source_target_pairs={{0,1},{1,0},{2,3},{3,2},{4,5},{5,4},{6,7},{7,6},{8,9},{9,8},{10,11... | collective-permute-start | bytes 12296 | tf_op jit(solution)/shard_map/ppermute | solution.py:417
  58.2 2.9 %collective-permute-start.31 = (f32[8,128]{1,0:T(8,128)S(1)}, f32[8,128]{1,0:T(8,128)S(1)}, u32[]{:S(2)}, u32[]{:S(2)}) collective-permute-start(f32[8,128]{1,0:T(8,128)S(1)} %collective-permute-done.27.refs_3_), channel_id=1, source_target_pairs={{0,1},{1,0},{2,3},{3,2},{4,5},{5,4},{6,7},{7,6},{8,9},{9,8},{10,11... | collective-permute-start | bytes 12296 | tf_op jit(solution)/shard_map/ppermute | solution.py:417
  61.0 1.2 %collective-permute-start.32 = (f32[8,128]{1,0:T(8,128)S(1)}, f32[8,128]{1,0:T(8,128)S(1)}, u32[]{:S(2)}, u32[]{:S(2)}) collective-permute-start(f32[8,128]{1,0:T(8,128)S(1)} %collective-permute-done.28.refs_4_), channel_id=1, source_target_pairs={{0,1},{1,0},{2,3},{3,2},{4,5},{5,4},{6,7},{7,6},{8,9},{9,8},{10,11... | collective-permute-start | bytes 12296 | tf_op jit(solution)/shard_map/ppermute | solution.py:417

commit v16 on v15

--- a/solution.py
+++ b/solution.py
@@ -47,6 +47,17 @@
 def times(stacked, right):
     high, middle, low = split(right)
     parts = jnp.concatenate([high, middle, high, low, middle, high], axis=0)
+    return jnp.dot(stacked, parts, preferred_element_type=F32)
+
+
+def stack_leading(left):
+    high, middle, _ = [part.astype(F32) for part in split(left)]
+    return jnp.concatenate([high, high, middle], axis=0).T.astype(BF16)
+
+
+def times_leading(stacked, right):
+    high, middle, _ = split(right)
+    parts = jnp.concatenate([high, middle, high], axis=0)
     return jnp.dot(stacked, parts, preferred_element_type=F32)
 
 
@@ -270,24 +281,24 @@
     return high + low
 
 
-def first_kernel(even_ref, odd_ref, matrix, out_ref, blocks_ref):
-    pieces = blocks_ref.shape[0]
+def first_kernel(even_ref, odd_ref, matrix, out_ref, odd_out_ref):
+    pieces = 2 * even_ref.shape[0]
+    odd_out_ref[...] = odd_ref[...]
     values = [(odd_ref if k % 2 else even_ref)[k // 2] for k in range(pieces)]
-    for k, value in enumerate(values):
-        blocks_ref[k] = value
     rows = 2 * values[0].shape[1]
     joined = jnp.concatenate(values, axis=1)
     out_ref[:, rows:] = gram_parts(joined, joined)
     out_ref[:, :rows] = apply_dense(values, matrix)
 
 
-def collect_kernel(near_ref, far_ref, residual_ref, direction_ref):
-    pieces = near_ref.shape[0]
+def collect_kernel(even_ref, odd_ref, far_even_ref, far_odd_ref, residual_ref, direction_ref):
+    pieces = 2 * even_ref.shape[0]
     for k in range(pieces):
-        residual_ref[0, k] = near_ref[k]
-        residual_ref[1, k] = far_ref[k]
-        direction_ref[k] = near_ref[k]
-    direction_ref[pieces] = far_ref[0]
+        near = (odd_ref if k % 2 else even_ref)[k // 2]
+        residual_ref[0, k] = near
+        residual_ref[1, k] = (far_odd_ref if k % 2 else far_even_ref)[k // 2]
+        direction_ref[k] = near
+    direction_ref[pieces] = far_even_ref[0]
 
 
 def add_halves(mine_ref, other_ref, width):
@@ -310,7 +321,7 @@
             at = pl.multiple_of((place * parts + i) * size, size)
             out_ref[pl.ds(at, size)] = half[:, lanes]
     products = symmetric_parts(near, near_ref[0]) + symmetric_parts(
-        far, far_ref[far_ref.shape[0] - 1]
+        far, far_ref[0 if first else far_ref.shape[0] - 1]
     )
     out_ref[2 * parts * size :] = pack(finish(products))
 
@@ -362,9 +373,9 @@
     new_norm[...] = next_norm
     step = times(alpha, direction_ref[0])
     new_solution[...] = solution_ref[...] + step if with_solution else step
-    beta = stack(mul(inverse_ref[:, :size], next_norm[:, :size]))
+    beta = stack_leading(mul(inverse_ref[:, :size], next_norm[:, :size]))
     directions = [
-        residual + times(beta, direction_ref[k])
+        residual + times_leading(beta, direction_ref[k])
         for k, residual in enumerate(residuals[0] + residuals[1][:1])
     ]
     if last:
@@ -422,22 +433,26 @@
         if pieces != 8:
             found = [value] + [swap(value, k) for k in range(1, pieces)]
             return found, [(k, k) for k in range(pieces)]
-
-        def fetch(source, masks):
+        turns = ((7, 5), (3, 6), (2, 4), (1, 1))
+        fetched = []
+        passed = []
+        places = {0: (0, 0)}
+        for turn, masks in enumerate(turns, 1):
             pairs = [
                 (i * 2 + core, (i ^ mask) * 2 + core)
                 for core, mask in enumerate(masks)
                 for i in range(pieces)
             ]
-            return lax.ppermute(source, ("row", "col"), pairs)
-
-        fetched = [fetch(value, masks) for masks in ((1, 4), (3, 6), (2, 1))]
-        fetched.append(fetch(fetched[0], (6, 1)))
-        found = [value, *fetched, *map(across, fetched)]
-        return found, [(0, 0), (1, 3), (3, 7), (2, 6), (5, 1), (8, 4), (6, 2), (4, 8)]
+            fetched.append(lax.ppermute(value, ("row", "col"), pairs))
+            if masks[0] == masks[1]:
+                places[masks[0]] = (turn, turn)
+            else:
+                passed.append(across(fetched[-1]))
+                places[masks[0]] = (turn, turn + len(turns))
+                places[masks[1]] = (turn + len(turns), turn)
+        return [value, *fetched, *passed], [places[k] for k in range(pieces)]
 
     right_side = signs.astype(F32) * vertex_weight[None, :] * column_scale[:, None]
-    far_side = across(right_side)[None]
     even = [right_side] + [swap(right_side, k) for k in range(2, pieces, 2)]
 
     matrix = shape(2, depth, group, dtype=BF16)
@@ -476,6 +491,7 @@
         name="join",
     )(*[even[k] for k in order], blocks_sum)
     odd = swap(even, 1)
+    far_even = across(even)
     dense, _ = pl.pallas_call(
         functools.partial(dense_kernel, rows_dev),
         out_shape=(matrix, total),
@@ -495,9 +511,9 @@
     packed = shape(sketch * sketch // LANES, LANES)
     payload = shape(2 * sketch * (rows_dev // LANES) + packed.shape[0], LANES)
 
-    partial_sum, blocks = pl.pallas_call(
+    partial_sum, odd = pl.pallas_call(
         first_kernel,
-        out_shape=(shape(sketch, group + LANES), shape(pieces, sketch, rows_dev)),
+        out_shape=(shape(sketch, group + LANES), joined),
         in_specs=[VMEM] * 3,
         out_specs=(VMEM, VMEM),
         compiler_params=params(matrix, state, state),
@@ -510,7 +526,7 @@
         first = iteration == 0
         last = iteration == ITERS - 2
         sums = (partial_sum, across(partial_sum))
-        given = (even, far_side) if first else (direction, direction)
+        given = (even, far_even) if first else (direction, direction)
         outs = pl.pallas_call(
             functools.partial(image_kernel, first),
             out_shape=(payload, small) if first else (payload,),
@@ -525,11 +541,11 @@
             residual, direction = pl.pallas_call(
                 collect_kernel,
                 out_shape=(held, state),
-                in_specs=[VMEM] * 2,
+                in_specs=[VMEM] * 4,
                 out_specs=(VMEM, VMEM),
                 compiler_params=params(held, held, state),
                 name="collect",
-            )(blocks, across(blocks))
+            )(even, odd, far_even, across(odd))
         inverse = pl.pallas_call(
             inverse_kernel,
             out_shape=small,

time: 64.1 us -> 60.5 us (0.944)
  waiting for transfers between devices: 18 us -> 12.3 us
  starting transfers between devices: 26.6 us -> 29.1 us
    ppermute x12, waiting for transfers between devices: 11.7 us -> 7.52 us  [exchange(): fetched.append(lax.ppermute(value, ('row', 'col'), pairs))]
    ppermute x12, starting transfers between devices: 16.6 us -> 18.4 us  [exchange(): fetched.append(lax.ppermute(value, ('row', 'col'), pairs))]
    ppermute x17 -> x14, waiting for transfers between devices: 4.79 us -> 3.13 us  [across(): lax.ppermute(value, 'col', [(i, (i + 1) % col_devices) for i in range(col...]
    ppermute x17 -> x14, starting transfers between devices: 2.82 us -> 3.5 us  [across(): lax.ppermute(value, 'col', [(i, (i + 1) % col_devices) for i in range(col...]
  transfers between devices with their start and end apart: 33 -> 30, of which waited for: 18 -> 13; matrix products, arithmetic and copies ran while one was open for 0% -> 0% of each run, Pallas kernels for 12% -> 13%
where the time goes in v16:
time: 60.5 us; the launch traced here: 60.4 us
  starting transfers between devices  29.1 us (48%)
  Pallas kernels  16.6 us (27%)
  waiting for transfers between devices  12.3 us (20%)
  between operations  1.43 us (2%)
  other arithmetic  0.85 us (1%)
    ppermute x12, starting transfers between devices, exchange(): fetched.append(lax.ppermute(value, ('row', 'col'), pairs))  18.4 us
    ppermute x12, waiting for transfers between devices, exchange(): fetched.append(lax.ppermute(value, ('row', 'col'), pairs))  7.52 us
    ppermute x4, starting transfers between devices, swap(): return lax.ppermute(value, 'row', [(i, i ^ mask) for i in range(pieces)])  7.2 us
    pallas_call x2, Pallas kernels, per_device(): pl.pallas_call(functools.partial(step_kernel, len(found), places, not fir...  5.89 us
    ppermute x14, starting transfers between devices, across(): lax.ppermute(value, 'col', [(i, (i + 1) % col_devices) for i in range(col...  3.5 us
    pallas_call x1, Pallas kernels, per_device(): pl.pallas_call(functools.partial(dense_kernel, rows_dev), out_shape=(matr...  3.13 us
    ppermute x14, waiting for transfers between devices, across(): lax.ppermute(value, 'col', [(i, (i + 1) % col_devices) for i in range(col...  3.13 us
    pallas_call x1, Pallas kernels, per_device(): pl.pallas_call(functools.partial(gather_kernel, rows_dev), out_shape=(tot...  2.12 us
  transfers between devices with their start and end apart: 30, of which 13 were waited for; matrix products, arithmetic and copies ran while one was open for 0% of the time, Pallas kernels for 13%

profile of v16, /device:TPU:0, one launch (start us, length us, event | category | flops | bytes accessed | tf_op | source)
XLA Modules:
  0.0 60.4 jit_solution(4825325419225737804)
XLA Ops:
  0.6 0.8 %multiply_multiply_fusion.refs_3_ = f32[32,256]{1,0:T(8,128)S(1)} fusion(s32[32,256]{1,0:T(8,128)} %param.11, f32[32]{0:T(128)} %param.13, f32[256]{0:T(256)} %param.12), kind=kLoop, calls=%fused_computation | loop fusion | flops 24576 | bytes 66688 | tf_op jit(solution)/shard_map/mul | solution.py:455
  1.5 4.0 %collective-permute-start = (f32[32,256]{1,0:T(8,128)S(1)}, f32[32,256]{1,0:T(8,128)S(1)}, u32[]{:S(2)}, u32[]{:S(2)}) collective-permute-start(f32[32,256]{1,0:T(8,128)S(1)} %multiply_multiply_fusion.refs_3_), channel_id=1, source_target_pairs={{0,8},{2,10},{4,12},{6,14},{8,0},{10,2},{12,4},{14,6},{1,9},{3,11}... | collective-permute-start | bytes 98312 | tf_op jit(solution)/shard_map/ppermute | solution.py:425
  5.5 1.3 %collective-permute-start.1 = (f32[32,256]{1,0:T(8,128)S(1)}, f32[32,256]{1,0:T(8,128)S(1)}, u32[]{:S(2)}, u32[]{:S(2)}) collective-permute-start(f32[32,256]{1,0:T(8,128)S(1)} %multiply_multiply_fusion.refs_3_), channel_id=1, source_target_pairs={{0,12},{2,14},{4,8},{6,10},{8,4},{10,6},{12,0},{14,2},{1,13},{3,15... | collective-permute-start | bytes 98312 | tf_op jit(solution)/shard_map/ppermute | solution.py:425
  6.9 0.2 collective-permute-start.2
  7.8 2.1 %gather.1 = (f32[64,128,128]{2,1,0:T(8,128)S(1)}, bf16[82,128,128]{2,1,0:T(8,128)(2,1)S(1)}) custom-call(s32[1]{0:T(128)S(6)} %copy.11.count_ref, s32[130]{0:T(256)} %rows_hbm.3, s32[130]{0:T(256)} %cols_hbm.3, bf16[130,128,128]{2,1,0:T(8,128)(2,1)} %tiles_ref.1), custom_call_target="tpu_custom_call" | custom-call | flops 8519680 | bytes 8519680 | tf_op jit(solution)/shard_map/gather/pallas_call | solution.py:468
  9.9 0.0 collective-permute-done.refs_0_
  9.9 1.3 %collective-permute-done.1.refs_1_ = f32[32,256]{1,0:T(8,128)S(1)} collective-permute-done((f32[32,256]{1,0:T(8,128)S(1)}, f32[32,256]{1,0:T(8,128)S(1)}, u32[]{:S(2)}, u32[]{:S(2)}) %collective-permute-start.1) | collective-permute-done | bytes 32800 | tf_op jit(solution)/shard_map/ppermute | solution.py:425
  11.2 0.0 collective-permute-done.2.refs_2_
  11.2 1.6 %collective-permute-start.3 = (f32[4,32,256]{2,1,0:T(8,128)S(1)}, f32[4,32,256]{2,1,0:T(8,128)S(1)}, u32[]{:S(2)}, u32[]{:S(2)}) collective-permute-start(f32[4,32,256]{2,1,0:T(8,128)S(1)} %join.1.joined_ref.even_ref.near_ref), channel_id=1, source_target_pairs={{0,2},{2,0},{4,6},{6,4},{8,10},{10,8},{12,14},{14,12},{1,3},{3,1},... | collective-permute-start | bytes 393224 | tf_op jit(solution)/shard_map/ppermute | solution.py:425
  12.8 0.0 collective-permute-start.5
  12.8 3.1 %dense.1 = (bf16[2,2048,512]{2,1,0:T(8,128)(2,1)S(1)}, f32[64,128,128]{2,1,0:T(8,128)S(1)}) custom-call(s32[1]{0:T(128)S(6)} %copy.11.count_ref, s32[130]{0:T(256)} %rows_hbm.3, s32[130]{0:T(256)} %cols_hbm.3, bf16[82,128,128]{2,1,0:T(8,128)(2,1)S(1)} %get-tuple-element.24.rest, ...), custom_call_target="tpu_custom_call", output_to_operand_aliasing={{1}: (4, {})} | custom-call | flops 8519680 | bytes 8519680 | tf_op jit(solution)/shard_map/dense/pallas_call | solution.py:495
  16.0 0.3 collective-permute-done.3.odd_ref
  16.3 0.9 %first.1 = (f32[32,640]{1,0:T(8,128)S(1)}, f32[4,32,256]{2,1,0:T(8,128)S(1)}) custom-call(f32[4,32,256]{2,1,0:T(8,128)S(1)} %join.1.joined_ref.even_ref.near_ref, f32[4,32,256]{2,1,0:T(8,128)S(1)} %collective-permute-done.3.odd_ref, bf16[2,2048,512]{2,1,0:T(8,128)(2,1)S(1)} %get-tuple-element.25.matrix.refs_12_), custom_call_target="tpu_custom_call" | custom-call | tf_op jit(solution)/shard_map/first/pallas_call | solution.py:514
  17.2 0.2 collective-permute-start.4
  17.4 0.0 collective-permute-done.5.far_ref.far_even_ref
  17.4 1.1 %collective-permute-done.4.other_ref = f32[32,640]{1,0:T(8,128)S(1)} collective-permute-done((f32[32,640]{1,0:T(8,128)S(1)}, f32[32,640]{1,0:T(8,128)S(1)}, u32[]{:S(2)}, u32[]{:S(2)}) %collective-permute-start.4) | collective-permute-done | bytes 81952 | tf_op jit(solution)/shard_map/ppermute | solution.py:428
  18.5 0.3 image.2
  18.8 3.0 %collective-permute-start.6 = (f32[136,128]{1,0:T(8,128)S(1)}, f32[136,128]{1,0:T(8,128)S(1)}, u32[]{:S(2)}, u32[]{:S(2)}) collective-permute-start(f32[136,128]{1,0:T(8,128)S(1)} %get-tuple-element.27.refs_0_), channel_id=1, source_target_pairs={{0,14},{2,12},{4,10},{6,8},{8,6},{10,4},{12,2},{14,0},{1,11},{3,9}... | collective-permute-start | bytes 208904 | tf_op jit(solution)/shard_map/ppermute | solution.py:446
  21.8 0.0 collective-permute-start.7
  21.8 3.1 %collective-permute-start.8 = (f32[136,128]{1,0:T(8,128)S(1)}, f32[136,128]{1,0:T(8,128)S(1)}, u32[]{:S(2)}, u32[]{:S(2)}) collective-permute-start(f32[136,128]{1,0:T(8,128)S(1)} %get-tuple-element.27.refs_0_), channel_id=1, source_target_pairs={{0,4},{2,6},{4,0},{6,2},{8,12},{10,14},{12,8},{14,10},{1,9},{3,11}... | collective-permute-start | bytes 208904 | tf_op jit(solution)/shard_map/ppermute | solution.py:446
  25.0 0.4 collective-permute-start.9
  25.3 1.0 %collective-permute-done.6.refs_1_ = f32[136,128]{1,0:T(8,128)S(1)} collective-permute-done((f32[136,128]{1,0:T(8,128)S(1)}, f32[136,128]{1,0:T(8,128)S(1)}, u32[]{:S(2)}, u32[]{:S(2)}) %collective-permute-start.6) | collective-permute-done | bytes 69664 | tf_op jit(solution)/shard_map/ppermute | solution.py:446
  26.3 0.5 collective-permute-start.10
  26.8 0.9 %collective-permute-done.7.refs_2_ = f32[136,128]{1,0:T(8,128)S(1)} collective-permute-done((f32[136,128]{1,0:T(8,128)S(1)}, f32[136,128]{1,0:T(8,128)S(1)}, u32[]{:S(2)}, u32[]{:S(2)}) %collective-permute-start.7) | collective-permute-done | bytes 69664 | tf_op jit(solution)/shard_map/ppermute | solution.py:446
  27.7 0.8 %collective-permute-done.8.refs_3_ = f32[136,128]{1,0:T(8,128)S(1)} collective-permute-done((f32[136,128]{1,0:T(8,128)S(1)}, f32[136,128]{1,0:T(8,128)S(1)}, u32[]{:S(2)}, u32[]{:S(2)}) %collective-permute-start.8) | collective-permute-done | bytes 69664 | tf_op jit(solution)/shard_map/ppermute | solution.py:446
  28.5 0.6 %collective-permute-start.12 = (f32[136,128]{1,0:T(8,128)S(1)}, f32[136,128]{1,0:T(8,128)S(1)}, u32[]{:S(2)}, u32[]{:S(2)}) collective-permute-start(f32[136,128]{1,0:T(8,128)S(1)} %collective-permute-done.8.refs_3_), channel_id=1, source_target_pairs={{0,1},{1,0},{2,3},{3,2},{4,5},{5,4},{6,7},{7,6},{8,9},{9,8},{10,11... | collective-permute-start | bytes 208904 | tf_op jit(solution)/shard_map/ppermute | solution.py:428
  29.1 0.9 %inverse.2.refs_11_ = f32[32,128]{1,0:T(8,128)S(1)} custom-call(f32[32,128]{1,0:T(8,128)S(1)} %get-tuple-element.31.norm_ref.refs_10_), custom_call_target="tpu_custom_call" | custom-call | tf_op jit(solution)/shard_map/inverse/pallas_call | solution.py:549
  30.0 0.0 collective-permute-done.13.far_odd_ref
  30.0 0.1 collect.1
  30.1 0.0 collective-permute-done.10.refs_5_
  30.1 2.9 %step.2 = (f32[32,512]{1,0:T(8,128)S(1)}, f32[9,32,256]{2,1,0:T(8,128)S(1)}, f32[2,8,32,256]{3,2,1,0:T(8,128)S(1)}, f32[32,128]{1,0:T(8,128)S(1)}, f32[32,256]{1,0:T(8,128)S(1)}) custom-call(f32[136,128]{1,0:T(8,128)S(1)} %get-tuple-element.27.refs_0_, f32[136,128]{1,0:T(8,128)S(1)} %collective-permute-done.6.refs_1_, ...), custom_call_target="tpu_custom_call" | custom-call | tf_op jit(solution)/shard_map/step/pallas_call | solution.py:558
  33.1 0.2 collective-permute-start.14
  33.3 1.0 %collective-permute-done.14.other_ref = f32[32,512]{1,0:T(8,128)S(1)} collective-permute-done((f32[32,512]{1,0:T(8,128)S(1)}, f32[32,512]{1,0:T(8,128)S(1)}, u32[]{:S(2)}, u32[]{:S(2)}) %collective-permute-start.14) | collective-permute-done | bytes 65568 | tf_op jit(solution)/shard_map/ppermute | solution.py:428
  34.3 0.3 image.3.refs_0_
  34.7 2.4 %collective-permute-start.15 = (f32[136,128]{1,0:T(8,128)S(1)}, f32[136,128]{1,0:T(8,128)S(1)}, u32[]{:S(2)}, u32[]{:S(2)}) collective-permute-start(f32[136,128]{1,0:T(8,128)S(1)} %image.3.refs_0_), channel_id=1, source_target_pairs={{0,14},{2,12},{4,10},{6,8},{8,6},{10,4},{12,2},{14,0},{1,11},{3,9}... | collective-permute-start | bytes 208904 | tf_op jit(solution)/shard_map/ppermute | solution.py:446
  37.1 0.0 collective-permute-start.16
  37.1 2.7 %collective-permute-start.17 = (f32[136,128]{1,0:T(8,128)S(1)}, f32[136,128]{1,0:T(8,128)S(1)}, u32[]{:S(2)}, u32[]{:S(2)}) collective-permute-start(f32[136,128]{1,0:T(8,128)S(1)} %image.3.refs_0_), channel_id=1, source_target_pairs={{0,4},{2,6},{4,0},{6,2},{8,12},{10,14},{12,8},{14,10},{1,9},{3,11}... | collective-permute-start | bytes 208904 | tf_op jit(solution)/shard_map/ppermute | solution.py:446
  39.8 0.8 %collective-permute-start.18 = (f32[136,128]{1,0:T(8,128)S(1)}, f32[136,128]{1,0:T(8,128)S(1)}, u32[]{:S(2)}, u32[]{:S(2)}) collective-permute-start(f32[136,128]{1,0:T(8,128)S(1)} %image.3.refs_0_), channel_id=1, source_target_pairs={{0,2},{2,0},{4,6},{6,4},{8,10},{10,8},{12,14},{14,12},{1,3},{3,1},... | collective-permute-start | bytes 208904 | tf_op jit(solution)/shard_map/ppermute | solution.py:446
  40.6 2.0 %collective-permute-done.15.refs_1_ = f32[136,128]{1,0:T(8,128)S(1)} collective-permute-done((f32[136,128]{1,0:T(8,128)S(1)}, f32[136,128]{1,0:T(8,128)S(1)}, u32[]{:S(2)}, u32[]{:S(2)}) %collective-permute-start.15) | collective-permute-done | bytes 69664 | tf_op jit(solution)/shard_map/ppermute | solution.py:446
  42.6 0.6 %collective-permute-start.19 = (f32[136,128]{1,0:T(8,128)S(1)}, f32[136,128]{1,0:T(8,128)S(1)}, u32[]{:S(2)}, u32[]{:S(2)}) collective-permute-start(f32[136,128]{1,0:T(8,128)S(1)} %collective-permute-done.15.refs_1_), channel_id=1, source_target_pairs={{0,1},{1,0},{2,3},{3,2},{4,5},{5,4},{6,7},{7,6},{8,9},{9,8},{10,11... | collective-permute-start | bytes 208904 | tf_op jit(solution)/shard_map/ppermute | solution.py:428
  43.2 0.3 collective-permute-done.16.refs_2_
  43.5 0.0 collective-permute-done.17.refs_3_
  43.5 0.6 collective-permute-start.21
  44.1 0.9 %inverse.3.refs_11_ = f32[32,128]{1,0:T(8,128)S(1)} custom-call(f32[32,128]{1,0:T(8,128)S(1)} %get-tuple-element.35.norm_ref.refs_10_), custom_call_target="tpu_custom_call" | custom-call | tf_op jit(solution)/shard_map/inverse/pallas_call | solution.py:549
  45.0 0.0 collective-permute-done.18.refs_4_
  45.0 0.0 collective-permute-done.20.refs_6_
  45.1 0.0 collective-permute-done.21.refs_7_
  45.1 2.9 %step.3 = (f32[32,512]{1,0:T(8,128)S(1)}, f32[2,32,256]{2,1,0:T(8,128)S(1)}, f32[32,256]{1,0:T(8,128)S(1)}, f32[32,128]{1,0:T(8,128)S(1)}, f32[32,256]{1,0:T(8,128)S(1)}) custom-call(f32[136,128]{1,0:T(8,128)S(1)} %image.3.refs_0_, f32[136,128]{1,0:T(8,128)S(1)} %collective-permute-done.15.refs_1_, f32[136,128]{1,0:T(8,128)S(1)} %collective-permute-done.16.refs_2_, ...), custom_call_target="tpu_custom_call" | custom-call | tf_op jit(solution)/shard_map/step/pallas_call | solution.py:558
  48.0 0.3 collective-permute-start.22
  48.3 1.0 %collective-permute-done.22.other_ref = f32[32,512]{1,0:T(8,128)S(1)} collective-permute-done((f32[32,512]{1,0:T(8,128)S(1)}, f32[32,512]{1,0:T(8,128)S(1)}, u32[]{:S(2)}, u32[]{:S(2)}) %collective-permute-start.22) | collective-permute-done | bytes 65568 | tf_op jit(solution)/shard_map/ppermute | solution.py:428
  49.3 0.3 last_image.1
  49.6 2.5 %collective-permute-start.23 = (f32[8,128]{1,0:T(8,128)S(1)}, f32[8,128]{1,0:T(8,128)S(1)}, u32[]{:S(2)}, u32[]{:S(2)}) collective-permute-start(f32[8,128]{1,0:T(8,128)S(1)} %get-tuple-element.39.refs_0_), channel_id=1, source_target_pairs={{0,14},{2,12},{4,10},{6,8},{8,6},{10,4},{12,2},{14,0},{1,11},{3,9}... | collective-permute-start | bytes 12296 | tf_op jit(solution)/shard_map/ppermute | solution.py:446
  52.1 0.1 collective-permute-start.24
  52.3 2.8 %collective-permute-start.25 = (f32[8,128]{1,0:T(8,128)S(1)}, f32[8,128]{1,0:T(8,128)S(1)}, u32[]{:S(2)}, u32[]{:S(2)}) collective-permute-start(f32[8,128]{1,0:T(8,128)S(1)} %get-tuple-element.39.refs_0_), channel_id=1, source_target_pairs={{0,4},{2,6},{4,0},{6,2},{8,12},{10,14},{12,8},{14,10},{1,9},{3,11}... | collective-permute-start | bytes 12296 | tf_op jit(solution)/shard_map/ppermute | solution.py:446
  55.1 0.6 collective-permute-start.26
  55.6 0.3 collective-permute-done.23.refs_1_
  55.9 0.7 %collective-permute-done.24.refs_2_ = f32[8,128]{1,0:T(8,128)S(1)} collective-permute-done((f32[8,128]{1,0:T(8,128)S(1)}, f32[8,128]{1,0:T(8,128)S(1)}, u32[]{:S(2)}, u32[]{:S(2)}) %collective-permute-start.24) | collective-permute-done | bytes 4128 | tf_op jit(solution)/shard_map/ppermute | solution.py:446
  56.7 0.0 collective-permute-start.28
  56.7 0.0 collective-permute-done.25.refs_3_
  56.7 0.5 collective-permute-start.29
  57.2 1.5 %collective-permute-done.26.refs_4_ = f32[8,128]{1,0:T(8,128)S(1)} collective-permute-done((f32[8,128]{1,0:T(8,128)S(1)}, f32[8,128]{1,0:T(8,128)S(1)}, u32[]{:S(2)}, u32[]{:S(2)}) %collective-permute-start.26) | collective-permute-done | bytes 4128 | tf_op jit(solution)/shard_map/ppermute | solution.py:446
  58.7 0.0 collective-permute-done.27.refs_5_
  58.7 0.0 collective-permute-done.28.refs_6_
  58.7 1.7 %last.1 = (f32[32,256]{1,0:T(8,128)}, f32[32,256]{1,0:T(8,128)}) custom-call(f32[8,128]{1,0:T(8,128)S(1)} %get-tuple-element.39.refs_0_, f32[8,128]{1,0:T(8,128)S(1)} %collective-permute-done.23.refs_1_, f32[8,128]{1,0:T(8,128)S(1)} %collective-permute-done.24.refs_2_, f32[8,128]{1,0:T(8,128)S(1)} %collective-permute-done.25.refs_3_, ...), custom_call_target="tpu_custom_call" | custom-call | tf_op jit(solution)/shard_map/last/pallas_call | solution.py:581
  (10 shorter events, 0.0 us)
Async XLA Ops:
  1.5 8.4 %collective-permute-start = (f32[32,256]{1,0:T(8,128)S(1)}, f32[32,256]{1,0:T(8,128)S(1)}, u32[]{:S(2)}, u32[]{:S(2)}) collective-permute-start(f32[32,256]{1,0:T(8,128)S(1)} %multiply_multiply_fusion.refs_3_), channel_id=1, source_target_pairs={{0,8},{2,10},{4,12},{6,14},{8,0},{10,2},{12,4},{14,6},{1,9},{3,11}... | collective-permute-start | bytes 98312 | tf_op jit(solution)/shard_map/ppermute | solution.py:425
  5.5 5.7 %collective-permute-start.1 = (f32[32,256]{1,0:T(8,128)S(1)}, f32[32,256]{1,0:T(8,128)S(1)}, u32[]{:S(2)}, u32[]{:S(2)}) collective-permute-start(f32[32,256]{1,0:T(8,128)S(1)} %multiply_multiply_fusion.refs_3_), channel_id=1, source_target_pairs={{0,12},{2,14},{4,8},{6,10},{8,4},{10,6},{12,0},{14,2},{1,13},{3,15... | collective-permute-start | bytes 98312 | tf_op jit(solution)/shard_map/ppermute | solution.py:425
  6.9 4.4 %collective-permute-start.2 = (f32[32,256]{1,0:T(8,128)S(1)}, f32[32,256]{1,0:T(8,128)S(1)}, u32[]{:S(2)}, u32[]{:S(2)}) collective-permute-start(f32[32,256]{1,0:T(8,128)S(1)} %multiply_multiply_fusion.refs_3_), channel_id=1, source_target_pairs={{0,4},{2,6},{4,0},{6,2},{8,12},{10,14},{12,8},{14,10},{1,5},{3,7},... | collective-permute-start | bytes 98312 | tf_op jit(solution)/shard_map/ppermute | solution.py:425
  11.2 5.0 %collective-permute-start.3 = (f32[4,32,256]{2,1,0:T(8,128)S(1)}, f32[4,32,256]{2,1,0:T(8,128)S(1)}, u32[]{:S(2)}, u32[]{:S(2)}) collective-permute-start(f32[4,32,256]{2,1,0:T(8,128)S(1)} %join.1.joined_ref.even_ref.near_ref), channel_id=1, source_target_pairs={{0,2},{2,0},{4,6},{6,4},{8,10},{10,8},{12,14},{14,12},{1,3},{3,1},... | collective-permute-start | bytes 393224 | tf_op jit(solution)/shard_map/ppermute | solution.py:425
  12.8 4.6 %collective-permute-start.5 = (f32[4,32,256]{2,1,0:T(8,128)S(1)}, f32[4,32,256]{2,1,0:T(8,128)S(1)}, u32[]{:S(2)}, u32[]{:S(2)}) collective-permute-start(f32[4,32,256]{2,1,0:T(8,128)S(1)} %join.1.joined_ref.even_ref.near_ref), channel_id=1, source_target_pairs={{0,1},{1,0},{2,3},{3,2},{4,5},{5,4},{6,7},{7,6},{8,9},{9,8},{10,11... | collective-permute-start | bytes 393224 | tf_op jit(solution)/shard_map/ppermute | solution.py:428
  17.2 1.3 %collective-permute-start.4 = (f32[32,640]{1,0:T(8,128)S(1)}, f32[32,640]{1,0:T(8,128)S(1)}, u32[]{:S(2)}, u32[]{:S(2)}) collective-permute-start(f32[32,640]{1,0:T(8,128)S(1)} %get-tuple-element.26.mine_ref), channel_id=1, source_target_pairs={{0,1},{1,0},{2,3},{3,2},{4,5},{5,4},{6,7},{7,6},{8,9},{9,8},{10,11... | collective-permute-start | bytes 245768 | tf_op jit(solution)/shard_map/ppermute | solution.py:428
  18.8 7.5 %collective-permute-start.6 = (f32[136,128]{1,0:T(8,128)S(1)}, f32[136,128]{1,0:T(8,128)S(1)}, u32[]{:S(2)}, u32[]{:S(2)}) collective-permute-start(f32[136,128]{1,0:T(8,128)S(1)} %get-tuple-element.27.refs_0_), channel_id=1, source_target_pairs={{0,14},{2,12},{4,10},{6,8},{8,6},{10,4},{12,2},{14,0},{1,11},{3,9}... | collective-permute-start | bytes 208904 | tf_op jit(solution)/shard_map/ppermute | solution.py:446
  21.8 5.9 %collective-permute-start.7 = (f32[136,128]{1,0:T(8,128)S(1)}, f32[136,128]{1,0:T(8,128)S(1)}, u32[]{:S(2)}, u32[]{:S(2)}) collective-permute-start(f32[136,128]{1,0:T(8,128)S(1)} %get-tuple-element.27.refs_0_), channel_id=1, source_target_pairs={{0,6},{2,4},{4,2},{6,0},{8,14},{10,12},{12,10},{14,8},{1,13},{3,15... | collective-permute-start | bytes 208904 | tf_op jit(solution)/shard_map/ppermute | solution.py:446
  21.8 6.6 %collective-permute-start.8 = (f32[136,128]{1,0:T(8,128)S(1)}, f32[136,128]{1,0:T(8,128)S(1)}, u32[]{:S(2)}, u32[]{:S(2)}) collective-permute-start(f32[136,128]{1,0:T(8,128)S(1)} %get-tuple-element.27.refs_0_), channel_id=1, source_target_pairs={{0,4},{2,6},{4,0},{6,2},{8,12},{10,14},{12,8},{14,10},{1,9},{3,11}... | collective-permute-start | bytes 208904 | tf_op jit(solution)/shard_map/ppermute | solution.py:446
  25.0 5.0 %collective-permute-start.13 = (f32[4,32,256]{2,1,0:T(8,128)S(1)}, f32[4,32,256]{2,1,0:T(8,128)S(1)}, u32[]{:S(2)}, u32[]{:S(2)}) collective-permute-start(f32[4,32,256]{2,1,0:T(8,128)S(1)} %get-tuple-element.28.odd_ref), channel_id=1, source_target_pairs={{0,1},{1,0},{2,3},{3,2},{4,5},{5,4},{6,7},{7,6},{8,9},{9,8},{10,11... | collective-permute-start | bytes 393224 | tf_op jit(solution)/shard_map/ppermute | solution.py:428
  25.0 5.1 %collective-permute-start.9 = (f32[136,128]{1,0:T(8,128)S(1)}, f32[136,128]{1,0:T(8,128)S(1)}, u32[]{:S(2)}, u32[]{:S(2)}) collective-permute-start(f32[136,128]{1,0:T(8,128)S(1)} %get-tuple-element.27.refs_0_), channel_id=1, source_target_pairs={{0,2},{2,0},{4,6},{6,4},{8,10},{10,8},{12,14},{14,12},{1,3},{3,1},... | collective-permute-start | bytes 208904 | tf_op jit(solution)/shard_map/ppermute | solution.py:446
  26.3 3.8 %collective-permute-start.10 = (f32[136,128]{1,0:T(8,128)S(1)}, f32[136,128]{1,0:T(8,128)S(1)}, u32[]{:S(2)}, u32[]{:S(2)}) collective-permute-start(f32[136,128]{1,0:T(8,128)S(1)} %collective-permute-done.6.refs_1_), channel_id=1, source_target_pairs={{0,1},{1,0},{2,3},{3,2},{4,5},{5,4},{6,7},{7,6},{8,9},{9,8},{10,11... | collective-permute-start | bytes 208904 | tf_op jit(solution)/shard_map/ppermute | solution.py:428
  27.7 2.4 %collective-permute-start.11 = (f32[136,128]{1,0:T(8,128)S(1)}, f32[136,128]{1,0:T(8,128)S(1)}, u32[]{:S(2)}, u32[]{:S(2)}) collective-permute-start(f32[136,128]{1,0:T(8,128)S(1)} %collective-permute-done.7.refs_2_), channel_id=1, source_target_pairs={{0,1},{1,0},{2,3},{3,2},{4,5},{5,4},{6,7},{7,6},{8,9},{9,8},{10,11... | collective-permute-start | bytes 208904 | tf_op jit(solution)/shard_map/ppermute | solution.py:428
  28.5 1.6 %collective-permute-start.12 = (f32[136,128]{1,0:T(8,128)S(1)}, f32[136,128]{1,0:T(8,128)S(1)}, u32[]{:S(2)}, u32[]{:S(2)}) collective-permute-start(f32[136,128]{1,0:T(8,128)S(1)} %collective-permute-done.8.refs_3_), channel_id=1, source_target_pairs={{0,1},{1,0},{2,3},{3,2},{4,5},{5,4},{6,7},{7,6},{8,9},{9,8},{10,11... | collective-permute-start | bytes 208904 | tf_op jit(solution)/shard_map/ppermute | solution.py:428
  33.1 1.3 %collective-permute-start.14 = (f32[32,512]{1,0:T(8,128)S(1)}, f32[32,512]{1,0:T(8,128)S(1)}, u32[]{:S(2)}, u32[]{:S(2)}) collective-permute-start(f32[32,512]{1,0:T(8,128)S(1)} %get-tuple-element.32.mine_ref), channel_id=1, source_target_pairs={{0,1},{1,0},{2,3},{3,2},{4,5},{5,4},{6,7},{7,6},{8,9},{9,8},{10,11... | collective-permute-start | bytes 196616 | tf_op jit(solution)/shard_map/ppermute | solution.py:428
  34.7 7.9 %collective-permute-start.15 = (f32[136,128]{1,0:T(8,128)S(1)}, f32[136,128]{1,0:T(8,128)S(1)}, u32[]{:S(2)}, u32[]{:S(2)}) collective-permute-start(f32[136,128]{1,0:T(8,128)S(1)} %image.3.refs_0_), channel_id=1, source_target_pairs={{0,14},{2,12},{4,10},{6,8},{8,6},{10,4},{12,2},{14,0},{1,11},{3,9}... | collective-permute-start | bytes 208904 | tf_op jit(solution)/shard_map/ppermute | solution.py:446
  37.1 6.4 %collective-permute-start.16 = (f32[136,128]{1,0:T(8,128)S(1)}, f32[136,128]{1,0:T(8,128)S(1)}, u32[]{:S(2)}, u32[]{:S(2)}) collective-permute-start(f32[136,128]{1,0:T(8,128)S(1)} %image.3.refs_0_), channel_id=1, source_target_pairs={{0,6},{2,4},{4,2},{6,0},{8,14},{10,12},{12,10},{14,8},{1,13},{3,15... | collective-permute-start | bytes 208904 | tf_op jit(solution)/shard_map/ppermute | solution.py:446
  37.1 6.4 %collective-permute-start.17 = (f32[136,128]{1,0:T(8,128)S(1)}, f32[136,128]{1,0:T(8,128)S(1)}, u32[]{:S(2)}, u32[]{:S(2)}) collective-permute-start(f32[136,128]{1,0:T(8,128)S(1)} %image.3.refs_0_), channel_id=1, source_target_pairs={{0,4},{2,6},{4,0},{6,2},{8,12},{10,14},{12,8},{14,10},{1,9},{3,11}... | collective-permute-start | bytes 208904 | tf_op jit(solution)/shard_map/ppermute | solution.py:446
  39.8 5.2 %collective-permute-start.18 = (f32[136,128]{1,0:T(8,128)S(1)}, f32[136,128]{1,0:T(8,128)S(1)}, u32[]{:S(2)}, u32[]{:S(2)}) collective-permute-start(f32[136,128]{1,0:T(8,128)S(1)} %image.3.refs_0_), channel_id=1, source_target_pairs={{0,2},{2,0},{4,6},{6,4},{8,10},{10,8},{12,14},{14,12},{1,3},{3,1},... | collective-permute-start | bytes 208904 | tf_op jit(solution)/shard_map/ppermute | solution.py:446
  42.6 2.5 %collective-permute-start.19 = (f32[136,128]{1,0:T(8,128)S(1)}, f32[136,128]{1,0:T(8,128)S(1)}, u32[]{:S(2)}, u32[]{:S(2)}) collective-permute-start(f32[136,128]{1,0:T(8,128)S(1)} %collective-permute-done.15.refs_1_), channel_id=1, source_target_pairs={{0,1},{1,0},{2,3},{3,2},{4,5},{5,4},{6,7},{7,6},{8,9},{9,8},{10,11... | collective-permute-start | bytes 208904 | tf_op jit(solution)/shard_map/ppermute | solution.py:428
  43.5 1.5 %collective-permute-start.20 = (f32[136,128]{1,0:T(8,128)S(1)}, f32[136,128]{1,0:T(8,128)S(1)}, u32[]{:S(2)}, u32[]{:S(2)}) collective-permute-start(f32[136,128]{1,0:T(8,128)S(1)} %collective-permute-done.16.refs_2_), channel_id=1, source_target_pairs={{0,1},{1,0},{2,3},{3,2},{4,5},{5,4},{6,7},{7,6},{8,9},{9,8},{10,11... | collective-permute-start | bytes 208904 | tf_op jit(solution)/shard_map/ppermute | solution.py:428
  43.5 1.5 %collective-permute-start.21 = (f32[136,128]{1,0:T(8,128)S(1)}, f32[136,128]{1,0:T(8,128)S(1)}, u32[]{:S(2)}, u32[]{:S(2)}) collective-permute-start(f32[136,128]{1,0:T(8,128)S(1)} %collective-permute-done.17.refs_3_), channel_id=1, source_target_pairs={{0,1},{1,0},{2,3},{3,2},{4,5},{5,4},{6,7},{7,6},{8,9},{9,8},{10,11... | collective-permute-start | bytes 208904 | tf_op jit(solution)/shard_map/ppermute | solution.py:428
  48.0 1.3 %collective-permute-start.22 = (f32[32,512]{1,0:T(8,128)S(1)}, f32[32,512]{1,0:T(8,128)S(1)}, u32[]{:S(2)}, u32[]{:S(2)}) collective-permute-start(f32[32,512]{1,0:T(8,128)S(1)} %get-tuple-element.37.mine_ref), channel_id=1, source_target_pairs={{0,1},{1,0},{2,3},{3,2},{4,5},{5,4},{6,7},{7,6},{8,9},{9,8},{10,11... | collective-permute-start | bytes 196616 | tf_op jit(solution)/shard_map/ppermute | solution.py:428
  49.6 6.3 %collective-permute-start.23 = (f32[8,128]{1,0:T(8,128)S(1)}, f32[8,128]{1,0:T(8,128)S(1)}, u32[]{:S(2)}, u32[]{:S(2)}) collective-permute-start(f32[8,128]{1,0:T(8,128)S(1)} %get-tuple-element.39.refs_0_), channel_id=1, source_target_pairs={{0,14},{2,12},{4,10},{6,8},{8,6},{10,4},{12,2},{14,0},{1,11},{3,9}... | collective-permute-start | bytes 12296 | tf_op jit(solution)/shard_map/ppermute | solution.py:446
  52.1 4.5 %collective-permute-start.24 = (f32[8,128]{1,0:T(8,128)S(1)}, f32[8,128]{1,0:T(8,128)S(1)}, u32[]{:S(2)}, u32[]{:S(2)}) collective-permute-start(f32[8,128]{1,0:T(8,128)S(1)} %get-tuple-element.39.refs_0_), channel_id=1, source_target_pairs={{0,6},{2,4},{4,2},{6,0},{8,14},{10,12},{12,10},{14,8},{1,13},{3,15... | collective-permute-start | bytes 12296 | tf_op jit(solution)/shard_map/ppermute | solution.py:446
  52.3 4.4 %collective-permute-start.25 = (f32[8,128]{1,0:T(8,128)S(1)}, f32[8,128]{1,0:T(8,128)S(1)}, u32[]{:S(2)}, u32[]{:S(2)}) collective-permute-start(f32[8,128]{1,0:T(8,128)S(1)} %get-tuple-element.39.refs_0_), channel_id=1, source_target_pairs={{0,4},{2,6},{4,0},{6,2},{8,12},{10,14},{12,8},{14,10},{1,9},{3,11}... | collective-permute-start | bytes 12296 | tf_op jit(solution)/shard_map/ppermute | solution.py:446
  55.1 3.6 %collective-permute-start.26 = (f32[8,128]{1,0:T(8,128)S(1)}, f32[8,128]{1,0:T(8,128)S(1)}, u32[]{:S(2)}, u32[]{:S(2)}) collective-permute-start(f32[8,128]{1,0:T(8,128)S(1)} %get-tuple-element.39.refs_0_), channel_id=1, source_target_pairs={{0,2},{2,0},{4,6},{6,4},{8,10},{10,8},{12,14},{14,12},{1,3},{3,1},... | collective-permute-start | bytes 12296 | tf_op jit(solution)/shard_map/ppermute | solution.py:446
  55.9 2.7 %collective-permute-start.27 = (f32[8,128]{1,0:T(8,128)S(1)}, f32[8,128]{1,0:T(8,128)S(1)}, u32[]{:S(2)}, u32[]{:S(2)}) collective-permute-start(f32[8,128]{1,0:T(8,128)S(1)} %collective-permute-done.23.refs_1_), channel_id=1, source_target_pairs={{0,1},{1,0},{2,3},{3,2},{4,5},{5,4},{6,7},{7,6},{8,9},{9,8},{10,11... | collective-permute-start | bytes 12296 | tf_op jit(solution)/shard_map/ppermute | solution.py:428
  56.7 2.0 %collective-permute-start.28 = (f32[8,128]{1,0:T(8,128)S(1)}, f32[8,128]{1,0:T(8,128)S(1)}, u32[]{:S(2)}, u32[]{:S(2)}) collective-permute-start(f32[8,128]{1,0:T(8,128)S(1)} %collective-permute-done.24.refs_2_), channel_id=1, source_target_pairs={{0,1},{1,0},{2,3},{3,2},{4,5},{5,4},{6,7},{7,6},{8,9},{9,8},{10,11... | collective-permute-start | bytes 12296 | tf_op jit(solution)/shard_map/ppermute | solution.py:428
  56.7 2.0 %collective-permute-start.29 = (f32[8,128]{1,0:T(8,128)S(1)}, f32[8,128]{1,0:T(8,128)S(1)}, u32[]{:S(2)}, u32[]{:S(2)}) collective-permute-start(f32[8,128]{1,0:T(8,128)S(1)} %collective-permute-done.25.refs_3_), channel_id=1, source_target_pairs={{0,1},{1,0},{2,3},{3,2},{4,5},{5,4},{6,7},{7,6},{8,9},{9,8},{10,11... | collective-permute-start | bytes 12296 | tf_op jit(solution)/shard_map/ppermute | solution.py:428

commit v17 on v16

--- a/solution.py
+++ b/solution.py
@@ -32,10 +32,6 @@
     middle = rest.astype(BF16)
     low = (rest - middle.astype(F32)).astype(BF16)
     return high, middle, low
-
-
-def mul(left, right):
-    return jnp.dot(left, right, precision=lax.Precision.HIGHEST, preferred_element_type=F32)
 
 
 def stack(left):
@@ -363,6 +359,7 @@
 
     behind = slice(2 * parts * size, None)
     products = add_up([pick(images, pair, core, behind) for pair in places])
+    inverse = stack(inverse_ref[:, :size])
     alpha = stack(solve_wide(norm_ref[...], unpack(products, size, 1))[:, :size])
     residuals = [
         [residual_ref[side, k] - times(alpha, image(k, half)) for k in range(pieces)]
@@ -373,7 +370,7 @@
     new_norm[...] = next_norm
     step = times(alpha, direction_ref[0])
     new_solution[...] = solution_ref[...] + step if with_solution else step
-    beta = stack_leading(mul(inverse_ref[:, :size], next_norm[:, :size]))
+    beta = stack_leading(times(inverse, next_norm)[:, :size])
     directions = [
         residual + times_leading(beta, direction_ref[k])
         for k, residual in enumerate(residuals[0] + residuals[1][:1])
@@ -429,11 +426,10 @@
             value, "col", [(i, (i + 1) % col_devices) for i in range(col_devices)]
         )
 
-    def exchange(value):
+    def exchange(value, turns=((7, 5), (3, 6), (2, 4), (1, 1))):
         if pieces != 8:
             found = [value] + [swap(value, k) for k in range(1, pieces)]
             return found, [(k, k) for k in range(pieces)]
-        turns = ((7, 5), (3, 6), (2, 4), (1, 1))
         fetched = []
         passed = []
         places = {0: (0, 0)}
@@ -577,7 +573,7 @@
         compiler_params=params(state),
         name="last_image",
     )(partial_sum, across(partial_sum), direction)
-    found, places = exchange(gram)
+    found, places = exchange(gram, ((6, 7), (3, 5), (2, 4), (1, 1)))
     return pl.pallas_call(
         functools.partial(last_kernel, len(found), places),
         out_shape=(piece, piece),

time: 60.5 us -> 60 us (level)
  starting transfers between devices: 29.1 us -> 28 us
  waiting for transfers between devices: 12.3 us -> 13.1 us
    ppermute x14, starting transfers between devices: 3.5 us -> 2.67 us  [across(): lax.ppermute(value, 'col', [(i, (i + 1) % col_devices) for i in range(col...]
  transfers between devices with their start and end apart: 30 -> 30, of which waited for: 13 -> 14; matrix products, arithmetic and copies ran while one was open for 0% -> 0% of each run, Pallas kernels for 13% -> 13%
where the time goes in v17:
time: 60 us; the launch traced here: 59.8 us
  starting transfers between devices  28 us (47%)
  Pallas kernels  16.5 us (28%)
  waiting for transfers between devices  13.1 us (22%)
  between operations  1.43 us (2%)
  other arithmetic  0.85 us (1%)
    ppermute x12, starting transfers between devices, exchange(): fetched.append(lax.ppermute(value, ('row', 'col'), pairs))  18.1 us
    ppermute x12, waiting for transfers between devices, exchange(): fetched.append(lax.ppermute(value, ('row', 'col'), pairs))  7.74 us
    ppermute x4, starting transfers between devices, swap(): return lax.ppermute(value, 'row', [(i, i ^ mask) for i in range(pieces)])  7.2 us
    pallas_call x2, Pallas kernels, per_device(): pl.pallas_call(functools.partial(step_kernel, len(found), places, not fir...  5.85 us
    ppermute x14, waiting for transfers between devices, across(): lax.ppermute(value, 'col', [(i, (i + 1) % col_devices) for i in range(col...  3.56 us
    pallas_call x1, Pallas kernels, per_device(): pl.pallas_call(functools.partial(dense_kernel, rows_dev), out_shape=(matr...  3.02 us
    ppermute x14, starting transfers between devices, across(): lax.ppermute(value, 'col', [(i, (i + 1) % col_devices) for i in range(col...  2.67 us
    pallas_call x1, Pallas kernels, per_device(): pl.pallas_call(functools.partial(gather_kernel, rows_dev), out_shape=(tot...  2.12 us
  transfers between devices with their start and end apart: 30, of which 14 were waited for; matrix products, arithmetic and copies ran while one was open for 0% of the time, Pallas kernels for 13%

profile of v17, /device:TPU:0, one launch (start us, length us, event | category | flops | bytes accessed | tf_op | source)
XLA Modules:
  0.0 59.8 jit_solution(13906711138103559940)
XLA Ops:
  0.6 0.8 %multiply_multiply_fusion.refs_3_ = f32[32,256]{1,0:T(8,128)S(1)} fusion(s32[32,256]{1,0:T(8,128)} %param.11, f32[32]{0:T(128)} %param.13, f32[256]{0:T(256)} %param.12), kind=kLoop, calls=%fused_computation | loop fusion | flops 24576 | bytes 66688 | tf_op jit(solution)/shard_map/mul | solution.py:451
  1.5 4.0 %collective-permute-start = (f32[32,256]{1,0:T(8,128)S(1)}, f32[32,256]{1,0:T(8,128)S(1)}, u32[]{:S(2)}, u32[]{:S(2)}) collective-permute-start(f32[32,256]{1,0:T(8,128)S(1)} %multiply_multiply_fusion.refs_3_), channel_id=1, source_target_pairs={{0,8},{2,10},{4,12},{6,14},{8,0},{10,2},{12,4},{14,6},{1,9},{3,11}... | collective-permute-start | bytes 98312 | tf_op jit(solution)/shard_map/ppermute | solution.py:422
  5.5 1.3 %collective-permute-start.1 = (f32[32,256]{1,0:T(8,128)S(1)}, f32[32,256]{1,0:T(8,128)S(1)}, u32[]{:S(2)}, u32[]{:S(2)}) collective-permute-start(f32[32,256]{1,0:T(8,128)S(1)} %multiply_multiply_fusion.refs_3_), channel_id=1, source_target_pairs={{0,12},{2,14},{4,8},{6,10},{8,4},{10,6},{12,0},{14,2},{1,13},{3,15... | collective-permute-start | bytes 98312 | tf_op jit(solution)/shard_map/ppermute | solution.py:422
  6.9 0.2 collective-permute-start.2
  7.8 2.1 %gather.1 = (f32[64,128,128]{2,1,0:T(8,128)S(1)}, bf16[82,128,128]{2,1,0:T(8,128)(2,1)S(1)}) custom-call(s32[1]{0:T(128)S(6)} %copy.11.count_ref, s32[130]{0:T(256)} %rows_hbm.3, s32[130]{0:T(256)} %cols_hbm.3, bf16[130,128,128]{2,1,0:T(8,128)(2,1)} %tiles_ref.1), custom_call_target="tpu_custom_call" | custom-call | flops 8519680 | bytes 8519680 | tf_op jit(solution)/shard_map/gather/pallas_call | solution.py:464
  9.9 0.0 collective-permute-done.refs_0_
  9.9 1.3 %collective-permute-done.1.refs_1_ = f32[32,256]{1,0:T(8,128)S(1)} collective-permute-done((f32[32,256]{1,0:T(8,128)S(1)}, f32[32,256]{1,0:T(8,128)S(1)}, u32[]{:S(2)}, u32[]{:S(2)}) %collective-permute-start.1) | collective-permute-done | bytes 32800 | tf_op jit(solution)/shard_map/ppermute | solution.py:422
  11.2 0.0 collective-permute-done.2.refs_2_
  11.2 1.6 %collective-permute-start.3 = (f32[4,32,256]{2,1,0:T(8,128)S(1)}, f32[4,32,256]{2,1,0:T(8,128)S(1)}, u32[]{:S(2)}, u32[]{:S(2)}) collective-permute-start(f32[4,32,256]{2,1,0:T(8,128)S(1)} %join.1.joined_ref.even_ref.near_ref), channel_id=1, source_target_pairs={{0,2},{2,0},{4,6},{6,4},{8,10},{10,8},{12,14},{14,12},{1,3},{3,1},... | collective-permute-start | bytes 393224 | tf_op jit(solution)/shard_map/ppermute | solution.py:422
  12.8 0.0 collective-permute-start.5
  12.8 3.0 %dense.1 = (bf16[2,2048,512]{2,1,0:T(8,128)(2,1)S(1)}, f32[64,128,128]{2,1,0:T(8,128)S(1)}) custom-call(s32[1]{0:T(128)S(6)} %copy.11.count_ref, s32[130]{0:T(256)} %rows_hbm.3, s32[130]{0:T(256)} %cols_hbm.3, bf16[82,128,128]{2,1,0:T(8,128)(2,1)S(1)} %get-tuple-element.24.rest, ...), custom_call_target="tpu_custom_call", output_to_operand_aliasing={{1}: (4, {})} | custom-call | flops 8519680 | bytes 8519680 | tf_op jit(solution)/shard_map/dense/pallas_call | solution.py:491
  15.9 0.4 collective-permute-done.3.odd_ref
  16.3 0.9 %first.1 = (f32[32,640]{1,0:T(8,128)S(1)}, f32[4,32,256]{2,1,0:T(8,128)S(1)}) custom-call(f32[4,32,256]{2,1,0:T(8,128)S(1)} %join.1.joined_ref.even_ref.near_ref, f32[4,32,256]{2,1,0:T(8,128)S(1)} %collective-permute-done.3.odd_ref, bf16[2,2048,512]{2,1,0:T(8,128)(2,1)S(1)} %get-tuple-element.25.matrix.refs_12_), custom_call_target="tpu_custom_call" | custom-call | tf_op jit(solution)/shard_map/first/pallas_call | solution.py:510
  17.2 0.1 collective-permute-start.4
  17.3 0.0 collective-permute-done.5.far_ref.far_even_ref
  17.3 1.2 %collective-permute-done.4.other_ref = f32[32,640]{1,0:T(8,128)S(1)} collective-permute-done((f32[32,640]{1,0:T(8,128)S(1)}, f32[32,640]{1,0:T(8,128)S(1)}, u32[]{:S(2)}, u32[]{:S(2)}) %collective-permute-start.4) | collective-permute-done | bytes 81952 | tf_op jit(solution)/shard_map/ppermute | solution.py:425
  18.5 0.3 image.2
  18.8 3.1 %collective-permute-start.6 = (f32[136,128]{1,0:T(8,128)S(1)}, f32[136,128]{1,0:T(8,128)S(1)}, u32[]{:S(2)}, u32[]{:S(2)}) collective-permute-start(f32[136,128]{1,0:T(8,128)S(1)} %get-tuple-element.27.refs_0_), channel_id=1, source_target_pairs={{0,14},{2,12},{4,10},{6,8},{8,6},{10,4},{12,2},{14,0},{1,11},{3,9}... | collective-permute-start | bytes 208904 | tf_op jit(solution)/shard_map/ppermute | solution.py:442
  22.0 1.8 %collective-permute-start.8 = (f32[136,128]{1,0:T(8,128)S(1)}, f32[136,128]{1,0:T(8,128)S(1)}, u32[]{:S(2)}, u32[]{:S(2)}) collective-permute-start(f32[136,128]{1,0:T(8,128)S(1)} %get-tuple-element.27.refs_0_), channel_id=1, source_target_pairs={{0,4},{2,6},{4,0},{6,2},{8,12},{10,14},{12,8},{14,10},{1,9},{3,11}... | collective-permute-start | bytes 208904 | tf_op jit(solution)/shard_map/ppermute | solution.py:442
  23.8 0.0 collective-permute-start.13
  23.8 1.7 %collective-permute-start.9 = (f32[136,128]{1,0:T(8,128)S(1)}, f32[136,128]{1,0:T(8,128)S(1)}, u32[]{:S(2)}, u32[]{:S(2)}) collective-permute-start(f32[136,128]{1,0:T(8,128)S(1)} %get-tuple-element.27.refs_0_), channel_id=1, source_target_pairs={{0,2},{2,0},{4,6},{6,4},{8,10},{10,8},{12,14},{14,12},{1,3},{3,1},... | collective-permute-start | bytes 208904 | tf_op jit(solution)/shard_map/ppermute | solution.py:442
  25.5 0.8 %collective-permute-done.6.refs_1_ = f32[136,128]{1,0:T(8,128)S(1)} collective-permute-done((f32[136,128]{1,0:T(8,128)S(1)}, f32[136,128]{1,0:T(8,128)S(1)}, u32[]{:S(2)}, u32[]{:S(2)}) %collective-permute-start.6) | collective-permute-done | bytes 69664 | tf_op jit(solution)/shard_map/ppermute | solution.py:442
  26.2 0.4 collective-permute-start.10
  26.6 1.2 %collective-permute-done.7.refs_2_ = f32[136,128]{1,0:T(8,128)S(1)} collective-permute-done((f32[136,128]{1,0:T(8,128)S(1)}, f32[136,128]{1,0:T(8,128)S(1)}, u32[]{:S(2)}, u32[]{:S(2)}) %collective-permute-start.7) | collective-permute-done | bytes 69664 | tf_op jit(solution)/shard_map/ppermute | solution.py:442
  27.8 0.7 %collective-permute-done.8.refs_3_ = f32[136,128]{1,0:T(8,128)S(1)} collective-permute-done((f32[136,128]{1,0:T(8,128)S(1)}, f32[136,128]{1,0:T(8,128)S(1)}, u32[]{:S(2)}, u32[]{:S(2)}) %collective-permute-start.8) | collective-permute-done | bytes 69664 | tf_op jit(solution)/shard_map/ppermute | solution.py:442
  28.5 0.6 %collective-permute-start.12 = (f32[136,128]{1,0:T(8,128)S(1)}, f32[136,128]{1,0:T(8,128)S(1)}, u32[]{:S(2)}, u32[]{:S(2)}) collective-permute-start(f32[136,128]{1,0:T(8,128)S(1)} %collective-permute-done.8.refs_3_), channel_id=1, source_target_pairs={{0,1},{1,0},{2,3},{3,2},{4,5},{5,4},{6,7},{7,6},{8,9},{9,8},{10,11... | collective-permute-start | bytes 208904 | tf_op jit(solution)/shard_map/ppermute | solution.py:425
  29.1 0.9 %inverse.2.refs_11_ = f32[32,128]{1,0:T(8,128)S(1)} custom-call(f32[32,128]{1,0:T(8,128)S(1)} %get-tuple-element.31.norm_ref.refs_10_), custom_call_target="tpu_custom_call" | custom-call | tf_op jit(solution)/shard_map/inverse/pallas_call | solution.py:545
  30.0 0.0 collective-permute-done.13.far_odd_ref
  30.0 0.1 collect.1
  30.1 0.0 collective-permute-done.10.refs_5_
  30.1 0.0 collective-permute-done.11.refs_6_
  30.1 2.9 %step.2 = (f32[32,512]{1,0:T(8,128)S(1)}, f32[9,32,256]{2,1,0:T(8,128)S(1)}, f32[2,8,32,256]{3,2,1,0:T(8,128)S(1)}, f32[32,128]{1,0:T(8,128)S(1)}, f32[32,256]{1,0:T(8,128)S(1)}) custom-call(f32[136,128]{1,0:T(8,128)S(1)} %get-tuple-element.27.refs_0_, f32[136,128]{1,0:T(8,128)S(1)} %collective-permute-done.6.refs_1_, ...), custom_call_target="tpu_custom_call" | custom-call | tf_op jit(solution)/shard_map/step/pallas_call | solution.py:554
  33.1 0.2 collective-permute-start.14
  33.3 1.0 %collective-permute-done.14.other_ref = f32[32,512]{1,0:T(8,128)S(1)} collective-permute-done((f32[32,512]{1,0:T(8,128)S(1)}, f32[32,512]{1,0:T(8,128)S(1)}, u32[]{:S(2)}, u32[]{:S(2)}) %collective-permute-start.14) | collective-permute-done | bytes 65568 | tf_op jit(solution)/shard_map/ppermute | solution.py:425
  34.3 0.3 image.3.refs_0_
  34.7 2.4 %collective-permute-start.15 = (f32[136,128]{1,0:T(8,128)S(1)}, f32[136,128]{1,0:T(8,128)S(1)}, u32[]{:S(2)}, u32[]{:S(2)}) collective-permute-start(f32[136,128]{1,0:T(8,128)S(1)} %image.3.refs_0_), channel_id=1, source_target_pairs={{0,14},{2,12},{4,10},{6,8},{8,6},{10,4},{12,2},{14,0},{1,11},{3,9}... | collective-permute-start | bytes 208904 | tf_op jit(solution)/shard_map/ppermute | solution.py:442
  37.1 0.2 collective-permute-start.16
  37.3 2.8 %collective-permute-start.17 = (f32[136,128]{1,0:T(8,128)S(1)}, f32[136,128]{1,0:T(8,128)S(1)}, u32[]{:S(2)}, u32[]{:S(2)}) collective-permute-start(f32[136,128]{1,0:T(8,128)S(1)} %image.3.refs_0_), channel_id=1, source_target_pairs={{0,4},{2,6},{4,0},{6,2},{8,12},{10,14},{12,8},{14,10},{1,9},{3,11}... | collective-permute-start | bytes 208904 | tf_op jit(solution)/shard_map/ppermute | solution.py:442
  40.1 0.5 collective-permute-start.18
  40.6 1.8 %collective-permute-done.15.refs_1_ = f32[136,128]{1,0:T(8,128)S(1)} collective-permute-done((f32[136,128]{1,0:T(8,128)S(1)}, f32[136,128]{1,0:T(8,128)S(1)}, u32[]{:S(2)}, u32[]{:S(2)}) %collective-permute-start.15) | collective-permute-done | bytes 69664 | tf_op jit(solution)/shard_map/ppermute | solution.py:442
  42.4 0.1 collective-permute-start.19
  42.5 0.9 %collective-permute-done.16.refs_2_ = f32[136,128]{1,0:T(8,128)S(1)} collective-permute-done((f32[136,128]{1,0:T(8,128)S(1)}, f32[136,128]{1,0:T(8,128)S(1)}, u32[]{:S(2)}, u32[]{:S(2)}) %collective-permute-start.16) | collective-permute-done | bytes 69664 | tf_op jit(solution)/shard_map/ppermute | solution.py:442
  43.4 0.0 collective-permute-start.20
  43.4 0.9 %collective-permute-done.17.refs_3_ = f32[136,128]{1,0:T(8,128)S(1)} collective-permute-done((f32[136,128]{1,0:T(8,128)S(1)}, f32[136,128]{1,0:T(8,128)S(1)}, u32[]{:S(2)}, u32[]{:S(2)}) %collective-permute-start.17) | collective-permute-done | bytes 69664 | tf_op jit(solution)/shard_map/ppermute | solution.py:442
  44.2 0.9 %inverse.3.refs_11_ = f32[32,128]{1,0:T(8,128)S(1)} custom-call(f32[32,128]{1,0:T(8,128)S(1)} %get-tuple-element.35.norm_ref.refs_10_), custom_call_target="tpu_custom_call" | custom-call | tf_op jit(solution)/shard_map/inverse/pallas_call | solution.py:545
  45.2 0.0 collective-permute-done.18.refs_4_
  45.2 0.0 collective-permute-done.20.refs_6_
  45.2 0.3 collective-permute-done.21.refs_7_
  45.5 2.9 %step.3 = (f32[32,512]{1,0:T(8,128)S(1)}, f32[2,32,256]{2,1,0:T(8,128)S(1)}, f32[32,256]{1,0:T(8,128)S(1)}, f32[32,128]{1,0:T(8,128)S(1)}, f32[32,256]{1,0:T(8,128)S(1)}) custom-call(f32[136,128]{1,0:T(8,128)S(1)} %image.3.refs_0_, f32[136,128]{1,0:T(8,128)S(1)} %collective-permute-done.15.refs_1_, f32[136,128]{1,0:T(8,128)S(1)} %collective-permute-done.16.refs_2_, ...), custom_call_target="tpu_custom_call" | custom-call | tf_op jit(solution)/shard_map/step/pallas_call | solution.py:554
  48.4 0.2 collective-permute-start.22
  48.7 1.0 %collective-permute-done.22.other_ref = f32[32,512]{1,0:T(8,128)S(1)} collective-permute-done((f32[32,512]{1,0:T(8,128)S(1)}, f32[32,512]{1,0:T(8,128)S(1)}, u32[]{:S(2)}, u32[]{:S(2)}) %collective-permute-start.22) | collective-permute-done | bytes 65568 | tf_op jit(solution)/shard_map/ppermute | solution.py:425
  49.7 0.3 last_image.1
  50.0 2.1 %collective-permute-start.23 = (f32[8,128]{1,0:T(8,128)S(1)}, f32[8,128]{1,0:T(8,128)S(1)}, u32[]{:S(2)}, u32[]{:S(2)}) collective-permute-start(f32[8,128]{1,0:T(8,128)S(1)} %get-tuple-element.39.refs_0_), channel_id=1, source_target_pairs={{0,12},{2,14},{4,8},{6,10},{8,4},{10,6},{12,0},{14,2},{1,15},{3,13... | collective-permute-start | bytes 12296 | tf_op jit(solution)/shard_map/ppermute | solution.py:442
  52.1 0.2 collective-permute-start.24
  52.3 2.2 %collective-permute-start.25 = (f32[8,128]{1,0:T(8,128)S(1)}, f32[8,128]{1,0:T(8,128)S(1)}, u32[]{:S(2)}, u32[]{:S(2)}) collective-permute-start(f32[8,128]{1,0:T(8,128)S(1)} %get-tuple-element.39.refs_0_), channel_id=1, source_target_pairs={{0,4},{2,6},{4,0},{6,2},{8,12},{10,14},{12,8},{14,10},{1,9},{3,11}... | collective-permute-start | bytes 12296 | tf_op jit(solution)/shard_map/ppermute | solution.py:442
  54.5 1.1 %collective-permute-start.26 = (f32[8,128]{1,0:T(8,128)S(1)}, f32[8,128]{1,0:T(8,128)S(1)}, u32[]{:S(2)}, u32[]{:S(2)}) collective-permute-start(f32[8,128]{1,0:T(8,128)S(1)} %get-tuple-element.39.refs_0_), channel_id=1, source_target_pairs={{0,2},{2,0},{4,6},{6,4},{8,10},{10,8},{12,14},{14,12},{1,3},{3,1},... | collective-permute-start | bytes 12296 | tf_op jit(solution)/shard_map/ppermute | solution.py:442
  55.6 0.4 collective-permute-start.27
  56.0 0.6 collective-permute-done.24.refs_2_
  56.6 0.1 collective-permute-start.28
  56.8 0.0 collective-permute-done.25.refs_3_
  56.8 0.4 collective-permute-start.29
  57.1 1.0 %collective-permute-done.26.refs_4_ = f32[8,128]{1,0:T(8,128)S(1)} collective-permute-done((f32[8,128]{1,0:T(8,128)S(1)}, f32[8,128]{1,0:T(8,128)S(1)}, u32[]{:S(2)}, u32[]{:S(2)}) %collective-permute-start.26) | collective-permute-done | bytes 4128 | tf_op jit(solution)/shard_map/ppermute | solution.py:442
  58.1 0.0 collective-permute-done.27.refs_5_
  58.1 1.7 %last.1 = (f32[32,256]{1,0:T(8,128)}, f32[32,256]{1,0:T(8,128)}) custom-call(f32[8,128]{1,0:T(8,128)S(1)} %get-tuple-element.39.refs_0_, f32[8,128]{1,0:T(8,128)S(1)} %collective-permute-done.23.refs_1_, f32[8,128]{1,0:T(8,128)S(1)} %collective-permute-done.24.refs_2_, f32[8,128]{1,0:T(8,128)S(1)} %collective-permute-done.25.refs_3_, ...), custom_call_target="tpu_custom_call" | custom-call | tf_op jit(solution)/shard_map/last/pallas_call | solution.py:577
  (10 shorter events, 0.0 us)
Async XLA Ops:
  1.5 8.4 %collective-permute-start = (f32[32,256]{1,0:T(8,128)S(1)}, f32[32,256]{1,0:T(8,128)S(1)}, u32[]{:S(2)}, u32[]{:S(2)}) collective-permute-start(f32[32,256]{1,0:T(8,128)S(1)} %multiply_multiply_fusion.refs_3_), channel_id=1, source_target_pairs={{0,8},{2,10},{4,12},{6,14},{8,0},{10,2},{12,4},{14,6},{1,9},{3,11}... | collective-permute-start | bytes 98312 | tf_op jit(solution)/shard_map/ppermute | solution.py:422
  5.5 5.7 %collective-permute-start.1 = (f32[32,256]{1,0:T(8,128)S(1)}, f32[32,256]{1,0:T(8,128)S(1)}, u32[]{:S(2)}, u32[]{:S(2)}) collective-permute-start(f32[32,256]{1,0:T(8,128)S(1)} %multiply_multiply_fusion.refs_3_), channel_id=1, source_target_pairs={{0,12},{2,14},{4,8},{6,10},{8,4},{10,6},{12,0},{14,2},{1,13},{3,15... | collective-permute-start | bytes 98312 | tf_op jit(solution)/shard_map/ppermute | solution.py:422
  6.9 4.4 %collective-permute-start.2 = (f32[32,256]{1,0:T(8,128)S(1)}, f32[32,256]{1,0:T(8,128)S(1)}, u32[]{:S(2)}, u32[]{:S(2)}) collective-permute-start(f32[32,256]{1,0:T(8,128)S(1)} %multiply_multiply_fusion.refs_3_), channel_id=1, source_target_pairs={{0,4},{2,6},{4,0},{6,2},{8,12},{10,14},{12,8},{14,10},{1,5},{3,7},... | collective-permute-start | bytes 98312 | tf_op jit(solution)/shard_map/ppermute | solution.py:422
  11.2 5.0 %collective-permute-start.3 = (f32[4,32,256]{2,1,0:T(8,128)S(1)}, f32[4,32,256]{2,1,0:T(8,128)S(1)}, u32[]{:S(2)}, u32[]{:S(2)}) collective-permute-start(f32[4,32,256]{2,1,0:T(8,128)S(1)} %join.1.joined_ref.even_ref.near_ref), channel_id=1, source_target_pairs={{0,2},{2,0},{4,6},{6,4},{8,10},{10,8},{12,14},{14,12},{1,3},{3,1},... | collective-permute-start | bytes 393224 | tf_op jit(solution)/shard_map/ppermute | solution.py:422
  12.8 4.5 %collective-permute-start.5 = (f32[4,32,256]{2,1,0:T(8,128)S(1)}, f32[4,32,256]{2,1,0:T(8,128)S(1)}, u32[]{:S(2)}, u32[]{:S(2)}) collective-permute-start(f32[4,32,256]{2,1,0:T(8,128)S(1)} %join.1.joined_ref.even_ref.near_ref), channel_id=1, source_target_pairs={{0,1},{1,0},{2,3},{3,2},{4,5},{5,4},{6,7},{7,6},{8,9},{9,8},{10,11... | collective-permute-start | bytes 393224 | tf_op jit(solution)/shard_map/ppermute | solution.py:425
  17.2 1.3 %collective-permute-start.4 = (f32[32,640]{1,0:T(8,128)S(1)}, f32[32,640]{1,0:T(8,128)S(1)}, u32[]{:S(2)}, u32[]{:S(2)}) collective-permute-start(f32[32,640]{1,0:T(8,128)S(1)} %get-tuple-element.26.mine_ref), channel_id=1, source_target_pairs={{0,1},{1,0},{2,3},{3,2},{4,5},{5,4},{6,7},{7,6},{8,9},{9,8},{10,11... | collective-permute-start | bytes 245768 | tf_op jit(solution)/shard_map/ppermute | solution.py:425
  18.8 7.4 %collective-permute-start.6 = (f32[136,128]{1,0:T(8,128)S(1)}, f32[136,128]{1,0:T(8,128)S(1)}, u32[]{:S(2)}, u32[]{:S(2)}) collective-permute-start(f32[136,128]{1,0:T(8,128)S(1)} %get-tuple-element.27.refs_0_), channel_id=1, source_target_pairs={{0,14},{2,12},{4,10},{6,8},{8,6},{10,4},{12,2},{14,0},{1,11},{3,9}... | collective-permute-start | bytes 208904 | tf_op jit(solution)/shard_map/ppermute | solution.py:442
  22.0 5.8 %collective-permute-start.7 = (f32[136,128]{1,0:T(8,128)S(1)}, f32[136,128]{1,0:T(8,128)S(1)}, u32[]{:S(2)}, u32[]{:S(2)}) collective-permute-start(f32[136,128]{1,0:T(8,128)S(1)} %get-tuple-element.27.refs_0_), channel_id=1, source_target_pairs={{0,6},{2,4},{4,2},{6,0},{8,14},{10,12},{12,10},{14,8},{1,13},{3,15... | collective-permute-start | bytes 208904 | tf_op jit(solution)/shard_map/ppermute | solution.py:442
  22.0 6.5 %collective-permute-start.8 = (f32[136,128]{1,0:T(8,128)S(1)}, f32[136,128]{1,0:T(8,128)S(1)}, u32[]{:S(2)}, u32[]{:S(2)}) collective-permute-start(f32[136,128]{1,0:T(8,128)S(1)} %get-tuple-element.27.refs_0_), channel_id=1, source_target_pairs={{0,4},{2,6},{4,0},{6,2},{8,12},{10,14},{12,8},{14,10},{1,9},{3,11}... | collective-permute-start | bytes 208904 | tf_op jit(solution)/shard_map/ppermute | solution.py:442
  23.8 6.2 %collective-permute-start.13 = (f32[4,32,256]{2,1,0:T(8,128)S(1)}, f32[4,32,256]{2,1,0:T(8,128)S(1)}, u32[]{:S(2)}, u32[]{:S(2)}) collective-permute-start(f32[4,32,256]{2,1,0:T(8,128)S(1)} %get-tuple-element.28.odd_ref), channel_id=1, source_target_pairs={{0,1},{1,0},{2,3},{3,2},{4,5},{5,4},{6,7},{7,6},{8,9},{9,8},{10,11... | collective-permute-start | bytes 393224 | tf_op jit(solution)/shard_map/ppermute | solution.py:425
  23.8 6.3 %collective-permute-start.9 = (f32[136,128]{1,0:T(8,128)S(1)}, f32[136,128]{1,0:T(8,128)S(1)}, u32[]{:S(2)}, u32[]{:S(2)}) collective-permute-start(f32[136,128]{1,0:T(8,128)S(1)} %get-tuple-element.27.refs_0_), channel_id=1, source_target_pairs={{0,2},{2,0},{4,6},{6,4},{8,10},{10,8},{12,14},{14,12},{1,3},{3,1},... | collective-permute-start | bytes 208904 | tf_op jit(solution)/shard_map/ppermute | solution.py:442
  26.2 3.9 %collective-permute-start.10 = (f32[136,128]{1,0:T(8,128)S(1)}, f32[136,128]{1,0:T(8,128)S(1)}, u32[]{:S(2)}, u32[]{:S(2)}) collective-permute-start(f32[136,128]{1,0:T(8,128)S(1)} %collective-permute-done.6.refs_1_), channel_id=1, source_target_pairs={{0,1},{1,0},{2,3},{3,2},{4,5},{5,4},{6,7},{7,6},{8,9},{9,8},{10,11... | collective-permute-start | bytes 208904 | tf_op jit(solution)/shard_map/ppermute | solution.py:425
  27.8 2.3 %collective-permute-start.11 = (f32[136,128]{1,0:T(8,128)S(1)}, f32[136,128]{1,0:T(8,128)S(1)}, u32[]{:S(2)}, u32[]{:S(2)}) collective-permute-start(f32[136,128]{1,0:T(8,128)S(1)} %collective-permute-done.7.refs_2_), channel_id=1, source_target_pairs={{0,1},{1,0},{2,3},{3,2},{4,5},{5,4},{6,7},{7,6},{8,9},{9,8},{10,11... | collective-permute-start | bytes 208904 | tf_op jit(solution)/shard_map/ppermute | solution.py:425
  28.5 1.6 %collective-permute-start.12 = (f32[136,128]{1,0:T(8,128)S(1)}, f32[136,128]{1,0:T(8,128)S(1)}, u32[]{:S(2)}, u32[]{:S(2)}) collective-permute-start(f32[136,128]{1,0:T(8,128)S(1)} %collective-permute-done.8.refs_3_), channel_id=1, source_target_pairs={{0,1},{1,0},{2,3},{3,2},{4,5},{5,4},{6,7},{7,6},{8,9},{9,8},{10,11... | collective-permute-start | bytes 208904 | tf_op jit(solution)/shard_map/ppermute | solution.py:425
  33.1 1.3 %collective-permute-start.14 = (f32[32,512]{1,0:T(8,128)S(1)}, f32[32,512]{1,0:T(8,128)S(1)}, u32[]{:S(2)}, u32[]{:S(2)}) collective-permute-start(f32[32,512]{1,0:T(8,128)S(1)} %get-tuple-element.32.mine_ref), channel_id=1, source_target_pairs={{0,1},{1,0},{2,3},{3,2},{4,5},{5,4},{6,7},{7,6},{8,9},{9,8},{10,11... | collective-permute-start | bytes 196616 | tf_op jit(solution)/shard_map/ppermute | solution.py:425
  34.7 7.7 %collective-permute-start.15 = (f32[136,128]{1,0:T(8,128)S(1)}, f32[136,128]{1,0:T(8,128)S(1)}, u32[]{:S(2)}, u32[]{:S(2)}) collective-permute-start(f32[136,128]{1,0:T(8,128)S(1)} %image.3.refs_0_), channel_id=1, source_target_pairs={{0,14},{2,12},{4,10},{6,8},{8,6},{10,4},{12,2},{14,0},{1,11},{3,9}... | collective-permute-start | bytes 208904 | tf_op jit(solution)/shard_map/ppermute | solution.py:442
  37.1 6.3 %collective-permute-start.16 = (f32[136,128]{1,0:T(8,128)S(1)}, f32[136,128]{1,0:T(8,128)S(1)}, u32[]{:S(2)}, u32[]{:S(2)}) collective-permute-start(f32[136,128]{1,0:T(8,128)S(1)} %image.3.refs_0_), channel_id=1, source_target_pairs={{0,6},{2,4},{4,2},{6,0},{8,14},{10,12},{12,10},{14,8},{1,13},{3,15... | collective-permute-start | bytes 208904 | tf_op jit(solution)/shard_map/ppermute | solution.py:442
  37.3 7.0 %collective-permute-start.17 = (f32[136,128]{1,0:T(8,128)S(1)}, f32[136,128]{1,0:T(8,128)S(1)}, u32[]{:S(2)}, u32[]{:S(2)}) collective-permute-start(f32[136,128]{1,0:T(8,128)S(1)} %image.3.refs_0_), channel_id=1, source_target_pairs={{0,4},{2,6},{4,0},{6,2},{8,12},{10,14},{12,8},{14,10},{1,9},{3,11}... | collective-permute-start | bytes 208904 | tf_op jit(solution)/shard_map/ppermute | solution.py:442
  40.1 5.1 %collective-permute-start.18 = (f32[136,128]{1,0:T(8,128)S(1)}, f32[136,128]{1,0:T(8,128)S(1)}, u32[]{:S(2)}, u32[]{:S(2)}) collective-permute-start(f32[136,128]{1,0:T(8,128)S(1)} %image.3.refs_0_), channel_id=1, source_target_pairs={{0,2},{2,0},{4,6},{6,4},{8,10},{10,8},{12,14},{14,12},{1,3},{3,1},... | collective-permute-start | bytes 208904 | tf_op jit(solution)/shard_map/ppermute | solution.py:442
  42.4 2.8 %collective-permute-start.19 = (f32[136,128]{1,0:T(8,128)S(1)}, f32[136,128]{1,0:T(8,128)S(1)}, u32[]{:S(2)}, u32[]{:S(2)}) collective-permute-start(f32[136,128]{1,0:T(8,128)S(1)} %collective-permute-done.15.refs_1_), channel_id=1, source_target_pairs={{0,1},{1,0},{2,3},{3,2},{4,5},{5,4},{6,7},{7,6},{8,9},{9,8},{10,11... | collective-permute-start | bytes 208904 | tf_op jit(solution)/shard_map/ppermute | solution.py:425
  43.4 1.8 %collective-permute-start.20 = (f32[136,128]{1,0:T(8,128)S(1)}, f32[136,128]{1,0:T(8,128)S(1)}, u32[]{:S(2)}, u32[]{:S(2)}) collective-permute-start(f32[136,128]{1,0:T(8,128)S(1)} %collective-permute-done.16.refs_2_), channel_id=1, source_target_pairs={{0,1},{1,0},{2,3},{3,2},{4,5},{5,4},{6,7},{7,6},{8,9},{9,8},{10,11... | collective-permute-start | bytes 208904 | tf_op jit(solution)/shard_map/ppermute | solution.py:425
  44.2 1.3 %collective-permute-start.21 = (f32[136,128]{1,0:T(8,128)S(1)}, f32[136,128]{1,0:T(8,128)S(1)}, u32[]{:S(2)}, u32[]{:S(2)}) collective-permute-start(f32[136,128]{1,0:T(8,128)S(1)} %collective-permute-done.17.refs_3_), channel_id=1, source_target_pairs={{0,1},{1,0},{2,3},{3,2},{4,5},{5,4},{6,7},{7,6},{8,9},{9,8},{10,11... | collective-permute-start | bytes 208904 | tf_op jit(solution)/shard_map/ppermute | solution.py:425
  48.4 1.3 %collective-permute-start.22 = (f32[32,512]{1,0:T(8,128)S(1)}, f32[32,512]{1,0:T(8,128)S(1)}, u32[]{:S(2)}, u32[]{:S(2)}) collective-permute-start(f32[32,512]{1,0:T(8,128)S(1)} %get-tuple-element.37.mine_ref), channel_id=1, source_target_pairs={{0,1},{1,0},{2,3},{3,2},{4,5},{5,4},{6,7},{7,6},{8,9},{9,8},{10,11... | collective-permute-start | bytes 196616 | tf_op jit(solution)/shard_map/ppermute | solution.py:425
  50.0 5.6 %collective-permute-start.23 = (f32[8,128]{1,0:T(8,128)S(1)}, f32[8,128]{1,0:T(8,128)S(1)}, u32[]{:S(2)}, u32[]{:S(2)}) collective-permute-start(f32[8,128]{1,0:T(8,128)S(1)} %get-tuple-element.39.refs_0_), channel_id=1, source_target_pairs={{0,12},{2,14},{4,8},{6,10},{8,4},{10,6},{12,0},{14,2},{1,15},{3,13... | collective-permute-start | bytes 12296 | tf_op jit(solution)/shard_map/ppermute | solution.py:442
  52.1 4.5 %collective-permute-start.24 = (f32[8,128]{1,0:T(8,128)S(1)}, f32[8,128]{1,0:T(8,128)S(1)}, u32[]{:S(2)}, u32[]{:S(2)}) collective-permute-start(f32[8,128]{1,0:T(8,128)S(1)} %get-tuple-element.39.refs_0_), channel_id=1, source_target_pairs={{0,6},{2,4},{4,2},{6,0},{8,14},{10,12},{12,10},{14,8},{1,11},{3,9}... | collective-permute-start | bytes 12296 | tf_op jit(solution)/shard_map/ppermute | solution.py:442
  52.3 4.4 %collective-permute-start.25 = (f32[8,128]{1,0:T(8,128)S(1)}, f32[8,128]{1,0:T(8,128)S(1)}, u32[]{:S(2)}, u32[]{:S(2)}) collective-permute-start(f32[8,128]{1,0:T(8,128)S(1)} %get-tuple-element.39.refs_0_), channel_id=1, source_target_pairs={{0,4},{2,6},{4,0},{6,2},{8,12},{10,14},{12,8},{14,10},{1,9},{3,11}... | collective-permute-start | bytes 12296 | tf_op jit(solution)/shard_map/ppermute | solution.py:442
  54.5 3.6 %collective-permute-start.26 = (f32[8,128]{1,0:T(8,128)S(1)}, f32[8,128]{1,0:T(8,128)S(1)}, u32[]{:S(2)}, u32[]{:S(2)}) collective-permute-start(f32[8,128]{1,0:T(8,128)S(1)} %get-tuple-element.39.refs_0_), channel_id=1, source_target_pairs={{0,2},{2,0},{4,6},{6,4},{8,10},{10,8},{12,14},{14,12},{1,3},{3,1},... | collective-permute-start | bytes 12296 | tf_op jit(solution)/shard_map/ppermute | solution.py:442
  55.6 2.5 %collective-permute-start.27 = (f32[8,128]{1,0:T(8,128)S(1)}, f32[8,128]{1,0:T(8,128)S(1)}, u32[]{:S(2)}, u32[]{:S(2)}) collective-permute-start(f32[8,128]{1,0:T(8,128)S(1)} %collective-permute-done.23.refs_1_), channel_id=1, source_target_pairs={{0,1},{1,0},{2,3},{3,2},{4,5},{5,4},{6,7},{7,6},{8,9},{9,8},{10,11... | collective-permute-start | bytes 12296 | tf_op jit(solution)/shard_map/ppermute | solution.py:425
  56.6 1.5 %collective-permute-start.28 = (f32[8,128]{1,0:T(8,128)S(1)}, f32[8,128]{1,0:T(8,128)S(1)}, u32[]{:S(2)}, u32[]{:S(2)}) collective-permute-start(f32[8,128]{1,0:T(8,128)S(1)} %collective-permute-done.24.refs_2_), channel_id=1, source_target_pairs={{0,1},{1,0},{2,3},{3,2},{4,5},{5,4},{6,7},{7,6},{8,9},{9,8},{10,11... | collective-permute-start | bytes 12296 | tf_op jit(solution)/shard_map/ppermute | solution.py:425
  56.8 1.4 %collective-permute-start.29 = (f32[8,128]{1,0:T(8,128)S(1)}, f32[8,128]{1,0:T(8,128)S(1)}, u32[]{:S(2)}, u32[]{:S(2)}) collective-permute-start(f32[8,128]{1,0:T(8,128)S(1)} %collective-permute-done.25.refs_3_), channel_id=1, source_target_pairs={{0,1},{1,0},{2,3},{3,2},{4,5},{5,4},{6,7},{7,6},{8,9},{9,8},{10,11... | collective-permute-start | bytes 12296 | tf_op jit(solution)/shard_map/ppermute | solution.py:425

commit v18 on v17

--- a/solution.py
+++ b/solution.py
@@ -9,7 +9,7 @@
 
 ITERS = 3
 LANES = 128
-PIVOTS = 8
+PIVOTS = 16
 CHUNKS = 5
 F32 = jnp.float32
 BF16 = jnp.bfloat16

time: 60 us -> 59.5 us (level)
  waiting for transfers between devices: 13.1 us -> 11.2 us
  starting transfers between devices: 28 us -> 29.8 us
    ppermute x14, starting transfers between devices: 2.67 us -> 4.4 us  [across(): lax.ppermute(value, 'col', [(i, (i + 1) % col_devices) for i in range(col...]
    ppermute x12, waiting for transfers between devices: 7.74 us -> 6.89 us  [exchange(): fetched.append(lax.ppermute(value, ('row', 'col'), pairs))]
    ppermute x14, waiting for transfers between devices: 3.56 us -> 2.87 us  [across(): lax.ppermute(value, 'col', [(i, (i + 1) % col_devices) for i in range(col...]
  transfers between devices with their start and end apart: 30 -> 30, of which waited for: 14 -> 13; matrix products, arithmetic and copies ran while one was open for 0% -> 0% of each run, Pallas kernels for 13% -> 13%
where the time goes in v18:
time: 59.5 us; the launch traced here: 59.3 us
  starting transfers between devices  29.8 us (50%)
  Pallas kernels  16.1 us (27%)
  waiting for transfers between devices  11.2 us (19%)
  between operations  1.42 us (2%)
  other arithmetic  0.85 us (1%)
    ppermute x12, starting transfers between devices, exchange(): fetched.append(lax.ppermute(value, ('row', 'col'), pairs))  18.2 us
    ppermute x4, starting transfers between devices, swap(): return lax.ppermute(value, 'row', [(i, i ^ mask) for i in range(pieces)])  7.2 us
    ppermute x12, waiting for transfers between devices, exchange(): fetched.append(lax.ppermute(value, ('row', 'col'), pairs))  6.89 us
    pallas_call x2, Pallas kernels, per_device(): pl.pallas_call(functools.partial(step_kernel, len(found), places, not fir...  5.55 us
    ppermute x14, starting transfers between devices, across(): lax.ppermute(value, 'col', [(i, (i + 1) % col_devices) for i in range(col...  4.4 us
    pallas_call x1, Pallas kernels, per_device(): pl.pallas_call(functools.partial(dense_kernel, rows_dev), out_shape=(matr...  3.33 us
    ppermute x14, waiting for transfers between devices, across(): lax.ppermute(value, 'col', [(i, (i + 1) % col_devices) for i in range(col...  2.87 us
    pallas_call x1, Pallas kernels, per_device(): pl.pallas_call(functools.partial(gather_kernel, rows_dev), out_shape=(tot...  2.12 us
  transfers between devices with their start and end apart: 30, of which 13 were waited for; matrix products, arithmetic and copies ran while one was open for 0% of the time, Pallas kernels for 13%

profile of v18, /device:TPU:0, one launch (start us, length us, event | category | flops | bytes accessed | tf_op | source)
XLA Modules:
  0.0 59.3 jit_solution(16928839992358501978)
XLA Ops:
  0.6 0.8 %multiply_multiply_fusion.refs_3_ = f32[32,256]{1,0:T(8,128)S(1)} fusion(s32[32,256]{1,0:T(8,128)} %param.11, f32[32]{0:T(128)} %param.13, f32[256]{0:T(256)} %param.12), kind=kLoop, calls=%fused_computation | loop fusion | flops 24576 | bytes 66688 | tf_op jit(solution)/shard_map/mul | solution.py:451
  1.5 4.0 %collective-permute-start = (f32[32,256]{1,0:T(8,128)S(1)}, f32[32,256]{1,0:T(8,128)S(1)}, u32[]{:S(2)}, u32[]{:S(2)}) collective-permute-start(f32[32,256]{1,0:T(8,128)S(1)} %multiply_multiply_fusion.refs_3_), channel_id=1, source_target_pairs={{0,8},{2,10},{4,12},{6,14},{8,0},{10,2},{12,4},{14,6},{1,9},{3,11}... | collective-permute-start | bytes 98312 | tf_op jit(solution)/shard_map/ppermute | solution.py:422
  5.5 1.3 %collective-permute-start.1 = (f32[32,256]{1,0:T(8,128)S(1)}, f32[32,256]{1,0:T(8,128)S(1)}, u32[]{:S(2)}, u32[]{:S(2)}) collective-permute-start(f32[32,256]{1,0:T(8,128)S(1)} %multiply_multiply_fusion.refs_3_), channel_id=1, source_target_pairs={{0,12},{2,14},{4,8},{6,10},{8,4},{10,6},{12,0},{14,2},{1,13},{3,15... | collective-permute-start | bytes 98312 | tf_op jit(solution)/shard_map/ppermute | solution.py:422
  6.9 0.2 collective-permute-start.2
  7.8 2.1 %gather.1 = (f32[64,128,128]{2,1,0:T(8,128)S(1)}, bf16[82,128,128]{2,1,0:T(8,128)(2,1)S(1)}) custom-call(s32[1]{0:T(128)S(6)} %copy.11.count_ref, s32[130]{0:T(256)} %rows_hbm.3, s32[130]{0:T(256)} %cols_hbm.3, bf16[130,128,128]{2,1,0:T(8,128)(2,1)} %tiles_ref.1), custom_call_target="tpu_custom_call" | custom-call | flops 8519680 | bytes 8519680 | tf_op jit(solution)/shard_map/gather/pallas_call | solution.py:464
  9.9 0.0 collective-permute-done.refs_0_
  9.9 1.3 %collective-permute-done.1.refs_1_ = f32[32,256]{1,0:T(8,128)S(1)} collective-permute-done((f32[32,256]{1,0:T(8,128)S(1)}, f32[32,256]{1,0:T(8,128)S(1)}, u32[]{:S(2)}, u32[]{:S(2)}) %collective-permute-start.1) | collective-permute-done | bytes 32800 | tf_op jit(solution)/shard_map/ppermute | solution.py:422
  11.2 0.0 collective-permute-done.2.refs_2_
  11.2 1.6 %collective-permute-start.3 = (f32[4,32,256]{2,1,0:T(8,128)S(1)}, f32[4,32,256]{2,1,0:T(8,128)S(1)}, u32[]{:S(2)}, u32[]{:S(2)}) collective-permute-start(f32[4,32,256]{2,1,0:T(8,128)S(1)} %join.1.joined_ref.even_ref.near_ref), channel_id=1, source_target_pairs={{0,2},{2,0},{4,6},{6,4},{8,10},{10,8},{12,14},{14,12},{1,3},{3,1},... | collective-permute-start | bytes 393224 | tf_op jit(solution)/shard_map/ppermute | solution.py:422
  12.8 3.3 %dense.1 = (bf16[2,2048,512]{2,1,0:T(8,128)(2,1)S(1)}, f32[64,128,128]{2,1,0:T(8,128)S(1)}) custom-call(s32[1]{0:T(128)S(6)} %copy.11.count_ref, s32[130]{0:T(256)} %rows_hbm.3, s32[130]{0:T(256)} %cols_hbm.3, bf16[82,128,128]{2,1,0:T(8,128)(2,1)S(1)} %get-tuple-element.24.rest, ...), custom_call_target="tpu_custom_call", output_to_operand_aliasing={{1}: (4, {})} | custom-call | flops 8519680 | bytes 8519680 | tf_op jit(solution)/shard_map/dense/pallas_call | solution.py:491
  16.2 0.1 collective-permute-done.3.odd_ref
  16.3 0.9 %first.1 = (f32[32,640]{1,0:T(8,128)S(1)}, f32[4,32,256]{2,1,0:T(8,128)S(1)}) custom-call(f32[4,32,256]{2,1,0:T(8,128)S(1)} %join.1.joined_ref.even_ref.near_ref, f32[4,32,256]{2,1,0:T(8,128)S(1)} %collective-permute-done.3.odd_ref, bf16[2,2048,512]{2,1,0:T(8,128)(2,1)S(1)} %get-tuple-element.25.matrix.refs_12_), custom_call_target="tpu_custom_call" | custom-call | tf_op jit(solution)/shard_map/first/pallas_call | solution.py:510
  17.2 0.5 collective-permute-start.4
  17.7 0.0 collective-permute-done.5.far_ref.far_even_ref
  17.7 0.9 %collective-permute-done.4.other_ref = f32[32,640]{1,0:T(8,128)S(1)} collective-permute-done((f32[32,640]{1,0:T(8,128)S(1)}, f32[32,640]{1,0:T(8,128)S(1)}, u32[]{:S(2)}, u32[]{:S(2)}) %collective-permute-start.4) | collective-permute-done | bytes 81952 | tf_op jit(solution)/shard_map/ppermute | solution.py:425
  18.6 0.3 image.2
  18.9 2.9 %collective-permute-start.6 = (f32[136,128]{1,0:T(8,128)S(1)}, f32[136,128]{1,0:T(8,128)S(1)}, u32[]{:S(2)}, u32[]{:S(2)}) collective-permute-start(f32[136,128]{1,0:T(8,128)S(1)} %get-tuple-element.27.refs_0_), channel_id=1, source_target_pairs={{0,14},{2,12},{4,10},{6,8},{8,6},{10,4},{12,2},{14,0},{1,11},{3,9}... | collective-permute-start | bytes 208904 | tf_op jit(solution)/shard_map/ppermute | solution.py:442
  21.8 0.0 collective-permute-start.7
  21.8 2.1 %collective-permute-start.8 = (f32[136,128]{1,0:T(8,128)S(1)}, f32[136,128]{1,0:T(8,128)S(1)}, u32[]{:S(2)}, u32[]{:S(2)}) collective-permute-start(f32[136,128]{1,0:T(8,128)S(1)} %get-tuple-element.27.refs_0_), channel_id=1, source_target_pairs={{0,4},{2,6},{4,0},{6,2},{8,12},{10,14},{12,8},{14,10},{1,9},{3,11}... | collective-permute-start | bytes 208904 | tf_op jit(solution)/shard_map/ppermute | solution.py:442
  23.9 0.0 collective-permute-start.13
  23.9 1.4 %collective-permute-start.9 = (f32[136,128]{1,0:T(8,128)S(1)}, f32[136,128]{1,0:T(8,128)S(1)}, u32[]{:S(2)}, u32[]{:S(2)}) collective-permute-start(f32[136,128]{1,0:T(8,128)S(1)} %get-tuple-element.27.refs_0_), channel_id=1, source_target_pairs={{0,2},{2,0},{4,6},{6,4},{8,10},{10,8},{12,14},{14,12},{1,3},{3,1},... | collective-permute-start | bytes 208904 | tf_op jit(solution)/shard_map/ppermute | solution.py:442
  25.3 1.1 %collective-permute-done.6.refs_1_ = f32[136,128]{1,0:T(8,128)S(1)} collective-permute-done((f32[136,128]{1,0:T(8,128)S(1)}, f32[136,128]{1,0:T(8,128)S(1)}, u32[]{:S(2)}, u32[]{:S(2)}) %collective-permute-start.6) | collective-permute-done | bytes 69664 | tf_op jit(solution)/shard_map/ppermute | solution.py:442
  26.5 0.6 %collective-permute-start.10 = (f32[136,128]{1,0:T(8,128)S(1)}, f32[136,128]{1,0:T(8,128)S(1)}, u32[]{:S(2)}, u32[]{:S(2)}) collective-permute-start(f32[136,128]{1,0:T(8,128)S(1)} %collective-permute-done.6.refs_1_), channel_id=1, source_target_pairs={{0,1},{1,0},{2,3},{3,2},{4,5},{5,4},{6,7},{7,6},{8,9},{9,8},{10,11... | collective-permute-start | bytes 208904 | tf_op jit(solution)/shard_map/ppermute | solution.py:425
  27.1 0.8 %collective-permute-done.7.refs_2_ = f32[136,128]{1,0:T(8,128)S(1)} collective-permute-done((f32[136,128]{1,0:T(8,128)S(1)}, f32[136,128]{1,0:T(8,128)S(1)}, u32[]{:S(2)}, u32[]{:S(2)}) %collective-permute-start.7) | collective-permute-done | bytes 69664 | tf_op jit(solution)/shard_map/ppermute | solution.py:442
  27.9 0.0 collective-permute-start.11
  27.9 0.5 collective-permute-done.8.refs_3_
  28.5 0.8 %collective-permute-start.12 = (f32[136,128]{1,0:T(8,128)S(1)}, f32[136,128]{1,0:T(8,128)S(1)}, u32[]{:S(2)}, u32[]{:S(2)}) collective-permute-start(f32[136,128]{1,0:T(8,128)S(1)} %collective-permute-done.8.refs_3_), channel_id=1, source_target_pairs={{0,1},{1,0},{2,3},{3,2},{4,5},{5,4},{6,7},{7,6},{8,9},{9,8},{10,11... | collective-permute-start | bytes 208904 | tf_op jit(solution)/shard_map/ppermute | solution.py:425
  29.2 0.8 %inverse.2.refs_11_ = f32[32,128]{1,0:T(8,128)S(1)} custom-call(f32[32,128]{1,0:T(8,128)S(1)} %get-tuple-element.31.norm_ref.refs_10_), custom_call_target="tpu_custom_call" | custom-call | tf_op jit(solution)/shard_map/inverse/pallas_call | solution.py:545
  30.0 0.1 collect.1
  30.1 0.0 collective-permute-done.9.refs_4_
  30.1 0.0 collective-permute-done.11.refs_6_
  30.1 0.0 collective-permute-done.12.refs_7_
  30.1 2.8 %step.2 = (f32[32,512]{1,0:T(8,128)S(1)}, f32[9,32,256]{2,1,0:T(8,128)S(1)}, f32[2,8,32,256]{3,2,1,0:T(8,128)S(1)}, f32[32,128]{1,0:T(8,128)S(1)}, f32[32,256]{1,0:T(8,128)S(1)}) custom-call(f32[136,128]{1,0:T(8,128)S(1)} %get-tuple-element.27.refs_0_, f32[136,128]{1,0:T(8,128)S(1)} %collective-permute-done.6.refs_1_, ...), custom_call_target="tpu_custom_call" | custom-call | tf_op jit(solution)/shard_map/step/pallas_call | solution.py:554
  32.9 0.4 collective-permute-start.14
  33.3 0.9 %collective-permute-done.14.other_ref = f32[32,512]{1,0:T(8,128)S(1)} collective-permute-done((f32[32,512]{1,0:T(8,128)S(1)}, f32[32,512]{1,0:T(8,128)S(1)}, u32[]{:S(2)}, u32[]{:S(2)}) %collective-permute-start.14) | collective-permute-done | bytes 65568 | tf_op jit(solution)/shard_map/ppermute | solution.py:425
  34.2 0.3 image.3.refs_0_
  34.5 2.3 %collective-permute-start.15 = (f32[136,128]{1,0:T(8,128)S(1)}, f32[136,128]{1,0:T(8,128)S(1)}, u32[]{:S(2)}, u32[]{:S(2)}) collective-permute-start(f32[136,128]{1,0:T(8,128)S(1)} %image.3.refs_0_), channel_id=1, source_target_pairs={{0,14},{2,12},{4,10},{6,8},{8,6},{10,4},{12,2},{14,0},{1,11},{3,9}... | collective-permute-start | bytes 208904 | tf_op jit(solution)/shard_map/ppermute | solution.py:442
  36.8 0.3 collective-permute-start.16
  37.1 2.5 %collective-permute-start.17 = (f32[136,128]{1,0:T(8,128)S(1)}, f32[136,128]{1,0:T(8,128)S(1)}, u32[]{:S(2)}, u32[]{:S(2)}) collective-permute-start(f32[136,128]{1,0:T(8,128)S(1)} %image.3.refs_0_), channel_id=1, source_target_pairs={{0,4},{2,6},{4,0},{6,2},{8,12},{10,14},{12,8},{14,10},{1,9},{3,11}... | collective-permute-start | bytes 208904 | tf_op jit(solution)/shard_map/ppermute | solution.py:442
  39.6 0.7 %collective-permute-start.18 = (f32[136,128]{1,0:T(8,128)S(1)}, f32[136,128]{1,0:T(8,128)S(1)}, u32[]{:S(2)}, u32[]{:S(2)}) collective-permute-start(f32[136,128]{1,0:T(8,128)S(1)} %image.3.refs_0_), channel_id=1, source_target_pairs={{0,2},{2,0},{4,6},{6,4},{8,10},{10,8},{12,14},{14,12},{1,3},{3,1},... | collective-permute-start | bytes 208904 | tf_op jit(solution)/shard_map/ppermute | solution.py:442
  40.3 2.2 %collective-permute-done.15.refs_1_ = f32[136,128]{1,0:T(8,128)S(1)} collective-permute-done((f32[136,128]{1,0:T(8,128)S(1)}, f32[136,128]{1,0:T(8,128)S(1)}, u32[]{:S(2)}, u32[]{:S(2)}) %collective-permute-start.15) | collective-permute-done | bytes 69664 | tf_op jit(solution)/shard_map/ppermute | solution.py:442
  42.5 0.3 collective-permute-start.19
  42.8 0.6 %collective-permute-done.16.refs_2_ = f32[136,128]{1,0:T(8,128)S(1)} collective-permute-done((f32[136,128]{1,0:T(8,128)S(1)}, f32[136,128]{1,0:T(8,128)S(1)}, u32[]{:S(2)}, u32[]{:S(2)}) %collective-permute-start.16) | collective-permute-done | bytes 69664 | tf_op jit(solution)/shard_map/ppermute | solution.py:442
  43.4 0.5 collective-permute-start.21
  43.9 0.8 %inverse.3.refs_11_ = f32[32,128]{1,0:T(8,128)S(1)} custom-call(f32[32,128]{1,0:T(8,128)S(1)} %get-tuple-element.35.norm_ref.refs_10_), custom_call_target="tpu_custom_call" | custom-call | tf_op jit(solution)/shard_map/inverse/pallas_call | solution.py:545
  44.7 0.0 collective-permute-done.19.refs_5_
  44.7 0.0 collective-permute-done.20.refs_6_
  44.7 0.1 collective-permute-done.21.refs_7_
  44.8 2.8 %step.3 = (f32[32,512]{1,0:T(8,128)S(1)}, f32[2,32,256]{2,1,0:T(8,128)S(1)}, f32[32,256]{1,0:T(8,128)S(1)}, f32[32,128]{1,0:T(8,128)S(1)}, f32[32,256]{1,0:T(8,128)S(1)}) custom-call(f32[136,128]{1,0:T(8,128)S(1)} %image.3.refs_0_, f32[136,128]{1,0:T(8,128)S(1)} %collective-permute-done.15.refs_1_, f32[136,128]{1,0:T(8,128)S(1)} %collective-permute-done.16.refs_2_, ...), custom_call_target="tpu_custom_call" | custom-call | tf_op jit(solution)/shard_map/step/pallas_call | solution.py:554
  47.6 0.4 collective-permute-start.22
  48.0 0.9 %collective-permute-done.22.other_ref = f32[32,512]{1,0:T(8,128)S(1)} collective-permute-done((f32[32,512]{1,0:T(8,128)S(1)}, f32[32,512]{1,0:T(8,128)S(1)}, u32[]{:S(2)}, u32[]{:S(2)}) %collective-permute-start.22) | collective-permute-done | bytes 65568 | tf_op jit(solution)/shard_map/ppermute | solution.py:425
  48.9 0.3 last_image.1
  49.2 2.5 %collective-permute-start.23 = (f32[8,128]{1,0:T(8,128)S(1)}, f32[8,128]{1,0:T(8,128)S(1)}, u32[]{:S(2)}, u32[]{:S(2)}) collective-permute-start(f32[8,128]{1,0:T(8,128)S(1)} %get-tuple-element.39.refs_0_), channel_id=1, source_target_pairs={{0,12},{2,14},{4,8},{6,10},{8,4},{10,6},{12,0},{14,2},{1,15},{3,13... | collective-permute-start | bytes 12296 | tf_op jit(solution)/shard_map/ppermute | solution.py:442
  51.8 0.4 collective-permute-start.24
  52.2 2.0 %collective-permute-start.25 = (f32[8,128]{1,0:T(8,128)S(1)}, f32[8,128]{1,0:T(8,128)S(1)}, u32[]{:S(2)}, u32[]{:S(2)}) collective-permute-start(f32[8,128]{1,0:T(8,128)S(1)} %get-tuple-element.39.refs_0_), channel_id=1, source_target_pairs={{0,4},{2,6},{4,0},{6,2},{8,12},{10,14},{12,8},{14,10},{1,9},{3,11}... | collective-permute-start | bytes 12296 | tf_op jit(solution)/shard_map/ppermute | solution.py:442
  54.1 1.1 %collective-permute-start.26 = (f32[8,128]{1,0:T(8,128)S(1)}, f32[8,128]{1,0:T(8,128)S(1)}, u32[]{:S(2)}, u32[]{:S(2)}) collective-permute-start(f32[8,128]{1,0:T(8,128)S(1)} %get-tuple-element.39.refs_0_), channel_id=1, source_target_pairs={{0,2},{2,0},{4,6},{6,4},{8,10},{10,8},{12,14},{14,12},{1,3},{3,1},... | collective-permute-start | bytes 12296 | tf_op jit(solution)/shard_map/ppermute | solution.py:442
  55.2 0.5 collective-permute-start.27
  55.7 0.5 collective-permute-done.24.refs_2_
  56.3 0.2 collective-permute-start.28
  56.4 0.0 collective-permute-done.25.refs_3_
  56.4 0.3 collective-permute-start.29
  56.8 1.0 %collective-permute-done.26.refs_4_ = f32[8,128]{1,0:T(8,128)S(1)} collective-permute-done((f32[8,128]{1,0:T(8,128)S(1)}, f32[8,128]{1,0:T(8,128)S(1)}, u32[]{:S(2)}, u32[]{:S(2)}) %collective-permute-start.26) | collective-permute-done | bytes 4128 | tf_op jit(solution)/shard_map/ppermute | solution.py:442
  57.8 0.0 collective-permute-done.27.refs_5_
  57.8 1.5 %last.1 = (f32[32,256]{1,0:T(8,128)}, f32[32,256]{1,0:T(8,128)}) custom-call(f32[8,128]{1,0:T(8,128)S(1)} %get-tuple-element.39.refs_0_, f32[8,128]{1,0:T(8,128)S(1)} %collective-permute-done.23.refs_1_, f32[8,128]{1,0:T(8,128)S(1)} %collective-permute-done.24.refs_2_, f32[8,128]{1,0:T(8,128)S(1)} %collective-permute-done.25.refs_3_, ...), custom_call_target="tpu_custom_call" | custom-call | tf_op jit(solution)/shard_map/last/pallas_call | solution.py:577
  (10 shorter events, 0.0 us)
Async XLA Ops:
  1.5 8.4 %collective-permute-start = (f32[32,256]{1,0:T(8,128)S(1)}, f32[32,256]{1,0:T(8,128)S(1)}, u32[]{:S(2)}, u32[]{:S(2)}) collective-permute-start(f32[32,256]{1,0:T(8,128)S(1)} %multiply_multiply_fusion.refs_3_), channel_id=1, source_target_pairs={{0,8},{2,10},{4,12},{6,14},{8,0},{10,2},{12,4},{14,6},{1,9},{3,11}... | collective-permute-start | bytes 98312 | tf_op jit(solution)/shard_map/ppermute | solution.py:422
  5.5 5.7 %collective-permute-start.1 = (f32[32,256]{1,0:T(8,128)S(1)}, f32[32,256]{1,0:T(8,128)S(1)}, u32[]{:S(2)}, u32[]{:S(2)}) collective-permute-start(f32[32,256]{1,0:T(8,128)S(1)} %multiply_multiply_fusion.refs_3_), channel_id=1, source_target_pairs={{0,12},{2,14},{4,8},{6,10},{8,4},{10,6},{12,0},{14,2},{1,13},{3,15... | collective-permute-start | bytes 98312 | tf_op jit(solution)/shard_map/ppermute | solution.py:422
  6.9 4.4 %collective-permute-start.2 = (f32[32,256]{1,0:T(8,128)S(1)}, f32[32,256]{1,0:T(8,128)S(1)}, u32[]{:S(2)}, u32[]{:S(2)}) collective-permute-start(f32[32,256]{1,0:T(8,128)S(1)} %multiply_multiply_fusion.refs_3_), channel_id=1, source_target_pairs={{0,4},{2,6},{4,0},{6,2},{8,12},{10,14},{12,8},{14,10},{1,5},{3,7},... | collective-permute-start | bytes 98312 | tf_op jit(solution)/shard_map/ppermute | solution.py:422
  11.2 5.0 %collective-permute-start.3 = (f32[4,32,256]{2,1,0:T(8,128)S(1)}, f32[4,32,256]{2,1,0:T(8,128)S(1)}, u32[]{:S(2)}, u32[]{:S(2)}) collective-permute-start(f32[4,32,256]{2,1,0:T(8,128)S(1)} %join.1.joined_ref.even_ref.near_ref), channel_id=1, source_target_pairs={{0,2},{2,0},{4,6},{6,4},{8,10},{10,8},{12,14},{14,12},{1,3},{3,1},... | collective-permute-start | bytes 393224 | tf_op jit(solution)/shard_map/ppermute | solution.py:422
  12.8 4.8 %collective-permute-start.5 = (f32[4,32,256]{2,1,0:T(8,128)S(1)}, f32[4,32,256]{2,1,0:T(8,128)S(1)}, u32[]{:S(2)}, u32[]{:S(2)}) collective-permute-start(f32[4,32,256]{2,1,0:T(8,128)S(1)} %join.1.joined_ref.even_ref.near_ref), channel_id=1, source_target_pairs={{0,1},{1,0},{2,3},{3,2},{4,5},{5,4},{6,7},{7,6},{8,9},{9,8},{10,11... | collective-permute-start | bytes 393224 | tf_op jit(solution)/shard_map/ppermute | solution.py:425
  17.2 1.4 %collective-permute-start.4 = (f32[32,640]{1,0:T(8,128)S(1)}, f32[32,640]{1,0:T(8,128)S(1)}, u32[]{:S(2)}, u32[]{:S(2)}) collective-permute-start(f32[32,640]{1,0:T(8,128)S(1)} %get-tuple-element.26.mine_ref), channel_id=1, source_target_pairs={{0,1},{1,0},{2,3},{3,2},{4,5},{5,4},{6,7},{7,6},{8,9},{9,8},{10,11... | collective-permute-start | bytes 245768 | tf_op jit(solution)/shard_map/ppermute | solution.py:425
  18.9 7.5 %collective-permute-start.6 = (f32[136,128]{1,0:T(8,128)S(1)}, f32[136,128]{1,0:T(8,128)S(1)}, u32[]{:S(2)}, u32[]{:S(2)}) collective-permute-start(f32[136,128]{1,0:T(8,128)S(1)} %get-tuple-element.27.refs_0_), channel_id=1, source_target_pairs={{0,14},{2,12},{4,10},{6,8},{8,6},{10,4},{12,2},{14,0},{1,11},{3,9}... | collective-permute-start | bytes 208904 | tf_op jit(solution)/shard_map/ppermute | solution.py:442
  21.8 6.1 %collective-permute-start.7 = (f32[136,128]{1,0:T(8,128)S(1)}, f32[136,128]{1,0:T(8,128)S(1)}, u32[]{:S(2)}, u32[]{:S(2)}) collective-permute-start(f32[136,128]{1,0:T(8,128)S(1)} %get-tuple-element.27.refs_0_), channel_id=1, source_target_pairs={{0,6},{2,4},{4,2},{6,0},{8,14},{10,12},{12,10},{14,8},{1,13},{3,15... | collective-permute-start | bytes 208904 | tf_op jit(solution)/shard_map/ppermute | solution.py:442
  21.8 6.6 %collective-permute-start.8 = (f32[136,128]{1,0:T(8,128)S(1)}, f32[136,128]{1,0:T(8,128)S(1)}, u32[]{:S(2)}, u32[]{:S(2)}) collective-permute-start(f32[136,128]{1,0:T(8,128)S(1)} %get-tuple-element.27.refs_0_), channel_id=1, source_target_pairs={{0,4},{2,6},{4,0},{6,2},{8,12},{10,14},{12,8},{14,10},{1,9},{3,11}... | collective-permute-start | bytes 208904 | tf_op jit(solution)/shard_map/ppermute | solution.py:442
  23.9 6.1 %collective-permute-start.13 = (f32[4,32,256]{2,1,0:T(8,128)S(1)}, f32[4,32,256]{2,1,0:T(8,128)S(1)}, u32[]{:S(2)}, u32[]{:S(2)}) collective-permute-start(f32[4,32,256]{2,1,0:T(8,128)S(1)} %get-tuple-element.28.odd_ref), channel_id=1, source_target_pairs={{0,1},{1,0},{2,3},{3,2},{4,5},{5,4},{6,7},{7,6},{8,9},{9,8},{10,11... | collective-permute-start | bytes 393224 | tf_op jit(solution)/shard_map/ppermute | solution.py:425
  23.9 6.1 %collective-permute-start.9 = (f32[136,128]{1,0:T(8,128)S(1)}, f32[136,128]{1,0:T(8,128)S(1)}, u32[]{:S(2)}, u32[]{:S(2)}) collective-permute-start(f32[136,128]{1,0:T(8,128)S(1)} %get-tuple-element.27.refs_0_), channel_id=1, source_target_pairs={{0,2},{2,0},{4,6},{6,4},{8,10},{10,8},{12,14},{14,12},{1,3},{3,1},... | collective-permute-start | bytes 208904 | tf_op jit(solution)/shard_map/ppermute | solution.py:442
  26.5 3.6 %collective-permute-start.10 = (f32[136,128]{1,0:T(8,128)S(1)}, f32[136,128]{1,0:T(8,128)S(1)}, u32[]{:S(2)}, u32[]{:S(2)}) collective-permute-start(f32[136,128]{1,0:T(8,128)S(1)} %collective-permute-done.6.refs_1_), channel_id=1, source_target_pairs={{0,1},{1,0},{2,3},{3,2},{4,5},{5,4},{6,7},{7,6},{8,9},{9,8},{10,11... | collective-permute-start | bytes 208904 | tf_op jit(solution)/shard_map/ppermute | solution.py:425
  27.9 2.2 %collective-permute-start.11 = (f32[136,128]{1,0:T(8,128)S(1)}, f32[136,128]{1,0:T(8,128)S(1)}, u32[]{:S(2)}, u32[]{:S(2)}) collective-permute-start(f32[136,128]{1,0:T(8,128)S(1)} %collective-permute-done.7.refs_2_), channel_id=1, source_target_pairs={{0,1},{1,0},{2,3},{3,2},{4,5},{5,4},{6,7},{7,6},{8,9},{9,8},{10,11... | collective-permute-start | bytes 208904 | tf_op jit(solution)/shard_map/ppermute | solution.py:425
  28.5 1.7 %collective-permute-start.12 = (f32[136,128]{1,0:T(8,128)S(1)}, f32[136,128]{1,0:T(8,128)S(1)}, u32[]{:S(2)}, u32[]{:S(2)}) collective-permute-start(f32[136,128]{1,0:T(8,128)S(1)} %collective-permute-done.8.refs_3_), channel_id=1, source_target_pairs={{0,1},{1,0},{2,3},{3,2},{4,5},{5,4},{6,7},{7,6},{8,9},{9,8},{10,11... | collective-permute-start | bytes 208904 | tf_op jit(solution)/shard_map/ppermute | solution.py:425
  32.9 1.3 %collective-permute-start.14 = (f32[32,512]{1,0:T(8,128)S(1)}, f32[32,512]{1,0:T(8,128)S(1)}, u32[]{:S(2)}, u32[]{:S(2)}) collective-permute-start(f32[32,512]{1,0:T(8,128)S(1)} %get-tuple-element.32.mine_ref), channel_id=1, source_target_pairs={{0,1},{1,0},{2,3},{3,2},{4,5},{5,4},{6,7},{7,6},{8,9},{9,8},{10,11... | collective-permute-start | bytes 196616 | tf_op jit(solution)/shard_map/ppermute | solution.py:425
  34.5 8.0 %collective-permute-start.15 = (f32[136,128]{1,0:T(8,128)S(1)}, f32[136,128]{1,0:T(8,128)S(1)}, u32[]{:S(2)}, u32[]{:S(2)}) collective-permute-start(f32[136,128]{1,0:T(8,128)S(1)} %image.3.refs_0_), channel_id=1, source_target_pairs={{0,14},{2,12},{4,10},{6,8},{8,6},{10,4},{12,2},{14,0},{1,11},{3,9}... | collective-permute-start | bytes 208904 | tf_op jit(solution)/shard_map/ppermute | solution.py:442
  36.8 6.6 %collective-permute-start.16 = (f32[136,128]{1,0:T(8,128)S(1)}, f32[136,128]{1,0:T(8,128)S(1)}, u32[]{:S(2)}, u32[]{:S(2)}) collective-permute-start(f32[136,128]{1,0:T(8,128)S(1)} %image.3.refs_0_), channel_id=1, source_target_pairs={{0,6},{2,4},{4,2},{6,0},{8,14},{10,12},{12,10},{14,8},{1,13},{3,15... | collective-permute-start | bytes 208904 | tf_op jit(solution)/shard_map/ppermute | solution.py:442
  37.1 6.3 %collective-permute-start.17 = (f32[136,128]{1,0:T(8,128)S(1)}, f32[136,128]{1,0:T(8,128)S(1)}, u32[]{:S(2)}, u32[]{:S(2)}) collective-permute-start(f32[136,128]{1,0:T(8,128)S(1)} %image.3.refs_0_), channel_id=1, source_target_pairs={{0,4},{2,6},{4,0},{6,2},{8,12},{10,14},{12,8},{14,10},{1,9},{3,11}... | collective-permute-start | bytes 208904 | tf_op jit(solution)/shard_map/ppermute | solution.py:442
  39.6 5.1 %collective-permute-start.18 = (f32[136,128]{1,0:T(8,128)S(1)}, f32[136,128]{1,0:T(8,128)S(1)}, u32[]{:S(2)}, u32[]{:S(2)}) collective-permute-start(f32[136,128]{1,0:T(8,128)S(1)} %image.3.refs_0_), channel_id=1, source_target_pairs={{0,2},{2,0},{4,6},{6,4},{8,10},{10,8},{12,14},{14,12},{1,3},{3,1},... | collective-permute-start | bytes 208904 | tf_op jit(solution)/shard_map/ppermute | solution.py:442
  42.5 2.2 %collective-permute-start.19 = (f32[136,128]{1,0:T(8,128)S(1)}, f32[136,128]{1,0:T(8,128)S(1)}, u32[]{:S(2)}, u32[]{:S(2)}) collective-permute-start(f32[136,128]{1,0:T(8,128)S(1)} %collective-permute-done.15.refs_1_), channel_id=1, source_target_pairs={{0,1},{1,0},{2,3},{3,2},{4,5},{5,4},{6,7},{7,6},{8,9},{9,8},{10,11... | collective-permute-start | bytes 208904 | tf_op jit(solution)/shard_map/ppermute | solution.py:425
  43.4 1.3 %collective-permute-start.20 = (f32[136,128]{1,0:T(8,128)S(1)}, f32[136,128]{1,0:T(8,128)S(1)}, u32[]{:S(2)}, u32[]{:S(2)}) collective-permute-start(f32[136,128]{1,0:T(8,128)S(1)} %collective-permute-done.16.refs_2_), channel_id=1, source_target_pairs={{0,1},{1,0},{2,3},{3,2},{4,5},{5,4},{6,7},{7,6},{8,9},{9,8},{10,11... | collective-permute-start | bytes 208904 | tf_op jit(solution)/shard_map/ppermute | solution.py:425
  43.4 1.4 %collective-permute-start.21 = (f32[136,128]{1,0:T(8,128)S(1)}, f32[136,128]{1,0:T(8,128)S(1)}, u32[]{:S(2)}, u32[]{:S(2)}) collective-permute-start(f32[136,128]{1,0:T(8,128)S(1)} %collective-permute-done.17.refs_3_), channel_id=1, source_target_pairs={{0,1},{1,0},{2,3},{3,2},{4,5},{5,4},{6,7},{7,6},{8,9},{9,8},{10,11... | collective-permute-start | bytes 208904 | tf_op jit(solution)/shard_map/ppermute | solution.py:425
  47.6 1.3 %collective-permute-start.22 = (f32[32,512]{1,0:T(8,128)S(1)}, f32[32,512]{1,0:T(8,128)S(1)}, u32[]{:S(2)}, u32[]{:S(2)}) collective-permute-start(f32[32,512]{1,0:T(8,128)S(1)} %get-tuple-element.37.mine_ref), channel_id=1, source_target_pairs={{0,1},{1,0},{2,3},{3,2},{4,5},{5,4},{6,7},{7,6},{8,9},{9,8},{10,11... | collective-permute-start | bytes 196616 | tf_op jit(solution)/shard_map/ppermute | solution.py:425
  49.2 6.0 %collective-permute-start.23 = (f32[8,128]{1,0:T(8,128)S(1)}, f32[8,128]{1,0:T(8,128)S(1)}, u32[]{:S(2)}, u32[]{:S(2)}) collective-permute-start(f32[8,128]{1,0:T(8,128)S(1)} %get-tuple-element.39.refs_0_), channel_id=1, source_target_pairs={{0,12},{2,14},{4,8},{6,10},{8,4},{10,6},{12,0},{14,2},{1,15},{3,13... | collective-permute-start | bytes 12296 | tf_op jit(solution)/shard_map/ppermute | solution.py:442
  51.8 4.5 %collective-permute-start.24 = (f32[8,128]{1,0:T(8,128)S(1)}, f32[8,128]{1,0:T(8,128)S(1)}, u32[]{:S(2)}, u32[]{:S(2)}) collective-permute-start(f32[8,128]{1,0:T(8,128)S(1)} %get-tuple-element.39.refs_0_), channel_id=1, source_target_pairs={{0,6},{2,4},{4,2},{6,0},{8,14},{10,12},{12,10},{14,8},{1,11},{3,9}... | collective-permute-start | bytes 12296 | tf_op jit(solution)/shard_map/ppermute | solution.py:442
  52.2 4.3 %collective-permute-start.25 = (f32[8,128]{1,0:T(8,128)S(1)}, f32[8,128]{1,0:T(8,128)S(1)}, u32[]{:S(2)}, u32[]{:S(2)}) collective-permute-start(f32[8,128]{1,0:T(8,128)S(1)} %get-tuple-element.39.refs_0_), channel_id=1, source_target_pairs={{0,4},{2,6},{4,0},{6,2},{8,12},{10,14},{12,8},{14,10},{1,9},{3,11}... | collective-permute-start | bytes 12296 | tf_op jit(solution)/shard_map/ppermute | solution.py:442
  54.1 3.6 %collective-permute-start.26 = (f32[8,128]{1,0:T(8,128)S(1)}, f32[8,128]{1,0:T(8,128)S(1)}, u32[]{:S(2)}, u32[]{:S(2)}) collective-permute-start(f32[8,128]{1,0:T(8,128)S(1)} %get-tuple-element.39.refs_0_), channel_id=1, source_target_pairs={{0,2},{2,0},{4,6},{6,4},{8,10},{10,8},{12,14},{14,12},{1,3},{3,1},... | collective-permute-start | bytes 12296 | tf_op jit(solution)/shard_map/ppermute | solution.py:442
  55.2 2.5 %collective-permute-start.27 = (f32[8,128]{1,0:T(8,128)S(1)}, f32[8,128]{1,0:T(8,128)S(1)}, u32[]{:S(2)}, u32[]{:S(2)}) collective-permute-start(f32[8,128]{1,0:T(8,128)S(1)} %collective-permute-done.23.refs_1_), channel_id=1, source_target_pairs={{0,1},{1,0},{2,3},{3,2},{4,5},{5,4},{6,7},{7,6},{8,9},{9,8},{10,11... | collective-permute-start | bytes 12296 | tf_op jit(solution)/shard_map/ppermute | solution.py:425
  56.3 1.5 %collective-permute-start.28 = (f32[8,128]{1,0:T(8,128)S(1)}, f32[8,128]{1,0:T(8,128)S(1)}, u32[]{:S(2)}, u32[]{:S(2)}) collective-permute-start(f32[8,128]{1,0:T(8,128)S(1)} %collective-permute-done.24.refs_2_), channel_id=1, source_target_pairs={{0,1},{1,0},{2,3},{3,2},{4,5},{5,4},{6,7},{7,6},{8,9},{9,8},{10,11... | collective-permute-start | bytes 12296 | tf_op jit(solution)/shard_map/ppermute | solution.py:425
  56.4 1.4 %collective-permute-start.29 = (f32[8,128]{1,0:T(8,128)S(1)}, f32[8,128]{1,0:T(8,128)S(1)}, u32[]{:S(2)}, u32[]{:S(2)}) collective-permute-start(f32[8,128]{1,0:T(8,128)S(1)} %collective-permute-done.25.refs_3_), channel_id=1, source_target_pairs={{0,1},{1,0},{2,3},{3,2},{4,5},{5,4},{6,7},{7,6},{8,9},{9,8},{10,11... | collective-permute-start | bytes 12296 | tf_op jit(solution)/shard_map/ppermute | solution.py:425

commit v19 on v18

--- a/solution.py
+++ b/solution.py
@@ -10,6 +10,7 @@
 ITERS = 3
 LANES = 128
 PIVOTS = 16
+TAIL = 16
 CHUNKS = 5
 F32 = jnp.float32
 BF16 = jnp.bfloat16
@@ -277,24 +278,68 @@
     return high + low
 
 
-def first_kernel(even_ref, odd_ref, matrix, out_ref, odd_out_ref):
+def message_kernel(
+    signs_hbm, weight_hbm, scale_hbm, out_ref, scale_out, signs_ref, weight_ref, scale_ref, sems
+):
+    copies = copy_lists(
+        (signs_hbm, weight_hbm, scale_hbm), (signs_ref, weight_ref, scale_ref), sems
+    )
+    for copy in copies:
+        copy.wait()
+    size, width = signs_ref.shape
+    out_ref[:size] = signs_ref[...].astype(F32).astype(BF16)
+    row_ids = lax.broadcasted_iota(jnp.int32, (TAIL, width), 0)
+    tail = jnp.zeros((TAIL, width), F32)
+    for i, part in enumerate(split(weight_ref[...].reshape(1, width))):
+        tail = jnp.where(row_ids == i, part.astype(F32), tail)
+    out_ref[size:] = tail.astype(BF16)
+    scale = scale_ref[...].reshape(1, size)
+    scale = jnp.concatenate([scale, jnp.zeros((1, LANES - size), F32)], axis=1)
+    rows = lax.broadcasted_iota(jnp.int32, (size, LANES), 0)
+    lanes = lax.broadcasted_iota(jnp.int32, (size, LANES), 1)
+    column = jnp.sum(jnp.where(rows == lanes, scale, 0.0), axis=1, keepdims=True)
+    scale_out[...] = jnp.broadcast_to(column, (size, LANES))
+
+
+def right_side_of(message, scale):
+    size, width = message.shape
+    size = size - TAIL
+    tail = message[size:].astype(F32)
+    weight = (tail[0:1] + tail[1:2]) + tail[2:3]
+    scale = jnp.concatenate([scale] * (width // LANES), axis=1)
+    return message[:size].astype(F32) * weight * scale
+
+
+def first_kernel(
+    even_ref, far_even_ref, odd_ref, scale_ref, matrix, out_ref, ends_ref, odd_out_ref
+):
     pieces = 2 * even_ref.shape[0]
     odd_out_ref[...] = odd_ref[...]
-    values = [(odd_ref if k % 2 else even_ref)[k // 2] for k in range(pieces)]
+    scale = scale_ref[...]
+    values = [
+        right_side_of((odd_ref if k % 2 else even_ref)[k // 2], scale) for k in range(pieces)
+    ]
+    ends_ref[0] = values[0]
+    ends_ref[1] = right_side_of(far_even_ref[0], scale)
     rows = 2 * values[0].shape[1]
     joined = jnp.concatenate(values, axis=1)
     out_ref[:, rows:] = gram_parts(joined, joined)
     out_ref[:, :rows] = apply_dense(values, matrix)
 
 
-def collect_kernel(even_ref, odd_ref, far_even_ref, far_odd_ref, residual_ref, direction_ref):
+def collect_kernel(
+    even_ref, odd_ref, far_even_ref, far_odd_ref, scale_ref, residual_ref, direction_ref
+):
     pieces = 2 * even_ref.shape[0]
+    scale = scale_ref[...]
     for k in range(pieces):
-        near = (odd_ref if k % 2 else even_ref)[k // 2]
+        near = right_side_of((odd_ref if k % 2 else even_ref)[k // 2], scale)
+        far = right_side_of((far_odd_ref if k % 2 else far_even_ref)[k // 2], scale)
         residual_ref[0, k] = near
-        residual_ref[1, k] = (far_odd_ref if k % 2 else far_even_ref)[k // 2]
+        residual_ref[1, k] = far
         direction_ref[k] = near
-    direction_ref[pieces] = far_even_ref[0]
+        if k == 0:
+            direction_ref[pieces] = far
 
 
 def add_halves(mine_ref, other_ref, width):
@@ -317,7 +362,7 @@
             at = pl.multiple_of((place * parts + i) * size, size)
             out_ref[pl.ds(at, size)] = half[:, lanes]
     products = symmetric_parts(near, near_ref[0]) + symmetric_parts(
-        far, far_ref[0 if first else far_ref.shape[0] - 1]
+        far, far_ref[far_ref.shape[0] - 1]
     )
     out_ref[2 * parts * size :] = pack(finish(products))
 
@@ -448,13 +493,26 @@
                 places[masks[1]] = (turn + len(turns), turn)
         return [value, *fetched, *passed], [places[k] for k in range(pieces)]
 
-    right_side = signs.astype(F32) * vertex_weight[None, :] * column_scale[:, None]
-    even = [right_side] + [swap(right_side, k) for k in range(2, pieces, 2)]
+    height = sketch + TAIL
+    given = (signs, vertex_weight, column_scale)
+    message, scale = pl.pallas_call(
+        message_kernel,
+        out_shape=(shape(height, rows_dev, dtype=BF16), shape(sketch, LANES)),
+        in_specs=[HBM] * 3,
+        out_specs=(VMEM, VMEM),
+        scratch_shapes=[
+            *[pltpu.VMEM(x.shape, x.dtype) for x in given],
+            pltpu.SemaphoreType.DMA((len(given),)),
+        ],
+        compiler_params=params(),
+        name="message",
+    )(*[pltpu.with_memory_space_constraint(x, pltpu.HBM) for x in given])
+    even = [message] + [swap(message, k) for k in range(2, pieces, 2)]
 
     matrix = shape(2, depth, group, dtype=BF16)
     total = shape(depth // tile * (group // tile), tile, tile)
     slots = tiles.shape[0]
-    half = slots * 3 // 8
+    half = slots // 2
     rest = shape(slots - half, tile, tile, dtype=BF16)
     lists = [pltpu.with_memory_space_constraint(x, pltpu.HBM) for x in (tile_rows, tile_cols)]
     lists_scratch = [pltpu.SMEM(x.shape, jnp.int32) for x in lists]
@@ -476,7 +534,7 @@
         cost_estimate=cost,
         name="gather",
     )(tile_count, *lists, pltpu.with_memory_space_constraint(tiles, pltpu.HBM))
-    joined = shape(pieces // 2, sketch, rows_dev)
+    joined = shape(pieces // 2, height, rows_dev, dtype=BF16)
     order = [*range(pieces // 4, pieces // 2), *range(1, pieces // 4), 0]
     even = pl.pallas_call(
         functools.partial(join_kernel, order),
@@ -507,14 +565,14 @@
     packed = shape(sketch * sketch // LANES, LANES)
     payload = shape(2 * sketch * (rows_dev // LANES) + packed.shape[0], LANES)
 
-    partial_sum, odd = pl.pallas_call(
+    partial_sum, ends, odd = pl.pallas_call(
         first_kernel,
-        out_shape=(shape(sketch, group + LANES), joined),
-        in_specs=[VMEM] * 3,
-        out_specs=(VMEM, VMEM),
+        out_shape=(shape(sketch, group + LANES), shape(2, sketch, rows_dev), joined),
+        in_specs=[VMEM] * 5,
+        out_specs=(VMEM,) * 3,
         compiler_params=params(matrix, state, state),
         name="first",
-    )(even, odd, dense)
+    )(even, far_even, odd, scale, dense)
     norm = None
     solution = None
     direction = None
@@ -522,7 +580,7 @@
         first = iteration == 0
         last = iteration == ITERS - 2
         sums = (partial_sum, across(partial_sum))
-        given = (even, far_even) if first else (direction, direction)
+        given = (ends, ends) if first else (direction, direction)
         outs = pl.pallas_call(
             functools.partial(image_kernel, first),
             out_shape=(payload, small) if first else (payload,),
@@ -537,11 +595,11 @@
             residual, direction = pl.pallas_call(
                 collect_kernel,
                 out_shape=(held, state),
-                in_specs=[VMEM] * 4,
+                in_specs=[VMEM] * 5,
                 out_specs=(VMEM, VMEM),
                 compiler_params=params(held, held, state),
                 name="collect",
-            )(even, odd, far_even, across(odd))
+            )(even, odd, far_even, across(odd), scale)
         inverse = pl.pallas_call(
             inverse_kernel,
             out_shape=small,

time: 59.5 us -> 59.6 us (level)
  waiting for transfers between devices: 11.2 us -> 12.9 us
  other arithmetic: 0.85 us -> 0 us
  starting transfers between devices: 29.8 us -> 29.2 us
    pallas_call x1, Pallas kernels: 3.33 us -> 2.23 us  [per_device(): pl.pallas_call(functools.partial(dense_kernel, rows_dev), out_shape=(matr...]
    ppermute x4, waiting for transfers between devices: 1.45 us -> 2.47 us  [swap(): return lax.ppermute(value, 'row', [(i, i ^ mask) for i in range(pieces)])]
    mul x1 -> x0, other arithmetic: 0.85 us -> none  [per_device(): signs.astype(F32) * vertex_weight[None, :] * column_scale[:, None]]
    pallas_call x1 -> x2, Pallas kernels: 0.89 us -> 1.65 us  [the longest x1 0.87 us: per_device(): pl.pallas_call(message_kernel, out_shape=(shape(height, rows_dev, dtype=B...]
  transfers between devices with their start and end apart: 30 -> 30, of which waited for: 13 -> 13; matrix products, arithmetic and copies ran while one was open for 0% -> 0% of each run, Pallas kernels for 13% -> 10%
where the time goes in v19:
time: 59.6 us; the launch traced here: 59.4 us
  starting transfers between devices  29.2 us (49%)
  Pallas kernels  15.9 us (27%)
  waiting for transfers between devices  12.9 us (22%)
  between operations  1.46 us (2%)
    ppermute x12, starting transfers between devices, exchange(): fetched.append(lax.ppermute(value, ('row', 'col'), pairs))  17.7 us
    ppermute x4, starting transfers between devices, swap(): return lax.ppermute(value, 'row', [(i, i ^ mask) for i in range(pieces)])  7.27 us
    ppermute x12, waiting for transfers between devices, exchange(): fetched.append(lax.ppermute(value, ('row', 'col'), pairs))  7.17 us
    pallas_call x2, Pallas kernels, per_device(): pl.pallas_call(functools.partial(step_kernel, len(found), places, not fir...  5.56 us
    ppermute x14, starting transfers between devices, across(): lax.ppermute(value, 'col', [(i, (i + 1) % col_devices) for i in range(col...  4.16 us
    ppermute x14, waiting for transfers between devices, across(): lax.ppermute(value, 'col', [(i, (i + 1) % col_devices) for i in range(col...  3.21 us
    ppermute x4, waiting for transfers between devices, swap(): return lax.ppermute(value, 'row', [(i, i ^ mask) for i in range(pieces)])  2.47 us
    pallas_call x1, Pallas kernels, per_device(): pl.pallas_call(functools.partial(gather_kernel, rows_dev), out_shape=(tot...  2.28 us
  transfers between devices with their start and end apart: 30, of which 13 were waited for; matrix products, arithmetic and copies ran while one was open for 0% of the time, Pallas kernels for 10%

profile of v19, /device:TPU:0, one launch (start us, length us, event | category | flops | bytes accessed | tf_op | source)
XLA Modules:
  0.0 59.4 jit_solution(6439614690124149534)
XLA Ops:
  0.6 0.9 %message.1 = (bf16[48,256]{1,0:T(8,128)(2,1)S(1)}, f32[32,128]{1,0:T(8,128)S(1)}) custom-call(s32[32,256]{1,0:T(8,128)} %signs_hbm.1, f32[256]{0:T(256)} %weight_hbm.1, f32[32]{0:T(128)} %scale_hbm.1), custom_call_target="tpu_custom_call" | custom-call | tf_op jit(solution)/shard_map/message/pallas_call | solution.py:498
  1.5 4.1 %collective-permute-start = (bf16[48,256]{1,0:T(8,128)(2,1)S(1)}, bf16[48,256]{1,0:T(8,128)(2,1)S(1)}, u32[]{:S(2)}, u32[]{:S(2)}) collective-permute-start(bf16[48,256]{1,0:T(8,128)(2,1)S(1)} %get-tuple-element.26.refs_3_), channel_id=1, source_target_pairs={{0,8},{2,10},{4,12},{6,14},{8,0},{10,2},{12,4},{14,6},{1,9},{3,11}... | collective-permute-start | bytes 73736 | tf_op jit(solution)/shard_map/ppermute | solution.py:467
  5.6 1.3 %collective-permute-start.1 = (bf16[48,256]{1,0:T(8,128)(2,1)S(1)}, bf16[48,256]{1,0:T(8,128)(2,1)S(1)}, u32[]{:S(2)}, u32[]{:S(2)}) collective-permute-start(bf16[48,256]{1,0:T(8,128)(2,1)S(1)} %get-tuple-element.26.refs_3_), channel_id=1, source_target_pairs={{0,12},{2,14},{4,8},{6,10},{8,4},{10,6},{12,0},{14,2},{1,13},{3,15... | collective-permute-start | bytes 73736 | tf_op jit(solution)/shard_map/ppermute | solution.py:467
  7.0 0.2 collective-permute-start.2
  7.8 2.3 %gather.1 = (f32[64,128,128]{2,1,0:T(8,128)S(1)}, bf16[65,128,128]{2,1,0:T(8,128)(2,1)S(1)}) custom-call(s32[1]{0:T(128)S(6)} %copy.11.count_ref, s32[130]{0:T(256)} %rows_hbm.3, s32[130]{0:T(256)} %cols_hbm.3, bf16[130,128,128]{2,1,0:T(8,128)(2,1)} %tiles_ref.1), custom_call_target="tpu_custom_call" | custom-call | flops 8519680 | bytes 8519680 | tf_op jit(solution)/shard_map/gather/pallas_call | solution.py:522
  10.1 0.0 collective-permute-done.refs_0_
  10.1 1.1 %collective-permute-done.1.refs_1_ = bf16[48,256]{1,0:T(8,128)(2,1)S(1)} collective-permute-done((bf16[48,256]{1,0:T(8,128)(2,1)S(1)}, bf16[48,256]{1,0:T(8,128)(2,1)S(1)}, u32[]{:S(2)}, u32[]{:S(2)}) %collective-permute-start.1) | collective-permute-done | bytes 24608 | tf_op jit(solution)/shard_map/ppermute | solution.py:467
  11.2 0.0 collective-permute-done.2.refs_2_
  11.2 0.1 collective-permute-start.3
  11.3 1.6 %collective-permute-start.4 = (bf16[4,48,256]{2,1,0:T(8,128)(2,1)S(1)}, bf16[4,48,256]{2,1,0:T(8,128)(2,1)S(1)}, u32[]{:S(2)}, u32[]{:S(2)}) collective-permute-start(bf16[4,48,256]{2,1,0:T(8,128)(2,1)S(1)} %join.1.joined_ref.even_ref), channel_id=1, source_target_pairs={{0,2},{2,0},{4,6},{6,4},{8,10},{10,8},{12,14},{14,12},{1,3},{3,1},... | collective-permute-start | bytes 294920 | tf_op jit(solution)/shard_map/ppermute | solution.py:467
  12.9 2.2 %dense.1 = (bf16[2,2048,512]{2,1,0:T(8,128)(2,1)S(1)}, f32[64,128,128]{2,1,0:T(8,128)S(1)}) custom-call(s32[1]{0:T(128)S(6)} %copy.11.count_ref, s32[130]{0:T(256)} %rows_hbm.3, s32[130]{0:T(256)} %cols_hbm.3, bf16[65,128,128]{2,1,0:T(8,128)(2,1)S(1)} %get-tuple-element.29.rest, ...), custom_call_target="tpu_custom_call", output_to_operand_aliasing={{1}: (4, {})} | custom-call | flops 8519680 | bytes 8519680 | tf_op jit(solution)/shard_map/dense/pallas_call | solution.py:549
  15.2 0.0 collective-permute-done.3.far_even_ref
  15.2 1.4 %collective-permute-done.4.odd_ref = bf16[4,48,256]{2,1,0:T(8,128)(2,1)S(1)} collective-permute-done((bf16[4,48,256]{2,1,0:T(8,128)(2,1)S(1)}, bf16[4,48,256]{2,1,0:T(8,128)(2,1)S(1)}, u32[]{:S(2)}, u32[]{:S(2)}) %collective-permute-start.4) | collective-permute-done | bytes 98336 | tf_op jit(solution)/shard_map/ppermute | solution.py:467
  16.5 0.8 %first.1 = (f32[32,640]{1,0:T(8,128)S(1)}, f32[2,32,256]{2,1,0:T(8,128)S(1)}, bf16[4,48,256]{2,1,0:T(8,128)(2,1)S(1)}) custom-call(bf16[4,48,256]{2,1,0:T(8,128)(2,1)S(1)} %join.1.joined_ref.even_ref, bf16[4,48,256]{2,1,0:T(8,128)(2,1)S(1)} %collective-permute-done.3.far_even_ref, bf16[4,48,256]{2,1,0:T(8,128)(2,1)S(1)} %collective-permute-done.4.odd_ref, ...), custom_call_target="tpu_custom_call" | custom-call | tf_op jit(solution)/shard_map/first/pallas_call | solution.py:568
  17.3 0.1 collective-permute-start.5
  17.4 1.3 %collective-permute-done.5.other_ref = f32[32,640]{1,0:T(8,128)S(1)} collective-permute-done((f32[32,640]{1,0:T(8,128)S(1)}, f32[32,640]{1,0:T(8,128)S(1)}, u32[]{:S(2)}, u32[]{:S(2)}) %collective-permute-start.5) | collective-permute-done | bytes 81952 | tf_op jit(solution)/shard_map/ppermute | solution.py:470
  18.7 0.3 image.2
  19.0 3.0 %collective-permute-start.6 = (f32[136,128]{1,0:T(8,128)S(1)}, f32[136,128]{1,0:T(8,128)S(1)}, u32[]{:S(2)}, u32[]{:S(2)}) collective-permute-start(f32[136,128]{1,0:T(8,128)S(1)} %get-tuple-element.33.refs_0_), channel_id=1, source_target_pairs={{0,14},{2,12},{4,10},{6,8},{8,6},{10,4},{12,2},{14,0},{1,11},{3,9}... | collective-permute-start | bytes 208904 | tf_op jit(solution)/shard_map/ppermute | solution.py:487
  22.0 0.2 collective-permute-start.7
  22.2 1.8 %collective-permute-start.8 = (f32[136,128]{1,0:T(8,128)S(1)}, f32[136,128]{1,0:T(8,128)S(1)}, u32[]{:S(2)}, u32[]{:S(2)}) collective-permute-start(f32[136,128]{1,0:T(8,128)S(1)} %get-tuple-element.33.refs_0_), channel_id=1, source_target_pairs={{0,4},{2,6},{4,0},{6,2},{8,12},{10,14},{12,8},{14,10},{1,9},{3,11}... | collective-permute-start | bytes 208904 | tf_op jit(solution)/shard_map/ppermute | solution.py:487
  24.0 1.5 %collective-permute-start.9 = (f32[136,128]{1,0:T(8,128)S(1)}, f32[136,128]{1,0:T(8,128)S(1)}, u32[]{:S(2)}, u32[]{:S(2)}) collective-permute-start(f32[136,128]{1,0:T(8,128)S(1)} %get-tuple-element.33.refs_0_), channel_id=1, source_target_pairs={{0,2},{2,0},{4,6},{6,4},{8,10},{10,8},{12,14},{14,12},{1,3},{3,1},... | collective-permute-start | bytes 208904 | tf_op jit(solution)/shard_map/ppermute | solution.py:487
  25.5 0.8 %collective-permute-done.6.refs_1_ = f32[136,128]{1,0:T(8,128)S(1)} collective-permute-done((f32[136,128]{1,0:T(8,128)S(1)}, f32[136,128]{1,0:T(8,128)S(1)}, u32[]{:S(2)}, u32[]{:S(2)}) %collective-permute-start.6) | collective-permute-done | bytes 69664 | tf_op jit(solution)/shard_map/ppermute | solution.py:487
  26.3 0.6 collective-permute-start.10
  26.9 1.0 %collective-permute-done.7.refs_2_ = f32[136,128]{1,0:T(8,128)S(1)} collective-permute-done((f32[136,128]{1,0:T(8,128)S(1)}, f32[136,128]{1,0:T(8,128)S(1)}, u32[]{:S(2)}, u32[]{:S(2)}) %collective-permute-start.7) | collective-permute-done | bytes 69664 | tf_op jit(solution)/shard_map/ppermute | solution.py:487
  28.0 0.0 collective-permute-start.11
  28.0 0.7 %collective-permute-done.8.refs_3_ = f32[136,128]{1,0:T(8,128)S(1)} collective-permute-done((f32[136,128]{1,0:T(8,128)S(1)}, f32[136,128]{1,0:T(8,128)S(1)}, u32[]{:S(2)}, u32[]{:S(2)}) %collective-permute-start.8) | collective-permute-done | bytes 69664 | tf_op jit(solution)/shard_map/ppermute | solution.py:487
  28.6 0.8 %collective-permute-start.12 = (f32[136,128]{1,0:T(8,128)S(1)}, f32[136,128]{1,0:T(8,128)S(1)}, u32[]{:S(2)}, u32[]{:S(2)}) collective-permute-start(f32[136,128]{1,0:T(8,128)S(1)} %collective-permute-done.8.refs_3_), channel_id=1, source_target_pairs={{0,1},{1,0},{2,3},{3,2},{4,5},{5,4},{6,7},{7,6},{8,9},{9,8},{10,11... | collective-permute-start | bytes 208904 | tf_op jit(solution)/shard_map/ppermute | solution.py:470
  29.4 0.8 %inverse.2.refs_11_ = f32[32,128]{1,0:T(8,128)S(1)} custom-call(f32[32,128]{1,0:T(8,128)S(1)} %get-tuple-element.37.norm_ref.refs_10_), custom_call_target="tpu_custom_call" | custom-call | tf_op jit(solution)/shard_map/inverse/pallas_call | solution.py:603
  30.2 0.1 collect.1
  30.3 0.0 collective-permute-done.11.refs_6_
  30.3 2.8 %step.2 = (f32[32,512]{1,0:T(8,128)S(1)}, f32[9,32,256]{2,1,0:T(8,128)S(1)}, f32[2,8,32,256]{3,2,1,0:T(8,128)S(1)}, f32[32,128]{1,0:T(8,128)S(1)}, f32[32,256]{1,0:T(8,128)S(1)}) custom-call(f32[136,128]{1,0:T(8,128)S(1)} %get-tuple-element.33.refs_0_, f32[136,128]{1,0:T(8,128)S(1)} %collective-permute-done.6.refs_1_, ...), custom_call_target="tpu_custom_call" | custom-call | tf_op jit(solution)/shard_map/step/pallas_call | solution.py:612
  33.1 0.3 collective-permute-start.14
  33.5 0.9 %collective-permute-done.14.other_ref = f32[32,512]{1,0:T(8,128)S(1)} collective-permute-done((f32[32,512]{1,0:T(8,128)S(1)}, f32[32,512]{1,0:T(8,128)S(1)}, u32[]{:S(2)}, u32[]{:S(2)}) %collective-permute-start.14) | collective-permute-done | bytes 65568 | tf_op jit(solution)/shard_map/ppermute | solution.py:470
  34.4 0.3 image.3.refs_0_
  34.8 2.0 %collective-permute-start.15 = (f32[136,128]{1,0:T(8,128)S(1)}, f32[136,128]{1,0:T(8,128)S(1)}, u32[]{:S(2)}, u32[]{:S(2)}) collective-permute-start(f32[136,128]{1,0:T(8,128)S(1)} %image.3.refs_0_), channel_id=1, source_target_pairs={{0,14},{2,12},{4,10},{6,8},{8,6},{10,4},{12,2},{14,0},{1,11},{3,9}... | collective-permute-start | bytes 208904 | tf_op jit(solution)/shard_map/ppermute | solution.py:487
  36.7 0.5 collective-permute-start.16
  37.3 2.5 %collective-permute-start.17 = (f32[136,128]{1,0:T(8,128)S(1)}, f32[136,128]{1,0:T(8,128)S(1)}, u32[]{:S(2)}, u32[]{:S(2)}) collective-permute-start(f32[136,128]{1,0:T(8,128)S(1)} %image.3.refs_0_), channel_id=1, source_target_pairs={{0,4},{2,6},{4,0},{6,2},{8,12},{10,14},{12,8},{14,10},{1,9},{3,11}... | collective-permute-start | bytes 208904 | tf_op jit(solution)/shard_map/ppermute | solution.py:487
  39.7 0.5 collective-permute-start.18
  40.2 2.4 %collective-permute-done.15.refs_1_ = f32[136,128]{1,0:T(8,128)S(1)} collective-permute-done((f32[136,128]{1,0:T(8,128)S(1)}, f32[136,128]{1,0:T(8,128)S(1)}, u32[]{:S(2)}, u32[]{:S(2)}) %collective-permute-start.15) | collective-permute-done | bytes 69664 | tf_op jit(solution)/shard_map/ppermute | solution.py:487
  42.7 0.2 collective-permute-start.19
  42.9 0.7 %collective-permute-done.16.refs_2_ = f32[136,128]{1,0:T(8,128)S(1)} collective-permute-done((f32[136,128]{1,0:T(8,128)S(1)}, f32[136,128]{1,0:T(8,128)S(1)}, u32[]{:S(2)}, u32[]{:S(2)}) %collective-permute-start.16) | collective-permute-done | bytes 69664 | tf_op jit(solution)/shard_map/ppermute | solution.py:487
  43.5 0.5 collective-permute-start.21
  44.0 0.8 %inverse.3.refs_11_ = f32[32,128]{1,0:T(8,128)S(1)} custom-call(f32[32,128]{1,0:T(8,128)S(1)} %get-tuple-element.41.norm_ref.refs_10_), custom_call_target="tpu_custom_call" | custom-call | tf_op jit(solution)/shard_map/inverse/pallas_call | solution.py:603
  44.8 0.0 collective-permute-done.19.refs_5_
  44.8 0.0 collective-permute-done.20.refs_6_
  44.9 0.1 collective-permute-done.21.refs_7_
  45.0 2.8 %step.3 = (f32[32,512]{1,0:T(8,128)S(1)}, f32[2,32,256]{2,1,0:T(8,128)S(1)}, f32[32,256]{1,0:T(8,128)S(1)}, f32[32,128]{1,0:T(8,128)S(1)}, f32[32,256]{1,0:T(8,128)S(1)}) custom-call(f32[136,128]{1,0:T(8,128)S(1)} %image.3.refs_0_, f32[136,128]{1,0:T(8,128)S(1)} %collective-permute-done.15.refs_1_, f32[136,128]{1,0:T(8,128)S(1)} %collective-permute-done.16.refs_2_, ...), custom_call_target="tpu_custom_call" | custom-call | tf_op jit(solution)/shard_map/step/pallas_call | solution.py:612
  47.7 0.4 collective-permute-start.22
  48.1 0.9 %collective-permute-done.22.other_ref = f32[32,512]{1,0:T(8,128)S(1)} collective-permute-done((f32[32,512]{1,0:T(8,128)S(1)}, f32[32,512]{1,0:T(8,128)S(1)}, u32[]{:S(2)}, u32[]{:S(2)}) %collective-permute-start.22) | collective-permute-done | bytes 65568 | tf_op jit(solution)/shard_map/ppermute | solution.py:470
  49.0 0.3 last_image.1
  49.3 2.3 %collective-permute-start.23 = (f32[8,128]{1,0:T(8,128)S(1)}, f32[8,128]{1,0:T(8,128)S(1)}, u32[]{:S(2)}, u32[]{:S(2)}) collective-permute-start(f32[8,128]{1,0:T(8,128)S(1)} %get-tuple-element.45.refs_0_), channel_id=1, source_target_pairs={{0,12},{2,14},{4,8},{6,10},{8,4},{10,6},{12,0},{14,2},{1,15},{3,13... | collective-permute-start | bytes 12296 | tf_op jit(solution)/shard_map/ppermute | solution.py:487
  51.7 0.8 %collective-permute-start.24 = (f32[8,128]{1,0:T(8,128)S(1)}, f32[8,128]{1,0:T(8,128)S(1)}, u32[]{:S(2)}, u32[]{:S(2)}) collective-permute-start(f32[8,128]{1,0:T(8,128)S(1)} %get-tuple-element.45.refs_0_), channel_id=1, source_target_pairs={{0,6},{2,4},{4,2},{6,0},{8,14},{10,12},{12,10},{14,8},{1,11},{3,9}... | collective-permute-start | bytes 12296 | tf_op jit(solution)/shard_map/ppermute | solution.py:487
  52.4 1.8 %collective-permute-start.25 = (f32[8,128]{1,0:T(8,128)S(1)}, f32[8,128]{1,0:T(8,128)S(1)}, u32[]{:S(2)}, u32[]{:S(2)}) collective-permute-start(f32[8,128]{1,0:T(8,128)S(1)} %get-tuple-element.45.refs_0_), channel_id=1, source_target_pairs={{0,4},{2,6},{4,0},{6,2},{8,12},{10,14},{12,8},{14,10},{1,9},{3,11}... | collective-permute-start | bytes 12296 | tf_op jit(solution)/shard_map/ppermute | solution.py:487
  54.3 0.9 %collective-permute-start.26 = (f32[8,128]{1,0:T(8,128)S(1)}, f32[8,128]{1,0:T(8,128)S(1)}, u32[]{:S(2)}, u32[]{:S(2)}) collective-permute-start(f32[8,128]{1,0:T(8,128)S(1)} %get-tuple-element.45.refs_0_), channel_id=1, source_target_pairs={{0,2},{2,0},{4,6},{6,4},{8,10},{10,8},{12,14},{14,12},{1,3},{3,1},... | collective-permute-start | bytes 12296 | tf_op jit(solution)/shard_map/ppermute | solution.py:487
  55.1 0.7 %collective-permute-start.27 = (f32[8,128]{1,0:T(8,128)S(1)}, f32[8,128]{1,0:T(8,128)S(1)}, u32[]{:S(2)}, u32[]{:S(2)}) collective-permute-start(f32[8,128]{1,0:T(8,128)S(1)} %collective-permute-done.23.refs_1_), channel_id=1, source_target_pairs={{0,1},{1,0},{2,3},{3,2},{4,5},{5,4},{6,7},{7,6},{8,9},{9,8},{10,11... | collective-permute-start | bytes 12296 | tf_op jit(solution)/shard_map/ppermute | solution.py:470
  55.9 0.3 collective-permute-done.24.refs_2_
  56.2 0.4 collective-permute-start.28
  56.6 0.0 collective-permute-done.25.refs_3_
  56.6 0.1 collective-permute-start.29
  56.7 1.2 %collective-permute-done.26.refs_4_ = f32[8,128]{1,0:T(8,128)S(1)} collective-permute-done((f32[8,128]{1,0:T(8,128)S(1)}, f32[8,128]{1,0:T(8,128)S(1)}, u32[]{:S(2)}, u32[]{:S(2)}) %collective-permute-start.26) | collective-permute-done | bytes 4128 | tf_op jit(solution)/shard_map/ppermute | solution.py:487
  57.9 0.0 collective-permute-done.27.refs_5_
  57.9 0.0 collective-permute-done.28.refs_6_
  57.9 0.0 collective-permute-done.29.refs_7_
  57.9 1.5 %last.1 = (f32[32,256]{1,0:T(8,128)}, f32[32,256]{1,0:T(8,128)}) custom-call(f32[8,128]{1,0:T(8,128)S(1)} %get-tuple-element.45.refs_0_, f32[8,128]{1,0:T(8,128)S(1)} %collective-permute-done.23.refs_1_, f32[8,128]{1,0:T(8,128)S(1)} %collective-permute-done.24.refs_2_, f32[8,128]{1,0:T(8,128)S(1)} %collective-permute-done.25.refs_3_, ...), custom_call_target="tpu_custom_call" | custom-call | tf_op jit(solution)/shard_map/last/pallas_call | solution.py:635
  (10 shorter events, 0.0 us)
Async XLA Ops:
  1.5 8.6 %collective-permute-start = (bf16[48,256]{1,0:T(8,128)(2,1)S(1)}, bf16[48,256]{1,0:T(8,128)(2,1)S(1)}, u32[]{:S(2)}, u32[]{:S(2)}) collective-permute-start(bf16[48,256]{1,0:T(8,128)(2,1)S(1)} %get-tuple-element.26.refs_3_), channel_id=1, source_target_pairs={{0,8},{2,10},{4,12},{6,14},{8,0},{10,2},{12,4},{14,6},{1,9},{3,11}... | collective-permute-start | bytes 73736 | tf_op jit(solution)/shard_map/ppermute | solution.py:467
  5.6 5.6 %collective-permute-start.1 = (bf16[48,256]{1,0:T(8,128)(2,1)S(1)}, bf16[48,256]{1,0:T(8,128)(2,1)S(1)}, u32[]{:S(2)}, u32[]{:S(2)}) collective-permute-start(bf16[48,256]{1,0:T(8,128)(2,1)S(1)} %get-tuple-element.26.refs_3_), channel_id=1, source_target_pairs={{0,12},{2,14},{4,8},{6,10},{8,4},{10,6},{12,0},{14,2},{1,13},{3,15... | collective-permute-start | bytes 73736 | tf_op jit(solution)/shard_map/ppermute | solution.py:467
  7.0 4.3 %collective-permute-start.2 = (bf16[48,256]{1,0:T(8,128)(2,1)S(1)}, bf16[48,256]{1,0:T(8,128)(2,1)S(1)}, u32[]{:S(2)}, u32[]{:S(2)}) collective-permute-start(bf16[48,256]{1,0:T(8,128)(2,1)S(1)} %get-tuple-element.26.refs_3_), channel_id=1, source_target_pairs={{0,4},{2,6},{4,0},{6,2},{8,12},{10,14},{12,8},{14,10},{1,5},{3,7},... | collective-permute-start | bytes 73736 | tf_op jit(solution)/shard_map/ppermute | solution.py:467
  11.2 3.9 %collective-permute-start.3 = (bf16[4,48,256]{2,1,0:T(8,128)(2,1)S(1)}, bf16[4,48,256]{2,1,0:T(8,128)(2,1)S(1)}, u32[]{:S(2)}, u32[]{:S(2)}) collective-permute-start(bf16[4,48,256]{2,1,0:T(8,128)(2,1)S(1)} %join.1.joined_ref.even_ref), channel_id=1, source_target_pairs={{0,1},{1,0},{2,3},{3,2},{4,5},{5,4},{6,7},{7,6},{8,9},{9,8},{10,11... | collective-permute-start | bytes 294920 | tf_op jit(solution)/shard_map/ppermute | solution.py:470
  11.3 5.2 %collective-permute-start.4 = (bf16[4,48,256]{2,1,0:T(8,128)(2,1)S(1)}, bf16[4,48,256]{2,1,0:T(8,128)(2,1)S(1)}, u32[]{:S(2)}, u32[]{:S(2)}) collective-permute-start(bf16[4,48,256]{2,1,0:T(8,128)(2,1)S(1)} %join.1.joined_ref.even_ref), channel_id=1, source_target_pairs={{0,2},{2,0},{4,6},{6,4},{8,10},{10,8},{12,14},{14,12},{1,3},{3,1},... | collective-permute-start | bytes 294920 | tf_op jit(solution)/shard_map/ppermute | solution.py:467
  17.3 1.3 %collective-permute-start.5 = (f32[32,640]{1,0:T(8,128)S(1)}, f32[32,640]{1,0:T(8,128)S(1)}, u32[]{:S(2)}, u32[]{:S(2)}) collective-permute-start(f32[32,640]{1,0:T(8,128)S(1)} %get-tuple-element.31.mine_ref), channel_id=1, source_target_pairs={{0,1},{1,0},{2,3},{3,2},{4,5},{5,4},{6,7},{7,6},{8,9},{9,8},{10,11... | collective-permute-start | bytes 245768 | tf_op jit(solution)/shard_map/ppermute | solution.py:470
  19.0 7.3 %collective-permute-start.6 = (f32[136,128]{1,0:T(8,128)S(1)}, f32[136,128]{1,0:T(8,128)S(1)}, u32[]{:S(2)}, u32[]{:S(2)}) collective-permute-start(f32[136,128]{1,0:T(8,128)S(1)} %get-tuple-element.33.refs_0_), channel_id=1, source_target_pairs={{0,14},{2,12},{4,10},{6,8},{8,6},{10,4},{12,2},{14,0},{1,11},{3,9}... | collective-permute-start | bytes 208904 | tf_op jit(solution)/shard_map/ppermute | solution.py:487
  22.0 6.0 %collective-permute-start.7 = (f32[136,128]{1,0:T(8,128)S(1)}, f32[136,128]{1,0:T(8,128)S(1)}, u32[]{:S(2)}, u32[]{:S(2)}) collective-permute-start(f32[136,128]{1,0:T(8,128)S(1)} %get-tuple-element.33.refs_0_), channel_id=1, source_target_pairs={{0,6},{2,4},{4,2},{6,0},{8,14},{10,12},{12,10},{14,8},{1,13},{3,15... | collective-permute-start | bytes 208904 | tf_op jit(solution)/shard_map/ppermute | solution.py:487
  22.2 6.4 %collective-permute-start.8 = (f32[136,128]{1,0:T(8,128)S(1)}, f32[136,128]{1,0:T(8,128)S(1)}, u32[]{:S(2)}, u32[]{:S(2)}) collective-permute-start(f32[136,128]{1,0:T(8,128)S(1)} %get-tuple-element.33.refs_0_), channel_id=1, source_target_pairs={{0,4},{2,6},{4,0},{6,2},{8,12},{10,14},{12,8},{14,10},{1,9},{3,11}... | collective-permute-start | bytes 208904 | tf_op jit(solution)/shard_map/ppermute | solution.py:487
  24.0 6.2 %collective-permute-start.13 = (bf16[4,48,256]{2,1,0:T(8,128)(2,1)S(1)}, bf16[4,48,256]{2,1,0:T(8,128)(2,1)S(1)}, u32[]{:S(2)}, u32[]{:S(2)}) collective-permute-start(bf16[4,48,256]{2,1,0:T(8,128)(2,1)S(1)} %get-tuple-element.34.odd_ref), channel_id=1, source_target_pairs={{0,1},{1,0},{2,3},{3,2},{4,5},{5,4},{6,7},{7,6},{8,9},{9,8},{10,11... | collective-permute-start | bytes 294920 | tf_op jit(solution)/shard_map/ppermute | solution.py:470
  24.0 6.3 %collective-permute-start.9 = (f32[136,128]{1,0:T(8,128)S(1)}, f32[136,128]{1,0:T(8,128)S(1)}, u32[]{:S(2)}, u32[]{:S(2)}) collective-permute-start(f32[136,128]{1,0:T(8,128)S(1)} %get-tuple-element.33.refs_0_), channel_id=1, source_target_pairs={{0,2},{2,0},{4,6},{6,4},{8,10},{10,8},{12,14},{14,12},{1,3},{3,1},... | collective-permute-start | bytes 208904 | tf_op jit(solution)/shard_map/ppermute | solution.py:487
  26.3 4.0 %collective-permute-start.10 = (f32[136,128]{1,0:T(8,128)S(1)}, f32[136,128]{1,0:T(8,128)S(1)}, u32[]{:S(2)}, u32[]{:S(2)}) collective-permute-start(f32[136,128]{1,0:T(8,128)S(1)} %collective-permute-done.6.refs_1_), channel_id=1, source_target_pairs={{0,1},{1,0},{2,3},{3,2},{4,5},{5,4},{6,7},{7,6},{8,9},{9,8},{10,11... | collective-permute-start | bytes 208904 | tf_op jit(solution)/shard_map/ppermute | solution.py:470
  28.0 2.4 %collective-permute-start.11 = (f32[136,128]{1,0:T(8,128)S(1)}, f32[136,128]{1,0:T(8,128)S(1)}, u32[]{:S(2)}, u32[]{:S(2)}) collective-permute-start(f32[136,128]{1,0:T(8,128)S(1)} %collective-permute-done.7.refs_2_), channel_id=1, source_target_pairs={{0,1},{1,0},{2,3},{3,2},{4,5},{5,4},{6,7},{7,6},{8,9},{9,8},{10,11... | collective-permute-start | bytes 208904 | tf_op jit(solution)/shard_map/ppermute | solution.py:470
  28.6 1.7 %collective-permute-start.12 = (f32[136,128]{1,0:T(8,128)S(1)}, f32[136,128]{1,0:T(8,128)S(1)}, u32[]{:S(2)}, u32[]{:S(2)}) collective-permute-start(f32[136,128]{1,0:T(8,128)S(1)} %collective-permute-done.8.refs_3_), channel_id=1, source_target_pairs={{0,1},{1,0},{2,3},{3,2},{4,5},{5,4},{6,7},{7,6},{8,9},{9,8},{10,11... | collective-permute-start | bytes 208904 | tf_op jit(solution)/shard_map/ppermute | solution.py:470
  33.1 1.3 %collective-permute-start.14 = (f32[32,512]{1,0:T(8,128)S(1)}, f32[32,512]{1,0:T(8,128)S(1)}, u32[]{:S(2)}, u32[]{:S(2)}) collective-permute-start(f32[32,512]{1,0:T(8,128)S(1)} %get-tuple-element.38.mine_ref), channel_id=1, source_target_pairs={{0,1},{1,0},{2,3},{3,2},{4,5},{5,4},{6,7},{7,6},{8,9},{9,8},{10,11... | collective-permute-start | bytes 196616 | tf_op jit(solution)/shard_map/ppermute | solution.py:470
  34.8 7.9 %collective-permute-start.15 = (f32[136,128]{1,0:T(8,128)S(1)}, f32[136,128]{1,0:T(8,128)S(1)}, u32[]{:S(2)}, u32[]{:S(2)}) collective-permute-start(f32[136,128]{1,0:T(8,128)S(1)} %image.3.refs_0_), channel_id=1, source_target_pairs={{0,14},{2,12},{4,10},{6,8},{8,6},{10,4},{12,2},{14,0},{1,11},{3,9}... | collective-permute-start | bytes 208904 | tf_op jit(solution)/shard_map/ppermute | solution.py:487
  36.7 6.8 %collective-permute-start.16 = (f32[136,128]{1,0:T(8,128)S(1)}, f32[136,128]{1,0:T(8,128)S(1)}, u32[]{:S(2)}, u32[]{:S(2)}) collective-permute-start(f32[136,128]{1,0:T(8,128)S(1)} %image.3.refs_0_), channel_id=1, source_target_pairs={{0,6},{2,4},{4,2},{6,0},{8,14},{10,12},{12,10},{14,8},{1,13},{3,15... | collective-permute-start | bytes 208904 | tf_op jit(solution)/shard_map/ppermute | solution.py:487
  37.3 6.3 %collective-permute-start.17 = (f32[136,128]{1,0:T(8,128)S(1)}, f32[136,128]{1,0:T(8,128)S(1)}, u32[]{:S(2)}, u32[]{:S(2)}) collective-permute-start(f32[136,128]{1,0:T(8,128)S(1)} %image.3.refs_0_), channel_id=1, source_target_pairs={{0,4},{2,6},{4,0},{6,2},{8,12},{10,14},{12,8},{14,10},{1,9},{3,11}... | collective-permute-start | bytes 208904 | tf_op jit(solution)/shard_map/ppermute | solution.py:487
  39.7 5.1 %collective-permute-start.18 = (f32[136,128]{1,0:T(8,128)S(1)}, f32[136,128]{1,0:T(8,128)S(1)}, u32[]{:S(2)}, u32[]{:S(2)}) collective-permute-start(f32[136,128]{1,0:T(8,128)S(1)} %image.3.refs_0_), channel_id=1, source_target_pairs={{0,2},{2,0},{4,6},{6,4},{8,10},{10,8},{12,14},{14,12},{1,3},{3,1},... | collective-permute-start | bytes 208904 | tf_op jit(solution)/shard_map/ppermute | solution.py:487
  42.7 2.2 %collective-permute-start.19 = (f32[136,128]{1,0:T(8,128)S(1)}, f32[136,128]{1,0:T(8,128)S(1)}, u32[]{:S(2)}, u32[]{:S(2)}) collective-permute-start(f32[136,128]{1,0:T(8,128)S(1)} %collective-permute-done.15.refs_1_), channel_id=1, source_target_pairs={{0,1},{1,0},{2,3},{3,2},{4,5},{5,4},{6,7},{7,6},{8,9},{9,8},{10,11... | collective-permute-start | bytes 208904 | tf_op jit(solution)/shard_map/ppermute | solution.py:470
  43.5 1.3 %collective-permute-start.20 = (f32[136,128]{1,0:T(8,128)S(1)}, f32[136,128]{1,0:T(8,128)S(1)}, u32[]{:S(2)}, u32[]{:S(2)}) collective-permute-start(f32[136,128]{1,0:T(8,128)S(1)} %collective-permute-done.16.refs_2_), channel_id=1, source_target_pairs={{0,1},{1,0},{2,3},{3,2},{4,5},{5,4},{6,7},{7,6},{8,9},{9,8},{10,11... | collective-permute-start | bytes 208904 | tf_op jit(solution)/shard_map/ppermute | solution.py:470
  43.5 1.4 %collective-permute-start.21 = (f32[136,128]{1,0:T(8,128)S(1)}, f32[136,128]{1,0:T(8,128)S(1)}, u32[]{:S(2)}, u32[]{:S(2)}) collective-permute-start(f32[136,128]{1,0:T(8,128)S(1)} %collective-permute-done.17.refs_3_), channel_id=1, source_target_pairs={{0,1},{1,0},{2,3},{3,2},{4,5},{5,4},{6,7},{7,6},{8,9},{9,8},{10,11... | collective-permute-start | bytes 208904 | tf_op jit(solution)/shard_map/ppermute | solution.py:470
  47.7 1.3 %collective-permute-start.22 = (f32[32,512]{1,0:T(8,128)S(1)}, f32[32,512]{1,0:T(8,128)S(1)}, u32[]{:S(2)}, u32[]{:S(2)}) collective-permute-start(f32[32,512]{1,0:T(8,128)S(1)} %get-tuple-element.43.mine_ref), channel_id=1, source_target_pairs={{0,1},{1,0},{2,3},{3,2},{4,5},{5,4},{6,7},{7,6},{8,9},{9,8},{10,11... | collective-permute-start | bytes 196616 | tf_op jit(solution)/shard_map/ppermute | solution.py:470
  49.3 5.8 %collective-permute-start.23 = (f32[8,128]{1,0:T(8,128)S(1)}, f32[8,128]{1,0:T(8,128)S(1)}, u32[]{:S(2)}, u32[]{:S(2)}) collective-permute-start(f32[8,128]{1,0:T(8,128)S(1)} %get-tuple-element.45.refs_0_), channel_id=1, source_target_pairs={{0,12},{2,14},{4,8},{6,10},{8,4},{10,6},{12,0},{14,2},{1,15},{3,13... | collective-permute-start | bytes 12296 | tf_op jit(solution)/shard_map/ppermute | solution.py:487
  51.7 4.5 %collective-permute-start.24 = (f32[8,128]{1,0:T(8,128)S(1)}, f32[8,128]{1,0:T(8,128)S(1)}, u32[]{:S(2)}, u32[]{:S(2)}) collective-permute-start(f32[8,128]{1,0:T(8,128)S(1)} %get-tuple-element.45.refs_0_), channel_id=1, source_target_pairs={{0,6},{2,4},{4,2},{6,0},{8,14},{10,12},{12,10},{14,8},{1,11},{3,9}... | collective-permute-start | bytes 12296 | tf_op jit(solution)/shard_map/ppermute | solution.py:487
  52.4 4.1 %collective-permute-start.25 = (f32[8,128]{1,0:T(8,128)S(1)}, f32[8,128]{1,0:T(8,128)S(1)}, u32[]{:S(2)}, u32[]{:S(2)}) collective-permute-start(f32[8,128]{1,0:T(8,128)S(1)} %get-tuple-element.45.refs_0_), channel_id=1, source_target_pairs={{0,4},{2,6},{4,0},{6,2},{8,12},{10,14},{12,8},{14,10},{1,9},{3,11}... | collective-permute-start | bytes 12296 | tf_op jit(solution)/shard_map/ppermute | solution.py:487
  54.3 3.6 %collective-permute-start.26 = (f32[8,128]{1,0:T(8,128)S(1)}, f32[8,128]{1,0:T(8,128)S(1)}, u32[]{:S(2)}, u32[]{:S(2)}) collective-permute-start(f32[8,128]{1,0:T(8,128)S(1)} %get-tuple-element.45.refs_0_), channel_id=1, source_target_pairs={{0,2},{2,0},{4,6},{6,4},{8,10},{10,8},{12,14},{14,12},{1,3},{3,1},... | collective-permute-start | bytes 12296 | tf_op jit(solution)/shard_map/ppermute | solution.py:487
  55.1 2.7 %collective-permute-start.27 = (f32[8,128]{1,0:T(8,128)S(1)}, f32[8,128]{1,0:T(8,128)S(1)}, u32[]{:S(2)}, u32[]{:S(2)}) collective-permute-start(f32[8,128]{1,0:T(8,128)S(1)} %collective-permute-done.23.refs_1_), channel_id=1, source_target_pairs={{0,1},{1,0},{2,3},{3,2},{4,5},{5,4},{6,7},{7,6},{8,9},{9,8},{10,11... | collective-permute-start | bytes 12296 | tf_op jit(solution)/shard_map/ppermute | solution.py:470
  56.2 1.7 %collective-permute-start.28 = (f32[8,128]{1,0:T(8,128)S(1)}, f32[8,128]{1,0:T(8,128)S(1)}, u32[]{:S(2)}, u32[]{:S(2)}) collective-permute-start(f32[8,128]{1,0:T(8,128)S(1)} %collective-permute-done.24.refs_2_), channel_id=1, source_target_pairs={{0,1},{1,0},{2,3},{3,2},{4,5},{5,4},{6,7},{7,6},{8,9},{9,8},{10,11... | collective-permute-start | bytes 12296 | tf_op jit(solution)/shard_map/ppermute | solution.py:470
  56.6 1.3 %collective-permute-start.29 = (f32[8,128]{1,0:T(8,128)S(1)}, f32[8,128]{1,0:T(8,128)S(1)}, u32[]{:S(2)}, u32[]{:S(2)}) collective-permute-start(f32[8,128]{1,0:T(8,128)S(1)} %collective-permute-done.25.refs_3_), channel_id=1, source_target_pairs={{0,1},{1,0},{2,3},{3,2},{4,5},{5,4},{6,7},{7,6},{8,9},{9,8},{10,11... | collective-permute-start | bytes 12296 | tf_op jit(solution)/shard_map/ppermute | solution.py:470

commit v20 on v19

--- a/solution.py
+++ b/solution.py
@@ -11,6 +11,7 @@
 LANES = 128
 PIVOTS = 16
 TAIL = 16
+UNROLL = 4
 CHUNKS = 5
 F32 = jnp.float32
 BF16 = jnp.bfloat16
@@ -156,18 +157,22 @@
         return place(jnp.minimum(slot, slots - 1))
 
     def add(turn, places):
-        slot = start + 2 * turn
-        values = [tiles[slot + i - first_tile].astype(F32) for i in range(2)]
-        following = (after(slot + 2), after(slot + 3))
+        slot = start + UNROLL * turn
+        values = [tiles[slot + i - first_tile].astype(F32) for i in range(UNROLL)]
+        following = tuple(after(slot + UNROLL + i) for i in range(UNROLL))
         for at, value in zip(places, values):
             total[at] = total[at] + value
         return following
 
-    places = lax.fori_loop(0, (stop - start) // 2, add, (after(start), after(start + 1)))
-
-    @pl.when(lax.rem(stop - start, 2) == 1)
-    def _():
-        total[places[0]] = total[places[0]] + tiles[stop - 1 - first_tile].astype(F32)
+    def add_one(slot, at):
+        value = tiles[slot - first_tile].astype(F32)
+        following = after(slot + 1)
+        total[at] = total[at] + value
+        return following
+
+    turns = (stop - start) // UNROLL
+    places = lax.fori_loop(0, turns, add, tuple(after(start + i) for i in range(UNROLL)))
+    lax.fori_loop(start + UNROLL * turns, stop, add_one, places[0])
 
 
 def copy_lists(hbm_refs, smem_refs, sems):

time: 59.6 us -> 60 us (level)
  Pallas kernels: 15.9 us -> 18.5 us
  waiting for transfers between devices: 12.9 us -> 11.2 us
  starting transfers between devices: 29.2 us -> 28.5 us
    pallas_call x1, Pallas kernels: 2.23 us -> 4.35 us  [per_device(): pl.pallas_call(functools.partial(dense_kernel, rows_dev), out_shape=(matr...]
    ppermute x4, waiting for transfers between devices: 2.47 us -> 0.63 us  [swap(): return lax.ppermute(value, 'row', [(i, i ^ mask) for i in range(pieces)])]
    ppermute x12, starting transfers between devices: 17.7 us -> 16.9 us  [exchange(): fetched.append(lax.ppermute(value, ('row', 'col'), pairs))]
  transfers between devices with their start and end apart: 30 -> 30, of which waited for: 13 -> 13; matrix products, arithmetic and copies ran while one was open for 0% -> 0% of each run, Pallas kernels for 10% -> 15%
where the time goes in v20:
time: 60 us; the launch traced here: 59.8 us
  starting transfers between devices  28.5 us (48%)
  Pallas kernels  18.5 us (31%)
  waiting for transfers between devices  11.2 us (19%)
  between operations  1.46 us (2%)
    ppermute x12, starting transfers between devices, exchange(): fetched.append(lax.ppermute(value, ('row', 'col'), pairs))  16.9 us
    ppermute x12, waiting for transfers between devices, exchange(): fetched.append(lax.ppermute(value, ('row', 'col'), pairs))  7.53 us
    ppermute x4, starting transfers between devices, swap(): return lax.ppermute(value, 'row', [(i, i ^ mask) for i in range(pieces)])  7.27 us
    pallas_call x2, Pallas kernels, per_device(): pl.pallas_call(functools.partial(step_kernel, len(found), places, not fir...  5.56 us
    ppermute x14, starting transfers between devices, across(): lax.ppermute(value, 'col', [(i, (i + 1) % col_devices) for i in range(col...  4.42 us
    pallas_call x1, Pallas kernels, per_device(): pl.pallas_call(functools.partial(dense_kernel, rows_dev), out_shape=(matr...  4.35 us
    ppermute x14, waiting for transfers between devices, across(): lax.ppermute(value, 'col', [(i, (i + 1) % col_devices) for i in range(col...  3.06 us
    pallas_call x1, Pallas kernels, per_device(): pl.pallas_call(functools.partial(gather_kernel, rows_dev), out_shape=(tot...  2.75 us
  transfers between devices with their start and end apart: 30, of which 13 were waited for; matrix products, arithmetic and copies ran while one was open for 0% of the time, Pallas kernels for 15%

profile of v20, /device:TPU:0, one launch (start us, length us, event | category | flops | bytes accessed | tf_op | source)
XLA Modules:
  0.0 59.8 jit_solution(8294606285545522141)
XLA Ops:
  0.6 0.9 %message.1 = (bf16[48,256]{1,0:T(8,128)(2,1)S(1)}, f32[32,128]{1,0:T(8,128)S(1)}) custom-call(s32[32,256]{1,0:T(8,128)} %signs_hbm.1, f32[256]{0:T(256)} %weight_hbm.1, f32[32]{0:T(128)} %scale_hbm.1), custom_call_target="tpu_custom_call" | custom-call | tf_op jit(solution)/shard_map/message/pallas_call | solution.py:503
  1.5 4.1 %collective-permute-start = (bf16[48,256]{1,0:T(8,128)(2,1)S(1)}, bf16[48,256]{1,0:T(8,128)(2,1)S(1)}, u32[]{:S(2)}, u32[]{:S(2)}) collective-permute-start(bf16[48,256]{1,0:T(8,128)(2,1)S(1)} %get-tuple-element.26.refs_3_), channel_id=1, source_target_pairs={{0,8},{2,10},{4,12},{6,14},{8,0},{10,2},{12,4},{14,6},{1,9},{3,11}... | collective-permute-start | bytes 73736 | tf_op jit(solution)/shard_map/ppermute | solution.py:472
  5.6 1.3 %collective-permute-start.1 = (bf16[48,256]{1,0:T(8,128)(2,1)S(1)}, bf16[48,256]{1,0:T(8,128)(2,1)S(1)}, u32[]{:S(2)}, u32[]{:S(2)}) collective-permute-start(bf16[48,256]{1,0:T(8,128)(2,1)S(1)} %get-tuple-element.26.refs_3_), channel_id=1, source_target_pairs={{0,12},{2,14},{4,8},{6,10},{8,4},{10,6},{12,0},{14,2},{1,13},{3,15... | collective-permute-start | bytes 73736 | tf_op jit(solution)/shard_map/ppermute | solution.py:472
  7.0 0.2 collective-permute-start.2
  7.8 2.8 %gather.1 = (f32[64,128,128]{2,1,0:T(8,128)S(1)}, bf16[65,128,128]{2,1,0:T(8,128)(2,1)S(1)}) custom-call(s32[1]{0:T(128)S(6)} %copy.11.count_ref, s32[130]{0:T(256)} %rows_hbm.3, s32[130]{0:T(256)} %cols_hbm.3, bf16[130,128,128]{2,1,0:T(8,128)(2,1)} %tiles_ref.1), custom_call_target="tpu_custom_call" | custom-call | flops 8519680 | bytes 8519680 | tf_op jit(solution)/shard_map/gather/pallas_call | solution.py:527
  10.6 0.0 collective-permute-done.refs_0_
  10.6 0.6 %collective-permute-done.1.refs_1_ = bf16[48,256]{1,0:T(8,128)(2,1)S(1)} collective-permute-done((bf16[48,256]{1,0:T(8,128)(2,1)S(1)}, bf16[48,256]{1,0:T(8,128)(2,1)S(1)}, u32[]{:S(2)}, u32[]{:S(2)}) %collective-permute-start.1) | collective-permute-done | bytes 24608 | tf_op jit(solution)/shard_map/ppermute | solution.py:472
  11.2 0.1 collective-permute-start.3
  11.3 1.6 %collective-permute-start.4 = (bf16[4,48,256]{2,1,0:T(8,128)(2,1)S(1)}, bf16[4,48,256]{2,1,0:T(8,128)(2,1)S(1)}, u32[]{:S(2)}, u32[]{:S(2)}) collective-permute-start(bf16[4,48,256]{2,1,0:T(8,128)(2,1)S(1)} %join.1.joined_ref.even_ref), channel_id=1, source_target_pairs={{0,2},{2,0},{4,6},{6,4},{8,10},{10,8},{12,14},{14,12},{1,3},{3,1},... | collective-permute-start | bytes 294920 | tf_op jit(solution)/shard_map/ppermute | solution.py:472
  12.9 4.4 %dense.1 = (bf16[2,2048,512]{2,1,0:T(8,128)(2,1)S(1)}, f32[64,128,128]{2,1,0:T(8,128)S(1)}) custom-call(s32[1]{0:T(128)S(6)} %copy.11.count_ref, s32[130]{0:T(256)} %rows_hbm.3, s32[130]{0:T(256)} %cols_hbm.3, bf16[65,128,128]{2,1,0:T(8,128)(2,1)S(1)} %get-tuple-element.29.rest, ...), custom_call_target="tpu_custom_call", output_to_operand_aliasing={{1}: (4, {})} | custom-call | flops 8519680 | bytes 8519680 | tf_op jit(solution)/shard_map/dense/pallas_call | solution.py:554
  17.3 0.0 collective-permute-done.4.odd_ref
  17.3 0.8 %first.1 = (f32[32,640]{1,0:T(8,128)S(1)}, f32[2,32,256]{2,1,0:T(8,128)S(1)}, bf16[4,48,256]{2,1,0:T(8,128)(2,1)S(1)}) custom-call(bf16[4,48,256]{2,1,0:T(8,128)(2,1)S(1)} %join.1.joined_ref.even_ref, bf16[4,48,256]{2,1,0:T(8,128)(2,1)S(1)} %collective-permute-done.3.far_even_ref, bf16[4,48,256]{2,1,0:T(8,128)(2,1)S(1)} %collective-permute-done.4.odd_ref, ...), custom_call_target="tpu_custom_call" | custom-call | tf_op jit(solution)/shard_map/first/pallas_call | solution.py:573
  18.1 0.2 collective-permute-start.5
  18.3 1.1 %collective-permute-done.5.other_ref = f32[32,640]{1,0:T(8,128)S(1)} collective-permute-done((f32[32,640]{1,0:T(8,128)S(1)}, f32[32,640]{1,0:T(8,128)S(1)}, u32[]{:S(2)}, u32[]{:S(2)}) %collective-permute-start.5) | collective-permute-done | bytes 81952 | tf_op jit(solution)/shard_map/ppermute | solution.py:475
  19.4 0.3 image.2
  19.8 2.4 %collective-permute-start.6 = (f32[136,128]{1,0:T(8,128)S(1)}, f32[136,128]{1,0:T(8,128)S(1)}, u32[]{:S(2)}, u32[]{:S(2)}) collective-permute-start(f32[136,128]{1,0:T(8,128)S(1)} %get-tuple-element.33.refs_0_), channel_id=1, source_target_pairs={{0,14},{2,12},{4,10},{6,8},{8,6},{10,4},{12,2},{14,0},{1,11},{3,9}... | collective-permute-start | bytes 208904 | tf_op jit(solution)/shard_map/ppermute | solution.py:492
  22.1 0.4 collective-permute-start.7
  22.5 1.6 %collective-permute-start.8 = (f32[136,128]{1,0:T(8,128)S(1)}, f32[136,128]{1,0:T(8,128)S(1)}, u32[]{:S(2)}, u32[]{:S(2)}) collective-permute-start(f32[136,128]{1,0:T(8,128)S(1)} %get-tuple-element.33.refs_0_), channel_id=1, source_target_pairs={{0,4},{2,6},{4,0},{6,2},{8,12},{10,14},{12,8},{14,10},{1,9},{3,11}... | collective-permute-start | bytes 208904 | tf_op jit(solution)/shard_map/ppermute | solution.py:492
  24.1 0.0 collective-permute-start.13
  24.1 1.5 %collective-permute-start.9 = (f32[136,128]{1,0:T(8,128)S(1)}, f32[136,128]{1,0:T(8,128)S(1)}, u32[]{:S(2)}, u32[]{:S(2)}) collective-permute-start(f32[136,128]{1,0:T(8,128)S(1)} %get-tuple-element.33.refs_0_), channel_id=1, source_target_pairs={{0,2},{2,0},{4,6},{6,4},{8,10},{10,8},{12,14},{14,12},{1,3},{3,1},... | collective-permute-start | bytes 208904 | tf_op jit(solution)/shard_map/ppermute | solution.py:492
  25.6 1.9 %collective-permute-done.6.refs_1_ = f32[136,128]{1,0:T(8,128)S(1)} collective-permute-done((f32[136,128]{1,0:T(8,128)S(1)}, f32[136,128]{1,0:T(8,128)S(1)}, u32[]{:S(2)}, u32[]{:S(2)}) %collective-permute-start.6) | collective-permute-done | bytes 69664 | tf_op jit(solution)/shard_map/ppermute | solution.py:492
  27.6 0.9 %collective-permute-done.7.refs_2_ = f32[136,128]{1,0:T(8,128)S(1)} collective-permute-done((f32[136,128]{1,0:T(8,128)S(1)}, f32[136,128]{1,0:T(8,128)S(1)}, u32[]{:S(2)}, u32[]{:S(2)}) %collective-permute-start.7) | collective-permute-done | bytes 69664 | tf_op jit(solution)/shard_map/ppermute | solution.py:492
  28.5 0.0 collective-permute-start.11
  28.5 0.0 collective-permute-done.8.refs_3_
  28.5 0.9 %collective-permute-start.12 = (f32[136,128]{1,0:T(8,128)S(1)}, f32[136,128]{1,0:T(8,128)S(1)}, u32[]{:S(2)}, u32[]{:S(2)}) collective-permute-start(f32[136,128]{1,0:T(8,128)S(1)} %collective-permute-done.8.refs_3_), channel_id=1, source_target_pairs={{0,1},{1,0},{2,3},{3,2},{4,5},{5,4},{6,7},{7,6},{8,9},{9,8},{10,11... | collective-permute-start | bytes 208904 | tf_op jit(solution)/shard_map/ppermute | solution.py:475
  29.4 0.8 %inverse.2.refs_11_ = f32[32,128]{1,0:T(8,128)S(1)} custom-call(f32[32,128]{1,0:T(8,128)S(1)} %get-tuple-element.37.norm_ref.refs_10_), custom_call_target="tpu_custom_call" | custom-call | tf_op jit(solution)/shard_map/inverse/pallas_call | solution.py:608
  30.2 0.0 collective-permute-done.13.far_odd_ref
  30.2 0.1 collect.1
  30.3 0.0 collective-permute-done.9.refs_4_
  30.3 0.0 collective-permute-done.11.refs_6_
  30.3 0.0 collective-permute-done.12.refs_7_
  30.3 2.8 %step.2 = (f32[32,512]{1,0:T(8,128)S(1)}, f32[9,32,256]{2,1,0:T(8,128)S(1)}, f32[2,8,32,256]{3,2,1,0:T(8,128)S(1)}, f32[32,128]{1,0:T(8,128)S(1)}, f32[32,256]{1,0:T(8,128)S(1)}) custom-call(f32[136,128]{1,0:T(8,128)S(1)} %get-tuple-element.33.refs_0_, f32[136,128]{1,0:T(8,128)S(1)} %collective-permute-done.6.refs_1_, ...), custom_call_target="tpu_custom_call" | custom-call | tf_op jit(solution)/shard_map/step/pallas_call | solution.py:617
  33.1 0.3 collective-permute-start.14
  33.5 0.9 %collective-permute-done.14.other_ref = f32[32,512]{1,0:T(8,128)S(1)} collective-permute-done((f32[32,512]{1,0:T(8,128)S(1)}, f32[32,512]{1,0:T(8,128)S(1)}, u32[]{:S(2)}, u32[]{:S(2)}) %collective-permute-start.14) | collective-permute-done | bytes 65568 | tf_op jit(solution)/shard_map/ppermute | solution.py:475
  34.4 0.3 image.3.refs_0_
  34.8 2.1 %collective-permute-start.15 = (f32[136,128]{1,0:T(8,128)S(1)}, f32[136,128]{1,0:T(8,128)S(1)}, u32[]{:S(2)}, u32[]{:S(2)}) collective-permute-start(f32[136,128]{1,0:T(8,128)S(1)} %image.3.refs_0_), channel_id=1, source_target_pairs={{0,14},{2,12},{4,10},{6,8},{8,6},{10,4},{12,2},{14,0},{1,11},{3,9}... | collective-permute-start | bytes 208904 | tf_op jit(solution)/shard_map/ppermute | solution.py:492
  36.9 0.7 %collective-permute-start.16 = (f32[136,128]{1,0:T(8,128)S(1)}, f32[136,128]{1,0:T(8,128)S(1)}, u32[]{:S(2)}, u32[]{:S(2)}) collective-permute-start(f32[136,128]{1,0:T(8,128)S(1)} %image.3.refs_0_), channel_id=1, source_target_pairs={{0,6},{2,4},{4,2},{6,0},{8,14},{10,12},{12,10},{14,8},{1,13},{3,15... | collective-permute-start | bytes 208904 | tf_op jit(solution)/shard_map/ppermute | solution.py:492
  37.6 2.3 %collective-permute-start.17 = (f32[136,128]{1,0:T(8,128)S(1)}, f32[136,128]{1,0:T(8,128)S(1)}, u32[]{:S(2)}, u32[]{:S(2)}) collective-permute-start(f32[136,128]{1,0:T(8,128)S(1)} %image.3.refs_0_), channel_id=1, source_target_pairs={{0,4},{2,6},{4,0},{6,2},{8,12},{10,14},{12,8},{14,10},{1,9},{3,11}... | collective-permute-start | bytes 208904 | tf_op jit(solution)/shard_map/ppermute | solution.py:492
  39.8 0.5 collective-permute-start.18
  40.4 2.1 %collective-permute-done.15.refs_1_ = f32[136,128]{1,0:T(8,128)S(1)} collective-permute-done((f32[136,128]{1,0:T(8,128)S(1)}, f32[136,128]{1,0:T(8,128)S(1)}, u32[]{:S(2)}, u32[]{:S(2)}) %collective-permute-start.15) | collective-permute-done | bytes 69664 | tf_op jit(solution)/shard_map/ppermute | solution.py:492
  42.4 0.3 collective-permute-start.19
  42.7 0.9 %collective-permute-done.16.refs_2_ = f32[136,128]{1,0:T(8,128)S(1)} collective-permute-done((f32[136,128]{1,0:T(8,128)S(1)}, f32[136,128]{1,0:T(8,128)S(1)}, u32[]{:S(2)}, u32[]{:S(2)}) %collective-permute-start.16) | collective-permute-done | bytes 69664 | tf_op jit(solution)/shard_map/ppermute | solution.py:492
  43.6 0.0 collective-permute-start.20
  43.6 0.2 collective-permute-done.17.refs_3_
  43.8 0.9 %collective-permute-start.21 = (f32[136,128]{1,0:T(8,128)S(1)}, f32[136,128]{1,0:T(8,128)S(1)}, u32[]{:S(2)}, u32[]{:S(2)}) collective-permute-start(f32[136,128]{1,0:T(8,128)S(1)} %collective-permute-done.17.refs_3_), channel_id=1, source_target_pairs={{0,1},{1,0},{2,3},{3,2},{4,5},{5,4},{6,7},{7,6},{8,9},{9,8},{10,11... | collective-permute-start | bytes 208904 | tf_op jit(solution)/shard_map/ppermute | solution.py:475
  44.7 0.8 %inverse.3.refs_11_ = f32[32,128]{1,0:T(8,128)S(1)} custom-call(f32[32,128]{1,0:T(8,128)S(1)} %get-tuple-element.41.norm_ref.refs_10_), custom_call_target="tpu_custom_call" | custom-call | tf_op jit(solution)/shard_map/inverse/pallas_call | solution.py:608
  45.4 0.0 collective-permute-done.18.refs_4_
  45.5 0.0 collective-permute-done.20.refs_6_
  45.5 0.1 collective-permute-done.21.refs_7_
  45.6 2.8 %step.3 = (f32[32,512]{1,0:T(8,128)S(1)}, f32[2,32,256]{2,1,0:T(8,128)S(1)}, f32[32,256]{1,0:T(8,128)S(1)}, f32[32,128]{1,0:T(8,128)S(1)}, f32[32,256]{1,0:T(8,128)S(1)}) custom-call(f32[136,128]{1,0:T(8,128)S(1)} %image.3.refs_0_, f32[136,128]{1,0:T(8,128)S(1)} %collective-permute-done.15.refs_1_, f32[136,128]{1,0:T(8,128)S(1)} %collective-permute-done.16.refs_2_, ...), custom_call_target="tpu_custom_call" | custom-call | tf_op jit(solution)/shard_map/step/pallas_call | solution.py:617
  48.3 0.4 collective-permute-start.22
  48.7 0.9 %collective-permute-done.22.other_ref = f32[32,512]{1,0:T(8,128)S(1)} collective-permute-done((f32[32,512]{1,0:T(8,128)S(1)}, f32[32,512]{1,0:T(8,128)S(1)}, u32[]{:S(2)}, u32[]{:S(2)}) %collective-permute-start.22) | collective-permute-done | bytes 65568 | tf_op jit(solution)/shard_map/ppermute | solution.py:475
  49.6 0.3 last_image.1
  50.0 1.9 %collective-permute-start.23 = (f32[8,128]{1,0:T(8,128)S(1)}, f32[8,128]{1,0:T(8,128)S(1)}, u32[]{:S(2)}, u32[]{:S(2)}) collective-permute-start(f32[8,128]{1,0:T(8,128)S(1)} %get-tuple-element.45.refs_0_), channel_id=1, source_target_pairs={{0,12},{2,14},{4,8},{6,10},{8,4},{10,6},{12,0},{14,2},{1,15},{3,13... | collective-permute-start | bytes 12296 | tf_op jit(solution)/shard_map/ppermute | solution.py:492
  51.9 1.1 %collective-permute-start.24 = (f32[8,128]{1,0:T(8,128)S(1)}, f32[8,128]{1,0:T(8,128)S(1)}, u32[]{:S(2)}, u32[]{:S(2)}) collective-permute-start(f32[8,128]{1,0:T(8,128)S(1)} %get-tuple-element.45.refs_0_), channel_id=1, source_target_pairs={{0,6},{2,4},{4,2},{6,0},{8,14},{10,12},{12,10},{14,8},{1,11},{3,9}... | collective-permute-start | bytes 12296 | tf_op jit(solution)/shard_map/ppermute | solution.py:492
  52.9 1.7 %collective-permute-start.25 = (f32[8,128]{1,0:T(8,128)S(1)}, f32[8,128]{1,0:T(8,128)S(1)}, u32[]{:S(2)}, u32[]{:S(2)}) collective-permute-start(f32[8,128]{1,0:T(8,128)S(1)} %get-tuple-element.45.refs_0_), channel_id=1, source_target_pairs={{0,4},{2,6},{4,0},{6,2},{8,12},{10,14},{12,8},{14,10},{1,9},{3,11}... | collective-permute-start | bytes 12296 | tf_op jit(solution)/shard_map/ppermute | solution.py:492
  54.6 0.8 %collective-permute-start.26 = (f32[8,128]{1,0:T(8,128)S(1)}, f32[8,128]{1,0:T(8,128)S(1)}, u32[]{:S(2)}, u32[]{:S(2)}) collective-permute-start(f32[8,128]{1,0:T(8,128)S(1)} %get-tuple-element.45.refs_0_), channel_id=1, source_target_pairs={{0,2},{2,0},{4,6},{6,4},{8,10},{10,8},{12,14},{14,12},{1,3},{3,1},... | collective-permute-start | bytes 12296 | tf_op jit(solution)/shard_map/ppermute | solution.py:492
  55.4 0.1 collective-permute-done.23.refs_1_
  55.4 0.8 %collective-permute-start.27 = (f32[8,128]{1,0:T(8,128)S(1)}, f32[8,128]{1,0:T(8,128)S(1)}, u32[]{:S(2)}, u32[]{:S(2)}) collective-permute-start(f32[8,128]{1,0:T(8,128)S(1)} %collective-permute-done.23.refs_1_), channel_id=1, source_target_pairs={{0,1},{1,0},{2,3},{3,2},{4,5},{5,4},{6,7},{7,6},{8,9},{9,8},{10,11... | collective-permute-start | bytes 12296 | tf_op jit(solution)/shard_map/ppermute | solution.py:475
  56.2 0.2 collective-permute-done.24.refs_2_
  56.4 0.5 collective-permute-start.28
  56.9 0.0 collective-permute-start.29
  56.9 1.3 %collective-permute-done.26.refs_4_ = f32[8,128]{1,0:T(8,128)S(1)} collective-permute-done((f32[8,128]{1,0:T(8,128)S(1)}, f32[8,128]{1,0:T(8,128)S(1)}, u32[]{:S(2)}, u32[]{:S(2)}) %collective-permute-start.26) | collective-permute-done | bytes 4128 | tf_op jit(solution)/shard_map/ppermute | solution.py:492
  58.2 1.5 %last.1 = (f32[32,256]{1,0:T(8,128)}, f32[32,256]{1,0:T(8,128)}) custom-call(f32[8,128]{1,0:T(8,128)S(1)} %get-tuple-element.45.refs_0_, f32[8,128]{1,0:T(8,128)S(1)} %collective-permute-done.23.refs_1_, f32[8,128]{1,0:T(8,128)S(1)} %collective-permute-done.24.refs_2_, f32[8,128]{1,0:T(8,128)S(1)} %collective-permute-done.25.refs_3_, ...), custom_call_target="tpu_custom_call" | custom-call | tf_op jit(solution)/shard_map/last/pallas_call | solution.py:640
  (10 shorter events, 0.0 us)
Async XLA Ops:
  1.5 9.1 %collective-permute-start = (bf16[48,256]{1,0:T(8,128)(2,1)S(1)}, bf16[48,256]{1,0:T(8,128)(2,1)S(1)}, u32[]{:S(2)}, u32[]{:S(2)}) collective-permute-start(bf16[48,256]{1,0:T(8,128)(2,1)S(1)} %get-tuple-element.26.refs_3_), channel_id=1, source_target_pairs={{0,8},{2,10},{4,12},{6,14},{8,0},{10,2},{12,4},{14,6},{1,9},{3,11}... | collective-permute-start | bytes 73736 | tf_op jit(solution)/shard_map/ppermute | solution.py:472
  5.6 5.6 %collective-permute-start.1 = (bf16[48,256]{1,0:T(8,128)(2,1)S(1)}, bf16[48,256]{1,0:T(8,128)(2,1)S(1)}, u32[]{:S(2)}, u32[]{:S(2)}) collective-permute-start(bf16[48,256]{1,0:T(8,128)(2,1)S(1)} %get-tuple-element.26.refs_3_), channel_id=1, source_target_pairs={{0,12},{2,14},{4,8},{6,10},{8,4},{10,6},{12,0},{14,2},{1,13},{3,15... | collective-permute-start | bytes 73736 | tf_op jit(solution)/shard_map/ppermute | solution.py:472
  7.0 4.3 %collective-permute-start.2 = (bf16[48,256]{1,0:T(8,128)(2,1)S(1)}, bf16[48,256]{1,0:T(8,128)(2,1)S(1)}, u32[]{:S(2)}, u32[]{:S(2)}) collective-permute-start(bf16[48,256]{1,0:T(8,128)(2,1)S(1)} %get-tuple-element.26.refs_3_), channel_id=1, source_target_pairs={{0,4},{2,6},{4,0},{6,2},{8,12},{10,14},{12,8},{14,10},{1,5},{3,7},... | collective-permute-start | bytes 73736 | tf_op jit(solution)/shard_map/ppermute | solution.py:472
  11.2 6.0 %collective-permute-start.3 = (bf16[4,48,256]{2,1,0:T(8,128)(2,1)S(1)}, bf16[4,48,256]{2,1,0:T(8,128)(2,1)S(1)}, u32[]{:S(2)}, u32[]{:S(2)}) collective-permute-start(bf16[4,48,256]{2,1,0:T(8,128)(2,1)S(1)} %join.1.joined_ref.even_ref), channel_id=1, source_target_pairs={{0,1},{1,0},{2,3},{3,2},{4,5},{5,4},{6,7},{7,6},{8,9},{9,8},{10,11... | collective-permute-start | bytes 294920 | tf_op jit(solution)/shard_map/ppermute | solution.py:475
  11.3 6.0 %collective-permute-start.4 = (bf16[4,48,256]{2,1,0:T(8,128)(2,1)S(1)}, bf16[4,48,256]{2,1,0:T(8,128)(2,1)S(1)}, u32[]{:S(2)}, u32[]{:S(2)}) collective-permute-start(bf16[4,48,256]{2,1,0:T(8,128)(2,1)S(1)} %join.1.joined_ref.even_ref), channel_id=1, source_target_pairs={{0,2},{2,0},{4,6},{6,4},{8,10},{10,8},{12,14},{14,12},{1,3},{3,1},... | collective-permute-start | bytes 294920 | tf_op jit(solution)/shard_map/ppermute | solution.py:472
  18.1 1.3 %collective-permute-start.5 = (f32[32,640]{1,0:T(8,128)S(1)}, f32[32,640]{1,0:T(8,128)S(1)}, u32[]{:S(2)}, u32[]{:S(2)}) collective-permute-start(f32[32,640]{1,0:T(8,128)S(1)} %get-tuple-element.31.mine_ref), channel_id=1, source_target_pairs={{0,1},{1,0},{2,3},{3,2},{4,5},{5,4},{6,7},{7,6},{8,9},{9,8},{10,11... | collective-permute-start | bytes 245768 | tf_op jit(solution)/shard_map/ppermute | solution.py:475
  19.8 7.8 %collective-permute-start.6 = (f32[136,128]{1,0:T(8,128)S(1)}, f32[136,128]{1,0:T(8,128)S(1)}, u32[]{:S(2)}, u32[]{:S(2)}) collective-permute-start(f32[136,128]{1,0:T(8,128)S(1)} %get-tuple-element.33.refs_0_), channel_id=1, source_target_pairs={{0,14},{2,12},{4,10},{6,8},{8,6},{10,4},{12,2},{14,0},{1,11},{3,9}... | collective-permute-start | bytes 208904 | tf_op jit(solution)/shard_map/ppermute | solution.py:492
  22.1 6.3 %collective-permute-start.7 = (f32[136,128]{1,0:T(8,128)S(1)}, f32[136,128]{1,0:T(8,128)S(1)}, u32[]{:S(2)}, u32[]{:S(2)}) collective-permute-start(f32[136,128]{1,0:T(8,128)S(1)} %get-tuple-element.33.refs_0_), channel_id=1, source_target_pairs={{0,6},{2,4},{4,2},{6,0},{8,14},{10,12},{12,10},{14,8},{1,13},{3,15... | collective-permute-start | bytes 208904 | tf_op jit(solution)/shard_map/ppermute | solution.py:492
  22.5 6.0 %collective-permute-start.8 = (f32[136,128]{1,0:T(8,128)S(1)}, f32[136,128]{1,0:T(8,128)S(1)}, u32[]{:S(2)}, u32[]{:S(2)}) collective-permute-start(f32[136,128]{1,0:T(8,128)S(1)} %get-tuple-element.33.refs_0_), channel_id=1, source_target_pairs={{0,4},{2,6},{4,0},{6,2},{8,12},{10,14},{12,8},{14,10},{1,9},{3,11}... | collective-permute-start | bytes 208904 | tf_op jit(solution)/shard_map/ppermute | solution.py:492
  24.1 6.1 %collective-permute-start.13 = (bf16[4,48,256]{2,1,0:T(8,128)(2,1)S(1)}, bf16[4,48,256]{2,1,0:T(8,128)(2,1)S(1)}, u32[]{:S(2)}, u32[]{:S(2)}) collective-permute-start(bf16[4,48,256]{2,1,0:T(8,128)(2,1)S(1)} %get-tuple-element.34.odd_ref), channel_id=1, source_target_pairs={{0,1},{1,0},{2,3},{3,2},{4,5},{5,4},{6,7},{7,6},{8,9},{9,8},{10,11... | collective-permute-start | bytes 294920 | tf_op jit(solution)/shard_map/ppermute | solution.py:475
  24.1 6.2 %collective-permute-start.9 = (f32[136,128]{1,0:T(8,128)S(1)}, f32[136,128]{1,0:T(8,128)S(1)}, u32[]{:S(2)}, u32[]{:S(2)}) collective-permute-start(f32[136,128]{1,0:T(8,128)S(1)} %get-tuple-element.33.refs_0_), channel_id=1, source_target_pairs={{0,2},{2,0},{4,6},{6,4},{8,10},{10,8},{12,14},{14,12},{1,3},{3,1},... | collective-permute-start | bytes 208904 | tf_op jit(solution)/shard_map/ppermute | solution.py:492
  27.6 2.7 %collective-permute-start.10 = (f32[136,128]{1,0:T(8,128)S(1)}, f32[136,128]{1,0:T(8,128)S(1)}, u32[]{:S(2)}, u32[]{:S(2)}) collective-permute-start(f32[136,128]{1,0:T(8,128)S(1)} %collective-permute-done.6.refs_1_), channel_id=1, source_target_pairs={{0,1},{1,0},{2,3},{3,2},{4,5},{5,4},{6,7},{7,6},{8,9},{9,8},{10,11... | collective-permute-start | bytes 208904 | tf_op jit(solution)/shard_map/ppermute | solution.py:475
  28.5 1.9 %collective-permute-start.11 = (f32[136,128]{1,0:T(8,128)S(1)}, f32[136,128]{1,0:T(8,128)S(1)}, u32[]{:S(2)}, u32[]{:S(2)}) collective-permute-start(f32[136,128]{1,0:T(8,128)S(1)} %collective-permute-done.7.refs_2_), channel_id=1, source_target_pairs={{0,1},{1,0},{2,3},{3,2},{4,5},{5,4},{6,7},{7,6},{8,9},{9,8},{10,11... | collective-permute-start | bytes 208904 | tf_op jit(solution)/shard_map/ppermute | solution.py:475
  28.5 1.9 %collective-permute-start.12 = (f32[136,128]{1,0:T(8,128)S(1)}, f32[136,128]{1,0:T(8,128)S(1)}, u32[]{:S(2)}, u32[]{:S(2)}) collective-permute-start(f32[136,128]{1,0:T(8,128)S(1)} %collective-permute-done.8.refs_3_), channel_id=1, source_target_pairs={{0,1},{1,0},{2,3},{3,2},{4,5},{5,4},{6,7},{7,6},{8,9},{9,8},{10,11... | collective-permute-start | bytes 208904 | tf_op jit(solution)/shard_map/ppermute | solution.py:475
  33.1 1.3 %collective-permute-start.14 = (f32[32,512]{1,0:T(8,128)S(1)}, f32[32,512]{1,0:T(8,128)S(1)}, u32[]{:S(2)}, u32[]{:S(2)}) collective-permute-start(f32[32,512]{1,0:T(8,128)S(1)} %get-tuple-element.38.mine_ref), channel_id=1, source_target_pairs={{0,1},{1,0},{2,3},{3,2},{4,5},{5,4},{6,7},{7,6},{8,9},{9,8},{10,11... | collective-permute-start | bytes 196616 | tf_op jit(solution)/shard_map/ppermute | solution.py:475
  34.8 7.7 %collective-permute-start.15 = (f32[136,128]{1,0:T(8,128)S(1)}, f32[136,128]{1,0:T(8,128)S(1)}, u32[]{:S(2)}, u32[]{:S(2)}) collective-permute-start(f32[136,128]{1,0:T(8,128)S(1)} %image.3.refs_0_), channel_id=1, source_target_pairs={{0,14},{2,12},{4,10},{6,8},{8,6},{10,4},{12,2},{14,0},{1,11},{3,9}... | collective-permute-start | bytes 208904 | tf_op jit(solution)/shard_map/ppermute | solution.py:492
  36.9 6.7 %collective-permute-start.16 = (f32[136,128]{1,0:T(8,128)S(1)}, f32[136,128]{1,0:T(8,128)S(1)}, u32[]{:S(2)}, u32[]{:S(2)}) collective-permute-start(f32[136,128]{1,0:T(8,128)S(1)} %image.3.refs_0_), channel_id=1, source_target_pairs={{0,6},{2,4},{4,2},{6,0},{8,14},{10,12},{12,10},{14,8},{1,13},{3,15... | collective-permute-start | bytes 208904 | tf_op jit(solution)/shard_map/ppermute | solution.py:492
  37.6 6.2 %collective-permute-start.17 = (f32[136,128]{1,0:T(8,128)S(1)}, f32[136,128]{1,0:T(8,128)S(1)}, u32[]{:S(2)}, u32[]{:S(2)}) collective-permute-start(f32[136,128]{1,0:T(8,128)S(1)} %image.3.refs_0_), channel_id=1, source_target_pairs={{0,4},{2,6},{4,0},{6,2},{8,12},{10,14},{12,8},{14,10},{1,9},{3,11}... | collective-permute-start | bytes 208904 | tf_op jit(solution)/shard_map/ppermute | solution.py:492
  39.8 5.6 %collective-permute-start.18 = (f32[136,128]{1,0:T(8,128)S(1)}, f32[136,128]{1,0:T(8,128)S(1)}, u32[]{:S(2)}, u32[]{:S(2)}) collective-permute-start(f32[136,128]{1,0:T(8,128)S(1)} %image.3.refs_0_), channel_id=1, source_target_pairs={{0,2},{2,0},{4,6},{6,4},{8,10},{10,8},{12,14},{14,12},{1,3},{3,1},... | collective-permute-start | bytes 208904 | tf_op jit(solution)/shard_map/ppermute | solution.py:492
  42.4 3.0 %collective-permute-start.19 = (f32[136,128]{1,0:T(8,128)S(1)}, f32[136,128]{1,0:T(8,128)S(1)}, u32[]{:S(2)}, u32[]{:S(2)}) collective-permute-start(f32[136,128]{1,0:T(8,128)S(1)} %collective-permute-done.15.refs_1_), channel_id=1, source_target_pairs={{0,1},{1,0},{2,3},{3,2},{4,5},{5,4},{6,7},{7,6},{8,9},{9,8},{10,11... | collective-permute-start | bytes 208904 | tf_op jit(solution)/shard_map/ppermute | solution.py:475
  43.6 1.9 %collective-permute-start.20 = (f32[136,128]{1,0:T(8,128)S(1)}, f32[136,128]{1,0:T(8,128)S(1)}, u32[]{:S(2)}, u32[]{:S(2)}) collective-permute-start(f32[136,128]{1,0:T(8,128)S(1)} %collective-permute-done.16.refs_2_), channel_id=1, source_target_pairs={{0,1},{1,0},{2,3},{3,2},{4,5},{5,4},{6,7},{7,6},{8,9},{9,8},{10,11... | collective-permute-start | bytes 208904 | tf_op jit(solution)/shard_map/ppermute | solution.py:475
  43.8 1.8 %collective-permute-start.21 = (f32[136,128]{1,0:T(8,128)S(1)}, f32[136,128]{1,0:T(8,128)S(1)}, u32[]{:S(2)}, u32[]{:S(2)}) collective-permute-start(f32[136,128]{1,0:T(8,128)S(1)} %collective-permute-done.17.refs_3_), channel_id=1, source_target_pairs={{0,1},{1,0},{2,3},{3,2},{4,5},{5,4},{6,7},{7,6},{8,9},{9,8},{10,11... | collective-permute-start | bytes 208904 | tf_op jit(solution)/shard_map/ppermute | solution.py:475
  48.3 1.3 %collective-permute-start.22 = (f32[32,512]{1,0:T(8,128)S(1)}, f32[32,512]{1,0:T(8,128)S(1)}, u32[]{:S(2)}, u32[]{:S(2)}) collective-permute-start(f32[32,512]{1,0:T(8,128)S(1)} %get-tuple-element.43.mine_ref), channel_id=1, source_target_pairs={{0,1},{1,0},{2,3},{3,2},{4,5},{5,4},{6,7},{7,6},{8,9},{9,8},{10,11... | collective-permute-start | bytes 196616 | tf_op jit(solution)/shard_map/ppermute | solution.py:475
  50.0 5.5 %collective-permute-start.23 = (f32[8,128]{1,0:T(8,128)S(1)}, f32[8,128]{1,0:T(8,128)S(1)}, u32[]{:S(2)}, u32[]{:S(2)}) collective-permute-start(f32[8,128]{1,0:T(8,128)S(1)} %get-tuple-element.45.refs_0_), channel_id=1, source_target_pairs={{0,12},{2,14},{4,8},{6,10},{8,4},{10,6},{12,0},{14,2},{1,15},{3,13... | collective-permute-start | bytes 12296 | tf_op jit(solution)/shard_map/ppermute | solution.py:492
  51.9 4.5 %collective-permute-start.24 = (f32[8,128]{1,0:T(8,128)S(1)}, f32[8,128]{1,0:T(8,128)S(1)}, u32[]{:S(2)}, u32[]{:S(2)}) collective-permute-start(f32[8,128]{1,0:T(8,128)S(1)} %get-tuple-element.45.refs_0_), channel_id=1, source_target_pairs={{0,6},{2,4},{4,2},{6,0},{8,14},{10,12},{12,10},{14,8},{1,11},{3,9}... | collective-permute-start | bytes 12296 | tf_op jit(solution)/shard_map/ppermute | solution.py:492
  52.9 4.0 %collective-permute-start.25 = (f32[8,128]{1,0:T(8,128)S(1)}, f32[8,128]{1,0:T(8,128)S(1)}, u32[]{:S(2)}, u32[]{:S(2)}) collective-permute-start(f32[8,128]{1,0:T(8,128)S(1)} %get-tuple-element.45.refs_0_), channel_id=1, source_target_pairs={{0,4},{2,6},{4,0},{6,2},{8,12},{10,14},{12,8},{14,10},{1,9},{3,11}... | collective-permute-start | bytes 12296 | tf_op jit(solution)/shard_map/ppermute | solution.py:492
  54.6 3.6 %collective-permute-start.26 = (f32[8,128]{1,0:T(8,128)S(1)}, f32[8,128]{1,0:T(8,128)S(1)}, u32[]{:S(2)}, u32[]{:S(2)}) collective-permute-start(f32[8,128]{1,0:T(8,128)S(1)} %get-tuple-element.45.refs_0_), channel_id=1, source_target_pairs={{0,2},{2,0},{4,6},{6,4},{8,10},{10,8},{12,14},{14,12},{1,3},{3,1},... | collective-permute-start | bytes 12296 | tf_op jit(solution)/shard_map/ppermute | solution.py:492
  55.4 2.8 %collective-permute-start.27 = (f32[8,128]{1,0:T(8,128)S(1)}, f32[8,128]{1,0:T(8,128)S(1)}, u32[]{:S(2)}, u32[]{:S(2)}) collective-permute-start(f32[8,128]{1,0:T(8,128)S(1)} %collective-permute-done.23.refs_1_), channel_id=1, source_target_pairs={{0,1},{1,0},{2,3},{3,2},{4,5},{5,4},{6,7},{7,6},{8,9},{9,8},{10,11... | collective-permute-start | bytes 12296 | tf_op jit(solution)/shard_map/ppermute | solution.py:475
  56.4 1.8 %collective-permute-start.28 = (f32[8,128]{1,0:T(8,128)S(1)}, f32[8,128]{1,0:T(8,128)S(1)}, u32[]{:S(2)}, u32[]{:S(2)}) collective-permute-start(f32[8,128]{1,0:T(8,128)S(1)} %collective-permute-done.24.refs_2_), channel_id=1, source_target_pairs={{0,1},{1,0},{2,3},{3,2},{4,5},{5,4},{6,7},{7,6},{8,9},{9,8},{10,11... | collective-permute-start | bytes 12296 | tf_op jit(solution)/shard_map/ppermute | solution.py:475
  56.9 1.3 %collective-permute-start.29 = (f32[8,128]{1,0:T(8,128)S(1)}, f32[8,128]{1,0:T(8,128)S(1)}, u32[]{:S(2)}, u32[]{:S(2)}) collective-permute-start(f32[8,128]{1,0:T(8,128)S(1)} %collective-permute-done.25.refs_3_), channel_id=1, source_target_pairs={{0,1},{1,0},{2,3},{3,2},{4,5},{5,4},{6,7},{7,6},{8,9},{9,8},{10,11... | collective-permute-start | bytes 12296 | tf_op jit(solution)/shard_map/ppermute | solution.py:475

commit v21 on v19

--- a/solution.py
+++ b/solution.py
@@ -11,7 +11,7 @@
 LANES = 128
 PIVOTS = 16
 TAIL = 16
-CHUNKS = 5
+CHUNKS = 4
 F32 = jnp.float32
 BF16 = jnp.bfloat16
 SPARE_BYTES = 4 * 1024 * 1024
@@ -512,7 +512,7 @@
     matrix = shape(2, depth, group, dtype=BF16)
     total = shape(depth // tile * (group // tile), tile, tile)
     slots = tiles.shape[0]
-    half = slots // 2
+    half = slots // 2 // (2 * CHUNKS) * (2 * CHUNKS)
     rest = shape(slots - half, tile, tile, dtype=BF16)
     lists = [pltpu.with_memory_space_constraint(x, pltpu.HBM) for x in (tile_rows, tile_cols)]
     lists_scratch = [pltpu.SMEM(x.shape, jnp.int32) for x in lists]

time: 59.6 us -> 59.7 us (level)
  no operation moved by 1% of the time
where the time goes in v21:
time: 59.7 us; the launch traced here: 59.5 us
  starting transfers between devices  29.2 us (49%)
  Pallas kernels  15.9 us (27%)
  waiting for transfers between devices  12.9 us (22%)
  between operations  1.46 us (2%)
    ppermute x12, starting transfers between devices, exchange(): fetched.append(lax.ppermute(value, ('row', 'col'), pairs))  17.6 us
    ppermute x4, starting transfers between devices, swap(): return lax.ppermute(value, 'row', [(i, i ^ mask) for i in range(pieces)])  7.27 us
    ppermute x12, waiting for transfers between devices, exchange(): fetched.append(lax.ppermute(value, ('row', 'col'), pairs))  7.18 us
    pallas_call x2, Pallas kernels, per_device(): pl.pallas_call(functools.partial(step_kernel, len(found), places, not fir...  5.56 us
    ppermute x14, starting transfers between devices, across(): lax.ppermute(value, 'col', [(i, (i + 1) % col_devices) for i in range(col...  4.31 us
    ppermute x14, waiting for transfers between devices, across(): lax.ppermute(value, 'col', [(i, (i + 1) % col_devices) for i in range(col...  3.21 us
    ppermute x4, waiting for transfers between devices, swap(): return lax.ppermute(value, 'row', [(i, i ^ mask) for i in range(pieces)])  2.49 us
    pallas_call x1, Pallas kernels, per_device(): pl.pallas_call(functools.partial(gather_kernel, rows_dev), out_shape=(tot...  2.26 us
  transfers between devices with their start and end apart: 30, of which 13 were waited for; matrix products, arithmetic and copies ran while one was open for 0% of the time, Pallas kernels for 10%

profile of v21, /device:TPU:0, one launch (start us, length us, event | category | flops | bytes accessed | tf_op | source)
XLA Modules:
  0.0 59.5 jit_solution(6838695258048935365)
XLA Ops:
  0.6 0.9 %message.1 = (bf16[48,256]{1,0:T(8,128)(2,1)S(1)}, f32[32,128]{1,0:T(8,128)S(1)}) custom-call(s32[32,256]{1,0:T(8,128)} %signs_hbm.1, f32[256]{0:T(256)} %weight_hbm.1, f32[32]{0:T(128)} %scale_hbm.1), custom_call_target="tpu_custom_call" | custom-call | tf_op jit(solution)/shard_map/message/pallas_call | solution.py:498
  1.5 4.1 %collective-permute-start = (bf16[48,256]{1,0:T(8,128)(2,1)S(1)}, bf16[48,256]{1,0:T(8,128)(2,1)S(1)}, u32[]{:S(2)}, u32[]{:S(2)}) collective-permute-start(bf16[48,256]{1,0:T(8,128)(2,1)S(1)} %get-tuple-element.26.refs_3_), channel_id=1, source_target_pairs={{0,8},{2,10},{4,12},{6,14},{8,0},{10,2},{12,4},{14,6},{1,9},{3,11}... | collective-permute-start | bytes 73736 | tf_op jit(solution)/shard_map/ppermute | solution.py:467
  5.6 1.3 %collective-permute-start.1 = (bf16[48,256]{1,0:T(8,128)(2,1)S(1)}, bf16[48,256]{1,0:T(8,128)(2,1)S(1)}, u32[]{:S(2)}, u32[]{:S(2)}) collective-permute-start(bf16[48,256]{1,0:T(8,128)(2,1)S(1)} %get-tuple-element.26.refs_3_), channel_id=1, source_target_pairs={{0,12},{2,14},{4,8},{6,10},{8,4},{10,6},{12,0},{14,2},{1,13},{3,15... | collective-permute-start | bytes 73736 | tf_op jit(solution)/shard_map/ppermute | solution.py:467
  7.0 0.2 collective-permute-start.2
  7.8 2.3 %gather.1 = (f32[64,128,128]{2,1,0:T(8,128)S(1)}, bf16[66,128,128]{2,1,0:T(8,128)(2,1)S(1)}) custom-call(s32[1]{0:T(128)S(6)} %copy.11.count_ref, s32[130]{0:T(256)} %rows_hbm.3, s32[130]{0:T(256)} %cols_hbm.3, bf16[130,128,128]{2,1,0:T(8,128)(2,1)} %tiles_ref.1), custom_call_target="tpu_custom_call" | custom-call | flops 8519680 | bytes 8519680 | tf_op jit(solution)/shard_map/gather/pallas_call | solution.py:522
  10.1 0.0 collective-permute-done.refs_0_
  10.1 1.1 %collective-permute-done.1.refs_1_ = bf16[48,256]{1,0:T(8,128)(2,1)S(1)} collective-permute-done((bf16[48,256]{1,0:T(8,128)(2,1)S(1)}, bf16[48,256]{1,0:T(8,128)(2,1)S(1)}, u32[]{:S(2)}, u32[]{:S(2)}) %collective-permute-start.1) | collective-permute-done | bytes 24608 | tf_op jit(solution)/shard_map/ppermute | solution.py:467
  11.2 0.1 collective-permute-start.3
  11.3 1.6 %collective-permute-start.4 = (bf16[4,48,256]{2,1,0:T(8,128)(2,1)S(1)}, bf16[4,48,256]{2,1,0:T(8,128)(2,1)S(1)}, u32[]{:S(2)}, u32[]{:S(2)}) collective-permute-start(bf16[4,48,256]{2,1,0:T(8,128)(2,1)S(1)} %join.1.joined_ref.even_ref), channel_id=1, source_target_pairs={{0,2},{2,0},{4,6},{6,4},{8,10},{10,8},{12,14},{14,12},{1,3},{3,1},... | collective-permute-start | bytes 294920 | tf_op jit(solution)/shard_map/ppermute | solution.py:467
  12.9 2.2 %dense.1 = (bf16[2,2048,512]{2,1,0:T(8,128)(2,1)S(1)}, f32[64,128,128]{2,1,0:T(8,128)S(1)}) custom-call(s32[1]{0:T(128)S(6)} %copy.11.count_ref, s32[130]{0:T(256)} %rows_hbm.3, s32[130]{0:T(256)} %cols_hbm.3, bf16[66,128,128]{2,1,0:T(8,128)(2,1)S(1)} %get-tuple-element.29.rest, ...), custom_call_target="tpu_custom_call", output_to_operand_aliasing={{1}: (4, {})} | custom-call | flops 8519680 | bytes 8519680 | tf_op jit(solution)/shard_map/dense/pallas_call | solution.py:549
  15.2 0.0 collective-permute-done.3.far_even_ref
  15.2 1.4 %collective-permute-done.4.odd_ref = bf16[4,48,256]{2,1,0:T(8,128)(2,1)S(1)} collective-permute-done((bf16[4,48,256]{2,1,0:T(8,128)(2,1)S(1)}, bf16[4,48,256]{2,1,0:T(8,128)(2,1)S(1)}, u32[]{:S(2)}, u32[]{:S(2)}) %collective-permute-start.4) | collective-permute-done | bytes 98336 | tf_op jit(solution)/shard_map/ppermute | solution.py:467
  16.5 0.8 %first.1 = (f32[32,640]{1,0:T(8,128)S(1)}, f32[2,32,256]{2,1,0:T(8,128)S(1)}, bf16[4,48,256]{2,1,0:T(8,128)(2,1)S(1)}) custom-call(bf16[4,48,256]{2,1,0:T(8,128)(2,1)S(1)} %join.1.joined_ref.even_ref, bf16[4,48,256]{2,1,0:T(8,128)(2,1)S(1)} %collective-permute-done.3.far_even_ref, bf16[4,48,256]{2,1,0:T(8,128)(2,1)S(1)} %collective-permute-done.4.odd_ref, ...), custom_call_target="tpu_custom_call" | custom-call | tf_op jit(solution)/shard_map/first/pallas_call | solution.py:568
  17.3 0.1 collective-permute-start.5
  17.4 1.3 %collective-permute-done.5.other_ref = f32[32,640]{1,0:T(8,128)S(1)} collective-permute-done((f32[32,640]{1,0:T(8,128)S(1)}, f32[32,640]{1,0:T(8,128)S(1)}, u32[]{:S(2)}, u32[]{:S(2)}) %collective-permute-start.5) | collective-permute-done | bytes 81952 | tf_op jit(solution)/shard_map/ppermute | solution.py:470
  18.7 0.3 image.2
  19.0 3.0 %collective-permute-start.6 = (f32[136,128]{1,0:T(8,128)S(1)}, f32[136,128]{1,0:T(8,128)S(1)}, u32[]{:S(2)}, u32[]{:S(2)}) collective-permute-start(f32[136,128]{1,0:T(8,128)S(1)} %get-tuple-element.33.refs_0_), channel_id=1, source_target_pairs={{0,14},{2,12},{4,10},{6,8},{8,6},{10,4},{12,2},{14,0},{1,11},{3,9}... | collective-permute-start | bytes 208904 | tf_op jit(solution)/shard_map/ppermute | solution.py:487
  22.0 0.2 collective-permute-start.7
  22.2 1.8 %collective-permute-start.8 = (f32[136,128]{1,0:T(8,128)S(1)}, f32[136,128]{1,0:T(8,128)S(1)}, u32[]{:S(2)}, u32[]{:S(2)}) collective-permute-start(f32[136,128]{1,0:T(8,128)S(1)} %get-tuple-element.33.refs_0_), channel_id=1, source_target_pairs={{0,4},{2,6},{4,0},{6,2},{8,12},{10,14},{12,8},{14,10},{1,9},{3,11}... | collective-permute-start | bytes 208904 | tf_op jit(solution)/shard_map/ppermute | solution.py:487
  24.0 0.0 collective-permute-start.13
  24.0 1.5 %collective-permute-start.9 = (f32[136,128]{1,0:T(8,128)S(1)}, f32[136,128]{1,0:T(8,128)S(1)}, u32[]{:S(2)}, u32[]{:S(2)}) collective-permute-start(f32[136,128]{1,0:T(8,128)S(1)} %get-tuple-element.33.refs_0_), channel_id=1, source_target_pairs={{0,2},{2,0},{4,6},{6,4},{8,10},{10,8},{12,14},{14,12},{1,3},{3,1},... | collective-permute-start | bytes 208904 | tf_op jit(solution)/shard_map/ppermute | solution.py:487
  25.5 0.7 %collective-permute-done.6.refs_1_ = f32[136,128]{1,0:T(8,128)S(1)} collective-permute-done((f32[136,128]{1,0:T(8,128)S(1)}, f32[136,128]{1,0:T(8,128)S(1)}, u32[]{:S(2)}, u32[]{:S(2)}) %collective-permute-start.6) | collective-permute-done | bytes 69664 | tf_op jit(solution)/shard_map/ppermute | solution.py:487
  26.2 1.5 %collective-permute-done.7.refs_2_ = f32[136,128]{1,0:T(8,128)S(1)} collective-permute-done((f32[136,128]{1,0:T(8,128)S(1)}, f32[136,128]{1,0:T(8,128)S(1)}, u32[]{:S(2)}, u32[]{:S(2)}) %collective-permute-start.7) | collective-permute-done | bytes 69664 | tf_op jit(solution)/shard_map/ppermute | solution.py:487
  27.8 0.0 collective-permute-start.11
  27.8 0.8 %collective-permute-done.8.refs_3_ = f32[136,128]{1,0:T(8,128)S(1)} collective-permute-done((f32[136,128]{1,0:T(8,128)S(1)}, f32[136,128]{1,0:T(8,128)S(1)}, u32[]{:S(2)}, u32[]{:S(2)}) %collective-permute-start.8) | collective-permute-done | bytes 69664 | tf_op jit(solution)/shard_map/ppermute | solution.py:487
  28.6 0.9 %collective-permute-start.12 = (f32[136,128]{1,0:T(8,128)S(1)}, f32[136,128]{1,0:T(8,128)S(1)}, u32[]{:S(2)}, u32[]{:S(2)}) collective-permute-start(f32[136,128]{1,0:T(8,128)S(1)} %collective-permute-done.8.refs_3_), channel_id=1, source_target_pairs={{0,1},{1,0},{2,3},{3,2},{4,5},{5,4},{6,7},{7,6},{8,9},{9,8},{10,11... | collective-permute-start | bytes 208904 | tf_op jit(solution)/shard_map/ppermute | solution.py:470
  29.4 0.8 %inverse.2.refs_11_ = f32[32,128]{1,0:T(8,128)S(1)} custom-call(f32[32,128]{1,0:T(8,128)S(1)} %get-tuple-element.37.norm_ref.refs_10_), custom_call_target="tpu_custom_call" | custom-call | tf_op jit(solution)/shard_map/inverse/pallas_call | solution.py:603
  30.2 0.0 collective-permute-done.13.far_odd_ref
  30.2 0.1 collect.1
  30.3 0.0 collective-permute-done.9.refs_4_
  30.3 0.0 collective-permute-done.12.refs_7_
  30.3 2.8 %step.2 = (f32[32,512]{1,0:T(8,128)S(1)}, f32[9,32,256]{2,1,0:T(8,128)S(1)}, f32[2,8,32,256]{3,2,1,0:T(8,128)S(1)}, f32[32,128]{1,0:T(8,128)S(1)}, f32[32,256]{1,0:T(8,128)S(1)}) custom-call(f32[136,128]{1,0:T(8,128)S(1)} %get-tuple-element.33.refs_0_, f32[136,128]{1,0:T(8,128)S(1)} %collective-permute-done.6.refs_1_, ...), custom_call_target="tpu_custom_call" | custom-call | tf_op jit(solution)/shard_map/step/pallas_call | solution.py:612
  33.1 0.3 collective-permute-start.14
  33.5 0.9 %collective-permute-done.14.other_ref = f32[32,512]{1,0:T(8,128)S(1)} collective-permute-done((f32[32,512]{1,0:T(8,128)S(1)}, f32[32,512]{1,0:T(8,128)S(1)}, u32[]{:S(2)}, u32[]{:S(2)}) %collective-permute-start.14) | collective-permute-done | bytes 65568 | tf_op jit(solution)/shard_map/ppermute | solution.py:470
  34.4 0.3 image.3.refs_0_
  34.8 2.0 %collective-permute-start.15 = (f32[136,128]{1,0:T(8,128)S(1)}, f32[136,128]{1,0:T(8,128)S(1)}, u32[]{:S(2)}, u32[]{:S(2)}) collective-permute-start(f32[136,128]{1,0:T(8,128)S(1)} %image.3.refs_0_), channel_id=1, source_target_pairs={{0,14},{2,12},{4,10},{6,8},{8,6},{10,4},{12,2},{14,0},{1,11},{3,9}... | collective-permute-start | bytes 208904 | tf_op jit(solution)/shard_map/ppermute | solution.py:487
  36.7 0.5 collective-permute-start.16
  37.3 2.4 %collective-permute-start.17 = (f32[136,128]{1,0:T(8,128)S(1)}, f32[136,128]{1,0:T(8,128)S(1)}, u32[]{:S(2)}, u32[]{:S(2)}) collective-permute-start(f32[136,128]{1,0:T(8,128)S(1)} %image.3.refs_0_), channel_id=1, source_target_pairs={{0,4},{2,6},{4,0},{6,2},{8,12},{10,14},{12,8},{14,10},{1,9},{3,11}... | collective-permute-start | bytes 208904 | tf_op jit(solution)/shard_map/ppermute | solution.py:487
  39.7 0.5 collective-permute-start.18
  40.2 2.5 %collective-permute-done.15.refs_1_ = f32[136,128]{1,0:T(8,128)S(1)} collective-permute-done((f32[136,128]{1,0:T(8,128)S(1)}, f32[136,128]{1,0:T(8,128)S(1)}, u32[]{:S(2)}, u32[]{:S(2)}) %collective-permute-start.15) | collective-permute-done | bytes 69664 | tf_op jit(solution)/shard_map/ppermute | solution.py:487
  42.7 0.8 %collective-permute-start.19 = (f32[136,128]{1,0:T(8,128)S(1)}, f32[136,128]{1,0:T(8,128)S(1)}, u32[]{:S(2)}, u32[]{:S(2)}) collective-permute-start(f32[136,128]{1,0:T(8,128)S(1)} %collective-permute-done.15.refs_1_), channel_id=1, source_target_pairs={{0,1},{1,0},{2,3},{3,2},{4,5},{5,4},{6,7},{7,6},{8,9},{9,8},{10,11... | collective-permute-start | bytes 208904 | tf_op jit(solution)/shard_map/ppermute | solution.py:470
  43.5 0.2 collective-permute-done.16.refs_2_
  43.7 0.0 collective-permute-start.20
  43.7 0.0 collective-permute-done.17.refs_3_
  43.7 0.5 collective-permute-start.21
  44.2 0.8 %inverse.3.refs_11_ = f32[32,128]{1,0:T(8,128)S(1)} custom-call(f32[32,128]{1,0:T(8,128)S(1)} %get-tuple-element.41.norm_ref.refs_10_), custom_call_target="tpu_custom_call" | custom-call | tf_op jit(solution)/shard_map/inverse/pallas_call | solution.py:603
  45.0 0.0 collective-permute-done.18.refs_4_
  45.0 0.1 collective-permute-done.21.refs_7_
  45.1 2.8 %step.3 = (f32[32,512]{1,0:T(8,128)S(1)}, f32[2,32,256]{2,1,0:T(8,128)S(1)}, f32[32,256]{1,0:T(8,128)S(1)}, f32[32,128]{1,0:T(8,128)S(1)}, f32[32,256]{1,0:T(8,128)S(1)}) custom-call(f32[136,128]{1,0:T(8,128)S(1)} %image.3.refs_0_, f32[136,128]{1,0:T(8,128)S(1)} %collective-permute-done.15.refs_1_, f32[136,128]{1,0:T(8,128)S(1)} %collective-permute-done.16.refs_2_, ...), custom_call_target="tpu_custom_call" | custom-call | tf_op jit(solution)/shard_map/step/pallas_call | solution.py:612
  47.9 0.4 collective-permute-start.22
  48.2 0.9 %collective-permute-done.22.other_ref = f32[32,512]{1,0:T(8,128)S(1)} collective-permute-done((f32[32,512]{1,0:T(8,128)S(1)}, f32[32,512]{1,0:T(8,128)S(1)}, u32[]{:S(2)}, u32[]{:S(2)}) %collective-permute-start.22) | collective-permute-done | bytes 65568 | tf_op jit(solution)/shard_map/ppermute | solution.py:470
  49.1 0.3 last_image.1
  49.5 2.2 %collective-permute-start.23 = (f32[8,128]{1,0:T(8,128)S(1)}, f32[8,128]{1,0:T(8,128)S(1)}, u32[]{:S(2)}, u32[]{:S(2)}) collective-permute-start(f32[8,128]{1,0:T(8,128)S(1)} %get-tuple-element.45.refs_0_), channel_id=1, source_target_pairs={{0,12},{2,14},{4,8},{6,10},{8,4},{10,6},{12,0},{14,2},{1,15},{3,13... | collective-permute-start | bytes 12296 | tf_op jit(solution)/shard_map/ppermute | solution.py:487
  51.7 0.9 %collective-permute-start.24 = (f32[8,128]{1,0:T(8,128)S(1)}, f32[8,128]{1,0:T(8,128)S(1)}, u32[]{:S(2)}, u32[]{:S(2)}) collective-permute-start(f32[8,128]{1,0:T(8,128)S(1)} %get-tuple-element.45.refs_0_), channel_id=1, source_target_pairs={{0,6},{2,4},{4,2},{6,0},{8,14},{10,12},{12,10},{14,8},{1,11},{3,9}... | collective-permute-start | bytes 12296 | tf_op jit(solution)/shard_map/ppermute | solution.py:487
  52.6 1.7 %collective-permute-start.25 = (f32[8,128]{1,0:T(8,128)S(1)}, f32[8,128]{1,0:T(8,128)S(1)}, u32[]{:S(2)}, u32[]{:S(2)}) collective-permute-start(f32[8,128]{1,0:T(8,128)S(1)} %get-tuple-element.45.refs_0_), channel_id=1, source_target_pairs={{0,4},{2,6},{4,0},{6,2},{8,12},{10,14},{12,8},{14,10},{1,9},{3,11}... | collective-permute-start | bytes 12296 | tf_op jit(solution)/shard_map/ppermute | solution.py:487
  54.3 0.9 %collective-permute-start.26 = (f32[8,128]{1,0:T(8,128)S(1)}, f32[8,128]{1,0:T(8,128)S(1)}, u32[]{:S(2)}, u32[]{:S(2)}) collective-permute-start(f32[8,128]{1,0:T(8,128)S(1)} %get-tuple-element.45.refs_0_), channel_id=1, source_target_pairs={{0,2},{2,0},{4,6},{6,4},{8,10},{10,8},{12,14},{14,12},{1,3},{3,1},... | collective-permute-start | bytes 12296 | tf_op jit(solution)/shard_map/ppermute | solution.py:487
  55.1 0.0 collective-permute-done.23.refs_1_
  55.1 0.7 %collective-permute-start.27 = (f32[8,128]{1,0:T(8,128)S(1)}, f32[8,128]{1,0:T(8,128)S(1)}, u32[]{:S(2)}, u32[]{:S(2)}) collective-permute-start(f32[8,128]{1,0:T(8,128)S(1)} %collective-permute-done.23.refs_1_), channel_id=1, source_target_pairs={{0,1},{1,0},{2,3},{3,2},{4,5},{5,4},{6,7},{7,6},{8,9},{9,8},{10,11... | collective-permute-start | bytes 12296 | tf_op jit(solution)/shard_map/ppermute | solution.py:470
  55.9 0.3 collective-permute-done.24.refs_2_
  56.2 0.4 collective-permute-start.28
  56.6 0.0 collective-permute-done.25.refs_3_
  56.6 0.1 collective-permute-start.29
  56.7 1.2 %collective-permute-done.26.refs_4_ = f32[8,128]{1,0:T(8,128)S(1)} collective-permute-done((f32[8,128]{1,0:T(8,128)S(1)}, f32[8,128]{1,0:T(8,128)S(1)}, u32[]{:S(2)}, u32[]{:S(2)}) %collective-permute-start.26) | collective-permute-done | bytes 4128 | tf_op jit(solution)/shard_map/ppermute | solution.py:487
  57.9 1.5 %last.1 = (f32[32,256]{1,0:T(8,128)}, f32[32,256]{1,0:T(8,128)}) custom-call(f32[8,128]{1,0:T(8,128)S(1)} %get-tuple-element.45.refs_0_, f32[8,128]{1,0:T(8,128)S(1)} %collective-permute-done.23.refs_1_, f32[8,128]{1,0:T(8,128)S(1)} %collective-permute-done.24.refs_2_, f32[8,128]{1,0:T(8,128)S(1)} %collective-permute-done.25.refs_3_, ...), custom_call_target="tpu_custom_call" | custom-call | tf_op jit(solution)/shard_map/last/pallas_call | solution.py:635
  (10 shorter events, 0.0 us)
Async XLA Ops:
  1.5 8.6 %collective-permute-start = (bf16[48,256]{1,0:T(8,128)(2,1)S(1)}, bf16[48,256]{1,0:T(8,128)(2,1)S(1)}, u32[]{:S(2)}, u32[]{:S(2)}) collective-permute-start(bf16[48,256]{1,0:T(8,128)(2,1)S(1)} %get-tuple-element.26.refs_3_), channel_id=1, source_target_pairs={{0,8},{2,10},{4,12},{6,14},{8,0},{10,2},{12,4},{14,6},{1,9},{3,11}... | collective-permute-start | bytes 73736 | tf_op jit(solution)/shard_map/ppermute | solution.py:467
  5.6 5.6 %collective-permute-start.1 = (bf16[48,256]{1,0:T(8,128)(2,1)S(1)}, bf16[48,256]{1,0:T(8,128)(2,1)S(1)}, u32[]{:S(2)}, u32[]{:S(2)}) collective-permute-start(bf16[48,256]{1,0:T(8,128)(2,1)S(1)} %get-tuple-element.26.refs_3_), channel_id=1, source_target_pairs={{0,12},{2,14},{4,8},{6,10},{8,4},{10,6},{12,0},{14,2},{1,13},{3,15... | collective-permute-start | bytes 73736 | tf_op jit(solution)/shard_map/ppermute | solution.py:467
  7.0 4.3 %collective-permute-start.2 = (bf16[48,256]{1,0:T(8,128)(2,1)S(1)}, bf16[48,256]{1,0:T(8,128)(2,1)S(1)}, u32[]{:S(2)}, u32[]{:S(2)}) collective-permute-start(bf16[48,256]{1,0:T(8,128)(2,1)S(1)} %get-tuple-element.26.refs_3_), channel_id=1, source_target_pairs={{0,4},{2,6},{4,0},{6,2},{8,12},{10,14},{12,8},{14,10},{1,5},{3,7},... | collective-permute-start | bytes 73736 | tf_op jit(solution)/shard_map/ppermute | solution.py:467
  11.2 3.9 %collective-permute-start.3 = (bf16[4,48,256]{2,1,0:T(8,128)(2,1)S(1)}, bf16[4,48,256]{2,1,0:T(8,128)(2,1)S(1)}, u32[]{:S(2)}, u32[]{:S(2)}) collective-permute-start(bf16[4,48,256]{2,1,0:T(8,128)(2,1)S(1)} %join.1.joined_ref.even_ref), channel_id=1, source_target_pairs={{0,1},{1,0},{2,3},{3,2},{4,5},{5,4},{6,7},{7,6},{8,9},{9,8},{10,11... | collective-permute-start | bytes 294920 | tf_op jit(solution)/shard_map/ppermute | solution.py:470
  11.3 5.2 %collective-permute-start.4 = (bf16[4,48,256]{2,1,0:T(8,128)(2,1)S(1)}, bf16[4,48,256]{2,1,0:T(8,128)(2,1)S(1)}, u32[]{:S(2)}, u32[]{:S(2)}) collective-permute-start(bf16[4,48,256]{2,1,0:T(8,128)(2,1)S(1)} %join.1.joined_ref.even_ref), channel_id=1, source_target_pairs={{0,2},{2,0},{4,6},{6,4},{8,10},{10,8},{12,14},{14,12},{1,3},{3,1},... | collective-permute-start | bytes 294920 | tf_op jit(solution)/shard_map/ppermute | solution.py:467
  17.3 1.3 %collective-permute-start.5 = (f32[32,640]{1,0:T(8,128)S(1)}, f32[32,640]{1,0:T(8,128)S(1)}, u32[]{:S(2)}, u32[]{:S(2)}) collective-permute-start(f32[32,640]{1,0:T(8,128)S(1)} %get-tuple-element.31.mine_ref), channel_id=1, source_target_pairs={{0,1},{1,0},{2,3},{3,2},{4,5},{5,4},{6,7},{7,6},{8,9},{9,8},{10,11... | collective-permute-start | bytes 245768 | tf_op jit(solution)/shard_map/ppermute | solution.py:470
  19.0 7.2 %collective-permute-start.6 = (f32[136,128]{1,0:T(8,128)S(1)}, f32[136,128]{1,0:T(8,128)S(1)}, u32[]{:S(2)}, u32[]{:S(2)}) collective-permute-start(f32[136,128]{1,0:T(8,128)S(1)} %get-tuple-element.33.refs_0_), channel_id=1, source_target_pairs={{0,14},{2,12},{4,10},{6,8},{8,6},{10,4},{12,2},{14,0},{1,11},{3,9}... | collective-permute-start | bytes 208904 | tf_op jit(solution)/shard_map/ppermute | solution.py:487
  22.0 5.8 %collective-permute-start.7 = (f32[136,128]{1,0:T(8,128)S(1)}, f32[136,128]{1,0:T(8,128)S(1)}, u32[]{:S(2)}, u32[]{:S(2)}) collective-permute-start(f32[136,128]{1,0:T(8,128)S(1)} %get-tuple-element.33.refs_0_), channel_id=1, source_target_pairs={{0,6},{2,4},{4,2},{6,0},{8,14},{10,12},{12,10},{14,8},{1,13},{3,15... | collective-permute-start | bytes 208904 | tf_op jit(solution)/shard_map/ppermute | solution.py:487
  22.2 6.3 %collective-permute-start.8 = (f32[136,128]{1,0:T(8,128)S(1)}, f32[136,128]{1,0:T(8,128)S(1)}, u32[]{:S(2)}, u32[]{:S(2)}) collective-permute-start(f32[136,128]{1,0:T(8,128)S(1)} %get-tuple-element.33.refs_0_), channel_id=1, source_target_pairs={{0,4},{2,6},{4,0},{6,2},{8,12},{10,14},{12,8},{14,10},{1,9},{3,11}... | collective-permute-start | bytes 208904 | tf_op jit(solution)/shard_map/ppermute | solution.py:487
  24.0 6.2 %collective-permute-start.13 = (bf16[4,48,256]{2,1,0:T(8,128)(2,1)S(1)}, bf16[4,48,256]{2,1,0:T(8,128)(2,1)S(1)}, u32[]{:S(2)}, u32[]{:S(2)}) collective-permute-start(bf16[4,48,256]{2,1,0:T(8,128)(2,1)S(1)} %get-tuple-element.34.odd_ref), channel_id=1, source_target_pairs={{0,1},{1,0},{2,3},{3,2},{4,5},{5,4},{6,7},{7,6},{8,9},{9,8},{10,11... | collective-permute-start | bytes 294920 | tf_op jit(solution)/shard_map/ppermute | solution.py:470
  24.0 6.3 %collective-permute-start.9 = (f32[136,128]{1,0:T(8,128)S(1)}, f32[136,128]{1,0:T(8,128)S(1)}, u32[]{:S(2)}, u32[]{:S(2)}) collective-permute-start(f32[136,128]{1,0:T(8,128)S(1)} %get-tuple-element.33.refs_0_), channel_id=1, source_target_pairs={{0,2},{2,0},{4,6},{6,4},{8,10},{10,8},{12,14},{14,12},{1,3},{3,1},... | collective-permute-start | bytes 208904 | tf_op jit(solution)/shard_map/ppermute | solution.py:487
  26.2 4.1 %collective-permute-start.10 = (f32[136,128]{1,0:T(8,128)S(1)}, f32[136,128]{1,0:T(8,128)S(1)}, u32[]{:S(2)}, u32[]{:S(2)}) collective-permute-start(f32[136,128]{1,0:T(8,128)S(1)} %collective-permute-done.6.refs_1_), channel_id=1, source_target_pairs={{0,1},{1,0},{2,3},{3,2},{4,5},{5,4},{6,7},{7,6},{8,9},{9,8},{10,11... | collective-permute-start | bytes 208904 | tf_op jit(solution)/shard_map/ppermute | solution.py:470
  27.8 2.6 %collective-permute-start.11 = (f32[136,128]{1,0:T(8,128)S(1)}, f32[136,128]{1,0:T(8,128)S(1)}, u32[]{:S(2)}, u32[]{:S(2)}) collective-permute-start(f32[136,128]{1,0:T(8,128)S(1)} %collective-permute-done.7.refs_2_), channel_id=1, source_target_pairs={{0,1},{1,0},{2,3},{3,2},{4,5},{5,4},{6,7},{7,6},{8,9},{9,8},{10,11... | collective-permute-start | bytes 208904 | tf_op jit(solution)/shard_map/ppermute | solution.py:470
  28.6 1.8 %collective-permute-start.12 = (f32[136,128]{1,0:T(8,128)S(1)}, f32[136,128]{1,0:T(8,128)S(1)}, u32[]{:S(2)}, u32[]{:S(2)}) collective-permute-start(f32[136,128]{1,0:T(8,128)S(1)} %collective-permute-done.8.refs_3_), channel_id=1, source_target_pairs={{0,1},{1,0},{2,3},{3,2},{4,5},{5,4},{6,7},{7,6},{8,9},{9,8},{10,11... | collective-permute-start | bytes 208904 | tf_op jit(solution)/shard_map/ppermute | solution.py:470
  33.1 1.3 %collective-permute-start.14 = (f32[32,512]{1,0:T(8,128)S(1)}, f32[32,512]{1,0:T(8,128)S(1)}, u32[]{:S(2)}, u32[]{:S(2)}) collective-permute-start(f32[32,512]{1,0:T(8,128)S(1)} %get-tuple-element.38.mine_ref), channel_id=1, source_target_pairs={{0,1},{1,0},{2,3},{3,2},{4,5},{5,4},{6,7},{7,6},{8,9},{9,8},{10,11... | collective-permute-start | bytes 196616 | tf_op jit(solution)/shard_map/ppermute | solution.py:470
  34.8 7.9 %collective-permute-start.15 = (f32[136,128]{1,0:T(8,128)S(1)}, f32[136,128]{1,0:T(8,128)S(1)}, u32[]{:S(2)}, u32[]{:S(2)}) collective-permute-start(f32[136,128]{1,0:T(8,128)S(1)} %image.3.refs_0_), channel_id=1, source_target_pairs={{0,14},{2,12},{4,10},{6,8},{8,6},{10,4},{12,2},{14,0},{1,11},{3,9}... | collective-permute-start | bytes 208904 | tf_op jit(solution)/shard_map/ppermute | solution.py:487
  36.7 6.9 %collective-permute-start.16 = (f32[136,128]{1,0:T(8,128)S(1)}, f32[136,128]{1,0:T(8,128)S(1)}, u32[]{:S(2)}, u32[]{:S(2)}) collective-permute-start(f32[136,128]{1,0:T(8,128)S(1)} %image.3.refs_0_), channel_id=1, source_target_pairs={{0,6},{2,4},{4,2},{6,0},{8,14},{10,12},{12,10},{14,8},{1,13},{3,15... | collective-permute-start | bytes 208904 | tf_op jit(solution)/shard_map/ppermute | solution.py:487
  37.3 6.4 %collective-permute-start.17 = (f32[136,128]{1,0:T(8,128)S(1)}, f32[136,128]{1,0:T(8,128)S(1)}, u32[]{:S(2)}, u32[]{:S(2)}) collective-permute-start(f32[136,128]{1,0:T(8,128)S(1)} %image.3.refs_0_), channel_id=1, source_target_pairs={{0,4},{2,6},{4,0},{6,2},{8,12},{10,14},{12,8},{14,10},{1,9},{3,11}... | collective-permute-start | bytes 208904 | tf_op jit(solution)/shard_map/ppermute | solution.py:487
  39.7 5.2 %collective-permute-start.18 = (f32[136,128]{1,0:T(8,128)S(1)}, f32[136,128]{1,0:T(8,128)S(1)}, u32[]{:S(2)}, u32[]{:S(2)}) collective-permute-start(f32[136,128]{1,0:T(8,128)S(1)} %image.3.refs_0_), channel_id=1, source_target_pairs={{0,2},{2,0},{4,6},{6,4},{8,10},{10,8},{12,14},{14,12},{1,3},{3,1},... | collective-permute-start | bytes 208904 | tf_op jit(solution)/shard_map/ppermute | solution.py:487
  42.7 2.3 %collective-permute-start.19 = (f32[136,128]{1,0:T(8,128)S(1)}, f32[136,128]{1,0:T(8,128)S(1)}, u32[]{:S(2)}, u32[]{:S(2)}) collective-permute-start(f32[136,128]{1,0:T(8,128)S(1)} %collective-permute-done.15.refs_1_), channel_id=1, source_target_pairs={{0,1},{1,0},{2,3},{3,2},{4,5},{5,4},{6,7},{7,6},{8,9},{9,8},{10,11... | collective-permute-start | bytes 208904 | tf_op jit(solution)/shard_map/ppermute | solution.py:470
  43.7 1.3 %collective-permute-start.20 = (f32[136,128]{1,0:T(8,128)S(1)}, f32[136,128]{1,0:T(8,128)S(1)}, u32[]{:S(2)}, u32[]{:S(2)}) collective-permute-start(f32[136,128]{1,0:T(8,128)S(1)} %collective-permute-done.16.refs_2_), channel_id=1, source_target_pairs={{0,1},{1,0},{2,3},{3,2},{4,5},{5,4},{6,7},{7,6},{8,9},{9,8},{10,11... | collective-permute-start | bytes 208904 | tf_op jit(solution)/shard_map/ppermute | solution.py:470
  43.7 1.4 %collective-permute-start.21 = (f32[136,128]{1,0:T(8,128)S(1)}, f32[136,128]{1,0:T(8,128)S(1)}, u32[]{:S(2)}, u32[]{:S(2)}) collective-permute-start(f32[136,128]{1,0:T(8,128)S(1)} %collective-permute-done.17.refs_3_), channel_id=1, source_target_pairs={{0,1},{1,0},{2,3},{3,2},{4,5},{5,4},{6,7},{7,6},{8,9},{9,8},{10,11... | collective-permute-start | bytes 208904 | tf_op jit(solution)/shard_map/ppermute | solution.py:470
  47.9 1.3 %collective-permute-start.22 = (f32[32,512]{1,0:T(8,128)S(1)}, f32[32,512]{1,0:T(8,128)S(1)}, u32[]{:S(2)}, u32[]{:S(2)}) collective-permute-start(f32[32,512]{1,0:T(8,128)S(1)} %get-tuple-element.43.mine_ref), channel_id=1, source_target_pairs={{0,1},{1,0},{2,3},{3,2},{4,5},{5,4},{6,7},{7,6},{8,9},{9,8},{10,11... | collective-permute-start | bytes 196616 | tf_op jit(solution)/shard_map/ppermute | solution.py:470
  49.5 5.7 %collective-permute-start.23 = (f32[8,128]{1,0:T(8,128)S(1)}, f32[8,128]{1,0:T(8,128)S(1)}, u32[]{:S(2)}, u32[]{:S(2)}) collective-permute-start(f32[8,128]{1,0:T(8,128)S(1)} %get-tuple-element.45.refs_0_), channel_id=1, source_target_pairs={{0,12},{2,14},{4,8},{6,10},{8,4},{10,6},{12,0},{14,2},{1,15},{3,13... | collective-permute-start | bytes 12296 | tf_op jit(solution)/shard_map/ppermute | solution.py:487
  51.7 4.5 %collective-permute-start.24 = (f32[8,128]{1,0:T(8,128)S(1)}, f32[8,128]{1,0:T(8,128)S(1)}, u32[]{:S(2)}, u32[]{:S(2)}) collective-permute-start(f32[8,128]{1,0:T(8,128)S(1)} %get-tuple-element.45.refs_0_), channel_id=1, source_target_pairs={{0,6},{2,4},{4,2},{6,0},{8,14},{10,12},{12,10},{14,8},{1,11},{3,9}... | collective-permute-start | bytes 12296 | tf_op jit(solution)/shard_map/ppermute | solution.py:487
  52.6 4.0 %collective-permute-start.25 = (f32[8,128]{1,0:T(8,128)S(1)}, f32[8,128]{1,0:T(8,128)S(1)}, u32[]{:S(2)}, u32[]{:S(2)}) collective-permute-start(f32[8,128]{1,0:T(8,128)S(1)} %get-tuple-element.45.refs_0_), channel_id=1, source_target_pairs={{0,4},{2,6},{4,0},{6,2},{8,12},{10,14},{12,8},{14,10},{1,9},{3,11}... | collective-permute-start | bytes 12296 | tf_op jit(solution)/shard_map/ppermute | solution.py:487
  54.3 3.6 %collective-permute-start.26 = (f32[8,128]{1,0:T(8,128)S(1)}, f32[8,128]{1,0:T(8,128)S(1)}, u32[]{:S(2)}, u32[]{:S(2)}) collective-permute-start(f32[8,128]{1,0:T(8,128)S(1)} %get-tuple-element.45.refs_0_), channel_id=1, source_target_pairs={{0,2},{2,0},{4,6},{6,4},{8,10},{10,8},{12,14},{14,12},{1,3},{3,1},... | collective-permute-start | bytes 12296 | tf_op jit(solution)/shard_map/ppermute | solution.py:487
  55.1 2.8 %collective-permute-start.27 = (f32[8,128]{1,0:T(8,128)S(1)}, f32[8,128]{1,0:T(8,128)S(1)}, u32[]{:S(2)}, u32[]{:S(2)}) collective-permute-start(f32[8,128]{1,0:T(8,128)S(1)} %collective-permute-done.23.refs_1_), channel_id=1, source_target_pairs={{0,1},{1,0},{2,3},{3,2},{4,5},{5,4},{6,7},{7,6},{8,9},{9,8},{10,11... | collective-permute-start | bytes 12296 | tf_op jit(solution)/shard_map/ppermute | solution.py:470
  56.2 1.7 %collective-permute-start.28 = (f32[8,128]{1,0:T(8,128)S(1)}, f32[8,128]{1,0:T(8,128)S(1)}, u32[]{:S(2)}, u32[]{:S(2)}) collective-permute-start(f32[8,128]{1,0:T(8,128)S(1)} %collective-permute-done.24.refs_2_), channel_id=1, source_target_pairs={{0,1},{1,0},{2,3},{3,2},{4,5},{5,4},{6,7},{7,6},{8,9},{9,8},{10,11... | collective-permute-start | bytes 12296 | tf_op jit(solution)/shard_map/ppermute | solution.py:470
  56.6 1.3 %collective-permute-start.29 = (f32[8,128]{1,0:T(8,128)S(1)}, f32[8,128]{1,0:T(8,128)S(1)}, u32[]{:S(2)}, u32[]{:S(2)}) collective-permute-start(f32[8,128]{1,0:T(8,128)S(1)} %collective-permute-done.25.refs_3_), channel_id=1, source_target_pairs={{0,1},{1,0},{2,3},{3,2},{4,5},{5,4},{6,7},{7,6},{8,9},{9,8},{10,11... | collective-permute-start | bytes 12296 | tf_op jit(solution)/shard_map/ppermute | solution.py:470

commit v22 on v21

--- a/solution.py
+++ b/solution.py
@@ -471,7 +471,7 @@
             value, "col", [(i, (i + 1) % col_devices) for i in range(col_devices)]
         )
 
-    def exchange(value, turns=((7, 5), (3, 6), (2, 4), (1, 1))):
+    def exchange(value, turns=((7, 6), (3, 5), (2, 4), (1, 1))):
         if pieces != 8:
             found = [value] + [swap(value, k) for k in range(1, pieces)]
             return found, [(k, k) for k in range(pieces)]

time: 59.7 us -> 59.8 us (level)
  waiting for transfers between devices: 12.9 us -> 16.1 us
  starting transfers between devices: 29.2 us -> 26 us
    ppermute x14, starting transfers between devices: 4.31 us -> 1.36 us  [across(): lax.ppermute(value, 'col', [(i, (i + 1) % col_devices) for i in range(col...]
    ppermute x12, waiting for transfers between devices: 7.18 us -> 9.13 us  [exchange(): fetched.append(lax.ppermute(value, ('row', 'col'), pairs))]
    ppermute x14, waiting for transfers between devices: 3.21 us -> 4.53 us  [across(): lax.ppermute(value, 'col', [(i, (i + 1) % col_devices) for i in range(col...]
  transfers between devices with their start and end apart: 30 -> 30, of which waited for: 13 -> 17; matrix products, arithmetic and copies ran while one was open for 0% -> 0% of each run, Pallas kernels for 10% -> 10%
where the time goes in v22:
time: 59.8 us; the launch traced here: 59.5 us
  starting transfers between devices  26 us (43%)
  waiting for transfers between devices  16.1 us (27%)
  Pallas kernels  16 us (27%)
  between operations  1.45 us (2%)
    ppermute x12, starting transfers between devices, exchange(): fetched.append(lax.ppermute(value, ('row', 'col'), pairs))  17.3 us
    ppermute x12, waiting for transfers between devices, exchange(): fetched.append(lax.ppermute(value, ('row', 'col'), pairs))  9.13 us
    ppermute x4, starting transfers between devices, swap(): return lax.ppermute(value, 'row', [(i, i ^ mask) for i in range(pieces)])  7.27 us
    pallas_call x2, Pallas kernels, per_device(): pl.pallas_call(functools.partial(step_kernel, len(found), places, not fir...  5.56 us
    ppermute x14, waiting for transfers between devices, across(): lax.ppermute(value, 'col', [(i, (i + 1) % col_devices) for i in range(col...  4.53 us
    ppermute x4, waiting for transfers between devices, swap(): return lax.ppermute(value, 'row', [(i, i ^ mask) for i in range(pieces)])  2.39 us
    pallas_call x1, Pallas kernels, per_device(): pl.pallas_call(functools.partial(gather_kernel, rows_dev), out_shape=(tot...  2.36 us
    pallas_call x1, Pallas kernels, per_device(): pl.pallas_call(functools.partial(dense_kernel, rows_dev), out_shape=(matr...  2.23 us
  transfers between devices with their start and end apart: 30, of which 17 were waited for; matrix products, arithmetic and copies ran while one was open for 0% of the time, Pallas kernels for 10%

profile of v22, /device:TPU:0, one launch (start us, length us, event | category | flops | bytes accessed | tf_op | source)
XLA Modules:
  0.0 59.5 jit_solution(15889173207982422415)
XLA Ops:
  0.6 0.9 %message.1 = (bf16[48,256]{1,0:T(8,128)(2,1)S(1)}, f32[32,128]{1,0:T(8,128)S(1)}) custom-call(s32[32,256]{1,0:T(8,128)} %signs_hbm.1, f32[256]{0:T(256)} %weight_hbm.1, f32[32]{0:T(128)} %scale_hbm.1), custom_call_target="tpu_custom_call" | custom-call | tf_op jit(solution)/shard_map/message/pallas_call | solution.py:498
  1.5 4.1 %collective-permute-start = (bf16[48,256]{1,0:T(8,128)(2,1)S(1)}, bf16[48,256]{1,0:T(8,128)(2,1)S(1)}, u32[]{:S(2)}, u32[]{:S(2)}) collective-permute-start(bf16[48,256]{1,0:T(8,128)(2,1)S(1)} %get-tuple-element.26.refs_3_), channel_id=1, source_target_pairs={{0,8},{2,10},{4,12},{6,14},{8,0},{10,2},{12,4},{14,6},{1,9},{3,11}... | collective-permute-start | bytes 73736 | tf_op jit(solution)/shard_map/ppermute | solution.py:467
  5.6 1.3 %collective-permute-start.1 = (bf16[48,256]{1,0:T(8,128)(2,1)S(1)}, bf16[48,256]{1,0:T(8,128)(2,1)S(1)}, u32[]{:S(2)}, u32[]{:S(2)}) collective-permute-start(bf16[48,256]{1,0:T(8,128)(2,1)S(1)} %get-tuple-element.26.refs_3_), channel_id=1, source_target_pairs={{0,12},{2,14},{4,8},{6,10},{8,4},{10,6},{12,0},{14,2},{1,13},{3,15... | collective-permute-start | bytes 73736 | tf_op jit(solution)/shard_map/ppermute | solution.py:467
  7.0 0.2 collective-permute-start.2
  7.8 2.4 %gather.1 = (f32[64,128,128]{2,1,0:T(8,128)S(1)}, bf16[66,128,128]{2,1,0:T(8,128)(2,1)S(1)}) custom-call(s32[1]{0:T(128)S(6)} %copy.11.count_ref, s32[130]{0:T(256)} %rows_hbm.3, s32[130]{0:T(256)} %cols_hbm.3, bf16[130,128,128]{2,1,0:T(8,128)(2,1)} %tiles_ref.1), custom_call_target="tpu_custom_call" | custom-call | flops 8519680 | bytes 8519680 | tf_op jit(solution)/shard_map/gather/pallas_call | solution.py:522
  10.2 0.0 collective-permute-done.refs_0_
  10.2 1.0 %collective-permute-done.1.refs_1_ = bf16[48,256]{1,0:T(8,128)(2,1)S(1)} collective-permute-done((bf16[48,256]{1,0:T(8,128)(2,1)S(1)}, bf16[48,256]{1,0:T(8,128)(2,1)S(1)}, u32[]{:S(2)}, u32[]{:S(2)}) %collective-permute-start.1) | collective-permute-done | bytes 24608 | tf_op jit(solution)/shard_map/ppermute | solution.py:467
  11.2 0.0 collective-permute-done.2.refs_2_
  11.2 0.1 collective-permute-start.3
  11.3 1.6 %collective-permute-start.4 = (bf16[4,48,256]{2,1,0:T(8,128)(2,1)S(1)}, bf16[4,48,256]{2,1,0:T(8,128)(2,1)S(1)}, u32[]{:S(2)}, u32[]{:S(2)}) collective-permute-start(bf16[4,48,256]{2,1,0:T(8,128)(2,1)S(1)} %join.1.joined_ref.even_ref), channel_id=1, source_target_pairs={{0,2},{2,0},{4,6},{6,4},{8,10},{10,8},{12,14},{14,12},{1,3},{3,1},... | collective-permute-start | bytes 294920 | tf_op jit(solution)/shard_map/ppermute | solution.py:467
  12.9 2.2 %dense.1 = (bf16[2,2048,512]{2,1,0:T(8,128)(2,1)S(1)}, f32[64,128,128]{2,1,0:T(8,128)S(1)}) custom-call(s32[1]{0:T(128)S(6)} %copy.11.count_ref, s32[130]{0:T(256)} %rows_hbm.3, s32[130]{0:T(256)} %cols_hbm.3, bf16[66,128,128]{2,1,0:T(8,128)(2,1)S(1)} %get-tuple-element.29.rest, ...), custom_call_target="tpu_custom_call", output_to_operand_aliasing={{1}: (4, {})} | custom-call | flops 8519680 | bytes 8519680 | tf_op jit(solution)/shard_map/dense/pallas_call | solution.py:549
  15.2 0.0 collective-permute-done.3.far_even_ref
  15.2 1.4 %collective-permute-done.4.odd_ref = bf16[4,48,256]{2,1,0:T(8,128)(2,1)S(1)} collective-permute-done((bf16[4,48,256]{2,1,0:T(8,128)(2,1)S(1)}, bf16[4,48,256]{2,1,0:T(8,128)(2,1)S(1)}, u32[]{:S(2)}, u32[]{:S(2)}) %collective-permute-start.4) | collective-permute-done | bytes 98336 | tf_op jit(solution)/shard_map/ppermute | solution.py:467
  16.5 0.8 %first.1 = (f32[32,640]{1,0:T(8,128)S(1)}, f32[2,32,256]{2,1,0:T(8,128)S(1)}, bf16[4,48,256]{2,1,0:T(8,128)(2,1)S(1)}) custom-call(bf16[4,48,256]{2,1,0:T(8,128)(2,1)S(1)} %join.1.joined_ref.even_ref, bf16[4,48,256]{2,1,0:T(8,128)(2,1)S(1)} %collective-permute-done.3.far_even_ref, bf16[4,48,256]{2,1,0:T(8,128)(2,1)S(1)} %collective-permute-done.4.odd_ref, ...), custom_call_target="tpu_custom_call" | custom-call | tf_op jit(solution)/shard_map/first/pallas_call | solution.py:568
  17.3 0.1 collective-permute-start.5
  17.4 1.3 %collective-permute-done.5.other_ref = f32[32,640]{1,0:T(8,128)S(1)} collective-permute-done((f32[32,640]{1,0:T(8,128)S(1)}, f32[32,640]{1,0:T(8,128)S(1)}, u32[]{:S(2)}, u32[]{:S(2)}) %collective-permute-start.5) | collective-permute-done | bytes 81952 | tf_op jit(solution)/shard_map/ppermute | solution.py:470
  18.7 0.3 image.2
  19.0 3.0 %collective-permute-start.6 = (f32[136,128]{1,0:T(8,128)S(1)}, f32[136,128]{1,0:T(8,128)S(1)}, u32[]{:S(2)}, u32[]{:S(2)}) collective-permute-start(f32[136,128]{1,0:T(8,128)S(1)} %get-tuple-element.33.refs_0_), channel_id=1, source_target_pairs={{0,14},{2,12},{4,10},{6,8},{8,6},{10,4},{12,2},{14,0},{1,13},{3,15... | collective-permute-start | bytes 208904 | tf_op jit(solution)/shard_map/ppermute | solution.py:487
  22.0 0.9 %collective-permute-start.7 = (f32[136,128]{1,0:T(8,128)S(1)}, f32[136,128]{1,0:T(8,128)S(1)}, u32[]{:S(2)}, u32[]{:S(2)}) collective-permute-start(f32[136,128]{1,0:T(8,128)S(1)} %get-tuple-element.33.refs_0_), channel_id=1, source_target_pairs={{0,6},{2,4},{4,2},{6,0},{8,14},{10,12},{12,10},{14,8},{1,11},{3,9}... | collective-permute-start | bytes 208904 | tf_op jit(solution)/shard_map/ppermute | solution.py:487
  22.9 1.1 %collective-permute-start.8 = (f32[136,128]{1,0:T(8,128)S(1)}, f32[136,128]{1,0:T(8,128)S(1)}, u32[]{:S(2)}, u32[]{:S(2)}) collective-permute-start(f32[136,128]{1,0:T(8,128)S(1)} %get-tuple-element.33.refs_0_), channel_id=1, source_target_pairs={{0,4},{2,6},{4,0},{6,2},{8,12},{10,14},{12,8},{14,10},{1,9},{3,11}... | collective-permute-start | bytes 208904 | tf_op jit(solution)/shard_map/ppermute | solution.py:487
  24.0 0.3 collective-permute-start.13
  24.3 1.2 %collective-permute-start.9 = (f32[136,128]{1,0:T(8,128)S(1)}, f32[136,128]{1,0:T(8,128)S(1)}, u32[]{:S(2)}, u32[]{:S(2)}) collective-permute-start(f32[136,128]{1,0:T(8,128)S(1)} %get-tuple-element.33.refs_0_), channel_id=1, source_target_pairs={{0,2},{2,0},{4,6},{6,4},{8,10},{10,8},{12,14},{14,12},{1,3},{3,1},... | collective-permute-start | bytes 208904 | tf_op jit(solution)/shard_map/ppermute | solution.py:487
  25.5 1.0 %collective-permute-done.6.refs_1_ = f32[136,128]{1,0:T(8,128)S(1)} collective-permute-done((f32[136,128]{1,0:T(8,128)S(1)}, f32[136,128]{1,0:T(8,128)S(1)}, u32[]{:S(2)}, u32[]{:S(2)}) %collective-permute-start.6) | collective-permute-done | bytes 69664 | tf_op jit(solution)/shard_map/ppermute | solution.py:487
  26.5 0.0 collective-permute-start.10
  26.6 1.4 %collective-permute-done.7.refs_2_ = f32[136,128]{1,0:T(8,128)S(1)} collective-permute-done((f32[136,128]{1,0:T(8,128)S(1)}, f32[136,128]{1,0:T(8,128)S(1)}, u32[]{:S(2)}, u32[]{:S(2)}) %collective-permute-start.7) | collective-permute-done | bytes 69664 | tf_op jit(solution)/shard_map/ppermute | solution.py:487
  27.9 0.0 collective-permute-start.11
  27.9 1.2 %collective-permute-done.8.refs_3_ = f32[136,128]{1,0:T(8,128)S(1)} collective-permute-done((f32[136,128]{1,0:T(8,128)S(1)}, f32[136,128]{1,0:T(8,128)S(1)}, u32[]{:S(2)}, u32[]{:S(2)}) %collective-permute-start.8) | collective-permute-done | bytes 69664 | tf_op jit(solution)/shard_map/ppermute | solution.py:487
  29.2 0.0 collective-permute-start.12
  29.2 0.8 %inverse.2.refs_11_ = f32[32,128]{1,0:T(8,128)S(1)} custom-call(f32[32,128]{1,0:T(8,128)S(1)} %get-tuple-element.37.norm_ref.refs_10_), custom_call_target="tpu_custom_call" | custom-call | tf_op jit(solution)/shard_map/inverse/pallas_call | solution.py:603
  29.9 0.1 collect.1
  30.1 0.0 collective-permute-done.11.refs_6_
  30.1 0.3 collective-permute-done.12.refs_7_
  30.4 2.8 %step.2 = (f32[32,512]{1,0:T(8,128)S(1)}, f32[9,32,256]{2,1,0:T(8,128)S(1)}, f32[2,8,32,256]{3,2,1,0:T(8,128)S(1)}, f32[32,128]{1,0:T(8,128)S(1)}, f32[32,256]{1,0:T(8,128)S(1)}) custom-call(f32[136,128]{1,0:T(8,128)S(1)} %get-tuple-element.33.refs_0_, f32[136,128]{1,0:T(8,128)S(1)} %collective-permute-done.6.refs_1_, ...), custom_call_target="tpu_custom_call" | custom-call | tf_op jit(solution)/shard_map/step/pallas_call | solution.py:612
  33.2 0.2 collective-permute-start.14
  33.4 1.1 %collective-permute-done.14.other_ref = f32[32,512]{1,0:T(8,128)S(1)} collective-permute-done((f32[32,512]{1,0:T(8,128)S(1)}, f32[32,512]{1,0:T(8,128)S(1)}, u32[]{:S(2)}, u32[]{:S(2)}) %collective-permute-start.14) | collective-permute-done | bytes 65568 | tf_op jit(solution)/shard_map/ppermute | solution.py:470
  34.5 0.3 image.3.refs_0_
  34.8 2.1 %collective-permute-start.15 = (f32[136,128]{1,0:T(8,128)S(1)}, f32[136,128]{1,0:T(8,128)S(1)}, u32[]{:S(2)}, u32[]{:S(2)}) collective-permute-start(f32[136,128]{1,0:T(8,128)S(1)} %image.3.refs_0_), channel_id=1, source_target_pairs={{0,14},{2,12},{4,10},{6,8},{8,6},{10,4},{12,2},{14,0},{1,13},{3,15... | collective-permute-start | bytes 208904 | tf_op jit(solution)/shard_map/ppermute | solution.py:487
  36.9 0.8 %collective-permute-start.16 = (f32[136,128]{1,0:T(8,128)S(1)}, f32[136,128]{1,0:T(8,128)S(1)}, u32[]{:S(2)}, u32[]{:S(2)}) collective-permute-start(f32[136,128]{1,0:T(8,128)S(1)} %image.3.refs_0_), channel_id=1, source_target_pairs={{0,6},{2,4},{4,2},{6,0},{8,14},{10,12},{12,10},{14,8},{1,11},{3,9}... | collective-permute-start | bytes 208904 | tf_op jit(solution)/shard_map/ppermute | solution.py:487
  37.8 1.7 %collective-permute-start.17 = (f32[136,128]{1,0:T(8,128)S(1)}, f32[136,128]{1,0:T(8,128)S(1)}, u32[]{:S(2)}, u32[]{:S(2)}) collective-permute-start(f32[136,128]{1,0:T(8,128)S(1)} %image.3.refs_0_), channel_id=1, source_target_pairs={{0,4},{2,6},{4,0},{6,2},{8,12},{10,14},{12,8},{14,10},{1,9},{3,11}... | collective-permute-start | bytes 208904 | tf_op jit(solution)/shard_map/ppermute | solution.py:487
  39.5 1.0 %collective-permute-start.18 = (f32[136,128]{1,0:T(8,128)S(1)}, f32[136,128]{1,0:T(8,128)S(1)}, u32[]{:S(2)}, u32[]{:S(2)}) collective-permute-start(f32[136,128]{1,0:T(8,128)S(1)} %image.3.refs_0_), channel_id=1, source_target_pairs={{0,2},{2,0},{4,6},{6,4},{8,10},{10,8},{12,14},{14,12},{1,3},{3,1},... | collective-permute-start | bytes 208904 | tf_op jit(solution)/shard_map/ppermute | solution.py:487
  40.4 1.8 %collective-permute-done.15.refs_1_ = f32[136,128]{1,0:T(8,128)S(1)} collective-permute-done((f32[136,128]{1,0:T(8,128)S(1)}, f32[136,128]{1,0:T(8,128)S(1)}, u32[]{:S(2)}, u32[]{:S(2)}) %collective-permute-start.15) | collective-permute-done | bytes 69664 | tf_op jit(solution)/shard_map/ppermute | solution.py:487
  42.2 1.4 %collective-permute-done.16.refs_2_ = f32[136,128]{1,0:T(8,128)S(1)} collective-permute-done((f32[136,128]{1,0:T(8,128)S(1)}, f32[136,128]{1,0:T(8,128)S(1)}, u32[]{:S(2)}, u32[]{:S(2)}) %collective-permute-start.16) | collective-permute-done | bytes 69664 | tf_op jit(solution)/shard_map/ppermute | solution.py:487
  43.6 0.8 %collective-permute-done.17.refs_3_ = f32[136,128]{1,0:T(8,128)S(1)} collective-permute-done((f32[136,128]{1,0:T(8,128)S(1)}, f32[136,128]{1,0:T(8,128)S(1)}, u32[]{:S(2)}, u32[]{:S(2)}) %collective-permute-start.17) | collective-permute-done | bytes 69664 | tf_op jit(solution)/shard_map/ppermute | solution.py:487
  44.4 0.8 %inverse.3.refs_11_ = f32[32,128]{1,0:T(8,128)S(1)} custom-call(f32[32,128]{1,0:T(8,128)S(1)} %get-tuple-element.41.norm_ref.refs_10_), custom_call_target="tpu_custom_call" | custom-call | tf_op jit(solution)/shard_map/inverse/pallas_call | solution.py:603
  45.2 0.0 collective-permute-done.18.refs_4_
  45.2 0.0 collective-permute-done.20.refs_6_
  45.2 0.4 collective-permute-done.21.refs_7_
  45.7 2.8 %step.3 = (f32[32,512]{1,0:T(8,128)S(1)}, f32[2,32,256]{2,1,0:T(8,128)S(1)}, f32[32,256]{1,0:T(8,128)S(1)}, f32[32,128]{1,0:T(8,128)S(1)}, f32[32,256]{1,0:T(8,128)S(1)}) custom-call(f32[136,128]{1,0:T(8,128)S(1)} %image.3.refs_0_, f32[136,128]{1,0:T(8,128)S(1)} %collective-permute-done.15.refs_1_, f32[136,128]{1,0:T(8,128)S(1)} %collective-permute-done.16.refs_2_, ...), custom_call_target="tpu_custom_call" | custom-call | tf_op jit(solution)/shard_map/step/pallas_call | solution.py:612
  48.5 0.2 collective-permute-start.22
  48.6 1.1 %collective-permute-done.22.other_ref = f32[32,512]{1,0:T(8,128)S(1)} collective-permute-done((f32[32,512]{1,0:T(8,128)S(1)}, f32[32,512]{1,0:T(8,128)S(1)}, u32[]{:S(2)}, u32[]{:S(2)}) %collective-permute-start.22) | collective-permute-done | bytes 65568 | tf_op jit(solution)/shard_map/ppermute | solution.py:470
  49.7 0.3 last_image.1
  50.1 2.0 %collective-permute-start.23 = (f32[8,128]{1,0:T(8,128)S(1)}, f32[8,128]{1,0:T(8,128)S(1)}, u32[]{:S(2)}, u32[]{:S(2)}) collective-permute-start(f32[8,128]{1,0:T(8,128)S(1)} %get-tuple-element.45.refs_0_), channel_id=1, source_target_pairs={{0,12},{2,14},{4,8},{6,10},{8,4},{10,6},{12,0},{14,2},{1,15},{3,13... | collective-permute-start | bytes 12296 | tf_op jit(solution)/shard_map/ppermute | solution.py:487
  52.1 1.9 %collective-permute-start.25 = (f32[8,128]{1,0:T(8,128)S(1)}, f32[8,128]{1,0:T(8,128)S(1)}, u32[]{:S(2)}, u32[]{:S(2)}) collective-permute-start(f32[8,128]{1,0:T(8,128)S(1)} %get-tuple-element.45.refs_0_), channel_id=1, source_target_pairs={{0,4},{2,6},{4,0},{6,2},{8,12},{10,14},{12,8},{14,10},{1,9},{3,11}... | collective-permute-start | bytes 12296 | tf_op jit(solution)/shard_map/ppermute | solution.py:487
  54.0 1.5 %collective-permute-start.26 = (f32[8,128]{1,0:T(8,128)S(1)}, f32[8,128]{1,0:T(8,128)S(1)}, u32[]{:S(2)}, u32[]{:S(2)}) collective-permute-start(f32[8,128]{1,0:T(8,128)S(1)} %get-tuple-element.45.refs_0_), channel_id=1, source_target_pairs={{0,2},{2,0},{4,6},{6,4},{8,10},{10,8},{12,14},{14,12},{1,3},{3,1},... | collective-permute-start | bytes 12296 | tf_op jit(solution)/shard_map/ppermute | solution.py:487
  55.6 0.0 collective-permute-start.27
  55.6 1.0 %collective-permute-done.24.refs_2_ = f32[8,128]{1,0:T(8,128)S(1)} collective-permute-done((f32[8,128]{1,0:T(8,128)S(1)}, f32[8,128]{1,0:T(8,128)S(1)}, u32[]{:S(2)}, u32[]{:S(2)}) %collective-permute-start.24) | collective-permute-done | bytes 4128 | tf_op jit(solution)/shard_map/ppermute | solution.py:487
  56.6 0.0 collective-permute-start.28
  56.6 0.0 collective-permute-done.25.refs_3_
  56.6 0.5 collective-permute-start.29
  57.1 0.5 collective-permute-done.26.refs_4_
  57.7 0.0 collective-permute-done.27.refs_5_
  57.7 0.1 collective-permute-done.28.refs_6_
  57.8 0.2 collective-permute-done.29.refs_7_
  58.0 1.5 %last.1 = (f32[32,256]{1,0:T(8,128)}, f32[32,256]{1,0:T(8,128)}) custom-call(f32[8,128]{1,0:T(8,128)S(1)} %get-tuple-element.45.refs_0_, f32[8,128]{1,0:T(8,128)S(1)} %collective-permute-done.23.refs_1_, f32[8,128]{1,0:T(8,128)S(1)} %collective-permute-done.24.refs_2_, f32[8,128]{1,0:T(8,128)S(1)} %collective-permute-done.25.refs_3_, ...), custom_call_target="tpu_custom_call" | custom-call | tf_op jit(solution)/shard_map/last/pallas_call | solution.py:635
  (10 shorter events, 0.0 us)
Async XLA Ops:
  1.5 8.7 %collective-permute-start = (bf16[48,256]{1,0:T(8,128)(2,1)S(1)}, bf16[48,256]{1,0:T(8,128)(2,1)S(1)}, u32[]{:S(2)}, u32[]{:S(2)}) collective-permute-start(bf16[48,256]{1,0:T(8,128)(2,1)S(1)} %get-tuple-element.26.refs_3_), channel_id=1, source_target_pairs={{0,8},{2,10},{4,12},{6,14},{8,0},{10,2},{12,4},{14,6},{1,9},{3,11}... | collective-permute-start | bytes 73736 | tf_op jit(solution)/shard_map/ppermute | solution.py:467
  5.6 5.6 %collective-permute-start.1 = (bf16[48,256]{1,0:T(8,128)(2,1)S(1)}, bf16[48,256]{1,0:T(8,128)(2,1)S(1)}, u32[]{:S(2)}, u32[]{:S(2)}) collective-permute-start(bf16[48,256]{1,0:T(8,128)(2,1)S(1)} %get-tuple-element.26.refs_3_), channel_id=1, source_target_pairs={{0,12},{2,14},{4,8},{6,10},{8,4},{10,6},{12,0},{14,2},{1,13},{3,15... | collective-permute-start | bytes 73736 | tf_op jit(solution)/shard_map/ppermute | solution.py:467
  7.0 4.3 %collective-permute-start.2 = (bf16[48,256]{1,0:T(8,128)(2,1)S(1)}, bf16[48,256]{1,0:T(8,128)(2,1)S(1)}, u32[]{:S(2)}, u32[]{:S(2)}) collective-permute-start(bf16[48,256]{1,0:T(8,128)(2,1)S(1)} %get-tuple-element.26.refs_3_), channel_id=1, source_target_pairs={{0,4},{2,6},{4,0},{6,2},{8,12},{10,14},{12,8},{14,10},{1,5},{3,7},... | collective-permute-start | bytes 73736 | tf_op jit(solution)/shard_map/ppermute | solution.py:467
  11.2 3.9 %collective-permute-start.3 = (bf16[4,48,256]{2,1,0:T(8,128)(2,1)S(1)}, bf16[4,48,256]{2,1,0:T(8,128)(2,1)S(1)}, u32[]{:S(2)}, u32[]{:S(2)}) collective-permute-start(bf16[4,48,256]{2,1,0:T(8,128)(2,1)S(1)} %join.1.joined_ref.even_ref), channel_id=1, source_target_pairs={{0,1},{1,0},{2,3},{3,2},{4,5},{5,4},{6,7},{7,6},{8,9},{9,8},{10,11... | collective-permute-start | bytes 294920 | tf_op jit(solution)/shard_map/ppermute | solution.py:470
  11.3 5.2 %collective-permute-start.4 = (bf16[4,48,256]{2,1,0:T(8,128)(2,1)S(1)}, bf16[4,48,256]{2,1,0:T(8,128)(2,1)S(1)}, u32[]{:S(2)}, u32[]{:S(2)}) collective-permute-start(bf16[4,48,256]{2,1,0:T(8,128)(2,1)S(1)} %join.1.joined_ref.even_ref), channel_id=1, source_target_pairs={{0,2},{2,0},{4,6},{6,4},{8,10},{10,8},{12,14},{14,12},{1,3},{3,1},... | collective-permute-start | bytes 294920 | tf_op jit(solution)/shard_map/ppermute | solution.py:467
  17.3 1.3 %collective-permute-start.5 = (f32[32,640]{1,0:T(8,128)S(1)}, f32[32,640]{1,0:T(8,128)S(1)}, u32[]{:S(2)}, u32[]{:S(2)}) collective-permute-start(f32[32,640]{1,0:T(8,128)S(1)} %get-tuple-element.31.mine_ref), channel_id=1, source_target_pairs={{0,1},{1,0},{2,3},{3,2},{4,5},{5,4},{6,7},{7,6},{8,9},{9,8},{10,11... | collective-permute-start | bytes 245768 | tf_op jit(solution)/shard_map/ppermute | solution.py:470
  19.0 7.5 %collective-permute-start.6 = (f32[136,128]{1,0:T(8,128)S(1)}, f32[136,128]{1,0:T(8,128)S(1)}, u32[]{:S(2)}, u32[]{:S(2)}) collective-permute-start(f32[136,128]{1,0:T(8,128)S(1)} %get-tuple-element.33.refs_0_), channel_id=1, source_target_pairs={{0,14},{2,12},{4,10},{6,8},{8,6},{10,4},{12,2},{14,0},{1,13},{3,15... | collective-permute-start | bytes 208904 | tf_op jit(solution)/shard_map/ppermute | solution.py:487
  22.0 5.9 %collective-permute-start.7 = (f32[136,128]{1,0:T(8,128)S(1)}, f32[136,128]{1,0:T(8,128)S(1)}, u32[]{:S(2)}, u32[]{:S(2)}) collective-permute-start(f32[136,128]{1,0:T(8,128)S(1)} %get-tuple-element.33.refs_0_), channel_id=1, source_target_pairs={{0,6},{2,4},{4,2},{6,0},{8,14},{10,12},{12,10},{14,8},{1,11},{3,9}... | collective-permute-start | bytes 208904 | tf_op jit(solution)/shard_map/ppermute | solution.py:487
  22.9 6.3 %collective-permute-start.8 = (f32[136,128]{1,0:T(8,128)S(1)}, f32[136,128]{1,0:T(8,128)S(1)}, u32[]{:S(2)}, u32[]{:S(2)}) collective-permute-start(f32[136,128]{1,0:T(8,128)S(1)} %get-tuple-element.33.refs_0_), channel_id=1, source_target_pairs={{0,4},{2,6},{4,0},{6,2},{8,12},{10,14},{12,8},{14,10},{1,9},{3,11}... | collective-permute-start | bytes 208904 | tf_op jit(solution)/shard_map/ppermute | solution.py:487
  24.0 6.0 %collective-permute-start.13 = (bf16[4,48,256]{2,1,0:T(8,128)(2,1)S(1)}, bf16[4,48,256]{2,1,0:T(8,128)(2,1)S(1)}, u32[]{:S(2)}, u32[]{:S(2)}) collective-permute-start(bf16[4,48,256]{2,1,0:T(8,128)(2,1)S(1)} %get-tuple-element.34.odd_ref), channel_id=1, source_target_pairs={{0,1},{1,0},{2,3},{3,2},{4,5},{5,4},{6,7},{7,6},{8,9},{9,8},{10,11... | collective-permute-start | bytes 294920 | tf_op jit(solution)/shard_map/ppermute | solution.py:470
  24.3 5.8 %collective-permute-start.9 = (f32[136,128]{1,0:T(8,128)S(1)}, f32[136,128]{1,0:T(8,128)S(1)}, u32[]{:S(2)}, u32[]{:S(2)}) collective-permute-start(f32[136,128]{1,0:T(8,128)S(1)} %get-tuple-element.33.refs_0_), channel_id=1, source_target_pairs={{0,2},{2,0},{4,6},{6,4},{8,10},{10,8},{12,14},{14,12},{1,3},{3,1},... | collective-permute-start | bytes 208904 | tf_op jit(solution)/shard_map/ppermute | solution.py:487
  26.5 3.5 %collective-permute-start.10 = (f32[136,128]{1,0:T(8,128)S(1)}, f32[136,128]{1,0:T(8,128)S(1)}, u32[]{:S(2)}, u32[]{:S(2)}) collective-permute-start(f32[136,128]{1,0:T(8,128)S(1)} %collective-permute-done.6.refs_1_), channel_id=1, source_target_pairs={{0,1},{1,0},{2,3},{3,2},{4,5},{5,4},{6,7},{7,6},{8,9},{9,8},{10,11... | collective-permute-start | bytes 208904 | tf_op jit(solution)/shard_map/ppermute | solution.py:470
  27.9 2.1 %collective-permute-start.11 = (f32[136,128]{1,0:T(8,128)S(1)}, f32[136,128]{1,0:T(8,128)S(1)}, u32[]{:S(2)}, u32[]{:S(2)}) collective-permute-start(f32[136,128]{1,0:T(8,128)S(1)} %collective-permute-done.7.refs_2_), channel_id=1, source_target_pairs={{0,1},{1,0},{2,3},{3,2},{4,5},{5,4},{6,7},{7,6},{8,9},{9,8},{10,11... | collective-permute-start | bytes 208904 | tf_op jit(solution)/shard_map/ppermute | solution.py:470
  29.2 1.3 %collective-permute-start.12 = (f32[136,128]{1,0:T(8,128)S(1)}, f32[136,128]{1,0:T(8,128)S(1)}, u32[]{:S(2)}, u32[]{:S(2)}) collective-permute-start(f32[136,128]{1,0:T(8,128)S(1)} %collective-permute-done.8.refs_3_), channel_id=1, source_target_pairs={{0,1},{1,0},{2,3},{3,2},{4,5},{5,4},{6,7},{7,6},{8,9},{9,8},{10,11... | collective-permute-start | bytes 208904 | tf_op jit(solution)/shard_map/ppermute | solution.py:470
  33.2 1.3 %collective-permute-start.14 = (f32[32,512]{1,0:T(8,128)S(1)}, f32[32,512]{1,0:T(8,128)S(1)}, u32[]{:S(2)}, u32[]{:S(2)}) collective-permute-start(f32[32,512]{1,0:T(8,128)S(1)} %get-tuple-element.38.mine_ref), channel_id=1, source_target_pairs={{0,1},{1,0},{2,3},{3,2},{4,5},{5,4},{6,7},{7,6},{8,9},{9,8},{10,11... | collective-permute-start | bytes 196616 | tf_op jit(solution)/shard_map/ppermute | solution.py:470
  34.8 7.4 %collective-permute-start.15 = (f32[136,128]{1,0:T(8,128)S(1)}, f32[136,128]{1,0:T(8,128)S(1)}, u32[]{:S(2)}, u32[]{:S(2)}) collective-permute-start(f32[136,128]{1,0:T(8,128)S(1)} %image.3.refs_0_), channel_id=1, source_target_pairs={{0,14},{2,12},{4,10},{6,8},{8,6},{10,4},{12,2},{14,0},{1,13},{3,15... | collective-permute-start | bytes 208904 | tf_op jit(solution)/shard_map/ppermute | solution.py:487
  36.9 6.6 %collective-permute-start.16 = (f32[136,128]{1,0:T(8,128)S(1)}, f32[136,128]{1,0:T(8,128)S(1)}, u32[]{:S(2)}, u32[]{:S(2)}) collective-permute-start(f32[136,128]{1,0:T(8,128)S(1)} %image.3.refs_0_), channel_id=1, source_target_pairs={{0,6},{2,4},{4,2},{6,0},{8,14},{10,12},{12,10},{14,8},{1,11},{3,9}... | collective-permute-start | bytes 208904 | tf_op jit(solution)/shard_map/ppermute | solution.py:487
  37.8 6.7 %collective-permute-start.17 = (f32[136,128]{1,0:T(8,128)S(1)}, f32[136,128]{1,0:T(8,128)S(1)}, u32[]{:S(2)}, u32[]{:S(2)}) collective-permute-start(f32[136,128]{1,0:T(8,128)S(1)} %image.3.refs_0_), channel_id=1, source_target_pairs={{0,4},{2,6},{4,0},{6,2},{8,12},{10,14},{12,8},{14,10},{1,9},{3,11}... | collective-permute-start | bytes 208904 | tf_op jit(solution)/shard_map/ppermute | solution.py:487
  39.5 5.7 %collective-permute-start.18 = (f32[136,128]{1,0:T(8,128)S(1)}, f32[136,128]{1,0:T(8,128)S(1)}, u32[]{:S(2)}, u32[]{:S(2)}) collective-permute-start(f32[136,128]{1,0:T(8,128)S(1)} %image.3.refs_0_), channel_id=1, source_target_pairs={{0,2},{2,0},{4,6},{6,4},{8,10},{10,8},{12,14},{14,12},{1,3},{3,1},... | collective-permute-start | bytes 208904 | tf_op jit(solution)/shard_map/ppermute | solution.py:487
  42.2 3.0 %collective-permute-start.19 = (f32[136,128]{1,0:T(8,128)S(1)}, f32[136,128]{1,0:T(8,128)S(1)}, u32[]{:S(2)}, u32[]{:S(2)}) collective-permute-start(f32[136,128]{1,0:T(8,128)S(1)} %collective-permute-done.15.refs_1_), channel_id=1, source_target_pairs={{0,1},{1,0},{2,3},{3,2},{4,5},{5,4},{6,7},{7,6},{8,9},{9,8},{10,11... | collective-permute-start | bytes 208904 | tf_op jit(solution)/shard_map/ppermute | solution.py:470
  43.6 1.7 %collective-permute-start.20 = (f32[136,128]{1,0:T(8,128)S(1)}, f32[136,128]{1,0:T(8,128)S(1)}, u32[]{:S(2)}, u32[]{:S(2)}) collective-permute-start(f32[136,128]{1,0:T(8,128)S(1)} %collective-permute-done.16.refs_2_), channel_id=1, source_target_pairs={{0,1},{1,0},{2,3},{3,2},{4,5},{5,4},{6,7},{7,6},{8,9},{9,8},{10,11... | collective-permute-start | bytes 208904 | tf_op jit(solution)/shard_map/ppermute | solution.py:470
  44.4 1.3 %collective-permute-start.21 = (f32[136,128]{1,0:T(8,128)S(1)}, f32[136,128]{1,0:T(8,128)S(1)}, u32[]{:S(2)}, u32[]{:S(2)}) collective-permute-start(f32[136,128]{1,0:T(8,128)S(1)} %collective-permute-done.17.refs_3_), channel_id=1, source_target_pairs={{0,1},{1,0},{2,3},{3,2},{4,5},{5,4},{6,7},{7,6},{8,9},{9,8},{10,11... | collective-permute-start | bytes 208904 | tf_op jit(solution)/shard_map/ppermute | solution.py:470
  48.5 1.3 %collective-permute-start.22 = (f32[32,512]{1,0:T(8,128)S(1)}, f32[32,512]{1,0:T(8,128)S(1)}, u32[]{:S(2)}, u32[]{:S(2)}) collective-permute-start(f32[32,512]{1,0:T(8,128)S(1)} %get-tuple-element.43.mine_ref), channel_id=1, source_target_pairs={{0,1},{1,0},{2,3},{3,2},{4,5},{5,4},{6,7},{7,6},{8,9},{9,8},{10,11... | collective-permute-start | bytes 196616 | tf_op jit(solution)/shard_map/ppermute | solution.py:470
  50.1 5.5 %collective-permute-start.23 = (f32[8,128]{1,0:T(8,128)S(1)}, f32[8,128]{1,0:T(8,128)S(1)}, u32[]{:S(2)}, u32[]{:S(2)}) collective-permute-start(f32[8,128]{1,0:T(8,128)S(1)} %get-tuple-element.45.refs_0_), channel_id=1, source_target_pairs={{0,12},{2,14},{4,8},{6,10},{8,4},{10,6},{12,0},{14,2},{1,15},{3,13... | collective-permute-start | bytes 12296 | tf_op jit(solution)/shard_map/ppermute | solution.py:487
  52.1 4.5 %collective-permute-start.24 = (f32[8,128]{1,0:T(8,128)S(1)}, f32[8,128]{1,0:T(8,128)S(1)}, u32[]{:S(2)}, u32[]{:S(2)}) collective-permute-start(f32[8,128]{1,0:T(8,128)S(1)} %get-tuple-element.45.refs_0_), channel_id=1, source_target_pairs={{0,6},{2,4},{4,2},{6,0},{8,14},{10,12},{12,10},{14,8},{1,11},{3,9}... | collective-permute-start | bytes 12296 | tf_op jit(solution)/shard_map/ppermute | solution.py:487
  52.1 4.5 %collective-permute-start.25 = (f32[8,128]{1,0:T(8,128)S(1)}, f32[8,128]{1,0:T(8,128)S(1)}, u32[]{:S(2)}, u32[]{:S(2)}) collective-permute-start(f32[8,128]{1,0:T(8,128)S(1)} %get-tuple-element.45.refs_0_), channel_id=1, source_target_pairs={{0,4},{2,6},{4,0},{6,2},{8,12},{10,14},{12,8},{14,10},{1,9},{3,11}... | collective-permute-start | bytes 12296 | tf_op jit(solution)/shard_map/ppermute | solution.py:487
  54.0 3.6 %collective-permute-start.26 = (f32[8,128]{1,0:T(8,128)S(1)}, f32[8,128]{1,0:T(8,128)S(1)}, u32[]{:S(2)}, u32[]{:S(2)}) collective-permute-start(f32[8,128]{1,0:T(8,128)S(1)} %get-tuple-element.45.refs_0_), channel_id=1, source_target_pairs={{0,2},{2,0},{4,6},{6,4},{8,10},{10,8},{12,14},{14,12},{1,3},{3,1},... | collective-permute-start | bytes 12296 | tf_op jit(solution)/shard_map/ppermute | solution.py:487
  55.6 2.1 %collective-permute-start.27 = (f32[8,128]{1,0:T(8,128)S(1)}, f32[8,128]{1,0:T(8,128)S(1)}, u32[]{:S(2)}, u32[]{:S(2)}) collective-permute-start(f32[8,128]{1,0:T(8,128)S(1)} %collective-permute-done.23.refs_1_), channel_id=1, source_target_pairs={{0,1},{1,0},{2,3},{3,2},{4,5},{5,4},{6,7},{7,6},{8,9},{9,8},{10,11... | collective-permute-start | bytes 12296 | tf_op jit(solution)/shard_map/ppermute | solution.py:470
  56.6 1.2 %collective-permute-start.28 = (f32[8,128]{1,0:T(8,128)S(1)}, f32[8,128]{1,0:T(8,128)S(1)}, u32[]{:S(2)}, u32[]{:S(2)}) collective-permute-start(f32[8,128]{1,0:T(8,128)S(1)} %collective-permute-done.24.refs_2_), channel_id=1, source_target_pairs={{0,1},{1,0},{2,3},{3,2},{4,5},{5,4},{6,7},{7,6},{8,9},{9,8},{10,11... | collective-permute-start | bytes 12296 | tf_op jit(solution)/shard_map/ppermute | solution.py:470
  56.6 1.3 %collective-permute-start.29 = (f32[8,128]{1,0:T(8,128)S(1)}, f32[8,128]{1,0:T(8,128)S(1)}, u32[]{:S(2)}, u32[]{:S(2)}) collective-permute-start(f32[8,128]{1,0:T(8,128)S(1)} %collective-permute-done.25.refs_3_), channel_id=1, source_target_pairs={{0,1},{1,0},{2,3},{3,2},{4,5},{5,4},{6,7},{7,6},{8,9},{9,8},{10,11... | collective-permute-start | bytes 12296 | tf_op jit(solution)/shard_map/ppermute | solution.py:470
